TPU v7x, 32 devices: a whole 2x2x4 slice. The times are simulated.
32 devices in a mesh: seq: 2 (over x), head: 4 (over z), exp: 4 (over y, core).
Axes of the slice: x: 2, y: 2, z: 4, core: 2. Of those that a mesh axis runs over, the one named last changes fastest.
Arguments:
- x_in: bfloat16 [1024, 4096], P(('seq', 'exp'), 'head'), may hold values from -6 to 6
- z_in: bfloat16 [1024, 4096], P(('seq', 'exp'), 'head'), may hold values from -6 to 6
- b_in: bfloat16 [1024, 1024], P(('seq', 'exp'), 'head'), may hold values from -1.796875 to 1.796875
- c_in: bfloat16 [1024, 1024], P(('seq', 'exp'), 'head'), may hold values from -1.796875 to 1.796875
- dt_in: float32 [1024, 64], P(('seq', 'exp'), 'head'), may hold values from -5.4 to -1.7
- a_log: float32 [64], P('head'), may hold values from -12 to 2
- d_skip: float32 [64], P('head'), may hold values from 0.5 to 2
- norm_w: float32 [4096], P('head'), may hold values from 0.5 to 1.5
- w_out: bfloat16 [4096, 1344], P('head'), may hold values from -0.09375 to 0.09375
- resid: bfloat16 [8, 128, 1344], P(('seq', 'exp'), 'head'), may hold values from -30 to 30
- routes: int32 [8, 128, 6], P(('seq', 'exp'), 'head'), may hold values from 0 to 15, all different within a row; in each aligned block of 32 rows (0 to 31, 32 to 63, ..., all dimensions but the last counted through in order) at most 24 rows name the same one
- gates: float32 [8, 128, 6], P(('seq', 'exp'), 'head'), may hold values from 0.1 to 0.7
- moe_gain: float32 [1344], replicated, may hold values from 0.5 to 1.5
- w_up: bfloat16 [16, 1344, 928], P(('head', 'exp')), may hold values from -0.15625 to 0.15625
- w_down: bfloat16 [16, 928, 1344], P(('head', 'exp')), may hold values from -0.1875 to 0.1875
Outputs:
- output: bfloat16 [8, 128, 1344], P(('seq', 'exp'), 'head')
Inputs may be any that keep to these rules, and one draw needn't show every extreme that they name: `routes`: within the 32 aligned rows of one device no expert is named more than 24 times, and in every draw some expert is named exactly 24 times within some device's rows.
All inputs are finite; a program needn't handle non-finite values.
Results may differ from a plain program's by a relative error of at most 0.018.
Values may be sent and summed in bfloat16 or wider, within the bound.
No kernel may reach another device: no remote copies, remote signals or barrier semaphores. Data moves between devices by JAX's collectives and lax.ppermute only.
A program may use at most 64 MiB of HBM per device.

v0:
```python
import jax
import jax.numpy as jnp
from jax import lax
from jax.sharding import PartitionSpec as P

HEAD_DIM = 64
STATE = 128
STRETCH = 128


def prefix(shard, axis, combine, identity):
    count, index = (lax.axis_size(axis), lax.axis_index(axis))
    everything = jax.tree.map(
        lambda part, kind: lax.all_gather(part.astype(kind), axis),
        shard,
        (jnp.bfloat16, jnp.bfloat16),
    )
    start = jax.tree.map(
        lambda part, zero: jnp.broadcast_to(jnp.asarray(zero, part.dtype), part.shape),
        shard,
        identity,
    )

    def turn(k, before):
        reached = k < index
        new = combine(
            before, jax.tree.map(lambda part, own: part[k].astype(own.dtype), everything, shard)
        )
        return jax.tree.map(lambda a, b: jnp.where(reached, a, b), new, before)

    return lax.fori_loop(0, count, turn, start)


def stretch_pass(carry_state, pieces):
    x_part, b_part, c_part, rate_part, step_part = pieces
    per_group = x_part.shape[1] // b_part.shape[1]
    b_heads = jnp.repeat(b_part, per_group, axis=1)
    c_heads = jnp.repeat(c_part, per_group, axis=1)
    cumulative = jnp.cumsum(rate_part, axis=0)
    cum_heads = cumulative.T
    distance = cum_heads[:, :, None] - cum_heads[:, None, :]
    length = cumulative.shape[0]
    causal = (jnp.arange(length)[:, None] >= jnp.arange(length)[None, :])[None]
    decay_mat = jnp.where(causal, jnp.exp(jnp.where(causal, distance, 0.0)), 0.0)
    weighting = decay_mat * step_part.T[:, None, :]
    scores = jnp.einsum("thn,shn->hts", c_heads, b_heads, preferred_element_type=jnp.float32)
    mixing = (scores * weighting).astype(jnp.bfloat16)
    inside = jnp.einsum("hts,shp->thp", mixing, x_part, preferred_element_type=jnp.float32)
    state_low = carry_state.astype(jnp.bfloat16)
    carried = jnp.exp(cumulative)[:, :, None] * jnp.einsum(
        "thn,hpn->thp", c_heads, state_low, preferred_element_type=jnp.float32
    )
    tail_weight = jnp.exp(cumulative[-1][None, :] - cumulative) * step_part
    weighted_x = (tail_weight[:, :, None] * x_part.astype(jnp.float32)).astype(jnp.bfloat16)
    update = jnp.einsum("shp,shn->hpn", weighted_x, b_heads, preferred_element_type=jnp.float32)
    new_state = jnp.exp(cumulative[-1])[:, None, None] * carry_state + update
    return (new_state, inside + carried)


def by_stretch(values):
    return values.reshape((values.shape[0] // STRETCH, STRETCH) + values.shape[1:])


def join_pairs(earlier, later):
    return (earlier[0] + later[0], jnp.exp(later[0])[:, None, None] * earlier[1] + later[1])


def expert_rows(row_block, w_up, w_down):
    model_width = row_block.shape[-1]
    flat_rows = row_block.reshape(-1, model_width)
    up_proj = jnp.dot(flat_rows, w_up[0], preferred_element_type=jnp.float32)
    activated = jnp.square(jnp.maximum(up_proj, 0.0)).astype(jnp.bfloat16)
    produced = jnp.dot(activated, w_down[0], preferred_element_type=jnp.float32).astype(
        jnp.bfloat16
    )
    return produced.reshape(row_block.shape)


def per_device(
    x_in,
    z_in,
    b_in,
    c_in,
    dt_in,
    a_log,
    d_skip,
    norm_w,
    w_out,
    resid,
    routes,
    gates,
    moe_gain,
    w_up,
    w_down,
):
    length, head_count = dt_in.shape
    groups = b_in.shape[1] // STATE
    per_group = head_count // groups
    low_values = x_in.reshape(length, head_count, HEAD_DIM)
    b_groups = b_in.reshape(length, groups, STATE)
    c_groups = c_in.reshape(length, groups, STATE)
    step_size = jax.nn.softplus(dt_in)
    log_rate = -step_size * jnp.exp(a_log)[None, :]
    zero_state = jnp.zeros((head_count, HEAD_DIM, STATE), jnp.float32)
    zero_decay = jnp.zeros((head_count,), jnp.float32)
    last_state, local_out = lax.scan(
        stretch_pass,
        zero_state,
        (
            by_stretch(low_values),
            by_stretch(b_groups),
            by_stretch(c_groups),
            by_stretch(log_rate),
            by_stretch(step_size),
        ),
    )
    local_out = local_out.reshape(length, head_count, HEAD_DIM)
    decay_sum = jnp.sum(log_rate, axis=0)
    group_decays, group_states = (
        lax.all_gather(decay_sum[None].astype(jnp.bfloat16), "exp", axis=0, tiled=True).astype(
            jnp.float32
        ),
        lax.all_gather(last_state[None].astype(jnp.bfloat16), "exp", axis=0, tiled=True).astype(
            jnp.float32
        ),
    )

    def walk(carry_pair, item_pair):
        return (join_pairs(carry_pair, item_pair), carry_pair)

    span_pair, prefixes = lax.scan(walk, (zero_decay, zero_state), (group_decays, group_states))
    my_index = lax.axis_index("exp")
    inside_pair = (
        lax.dynamic_index_in_dim(prefixes[0], my_index, 0, keepdims=False),
        lax.dynamic_index_in_dim(prefixes[1], my_index, 0, keepdims=False),
    )
    chain_in = prefix((span_pair[0], span_pair[1]), "seq", join_pairs, (zero_decay, zero_state))
    before = join_pairs(chain_in, inside_pair)
    cum_device = jnp.cumsum(log_rate, axis=0)
    c_heads = jnp.repeat(c_groups, per_group, axis=1)
    before_low = before[1].astype(jnp.bfloat16)
    carried = jnp.exp(cum_device)[:, :, None] * jnp.einsum(
        "thn,hpn->thp", c_heads, before_low, preferred_element_type=jnp.float32
    )
    ssm_out = local_out + carried + d_skip[None, :, None] * low_values.astype(jnp.float32)
    gated_out = ssm_out * jax.nn.silu(
        z_in.astype(jnp.float32).reshape(length, head_count, HEAD_DIM)
    )
    grouped = gated_out.reshape(length, groups, -1)
    inverse = lax.rsqrt(jnp.mean(grouped * grouped, axis=2, keepdims=True) + 1e-05)
    normed = ((grouped * inverse).reshape(length, head_count * HEAD_DIM) * norm_w[None, :]).astype(
        jnp.bfloat16
    )
    rows_here = resid.shape[1]
    mixed = lax.psum_scatter(
        jnp.dot(normed, w_out, preferred_element_type=jnp.float32).astype(jnp.bfloat16),
        "head",
        scatter_dimension=0,
        tiled=True,
    ).astype(jnp.float32)
    hidden = (resid[0].astype(jnp.float32) + mixed).astype(jnp.bfloat16)
    hidden_f32 = hidden.astype(jnp.float32)
    norm_scale = lax.rsqrt(jnp.mean(hidden_f32 * hidden_f32, axis=1, keepdims=True) + 1e-05)
    moe_in = (hidden_f32 * norm_scale * moe_gain[None, :]).astype(jnp.bfloat16)
    head_size = lax.axis_size("head")
    exp_size = lax.axis_size("exp")
    experts_all = head_size * exp_size
    picks = routes.shape[2]
    room = min(rows_here, 8 * ((2 * rows_here * picks // experts_all + 7) // 8))
    flat_routes = routes[0].reshape(-1)
    onehot = (flat_routes[:, None] == jnp.arange(experts_all, dtype=jnp.int32)[None, :]).astype(
        jnp.int32
    )
    position = jnp.sum((jnp.cumsum(onehot, axis=0) - onehot) * onehot, axis=1)
    slot_id = flat_routes * room + position
    slot_table = (
        slot_id[:, None] == jnp.arange(experts_all * room, dtype=jnp.int32)[None, :]
    ).reshape(rows_here, picks, experts_all * room)
    chosen = jnp.sum(slot_table.astype(jnp.bfloat16), axis=1)
    outbound = lax.dot_general(
        chosen, moe_in, (((0,), (0,)), ((), ())), preferred_element_type=jnp.float32
    )
    outbound = outbound.astype(jnp.bfloat16).reshape(experts_all, room, moe_in.shape[1])
    produced = expert_rows(
        lax.all_to_all(outbound, ("head", "exp"), split_axis=0, concat_axis=0, tiled=True),
        w_up,
        w_down,
    )
    returned = lax.all_to_all(produced, ("head", "exp"), split_axis=0, concat_axis=0, tiled=True)
    returned_flat = returned.reshape(experts_all * room, moe_in.shape[1])
    picked_rows = returned_flat[slot_id.reshape(rows_here, picks)]
    moe_sum = jnp.sum(picked_rows.astype(jnp.float32) * gates[0][:, :, None], axis=1)
    return (hidden_f32 + moe_sum).astype(jnp.bfloat16)[None]


def solution(mesh):
    placed = (
        P(("seq", "exp"), "head"),
        P(("seq", "exp"), "head"),
        P(("seq", "exp"), "head"),
        P(("seq", "exp"), "head"),
        P(("seq", "exp"), "head"),
        P("head"),
        P("head"),
        P("head"),
        P("head", None),
        P(("seq", "exp"), "head", None),
        P(("seq", "exp"), "head", None),
        P(("seq", "exp"), "head", None),
        P(),
        P(("head", "exp"), None, None),
        P(("head", "exp"), None, None),
    )
    return jax.shard_map(
        per_device,
        mesh=mesh,
        in_specs=placed,
        out_specs=P(("seq", "exp"), "head", None),
        check_vma=False,
    )
```

profile of v0, /device:TPU:0, one launch (start us, length us, event | category | flops | bytes accessed | tf_op | source)
XLA Modules:
  0.0 186.5 jit_solution(3467291242561858253)
XLA Ops:
  6.6 0.8 exp.72
  7.4 0.9 fusion.67
  8.7 0.9 copy_bitcast_fusion
  9.6 1.1 copy.102
  10.7 1.3 fusion.62
  12.1 0.8 copy-done.3
  12.9 1.0 fusion.26
  15.6 8.3 %all-reduce.1 = bf16[64]{0:T(256)(128)(2,1)S(1)} all-reduce(bf16[64]{0:T(256)(128)(2,1)S(1)} %dynamic-update-slice), channel_id=2, replica_groups=mesh['seq'=2,'head'=4,'exp'=4] {'exp'}, use_global_device_ids=true, to_apply=%add.1 | all-reduce | flops 64 | bytes 256
  26.0 1.9 %copy.105 = f32[128,1024]{0,1:T(8,128)} copy(bf16[128,1024]{1,0:T(8,128)(2,1)} %param.20) | data formatting | bytes 786432 | tf_op jit(solution)/shard_map/reshape | solution.py:147
  28.7 1.2 reduce-window.6
  30.6 0.8 copy-done.1
  31.4 1.3 fusion.24
  32.7 0.8 all-gather.6.cloned.1.call-done
  33.5 2.8 %convert.12 = f32[4,16,64,128]{3,2,1,0:T(8,128)} convert(bf16[4,16,64,128]{3,2,1,0:T(8,128)(2,1)} %bitcast.158) | non-fusion elementwise | flops 524288 | bytes 3145728 | tf_op jit(solution)/shard_map/convert_element_type | solution.py:123
  36.3 13.2 %while.36 = (s32[]{:T(128)}, f32[16]{0:T(128)S(1)}, f32[16,64,128]{2,1,0:T(8,128)S(1)}, f32[4,16]{1,0:T(4,128)}, f32[4,16,64,128]{3,2,1,0:T(8,128)}, /*index=5*/...) while((s32[]{:T(128)}, f32[16]{0:T(128)S(1)}, ...), condition=%wide.region_3.4_spmd.clone, body=%wide.region_2.3_spmd.clone.sunk | while | flops 524323 | bytes 2622581 | solution.py:131
  36.4 0.8 bitcast_dynamic-update-slice_fusion.2
  37.2 1.2 bitcast_add_fusion.5
  38.4 1.3 dynamic_update_slice.17
  39.6 0.9 bitcast_dynamic-update-slice_fusion.2
  40.5 1.2 bitcast_add_fusion.5
  41.7 1.3 dynamic_update_slice.17
  42.9 0.8 bitcast_dynamic-update-slice_fusion.2
  43.8 1.2 bitcast_add_fusion.5
  44.9 1.3 dynamic_update_slice.17
  46.2 0.9 bitcast_dynamic-update-slice_fusion.2
  47.1 1.2 bitcast_add_fusion.5
  48.2 1.3 dynamic_update_slice.17
  49.7 4.9 %all-reduce.2 = bf16[32]{0:T(256)(128)(2,1)S(1)} all-reduce(bf16[32]{0:T(256)(128)(2,1)S(1)} %dynamic-update-slice.1), channel_id=4, replica_groups=mesh['seq'=2,'head'=4,'exp'=4] {'seq'}, use_global_device_ids=true, to_apply=%add.2 | all-reduce | flops 32 | bytes 128
  54.8 8.0 %all-gather.3 = bf16[32,64,128]{2,1,0:T(8,128)(2,1)S(1)} all-gather(bf16[16,64,128]{2,1,0:T(8,128)(2,1)S(1)} %convert_element_type.134), channel_id=5, replica_groups=mesh['seq'=2,'head'=4,'exp'=4] {'seq'}, dimensions={0}, use_global_device_ids=true | all-gather | bytes 786432 | tf_op jit(solution)/shard_map/all_gather | solution.py:14
  62.8 2.9 %while.37 = (s32[]{:T(128)}, f32[16,64,128]{2,1,0:T(8,128)}, s32[]{:T(128)}, bf16[2,16]{1,0:T(2,128)(2,1)S(1)}, bf16[2,16,64,128]{3,2,1,0:T(8,128)(2,1)S(1)}, /*index=5*/s32[]{:T(128)}, s32[]{:T(128)}) while((s32[]{:T(128)}, f32[16,64,128]{2,1,0:T(8,128)}, s32[]{:T(128)}, bf16[2,16]{1,0:T(2,128)(2,1)S(1)}, ...), condition=%wide.region_5.6_spmd.clone, body=%wide.region_4.5_spmd.clone.sunk | while | flops 655380 | bytes 1310985 | solution.py:31
  62.8 0.9 fusion.83
  63.7 2.0 %fusion.83 = f32[16,64,128]{2,1,0:T(8,128)} fusion(f32[16,64,128]{2,1,0:T(8,128)} %get-tuple-element.358, bf16[2,16,64,128]{3,2,1,0:T(8,128)(2,1)S(1)} %get-tuple-element.368, s32[]{:T(128)} %get-tuple-element.357, f32[16]{0:T(128)S(1)} %exponential_bitcast_fusion.3, pred[]{:T(512)S(6)} %compare.8, pred[]{:T(512)S(6)} %lt.52), kind=kLoop, calls=%fused_computation.10.clone.1 | loop fusion | flops 655360 | bytes 1310790 | tf_op jit(solution)/shard_map/while/body/eval_jaxpr/jit(_where)/select_n | solution.py:29
  66.4 2.7 %fusion.25 = f32[128,16,64]{0,2,1:T(8,128)} fusion(bf16[128,16,128]{2,0,1:T(8,128)(2,1)} %bitcast.151, f32[4,16,64,128]{3,2,1,0:T(8,128)} %get-tuple-element.167, s32[]{:T(128)S(6)} %select_n.54, f32[16,64,128]{2,1,0:T(8,128)} %get-tuple-element.166, f32[16]{0:T(128)S(1)} %exponential_bitcast_fusion.1, f32[128,16]{0,1:T(8,128)} %copy-done.9), kind=kOutput, calls=%fused_computation.33 | convolution fusion | flops 34078720 | bytes 2105412 | tf_op jit(solution)/shard_map/thn,hpn->thp/dot_general | solution.py:142
  69.1 3.8 %multiply_reduce_fusion.1 = (f32[128,16]{0,1:T(8,128)}, f32[128,16,64]{0,2,1:T(8,128)}) fusion(f32[128,16,64]{0,2,1:T(8,128)} %bitcast.162, bf16[128,16,64]{0,2,1:T(8,128)(2,1)S(1)} %bitcast.161, f32[16]{0:T(128)} %param.25, f32[128,16,64]{0,2,1:T(8,128)} %fusion.25, f32[128,16,64]{0,2,1:T(8,128)} %fusion.24, bf16[128,16,128]{2,0,1:T(8,128)(2,1)S(1)} %bitcast.152, ...), kind=kOutput, calls=%fused_computation.49 | convolution fusion | flops 103806976 | bytes 3448896 | tf_op jit(solution)/shard_map/while/body/eval_jaxpr/hts,shp->thp/dot_general | solution.py:48
  73.7 1.3 fusion.36
  75.0 1.8 convolution_convert_fusion.2
  77.5 20.0 %reduce-scatter.2.cloned.1.call-done = bf16[32,1344]{1,0:T(8,128)(2,1)} async-done(((bf16[128,1344]{1,0:T(8,128)(2,1)}), bf16[32,1344]{1,0:T(8,128)(2,1)}) %reduce-scatter.2.cloned.1.call-update) | async-done | bytes 86032 | tf_op jit(solution)/shard_map/reduce_scatter | solution.py:155
  97.4 1.0 fusion.48
  98.5 2.5 %convolution_convert_fusion = bf16[384,1344]{0,1:T(8,128)(2,1)} fusion(bf16[32,384]{1,0:T(8,128)(2,1)S(1)} %fusion.53, f32[1344]{0:T(1024)S(1)} %copy-done.13, f32[32]{0:T(128)S(1)} %add_rsqrt_fusion.1, bf16[32,1344]{1,0:T(8,128)(2,1)} %reduce-scatter.2.cloned.1.call-done, bf16[1,32,1344]{2,1,0:T(8,128)(2,1)S(1)} %copy-done.6), kind=kOutput, calls=%fused_computation.12 | convolution fusion | flops 33890304 | bytes 1234304 | tf_op jit(solution)/shard_map/dot_general | solution.py:180
  100.9 2.4 %copy.111 = bf16[384,1344]{1,0:T(8,128)(2,1)} copy(bf16[384,1344]{0,1:T(8,128)(2,1)} %convolution_convert_fusion) | data formatting | bytes 2064384 | tf_op jit(solution)/shard_map/convert_element_type | solution.py:183
  103.3 32.3 %all_to_all.10 = bf16[16,24,1344]{2,1,0:T(8,128)(2,1)} all-to-all(bf16[16,24,1344]{2,1,0:T(8,128)(2,1)} %bitcast.154), channel_id=1, replica_groups=mesh['seq'=2,'head'=4,'exp'=4] {'head','exp'}, dimensions={0} | all-to-all | bytes 2064384 | tf_op jit(solution)/shard_map/all_to_all | solution.py:185
  135.6 7.0 %convolution_convert_fusion.1 = bf16[384,1344]{0,1:T(8,128)(2,1)} fusion(bf16[1,928,1344]{2,1,0:T(8,128)(2,1)} %param.33, bf16[384,1344]{1,0:T(8,128)(2,1)} %bitcast.157, bf16[1,1344,928]{1,2,0:T(8,128)(2,1)} %param.32), kind=kOutput, calls=%fused_computation.13 | convolution fusion | flops 1917333504 | bytes 7053312 | tf_op jit(solution)/shard_map/dot_general | solution.py:73
  142.6 2.4 %copy.112 = bf16[384,1344]{1,0:T(8,128)(2,1)} copy(bf16[384,1344]{0,1:T(8,128)(2,1)} %convolution_convert_fusion.1) | data formatting | bytes 2064384 | tf_op jit(solution)/shard_map/convert_element_type | solution.py:73
  145.0 4.4 %all-to-all-start.1 = ((bf16[16,24,1344]{2,1,0:T(8,128)(2,1)}), bf16[16,24,1344]{2,1,0:T(8,128)(2,1)}, u32[]{:S(2)}, u32[]{:S(2)}) async-start(bf16[16,24,1344]{2,1,0:T(8,128)(2,1)} %bitcast.153), calls=%async_computation.2 | async-start | bytes 2162688 | tf_op jit(solution)/shard_map/all_to_all | solution.py:189
  149.7 23.2 %all-to-all-done.1 = bf16[16,24,1344]{2,1,0:T(8,128)(2,1)} async-done(((bf16[16,24,1344]{2,1,0:T(8,128)(2,1)}), bf16[16,24,1344]{2,1,0:T(8,128)(2,1)}, u32[]{:S(2)}, u32[]{:S(2)}) %all-to-all-start.1) | async-done | bytes 1032224 | tf_op jit(solution)/shard_map/all_to_all | solution.py:189
  172.9 2.9 %gather_fusion = bf16[192,1344]{1,0:T(8,128)(2,1)S(1)} fusion(bf16[384,1344]{1,0:T(8,128)(2,1)} %bitcast.27, s32[1024]{0:T(1024)S(1)} %pad_clamp_fusion), kind=kCustom, calls=%fused_computation | custom fusion | bytes 1032960 | tf_op jit(solution)/shard_map/gather | solution.py:191
  175.8 1.2 reshape.231
  177.1 1.9 %multiply_reduce_fusion = f32[32,1344]{1,0:T(8,128)S(1)} fusion(f32[32,6,1344]{2,1,0:T(8,128)} %reshape.231, f32[32,6]{1,0:T(8,128)S(1)} %bitcast.163), kind=kLoop, calls=%fused_computation.20 | loop fusion | flops 473088 | bytes 1204992 | tf_op jit(solution)/shard_map/reduce_sum | solution.py:192
  (94 shorter events, 7.9 us)
Async XLA Ops:
  6.5 68.4 %copy-start = (bf16[1024,1344]{0,1:T(8,128)(2,1)S(1)}, bf16[1024,1344]{0,1:T(8,128)(2,1)}, u32[]{:S(2)}) copy-start(bf16[1024,1344]{0,1:T(8,128)(2,1)} %param.27) | copy-start | bytes 8257540
  6.5 7.5 %copy-start.17 = (u32[32]{0:T(128)S(1)}, u32[32]{0:T(128)}, u32[]{:S(2)}) copy-start(u32[32]{0:T(128)} %constant.121) | copy-start | bytes 388
  6.5 17.5 %copy-start.16 = (u32[32]{0:T(128)S(1)}, u32[32]{0:T(128)}, u32[]{:S(2)}) copy-start(u32[32]{0:T(128)} %constant.126) | copy-start | bytes 388
  6.5 21.4 %copy-start.14 = (s32[1,32,6]{1,0,2:T(1,128)S(1)}, s32[1,32,6]{1,0,2:T(1,128)}, u32[]{:S(2)}) copy-start(s32[1,32,6]{1,0,2:T(1,128)} %param.29) | copy-start | bytes 2308
  6.5 24.0 %copy-start.10 = (bf16[128,256]{1,0:T(8,128)(2,1)S(1)}, bf16[128,256]{1,0:T(8,128)(2,1)}, u32[]{:S(2)}) copy-start(bf16[128,256]{1,0:T(8,128)(2,1)} %param.22) | copy-start | bytes 196612
  6.5 27.0 %all-gather.6.cloned.1.call-start = ((), (), s32[]{:S(2)}) async-start(), calls=%async_computation.4 | async-start | bytes 1310720 | tf_op jit(solution)/shard_map/all_gather | solution.py:123
  10.7 3.3 %copy-start.4 = (bf16[128,1024]{0,1:T(8,128)(2,1)}, bf16[128,1024]{0,1:T(8,128)(2,1)S(1)}, u32[]{:S(2)}) copy-start(bf16[128,1024]{0,1:T(8,128)(2,1)S(1)} %copy.102) | copy-start | bytes 786436
  12.1 0.8 copy-start.3
  13.9 83.5 %reduce-scatter.2.cloned.1.call-start = ((), (), s32[]{:S(2)}) async-start(), calls=%async_computation.3 | async-start | bytes 450560 | tf_op jit(solution)/shard_map/reduce_scatter | solution.py:155
  25.3 11.0 %copy-start.9 = (f32[128,16]{0,1:T(8,128)}, f32[128,16]{0,1:T(8,128)S(1)}, u32[]{:S(2)}) copy-start(f32[128,16]{0,1:T(8,128)S(1)} %copy.103) | copy-start | bytes 24580
  28.1 0.6 copy-start.11
  30.6 0.8 copy-start.1
  65.7 3.4 %copy-start.2 = (bf16[128,2,8,128]{3,0,2,1:T(8,128)(2,1)S(1)}, bf16[128,2,8,128]{3,0,2,1:T(8,128)(2,1)}, u32[]{:S(2)}) copy-start(bf16[128,2,8,128]{3,0,2,1:T(8,128)(2,1)} %copy-done.1) | copy-start | bytes 1572868
  65.7 3.4 %copy-start.5 = (bf16[128,1024]{0,1:T(8,128)(2,1)S(1)}, bf16[128,1024]{0,1:T(8,128)(2,1)}, u32[]{:S(2)}) copy-start(bf16[128,1024]{0,1:T(8,128)(2,1)} %copy-done.4) | copy-start | bytes 786436
  73.7 3.1 %copy-start.8 = (s32[16,2,128]{2,0,1:T(8,128)S(1)}, s32[16,2,128]{2,0,1:T(8,128)}, u32[]{:S(2)}) copy-start(s32[16,2,128]{2,0,1:T(8,128)} %reduce-window.6) | copy-start | bytes 49156
  73.7 3.5 %copy-start.12 = (s32[192]{0:T(256)S(1)}, s32[192]{0:T(256)}, u32[]{:S(2)}) copy-start(s32[192]{0:T(256)} %copy-done.11) | copy-start | bytes 2308
  74.9 22.5 %copy-start.6 = (bf16[1,32,1344]{2,1,0:T(8,128)(2,1)S(1)}, bf16[1,32,1344]{2,1,0:T(8,128)(2,1)}, u32[]{:S(2)}) copy-start(bf16[1,32,1344]{2,1,0:T(8,128)(2,1)} %param.28) | copy-start | bytes 258052
  74.9 23.5 %copy-start.13 = (f32[1344]{0:T(1024)S(1)}, f32[1344]{0:T(1024)}, u32[]{:S(2)}) copy-start(f32[1344]{0:T(1024)} %param.31) | copy-start | bytes 16132
  142.6 7.0 %copy-start.15 = (f32[1,32,6]{1,0,2:T(1,128)S(1)}, f32[1,32,6]{1,0,2:T(1,128)}, u32[]{:S(2)}) copy-start(f32[1,32,6]{1,0,2:T(1,128)} %param.30) | copy-start | bytes 2308
  145.0 27.9 %all-to-all-start.1 = ((bf16[16,24,1344]{2,1,0:T(8,128)(2,1)}), bf16[16,24,1344]{2,1,0:T(8,128)(2,1)}, u32[]{:S(2)}, u32[]{:S(2)}) async-start(bf16[16,24,1344]{2,1,0:T(8,128)(2,1)} %bitcast.153), calls=%async_computation.2 | async-start | bytes 2162688 | tf_op jit(solution)/shard_map/all_to_all | solution.py:189
  175.8 3.1 %copy-start.7 = (bf16[32,1344]{1,0:T(8,128)(2,1)S(1)}, bf16[32,1344]{1,0:T(8,128)(2,1)}, u32[]{:S(2)}) copy-start(bf16[32,1344]{1,0:T(8,128)(2,1)} %reduce-scatter.2.cloned.1.call-done) | copy-start | bytes 258052
Sparse Core Ops, SparseCore 0:
  14.1 19.4 all-gather.5
  76.9 20.4 reduce-scatter.1
where the time goes:
time: 189 us; the launch traced here: 186 us
  blocking collectives  53.6 us (28%)
  waiting for transfers between devices  44 us (23%)
  local copies, waits for them, and re-layouts  25.4 us (13%)
  other arithmetic  24 us (13%)
  matrix products  20 us (11%)
  between operations  15.1 us (8%)
  starting transfers between devices  4.46 us (2%)
    all_to_all x1, blocking collectives, per_device(): lax.all_to_all(outbound, ('head', 'exp'), split_axis=0, concat_axis=0, ti...  32.3 us
    all_to_all x1, waiting for transfers between devices, per_device(): lax.all_to_all(produced, ('head', 'exp'), split_axis=0, concat_axis=0, ti...  23.2 us
    reduce_scatter x1, waiting for transfers between devices, per_device(): lax.psum_scatter(jnp.dot(normed, w_out, preferred_element_type=jnp.float3...  20 us
    unnamed x2, blocking collectives  13.3 us
    all_gather x1, blocking collectives, prefix(): lax.all_gather(part.astype(kind), axis)  7.97 us
    dot_general x1, matrix products, expert_rows(): jnp.dot(activated, w_down[0], preferred_element_type=jnp.float32)  6.97 us
    unnamed x44, local copies, waits for them, and re-layouts  5.1 us
    dynamic_update_slice x4, local copies, waits for them, and re-layouts, per_device(): lax.scan(walk, (zero_decay, zero_state), (group_decays, group_states))  5.09 us
  transfers between devices with their start and end apart: 3, of which 3 were waited for; matrix products, arithmetic and copies ran while one was open for 5% of the time, Pallas kernels for 0%

commit v1 on v0

v1 whole, which is shorter than its diff:
```python
import functools

import jax
import jax.numpy as jnp
from jax import lax
from jax.experimental import pallas as pl
from jax.experimental.pallas import tpu as pltpu
from jax.sharding import PartitionSpec as P

HEAD_DIM = 64
STATE = 128
LANES = 128
TILE = 16
FAR = -1e30
F32 = jnp.float32
BF16 = jnp.bfloat16


def call(kernel, outs, name, megabytes=16):
    return pl.pallas_call(
        kernel,
        out_shape=outs,
        name=name,
        compiler_params=pltpu.CompilerParams(vmem_limit_bytes=megabytes << 20),
    )


def struct(shape, dtype):
    return jax.ShapeDtypeStruct(shape, dtype)


def decays(dt, a_log):
    step = jnp.maximum(dt, 0.0) + jnp.log1p(jnp.exp(-jnp.abs(dt)))
    rate = -step * jnp.exp(a_log)
    length = dt.shape[0]
    row = lax.broadcasted_iota(jnp.int32, (length, length), 0)
    col = lax.broadcasted_iota(jnp.int32, (length, length), 1)
    lower = (row >= col).astype(F32)
    cum = jnp.dot(lower, rate, precision=lax.Precision.HIGHEST, preferred_element_type=F32)
    return step, cum


def pair_lanes(values, pair):
    rows = values.shape[0]
    lane = lax.broadcasted_iota(jnp.int32, (rows, LANES), 1)
    left = jnp.broadcast_to(values[:, 2 * pair : 2 * pair + 1], (rows, LANES))
    right = jnp.broadcast_to(values[:, 2 * pair + 1 : 2 * pair + 2], (rows, LANES))
    return jnp.where(lane < HEAD_DIM, left, right)


def state_kernel(x_ref, b_ref, dt_ref, a_ref, packed_ref):
    step, cum = decays(dt_ref[...], a_ref[...])
    total = cum[-1:, :]
    tail = jnp.exp(total - cum) * step
    pairs = packed_ref.shape[0]
    groups = b_ref.shape[1] // STATE
    for pair in range(pairs):
        group = pair * groups // pairs
        x_pair = x_ref[:, pair * LANES : (pair + 1) * LANES].astype(F32)
        weighted = (pair_lanes(tail, pair) * x_pair).astype(BF16)
        b_group = b_ref[:, group * STATE : (group + 1) * STATE]
        state = lax.dot_general(
            b_group, weighted, (((0,), (0,)), ((), ())), preferred_element_type=F32
        )
        packed_ref[pair, 0:STATE, :] = state.astype(BF16)
        wide = jnp.broadcast_to(pair_lanes(total, pair), (TILE, LANES))
        high = wide.astype(BF16).astype(F32)
        row = lax.broadcasted_iota(jnp.int32, (TILE, LANES), 0)
        packed_ref[pair, STATE : STATE + TILE, :] = jnp.where(row == 0, high, wide - high).astype(BF16)


def inside_kernel(x_ref, b_ref, c_ref, dt_ref, a_ref, d_ref, out_ref):
    step, cum = decays(dt_ref[...], a_ref[...])
    cum_rows, step_rows = cum.T, step.T
    length = dt_ref.shape[0]
    pairs = x_ref.shape[1] // LANES
    groups = b_ref.shape[1] // STATE
    row = lax.broadcasted_iota(jnp.int32, (length, length), 0)
    col = lax.broadcasted_iota(jnp.int32, (length, length), 1)
    lane = lax.broadcasted_iota(jnp.int32, (length, LANES), 1)
    for group in range(groups):
        span = slice(group * STATE, (group + 1) * STATE)
        scores = lax.dot_general(
            c_ref[:, span], b_ref[:, span], (((1,), (1,)), ((), ())), preferred_element_type=F32
        )
        scores = jnp.where(row >= col, scores, 0.0)
        for pair in range(group * pairs // groups, (group + 1) * pairs // groups):
            x_pair = x_ref[:, pair * LANES : (pair + 1) * LANES]
            halves = []
            for head in (2 * pair, 2 * pair + 1):
                distance = cum[:, head : head + 1] - cum_rows[head : head + 1, :]
                decay = jnp.exp(jnp.where(row >= col, distance, FAR))
                mixing = (scores * (decay * step_rows[head : head + 1, :])).astype(BF16)
                halves.append(jnp.dot(mixing, x_pair, preferred_element_type=F32))
            inside = jnp.where(lane < HEAD_DIM, halves[0], halves[1])
            skip = pair_lanes(d_ref[...], pair) * x_pair.astype(F32)
            out_ref[:, pair * LANES : (pair + 1) * LANES] = inside + skip


def chain_kernel(packed_ref, out_ref):
    carry = jnp.zeros(packed_ref.shape[1:2] + (STATE, LANES), F32)
    for shard in range(packed_ref.shape[0]):
        out_ref[shard] = carry.astype(BF16)
        if shard < packed_ref.shape[0] - 1:
            block = packed_ref[shard].astype(F32)
            total = block[:, STATE : STATE + 1, :] + block[:, STATE + 1 : STATE + 2, :]
            carry = jnp.exp(total) * carry + block[:, 0:STATE, :]


def states_before(packed):
    pairs = packed.shape[0]
    seq, exp = lax.axis_size("seq"), lax.axis_size("exp")
    axes = ("seq", "exp") if pairs % (seq * exp) == 0 else ("exp",)
    shards = seq * exp if len(axes) == 2 else exp
    here = pairs // shards
    got = lax.all_to_all(packed, axes, split_axis=0, concat_axis=0, tiled=True)
    got = got.reshape(shards, here, STATE + TILE, LANES)
    if len(axes) == 2:
        before = call(chain_kernel, struct((shards, here, STATE, LANES), BF16), "chain")(got)
    else:
        block = got.astype(F32)
        totals, states = block[:, :, STATE : STATE + 1] + block[:, :, STATE + 1 : STATE + 2], block[:, :, :STATE]

        def walk(carry, item):
            return (carry[0] + item[0], jnp.exp(item[0]) * carry[1] + item[1]), carry

        zero = (jnp.zeros(totals.shape[1:], F32), jnp.zeros(states.shape[1:], F32))
        span, inner = lax.scan(walk, zero, (totals, states))
        everything = jax.tree.map(lambda part: lax.all_gather(part.astype(BF16), "seq").astype(F32), span)
        unused, outer = lax.scan(walk, zero, everything)
        chain = lax.dynamic_index_in_dim(outer[1], lax.axis_index("seq"), 0, keepdims=False)
        before = (jnp.exp(inner[0]) * chain[None] + inner[1]).astype(BF16)
    before = before.reshape(pairs, STATE, LANES)
    return lax.all_to_all(before, axes, split_axis=0, concat_axis=0, tiled=True)


def mixed_kernel(place_ref, local_ref, z_ref, c_ref, dt_ref, a_ref, norm_ref, before_ref, w_ref, *rest):
    outs, normed_ref = rest[:-1], rest[-1]
    step, cum = decays(dt_ref[...], a_ref[...])
    grown = jnp.exp(cum)
    pairs = before_ref.shape[0]
    groups = c_ref.shape[1] // STATE
    per_group = pairs // groups
    for group in range(groups):
        c_group = c_ref[:, group * STATE : (group + 1) * STATE]
        gated, squares = [], 0.0
        for pair in range(group * per_group, (group + 1) * per_group):
            span = slice(pair * LANES, (pair + 1) * LANES)
            carried = jnp.dot(c_group, before_ref[pair], preferred_element_type=F32)
            out = local_ref[:, span] + pair_lanes(grown, pair) * carried
            z = z_ref[:, span].astype(F32)
            value = out * (z / (1.0 + jnp.exp(-z)))
            gated.append(value)
            squares = squares + value * value
        mean = jnp.sum(squares, axis=1, keepdims=True) / (per_group * LANES)
        inverse = lax.rsqrt(mean + 1e-05)
        for offset, value in enumerate(gated):
            pair = group * per_group + offset
            span = slice(pair * LANES, (pair + 1) * LANES)
            normed_ref[:, span] = (value * inverse * norm_ref[:, span]).astype(BF16)
    count, rows = len(outs), outs[0].shape[0]
    blocks = []
    for shift in range(count):
        owner = lax.rem(place_ref[0] - shift + count, count)
        blocks.append(normed_ref[pl.ds(pl.multiple_of(owner * rows, rows), rows), :])
    product = jnp.dot(jnp.concatenate(blocks, axis=0), w_ref[...], preferred_element_type=F32)
    for shift in range(count):
        outs[shift][...] = product[shift * rows : (shift + 1) * rows].astype(BF16)


def rows_kernel(experts, resid_ref, routes_ref, gates_ref, gain_ref, *rest):
    parts, hidden_ref, rows_ref = rest[:-2], rest[-2], rest[-1]
    mixed = parts[0][...].astype(F32)
    for part in parts[1:]:
        mixed = mixed + part[...].astype(F32)
    hidden = (resid_ref[0].astype(F32) + mixed).astype(BF16)
    hidden_ref[...] = hidden
    value = hidden.astype(F32)
    scale = lax.rsqrt(jnp.mean(value * value, axis=1, keepdims=True) + 1e-05)
    width = value.shape[1]
    start = width // LANES * LANES
    extent = rows_ref.shape[1] - start
    count = value.shape[0]
    lane = lax.broadcasted_iota(jnp.int32, (count, extent), 1) + start - width
    expert = jnp.where(lane >= experts, lane - experts, lane)
    gate = jnp.zeros((count, extent), F32)
    for pick in range(routes_ref.shape[2]):
        same = routes_ref[0, :, pick : pick + 1] == expert
        gate = gate + jnp.where(same, gates_ref[0, :, pick : pick + 1], 0.0)
    high = gate.astype(BF16).astype(F32)
    gate = jnp.where(lane < experts, high, jnp.where(lane < 2 * experts, gate - high, 0.0))
    rows_ref[:, start:] = gate.astype(BF16)
    rows_ref[:, :width] = (value * scale * gain_ref[...]).astype(BF16)


def expert_kernel(experts, place_ref, rows_ref, up_ref, down_ref, near_ref, far_ref):
    width = up_ref.shape[1]
    start = width // LANES * LANES
    up = jnp.dot(rows_ref[:, :width], up_ref[0], preferred_element_type=F32)
    up = jnp.maximum(up, 0.0)
    activated = (up * up).astype(BF16)
    tail = rows_ref[:, start:].astype(F32)
    lane = lax.broadcasted_iota(jnp.int32, tail.shape, 1) + start - width
    mine = (lane == place_ref[1]) | (lane == place_ref[1] + experts)
    gate = jnp.sum(jnp.where(mine, tail, 0.0), axis=1, keepdims=True)
    out = jnp.dot(activated, down_ref[0], preferred_element_type=F32) * gate
    half = near_ref.shape[0]
    near_ref[...] = out[:half].astype(BF16)
    far_ref[...] = out[half:].astype(BF16)


def sum_kernel(kept_ref, got_ref, *outs):
    total = kept_ref[...].astype(F32) + got_ref[...].astype(F32)
    at = 0
    for out in outs:
        out[...] = total[at : at + out.shape[0]].astype(BF16)
        at += out.shape[0]


def last_kernel(hidden_ref, *rest):
    parts, out_ref = rest[:-1], rest[-1]
    total = parts[0][...].astype(F32)
    for part in parts[1:]:
        total = total + part[...].astype(F32)
    out_ref[0] = (hidden_ref[...].astype(F32) + total).astype(BF16)


def moved(value, axis, target):
    size = lax.axis_size(axis)
    return lax.ppermute(value, axis, [(i, target(i, size)) for i in range(size)])


def along_head(shift):
    return lambda i, size: (i + shift) % size


def along_chips(shift):
    return lambda i, size: (i // 2 + shift) % (size // 2) * 2 + i % 2


def partner(i, size):
    return i ^ 1


def per_device(
    x_in, z_in, b_in, c_in, dt_in, a_log, d_skip, norm_w, w_out, resid, routes, gates, moe_gain, w_up, w_down
):
    length, heads = dt_in.shape
    channels = x_in.shape[1]
    model = w_out.shape[1]
    head_size, exp_size = lax.axis_size("head"), lax.axis_size("exp")
    chips = exp_size // 2
    rows = resid.shape[1]
    experts = head_size * exp_size
    place = jnp.stack(
        [lax.axis_index("head"), lax.axis_index("head") * exp_size + lax.axis_index("exp")]
    ).astype(jnp.int32)
    a_row, d_row = a_log[None], d_skip[None]
    pairs = channels // LANES
    packed = call(state_kernel, struct((pairs, STATE + TILE, LANES), BF16), "state")(x_in, b_in, dt_in, a_row)
    local = call(inside_kernel, struct((length, channels), F32), "inside")(x_in, b_in, c_in, dt_in, a_row, d_row)
    before = states_before(packed)
    smem = pl.BlockSpec(memory_space=pltpu.SMEM)
    vmem = pl.BlockSpec(memory_space=pltpu.VMEM)
    mixed = pl.pallas_call(
        mixed_kernel,
        out_shape=[struct((rows, model), BF16)] * head_size,
        in_specs=[smem] + [vmem] * 8,
        scratch_shapes=[pltpu.VMEM((length, channels), BF16)],
        compiler_params=pltpu.CompilerParams(vmem_limit_bytes=24 << 20),
        name="mixed",
    )(place, local, z_in, c_in, dt_in, a_row, norm_w[None], before, w_out)
    parts = [mixed[0]] + [moved(mixed[s], "head", along_head(-s)) for s in range(1, head_size)]
    wide = -(-(model + 2 * experts) // LANES) * LANES
    hidden, own = call(
        functools.partial(rows_kernel, experts),
        [struct((rows, model), BF16), struct((rows, wide), BF16)],
        "rows",
    )(resid, routes, gates, moe_gain[None], *parts)
    by_head = jnp.concatenate([own] + [moved(own, "head", along_head(s)) for s in range(1, head_size)], axis=0)
    by_chip = jnp.concatenate(
        [by_head] + [moved(by_head, "exp", along_chips(s)) for s in range(1, chips)], axis=0
    )
    everything = jnp.concatenate([by_chip, moved(by_chip, "exp", partner)], axis=0)
    half = by_chip.shape[0]
    near, far = pl.pallas_call(
        functools.partial(expert_kernel, experts),
        out_shape=[struct((half, model), BF16)] * 2,
        in_specs=[smem] + [vmem] * 3,
        compiler_params=pltpu.CompilerParams(vmem_limit_bytes=32 << 20),
        name="experts",
    )(place, everything, w_up, w_down)
    quarter = half // chips
    sums = call(sum_kernel, [struct((quarter, model), BF16)] * chips, "sum")(near, moved(far, "exp", partner))
    kept = sums[0]
    for s in range(1, chips):
        got = moved(sums[s], "exp", along_chips(-s))
        count = head_size if s == chips - 1 else 1
        kept = call(sum_kernel, [struct((quarter // count, model), BF16)] * count, "sum")(kept, got)
        kept = kept[0] if count == 1 else kept
    back = [kept[0]] + [moved(kept[s], "head", along_head(-s)) for s in range(1, head_size)]
    return call(last_kernel, struct(resid.shape, BF16), "last")(hidden, *back)


def solution(mesh):
    placed = (
        P(("seq", "exp"), "head"),
        P(("seq", "exp"), "head"),
        P(("seq", "exp"), "head"),
        P(("seq", "exp"), "head"),
        P(("seq", "exp"), "head"),
        P("head"),
        P("head"),
        P("head"),
        P("head", None),
        P(("seq", "exp"), "head", None),
        P(("seq", "exp"), "head", None),
        P(("seq", "exp"), "head", None),
        P(),
        P(("head", "exp"), None, None),
        P(("head", "exp"), None, None),
    )
    return jax.shard_map(
        per_device,
        mesh=mesh,
        in_specs=placed,
        out_specs=P(("seq", "exp"), "head", None),
        check_vma=False,
    )
```

time: 189 us -> 108 us (0.57); the launches traced: 186 us -> 108 us
  blocking collectives: 53.6 us -> 12.2 us
  other arithmetic: 24 us -> 0.11 us
  matrix products: 20 us -> 0 us
  starting transfers between devices: 4.46 us -> 21.7 us
  between operations: 15.1 us -> 0.21 us
  Pallas kernels: 0 us -> 10.7 us
  waiting for transfers between devices: 44 us -> 35 us
  local copies, waits for them, and re-layouts: 25.4 us -> 27.6 us
    ppermute x0 -> x13, waiting for transfers between devices: none -> 35 us  [moved(): lax.ppermute(value, axis, [(i, target(i, size)) for i in range(size)])]
    all_to_all x1, waiting for transfers between devices: 23.2 us -> 0.01 us  [states_before(): return lax.all_to_all(before, axes, split_axis=0, concat_axis=0, tiled=True)]
    all_to_all x1, blocking collectives: 32.3 us -> 12.2 us  [states_before(): got = lax.all_to_all(packed, axes, split_axis=0, concat_axis=0, tiled=True)]
    dot_general x7 -> x0, matrix products: 20 us -> none  [the longest x1 6.97 us: expert_rows(): jnp.dot(activated, w_down[0], preferred_element_type=jnp.float32)]
    reduce_scatter x1 -> x0, waiting for transfers between devices: 20 us -> none  [per_device(): lax.psum_scatter(jnp.dot(normed, w_out, preferred_element_type=jnp.float3...]
    unnamed x44 -> x49, local copies, waits for them, and re-layouts: 5.1 us -> 23.5 us
    ppermute x0 -> x13, starting transfers between devices: none -> 17.6 us  [moved(): lax.ppermute(value, axis, [(i, target(i, size)) for i in range(size)])]
    unnamed x2 -> x0, blocking collectives: 13.3 us -> none
  transfers between devices with their start and end apart: 3 -> 14, of which waited for: 3 -> 9; matrix products, arithmetic and copies ran while one was open for 5% -> 10% of each run, Pallas kernels for 0% -> 1%
where the time goes in v1:
time: 108 us
  waiting for transfers between devices  35 us (32%)
  local copies, waits for them, and re-layouts  27.6 us (26%)
  starting transfers between devices  21.7 us (20%)
  blocking collectives  12.2 us (11%)
  Pallas kernels  10.7 us (10%)
    ppermute x13, waiting for transfers between devices, moved(): lax.ppermute(value, axis, [(i, target(i, size)) for i in range(size)])  35 us
    unnamed x49, local copies, waits for them, and re-layouts  23.5 us
    ppermute x13, starting transfers between devices, moved(): lax.ppermute(value, axis, [(i, target(i, size)) for i in range(size)])  17.6 us
    all_to_all x1, blocking collectives, states_before(): got = lax.all_to_all(packed, axes, split_axis=0, concat_axis=0, tiled=True)  12.2 us
    all_to_all x1, starting transfers between devices, states_before(): return lax.all_to_all(before, axes, split_axis=0, concat_axis=0, tiled=True)  4.05 us
    pallas_call x1, Pallas kernels, per_device(): pl.pallas_call(functools.partial(expert_kernel, experts), out_shape=[stru...  3.97 us
    pallas_call x1, Pallas kernels, per_device(): pl.pallas_call(mixed_kernel, out_shape=[struct((rows, model), BF16)] * he...  3.03 us
  transfers between devices with their start and end apart: 14, of which 9 were waited for; matrix products, arithmetic and copies ran while one was open for 10% of the time, Pallas kernels for 1%

profile of v1, /device:TPU:0, one launch (start us, length us, event | category | flops | bytes accessed | tf_op | source)
XLA Modules:
  0.0 107.6 jit_solution(10111549783637334775)
XLA Ops:
  0.0 0.8 copy.23.dt_ref
  0.8 0.9 copy-done.3
  1.8 0.8 copy-done.7
  2.6 0.7 copy-done.15
  3.2 0.8 state.1
  4.1 12.2 %all_to_all.10 = bf16[8,144,128]{2,1,0:T(8,128)(2,1)S(1)} all-to-all(bf16[8,144,128]{2,1,0:T(8,128)(2,1)S(1)} %state.1), channel_id=1, replica_groups=mesh['seq'=2,'head'=4,'exp'=4] {'seq','exp'}, dimensions={0} | all-to-all | bytes 589824 | tf_op jit(solution)/shard_map/all_to_all | solution.py:116
  16.3 0.8 chain.1
  17.1 4.1 %all-to-all-start.1 = ((bf16[8,128,128]{2,1,0:T(8,128)(2,1)}), bf16[8,128,128]{2,1,0:T(8,128)(2,1)}, u32[]{:S(2)}, u32[]{:S(2)}) async-start(bf16[8,128,128]{2,1,0:T(8,128)(2,1)} %bitcast.6), calls=%async_computation.1 | async-start | bytes 524288 | tf_op jit(solution)/shard_map/all_to_all | solution.py:134
  21.2 3.3 %copy.26.w_ref = bf16[1024,1344]{1,0:T(8,128)(2,1)S(1)} copy(bf16[1024,1344]{0,1:T(8,128)(2,1)} %param.23) | data formatting | bytes 5505024 | tf_op args[8]
  24.6 0.9 copy-done.4
  25.5 0.8 copy-done.8
  26.3 0.9 inside.1.local_ref
  27.4 0.9 copy-done.9
  28.3 3.0 %mixed.1 = (bf16[32,1344]{1,0:T(8,128)(2,1)S(1)}, bf16[32,1344]{1,0:T(8,128)(2,1)}, bf16[32,1344]{1,0:T(8,128)(2,1)}, bf16[32,1344]{1,0:T(8,128)(2,1)}) custom-call(s32[2]{0:T(128)S(1)} %pad_add_fusion.place_ref, f32[128,1024]{1,0:T(8,128)S(1)} %inside.1.local_ref, bf16[128,1024]{1,0:T(8,128)(2,1)S(1)} %copy-done.9, bf16[128,256]{1,0:T(8,128)(2,1)S(1)} %copy-done.6, ...), custom_call_target="tpu_custom_call" | custom-call | tf_op jit(solution)/shard_map/mixed/pallas_call | solution.py:265
  32.0 3.6 %collective-permute-start = (bf16[32,1344]{1,0:T(8,128)(2,1)}, bf16[32,1344]{1,0:T(8,128)(2,1)S(1)}, u32[]{:S(2)}, u32[]{:S(2)}) collective-permute-start(bf16[32,1344]{1,0:T(8,128)(2,1)} %get-tuple-element.20), channel_id=1, source_target_pairs={{0,12},{4,0},{8,4},{12,8},{1,13},{5,1},{9,5},{13,9},{2,14},{6,2},{... | collective-permute-start | bytes 258056 | tf_op jit(solution)/shard_map/ppermute | solution.py:230
  35.6 1.0 collective-permute-start.2
  36.7 0.8 copy.28.gates_ref
  37.5 0.7 broadcast_in_dim.12.gain_ref
  38.2 0.7 collective-permute-done.rest_1_
  38.9 5.8 %collective-permute-done.1.rest_2_ = bf16[32,1344]{1,0:T(8,128)(2,1)S(1)} collective-permute-done((bf16[32,1344]{1,0:T(8,128)(2,1)}, bf16[32,1344]{1,0:T(8,128)(2,1)S(1)}, u32[]{:S(2)}, u32[]{:S(2)}) %collective-permute-start.1) | collective-permute-done | bytes 86048 | tf_op jit(solution)/shard_map/ppermute | solution.py:230
  44.8 0.9 copy-done.10
  45.6 0.9 copy-done.14
  46.9 2.1 %collective-permute-start.4 = (bf16[32,1408]{1,0:T(8,128)(2,1)S(1)}, bf16[32,1408]{1,0:T(8,128)(2,1)S(1)}, u32[]{:S(2)}, u32[]{:S(2)}) collective-permute-start(bf16[32,1408]{1,0:T(8,128)(2,1)S(1)} %get-tuple-element.24), channel_id=1, source_target_pairs={{0,8},{4,12},{8,0},{12,4},{1,9},{5,13},{9,1},{13,5},{2,10},{6,14},... | collective-permute-start | bytes 270344 | tf_op jit(solution)/shard_map/ppermute | solution.py:230
  49.1 2.6 %collective-permute-start.5 = (bf16[32,1408]{1,0:T(8,128)(2,1)S(1)}, bf16[32,1408]{1,0:T(8,128)(2,1)S(1)}, u32[]{:S(2)}, u32[]{:S(2)}) collective-permute-start(bf16[32,1408]{1,0:T(8,128)(2,1)S(1)} %get-tuple-element.24), channel_id=1, source_target_pairs={{0,12},{4,0},{8,4},{12,8},{1,13},{5,1},{9,5},{13,9},{2,14},{6,2},{... | collective-permute-start | bytes 270344 | tf_op jit(solution)/shard_map/ppermute | solution.py:230
  51.6 0.6 constant_dynamic-update-slice_fusion.4
  52.3 1.9 %collective-permute-done.3 = bf16[32,1408]{1,0:T(8,128)(2,1)S(1)} collective-permute-done((bf16[32,1408]{1,0:T(8,128)(2,1)S(1)}, bf16[32,1408]{1,0:T(8,128)(2,1)S(1)}, u32[]{:S(2)}, u32[]{:S(2)}) %collective-permute-start.3) | collective-permute-done | bytes 90144 | tf_op jit(solution)/shard_map/ppermute | solution.py:230
  54.1 2.8 %collective-permute-done.4 = bf16[32,1408]{1,0:T(8,128)(2,1)S(1)} collective-permute-done((bf16[32,1408]{1,0:T(8,128)(2,1)S(1)}, bf16[32,1408]{1,0:T(8,128)(2,1)S(1)}, u32[]{:S(2)}, u32[]{:S(2)}) %collective-permute-start.4) | collective-permute-done | bytes 90144 | tf_op jit(solution)/shard_map/ppermute | solution.py:230
  57.0 1.5 %collective-permute-start.6 = (bf16[128,1408]{1,0:T(8,128)(2,1)S(1)}, bf16[128,1408]{1,0:T(8,128)(2,1)S(1)}, u32[]{:S(2)}, u32[]{:S(2)}) collective-permute-start(bf16[128,1408]{1,0:T(8,128)(2,1)S(1)} %pad_maximum_fusion), channel_id=1, source_target_pairs={{0,2},{1,3},{2,0},{3,1},{4,6},{5,7},{6,4},{7,5},{8,10},{9,11},{10,... | collective-permute-start | bytes 1081352 | tf_op jit(solution)/shard_map/ppermute | solution.py:230
  58.5 0.6 constant_dynamic-update-slice_fusion.3
  59.2 0.6 constant_dynamic-update-slice_fusion.2
  59.8 0.6 constant_dynamic-update-slice_fusion.1
  60.5 4.9 %collective-permute-done.6 = bf16[128,1408]{1,0:T(8,128)(2,1)S(1)} collective-permute-done((bf16[128,1408]{1,0:T(8,128)(2,1)S(1)}, bf16[128,1408]{1,0:T(8,128)(2,1)S(1)}, u32[]{:S(2)}, u32[]{:S(2)}) %collective-permute-start.6) | collective-permute-done | bytes 360480 | tf_op jit(solution)/shard_map/ppermute | solution.py:230
  65.4 0.8 constant_dynamic-update-slice_fusion
  66.2 1.1 %copy-done.1 = bf16[512,1408]{1,0:T(8,128)(2,1)} copy-done((bf16[512,1408]{1,0:T(8,128)(2,1)}, bf16[512,1408]{1,0:T(8,128)(2,1)S(1)}, u32[]{:S(2)}) %copy-start.1) | copy-done | bytes 1441816
  67.4 3.3 %copy.29.up_ref = bf16[1,1344,928]{2,1,0:T(8,128)(2,1)S(1)} copy(bf16[1,1344,928]{1,2,0:T(8,128)(2,1)} %param.28) | data formatting | bytes 4988928 | tf_op args[13]
  70.6 0.9 constant_dynamic-update-slice_fusion.5.rows_ref
  71.6 1.7 %copy-done = bf16[1,928,1344]{2,1,0:T(8,128)(2,1)S(1)} copy-done((bf16[1,928,1344]{2,1,0:T(8,128)(2,1)S(1)}, bf16[1,928,1344]{2,1,0:T(8,128)(2,1)}, u32[]{:S(2)}) %copy-start) | copy-done | bytes 2494488
  73.3 1.4 %copy-done.2 = bf16[512,1408]{1,0:T(8,128)(2,1)S(1)} copy-done((bf16[512,1408]{1,0:T(8,128)(2,1)S(1)}, bf16[512,1408]{1,0:T(8,128)(2,1)}, u32[]{:S(2)}) %copy-start.2) | copy-done | bytes 1441816
  74.7 4.0 %experts.1 = (bf16[256,1344]{1,0:T(8,128)(2,1)S(1)}, bf16[256,1344]{1,0:T(8,128)(2,1)S(1)}) custom-call(s32[2]{0:T(128)S(1)} %pad_add_fusion.place_ref, bf16[512,1408]{1,0:T(8,128)(2,1)S(1)} %copy-done.2, bf16[1,1344,928]{2,1,0:T(8,128)(2,1)S(1)} %copy.29.up_ref, bf16[1,928,1344]{2,1,0:T(8,128)(2,1)S(1)} %copy-done), custom_call_target="tpu_custom_call" | custom-call | tf_op jit(solution)/shard_map/experts/pallas_call | solution.py:286
  78.6 0.9 copy-done.5
  79.5 1.4 %copy.30 = bf16[256,1344]{0,1:T(8,128)(2,1)S(1)} copy(bf16[256,1344]{1,0:T(8,128)(2,1)} %copy-done.5) | data formatting | bytes 1376256 | tf_op jit(solution)/shard_map/experts/pallas_call | solution.py:286
  81.4 1.8 %collective-permute-done.8 = bf16[256,1344]{0,1:T(8,128)(2,1)S(1)} collective-permute-done((bf16[256,1344]{0,1:T(8,128)(2,1)S(1)}, bf16[256,1344]{0,1:T(8,128)(2,1)S(1)}, u32[]{:S(2)}, u32[]{:S(2)}) %collective-permute-start.8) | collective-permute-done | bytes 688160 | tf_op jit(solution)/shard_map/ppermute | solution.py:230
  83.7 1.3 %collective-permute-start.9 = (bf16[128,1344]{1,0:T(8,128)(2,1)S(1)}, bf16[128,1344]{1,0:T(8,128)(2,1)S(1)}, u32[]{:S(2)}, u32[]{:S(2)}) collective-permute-start(bf16[128,1344]{1,0:T(8,128)(2,1)S(1)} %get-tuple-element.28), channel_id=1, source_target_pairs={{0,2},{1,3},{2,0},{3,1},{4,6},{5,7},{6,4},{7,5},{8,10},{9,11},{10,... | collective-permute-start | bytes 1032200 | tf_op jit(solution)/shard_map/ppermute | solution.py:230
  85.0 9.5 %collective-permute-done.9.got_ref = bf16[128,1344]{1,0:T(8,128)(2,1)S(1)} collective-permute-done((bf16[128,1344]{1,0:T(8,128)(2,1)S(1)}, bf16[128,1344]{1,0:T(8,128)(2,1)S(1)}, u32[]{:S(2)}, u32[]{:S(2)}) %collective-permute-start.9) | collective-permute-done | bytes 344096 | tf_op jit(solution)/shard_map/ppermute | solution.py:230
  94.6 4.1 %collective-permute-start.10 = (bf16[32,1344]{1,0:T(8,128)(2,1)S(1)}, bf16[32,1344]{1,0:T(8,128)(2,1)S(1)}, u32[]{:S(2)}, u32[]{:S(2)}) collective-permute-start(bf16[32,1344]{1,0:T(8,128)(2,1)S(1)} %get-tuple-element.30), channel_id=1, source_target_pairs={{0,12},{4,0},{8,4},{12,8},{1,13},{5,1},{9,5},{13,9},{2,14},{6,2},{... | collective-permute-start | bytes 258056 | tf_op jit(solution)/shard_map/ppermute | solution.py:230
  99.3 2.4 %collective-permute-done.10.rest_1_ = bf16[32,1344]{1,0:T(8,128)(2,1)S(1)} collective-permute-done((bf16[32,1344]{1,0:T(8,128)(2,1)S(1)}, bf16[32,1344]{1,0:T(8,128)(2,1)S(1)}, u32[]{:S(2)}, u32[]{:S(2)}) %collective-permute-start.10) | collective-permute-done | bytes 86048 | tf_op jit(solution)/shard_map/ppermute | solution.py:230
  101.7 5.1 %collective-permute-done.11.rest_2_ = bf16[32,1344]{1,0:T(8,128)(2,1)S(1)} collective-permute-done((bf16[32,1344]{1,0:T(8,128)(2,1)S(1)}, bf16[32,1344]{1,0:T(8,128)(2,1)S(1)}, u32[]{:S(2)}, u32[]{:S(2)}) %collective-permute-start.11) | collective-permute-done | bytes 86048 | tf_op jit(solution)/shard_map/ppermute | solution.py:230
  106.9 0.7 last.1
  (46 shorter events, 3.1 us)
Async XLA Ops:
  0.8 1.0 copy-start.3
  1.7 0.8 copy-start.7
  2.6 0.7 copy-start.15
  17.1 10.3 %all-to-all-start.1 = ((bf16[8,128,128]{2,1,0:T(8,128)(2,1)}), bf16[8,128,128]{2,1,0:T(8,128)(2,1)}, u32[]{:S(2)}, u32[]{:S(2)}) async-start(bf16[8,128,128]{2,1,0:T(8,128)(2,1)} %bitcast.6), calls=%async_computation.1 | async-start | bytes 524288 | tf_op jit(solution)/shard_map/all_to_all | solution.py:134
  21.1 3.4 %copy-start.6 = (bf16[128,256]{1,0:T(8,128)(2,1)S(1)}, bf16[128,256]{1,0:T(8,128)(2,1)}, u32[]{:S(2)}) copy-start(bf16[128,256]{1,0:T(8,128)(2,1)} %c_ref.3) | copy-start | bytes 196612
  21.1 3.4 %copy-start.16 = (f32[16]{0:T(128)S(1)}, f32[16]{0:T(128)}, u32[]{:S(2)}) copy-start(f32[16]{0:T(128)} %param.20) | copy-start | bytes 196
  21.2 3.4 %copy-start.18 = (f32[16]{0:T(128)S(1)}, f32[16]{0:T(128)}, u32[]{:S(2)}) copy-start(f32[16]{0:T(128)} %param.21) | copy-start | bytes 196
  21.2 6.2 %copy-start.17 = (f32[1024]{0:T(1024)S(1)}, f32[1024]{0:T(1024)}, u32[]{:S(2)}) copy-start(f32[1024]{0:T(1024)} %param.22) | copy-start | bytes 12292
  24.6 1.0 copy-start.4
  25.5 0.8 copy-start.8
  27.4 1.0 copy-start.9
  28.3 8.3 %copy-start.19 = (s32[1,32,6]{1,0,2:T(1,128)S(1)}, s32[1,32,6]{1,0,2:T(1,128)}, u32[]{:S(2)}) copy-start(s32[1,32,6]{1,0,2:T(1,128)} %param.25) | copy-start | bytes 2308
  31.3 0.6 copy-start.13
  32.0 6.9 %collective-permute-start = (bf16[32,1344]{1,0:T(8,128)(2,1)}, bf16[32,1344]{1,0:T(8,128)(2,1)S(1)}, u32[]{:S(2)}, u32[]{:S(2)}) collective-permute-start(bf16[32,1344]{1,0:T(8,128)(2,1)} %get-tuple-element.20), channel_id=1, source_target_pairs={{0,12},{4,0},{8,4},{12,8},{1,13},{5,1},{9,5},{13,9},{2,14},{6,2},{... | collective-permute-start | bytes 258056 | tf_op jit(solution)/shard_map/ppermute | solution.py:230
  35.6 9.2 %collective-permute-start.1 = (bf16[32,1344]{1,0:T(8,128)(2,1)}, bf16[32,1344]{1,0:T(8,128)(2,1)S(1)}, u32[]{:S(2)}, u32[]{:S(2)}) collective-permute-start(bf16[32,1344]{1,0:T(8,128)(2,1)} %get-tuple-element.21), channel_id=1, source_target_pairs={{0,8},{4,12},{8,0},{12,4},{1,9},{5,13},{9,1},{13,5},{2,10},{6,14},... | collective-permute-start | bytes 258056 | tf_op jit(solution)/shard_map/ppermute | solution.py:230
  35.6 9.2 %collective-permute-start.2 = (bf16[32,1344]{1,0:T(8,128)(2,1)}, bf16[32,1344]{1,0:T(8,128)(2,1)S(1)}, u32[]{:S(2)}, u32[]{:S(2)}) collective-permute-start(bf16[32,1344]{1,0:T(8,128)(2,1)} %get-tuple-element.22), channel_id=1, source_target_pairs={{0,4},{4,8},{8,12},{12,0},{1,5},{5,9},{9,13},{13,1},{2,6},{6,10},{... | collective-permute-start | bytes 258056 | tf_op jit(solution)/shard_map/ppermute | solution.py:230
  44.8 0.9 copy-start.10
  45.6 0.9 copy-start.14
  46.8 19.5 %copy-start.11 = (bf16[32,1344]{1,0:T(8,128)(2,1)}, bf16[32,1344]{1,0:T(8,128)(2,1)S(1)}, u32[]{:S(2)}) copy-start(bf16[32,1344]{1,0:T(8,128)(2,1)S(1)} %get-tuple-element.23.hidden_ref) | copy-start | bytes 258052
  46.8 7.4 %collective-permute-start.3 = (bf16[32,1408]{1,0:T(8,128)(2,1)S(1)}, bf16[32,1408]{1,0:T(8,128)(2,1)S(1)}, u32[]{:S(2)}, u32[]{:S(2)}) collective-permute-start(bf16[32,1408]{1,0:T(8,128)(2,1)S(1)} %get-tuple-element.24), channel_id=1, source_target_pairs={{0,4},{4,8},{8,12},{12,0},{1,5},{5,9},{9,13},{13,1},{2,6},{6,10},{... | collective-permute-start | bytes 270344 | tf_op jit(solution)/shard_map/ppermute | solution.py:230
  46.9 10.1 %collective-permute-start.4 = (bf16[32,1408]{1,0:T(8,128)(2,1)S(1)}, bf16[32,1408]{1,0:T(8,128)(2,1)S(1)}, u32[]{:S(2)}, u32[]{:S(2)}) collective-permute-start(bf16[32,1408]{1,0:T(8,128)(2,1)S(1)} %get-tuple-element.24), channel_id=1, source_target_pairs={{0,8},{4,12},{8,0},{12,4},{1,9},{5,13},{9,1},{13,5},{2,10},{6,14},... | collective-permute-start | bytes 270344 | tf_op jit(solution)/shard_map/ppermute | solution.py:230
  49.1 7.9 %collective-permute-start.5 = (bf16[32,1408]{1,0:T(8,128)(2,1)S(1)}, bf16[32,1408]{1,0:T(8,128)(2,1)S(1)}, u32[]{:S(2)}, u32[]{:S(2)}) collective-permute-start(bf16[32,1408]{1,0:T(8,128)(2,1)S(1)} %get-tuple-element.24), channel_id=1, source_target_pairs={{0,12},{4,0},{8,4},{12,8},{1,13},{5,1},{9,5},{13,9},{2,14},{6,2},{... | collective-permute-start | bytes 270344 | tf_op jit(solution)/shard_map/ppermute | solution.py:230
  57.0 8.4 %collective-permute-start.6 = (bf16[128,1408]{1,0:T(8,128)(2,1)S(1)}, bf16[128,1408]{1,0:T(8,128)(2,1)S(1)}, u32[]{:S(2)}, u32[]{:S(2)}) collective-permute-start(bf16[128,1408]{1,0:T(8,128)(2,1)S(1)} %pad_maximum_fusion), channel_id=1, source_target_pairs={{0,2},{1,3},{2,0},{3,1},{4,6},{5,7},{6,4},{7,5},{8,10},{9,11},{10,... | collective-permute-start | bytes 1081352 | tf_op jit(solution)/shard_map/ppermute | solution.py:230
  66.2 1.1 %copy-start.1 = (bf16[512,1408]{1,0:T(8,128)(2,1)}, bf16[512,1408]{1,0:T(8,128)(2,1)S(1)}, u32[]{:S(2)}) copy-start(bf16[512,1408]{1,0:T(8,128)(2,1)S(1)} %get-tuple-element.34) | copy-start | bytes 4325380
  67.4 3.3 %collective-permute-start.7 = (bf16[256,1408]{1,0:T(8,128)(2,1)}, bf16[256,1408]{1,0:T(8,128)(2,1)S(1)}, u32[]{:S(2)}, u32[]{:S(2)}) collective-permute-start(bf16[256,1408]{1,0:T(8,128)(2,1)} %get-tuple-element.33), channel_id=1, source_target_pairs={{0,1},{1,0},{2,3},{3,2},{4,5},{5,4},{6,7},{7,6},{8,9},{9,8},{10,11... | collective-permute-start | bytes 2162696 | tf_op jit(solution)/shard_map/ppermute | solution.py:230
  71.6 1.7 %copy-start = (bf16[1,928,1344]{2,1,0:T(8,128)(2,1)S(1)}, bf16[1,928,1344]{2,1,0:T(8,128)(2,1)}, u32[]{:S(2)}) copy-start(bf16[1,928,1344]{2,1,0:T(8,128)(2,1)} %down_ref.1) | copy-start | bytes 7483396
  73.3 1.4 %copy-start.2 = (bf16[512,1408]{1,0:T(8,128)(2,1)S(1)}, bf16[512,1408]{1,0:T(8,128)(2,1)}, u32[]{:S(2)}) copy-start(bf16[512,1408]{1,0:T(8,128)(2,1)} %constant_dynamic-update-slice_fusion.5.rows_ref) | copy-start | bytes 4325380
  78.6 0.9 copy-start.5
  80.9 26.0 %copy-start.12 = (bf16[32,1344]{1,0:T(8,128)(2,1)S(1)}, bf16[32,1344]{1,0:T(8,128)(2,1)}, u32[]{:S(2)}) copy-start(bf16[32,1344]{1,0:T(8,128)(2,1)} %copy-done.11) | copy-start | bytes 258052
  80.9 2.3 %collective-permute-start.8 = (bf16[256,1344]{0,1:T(8,128)(2,1)S(1)}, bf16[256,1344]{0,1:T(8,128)(2,1)S(1)}, u32[]{:S(2)}, u32[]{:S(2)}) collective-permute-start(bf16[256,1344]{0,1:T(8,128)(2,1)S(1)} %copy.30), channel_id=1, source_target_pairs={{0,1},{1,0},{2,3},{3,2},{4,5},{5,4},{6,7},{7,6},{8,9},{9,8},{10,11... | collective-permute-start | bytes 2064392 | tf_op jit(solution)/shard_map/ppermute | solution.py:230
  83.7 10.8 %collective-permute-start.9 = (bf16[128,1344]{1,0:T(8,128)(2,1)S(1)}, bf16[128,1344]{1,0:T(8,128)(2,1)S(1)}, u32[]{:S(2)}, u32[]{:S(2)}) collective-permute-start(bf16[128,1344]{1,0:T(8,128)(2,1)S(1)} %get-tuple-element.28), channel_id=1, source_target_pairs={{0,2},{1,3},{2,0},{3,1},{4,6},{5,7},{6,4},{7,5},{8,10},{9,11},{10,... | collective-permute-start | bytes 1032200 | tf_op jit(solution)/shard_map/ppermute | solution.py:230
  94.6 7.1 %collective-permute-start.10 = (bf16[32,1344]{1,0:T(8,128)(2,1)S(1)}, bf16[32,1344]{1,0:T(8,128)(2,1)S(1)}, u32[]{:S(2)}, u32[]{:S(2)}) collective-permute-start(bf16[32,1344]{1,0:T(8,128)(2,1)S(1)} %get-tuple-element.30), channel_id=1, source_target_pairs={{0,12},{4,0},{8,4},{12,8},{1,13},{5,1},{9,5},{13,9},{2,14},{6,2},{... | collective-permute-start | bytes 258056 | tf_op jit(solution)/shard_map/ppermute | solution.py:230
  98.7 8.2 %collective-permute-start.11 = (bf16[32,1344]{1,0:T(8,128)(2,1)S(1)}, bf16[32,1344]{1,0:T(8,128)(2,1)S(1)}, u32[]{:S(2)}, u32[]{:S(2)}) collective-permute-start(bf16[32,1344]{1,0:T(8,128)(2,1)S(1)} %get-tuple-element.31), channel_id=1, source_target_pairs={{0,8},{4,12},{8,0},{12,4},{1,9},{5,13},{9,1},{13,5},{2,10},{6,14},... | collective-permute-start | bytes 258056 | tf_op jit(solution)/shard_map/ppermute | solution.py:230
  98.8 8.0 %collective-permute-start.12 = (bf16[32,1344]{1,0:T(8,128)(2,1)S(1)}, bf16[32,1344]{1,0:T(8,128)(2,1)S(1)}, u32[]{:S(2)}, u32[]{:S(2)}) collective-permute-start(bf16[32,1344]{1,0:T(8,128)(2,1)S(1)} %get-tuple-element.32), channel_id=1, source_target_pairs={{0,4},{4,8},{8,12},{12,0},{1,5},{5,9},{9,13},{13,1},{2,6},{6,10},{... | collective-permute-start | bytes 258056 | tf_op jit(solution)/shard_map/ppermute | solution.py:230

commit v2 on v1

v2 whole, which is shorter than its diff:
```python
import functools

import jax
import jax.numpy as jnp
from jax import lax
from jax.experimental import pallas as pl
from jax.experimental.pallas import tpu as pltpu
from jax.sharding import PartitionSpec as P

HEAD_DIM = 64
STATE = 128
LANES = 128
TILE = 16
FAR = -1e30
F32 = jnp.float32
BF16 = jnp.bfloat16
HBM = pl.BlockSpec(memory_space=pltpu.HBM)
VMEM = pl.BlockSpec(memory_space=pltpu.VMEM)
SMEM = pl.BlockSpec(memory_space=pltpu.SMEM)
NT = (((1,), (1,)), ((), ()))


def struct(shape, dtype):
    return jax.ShapeDtypeStruct(shape, dtype)


def call(kernel, name, outs, ins, scratch=(), megabytes=12, flops=0, moved_bytes=0):
    specs, args = [spec for spec, _ in ins], [arg for _, arg in ins]
    return pl.pallas_call(
        kernel,
        out_shape=outs,
        in_specs=specs,
        out_specs=jax.tree.map(lambda _: VMEM, outs),
        scratch_shapes=list(scratch),
        name=name,
        compiler_params=pltpu.CompilerParams(vmem_limit_bytes=megabytes << 20),
        cost_estimate=pl.CostEstimate(flops=flops, bytes_accessed=moved_bytes, transcendentals=0),
    )(*args)


def copies(sems, sources, targets):
    made = [pltpu.make_async_copy(s, t, sems.at[i]) for i, (s, t) in enumerate(zip(sources, targets))]
    for copy in made:
        copy.start()
    return made


def decays(dt_rows, a_log):
    heads, length = dt_rows.shape
    step = jnp.maximum(dt_rows, 0.0) + jnp.log1p(jnp.exp(-jnp.abs(dt_rows)))
    same = lax.broadcasted_iota(jnp.int32, (heads, heads), 0) == lax.broadcasted_iota(jnp.int32, (heads, heads), 1)
    a_column = jnp.sum(jnp.where(same, jnp.broadcast_to(a_log, (heads, heads)), 0.0), axis=1, keepdims=True)
    rate = -step * jnp.exp(a_column)
    row = lax.broadcasted_iota(jnp.int32, (length, length), 0)
    col = lax.broadcasted_iota(jnp.int32, (length, length), 1)
    upper = (row <= col).astype(F32)
    cum = jnp.dot(rate, upper, precision=lax.Precision.HIGHEST, preferred_element_type=F32)
    return step, cum


def pair_lanes(values, pair):
    rows = values.shape[0]
    lane = lax.broadcasted_iota(jnp.int32, (rows, LANES), 1)
    left = jnp.broadcast_to(values[:, 2 * pair : 2 * pair + 1], (rows, LANES))
    right = jnp.broadcast_to(values[:, 2 * pair + 1 : 2 * pair + 2], (rows, LANES))
    return jnp.where(lane < HEAD_DIM, left, right)


def state_kernel(place_ref, x_hbm, b_hbm, dt_hbm, a_hbm, *rest):
    outs, (x_ref, b_ref, dt_ref, a_ref, packed_ref, sems) = rest[:-6], rest[-6:]
    loads = copies(sems, (dt_hbm, a_hbm, x_hbm, b_hbm), (dt_ref, a_ref, x_ref, b_ref))
    loads[0].wait()
    loads[1].wait()
    step, cum = decays(dt_ref[...], a_ref[...])
    length = cum.shape[1]
    total = cum[:, length - 1 :]
    tail = (jnp.exp(total - cum) * step).T
    total = jnp.broadcast_to(total, cum.shape).T[0:1]
    loads[2].wait()
    loads[3].wait()
    pairs = packed_ref.shape[0]
    groups = b_ref.shape[1] // STATE
    for group in range(groups):
        turned = b_ref[:, group * STATE : (group + 1) * STATE].T
        for pair in range(group * pairs // groups, (group + 1) * pairs // groups):
            x_pair = x_ref[:, pair * LANES : (pair + 1) * LANES].astype(F32)
            weighted = (pair_lanes(tail, pair) * x_pair).astype(BF16)
            state = jnp.dot(turned, weighted, preferred_element_type=F32)
            packed_ref[pair, 0:STATE, :] = state.astype(BF16)
            wide = jnp.broadcast_to(pair_lanes(total, pair), (TILE, LANES))
            high = wide.astype(BF16).astype(F32)
            row = lax.broadcasted_iota(jnp.int32, (TILE, LANES), 0)
            packed_ref[pair, STATE : STATE + TILE, :] = jnp.where(row == 0, high, wide - high).astype(BF16)
    here = pairs // len(outs)
    for shift, out in enumerate(outs):
        out[...] = packed_ref[pl.ds((place_ref[2] ^ shift) * here, here)]


def inside_kernel(x_hbm, z_hbm, b_hbm, c_hbm, dt_hbm, a_hbm, d_hbm, norm_hbm, w_hbm, *rest):
    local_ref, grown_ref, c_ref, norm_ref, w_ref = rest[:5]
    x_ref, z_ref, b_ref, dt_ref, a_ref, d_ref, sems = rest[5:]
    loads = copies(
        sems,
        (dt_hbm, a_hbm, d_hbm, b_hbm, c_hbm, x_hbm, z_hbm, norm_hbm, w_hbm),
        (dt_ref, a_ref, d_ref, b_ref, c_ref, x_ref, z_ref, norm_ref, w_ref),
    )
    for load in loads[:7]:
        load.wait()
    step_rows, cum_rows = decays(dt_ref[...], a_ref[...])
    cum = cum_rows.T
    grown = jnp.exp(cum)
    length = cum.shape[0]
    pairs = x_ref.shape[1] // LANES
    groups = b_ref.shape[1] // STATE
    row = lax.broadcasted_iota(jnp.int32, (length, length), 0)
    col = lax.broadcasted_iota(jnp.int32, (length, length), 1)
    lane = lax.broadcasted_iota(jnp.int32, (length, LANES), 1)
    for group in range(groups):
        span = slice(group * STATE, (group + 1) * STATE)
        scores = lax.dot_general(c_ref[:, span], b_ref[:, span], NT, preferred_element_type=F32)
        scores = jnp.where(row >= col, scores, 0.0)
        for pair in range(group * pairs // groups, (group + 1) * pairs // groups):
            at = slice(pair * LANES, (pair + 1) * LANES)
            x_pair = x_ref[:, at]
            halves = []
            for head in (2 * pair, 2 * pair + 1):
                distance = cum[:, head : head + 1] - cum_rows[head : head + 1, :]
                decay = jnp.exp(jnp.where(row >= col, distance, FAR))
                mixing = (scores * (decay * step_rows[head : head + 1, :])).astype(BF16)
                halves.append(jnp.dot(mixing, x_pair, preferred_element_type=F32))
            inside = jnp.where(lane < HEAD_DIM, halves[0], halves[1])
            skip = pair_lanes(d_ref[...], pair) * x_pair.astype(F32)
            z = z_ref[:, at].astype(F32)
            gate = z / (1.0 + jnp.exp(-z))
            local_ref[:, at] = (inside + skip) * gate
            grown_ref[:, at] = pair_lanes(grown, pair) * gate
    loads[7].wait()
    loads[8].wait()


def prep_kernel(experts, width, resid_hbm, routes_hbm, gates_hbm, gain_hbm, up_hbm, down_hbm, *rest):
    gate_ref, resid_ref, gain_ref, up_ref, down_ref, routes_ref, gates_ref, sems = rest
    loads = copies(
        sems,
        (routes_hbm, gates_hbm, resid_hbm, gain_hbm, up_hbm, down_hbm),
        (routes_ref, gates_ref, resid_ref, gain_ref, up_ref, down_ref),
    )
    loads[0].wait()
    loads[1].wait()
    count, extent = gate_ref.shape
    start = width // LANES * LANES
    lane = lax.broadcasted_iota(jnp.int32, (extent, count), 0) + start - width
    expert = jnp.where(lane >= experts, lane - experts, lane)
    gate = jnp.zeros((extent, count), F32)
    for pick in range(routes_ref.shape[0]):
        gate = gate + jnp.where(routes_ref[pick] == expert, gates_ref[pick], 0.0)
    high = gate.astype(BF16).astype(F32)
    gate = jnp.where(lane < experts, high, jnp.where(lane < 2 * experts, gate - high, 0.0))
    gate_ref[...] = gate.T.astype(BF16)
    for load in loads[2:]:
        load.wait()


def chain_kernel(place_ref, *rest):
    count = (len(rest) - 1) // 2
    ins, outs, block_ref = rest[:count], rest[count : 2 * count], rest[-1]
    for shift in range(count):
        block_ref[place_ref[2] ^ shift] = ins[shift][...]
    carry = jnp.zeros(outs[0].shape, F32)
    for shard in range(count):
        block = block_ref[shard].astype(F32)
        block_ref[shard, :, 0:STATE, :] = carry.astype(BF16)
        total = block[:, STATE : STATE + 1, :] + block[:, STATE + 1 : STATE + 2, :]
        carry = jnp.exp(total) * carry + block[:, 0:STATE, :]
    for shift in range(count):
        outs[shift][...] = block_ref[place_ref[2] ^ shift, :, 0:STATE, :]


def chain_over_seq(place, got):
    mine = place[2]
    count = len(got)
    order = jnp.arange(count, dtype=jnp.int32) ^ mine
    block = jnp.stack(got)[order].astype(F32)
    totals = block[:, :, STATE : STATE + 1] + block[:, :, STATE + 1 : STATE + 2]

    def walk(carry, item):
        return (carry[0] + item[0], jnp.exp(item[0]) * carry[1] + item[1]), carry

    zero = (jnp.zeros(totals.shape[1:], F32), jnp.zeros(block[0, :, :STATE].shape, F32))
    span, inner = lax.scan(walk, zero, (totals, block[:, :, :STATE]))
    everything = jax.tree.map(lambda part: lax.all_gather(part.astype(BF16), "seq").astype(F32), span)
    unused, outer = lax.scan(walk, zero, everything)
    chain = lax.dynamic_index_in_dim(outer[1], lax.axis_index("seq"), 0, keepdims=False)
    before = (jnp.exp(inner[0]) * chain[None] + inner[1]).astype(BF16)[order]
    return [before[shift] for shift in range(count)]


def mixed_kernel(place_ref, local_ref, grown_ref, c_ref, norm_ref, w_ref, *rest):
    normed_ref, state_ref = rest[-2:]
    pairs = state_ref.shape[0]
    befores, outs = [], []
    held = 0
    for ref in rest[:-2]:
        if held < pairs:
            befores.append(ref)
            held += ref.shape[0]
        else:
            outs.append(ref)
    here = pairs // len(befores)
    for shift, before in enumerate(befores):
        state_ref[pl.ds((place_ref[2] ^ shift) * here, here)] = before[...]
    groups = c_ref.shape[1] // STATE
    per_group = pairs // groups
    for group in range(groups):
        c_group = c_ref[:, group * STATE : (group + 1) * STATE]
        gated, squares = [], 0.0
        for pair in range(group * per_group, (group + 1) * per_group):
            span = slice(pair * LANES, (pair + 1) * LANES)
            carried = jnp.dot(c_group, state_ref[pair], preferred_element_type=F32)
            value = local_ref[:, span] + grown_ref[:, span] * carried
            gated.append(value)
            squares = squares + value * value
        mean = jnp.sum(squares, axis=1, keepdims=True) / (per_group * LANES)
        inverse = lax.rsqrt(mean + 1e-05)
        for offset, value in enumerate(gated):
            pair = group * per_group + offset
            span = slice(pair * LANES, (pair + 1) * LANES)
            normed_ref[:, span] = (value * inverse * norm_ref[:, span]).astype(BF16)
    rows = outs[0].shape[0]
    blocks = []
    for shift in range(len(outs)):
        owner = place_ref[0] ^ shift
        blocks.append(normed_ref[pl.ds(pl.multiple_of(owner * rows, rows), rows), :])
    product = lax.dot_general(jnp.concatenate(blocks, axis=0), w_ref[...], NT, preferred_element_type=F32)
    for shift, out in enumerate(outs):
        out[...] = product[shift * rows : (shift + 1) * rows].astype(BF16)


def rows_kernel(resid_ref, gate_ref, gain_ref, *rest):
    parts, hidden_ref, rows_ref = rest[:-2], rest[-2], rest[-1]
    mixed = parts[0][...].astype(F32)
    for part in parts[1:]:
        mixed = mixed + part[...].astype(F32)
    hidden = (resid_ref[0].astype(F32) + mixed).astype(BF16)
    hidden_ref[...] = hidden
    value = hidden.astype(F32)
    scale = lax.rsqrt(jnp.mean(value * value, axis=1, keepdims=True) + 1e-05)
    width = value.shape[1]
    rows_ref[:, width // LANES * LANES :] = gate_ref[...]
    rows_ref[:, :width] = (value * scale * gain_ref[...]).astype(BF16)


def expert_kernel(experts, place_ref, up_ref, down_ref, mine_ref, partner_ref, kept_ref, sent_ref):
    width = up_ref.shape[2]
    start = width // LANES * LANES
    half = mine_ref.shape[0]
    rows = jnp.concatenate([mine_ref[:, :width], partner_ref[:, :width]], axis=0)
    up = lax.dot_general(rows, up_ref[0], NT, preferred_element_type=F32)
    up = jnp.maximum(up, 0.0)
    activated = (up * up).astype(BF16)
    tail = jnp.concatenate([mine_ref[:, start:], partner_ref[:, start:]], axis=0).astype(F32)
    lane = lax.broadcasted_iota(jnp.int32, tail.shape, 1) + start - width
    chosen = (lane == place_ref[1]) | (lane == place_ref[1] + experts)
    gate = jnp.sum(jnp.where(chosen, tail, 0.0), axis=1, keepdims=True)
    out = jnp.dot(activated, down_ref[0], preferred_element_type=F32) * gate
    kept_ref[...] = out[:half].astype(BF16)
    sent_ref[...] = out[half:].astype(BF16)


def split_sum_kernel(kept_ref, got_ref, *outs):
    rows = outs[0].shape[0]
    for at, out in enumerate(outs):
        span = slice(at * rows, (at + 1) * rows)
        out[...] = (kept_ref[span].astype(F32) + got_ref[span].astype(F32)).astype(BF16)


def piece_kernel(at, kept_ref, got_ref, *rest):
    parts, out_ref = rest[:-1], rest[-1]
    rows = out_ref.shape[0]
    span = slice(at * rows, (at + 1) * rows)
    total = kept_ref[span].astype(F32) + got_ref[span].astype(F32)
    for part in parts:
        total = total + part[...].astype(F32)
    out_ref[...] = total.astype(BF16)


def last_kernel(hidden_ref, *rest):
    parts, out_ref = rest[:-1], rest[-1]
    total = parts[0][...].astype(F32)
    for part in parts[1:]:
        total = total + part[...].astype(F32)
    out_ref[0] = (hidden_ref[...].astype(F32) + total).astype(BF16)


def swap(value, axis, mask):
    size = lax.axis_size(axis)
    return lax.ppermute(value, axis, [(i, i ^ mask) for i in range(size)])


def per_device(
    x_in, z_in, b_in, c_in, dt_in, a_log, d_skip, norm_w, w_out, resid, routes, gates, moe_gain, w_up, w_down
):
    length, heads = dt_in.shape
    channels = x_in.shape[1]
    model = w_out.shape[1]
    hidden_units = w_up.shape[2]
    seq_size, head_size, exp_size = lax.axis_size("seq"), lax.axis_size("head"), lax.axis_size("exp")
    chips = exp_size // 2
    rows = resid.shape[1]
    experts = head_size * exp_size
    pairs = channels // LANES
    axes = ("seq", "exp") if pairs % (seq_size * exp_size) == 0 else "exp"
    shards = lax.axis_size(axes)
    here = pairs // shards
    place = jnp.stack(
        [lax.axis_index("head"), lax.axis_index("head") * exp_size + lax.axis_index("exp"), lax.axis_index(axes)]
    ).astype(jnp.int32)
    dt_rows, a_row, d_row = dt_in.T, a_log[None], d_skip[None]
    dma = pltpu.SemaphoreType.DMA
    own = call(
        state_kernel,
        "state",
        [struct((here, STATE + TILE, LANES), BF16)] * shards,
        [(SMEM, place), (HBM, x_in), (HBM, b_in), (HBM, dt_rows), (HBM, a_row)],
        [pltpu.VMEM(x_in.shape, BF16), pltpu.VMEM(b_in.shape, BF16), pltpu.VMEM(dt_rows.shape, F32),
         pltpu.VMEM(a_row.shape, F32), pltpu.VMEM((pairs, STATE + TILE, LANES), BF16), dma((4,))],
        flops=1 << 25, moved_bytes=1 << 20,
    )
    got = [own[0]] + [swap(own[s], axes, s) for s in range(1, shards)]
    wide = -(-(model + 2 * experts) // LANES) * LANES
    local, grown, c_held, norm_held, w_held = call(
        inside_kernel,
        "inside",
        [struct((length, channels), F32), struct((length, channels), F32), struct(c_in.shape, BF16),
         struct((1, channels), F32), struct((model, channels), BF16)],
        [(HBM, value) for value in (x_in, z_in, b_in, c_in, dt_rows, a_row, d_row, norm_w[None], w_out.T)],
        [pltpu.VMEM(x_in.shape, BF16), pltpu.VMEM(z_in.shape, BF16), pltpu.VMEM(b_in.shape, BF16),
         pltpu.VMEM(dt_rows.shape, F32), pltpu.VMEM(a_row.shape, F32), pltpu.VMEM(d_row.shape, F32), dma((9,))],
        flops=1 << 27, moved_bytes=8 << 20,
    )
    turned = [jnp.transpose(value, (2, 0, 1)) for value in (routes, gates)]
    gate_lanes, resid_held, gain_held, up_held, down_held = call(
        functools.partial(prep_kernel, experts, model),
        "prep",
        [struct((rows, wide - model // LANES * LANES), BF16), struct(resid.shape, BF16), struct((1, model), F32),
         struct((1, hidden_units, model), BF16), struct(w_down.shape, BF16)],
        [(HBM, value) for value in (resid, *turned, moe_gain[None], jnp.swapaxes(w_up, 1, 2), w_down)],
        [pltpu.VMEM(turned[0].shape, jnp.int32), pltpu.VMEM(turned[1].shape, F32), dma((6,))],
        flops=1 << 20, moved_bytes=8 << 20,
    )
    if axes == "exp":
        before = chain_over_seq(place, got)
    else:
        before = call(
            chain_kernel,
            "chain",
            [struct((here, STATE, LANES), BF16)] * shards,
            [(SMEM, place)] + [(VMEM, value) for value in got],
            [pltpu.VMEM((shards, here, STATE + TILE, LANES), BF16)],
            flops=1 << 20, moved_bytes=1 << 19,
        )
    before = [before[0]] + [swap(before[s], axes, s) for s in range(1, shards)]
    mixed = call(
        mixed_kernel,
        "mixed",
        [struct((rows, model), BF16)] * head_size,
        [(SMEM, place)] + [(VMEM, value) for value in (local, grown, c_held, norm_held, w_held, *before)],
        [pltpu.VMEM((length, channels), BF16), pltpu.VMEM((pairs, STATE, LANES), BF16)],
        flops=1 << 29, moved_bytes=4 << 20,
    )
    order = list(range(head_size - 1, 0, -1))
    parts = [mixed[0]] + [swap(mixed[s], "head", s) for s in order]
    hidden, own_rows = call(
        rows_kernel,
        "rows",
        [struct((rows, model), BF16), struct((rows, wide), BF16)],
        [(VMEM, value) for value in (resid_held, gate_lanes, gain_held, *parts)],
    )
    near = {0: own_rows} | {s: swap(own_rows, "head", s) for s in order}
    sets = [near] + [{s: swap(near[s], "exp", 2 * d) for s in near} for d in range(1, chips)]
    produced = []
    for members in sets:
        mine = jnp.concatenate([members[s] for s in range(head_size)], axis=0)
        produced.append(
            call(
                functools.partial(expert_kernel, experts),
                "experts",
                [struct((head_size * rows, model), BF16)] * 2,
                [(SMEM, place)] + [(VMEM, value) for value in (up_held, down_held, mine, swap(mine, "exp", 1))],
                megabytes=16,
                flops=1 << 31, moved_bytes=8 << 20,
            )
        )
    returned = [(kept, swap(sent, "exp", 1)) for kept, sent in produced]
    arrived = {s: [] for s in range(head_size)}
    for d in range(1, chips):
        pieces = call(
            split_sum_kernel,
            "split",
            [struct((rows, model), BF16)] * head_size,
            [(VMEM, value) for value in returned[d]],
        )
        for s in order + [0]:
            arrived[s].append(swap(pieces[s], "exp", 2 * d))
    final = []
    for s in order + [0]:
        piece = call(
            functools.partial(piece_kernel, s),
            "piece",
            struct((rows, model), BF16),
            [(VMEM, value) for value in (*returned[0], *arrived[s])],
        )
        final.append(swap(piece, "head", s) if s else piece)
    return call(last_kernel, "last", struct(resid.shape, BF16), [(VMEM, value) for value in (hidden, *final)])


def solution(mesh):
    placed = (
        P(("seq", "exp"), "head"),
        P(("seq", "exp"), "head"),
        P(("seq", "exp"), "head"),
        P(("seq", "exp"), "head"),
        P(("seq", "exp"), "head"),
        P("head"),
        P("head"),
        P("head"),
        P("head", None),
        P(("seq", "exp"), "head", None),
        P(("seq", "exp"), "head", None),
        P(("seq", "exp"), "head", None),
        P(),
        P(("head", "exp"), None, None),
        P(("head", "exp"), None, None),
    )
    return jax.shard_map(
        per_device,
        mesh=mesh,
        in_specs=placed,
        out_specs=P(("seq", "exp"), "head", None),
        check_vma=False,
    )
```

time: 108 us -> 89.1 us (0.82)
  local copies, waits for them, and re-layouts: 27.6 us -> 11.3 us
  starting transfers between devices: 21.7 us -> 35.3 us
  blocking collectives: 12.2 us -> 0 us
  waiting for transfers between devices: 35 us -> 28.2 us
  Pallas kernels: 10.7 us -> 13.3 us
    ppermute x13 -> x35, starting transfers between devices: 17.6 us -> 35.3 us  [swap(): return lax.ppermute(value, axis, [(i, i ^ mask) for i in range(size)])]
    unnamed x49 -> x44, local copies, waits for them, and re-layouts: 23.5 us -> 11.3 us
    all_to_all x1 -> x0, blocking collectives: 12.2 us -> none  [states_before(): got = lax.all_to_all(packed, axes, split_axis=0, concat_axis=0, tiled=True)]
    ppermute x13 -> x35, waiting for transfers between devices: 35 us -> 28.2 us  [swap(): return lax.ppermute(value, axis, [(i, i ^ mask) for i in range(size)])]
    all_to_all x1 -> x0, starting transfers between devices: 4.05 us -> none  [states_before(): return lax.all_to_all(before, axes, split_axis=0, concat_axis=0, tiled=True)]
    pallas_call x9 -> x14, Pallas kernels: 10.7 us -> 13.3 us  [call(): pl.pallas_call(kernel, out_shape=outs, in_specs=specs, out_specs=jax.tree...]
    concatenate x2, local copies, waits for them, and re-layouts: 1.72 us -> 0.03 us  [per_device(): mine = jnp.concatenate([members[s] for s in range(head_size)], axis=0)]
    pallas_call x1 -> x0, local copies, waits for them, and re-layouts: 1.36 us -> none  [per_device(): pl.pallas_call(functools.partial(expert_kernel, experts), out_shape=[stru...]
  transfers between devices with their start and end apart: 14 -> 35, of which waited for: 9 -> 14; matrix products, arithmetic and copies ran while one was open for 10% -> 0% of each run, Pallas kernels for 1% -> 9%
where the time goes in v2:
time: 89.1 us; the launch traced here: 88.5 us
  starting transfers between devices  35.3 us (40%)
  waiting for transfers between devices  28.2 us (32%)
  Pallas kernels  13.3 us (15%)
  local copies, waits for them, and re-layouts  11.3 us (13%)
    ppermute x35, starting transfers between devices, swap(): return lax.ppermute(value, axis, [(i, i ^ mask) for i in range(size)])  35.3 us
    ppermute x35, waiting for transfers between devices, swap(): return lax.ppermute(value, axis, [(i, i ^ mask) for i in range(size)])  28.2 us
    pallas_call x14, Pallas kernels, call(): pl.pallas_call(kernel, out_shape=outs, in_specs=specs, out_specs=jax.tree...  13.3 us
    unnamed x44, local copies, waits for them, and re-layouts  11.3 us
  transfers between devices with their start and end apart: 35, of which 14 were waited for; matrix products, arithmetic and copies ran while one was open for 0% of the time, Pallas kernels for 9%

profile of v2, /device:TPU:0, one launch (start us, length us, event | category | flops | bytes accessed | tf_op | source)
XLA Modules:
  0.0 88.5 jit_solution(8901721661359258965)
XLA Ops:
  0.1 0.9 %copy-done.3 = bf16[128,1024]{1,0:T(8,128)(2,1)S(1)} copy-done((bf16[128,1024]{1,0:T(8,128)(2,1)S(1)}, bf16[128,1024]{1,0:T(8,128)(2,1)}, u32[]{:S(2)}) %copy-start.3) | copy-done | bytes 262168
  1.0 0.8 copy-done.6
  3.2 1.8 %state.1 = (bf16[1,144,128]{2,1,0:T(8,128)(2,1)S(1)}, bf16[1,144,128]{2,1,0:T(8,128)(2,1)S(1)}, bf16[1,144,128]{2,1,0:T(8,128)(2,1)S(1)}, bf16[1,144,128]{2,1,0:...) custom-call(s32[3]{0:T(128)S(1)} %pad_add_fusion.place_ref, ...), custom_call_target="tpu_custom_call" | custom-call | flops 33554432 | bytes 1048576 | tf_op jit(solution)/shard_map/state/pallas_call | solution.py:29
  5.5 2.6 %collective-permute-start.1 = (bf16[1,144,128]{2,1,0:T(8,128)(2,1)S(1)}, bf16[1,144,128]{2,1,0:T(8,128)(2,1)S(1)}, u32[]{:S(2)}, u32[]{:S(2)}) collective-permute-start(bf16[1,144,128]{2,1,0:T(8,128)(2,1)S(1)} %get-tuple-element.55), channel_id=1, source_target_pairs={{0,2},{1,3},{2,0},{3,1},{16,18},{17,19},{18,16},{19,17},{4,6},{5,7... | collective-permute-start | bytes 110600 | tf_op jit(solution)/shard_map/ppermute | solution.py:297
  8.2 1.7 %collective-permute-start.3 = (bf16[1,144,128]{2,1,0:T(8,128)(2,1)S(1)}, bf16[1,144,128]{2,1,0:T(8,128)(2,1)S(1)}, u32[]{:S(2)}, u32[]{:S(2)}) collective-permute-start(bf16[1,144,128]{2,1,0:T(8,128)(2,1)S(1)} %get-tuple-element.57), channel_id=1, source_target_pairs={{0,16},{1,17},{2,18},{3,19},{16,0},{17,1},{18,2},{19,3},{4,20},{5,... | collective-permute-start | bytes 110600 | tf_op jit(solution)/shard_map/ppermute | solution.py:297
  9.9 2.6 %collective-permute-start.5 = (bf16[1,144,128]{2,1,0:T(8,128)(2,1)S(1)}, bf16[1,144,128]{2,1,0:T(8,128)(2,1)S(1)}, u32[]{:S(2)}, u32[]{:S(2)}) collective-permute-start(bf16[1,144,128]{2,1,0:T(8,128)(2,1)S(1)} %get-tuple-element.59), channel_id=1, source_target_pairs={{0,18},{1,19},{2,16},{3,17},{16,2},{17,3},{18,0},{19,1},{4,22},{5,... | collective-permute-start | bytes 110600 | tf_op jit(solution)/shard_map/ppermute | solution.py:297
  12.7 0.8 collective-permute-done.4.rest_5_
  13.4 2.0 %collective-permute-done.5.rest_6_ = bf16[1,144,128]{2,1,0:T(8,128)(2,1)S(1)} collective-permute-done((bf16[1,144,128]{2,1,0:T(8,128)(2,1)S(1)}, bf16[1,144,128]{2,1,0:T(8,128)(2,1)S(1)}, u32[]{:S(2)}, u32[]{:S(2)}) %collective-permute-start.5) | collective-permute-done | bytes 36896 | tf_op jit(solution)/shard_map/ppermute | solution.py:297
  15.4 1.5 %collective-permute-done.6.rest_7_ = bf16[1,144,128]{2,1,0:T(8,128)(2,1)S(1)} collective-permute-done((bf16[1,144,128]{2,1,0:T(8,128)(2,1)S(1)}, bf16[1,144,128]{2,1,0:T(8,128)(2,1)S(1)}, u32[]{:S(2)}, u32[]{:S(2)}) %collective-permute-start.6) | collective-permute-done | bytes 36896 | tf_op jit(solution)/shard_map/ppermute | solution.py:297
  18.1 1.0 %collective-permute-start.11 = (bf16[1,128,128]{2,1,0:T(8,128)(2,1)S(1)}, bf16[1,128,128]{2,1,0:T(8,128)(2,1)S(1)}, u32[]{:S(2)}, u32[]{:S(2)}) collective-permute-start(bf16[1,128,128]{2,1,0:T(8,128)(2,1)S(1)} %get-tuple-element.66), channel_id=1, source_target_pairs={{0,17},{1,16},{2,19},{3,18},{16,1},{17,0},{18,3},{19,2},{4,21},{5,... | collective-permute-start | bytes 98312 | tf_op jit(solution)/shard_map/ppermute | solution.py:297
  19.1 1.1 %collective-permute-start.12 = (bf16[1,128,128]{2,1,0:T(8,128)(2,1)S(1)}, bf16[1,128,128]{2,1,0:T(8,128)(2,1)S(1)}, u32[]{:S(2)}, u32[]{:S(2)}) collective-permute-start(bf16[1,128,128]{2,1,0:T(8,128)(2,1)S(1)} %get-tuple-element.67), channel_id=1, source_target_pairs={{0,18},{1,19},{2,16},{3,17},{16,2},{17,3},{18,0},{19,1},{4,22},{5,... | collective-permute-start | bytes 98312 | tf_op jit(solution)/shard_map/ppermute | solution.py:297
  20.2 1.8 %collective-permute-start.13 = (bf16[1,128,128]{2,1,0:T(8,128)(2,1)S(1)}, bf16[1,128,128]{2,1,0:T(8,128)(2,1)S(1)}, u32[]{:S(2)}, u32[]{:S(2)}) collective-permute-start(bf16[1,128,128]{2,1,0:T(8,128)(2,1)S(1)} %get-tuple-element.68), channel_id=1, source_target_pairs={{0,19},{1,18},{2,17},{3,16},{16,3},{17,2},{18,1},{19,0},{4,23},{5,... | collective-permute-start | bytes 98312 | tf_op jit(solution)/shard_map/ppermute | solution.py:297
  22.7 1.2 %collective-permute-start.9 = (bf16[1,128,128]{2,1,0:T(8,128)(2,1)S(1)}, bf16[1,128,128]{2,1,0:T(8,128)(2,1)S(1)}, u32[]{:S(2)}, u32[]{:S(2)}) collective-permute-start(bf16[1,128,128]{2,1,0:T(8,128)(2,1)S(1)} %get-tuple-element.64), channel_id=1, source_target_pairs={{0,3},{1,2},{2,1},{3,0},{16,19},{17,18},{18,17},{19,16},{4,7},{5,6... | collective-permute-start | bytes 98312 | tf_op jit(solution)/shard_map/ppermute | solution.py:297
  23.9 1.8 %copy-done = bf16[1024,1344]{0,1:T(8,128)(2,1)S(1)} copy-done((bf16[1024,1344]{0,1:T(8,128)(2,1)S(1)}, bf16[1024,1344]{0,1:T(8,128)(2,1)}, u32[]{:S(2)}) %copy-start) | copy-done | bytes 2752536
  25.6 0.9 %copy-done.4 = bf16[128,1024]{1,0:T(8,128)(2,1)S(1)} copy-done((bf16[128,1024]{1,0:T(8,128)(2,1)S(1)}, bf16[128,1024]{1,0:T(8,128)(2,1)}, u32[]{:S(2)}) %copy-start.4) | copy-done | bytes 262168
  26.6 0.9 %copy-done.5 = bf16[128,1024]{1,0:T(8,128)(2,1)S(1)} copy-done((bf16[128,1024]{1,0:T(8,128)(2,1)S(1)}, bf16[128,1024]{1,0:T(8,128)(2,1)}, u32[]{:S(2)}) %copy-start.5) | copy-done | bytes 262168
  27.5 0.8 copy-done.7
  28.4 0.8 copy-done.9
  31.9 1.9 %inside.1 = (f32[128,1024]{1,0:T(8,128)S(1)}, f32[128,1024]{1,0:T(8,128)S(1)}, bf16[128,256]{1,0:T(8,128)(2,1)S(1)}, f32[1,1024]{1,0:T(1,128)S(1)}, bf16[1344,1024]{1,0:T(8,128)(2,1)S(1)}) custom-call(bf16[128,1024]{1,0:T(8,128)(2,1)S(1)} %copy-done.4, bf16[128,1024]{1,0:T(8,128)(2,1)S(1)} %copy-done.5, bf16[128,256]{1,0:T(8,128)(2,1)S(1)} %copy-done.7, ...), custom_call_target="tpu_custom_call" | custom-call | flops 134217728 | bytes 8388608 | tf_op jit(solution)/shard_map/inside/pallas_call | solution.py:29
  33.9 1.9 %mixed.1 = (bf16[32,1344]{1,0:T(8,128)(2,1)S(1)}, bf16[32,1344]{1,0:T(8,128)(2,1)S(1)}, bf16[32,1344]{1,0:T(8,128)(2,1)S(1)}, bf16[32,1344]{1,0:T(8,128)(2,1)S(1)}) custom-call(s32[3]{0:T(128)S(1)} %pad_add_fusion.place_ref, f32[128,1024]{1,0:T(8,128)S(1)} %get-tuple-element.48.local_ref, f32[128,1024]{1,0:T(8,128)S(1)} %get-tuple-element.49.grown_ref, ...), custom_call_target="tpu_custom_call" | custom-call | flops 536870912 | bytes 4194304 | tf_op jit(solution)/shard_map/mixed/pallas_call | solution.py:29
  35.8 3.7 %collective-permute-start.14 = (bf16[32,1344]{1,0:T(8,128)(2,1)S(1)}, bf16[32,1344]{1,0:T(8,128)(2,1)S(1)}, u32[]{:S(2)}, u32[]{:S(2)}) collective-permute-start(bf16[32,1344]{1,0:T(8,128)(2,1)S(1)} %get-tuple-element.70), channel_id=1, source_target_pairs={{0,12},{4,8},{8,4},{12,0},{1,13},{5,9},{9,5},{13,1},{2,14},{6,10},... | collective-permute-start | bytes 258056 | tf_op jit(solution)/shard_map/ppermute | solution.py:297
  39.5 0.8 collective-permute-start.16
  40.3 1.3 %prep.1 = (bf16[32,128]{1,0:T(8,128)(2,1)S(1)}, bf16[1,32,1344]{2,1,0:T(8,128)(2,1)S(1)}, f32[1,1344]{1,0:T(1,128)S(1)}, bf16[1,928,1344]{2,1,0:T(8,128)(2,1)S(1)}, bf16[1,928,1344]{2,1,0:T(8,128)(2,1)S(1)}) custom-call(bf16[1,32,1344]{2,1,0:T(8,128)(2,1)S(1)} %copy-done.8, s32[6,1,32]{2,1,0:T(1,128)S(1)} %bitcast.16, f32[6,1,32]{2,1,0:T(1,128)S(1)} %bitcast.17, ...), custom_call_target="tpu_custom_call" | custom-call | flops 1048576 | bytes 8388608 | tf_op jit(solution)/shard_map/prep/pallas_call | solution.py:29
  41.6 1.6 %collective-permute-done.14.rest_1_ = bf16[32,1344]{1,0:T(8,128)(2,1)S(1)} collective-permute-done((bf16[32,1344]{1,0:T(8,128)(2,1)S(1)}, bf16[32,1344]{1,0:T(8,128)(2,1)S(1)}, u32[]{:S(2)}, u32[]{:S(2)}) %collective-permute-start.14) | collective-permute-done | bytes 86048 | tf_op jit(solution)/shard_map/ppermute | solution.py:297
  43.2 4.5 %collective-permute-done.15.rest_2_ = bf16[32,1344]{1,0:T(8,128)(2,1)S(1)} collective-permute-done((bf16[32,1344]{1,0:T(8,128)(2,1)S(1)}, bf16[32,1344]{1,0:T(8,128)(2,1)S(1)}, u32[]{:S(2)}, u32[]{:S(2)}) %collective-permute-start.15) | collective-permute-done | bytes 86048 | tf_op jit(solution)/shard_map/ppermute | solution.py:297
  48.4 0.7 collective-permute-start.17
  49.1 2.3 %collective-permute-start.18 = (bf16[32,1408]{1,0:T(8,128)(2,1)S(1)}, bf16[32,1408]{1,0:T(8,128)(2,1)S(1)}, u32[]{:S(2)}, u32[]{:S(2)}) collective-permute-start(bf16[32,1408]{1,0:T(8,128)(2,1)S(1)} %get-tuple-element.76), channel_id=1, source_target_pairs={{0,8},{4,12},{8,0},{12,4},{1,9},{5,13},{9,1},{13,5},{2,10},{6,14},... | collective-permute-start | bytes 270344 | tf_op jit(solution)/shard_map/ppermute | solution.py:297
  51.5 1.3 %collective-permute-start.19 = (bf16[32,1408]{1,0:T(8,128)(2,1)S(1)}, bf16[32,1408]{1,0:T(8,128)(2,1)S(1)}, u32[]{:S(2)}, u32[]{:S(2)}) collective-permute-start(bf16[32,1408]{1,0:T(8,128)(2,1)S(1)} %get-tuple-element.76), channel_id=1, source_target_pairs={{0,12},{4,8},{8,4},{12,0},{1,13},{5,9},{9,5},{13,1},{2,14},{6,10},... | collective-permute-start | bytes 270344 | tf_op jit(solution)/shard_map/ppermute | solution.py:297
  52.8 0.8 collective-permute-done.17
  53.6 1.5 %collective-permute-start.23 = (bf16[32,1408]{1,0:T(8,128)(2,1)S(1)}, bf16[32,1408]{1,0:T(8,128)(2,1)S(1)}, u32[]{:S(2)}, u32[]{:S(2)}) collective-permute-start(bf16[32,1408]{1,0:T(8,128)(2,1)S(1)} %collective-permute-done.17), channel_id=1, source_target_pairs={{0,2},{1,3},{2,0},{3,1},{4,6},{5,7},{6,4},{7,5},{8,10},{9,11},{10,... | collective-permute-start | bytes 270344 | tf_op jit(solution)/shard_map/ppermute | solution.py:297
  55.2 3.3 %collective-permute-done.18 = bf16[32,1408]{1,0:T(8,128)(2,1)S(1)} collective-permute-done((bf16[32,1408]{1,0:T(8,128)(2,1)S(1)}, bf16[32,1408]{1,0:T(8,128)(2,1)S(1)}, u32[]{:S(2)}, u32[]{:S(2)}) %collective-permute-start.18) | collective-permute-done | bytes 90144 | tf_op jit(solution)/shard_map/ppermute | solution.py:297
  58.5 1.5 %collective-permute-start.24 = (bf16[32,1408]{1,0:T(8,128)(2,1)S(1)}, bf16[32,1408]{1,0:T(8,128)(2,1)S(1)}, u32[]{:S(2)}, u32[]{:S(2)}) collective-permute-start(bf16[32,1408]{1,0:T(8,128)(2,1)S(1)} %collective-permute-done.18), channel_id=1, source_target_pairs={{0,2},{1,3},{2,0},{3,1},{4,6},{5,7},{6,4},{7,5},{8,10},{9,11},{10,... | collective-permute-start | bytes 270344 | tf_op jit(solution)/shard_map/ppermute | solution.py:297
  60.6 2.4 %collective-permute-done.24 = bf16[32,1408]{1,0:T(8,128)(2,1)S(1)} collective-permute-done((bf16[32,1408]{1,0:T(8,128)(2,1)S(1)}, bf16[32,1408]{1,0:T(8,128)(2,1)S(1)}, u32[]{:S(2)}, u32[]{:S(2)}) %collective-permute-start.24) | collective-permute-done | bytes 90144 | tf_op jit(solution)/shard_map/ppermute | solution.py:297
  63.0 1.5 %collective-permute-done.25 = bf16[32,1408]{1,0:T(8,128)(2,1)S(1)} collective-permute-done((bf16[32,1408]{1,0:T(8,128)(2,1)S(1)}, bf16[32,1408]{1,0:T(8,128)(2,1)S(1)}, u32[]{:S(2)}, u32[]{:S(2)}) %collective-permute-start.25) | collective-permute-done | bytes 90144 | tf_op jit(solution)/shard_map/ppermute | solution.py:297
  65.2 1.1 %collective-permute-done.26.partner_ref = bf16[128,1408]{1,0:T(8,128)(2,1)S(1)} collective-permute-done((bf16[128,1408]{1,0:T(8,128)(2,1)S(1)}, bf16[128,1408]{1,0:T(8,128)(2,1)S(1)}, u32[]{:S(2)}, u32[]{:S(2)}) %collective-permute-start.26) | collective-permute-done | bytes 360480 | tf_op jit(solution)/shard_map/ppermute | solution.py:297
  66.3 2.4 %experts.3 = (bf16[128,1344]{1,0:T(8,128)(2,1)S(1)}, bf16[128,1344]{1,0:T(8,128)(2,1)S(1)}) custom-call(s32[3]{0:T(128)S(1)} %pad_add_fusion.place_ref, bf16[1,928,1344]{2,1,0:T(8,128)(2,1)S(1)} %get-tuple-element.74.up_ref, bf16[1,928,1344]{2,1,0:T(8,128)(2,1)S(1)} %get-tuple-element.75.down_ref, ...), custom_call_target="tpu_custom_call" | custom-call | flops 2147483648 | bytes 8388608 | tf_op jit(solution)/shard_map/experts/pallas_call | solution.py:29
  68.9 2.4 %experts.2 = (bf16[128,1344]{1,0:T(8,128)(2,1)S(1)}, bf16[128,1344]{1,0:T(8,128)(2,1)S(1)}) custom-call(s32[3]{0:T(128)S(1)} %pad_add_fusion.place_ref, bf16[1,928,1344]{2,1,0:T(8,128)(2,1)S(1)} %get-tuple-element.74.up_ref, bf16[1,928,1344]{2,1,0:T(8,128)(2,1)S(1)} %get-tuple-element.75.down_ref, ...), custom_call_target="tpu_custom_call" | custom-call | flops 2147483648 | bytes 8388608 | tf_op jit(solution)/shard_map/experts/pallas_call | solution.py:29
  71.8 1.0 %collective-permute-start.32 = (bf16[32,1344]{1,0:T(8,128)(2,1)S(1)}, bf16[32,1344]{1,0:T(8,128)(2,1)S(1)}, u32[]{:S(2)}, u32[]{:S(2)}) collective-permute-start(bf16[32,1344]{1,0:T(8,128)(2,1)S(1)} %get-tuple-element.83), channel_id=1, source_target_pairs={{0,2},{1,3},{2,0},{3,1},{4,6},{5,7},{6,4},{7,5},{8,10},{9,11},{10,... | collective-permute-start | bytes 258056 | tf_op jit(solution)/shard_map/ppermute | solution.py:297
  72.8 1.1 %collective-permute-start.30 = (bf16[32,1344]{1,0:T(8,128)(2,1)S(1)}, bf16[32,1344]{1,0:T(8,128)(2,1)S(1)}, u32[]{:S(2)}, u32[]{:S(2)}) collective-permute-start(bf16[32,1344]{1,0:T(8,128)(2,1)S(1)} %get-tuple-element.82), channel_id=1, source_target_pairs={{0,2},{1,3},{2,0},{3,1},{4,6},{5,7},{6,4},{7,5},{8,10},{9,11},{10,... | collective-permute-start | bytes 258056 | tf_op jit(solution)/shard_map/ppermute | solution.py:297
  73.9 1.0 %collective-permute-start.28 = (bf16[32,1344]{1,0:T(8,128)(2,1)S(1)}, bf16[32,1344]{1,0:T(8,128)(2,1)S(1)}, u32[]{:S(2)}, u32[]{:S(2)}) collective-permute-start(bf16[32,1344]{1,0:T(8,128)(2,1)S(1)} %get-tuple-element.81), channel_id=1, source_target_pairs={{0,2},{1,3},{2,0},{3,1},{4,6},{5,7},{6,4},{7,5},{8,10},{9,11},{10,... | collective-permute-start | bytes 258056 | tf_op jit(solution)/shard_map/ppermute | solution.py:297
  74.8 1.0 %collective-permute-start.34 = (bf16[32,1344]{1,0:T(8,128)(2,1)S(1)}, bf16[32,1344]{1,0:T(8,128)(2,1)S(1)}, u32[]{:S(2)}, u32[]{:S(2)}) collective-permute-start(bf16[32,1344]{1,0:T(8,128)(2,1)S(1)} %get-tuple-element.84), channel_id=1, source_target_pairs={{0,2},{1,3},{2,0},{3,1},{4,6},{5,7},{6,4},{7,5},{8,10},{9,11},{10,... | collective-permute-start | bytes 258056 | tf_op jit(solution)/shard_map/ppermute | solution.py:297
  75.9 1.4 %collective-permute-done.32.rest_0_ = bf16[32,1344]{1,0:T(8,128)(2,1)S(1)} collective-permute-done((bf16[32,1344]{1,0:T(8,128)(2,1)S(1)}, bf16[32,1344]{1,0:T(8,128)(2,1)S(1)}, u32[]{:S(2)}, u32[]{:S(2)}) %collective-permute-start.32) | collective-permute-done | bytes 86048 | tf_op jit(solution)/shard_map/ppermute | solution.py:297
  77.4 1.8 %collective-permute-done.30.rest_0_ = bf16[32,1344]{1,0:T(8,128)(2,1)S(1)} collective-permute-done((bf16[32,1344]{1,0:T(8,128)(2,1)S(1)}, bf16[32,1344]{1,0:T(8,128)(2,1)S(1)}, u32[]{:S(2)}, u32[]{:S(2)}) %collective-permute-start.30) | collective-permute-done | bytes 86048 | tf_op jit(solution)/shard_map/ppermute | solution.py:297
  79.3 0.8 collective-permute-start.31
  80.1 1.0 %collective-permute-done.28.rest_0_ = bf16[32,1344]{1,0:T(8,128)(2,1)S(1)} collective-permute-done((bf16[32,1344]{1,0:T(8,128)(2,1)S(1)}, bf16[32,1344]{1,0:T(8,128)(2,1)S(1)}, u32[]{:S(2)}, u32[]{:S(2)}) %collective-permute-start.28) | collective-permute-done | bytes 86048 | tf_op jit(solution)/shard_map/ppermute | solution.py:297
  81.2 2.1 %collective-permute-start.29 = (bf16[32,1344]{1,0:T(8,128)(2,1)S(1)}, bf16[32,1344]{1,0:T(8,128)(2,1)S(1)}, u32[]{:S(2)}, u32[]{:S(2)}) collective-permute-start(bf16[32,1344]{1,0:T(8,128)(2,1)S(1)} %piece.4), channel_id=1, source_target_pairs={{0,12},{4,8},{8,4},{12,0},{1,13},{5,9},{9,5},{13,1},{2,14},{6,10},... | collective-permute-start | bytes 258056 | tf_op jit(solution)/shard_map/ppermute | solution.py:297
  83.4 4.5 %collective-permute-done.31.rest_1_ = bf16[32,1344]{1,0:T(8,128)(2,1)S(1)} collective-permute-done((bf16[32,1344]{1,0:T(8,128)(2,1)S(1)}, bf16[32,1344]{1,0:T(8,128)(2,1)S(1)}, u32[]{:S(2)}, u32[]{:S(2)}) %collective-permute-start.31) | collective-permute-done | bytes 86048 | tf_op jit(solution)/shard_map/ppermute | solution.py:297
  87.8 0.7 last.1
  (84 shorter events, 9.8 us)
Async XLA Ops:
  0.1 1.0 %copy-start.3 = (bf16[128,1024]{1,0:T(8,128)(2,1)S(1)}, bf16[128,1024]{1,0:T(8,128)(2,1)}, u32[]{:S(2)}) copy-start(bf16[128,1024]{1,0:T(8,128)(2,1)} %x_hbm.3) | copy-start | bytes 786436
  1.0 0.8 copy-start.6
  5.0 4.9 %collective-permute-start = (bf16[1,144,128]{2,1,0:T(8,128)(2,1)S(1)}, bf16[1,144,128]{2,1,0:T(8,128)(2,1)S(1)}, u32[]{:S(2)}, u32[]{:S(2)}) collective-permute-start(bf16[1,144,128]{2,1,0:T(8,128)(2,1)S(1)} %get-tuple-element.54), channel_id=1, source_target_pairs={{0,1},{1,0},{2,3},{3,2},{16,17},{17,16},{18,19},{19,18},{4,5},{5,4... | collective-permute-start | bytes 110600 | tf_op jit(solution)/shard_map/ppermute | solution.py:297
  5.5 7.0 %collective-permute-start.1 = (bf16[1,144,128]{2,1,0:T(8,128)(2,1)S(1)}, bf16[1,144,128]{2,1,0:T(8,128)(2,1)S(1)}, u32[]{:S(2)}, u32[]{:S(2)}) collective-permute-start(bf16[1,144,128]{2,1,0:T(8,128)(2,1)S(1)} %get-tuple-element.55), channel_id=1, source_target_pairs={{0,2},{1,3},{2,0},{3,1},{16,18},{17,19},{18,16},{19,17},{4,6},{5,7... | collective-permute-start | bytes 110600 | tf_op jit(solution)/shard_map/ppermute | solution.py:297
  8.1 4.6 %collective-permute-start.2 = (bf16[1,144,128]{2,1,0:T(8,128)(2,1)S(1)}, bf16[1,144,128]{2,1,0:T(8,128)(2,1)S(1)}, u32[]{:S(2)}, u32[]{:S(2)}) collective-permute-start(bf16[1,144,128]{2,1,0:T(8,128)(2,1)S(1)} %get-tuple-element.56), channel_id=1, source_target_pairs={{0,3},{1,2},{2,1},{3,0},{16,19},{17,18},{18,17},{19,16},{4,7},{5,6... | collective-permute-start | bytes 110600 | tf_op jit(solution)/shard_map/ppermute | solution.py:297
  8.2 4.5 %collective-permute-start.3 = (bf16[1,144,128]{2,1,0:T(8,128)(2,1)S(1)}, bf16[1,144,128]{2,1,0:T(8,128)(2,1)S(1)}, u32[]{:S(2)}, u32[]{:S(2)}) collective-permute-start(bf16[1,144,128]{2,1,0:T(8,128)(2,1)S(1)} %get-tuple-element.57), channel_id=1, source_target_pairs={{0,16},{1,17},{2,18},{3,19},{16,0},{17,1},{18,2},{19,3},{4,20},{5,... | collective-permute-start | bytes 110600 | tf_op jit(solution)/shard_map/ppermute | solution.py:297
  9.9 3.5 %collective-permute-start.4 = (bf16[1,144,128]{2,1,0:T(8,128)(2,1)S(1)}, bf16[1,144,128]{2,1,0:T(8,128)(2,1)S(1)}, u32[]{:S(2)}, u32[]{:S(2)}) collective-permute-start(bf16[1,144,128]{2,1,0:T(8,128)(2,1)S(1)} %get-tuple-element.58), channel_id=1, source_target_pairs={{0,17},{1,16},{2,19},{3,18},{16,1},{17,0},{18,3},{19,2},{4,21},{5,... | collective-permute-start | bytes 110600 | tf_op jit(solution)/shard_map/ppermute | solution.py:297
  9.9 5.5 %collective-permute-start.5 = (bf16[1,144,128]{2,1,0:T(8,128)(2,1)S(1)}, bf16[1,144,128]{2,1,0:T(8,128)(2,1)S(1)}, u32[]{:S(2)}, u32[]{:S(2)}) collective-permute-start(bf16[1,144,128]{2,1,0:T(8,128)(2,1)S(1)} %get-tuple-element.59), channel_id=1, source_target_pairs={{0,18},{1,19},{2,16},{3,17},{16,2},{17,3},{18,0},{19,1},{4,22},{5,... | collective-permute-start | bytes 110600 | tf_op jit(solution)/shard_map/ppermute | solution.py:297
  12.5 4.3 %collective-permute-start.6 = (bf16[1,144,128]{2,1,0:T(8,128)(2,1)S(1)}, bf16[1,144,128]{2,1,0:T(8,128)(2,1)S(1)}, u32[]{:S(2)}, u32[]{:S(2)}) collective-permute-start(bf16[1,144,128]{2,1,0:T(8,128)(2,1)S(1)} %get-tuple-element.60), channel_id=1, source_target_pairs={{0,19},{1,18},{2,17},{3,16},{16,3},{17,2},{18,1},{19,0},{4,23},{5,... | collective-permute-start | bytes 110600 | tf_op jit(solution)/shard_map/ppermute | solution.py:297
  17.5 4.6 %collective-permute-start.10 = (bf16[1,128,128]{2,1,0:T(8,128)(2,1)S(1)}, bf16[1,128,128]{2,1,0:T(8,128)(2,1)S(1)}, u32[]{:S(2)}, u32[]{:S(2)}) collective-permute-start(bf16[1,128,128]{2,1,0:T(8,128)(2,1)S(1)} %get-tuple-element.65), channel_id=1, source_target_pairs={{0,16},{1,17},{2,18},{3,19},{16,0},{17,1},{18,2},{19,3},{4,20},{5,... | collective-permute-start | bytes 98312 | tf_op jit(solution)/shard_map/ppermute | solution.py:297
  18.1 4.6 %collective-permute-start.11 = (bf16[1,128,128]{2,1,0:T(8,128)(2,1)S(1)}, bf16[1,128,128]{2,1,0:T(8,128)(2,1)S(1)}, u32[]{:S(2)}, u32[]{:S(2)}) collective-permute-start(bf16[1,128,128]{2,1,0:T(8,128)(2,1)S(1)} %get-tuple-element.66), channel_id=1, source_target_pairs={{0,17},{1,16},{2,19},{3,18},{16,1},{17,0},{18,3},{19,2},{4,21},{5,... | collective-permute-start | bytes 98312 | tf_op jit(solution)/shard_map/ppermute | solution.py:297
  19.1 14.8 %collective-permute-start.12 = (bf16[1,128,128]{2,1,0:T(8,128)(2,1)S(1)}, bf16[1,128,128]{2,1,0:T(8,128)(2,1)S(1)}, u32[]{:S(2)}, u32[]{:S(2)}) collective-permute-start(bf16[1,128,128]{2,1,0:T(8,128)(2,1)S(1)} %get-tuple-element.67), channel_id=1, source_target_pairs={{0,18},{1,19},{2,16},{3,17},{16,2},{17,3},{18,0},{19,1},{4,22},{5,... | collective-permute-start | bytes 98312 | tf_op jit(solution)/shard_map/ppermute | solution.py:297
  20.2 13.7 %collective-permute-start.13 = (bf16[1,128,128]{2,1,0:T(8,128)(2,1)S(1)}, bf16[1,128,128]{2,1,0:T(8,128)(2,1)S(1)}, u32[]{:S(2)}, u32[]{:S(2)}) collective-permute-start(bf16[1,128,128]{2,1,0:T(8,128)(2,1)S(1)} %get-tuple-element.68), channel_id=1, source_target_pairs={{0,19},{1,18},{2,17},{3,16},{16,3},{17,2},{18,1},{19,0},{4,23},{5,... | collective-permute-start | bytes 98312 | tf_op jit(solution)/shard_map/ppermute | solution.py:297
  22.0 11.9 %collective-permute-start.7 = (bf16[1,128,128]{2,1,0:T(8,128)(2,1)S(1)}, bf16[1,128,128]{2,1,0:T(8,128)(2,1)S(1)}, u32[]{:S(2)}, u32[]{:S(2)}) collective-permute-start(bf16[1,128,128]{2,1,0:T(8,128)(2,1)S(1)} %get-tuple-element.62), channel_id=1, source_target_pairs={{0,1},{1,0},{2,3},{3,2},{16,17},{17,16},{18,19},{19,18},{4,5},{5,4... | collective-permute-start | bytes 98312 | tf_op jit(solution)/shard_map/ppermute | solution.py:297
  22.2 11.7 %collective-permute-start.8 = (bf16[1,128,128]{2,1,0:T(8,128)(2,1)S(1)}, bf16[1,128,128]{2,1,0:T(8,128)(2,1)S(1)}, u32[]{:S(2)}, u32[]{:S(2)}) collective-permute-start(bf16[1,128,128]{2,1,0:T(8,128)(2,1)S(1)} %get-tuple-element.63), channel_id=1, source_target_pairs={{0,2},{1,3},{2,0},{3,1},{16,18},{17,19},{18,16},{19,17},{4,6},{5,7... | collective-permute-start | bytes 98312 | tf_op jit(solution)/shard_map/ppermute | solution.py:297
  22.7 11.2 %collective-permute-start.9 = (bf16[1,128,128]{2,1,0:T(8,128)(2,1)S(1)}, bf16[1,128,128]{2,1,0:T(8,128)(2,1)S(1)}, u32[]{:S(2)}, u32[]{:S(2)}) collective-permute-start(bf16[1,128,128]{2,1,0:T(8,128)(2,1)S(1)} %get-tuple-element.64), channel_id=1, source_target_pairs={{0,3},{1,2},{2,1},{3,0},{16,19},{17,18},{18,17},{19,16},{4,7},{5,6... | collective-permute-start | bytes 98312 | tf_op jit(solution)/shard_map/ppermute | solution.py:297
  23.9 1.8 %copy-start = (bf16[1024,1344]{0,1:T(8,128)(2,1)S(1)}, bf16[1024,1344]{0,1:T(8,128)(2,1)}, u32[]{:S(2)}) copy-start(bf16[1024,1344]{0,1:T(8,128)(2,1)} %param.23) | copy-start | bytes 8257540
  25.6 0.9 %copy-start.4 = (bf16[128,1024]{1,0:T(8,128)(2,1)S(1)}, bf16[128,1024]{1,0:T(8,128)(2,1)}, u32[]{:S(2)}) copy-start(bf16[128,1024]{1,0:T(8,128)(2,1)} %x_hbm.3) | copy-start | bytes 786436
  26.6 0.9 %copy-start.5 = (bf16[128,1024]{1,0:T(8,128)(2,1)S(1)}, bf16[128,1024]{1,0:T(8,128)(2,1)}, u32[]{:S(2)}) copy-start(bf16[128,1024]{1,0:T(8,128)(2,1)} %z_hbm.1) | copy-start | bytes 786436
  27.5 0.8 copy-start.7
  28.4 0.8 copy-start.9
  31.9 8.4 %copy-start.2 = (bf16[1,928,1344]{2,1,0:T(8,128)(2,1)S(1)}, bf16[1,928,1344]{2,1,0:T(8,128)(2,1)}, u32[]{:S(2)}) copy-start(bf16[1,928,1344]{2,1,0:T(8,128)(2,1)} %down_hbm.1) | copy-start | bytes 7483396
  33.8 6.5 %copy-start.18 = (f32[1344]{0:T(1024)S(1)}, f32[1344]{0:T(1024)}, u32[]{:S(2)}) copy-start(f32[1344]{0:T(1024)} %param.27) | copy-start | bytes 16132
  33.8 6.5 %copy-start.1 = (bf16[1,1344,928]{1,2,0:T(8,128)(2,1)S(1)}, bf16[1,1344,928]{1,2,0:T(8,128)(2,1)}, u32[]{:S(2)}) copy-start(bf16[1,1344,928]{1,2,0:T(8,128)(2,1)} %param.28) | copy-start | bytes 7483396
  33.8 6.5 %copy-start.8 = (bf16[1,32,1344]{2,1,0:T(8,128)(2,1)S(1)}, bf16[1,32,1344]{2,1,0:T(8,128)(2,1)}, u32[]{:S(2)}) copy-start(bf16[1,32,1344]{2,1,0:T(8,128)(2,1)} %resid_hbm.1) | copy-start | bytes 258052
  33.8 6.5 %copy-start.13 = (s32[1,32,6]{1,0,2:T(1,128)S(1)}, s32[1,32,6]{1,0,2:T(1,128)}, u32[]{:S(2)}) copy-start(s32[1,32,6]{1,0,2:T(1,128)} %param.25) | copy-start | bytes 2308
  33.9 6.5 %copy-start.14 = (f32[1,32,6]{1,0,2:T(1,128)S(1)}, f32[1,32,6]{1,0,2:T(1,128)}, u32[]{:S(2)}) copy-start(f32[1,32,6]{1,0,2:T(1,128)} %param.26) | copy-start | bytes 2308
  35.8 7.4 %collective-permute-start.14 = (bf16[32,1344]{1,0:T(8,128)(2,1)S(1)}, bf16[32,1344]{1,0:T(8,128)(2,1)S(1)}, u32[]{:S(2)}, u32[]{:S(2)}) collective-permute-start(bf16[32,1344]{1,0:T(8,128)(2,1)S(1)} %get-tuple-element.70), channel_id=1, source_target_pairs={{0,12},{4,8},{8,4},{12,0},{1,13},{5,9},{9,5},{13,1},{2,14},{6,10},... | collective-permute-start | bytes 258056 | tf_op jit(solution)/shard_map/ppermute | solution.py:297
  39.5 8.2 %collective-permute-start.15 = (bf16[32,1344]{1,0:T(8,128)(2,1)S(1)}, bf16[32,1344]{1,0:T(8,128)(2,1)S(1)}, u32[]{:S(2)}, u32[]{:S(2)}) collective-permute-start(bf16[32,1344]{1,0:T(8,128)(2,1)S(1)} %get-tuple-element.71), channel_id=1, source_target_pairs={{0,8},{4,12},{8,0},{12,4},{1,9},{5,13},{9,1},{13,5},{2,10},{6,14},... | collective-permute-start | bytes 258056 | tf_op jit(solution)/shard_map/ppermute | solution.py:297
  39.5 8.2 %collective-permute-start.16 = (bf16[32,1344]{1,0:T(8,128)(2,1)S(1)}, bf16[32,1344]{1,0:T(8,128)(2,1)S(1)}, u32[]{:S(2)}, u32[]{:S(2)}) collective-permute-start(bf16[32,1344]{1,0:T(8,128)(2,1)S(1)} %get-tuple-element.72), channel_id=1, source_target_pairs={{0,4},{4,0},{8,12},{12,8},{1,5},{5,1},{9,13},{13,9},{2,6},{6,2},{1... | collective-permute-start | bytes 258056 | tf_op jit(solution)/shard_map/ppermute | solution.py:297
  47.8 5.0 %collective-permute-start.22 = (bf16[32,1408]{1,0:T(8,128)(2,1)S(1)}, bf16[32,1408]{1,0:T(8,128)(2,1)S(1)}, u32[]{:S(2)}, u32[]{:S(2)}) collective-permute-start(bf16[32,1408]{1,0:T(8,128)(2,1)S(1)} %get-tuple-element.76), channel_id=1, source_target_pairs={{0,2},{1,3},{2,0},{3,1},{4,6},{5,7},{6,4},{7,5},{8,10},{9,11},{10,... | collective-permute-start | bytes 270344 | tf_op jit(solution)/shard_map/ppermute | solution.py:297
  48.4 5.2 %collective-permute-start.17 = (bf16[32,1408]{1,0:T(8,128)(2,1)S(1)}, bf16[32,1408]{1,0:T(8,128)(2,1)S(1)}, u32[]{:S(2)}, u32[]{:S(2)}) collective-permute-start(bf16[32,1408]{1,0:T(8,128)(2,1)S(1)} %get-tuple-element.76), channel_id=1, source_target_pairs={{0,4},{4,0},{8,12},{12,8},{1,5},{5,1},{9,13},{13,9},{2,6},{6,2},{1... | collective-permute-start | bytes 270344 | tf_op jit(solution)/shard_map/ppermute | solution.py:297
  49.1 9.4 %collective-permute-start.18 = (bf16[32,1408]{1,0:T(8,128)(2,1)S(1)}, bf16[32,1408]{1,0:T(8,128)(2,1)S(1)}, u32[]{:S(2)}, u32[]{:S(2)}) collective-permute-start(bf16[32,1408]{1,0:T(8,128)(2,1)S(1)} %get-tuple-element.76), channel_id=1, source_target_pairs={{0,8},{4,12},{8,0},{12,4},{1,9},{5,13},{9,1},{13,5},{2,10},{6,14},... | collective-permute-start | bytes 270344 | tf_op jit(solution)/shard_map/ppermute | solution.py:297
  51.5 8.5 %collective-permute-start.19 = (bf16[32,1408]{1,0:T(8,128)(2,1)S(1)}, bf16[32,1408]{1,0:T(8,128)(2,1)S(1)}, u32[]{:S(2)}, u32[]{:S(2)}) collective-permute-start(bf16[32,1408]{1,0:T(8,128)(2,1)S(1)} %get-tuple-element.76), channel_id=1, source_target_pairs={{0,12},{4,8},{8,4},{12,0},{1,13},{5,9},{9,5},{13,1},{2,14},{6,10},... | collective-permute-start | bytes 270344 | tf_op jit(solution)/shard_map/ppermute | solution.py:297
  53.6 6.9 %collective-permute-start.23 = (bf16[32,1408]{1,0:T(8,128)(2,1)S(1)}, bf16[32,1408]{1,0:T(8,128)(2,1)S(1)}, u32[]{:S(2)}, u32[]{:S(2)}) collective-permute-start(bf16[32,1408]{1,0:T(8,128)(2,1)S(1)} %collective-permute-done.17), channel_id=1, source_target_pairs={{0,2},{1,3},{2,0},{3,1},{4,6},{5,7},{6,4},{7,5},{8,10},{9,11},{10,... | collective-permute-start | bytes 270344 | tf_op jit(solution)/shard_map/ppermute | solution.py:297
  58.5 4.5 %collective-permute-start.24 = (bf16[32,1408]{1,0:T(8,128)(2,1)S(1)}, bf16[32,1408]{1,0:T(8,128)(2,1)S(1)}, u32[]{:S(2)}, u32[]{:S(2)}) collective-permute-start(bf16[32,1408]{1,0:T(8,128)(2,1)S(1)} %collective-permute-done.18), channel_id=1, source_target_pairs={{0,2},{1,3},{2,0},{3,1},{4,6},{5,7},{6,4},{7,5},{8,10},{9,11},{10,... | collective-permute-start | bytes 270344 | tf_op jit(solution)/shard_map/ppermute | solution.py:297
  60.0 4.5 %collective-permute-start.25 = (bf16[32,1408]{1,0:T(8,128)(2,1)S(1)}, bf16[32,1408]{1,0:T(8,128)(2,1)S(1)}, u32[]{:S(2)}, u32[]{:S(2)}) collective-permute-start(bf16[32,1408]{1,0:T(8,128)(2,1)S(1)} %collective-permute-done.19), channel_id=1, source_target_pairs={{0,2},{1,3},{2,0},{3,1},{4,6},{5,7},{6,4},{7,5},{8,10},{9,11},{10,... | collective-permute-start | bytes 270344 | tf_op jit(solution)/shard_map/ppermute | solution.py:297
  64.5 1.7 %collective-permute-start.26 = (bf16[128,1408]{1,0:T(8,128)(2,1)S(1)}, bf16[128,1408]{1,0:T(8,128)(2,1)S(1)}, u32[]{:S(2)}, u32[]{:S(2)}) collective-permute-start(bf16[128,1408]{1,0:T(8,128)(2,1)S(1)} %constant_dynamic-update-slice_fusion.4.mine_ref), channel_id=1, source_target_pairs={{0,1},{1,0},{2,3},{3,2},{4,5},{5,4},{6,7},{7,6},{8,9},{9,8},{10,11... | collective-permute-start | bytes 1081352 | tf_op jit(solution)/shard_map/ppermute | solution.py:297
  64.6 4.2 %collective-permute-start.20 = (bf16[128,1408]{1,0:T(8,128)(2,1)S(1)}, bf16[128,1408]{1,0:T(8,128)(2,1)S(1)}, u32[]{:S(2)}, u32[]{:S(2)}) collective-permute-start(bf16[128,1408]{1,0:T(8,128)(2,1)S(1)} %constant_dynamic-update-slice_fusion.mine_ref), channel_id=1, source_target_pairs={{0,1},{1,0},{2,3},{3,2},{4,5},{5,4},{6,7},{7,6},{8,9},{9,8},{10,11... | collective-permute-start | bytes 1081352 | tf_op jit(solution)/shard_map/ppermute | solution.py:297
  68.7 3.0 %collective-permute-start.27 = (bf16[128,1344]{1,0:T(8,128)(2,1)S(1)}, bf16[128,1344]{1,0:T(8,128)(2,1)S(1)}, u32[]{:S(2)}, u32[]{:S(2)}) collective-permute-start(bf16[128,1344]{1,0:T(8,128)(2,1)S(1)} %get-tuple-element.80), channel_id=1, source_target_pairs={{0,1},{1,0},{2,3},{3,2},{4,5},{5,4},{6,7},{7,6},{8,9},{9,8},{10,11... | collective-permute-start | bytes 1032200 | tf_op jit(solution)/shard_map/ppermute | solution.py:297
  71.2 4.7 %collective-permute-start.21 = (bf16[128,1344]{1,0:T(8,128)(2,1)S(1)}, bf16[128,1344]{1,0:T(8,128)(2,1)S(1)}, u32[]{:S(2)}, u32[]{:S(2)}) collective-permute-start(bf16[128,1344]{1,0:T(8,128)(2,1)S(1)} %get-tuple-element.78), channel_id=1, source_target_pairs={{0,1},{1,0},{2,3},{3,2},{4,5},{5,4},{6,7},{7,6},{8,9},{9,8},{10,11... | collective-permute-start | bytes 1032200 | tf_op jit(solution)/shard_map/ppermute | solution.py:297
  71.8 5.5 %collective-permute-start.32 = (bf16[32,1344]{1,0:T(8,128)(2,1)S(1)}, bf16[32,1344]{1,0:T(8,128)(2,1)S(1)}, u32[]{:S(2)}, u32[]{:S(2)}) collective-permute-start(bf16[32,1344]{1,0:T(8,128)(2,1)S(1)} %get-tuple-element.83), channel_id=1, source_target_pairs={{0,2},{1,3},{2,0},{3,1},{4,6},{5,7},{6,4},{7,5},{8,10},{9,11},{10,... | collective-permute-start | bytes 258056 | tf_op jit(solution)/shard_map/ppermute | solution.py:297
  72.8 6.4 %collective-permute-start.30 = (bf16[32,1344]{1,0:T(8,128)(2,1)S(1)}, bf16[32,1344]{1,0:T(8,128)(2,1)S(1)}, u32[]{:S(2)}, u32[]{:S(2)}) collective-permute-start(bf16[32,1344]{1,0:T(8,128)(2,1)S(1)} %get-tuple-element.82), channel_id=1, source_target_pairs={{0,2},{1,3},{2,0},{3,1},{4,6},{5,7},{6,4},{7,5},{8,10},{9,11},{10,... | collective-permute-start | bytes 258056 | tf_op jit(solution)/shard_map/ppermute | solution.py:297
  73.9 7.3 %collective-permute-start.28 = (bf16[32,1344]{1,0:T(8,128)(2,1)S(1)}, bf16[32,1344]{1,0:T(8,128)(2,1)S(1)}, u32[]{:S(2)}, u32[]{:S(2)}) collective-permute-start(bf16[32,1344]{1,0:T(8,128)(2,1)S(1)} %get-tuple-element.81), channel_id=1, source_target_pairs={{0,2},{1,3},{2,0},{3,1},{4,6},{5,7},{6,4},{7,5},{8,10},{9,11},{10,... | collective-permute-start | bytes 258056 | tf_op jit(solution)/shard_map/ppermute | solution.py:297
  74.8 8.5 %collective-permute-start.34 = (bf16[32,1344]{1,0:T(8,128)(2,1)S(1)}, bf16[32,1344]{1,0:T(8,128)(2,1)S(1)}, u32[]{:S(2)}, u32[]{:S(2)}) collective-permute-start(bf16[32,1344]{1,0:T(8,128)(2,1)S(1)} %get-tuple-element.84), channel_id=1, source_target_pairs={{0,2},{1,3},{2,0},{3,1},{4,6},{5,7},{6,4},{7,5},{8,10},{9,11},{10,... | collective-permute-start | bytes 258056 | tf_op jit(solution)/shard_map/ppermute | solution.py:297
  77.3 6.0 %collective-permute-start.33 = (bf16[32,1344]{1,0:T(8,128)(2,1)S(1)}, bf16[32,1344]{1,0:T(8,128)(2,1)S(1)}, u32[]{:S(2)}, u32[]{:S(2)}) collective-permute-start(bf16[32,1344]{1,0:T(8,128)(2,1)S(1)} %piece.6), channel_id=1, source_target_pairs={{0,4},{4,0},{8,12},{12,8},{1,5},{5,1},{9,13},{13,9},{2,6},{6,2},{1... | collective-permute-start | bytes 258056 | tf_op jit(solution)/shard_map/ppermute | solution.py:297
  79.3 8.6 %collective-permute-start.31 = (bf16[32,1344]{1,0:T(8,128)(2,1)S(1)}, bf16[32,1344]{1,0:T(8,128)(2,1)S(1)}, u32[]{:S(2)}, u32[]{:S(2)}) collective-permute-start(bf16[32,1344]{1,0:T(8,128)(2,1)S(1)} %piece.5), channel_id=1, source_target_pairs={{0,8},{4,12},{8,0},{12,4},{1,9},{5,13},{9,1},{13,5},{2,10},{6,14},... | collective-permute-start | bytes 258056 | tf_op jit(solution)/shard_map/ppermute | solution.py:297
  81.2 6.6 %collective-permute-start.29 = (bf16[32,1344]{1,0:T(8,128)(2,1)S(1)}, bf16[32,1344]{1,0:T(8,128)(2,1)S(1)}, u32[]{:S(2)}, u32[]{:S(2)}) collective-permute-start(bf16[32,1344]{1,0:T(8,128)(2,1)S(1)} %piece.4), channel_id=1, source_target_pairs={{0,12},{4,8},{8,4},{12,0},{1,13},{5,9},{9,5},{13,1},{2,14},{6,10},... | collective-permute-start | bytes 258056 | tf_op jit(solution)/shard_map/ppermute | solution.py:297
  (6 other events, 4.0 us)

commit v3 on v2

--- a/solution.py
+++ b/solution.py
@@ -16,6 +16,7 @@
 BF16 = jnp.bfloat16
 HBM = pl.BlockSpec(memory_space=pltpu.HBM)
 VMEM = pl.BlockSpec(memory_space=pltpu.VMEM)
+ANY = pl.BlockSpec(memory_space=pl.ANY)
 SMEM = pl.BlockSpec(memory_space=pltpu.SMEM)
 NT = (((1,), (1,)), ((), ()))
 
@@ -66,8 +67,21 @@
     return jnp.where(lane < HEAD_DIM, left, right)
 
 
-def state_kernel(place_ref, x_hbm, b_hbm, dt_hbm, a_hbm, *rest):
-    outs, (x_ref, b_ref, dt_ref, a_ref, packed_ref, sems) = rest[:-6], rest[-6:]
+def unpacked(block):
+    block = block.astype(F32)
+    return block[:, STATE : STATE + 1, :] + block[:, STATE + 1 : STATE + 2, :], block[:, 0:STATE, :]
+
+
+def pack(ref, total, state):
+    ref[:, 0:STATE, :] = state.astype(BF16)
+    wide = jnp.broadcast_to(total, (ref.shape[0], TILE, LANES))
+    high = wide.astype(BF16).astype(F32)
+    row = lax.broadcasted_iota(jnp.int32, wide.shape, 1)
+    ref[:, STATE : STATE + TILE, :] = jnp.where(row == 0, high, wide - high).astype(BF16)
+
+
+def state_kernel(place_ref, x_hbm, b_hbm, dt_hbm, a_hbm, keep_ref, send_ref, *scratch):
+    x_ref, b_ref, dt_ref, a_ref, packed_ref, sems = scratch
     loads = copies(sems, (dt_hbm, a_hbm, x_hbm, b_hbm), (dt_ref, a_ref, x_ref, b_ref))
     loads[0].wait()
     loads[1].wait()
@@ -86,25 +100,58 @@
             x_pair = x_ref[:, pair * LANES : (pair + 1) * LANES].astype(F32)
             weighted = (pair_lanes(tail, pair) * x_pair).astype(BF16)
             state = jnp.dot(turned, weighted, preferred_element_type=F32)
-            packed_ref[pair, 0:STATE, :] = state.astype(BF16)
-            wide = jnp.broadcast_to(pair_lanes(total, pair), (TILE, LANES))
-            high = wide.astype(BF16).astype(F32)
-            row = lax.broadcasted_iota(jnp.int32, (TILE, LANES), 0)
-            packed_ref[pair, STATE : STATE + TILE, :] = jnp.where(row == 0, high, wide - high).astype(BF16)
-    here = pairs // len(outs)
-    for shift, out in enumerate(outs):
-        out[...] = packed_ref[pl.ds((place_ref[2] ^ shift) * here, here)]
-
-
-def inside_kernel(x_hbm, z_hbm, b_hbm, c_hbm, dt_hbm, a_hbm, d_hbm, norm_hbm, w_hbm, *rest):
-    local_ref, grown_ref, c_ref, norm_ref, w_ref = rest[:5]
-    x_ref, z_ref, b_ref, dt_ref, a_ref, d_ref, sems = rest[5:]
+            pack(packed_ref.at[pair : pair + 1], pair_lanes(total, pair)[None], state[None])
+    half = pairs // 2
+    keep_ref[...] = packed_ref[pl.ds(place_ref[2] * half, half)]
+    send_ref[...] = packed_ref[pl.ds((1 - place_ref[2]) * half, half)]
+
+
+def chip_state_kernel(place_ref, keep_ref, got_ref, out_ref):
+    first = place_ref[2] == 0
+    keep, got = unpacked(keep_ref[...]), unpacked(got_ref[...])
+    early = [jnp.where(first, mine, other) for mine, other in zip(keep, got)]
+    late = [jnp.where(first, other, mine) for mine, other in zip(keep, got)]
+    pack(out_ref, early[0] + late[0], jnp.exp(late[0]) * early[1] + late[1])
+
+
+def span_kernel(place_ref, after_ref, *rest):
+    ins, out_ref, block_ref = rest[:-2], rest[-2], rest[-1]
+    for mask, part in enumerate(ins):
+        block_ref[place_ref[3] ^ mask] = part[...]
+    total, state = unpacked(block_ref[0])
+    for chip in range(1, len(ins)):
+        here, own = unpacked(block_ref[chip])
+        total, state = total + here, jnp.exp(here) * state + own
+    pack(out_ref, total, state)
+
+
+def before_kernel(chips, place_ref, after_ref, keep_ref, got_ref, *rest):
+    ins, (mine_ref, send_ref, chip_ref, part_ref) = rest[:-4], rest[-4:]
+    for mask in range(chips):
+        chip_ref[place_ref[3] ^ mask] = ins[mask][...]
+    parts = len(ins) - chips
+    for mask in range(parts):
+        part_ref[place_ref[4] ^ mask] = ins[chips + mask][...]
+    carry = jnp.zeros(mine_ref.shape, F32)
+    for ref, count, own in ((part_ref, parts, place_ref[4]), (chip_ref, chips, place_ref[3])):
+        for index in range(count - 1):
+            total, state = unpacked(ref[index])
+            carry = jnp.where(index < own, jnp.exp(total) * carry + state, carry)
+    first = place_ref[2] == 0
+    total, state = (jnp.where(first, k, g) for k, g in zip(unpacked(keep_ref[...]), unpacked(got_ref[...])))
+    later = jnp.exp(total) * carry + state
+    mine_ref[...] = jnp.where(first, carry, later).astype(BF16)
+    send_ref[...] = jnp.where(first, later, carry).astype(BF16)
+
+
+def inside_kernel(x_hbm, z_hbm, b_hbm, c_hbm, dt_hbm, a_hbm, d_hbm, local_ref, grown_ref, c_ref, *scratch):
+    x_ref, z_ref, b_ref, dt_ref, a_ref, d_ref, sems = scratch
     loads = copies(
         sems,
-        (dt_hbm, a_hbm, d_hbm, b_hbm, c_hbm, x_hbm, z_hbm, norm_hbm, w_hbm),
-        (dt_ref, a_ref, d_ref, b_ref, c_ref, x_ref, z_ref, norm_ref, w_ref),
-    )
-    for load in loads[:7]:
+        (dt_hbm, a_hbm, d_hbm, b_hbm, c_hbm, x_hbm, z_hbm),
+        (dt_ref, a_ref, d_ref, b_ref, c_ref, x_ref, z_ref),
+    )
+    for load in loads:
         load.wait()
     step_rows, cum_rows = decays(dt_ref[...], a_ref[...])
     cum = cum_rows.T
@@ -134,16 +181,14 @@
             gate = z / (1.0 + jnp.exp(-z))
             local_ref[:, at] = (inside + skip) * gate
             grown_ref[:, at] = pair_lanes(grown, pair) * gate
-    loads[7].wait()
-    loads[8].wait()
-
-
-def prep_kernel(experts, width, resid_hbm, routes_hbm, gates_hbm, gain_hbm, up_hbm, down_hbm, *rest):
-    gate_ref, resid_ref, gain_ref, up_ref, down_ref, routes_ref, gates_ref, sems = rest
+
+
+def prep_kernel(experts, width, resid_hbm, routes_hbm, gates_hbm, gain_hbm, norm_hbm, w_hbm, up_hbm, down_hbm, *rest):
+    gate_ref, resid_ref, gain_ref, norm_ref, w_ref, up_ref, down_ref, routes_ref, gates_ref, sems = rest
     loads = copies(
         sems,
-        (routes_hbm, gates_hbm, resid_hbm, gain_hbm, up_hbm, down_hbm),
-        (routes_ref, gates_ref, resid_ref, gain_ref, up_ref, down_ref),
+        (routes_hbm, gates_hbm, resid_hbm, gain_hbm, norm_hbm, w_hbm, up_hbm, down_hbm),
+        (routes_ref, gates_ref, resid_ref, gain_ref, norm_ref, w_ref, up_ref, down_ref),
     )
     loads[0].wait()
     loads[1].wait()
@@ -161,54 +206,12 @@
         load.wait()
 
 
-def chain_kernel(place_ref, *rest):
-    count = (len(rest) - 1) // 2
-    ins, outs, block_ref = rest[:count], rest[count : 2 * count], rest[-1]
-    for shift in range(count):
-        block_ref[place_ref[2] ^ shift] = ins[shift][...]
-    carry = jnp.zeros(outs[0].shape, F32)
-    for shard in range(count):
-        block = block_ref[shard].astype(F32)
-        block_ref[shard, :, 0:STATE, :] = carry.astype(BF16)
-        total = block[:, STATE : STATE + 1, :] + block[:, STATE + 1 : STATE + 2, :]
-        carry = jnp.exp(total) * carry + block[:, 0:STATE, :]
-    for shift in range(count):
-        outs[shift][...] = block_ref[place_ref[2] ^ shift, :, 0:STATE, :]
-
-
-def chain_over_seq(place, got):
-    mine = place[2]
-    count = len(got)
-    order = jnp.arange(count, dtype=jnp.int32) ^ mine
-    block = jnp.stack(got)[order].astype(F32)
-    totals = block[:, :, STATE : STATE + 1] + block[:, :, STATE + 1 : STATE + 2]
-
-    def walk(carry, item):
-        return (carry[0] + item[0], jnp.exp(item[0]) * carry[1] + item[1]), carry
-
-    zero = (jnp.zeros(totals.shape[1:], F32), jnp.zeros(block[0, :, :STATE].shape, F32))
-    span, inner = lax.scan(walk, zero, (totals, block[:, :, :STATE]))
-    everything = jax.tree.map(lambda part: lax.all_gather(part.astype(BF16), "seq").astype(F32), span)
-    unused, outer = lax.scan(walk, zero, everything)
-    chain = lax.dynamic_index_in_dim(outer[1], lax.axis_index("seq"), 0, keepdims=False)
-    before = (jnp.exp(inner[0]) * chain[None] + inner[1]).astype(BF16)[order]
-    return [before[shift] for shift in range(count)]
-
-
-def mixed_kernel(place_ref, local_ref, grown_ref, c_ref, norm_ref, w_ref, *rest):
-    normed_ref, state_ref = rest[-2:]
-    pairs = state_ref.shape[0]
-    befores, outs = [], []
-    held = 0
-    for ref in rest[:-2]:
-        if held < pairs:
-            befores.append(ref)
-            held += ref.shape[0]
-        else:
-            outs.append(ref)
-    here = pairs // len(befores)
-    for shift, before in enumerate(befores):
-        state_ref[pl.ds((place_ref[2] ^ shift) * here, here)] = before[...]
+def mixed_kernel(place_ref, local_ref, grown_ref, c_ref, norm_ref, w_ref, mine_ref, got_ref, *rest):
+    outs, (normed_ref, state_ref) = rest[:-2], rest[-2:]
+    half = mine_ref.shape[0]
+    pairs = 2 * half
+    state_ref[pl.ds(place_ref[2] * half, half)] = mine_ref[...]
+    state_ref[pl.ds((1 - place_ref[2]) * half, half)] = got_ref[...]
     groups = c_ref.shape[1] // STATE
     per_group = pairs // groups
     for group in range(groups):
@@ -309,62 +312,71 @@
     rows = resid.shape[1]
     experts = head_size * exp_size
     pairs = channels // LANES
-    axes = ("seq", "exp") if pairs % (seq_size * exp_size) == 0 else "exp"
-    shards = lax.axis_size(axes)
-    here = pairs // shards
+    half = pairs // 2
+    exp_index, head_index = lax.axis_index("exp"), lax.axis_index("head")
     place = jnp.stack(
-        [lax.axis_index("head"), lax.axis_index("head") * exp_size + lax.axis_index("exp"), lax.axis_index(axes)]
+        [head_index, head_index * exp_size + exp_index, exp_index % 2, exp_index // 2, lax.axis_index("seq")]
     ).astype(jnp.int32)
     dt_rows, a_row, d_row = dt_in.T, a_log[None], d_skip[None]
     dma = pltpu.SemaphoreType.DMA
-    own = call(
+    packed = struct((half, STATE + TILE, LANES), BF16)
+
+    keep, send = call(
         state_kernel,
         "state",
-        [struct((here, STATE + TILE, LANES), BF16)] * shards,
+        [packed, packed],
         [(SMEM, place), (HBM, x_in), (HBM, b_in), (HBM, dt_rows), (HBM, a_row)],
         [pltpu.VMEM(x_in.shape, BF16), pltpu.VMEM(b_in.shape, BF16), pltpu.VMEM(dt_rows.shape, F32),
          pltpu.VMEM(a_row.shape, F32), pltpu.VMEM((pairs, STATE + TILE, LANES), BF16), dma((4,))],
-        flops=1 << 25, moved_bytes=1 << 20,
-    )
-    got = [own[0]] + [swap(own[s], axes, s) for s in range(1, shards)]
-    wide = -(-(model + 2 * experts) // LANES) * LANES
-    local, grown, c_held, norm_held, w_held = call(
+        megabytes=60, flops=1 << 25, moved_bytes=1 << 20,
+    )
+    local, grown, c_held = call(
         inside_kernel,
         "inside",
-        [struct((length, channels), F32), struct((length, channels), F32), struct(c_in.shape, BF16),
-         struct((1, channels), F32), struct((model, channels), BF16)],
-        [(HBM, value) for value in (x_in, z_in, b_in, c_in, dt_rows, a_row, d_row, norm_w[None], w_out.T)],
+        [struct((length, channels), F32), struct((length, channels), F32), struct(c_in.shape, BF16)],
+        [(HBM, value) for value in (x_in, z_in, b_in, c_in, dt_rows, a_row, d_row)],
         [pltpu.VMEM(x_in.shape, BF16), pltpu.VMEM(z_in.shape, BF16), pltpu.VMEM(b_in.shape, BF16),
-         pltpu.VMEM(dt_rows.shape, F32), pltpu.VMEM(a_row.shape, F32), pltpu.VMEM(d_row.shape, F32), dma((9,))],
-        flops=1 << 27, moved_bytes=8 << 20,
-    )
+         pltpu.VMEM(dt_rows.shape, F32), pltpu.VMEM(a_row.shape, F32), pltpu.VMEM(d_row.shape, F32), dma((7,))],
+        megabytes=60, flops=1 << 27, moved_bytes=4 << 20,
+    )
+    wide = -(-(model + 2 * experts) // LANES) * LANES
     turned = [jnp.transpose(value, (2, 0, 1)) for value in (routes, gates)]
-    gate_lanes, resid_held, gain_held, up_held, down_held = call(
+    gate_lanes, resid_held, gain_held, norm_held, w_held, up_held, down_held = call(
         functools.partial(prep_kernel, experts, model),
         "prep",
         [struct((rows, wide - model // LANES * LANES), BF16), struct(resid.shape, BF16), struct((1, model), F32),
+         struct((1, channels), F32), struct((model, channels), BF16),
          struct((1, hidden_units, model), BF16), struct(w_down.shape, BF16)],
-        [(HBM, value) for value in (resid, *turned, moe_gain[None], jnp.swapaxes(w_up, 1, 2), w_down)],
-        [pltpu.VMEM(turned[0].shape, jnp.int32), pltpu.VMEM(turned[1].shape, F32), dma((6,))],
-        flops=1 << 20, moved_bytes=8 << 20,
-    )
-    if axes == "exp":
-        before = chain_over_seq(place, got)
-    else:
-        before = call(
-            chain_kernel,
-            "chain",
-            [struct((here, STATE, LANES), BF16)] * shards,
-            [(SMEM, place)] + [(VMEM, value) for value in got],
-            [pltpu.VMEM((shards, here, STATE + TILE, LANES), BF16)],
-            flops=1 << 20, moved_bytes=1 << 19,
-        )
-    before = [before[0]] + [swap(before[s], axes, s) for s in range(1, shards)]
+        [(HBM, value) for value in (resid, *turned, moe_gain[None], norm_w[None], w_out.T,
+                                    jnp.swapaxes(w_up, 1, 2), w_down)],
+        [pltpu.VMEM(turned[0].shape, jnp.int32), pltpu.VMEM(turned[1].shape, F32), dma((8,))],
+        megabytes=48, flops=1 << 20, moved_bytes=8 << 20,
+    )
+    got = swap(send, "exp", 1)
+    chip = call(chip_state_kernel, "chip_state", packed, [(SMEM, place), (VMEM, keep), (VMEM, got)])
+    along_y = [chip] + [swap(chip, "exp", 2 * d) for d in range(1, chips)]
+    span = call(
+        span_kernel,
+        "span",
+        packed,
+        [(SMEM, place), (ANY, c_held)] + [(VMEM, value) for value in along_y],
+        [pltpu.VMEM((chips, *packed.shape), BF16)],
+    )
+    along_x = [span] + [swap(span, "seq", d) for d in range(1, seq_size)]
+    before, before_send = call(
+        functools.partial(before_kernel, chips),
+        "before",
+        [struct((half, STATE, LANES), BF16)] * 2,
+        [(SMEM, place), (ANY, gate_lanes)] + [(VMEM, value) for value in (keep, got, *along_y, *along_x)],
+        [pltpu.VMEM((chips, *packed.shape), BF16), pltpu.VMEM((seq_size, *packed.shape), BF16)],
+        megabytes=24,
+    )
+    before_got = swap(before_send, "exp", 1)
     mixed = call(
         mixed_kernel,
         "mixed",
         [struct((rows, model), BF16)] * head_size,
-        [(SMEM, place)] + [(VMEM, value) for value in (local, grown, c_held, norm_held, w_held, *before)],
+        [(SMEM, place)] + [(VMEM, value) for value in (local, grown, c_held, norm_held, w_held, before, before_got)],
         [pltpu.VMEM((length, channels), BF16), pltpu.VMEM((pairs, STATE, LANES), BF16)],
         flops=1 << 29, moved_bytes=4 << 20,
     )
@@ -376,41 +388,44 @@
         [struct((rows, model), BF16), struct((rows, wide), BF16)],
         [(VMEM, value) for value in (resid_held, gate_lanes, gain_held, *parts)],
     )
-    near = {0: own_rows} | {s: swap(own_rows, "head", s) for s in order}
-    sets = [near] + [{s: swap(near[s], "exp", 2 * d) for s in near} for d in range(1, chips)]
-    produced = []
-    for members in sets:
-        mine = jnp.concatenate([members[s] for s in range(head_size)], axis=0)
-        produced.append(
-            call(
-                functools.partial(expert_kernel, experts),
-                "experts",
-                [struct((head_size * rows, model), BF16)] * 2,
-                [(SMEM, place)] + [(VMEM, value) for value in (up_held, down_held, mine, swap(mine, "exp", 1))],
-                megabytes=16,
-                flops=1 << 31, moved_bytes=8 << 20,
-            )
+
+    def through_expert(members):
+        mine = jnp.concatenate(members, axis=0)
+        kept, sent = call(
+            functools.partial(expert_kernel, experts),
+            "experts",
+            [struct((head_size * rows, model), BF16)] * 2,
+            [(SMEM, place)] + [(VMEM, value) for value in (up_held, down_held, mine, swap(mine, "exp", 1))],
+            megabytes=16, flops=1 << 31, moved_bytes=8 << 20,
         )
-    returned = [(kept, swap(sent, "exp", 1)) for kept, sent in produced]
-    arrived = {s: [] for s in range(head_size)}
+        return kept, sent
+
+    near = [swap(own_rows, "head", s) for s in order] + [own_rows]
+    far = [[swap(member, "exp", 2 * d) for member in near] for d in range(1, chips)]
+    kept, sent = through_expert(near)
+    kept, sent, far = lax.optimization_barrier((kept, sent, far))
+    near_got = swap(sent, "exp", 1)
+    arrived = [[] for _ in near]
     for d in range(1, chips):
+        far_kept, far_sent = through_expert(far[d - 1])
+        far_got = swap(far_sent, "exp", 1)
         pieces = call(
             split_sum_kernel,
             "split",
             [struct((rows, model), BF16)] * head_size,
-            [(VMEM, value) for value in returned[d]],
+            [(VMEM, far_kept), (VMEM, far_got)],
         )
-        for s in order + [0]:
-            arrived[s].append(swap(pieces[s], "exp", 2 * d))
+        for at, piece in enumerate(pieces):
+            arrived[at].append(swap(piece, "exp", 2 * d))
     final = []
-    for s in order + [0]:
+    for at, mask in enumerate(order + [0]):
         piece = call(
-            functools.partial(piece_kernel, s),
+            functools.partial(piece_kernel, at),
             "piece",
             struct((rows, model), BF16),
-            [(VMEM, value) for value in (*returned[0], *arrived[s])],
+            [(VMEM, value) for value in (kept, near_got, *arrived[at])],
         )
-        final.append(swap(piece, "head", s) if s else piece)
+        final.append(swap(piece, "head", mask) if mask else piece)
     return call(last_kernel, "last", struct(resid.shape, BF16), [(VMEM, value) for value in (hidden, *final)])
 
 

time: 89.1 us -> 89.4 us (level)
  starting transfers between devices: 35.3 us -> 25.5 us
  Pallas kernels: 13.3 us -> 21.5 us
  waiting for transfers between devices: 28.2 us -> 32.4 us
  local copies, waits for them, and re-layouts: 11.3 us -> 9.29 us
    ppermute x35 -> x25, starting transfers between devices: 35.3 us -> 25.5 us  [swap(): return lax.ppermute(value, axis, [(i, i ^ mask) for i in range(size)])]
    pallas_call x14 -> x16, Pallas kernels: 13.3 us -> 21.5 us  [call(): pl.pallas_call(kernel, out_shape=outs, in_specs=specs, out_specs=jax.tree...]
    ppermute x35 -> x25, waiting for transfers between devices: 28.2 us -> 32.4 us  [swap(): return lax.ppermute(value, axis, [(i, i ^ mask) for i in range(size)])]
    unnamed x44 -> x34, local copies, waits for them, and re-layouts: 11.3 us -> 7.89 us
  transfers between devices with their start and end apart: 35 -> 25, of which waited for: 14 -> 19; matrix products, arithmetic and copies ran while one was open for 0% -> 1% of each run, Pallas kernels for 9% -> 13%
where the time goes in v3:
time: 89.4 us; the launch traced here: 89 us
  waiting for transfers between devices  32.4 us (36%)
  starting transfers between devices  25.5 us (29%)
  Pallas kernels  21.5 us (24%)
  local copies, waits for them, and re-layouts  9.29 us (10%)
    ppermute x25, waiting for transfers between devices, swap(): return lax.ppermute(value, axis, [(i, i ^ mask) for i in range(size)])  32.4 us
    ppermute x25, starting transfers between devices, swap(): return lax.ppermute(value, axis, [(i, i ^ mask) for i in range(size)])  25.5 us
    pallas_call x16, Pallas kernels, call(): pl.pallas_call(kernel, out_shape=outs, in_specs=specs, out_specs=jax.tree...  21.5 us
    unnamed x34, local copies, waits for them, and re-layouts  7.89 us
  transfers between devices with their start and end apart: 25, of which 19 were waited for; matrix products, arithmetic and copies ran while one was open for 1% of the time, Pallas kernels for 13%

profile of v3, /device:TPU:0, one launch (start us, length us, event | category | flops | bytes accessed | tf_op | source)
XLA Modules:
  0.0 89.0 jit_solution(13630943809692122197)
XLA Ops:
  0.7 3.2 %state.1 = (bf16[4,144,128]{2,1,0:T(8,128)(2,1)}, bf16[4,144,128]{2,1,0:T(8,128)(2,1)}) custom-call(s32[5]{0:T(128)} %stack.23.place_ref, bf16[128,1024]{1,0:T(8,128)(2,1)} %x_hbm.3, bf16[128,256]{1,0:T(8,128)(2,1)} %b_hbm.3, f32[16,128]{1,0:T(8,128)} %bitcast.18, f32[1,16]{1,0:T(1,128)} %bitcast.20), custom_call_target="tpu_custom_call" | custom-call | flops 33554432 | bytes 1048576 | tf_op jit(solution)/shard_map/state/pallas_call | solution.py:30
  4.4 1.2 %collective-permute-done.got_ref = bf16[4,144,128]{2,1,0:T(8,128)(2,1)S(1)} collective-permute-done((bf16[4,144,128]{2,1,0:T(8,128)(2,1)}, bf16[4,144,128]{2,1,0:T(8,128)(2,1)S(1)}, u32[]{:S(2)}, u32[]{:S(2)}) %collective-permute-start) | collective-permute-done | bytes 147488 | tf_op jit(solution)/shard_map/ppermute | solution.py:300
  5.6 0.9 %copy-done.1 = bf16[4,144,128]{2,1,0:T(8,128)(2,1)S(1)} copy-done((bf16[4,144,128]{2,1,0:T(8,128)(2,1)S(1)}, bf16[4,144,128]{2,1,0:T(8,128)(2,1)}, u32[]{:S(2)}) %copy-start.1) | copy-done | bytes 147480
  6.5 0.7 copy-done.8
  7.8 2.9 %collective-permute-start.1 = (bf16[4,144,128]{2,1,0:T(8,128)(2,1)S(1)}, bf16[4,144,128]{2,1,0:T(8,128)(2,1)S(1)}, u32[]{:S(2)}, u32[]{:S(2)}) collective-permute-start(bf16[4,144,128]{2,1,0:T(8,128)(2,1)S(1)} %chip_state.1.rest_0_), channel_id=1, source_target_pairs={{0,2},{1,3},{2,0},{3,1},{4,6},{5,7},{6,4},{7,5},{8,10},{9,11},{10,... | collective-permute-start | bytes 442376 | tf_op jit(solution)/shard_map/ppermute | solution.py:300
  10.7 3.4 %inside.1 = (f32[128,1024]{1,0:T(8,128)}, f32[128,1024]{1,0:T(8,128)}, bf16[128,256]{1,0:T(8,128)(2,1)}) custom-call(bf16[128,1024]{1,0:T(8,128)(2,1)} %x_hbm.3, bf16[128,1024]{1,0:T(8,128)(2,1)} %z_hbm.1, bf16[128,256]{1,0:T(8,128)(2,1)} %b_hbm.3, bf16[128,256]{1,0:T(8,128)(2,1)} %c_hbm.1, f32[16,128]{1,0:T(8,128)} %bitcast.19, f32[1,16]{1,0:T(1,128)} %bitcast.21, ...), custom_call_target="tpu_custom_call" | custom-call | flops 134217728 | bytes 4194304 | tf_op jit(solution)/shard_map/inside/pallas_call | solution.py:30
  14.1 0.8 collective-permute-done.1.rest_1_
  14.9 0.8 copy-done.5
  15.7 0.7 copy-done.9
  17.0 1.8 %collective-permute-start.2 = (bf16[4,144,128]{2,1,0:T(8,128)(2,1)S(1)}, bf16[4,144,128]{2,1,0:T(8,128)(2,1)S(1)}, u32[]{:S(2)}, u32[]{:S(2)}) collective-permute-start(bf16[4,144,128]{2,1,0:T(8,128)(2,1)S(1)} %span.1.rest_2_), channel_id=1, source_target_pairs={{0,16},{16,0},{1,17},{17,1},{2,18},{18,2},{3,19},{19,3},{4,20},{20... | collective-permute-start | bytes 442376 | tf_op jit(solution)/shard_map/ppermute | solution.py:300
  18.8 0.7 broadcast_in_dim.12.gain_hbm
  19.5 0.9 copy-done.7
  20.4 0.7 copy-done.11
  21.1 0.7 copy-done.12
  21.8 0.7 copy-done.13
  22.5 5.2 %prep.1 = (bf16[32,128]{1,0:T(8,128)(2,1)S(1)}, bf16[1,32,1344]{2,1,0:T(8,128)(2,1)S(1)}, f32[1,1344]{1,0:T(1,128)S(1)}, f32[1,1024]{1,0:T(1,128)S(1)}, bf16[134...) custom-call(bf16[1,32,1344]{2,1,0:T(8,128)(2,1)S(1)} %copy-done.7, ...), custom_call_target="tpu_custom_call" | custom-call | flops 1048576 | bytes 8388608 | tf_op jit(solution)/shard_map/prep/pallas_call | solution.py:30
  27.7 0.8 before.1
  28.6 1.3 %collective-permute-done.3.got_ref = bf16[4,128,128]{2,1,0:T(8,128)(2,1)S(1)} collective-permute-done((bf16[4,128,128]{2,1,0:T(8,128)(2,1)S(1)}, bf16[4,128,128]{2,1,0:T(8,128)(2,1)S(1)}, u32[]{:S(2)}, u32[]{:S(2)}) %collective-permute-start.3) | collective-permute-done | bytes 131104 | tf_op jit(solution)/shard_map/ppermute | solution.py:300
  29.9 1.8 %copy-done = bf16[1344,1024]{1,0:T(8,128)(2,1)S(1)} copy-done((bf16[1344,1024]{1,0:T(8,128)(2,1)S(1)}, bf16[1344,1024]{1,0:T(8,128)(2,1)}, u32[]{:S(2)}) %copy-start) | copy-done | bytes 2752536
  31.7 1.9 %mixed.1 = (bf16[32,1344]{1,0:T(8,128)(2,1)S(1)}, bf16[32,1344]{1,0:T(8,128)(2,1)S(1)}, bf16[32,1344]{1,0:T(8,128)(2,1)S(1)}, bf16[32,1344]{1,0:T(8,128)(2,1)S(1)}) custom-call(s32[5]{0:T(128)S(1)} %copy-done.10, f32[128,1024]{1,0:T(8,128)S(1)} %copy-done.3, f32[128,1024]{1,0:T(8,128)S(1)} %copy-done.4, bf16[128,256]{1,0:T(8,128)(2,1)S(1)} %copy-done.6, ...), custom_call_target="tpu_custom_call" | custom-call | flops 536870912 | bytes 4194304 | tf_op jit(solution)/shard_map/mixed/pallas_call | solution.py:30
  33.6 3.7 %collective-permute-start.4 = (bf16[32,1344]{1,0:T(8,128)(2,1)S(1)}, bf16[32,1344]{1,0:T(8,128)(2,1)S(1)}, u32[]{:S(2)}, u32[]{:S(2)}) collective-permute-start(bf16[32,1344]{1,0:T(8,128)(2,1)S(1)} %get-tuple-element.52), channel_id=1, source_target_pairs={{0,12},{4,8},{8,4},{12,0},{1,13},{5,9},{9,5},{13,1},{2,14},{6,10},... | collective-permute-start | bytes 258056 | tf_op jit(solution)/shard_map/ppermute | solution.py:300
  37.3 0.8 collective-permute-start.6
  38.1 2.9 %collective-permute-done.4.rest_1_ = bf16[32,1344]{1,0:T(8,128)(2,1)S(1)} collective-permute-done((bf16[32,1344]{1,0:T(8,128)(2,1)S(1)}, bf16[32,1344]{1,0:T(8,128)(2,1)S(1)}, u32[]{:S(2)}, u32[]{:S(2)}) %collective-permute-start.4) | collective-permute-done | bytes 86048 | tf_op jit(solution)/shard_map/ppermute | solution.py:300
  40.9 4.2 %collective-permute-done.5.rest_2_ = bf16[32,1344]{1,0:T(8,128)(2,1)S(1)} collective-permute-done((bf16[32,1344]{1,0:T(8,128)(2,1)S(1)}, bf16[32,1344]{1,0:T(8,128)(2,1)S(1)}, u32[]{:S(2)}, u32[]{:S(2)}) %collective-permute-start.5) | collective-permute-done | bytes 86048 | tf_op jit(solution)/shard_map/ppermute | solution.py:300
  45.3 2.5 %collective-permute-start.7 = (bf16[32,1408]{1,0:T(8,128)(2,1)S(1)}, bf16[32,1408]{1,0:T(8,128)(2,1)S(1)}, u32[]{:S(2)}, u32[]{:S(2)}) collective-permute-start(bf16[32,1408]{1,0:T(8,128)(2,1)S(1)} %get-tuple-element.58), channel_id=1, source_target_pairs={{0,12},{4,8},{8,4},{12,0},{1,13},{5,9},{9,5},{13,1},{2,14},{6,10},... | collective-permute-start | bytes 270344 | tf_op jit(solution)/shard_map/ppermute | solution.py:300
  47.9 1.9 %collective-permute-start.8 = (bf16[32,1408]{1,0:T(8,128)(2,1)S(1)}, bf16[32,1408]{1,0:T(8,128)(2,1)S(1)}, u32[]{:S(2)}, u32[]{:S(2)}) collective-permute-start(bf16[32,1408]{1,0:T(8,128)(2,1)S(1)} %get-tuple-element.58), channel_id=1, source_target_pairs={{0,8},{4,12},{8,0},{12,4},{1,9},{5,13},{9,1},{13,5},{2,10},{6,14},... | collective-permute-start | bytes 270344 | tf_op jit(solution)/shard_map/ppermute | solution.py:300
  49.8 2.8 %collective-permute-done.7 = bf16[32,1408]{1,0:T(8,128)(2,1)S(1)} collective-permute-done((bf16[32,1408]{1,0:T(8,128)(2,1)S(1)}, bf16[32,1408]{1,0:T(8,128)(2,1)S(1)}, u32[]{:S(2)}, u32[]{:S(2)}) %collective-permute-start.7) | collective-permute-done | bytes 90144 | tf_op jit(solution)/shard_map/ppermute | solution.py:300
  52.6 3.3 %collective-permute-done.8 = bf16[32,1408]{1,0:T(8,128)(2,1)S(1)} collective-permute-done((bf16[32,1408]{1,0:T(8,128)(2,1)S(1)}, bf16[32,1408]{1,0:T(8,128)(2,1)S(1)}, u32[]{:S(2)}, u32[]{:S(2)}) %collective-permute-start.8) | collective-permute-done | bytes 90144 | tf_op jit(solution)/shard_map/ppermute | solution.py:300
  56.0 1.6 %collective-permute-start.14 = (bf16[32,1408]{1,0:T(8,128)(2,1)S(1)}, bf16[32,1408]{1,0:T(8,128)(2,1)S(1)}, u32[]{:S(2)}, u32[]{:S(2)}) collective-permute-start(bf16[32,1408]{1,0:T(8,128)(2,1)S(1)} %get-tuple-element.58), channel_id=1, source_target_pairs={{0,2},{1,3},{2,0},{3,1},{4,6},{5,7},{6,4},{7,5},{8,10},{9,11},{10,... | collective-permute-start | bytes 270344 | tf_op jit(solution)/shard_map/ppermute | solution.py:300
  58.1 1.6 %collective-permute-start.12 = (bf16[32,1408]{1,0:T(8,128)(2,1)S(1)}, bf16[32,1408]{1,0:T(8,128)(2,1)S(1)}, u32[]{:S(2)}, u32[]{:S(2)}) collective-permute-start(bf16[32,1408]{1,0:T(8,128)(2,1)S(1)} %collective-permute-done.8), channel_id=1, source_target_pairs={{0,2},{1,3},{2,0},{3,1},{4,6},{5,7},{6,4},{7,5},{8,10},{9,11},{10,... | collective-permute-start | bytes 270344 | tf_op jit(solution)/shard_map/ppermute | solution.py:300
  60.1 2.4 %experts.2 = (bf16[128,1344]{1,0:T(8,128)(2,1)S(1)}, bf16[128,1344]{1,0:T(8,128)(2,1)S(1)}) custom-call(s32[5]{0:T(128)S(1)} %copy-done.10, bf16[1,928,1344]{2,1,0:T(8,128)(2,1)S(1)} %get-tuple-element.56.up_ref, bf16[1,928,1344]{2,1,0:T(8,128)(2,1)S(1)} %get-tuple-element.57.down_ref, bf16[128,1408]{1,0:T(8,128)(2,1)S(1)} %constant_dynamic-update-slice_fusion.mine_ref, ...), custom_call_target="tpu_custom_call" | custom-call | flops 2147483648 | bytes 8388608 | tf_op jit(solution)/shard_map/experts/pallas_call | solution.py:30
  62.5 0.9 %collective-permute-done.13 = bf16[32,1408]{1,0:T(8,128)(2,1)S(1)} collective-permute-done((bf16[32,1408]{1,0:T(8,128)(2,1)S(1)}, bf16[32,1408]{1,0:T(8,128)(2,1)S(1)}, u32[]{:S(2)}, u32[]{:S(2)}) %collective-permute-start.13) | collective-permute-done | bytes 90144 | tf_op jit(solution)/shard_map/ppermute | solution.py:300
  63.4 1.9 %collective-permute-done.12 = bf16[32,1408]{1,0:T(8,128)(2,1)S(1)} collective-permute-done((bf16[32,1408]{1,0:T(8,128)(2,1)S(1)}, bf16[32,1408]{1,0:T(8,128)(2,1)S(1)}, u32[]{:S(2)}, u32[]{:S(2)}) %collective-permute-start.12) | collective-permute-done | bytes 90144 | tf_op jit(solution)/shard_map/ppermute | solution.py:300
  65.3 1.5 %collective-permute-done.11 = bf16[32,1408]{1,0:T(8,128)(2,1)S(1)} collective-permute-done((bf16[32,1408]{1,0:T(8,128)(2,1)S(1)}, bf16[32,1408]{1,0:T(8,128)(2,1)S(1)}, u32[]{:S(2)}, u32[]{:S(2)}) %collective-permute-start.11) | collective-permute-done | bytes 90144 | tf_op jit(solution)/shard_map/ppermute | solution.py:300
  67.0 1.7 %collective-permute-done.16.partner_ref = bf16[128,1408]{1,0:T(8,128)(2,1)S(1)} collective-permute-done((bf16[128,1408]{1,0:T(8,128)(2,1)S(1)}, bf16[128,1408]{1,0:T(8,128)(2,1)S(1)}, u32[]{:S(2)}, u32[]{:S(2)}) %collective-permute-start.16) | collective-permute-done | bytes 360480 | tf_op jit(solution)/shard_map/ppermute | solution.py:300
  68.6 2.4 %experts.3 = (bf16[128,1344]{1,0:T(8,128)(2,1)S(1)}, bf16[128,1344]{1,0:T(8,128)(2,1)S(1)}) custom-call(s32[5]{0:T(128)S(1)} %copy-done.10, bf16[1,928,1344]{2,1,0:T(8,128)(2,1)S(1)} %get-tuple-element.56.up_ref, bf16[1,928,1344]{2,1,0:T(8,128)(2,1)S(1)} %get-tuple-element.57.down_ref, bf16[128,1408]{1,0:T(8,128)(2,1)S(1)} %constant_dynamic-update-slice_fusion.4.mine_ref, ...), custom_call_target="tpu_custom_call" | custom-call | flops 2147483648 | bytes 8388608 | tf_op jit(solution)/shard_map/experts/pallas_call | solution.py:30
  71.6 1.2 %collective-permute-done.17.got_ref = bf16[128,1344]{1,0:T(8,128)(2,1)S(1)} collective-permute-done((bf16[128,1344]{1,0:T(8,128)(2,1)S(1)}, bf16[128,1344]{1,0:T(8,128)(2,1)S(1)}, u32[]{:S(2)}, u32[]{:S(2)}) %collective-permute-start.17) | collective-permute-done | bytes 344096 | tf_op jit(solution)/shard_map/ppermute | solution.py:300
  72.8 1.6 %collective-permute-start.18 = (bf16[32,1344]{1,0:T(8,128)(2,1)S(1)}, bf16[32,1344]{1,0:T(8,128)(2,1)S(1)}, u32[]{:S(2)}, u32[]{:S(2)}) collective-permute-start(bf16[32,1344]{1,0:T(8,128)(2,1)S(1)} %get-tuple-element.69), channel_id=1, source_target_pairs={{0,2},{1,3},{2,0},{3,1},{4,6},{5,7},{6,4},{7,5},{8,10},{9,11},{10,... | collective-permute-start | bytes 258056 | tf_op jit(solution)/shard_map/ppermute | solution.py:300
  74.9 1.5 %collective-permute-start.22 = (bf16[32,1344]{1,0:T(8,128)(2,1)S(1)}, bf16[32,1344]{1,0:T(8,128)(2,1)S(1)}, u32[]{:S(2)}, u32[]{:S(2)}) collective-permute-start(bf16[32,1344]{1,0:T(8,128)(2,1)S(1)} %get-tuple-element.71), channel_id=1, source_target_pairs={{0,2},{1,3},{2,0},{3,1},{4,6},{5,7},{6,4},{7,5},{8,10},{9,11},{10,... | collective-permute-start | bytes 258056 | tf_op jit(solution)/shard_map/ppermute | solution.py:300
  76.9 1.3 %collective-permute-done.18.rest_0_ = bf16[32,1344]{1,0:T(8,128)(2,1)S(1)} collective-permute-done((bf16[32,1344]{1,0:T(8,128)(2,1)S(1)}, bf16[32,1344]{1,0:T(8,128)(2,1)S(1)}, u32[]{:S(2)}, u32[]{:S(2)}) %collective-permute-start.18) | collective-permute-done | bytes 86048 | tf_op jit(solution)/shard_map/ppermute | solution.py:300
  78.3 0.8 collective-permute-start.19
  79.1 1.0 %collective-permute-done.20.rest_0_ = bf16[32,1344]{1,0:T(8,128)(2,1)S(1)} collective-permute-done((bf16[32,1344]{1,0:T(8,128)(2,1)S(1)}, bf16[32,1344]{1,0:T(8,128)(2,1)S(1)}, u32[]{:S(2)}, u32[]{:S(2)}) %collective-permute-start.20) | collective-permute-done | bytes 86048 | tf_op jit(solution)/shard_map/ppermute | solution.py:300
  80.2 0.7 collective-permute-start.21
  80.9 1.2 %collective-permute-done.22.rest_0_ = bf16[32,1344]{1,0:T(8,128)(2,1)S(1)} collective-permute-done((bf16[32,1344]{1,0:T(8,128)(2,1)S(1)}, bf16[32,1344]{1,0:T(8,128)(2,1)S(1)}, u32[]{:S(2)}, u32[]{:S(2)}) %collective-permute-start.22) | collective-permute-done | bytes 86048 | tf_op jit(solution)/shard_map/ppermute | solution.py:300
  82.1 0.8 collective-permute-start.23
  83.4 2.1 %collective-permute-done.19.rest_0_ = bf16[32,1344]{1,0:T(8,128)(2,1)S(1)} collective-permute-done((bf16[32,1344]{1,0:T(8,128)(2,1)S(1)}, bf16[32,1344]{1,0:T(8,128)(2,1)S(1)}, u32[]{:S(2)}, u32[]{:S(2)}) %collective-permute-start.19) | collective-permute-done | bytes 86048 | tf_op jit(solution)/shard_map/ppermute | solution.py:300
  85.5 2.5 %collective-permute-done.21.rest_1_ = bf16[32,1344]{1,0:T(8,128)(2,1)S(1)} collective-permute-done((bf16[32,1344]{1,0:T(8,128)(2,1)S(1)}, bf16[32,1344]{1,0:T(8,128)(2,1)S(1)}, u32[]{:S(2)}, u32[]{:S(2)}) %collective-permute-start.21) | collective-permute-done | bytes 86048 | tf_op jit(solution)/shard_map/ppermute | solution.py:300
  88.3 0.7 last.1
  (56 shorter events, 6.4 us)
Async XLA Ops:
  3.9 1.7 %collective-permute-start = (bf16[4,144,128]{2,1,0:T(8,128)(2,1)}, bf16[4,144,128]{2,1,0:T(8,128)(2,1)S(1)}, u32[]{:S(2)}, u32[]{:S(2)}) collective-permute-start(bf16[4,144,128]{2,1,0:T(8,128)(2,1)} %get-tuple-element.48), channel_id=1, source_target_pairs={{0,1},{1,0},{2,3},{3,2},{4,5},{5,4},{6,7},{7,6},{8,9},{9,8},{10,11... | collective-permute-start | bytes 442376 | tf_op jit(solution)/shard_map/ppermute | solution.py:300
  5.6 0.9 %copy-start.1 = (bf16[4,144,128]{2,1,0:T(8,128)(2,1)S(1)}, bf16[4,144,128]{2,1,0:T(8,128)(2,1)}, u32[]{:S(2)}) copy-start(bf16[4,144,128]{2,1,0:T(8,128)(2,1)} %get-tuple-element.47.keep_ref) | copy-start | bytes 442372
  6.5 0.7 copy-start.8
  7.8 7.1 %collective-permute-start.1 = (bf16[4,144,128]{2,1,0:T(8,128)(2,1)S(1)}, bf16[4,144,128]{2,1,0:T(8,128)(2,1)S(1)}, u32[]{:S(2)}, u32[]{:S(2)}) collective-permute-start(bf16[4,144,128]{2,1,0:T(8,128)(2,1)S(1)} %chip_state.1.rest_0_), channel_id=1, source_target_pairs={{0,2},{1,3},{2,0},{3,1},{4,6},{5,7},{6,4},{7,5},{8,10},{9,11},{10,... | collective-permute-start | bytes 442376 | tf_op jit(solution)/shard_map/ppermute | solution.py:300
  14.9 0.8 copy-start.5
  15.7 0.7 copy-start.9
  17.0 10.6 %collective-permute-start.2 = (bf16[4,144,128]{2,1,0:T(8,128)(2,1)S(1)}, bf16[4,144,128]{2,1,0:T(8,128)(2,1)S(1)}, u32[]{:S(2)}, u32[]{:S(2)}) collective-permute-start(bf16[4,144,128]{2,1,0:T(8,128)(2,1)S(1)} %span.1.rest_2_), channel_id=1, source_target_pairs={{0,16},{16,0},{1,17},{17,1},{2,18},{18,2},{3,19},{19,3},{4,20},{20... | collective-permute-start | bytes 442376 | tf_op jit(solution)/shard_map/ppermute | solution.py:300
  19.5 0.9 copy-start.7
  20.4 0.7 copy-start.11
  21.1 0.7 copy-start.12
  21.8 0.7 copy-start.13
  22.5 5.2 %copy-start.2 = (bf16[4,144,128]{2,1,0:T(8,128)(2,1)S(1)}, bf16[4,144,128]{2,1,0:T(8,128)(2,1)}, u32[]{:S(2)}) copy-start(bf16[4,144,128]{2,1,0:T(8,128)(2,1)} %get-tuple-element.47.keep_ref) | copy-start | bytes 442372
  22.5 5.2 %copy-start.10 = (s32[5]{0:T(128)S(1)}, s32[5]{0:T(128)}, u32[]{:S(2)}) copy-start(s32[5]{0:T(128)} %stack.23.place_ref) | copy-start | bytes 64
  22.5 7.5 %copy-start.3 = (f32[128,1024]{1,0:T(8,128)S(1)}, f32[128,1024]{1,0:T(8,128)}, u32[]{:S(2)}) copy-start(f32[128,1024]{1,0:T(8,128)} %get-tuple-element.42.local_ref) | copy-start | bytes 1572868
  22.5 7.5 %copy-start.4 = (f32[128,1024]{1,0:T(8,128)S(1)}, f32[128,1024]{1,0:T(8,128)}, u32[]{:S(2)}) copy-start(f32[128,1024]{1,0:T(8,128)} %get-tuple-element.43.grown_ref) | copy-start | bytes 1572868
  22.5 7.4 %copy-start.6 = (bf16[128,256]{1,0:T(8,128)(2,1)S(1)}, bf16[128,256]{1,0:T(8,128)(2,1)}, u32[]{:S(2)}) copy-start(bf16[128,256]{1,0:T(8,128)(2,1)} %get-tuple-element.44.after_ref.c_ref) | copy-start | bytes 196612
  28.5 1.4 %collective-permute-start.3 = (bf16[4,128,128]{2,1,0:T(8,128)(2,1)S(1)}, bf16[4,128,128]{2,1,0:T(8,128)(2,1)S(1)}, u32[]{:S(2)}, u32[]{:S(2)}) collective-permute-start(bf16[4,128,128]{2,1,0:T(8,128)(2,1)S(1)} %get-tuple-element.50), channel_id=1, source_target_pairs={{0,1},{1,0},{2,3},{3,2},{4,5},{5,4},{6,7},{7,6},{8,9},{9,8},{10,11... | collective-permute-start | bytes 393224 | tf_op jit(solution)/shard_map/ppermute | solution.py:300
  29.9 1.8 %copy-start = (bf16[1344,1024]{1,0:T(8,128)(2,1)S(1)}, bf16[1344,1024]{1,0:T(8,128)(2,1)}, u32[]{:S(2)}) copy-start(bf16[1344,1024]{1,0:T(8,128)(2,1)} %get-tuple-element.46.w_ref) | copy-start | bytes 8257540
  33.6 7.3 %collective-permute-start.4 = (bf16[32,1344]{1,0:T(8,128)(2,1)S(1)}, bf16[32,1344]{1,0:T(8,128)(2,1)S(1)}, u32[]{:S(2)}, u32[]{:S(2)}) collective-permute-start(bf16[32,1344]{1,0:T(8,128)(2,1)S(1)} %get-tuple-element.52), channel_id=1, source_target_pairs={{0,12},{4,8},{8,4},{12,0},{1,13},{5,9},{9,5},{13,1},{2,14},{6,10},... | collective-permute-start | bytes 258056 | tf_op jit(solution)/shard_map/ppermute | solution.py:300
  37.3 7.9 %collective-permute-start.5 = (bf16[32,1344]{1,0:T(8,128)(2,1)S(1)}, bf16[32,1344]{1,0:T(8,128)(2,1)S(1)}, u32[]{:S(2)}, u32[]{:S(2)}) collective-permute-start(bf16[32,1344]{1,0:T(8,128)(2,1)S(1)} %get-tuple-element.53), channel_id=1, source_target_pairs={{0,8},{4,12},{8,0},{12,4},{1,9},{5,13},{9,1},{13,5},{2,10},{6,14},... | collective-permute-start | bytes 258056 | tf_op jit(solution)/shard_map/ppermute | solution.py:300
  37.3 7.9 %collective-permute-start.6 = (bf16[32,1344]{1,0:T(8,128)(2,1)S(1)}, bf16[32,1344]{1,0:T(8,128)(2,1)S(1)}, u32[]{:S(2)}, u32[]{:S(2)}) collective-permute-start(bf16[32,1344]{1,0:T(8,128)(2,1)S(1)} %get-tuple-element.54), channel_id=1, source_target_pairs={{0,4},{4,0},{8,12},{12,8},{1,5},{5,1},{9,13},{13,9},{2,6},{6,2},{1... | collective-permute-start | bytes 258056 | tf_op jit(solution)/shard_map/ppermute | solution.py:300
  45.3 7.2 %collective-permute-start.7 = (bf16[32,1408]{1,0:T(8,128)(2,1)S(1)}, bf16[32,1408]{1,0:T(8,128)(2,1)S(1)}, u32[]{:S(2)}, u32[]{:S(2)}) collective-permute-start(bf16[32,1408]{1,0:T(8,128)(2,1)S(1)} %get-tuple-element.58), channel_id=1, source_target_pairs={{0,12},{4,8},{8,4},{12,0},{1,13},{5,9},{9,5},{13,1},{2,14},{6,10},... | collective-permute-start | bytes 270344 | tf_op jit(solution)/shard_map/ppermute | solution.py:300
  47.9 8.0 %collective-permute-start.9 = (bf16[32,1408]{1,0:T(8,128)(2,1)S(1)}, bf16[32,1408]{1,0:T(8,128)(2,1)S(1)}, u32[]{:S(2)}, u32[]{:S(2)}) collective-permute-start(bf16[32,1408]{1,0:T(8,128)(2,1)S(1)} %get-tuple-element.58), channel_id=1, source_target_pairs={{0,4},{4,0},{8,12},{12,8},{1,5},{5,1},{9,13},{13,9},{2,6},{6,2},{1... | collective-permute-start | bytes 270344 | tf_op jit(solution)/shard_map/ppermute | solution.py:300
  47.9 8.0 %collective-permute-start.8 = (bf16[32,1408]{1,0:T(8,128)(2,1)S(1)}, bf16[32,1408]{1,0:T(8,128)(2,1)S(1)}, u32[]{:S(2)}, u32[]{:S(2)}) collective-permute-start(bf16[32,1408]{1,0:T(8,128)(2,1)S(1)} %get-tuple-element.58), channel_id=1, source_target_pairs={{0,8},{4,12},{8,0},{12,4},{1,9},{5,13},{9,1},{13,5},{2,10},{6,14},... | collective-permute-start | bytes 270344 | tf_op jit(solution)/shard_map/ppermute | solution.py:300
  55.9 4.2 %collective-permute-start.10 = (bf16[128,1408]{1,0:T(8,128)(2,1)S(1)}, bf16[128,1408]{1,0:T(8,128)(2,1)S(1)}, u32[]{:S(2)}, u32[]{:S(2)}) collective-permute-start(bf16[128,1408]{1,0:T(8,128)(2,1)S(1)} %constant_dynamic-update-slice_fusion.mine_ref), channel_id=1, source_target_pairs={{0,1},{1,0},{2,3},{3,2},{4,5},{5,4},{6,7},{7,6},{8,9},{9,8},{10,11... | collective-permute-start | bytes 1081352 | tf_op jit(solution)/shard_map/ppermute | solution.py:300
  56.0 6.5 %collective-permute-start.14 = (bf16[32,1408]{1,0:T(8,128)(2,1)S(1)}, bf16[32,1408]{1,0:T(8,128)(2,1)S(1)}, u32[]{:S(2)}, u32[]{:S(2)}) collective-permute-start(bf16[32,1408]{1,0:T(8,128)(2,1)S(1)} %get-tuple-element.58), channel_id=1, source_target_pairs={{0,2},{1,3},{2,0},{3,1},{4,6},{5,7},{6,4},{7,5},{8,10},{9,11},{10,... | collective-permute-start | bytes 270344 | tf_op jit(solution)/shard_map/ppermute | solution.py:300
  57.6 5.8 %collective-permute-start.13 = (bf16[32,1408]{1,0:T(8,128)(2,1)S(1)}, bf16[32,1408]{1,0:T(8,128)(2,1)S(1)}, u32[]{:S(2)}, u32[]{:S(2)}) collective-permute-start(bf16[32,1408]{1,0:T(8,128)(2,1)S(1)} %collective-permute-done.9), channel_id=1, source_target_pairs={{0,2},{1,3},{2,0},{3,1},{4,6},{5,7},{6,4},{7,5},{8,10},{9,11},{10,... | collective-permute-start | bytes 270344 | tf_op jit(solution)/shard_map/ppermute | solution.py:300
  58.1 7.3 %collective-permute-start.12 = (bf16[32,1408]{1,0:T(8,128)(2,1)S(1)}, bf16[32,1408]{1,0:T(8,128)(2,1)S(1)}, u32[]{:S(2)}, u32[]{:S(2)}) collective-permute-start(bf16[32,1408]{1,0:T(8,128)(2,1)S(1)} %collective-permute-done.8), channel_id=1, source_target_pairs={{0,2},{1,3},{2,0},{3,1},{4,6},{5,7},{6,4},{7,5},{8,10},{9,11},{10,... | collective-permute-start | bytes 270344 | tf_op jit(solution)/shard_map/ppermute | solution.py:300
  59.6 7.2 %collective-permute-start.11 = (bf16[32,1408]{1,0:T(8,128)(2,1)S(1)}, bf16[32,1408]{1,0:T(8,128)(2,1)S(1)}, u32[]{:S(2)}, u32[]{:S(2)}) collective-permute-start(bf16[32,1408]{1,0:T(8,128)(2,1)S(1)} %collective-permute-done.7), channel_id=1, source_target_pairs={{0,2},{1,3},{2,0},{3,1},{4,6},{5,7},{6,4},{7,5},{8,10},{9,11},{10,... | collective-permute-start | bytes 270344 | tf_op jit(solution)/shard_map/ppermute | solution.py:300
  66.9 1.7 %collective-permute-start.16 = (bf16[128,1408]{1,0:T(8,128)(2,1)S(1)}, bf16[128,1408]{1,0:T(8,128)(2,1)S(1)}, u32[]{:S(2)}, u32[]{:S(2)}) collective-permute-start(bf16[128,1408]{1,0:T(8,128)(2,1)S(1)} %constant_dynamic-update-slice_fusion.4.mine_ref), channel_id=1, source_target_pairs={{0,1},{1,0},{2,3},{3,2},{4,5},{5,4},{6,7},{7,6},{8,9},{9,8},{10,11... | collective-permute-start | bytes 1081352 | tf_op jit(solution)/shard_map/ppermute | solution.py:300
  71.0 1.7 %collective-permute-start.17 = (bf16[128,1344]{1,0:T(8,128)(2,1)S(1)}, bf16[128,1344]{1,0:T(8,128)(2,1)S(1)}, u32[]{:S(2)}, u32[]{:S(2)}) collective-permute-start(bf16[128,1344]{1,0:T(8,128)(2,1)S(1)} %get-tuple-element.68), channel_id=1, source_target_pairs={{0,1},{1,0},{2,3},{3,2},{4,5},{5,4},{6,7},{7,6},{8,9},{9,8},{10,11... | collective-permute-start | bytes 1032200 | tf_op jit(solution)/shard_map/ppermute | solution.py:300
  71.2 5.8 %collective-permute-start.15 = (bf16[128,1344]{1,0:T(8,128)(2,1)S(1)}, bf16[128,1344]{1,0:T(8,128)(2,1)S(1)}, u32[]{:S(2)}, u32[]{:S(2)}) collective-permute-start(bf16[128,1344]{1,0:T(8,128)(2,1)S(1)} %get-tuple-element.62), channel_id=1, source_target_pairs={{0,1},{1,0},{2,3},{3,2},{4,5},{5,4},{6,7},{7,6},{8,9},{9,8},{10,11... | collective-permute-start | bytes 1032200 | tf_op jit(solution)/shard_map/ppermute | solution.py:300
  72.8 5.4 %collective-permute-start.18 = (bf16[32,1344]{1,0:T(8,128)(2,1)S(1)}, bf16[32,1344]{1,0:T(8,128)(2,1)S(1)}, u32[]{:S(2)}, u32[]{:S(2)}) collective-permute-start(bf16[32,1344]{1,0:T(8,128)(2,1)S(1)} %get-tuple-element.69), channel_id=1, source_target_pairs={{0,2},{1,3},{2,0},{3,1},{4,6},{5,7},{6,4},{7,5},{8,10},{9,11},{10,... | collective-permute-start | bytes 258056 | tf_op jit(solution)/shard_map/ppermute | solution.py:300
  74.4 5.7 %collective-permute-start.20 = (bf16[32,1344]{1,0:T(8,128)(2,1)S(1)}, bf16[32,1344]{1,0:T(8,128)(2,1)S(1)}, u32[]{:S(2)}, u32[]{:S(2)}) collective-permute-start(bf16[32,1344]{1,0:T(8,128)(2,1)S(1)} %get-tuple-element.70), channel_id=1, source_target_pairs={{0,2},{1,3},{2,0},{3,1},{4,6},{5,7},{6,4},{7,5},{8,10},{9,11},{10,... | collective-permute-start | bytes 258056 | tf_op jit(solution)/shard_map/ppermute | solution.py:300
  74.9 7.2 %collective-permute-start.22 = (bf16[32,1344]{1,0:T(8,128)(2,1)S(1)}, bf16[32,1344]{1,0:T(8,128)(2,1)S(1)}, u32[]{:S(2)}, u32[]{:S(2)}) collective-permute-start(bf16[32,1344]{1,0:T(8,128)(2,1)S(1)} %get-tuple-element.71), channel_id=1, source_target_pairs={{0,2},{1,3},{2,0},{3,1},{4,6},{5,7},{6,4},{7,5},{8,10},{9,11},{10,... | collective-permute-start | bytes 258056 | tf_op jit(solution)/shard_map/ppermute | solution.py:300
  76.5 6.9 %collective-permute-start.24 = (bf16[32,1344]{1,0:T(8,128)(2,1)S(1)}, bf16[32,1344]{1,0:T(8,128)(2,1)S(1)}, u32[]{:S(2)}, u32[]{:S(2)}) collective-permute-start(bf16[32,1344]{1,0:T(8,128)(2,1)S(1)} %get-tuple-element.72), channel_id=1, source_target_pairs={{0,2},{1,3},{2,0},{3,1},{4,6},{5,7},{6,4},{7,5},{8,10},{9,11},{10,... | collective-permute-start | bytes 258056 | tf_op jit(solution)/shard_map/ppermute | solution.py:300
  78.3 7.3 %collective-permute-start.19 = (bf16[32,1344]{1,0:T(8,128)(2,1)S(1)}, bf16[32,1344]{1,0:T(8,128)(2,1)S(1)}, u32[]{:S(2)}, u32[]{:S(2)}) collective-permute-start(bf16[32,1344]{1,0:T(8,128)(2,1)S(1)} %piece.4), channel_id=1, source_target_pairs={{0,12},{4,8},{8,4},{12,0},{1,13},{5,9},{9,5},{13,1},{2,14},{6,10},... | collective-permute-start | bytes 258056 | tf_op jit(solution)/shard_map/ppermute | solution.py:300
  80.2 7.9 %collective-permute-start.21 = (bf16[32,1344]{1,0:T(8,128)(2,1)S(1)}, bf16[32,1344]{1,0:T(8,128)(2,1)S(1)}, u32[]{:S(2)}, u32[]{:S(2)}) collective-permute-start(bf16[32,1344]{1,0:T(8,128)(2,1)S(1)} %piece.5), channel_id=1, source_target_pairs={{0,8},{4,12},{8,0},{12,4},{1,9},{5,13},{9,1},{13,5},{2,10},{6,14},... | collective-permute-start | bytes 258056 | tf_op jit(solution)/shard_map/ppermute | solution.py:300
  82.1 6.2 %collective-permute-start.23 = (bf16[32,1344]{1,0:T(8,128)(2,1)S(1)}, bf16[32,1344]{1,0:T(8,128)(2,1)S(1)}, u32[]{:S(2)}, u32[]{:S(2)}) collective-permute-start(bf16[32,1344]{1,0:T(8,128)(2,1)S(1)} %piece.6), channel_id=1, source_target_pairs={{0,4},{4,0},{8,12},{12,8},{1,5},{5,1},{9,13},{13,9},{2,6},{6,2},{1... | collective-permute-start | bytes 258056 | tf_op jit(solution)/shard_map/ppermute | solution.py:300

commit v4 on v3

--- a/solution.py
+++ b/solution.py
@@ -17,7 +17,6 @@
 HBM = pl.BlockSpec(memory_space=pltpu.HBM)
 VMEM = pl.BlockSpec(memory_space=pltpu.VMEM)
 ANY = pl.BlockSpec(memory_space=pl.ANY)
-SMEM = pl.BlockSpec(memory_space=pltpu.SMEM)
 NT = (((1,), (1,)), ((), ()))
 
 
@@ -25,18 +24,25 @@
     return jax.ShapeDtypeStruct(shape, dtype)
 
 
-def call(kernel, name, outs, ins, scratch=(), megabytes=12, flops=0, moved_bytes=0):
-    specs, args = [spec for spec, _ in ins], [arg for _, arg in ins]
+def call(kernel, name, outs, ins, scratch=(), megabytes=12, pinned=True):
+    args = [pltpu.with_memory_space_constraint(arg, pltpu.HBM) if spec is HBM else arg for spec, arg in ins]
     return pl.pallas_call(
         kernel,
-        out_shape=outs,
-        in_specs=specs,
+        out_shape=jax.tree.map(lambda out: pltpu.VMEM(out.shape, out.dtype), outs) if pinned else outs,
+        in_specs=[spec for spec, _ in ins],
         out_specs=jax.tree.map(lambda _: VMEM, outs),
         scratch_shapes=list(scratch),
         name=name,
         compiler_params=pltpu.CompilerParams(vmem_limit_bytes=megabytes << 20),
-        cost_estimate=pl.CostEstimate(flops=flops, bytes_accessed=moved_bytes, transcendentals=0),
     )(*args)
+
+
+def core_index():
+    return lax.axis_index("exp") % 2
+
+
+def chip_index():
+    return lax.axis_index("exp") // 2
 
 
 def copies(sems, sources, targets):
@@ -80,7 +86,7 @@
     ref[:, STATE : STATE + TILE, :] = jnp.where(row == 0, high, wide - high).astype(BF16)
 
 
-def state_kernel(place_ref, x_hbm, b_hbm, dt_hbm, a_hbm, keep_ref, send_ref, *scratch):
+def state_kernel(x_hbm, b_hbm, dt_hbm, a_hbm, keep_ref, send_ref, *scratch):
     x_ref, b_ref, dt_ref, a_ref, packed_ref, sems = scratch
     loads = copies(sems, (dt_hbm, a_hbm, x_hbm, b_hbm), (dt_ref, a_ref, x_ref, b_ref))
     loads[0].wait()
@@ -102,22 +108,27 @@
             state = jnp.dot(turned, weighted, preferred_element_type=F32)
             pack(packed_ref.at[pair : pair + 1], pair_lanes(total, pair)[None], state[None])
     half = pairs // 2
-    keep_ref[...] = packed_ref[pl.ds(place_ref[2] * half, half)]
-    send_ref[...] = packed_ref[pl.ds((1 - place_ref[2]) * half, half)]
-
-
-def chip_state_kernel(place_ref, keep_ref, got_ref, out_ref):
-    first = place_ref[2] == 0
+    keep_ref[...] = packed_ref[pl.ds(core_index() * half, half)]
+    send_ref[...] = packed_ref[pl.ds((1 - core_index()) * half, half)]
+
+
+def chip_state_kernel(keep_ref, got_ref, out_ref):
+    first = core_index() == 0
     keep, got = unpacked(keep_ref[...]), unpacked(got_ref[...])
     early = [jnp.where(first, mine, other) for mine, other in zip(keep, got)]
     late = [jnp.where(first, other, mine) for mine, other in zip(keep, got)]
     pack(out_ref, early[0] + late[0], jnp.exp(late[0]) * early[1] + late[1])
 
 
-def span_kernel(place_ref, after_ref, *rest):
+def weights_kernel(after_ref, up_hbm, down_hbm, up_ref, down_ref, sems):
+    for load in copies(sems, (up_hbm, down_hbm), (up_ref, down_ref)):
+        load.wait()
+
+
+def span_kernel(after_ref, *rest):
     ins, out_ref, block_ref = rest[:-2], rest[-2], rest[-1]
     for mask, part in enumerate(ins):
-        block_ref[place_ref[3] ^ mask] = part[...]
+        block_ref[chip_index() ^ mask] = part[...]
     total, state = unpacked(block_ref[0])
     for chip in range(1, len(ins)):
         here, own = unpacked(block_ref[chip])
@@ -125,19 +136,19 @@
     pack(out_ref, total, state)
 
 
-def before_kernel(chips, place_ref, after_ref, keep_ref, got_ref, *rest):
+def before_kernel(chips, after_ref, keep_ref, got_ref, *rest):
     ins, (mine_ref, send_ref, chip_ref, part_ref) = rest[:-4], rest[-4:]
     for mask in range(chips):
-        chip_ref[place_ref[3] ^ mask] = ins[mask][...]
+        chip_ref[chip_index() ^ mask] = ins[mask][...]
     parts = len(ins) - chips
     for mask in range(parts):
-        part_ref[place_ref[4] ^ mask] = ins[chips + mask][...]
+        part_ref[lax.axis_index("seq") ^ mask] = ins[chips + mask][...]
     carry = jnp.zeros(mine_ref.shape, F32)
-    for ref, count, own in ((part_ref, parts, place_ref[4]), (chip_ref, chips, place_ref[3])):
+    for ref, count, own in ((part_ref, parts, lax.axis_index("seq")), (chip_ref, chips, chip_index())):
         for index in range(count - 1):
             total, state = unpacked(ref[index])
             carry = jnp.where(index < own, jnp.exp(total) * carry + state, carry)
-    first = place_ref[2] == 0
+    first = core_index() == 0
     total, state = (jnp.where(first, k, g) for k, g in zip(unpacked(keep_ref[...]), unpacked(got_ref[...])))
     later = jnp.exp(total) * carry + state
     mine_ref[...] = jnp.where(first, carry, later).astype(BF16)
@@ -183,12 +194,12 @@
             grown_ref[:, at] = pair_lanes(grown, pair) * gate
 
 
-def prep_kernel(experts, width, resid_hbm, routes_hbm, gates_hbm, gain_hbm, norm_hbm, w_hbm, up_hbm, down_hbm, *rest):
-    gate_ref, resid_ref, gain_ref, norm_ref, w_ref, up_ref, down_ref, routes_ref, gates_ref, sems = rest
+def prep_kernel(experts, width, resid_hbm, routes_hbm, gates_hbm, gain_hbm, norm_hbm, w_hbm, *rest):
+    gate_ref, resid_ref, gain_ref, norm_ref, w_ref, routes_ref, gates_ref, sems = rest
     loads = copies(
         sems,
-        (routes_hbm, gates_hbm, resid_hbm, gain_hbm, norm_hbm, w_hbm, up_hbm, down_hbm),
-        (routes_ref, gates_ref, resid_ref, gain_ref, norm_ref, w_ref, up_ref, down_ref),
+        (routes_hbm, gates_hbm, resid_hbm, gain_hbm, norm_hbm, w_hbm),
+        (routes_ref, gates_ref, resid_ref, gain_ref, norm_ref, w_ref),
     )
     loads[0].wait()
     loads[1].wait()
@@ -206,12 +217,12 @@
         load.wait()
 
 
-def mixed_kernel(place_ref, local_ref, grown_ref, c_ref, norm_ref, w_ref, mine_ref, got_ref, *rest):
+def mixed_kernel(local_ref, grown_ref, c_ref, norm_ref, w_ref, mine_ref, got_ref, *rest):
     outs, (normed_ref, state_ref) = rest[:-2], rest[-2:]
     half = mine_ref.shape[0]
     pairs = 2 * half
-    state_ref[pl.ds(place_ref[2] * half, half)] = mine_ref[...]
-    state_ref[pl.ds((1 - place_ref[2]) * half, half)] = got_ref[...]
+    state_ref[pl.ds(core_index() * half, half)] = mine_ref[...]
+    state_ref[pl.ds((1 - core_index()) * half, half)] = got_ref[...]
     groups = c_ref.shape[1] // STATE
     per_group = pairs // groups
     for group in range(groups):
@@ -232,14 +243,14 @@
     rows = outs[0].shape[0]
     blocks = []
     for shift in range(len(outs)):
-        owner = place_ref[0] ^ shift
+        owner = lax.axis_index("head") ^ shift
         blocks.append(normed_ref[pl.ds(pl.multiple_of(owner * rows, rows), rows), :])
     product = lax.dot_general(jnp.concatenate(blocks, axis=0), w_ref[...], NT, preferred_element_type=F32)
     for shift, out in enumerate(outs):
         out[...] = product[shift * rows : (shift + 1) * rows].astype(BF16)
 
 
-def rows_kernel(resid_ref, gate_ref, gain_ref, *rest):
+def rows_kernel(after_ref, resid_ref, gate_ref, gain_ref, *rest):
     parts, hidden_ref, rows_ref = rest[:-2], rest[-2], rest[-1]
     mixed = parts[0][...].astype(F32)
     for part in parts[1:]:
@@ -253,7 +264,7 @@
     rows_ref[:, :width] = (value * scale * gain_ref[...]).astype(BF16)
 
 
-def expert_kernel(experts, place_ref, up_ref, down_ref, mine_ref, partner_ref, kept_ref, sent_ref):
+def expert_kernel(experts, up_ref, down_ref, mine_ref, partner_ref, kept_ref, sent_ref):
     width = up_ref.shape[2]
     start = width // LANES * LANES
     half = mine_ref.shape[0]
@@ -263,7 +274,8 @@
     activated = (up * up).astype(BF16)
     tail = jnp.concatenate([mine_ref[:, start:], partner_ref[:, start:]], axis=0).astype(F32)
     lane = lax.broadcasted_iota(jnp.int32, tail.shape, 1) + start - width
-    chosen = (lane == place_ref[1]) | (lane == place_ref[1] + experts)
+    own = lax.axis_index("head") * lax.axis_size("exp") + lax.axis_index("exp")
+    chosen = (lane == own) | (lane == own + experts)
     gate = jnp.sum(jnp.where(chosen, tail, 0.0), axis=1, keepdims=True)
     out = jnp.dot(activated, down_ref[0], preferred_element_type=F32) * gate
     kept_ref[...] = out[:half].astype(BF16)
@@ -313,10 +325,6 @@
     experts = head_size * exp_size
     pairs = channels // LANES
     half = pairs // 2
-    exp_index, head_index = lax.axis_index("exp"), lax.axis_index("head")
-    place = jnp.stack(
-        [head_index, head_index * exp_size + exp_index, exp_index % 2, exp_index // 2, lax.axis_index("seq")]
-    ).astype(jnp.int32)
     dt_rows, a_row, d_row = dt_in.T, a_log[None], d_skip[None]
     dma = pltpu.SemaphoreType.DMA
     packed = struct((half, STATE + TILE, LANES), BF16)
@@ -325,10 +333,10 @@
         state_kernel,
         "state",
         [packed, packed],
-        [(SMEM, place), (HBM, x_in), (HBM, b_in), (HBM, dt_rows), (HBM, a_row)],
+        [(HBM, x_in), (HBM, b_in), (HBM, dt_rows), (HBM, a_row)],
         [pltpu.VMEM(x_in.shape, BF16), pltpu.VMEM(b_in.shape, BF16), pltpu.VMEM(dt_rows.shape, F32),
          pltpu.VMEM(a_row.shape, F32), pltpu.VMEM((pairs, STATE + TILE, LANES), BF16), dma((4,))],
-        megabytes=60, flops=1 << 25, moved_bytes=1 << 20,
+        megabytes=16,
     )
     local, grown, c_held = call(
         inside_kernel,
@@ -337,29 +345,27 @@
         [(HBM, value) for value in (x_in, z_in, b_in, c_in, dt_rows, a_row, d_row)],
         [pltpu.VMEM(x_in.shape, BF16), pltpu.VMEM(z_in.shape, BF16), pltpu.VMEM(b_in.shape, BF16),
          pltpu.VMEM(dt_rows.shape, F32), pltpu.VMEM(a_row.shape, F32), pltpu.VMEM(d_row.shape, F32), dma((7,))],
-        megabytes=60, flops=1 << 27, moved_bytes=4 << 20,
+        megabytes=16,
     )
     wide = -(-(model + 2 * experts) // LANES) * LANES
     turned = [jnp.transpose(value, (2, 0, 1)) for value in (routes, gates)]
-    gate_lanes, resid_held, gain_held, norm_held, w_held, up_held, down_held = call(
+    gate_lanes, resid_held, gain_held, norm_held, w_held = call(
         functools.partial(prep_kernel, experts, model),
         "prep",
         [struct((rows, wide - model // LANES * LANES), BF16), struct(resid.shape, BF16), struct((1, model), F32),
-         struct((1, channels), F32), struct((model, channels), BF16),
-         struct((1, hidden_units, model), BF16), struct(w_down.shape, BF16)],
-        [(HBM, value) for value in (resid, *turned, moe_gain[None], norm_w[None], w_out.T,
-                                    jnp.swapaxes(w_up, 1, 2), w_down)],
-        [pltpu.VMEM(turned[0].shape, jnp.int32), pltpu.VMEM(turned[1].shape, F32), dma((8,))],
-        megabytes=48, flops=1 << 20, moved_bytes=8 << 20,
+         struct((1, channels), F32), struct((model, channels), BF16)],
+        [(HBM, value) for value in (resid, *turned, moe_gain[None], norm_w[None], w_out.T)],
+        [pltpu.VMEM(turned[0].shape, jnp.int32), pltpu.VMEM(turned[1].shape, F32), dma((6,))],
+        megabytes=16,
     )
     got = swap(send, "exp", 1)
-    chip = call(chip_state_kernel, "chip_state", packed, [(SMEM, place), (VMEM, keep), (VMEM, got)])
+    chip = call(chip_state_kernel, "chip_state", packed, [(VMEM, keep), (VMEM, got)])
     along_y = [chip] + [swap(chip, "exp", 2 * d) for d in range(1, chips)]
     span = call(
         span_kernel,
         "span",
         packed,
-        [(SMEM, place), (ANY, c_held)] + [(VMEM, value) for value in along_y],
+        [(ANY, c_held)] + [(VMEM, value) for value in along_y],
         [pltpu.VMEM((chips, *packed.shape), BF16)],
     )
     along_x = [span] + [swap(span, "seq", d) for d in range(1, seq_size)]
@@ -367,7 +373,7 @@
         functools.partial(before_kernel, chips),
         "before",
         [struct((half, STATE, LANES), BF16)] * 2,
-        [(SMEM, place), (ANY, gate_lanes)] + [(VMEM, value) for value in (keep, got, *along_y, *along_x)],
+        [(ANY, gate_lanes)] + [(VMEM, value) for value in (keep, got, *along_y, *along_x)],
         [pltpu.VMEM((chips, *packed.shape), BF16), pltpu.VMEM((seq_size, *packed.shape), BF16)],
         megabytes=24,
     )
@@ -376,9 +382,16 @@
         mixed_kernel,
         "mixed",
         [struct((rows, model), BF16)] * head_size,
-        [(SMEM, place)] + [(VMEM, value) for value in (local, grown, c_held, norm_held, w_held, before, before_got)],
+        [(VMEM, value) for value in (local, grown, c_held, norm_held, w_held, before, before_got)],
         [pltpu.VMEM((length, channels), BF16), pltpu.VMEM((pairs, STATE, LANES), BF16)],
-        flops=1 << 29, moved_bytes=4 << 20,
+    )
+    up_turned = jnp.swapaxes(w_up, 1, 2)
+    up_held, down_held = call(
+        weights_kernel,
+        "weights",
+        [struct(up_turned.shape, BF16), struct(w_down.shape, BF16)],
+        [(ANY, mixed[0]), (HBM, up_turned), (HBM, w_down)],
+        [dma((2,))],
     )
     order = list(range(head_size - 1, 0, -1))
     parts = [mixed[0]] + [swap(mixed[s], "head", s) for s in order]
@@ -386,7 +399,7 @@
         rows_kernel,
         "rows",
         [struct((rows, model), BF16), struct((rows, wide), BF16)],
-        [(VMEM, value) for value in (resid_held, gate_lanes, gain_held, *parts)],
+        [(ANY, up_held)] + [(VMEM, value) for value in (resid_held, gate_lanes, gain_held, *parts)],
     )
 
     def through_expert(members):
@@ -395,13 +408,16 @@
             functools.partial(expert_kernel, experts),
             "experts",
             [struct((head_size * rows, model), BF16)] * 2,
-            [(SMEM, place)] + [(VMEM, value) for value in (up_held, down_held, mine, swap(mine, "exp", 1))],
-            megabytes=16, flops=1 << 31, moved_bytes=8 << 20,
+            [(VMEM, value) for value in (up_held, down_held, mine, swap(mine, "exp", 1))],
+            megabytes=16,
         )
         return kept, sent
 
-    near = [swap(own_rows, "head", s) for s in order] + [own_rows]
+    near = [own_rows] + [swap(own_rows, "head", s) for s in reversed(order)]
     far = [[swap(member, "exp", 2 * d) for member in near] for d in range(1, chips)]
+    near, early = lax.optimization_barrier((near, [members[:-1] for members in far]))
+    far = [members + others[-1:] for members, others in zip(early, far)]
+    near, far = near[::-1], [members[::-1] for members in far]
     kept, sent = through_expert(near)
     kept, sent, far = lax.optimization_barrier((kept, sent, far))
     near_got = swap(sent, "exp", 1)
@@ -426,7 +442,13 @@
             [(VMEM, value) for value in (kept, near_got, *arrived[at])],
         )
         final.append(swap(piece, "head", mask) if mask else piece)
-    return call(last_kernel, "last", struct(resid.shape, BF16), [(VMEM, value) for value in (hidden, *final)])
+    return call(
+        last_kernel,
+        "last",
+        struct(resid.shape, BF16),
+        [(VMEM, value) for value in (hidden, *final)],
+        pinned=False,
+    )
 
 
 def solution(mesh):

time: 89.4 us -> 72.3 us (0.81)
  local copies, waits for them, and re-layouts: 9.29 us -> 1.4 us
  Pallas kernels: 21.5 us -> 15.3 us
  waiting for transfers between devices: 32.4 us -> 28.4 us
  starting transfers between devices: 25.5 us -> 26.7 us
    unnamed x34 -> x6, local copies, waits for them, and re-layouts: 7.89 us -> 0.08 us
    pallas_call x16 -> x17, Pallas kernels: 21.5 us -> 15.3 us  [call(): pl.pallas_call(kernel, out_shape=jax.tree.map(lambda out: pltpu.VMEM(out....]
    ppermute x25, waiting for transfers between devices: 32.4 us -> 28.4 us  [swap(): return lax.ppermute(value, axis, [(i, i ^ mask) for i in range(size)])]
    ppermute x25, starting transfers between devices: 25.5 us -> 26.7 us  [swap(): return lax.ppermute(value, axis, [(i, i ^ mask) for i in range(size)])]
  transfers between devices with their start and end apart: 25 -> 25, of which waited for: 19 -> 21; matrix products, arithmetic and copies ran while one was open for 1% -> 2% of each run, Pallas kernels for 13% -> 12%
where the time goes in v4:
time: 72.3 us; the launch traced here: 72 us
  waiting for transfers between devices  28.4 us (39%)
  starting transfers between devices  26.7 us (37%)
  Pallas kernels  15.3 us (21%)
  local copies, waits for them, and re-layouts  1.4 us (2%)
    ppermute x25, waiting for transfers between devices, swap(): return lax.ppermute(value, axis, [(i, i ^ mask) for i in range(size)])  28.4 us
    ppermute x25, starting transfers between devices, swap(): return lax.ppermute(value, axis, [(i, i ^ mask) for i in range(size)])  26.7 us
    pallas_call x17, Pallas kernels, call(): pl.pallas_call(kernel, out_shape=jax.tree.map(lambda out: pltpu.VMEM(out....  15.3 us
  transfers between devices with their start and end apart: 25, of which 21 were waited for; matrix products, arithmetic and copies ran while one was open for 2% of the time, Pallas kernels for 12%

profile of v4, /device:TPU:0, one launch (start us, length us, event | category | flops | bytes accessed | tf_op | source)
XLA Modules:
  0.0 72.0 jit_solution(9285377887565028585)
XLA Ops:
  0.0 1.8 %state.1 = (bf16[4,144,128]{2,1,0:T(8,128)(2,1)S(1)}, bf16[4,144,128]{2,1,0:T(8,128)(2,1)S(1)}) custom-call(bf16[128,1024]{1,0:T(8,128)(2,1)} %x_hbm.3, bf16[128,256]{1,0:T(8,128)(2,1)} %b_hbm.3, f32[16,128]{1,0:T(8,128)} %bitcast.10, f32[1,16]{1,0:T(1,128)} %bitcast.15), custom_call_target="tpu_custom_call" | custom-call | tf_op jit(solution)/shard_map/state/pallas_call | solution.py:29
  1.8 0.5 collective-permute-start
  2.4 1.0 %collective-permute-done.got_ref = bf16[4,144,128]{2,1,0:T(8,128)(2,1)S(1)} collective-permute-done((bf16[4,144,128]{2,1,0:T(8,128)(2,1)S(1)}, bf16[4,144,128]{2,1,0:T(8,128)(2,1)S(1)}, u32[]{:S(2)}, u32[]{:S(2)}) %collective-permute-start) | collective-permute-done | bytes 147488 | tf_op jit(solution)/shard_map/ppermute | solution.py:312
  3.5 2.9 %collective-permute-start.1 = (bf16[4,144,128]{2,1,0:T(8,128)(2,1)S(1)}, bf16[4,144,128]{2,1,0:T(8,128)(2,1)S(1)}, u32[]{:S(2)}, u32[]{:S(2)}) collective-permute-start(bf16[4,144,128]{2,1,0:T(8,128)(2,1)S(1)} %chip_state.1.rest_0_), channel_id=1, source_target_pairs={{0,2},{1,3},{2,0},{3,1},{4,6},{5,7},{6,4},{7,5},{8,10},{9,11},{10,... | collective-permute-start | bytes 442376 | tf_op jit(solution)/shard_map/ppermute | solution.py:312
  6.4 2.4 %inside.1 = (f32[128,1024]{1,0:T(8,128)S(1)}, f32[128,1024]{1,0:T(8,128)S(1)}, bf16[128,256]{1,0:T(8,128)(2,1)S(1)}) custom-call(bf16[128,1024]{1,0:T(8,128)(2,1)} %x_hbm.3, bf16[128,1024]{1,0:T(8,128)(2,1)} %z_hbm.1, bf16[128,256]{1,0:T(8,128)(2,1)} %b_hbm.3, bf16[128,256]{1,0:T(8,128)(2,1)} %c_hbm.1, f32[16,128]{1,0:T(8,128)} %bitcast.11, ...), custom_call_target="tpu_custom_call" | custom-call | tf_op jit(solution)/shard_map/inside/pallas_call | solution.py:29
  8.8 1.7 %collective-permute-done.1.rest_1_ = bf16[4,144,128]{2,1,0:T(8,128)(2,1)S(1)} collective-permute-done((bf16[4,144,128]{2,1,0:T(8,128)(2,1)S(1)}, bf16[4,144,128]{2,1,0:T(8,128)(2,1)S(1)}, u32[]{:S(2)}, u32[]{:S(2)}) %collective-permute-start.1) | collective-permute-done | bytes 147488 | tf_op jit(solution)/shard_map/ppermute | solution.py:312
  10.7 1.8 %collective-permute-start.2 = (bf16[4,144,128]{2,1,0:T(8,128)(2,1)S(1)}, bf16[4,144,128]{2,1,0:T(8,128)(2,1)S(1)}, u32[]{:S(2)}, u32[]{:S(2)}) collective-permute-start(bf16[4,144,128]{2,1,0:T(8,128)(2,1)S(1)} %span.1.rest_2_), channel_id=1, source_target_pairs={{0,16},{16,0},{1,17},{17,1},{2,18},{18,2},{3,19},{19,3},{4,20},{20... | collective-permute-start | bytes 442376 | tf_op jit(solution)/shard_map/ppermute | solution.py:312
  12.4 1.3 %broadcast_in_dim.14.gain_hbm = f32[1,1344]{1,0:T(1,128)} reshape(f32[1344]{0:T(1024)} %param.27) | data formatting | bytes 10752 | tf_op jit(solution)/shard_map/broadcast_in_dim | solution.py:357
  13.7 1.9 %prep.1 = (bf16[32,128]{1,0:T(8,128)(2,1)S(1)}, bf16[1,32,1344]{2,1,0:T(8,128)(2,1)S(1)}, f32[1,1344]{1,0:T(1,128)S(1)}, f32[1,1024]{1,0:T(1,128)S(1)}, bf16[1344,1024]{1,0:T(8,128)(2,1)S(1)}) custom-call(bf16[1,32,1344]{2,1,0:T(8,128)(2,1)} %resid_hbm.1, s32[6,1,32]{2,1,0:T(1,128)} %bitcast.13, f32[6,1,32]{2,1,0:T(1,128)} %bitcast.14, ...), custom_call_target="tpu_custom_call" | custom-call | tf_op jit(solution)/shard_map/prep/pallas_call | solution.py:29
  15.7 0.4 collective-permute-done.2.rest_3_
  16.1 0.3 before.1
  16.5 1.3 %collective-permute-done.3.got_ref = bf16[4,128,128]{2,1,0:T(8,128)(2,1)S(1)} collective-permute-done((bf16[4,128,128]{2,1,0:T(8,128)(2,1)S(1)}, bf16[4,128,128]{2,1,0:T(8,128)(2,1)S(1)}, u32[]{:S(2)}, u32[]{:S(2)}) %collective-permute-start.3) | collective-permute-done | bytes 131104 | tf_op jit(solution)/shard_map/ppermute | solution.py:312
  17.8 1.3 %mixed.1 = (bf16[32,1344]{1,0:T(8,128)(2,1)S(1)}, bf16[32,1344]{1,0:T(8,128)(2,1)S(1)}, bf16[32,1344]{1,0:T(8,128)(2,1)S(1)}, bf16[32,1344]{1,0:T(8,128)(2,1)S(1)}) custom-call(f32[128,1024]{1,0:T(8,128)S(1)} %get-tuple-element.46.local_ref, f32[128,1024]{1,0:T(8,128)S(1)} %get-tuple-element.47.grown_ref, ...), custom_call_target="tpu_custom_call" | custom-call | tf_op jit(solution)/shard_map/mixed/pallas_call | solution.py:29
  19.1 3.6 %collective-permute-start.4 = (bf16[32,1344]{1,0:T(8,128)(2,1)S(1)}, bf16[32,1344]{1,0:T(8,128)(2,1)S(1)}, u32[]{:S(2)}, u32[]{:S(2)}) collective-permute-start(bf16[32,1344]{1,0:T(8,128)(2,1)S(1)} %get-tuple-element.60), channel_id=1, source_target_pairs={{0,12},{4,8},{8,4},{12,0},{1,13},{5,9},{9,5},{13,1},{2,14},{6,10},... | collective-permute-start | bytes 258056 | tf_op jit(solution)/shard_map/ppermute | solution.py:312
  22.8 0.8 %collective-permute-start.6 = (bf16[32,1344]{1,0:T(8,128)(2,1)S(1)}, bf16[32,1344]{1,0:T(8,128)(2,1)S(1)}, u32[]{:S(2)}, u32[]{:S(2)}) collective-permute-start(bf16[32,1344]{1,0:T(8,128)(2,1)S(1)} %get-tuple-element.62), channel_id=1, source_target_pairs={{0,4},{4,0},{8,12},{12,8},{1,5},{5,1},{9,13},{13,9},{2,6},{6,2},{1... | collective-permute-start | bytes 258056 | tf_op jit(solution)/shard_map/ppermute | solution.py:312
  23.6 2.5 %weights.1 = (bf16[1,928,1344]{2,1,0:T(8,128)(2,1)S(1)}, bf16[1,928,1344]{2,1,0:T(8,128)(2,1)S(1)}) custom-call(bf16[32,1344]{1,0:T(8,128)(2,1)S(1)} %get-tuple-element.56.after_ref.rest_0_, bf16[1,928,1344]{2,1,0:T(8,128)(2,1)} %bitcast.9, bf16[1,928,1344]{2,1,0:T(8,128)(2,1)} %down_hbm.1), custom_call_target="tpu_custom_call" | custom-call | tf_op jit(solution)/shard_map/weights/pallas_call | solution.py:29
  26.1 0.3 collective-permute-done.4.rest_1_
  26.4 4.2 %collective-permute-done.5.rest_2_ = bf16[32,1344]{1,0:T(8,128)(2,1)S(1)} collective-permute-done((bf16[32,1344]{1,0:T(8,128)(2,1)S(1)}, bf16[32,1344]{1,0:T(8,128)(2,1)S(1)}, u32[]{:S(2)}, u32[]{:S(2)}) %collective-permute-start.5) | collective-permute-done | bytes 86048 | tf_op jit(solution)/shard_map/ppermute | solution.py:312
  30.8 0.5 collective-permute-start.8
  31.3 2.6 %collective-permute-start.7 = (bf16[32,1408]{1,0:T(8,128)(2,1)S(1)}, bf16[32,1408]{1,0:T(8,128)(2,1)S(1)}, u32[]{:S(2)}, u32[]{:S(2)}) collective-permute-start(bf16[32,1408]{1,0:T(8,128)(2,1)S(1)} %get-tuple-element.69), channel_id=1, source_target_pairs={{0,4},{4,0},{8,12},{12,8},{1,5},{5,1},{9,13},{13,9},{2,6},{6,2},{1... | collective-permute-start | bytes 270344 | tf_op jit(solution)/shard_map/ppermute | solution.py:312
  33.9 1.5 %collective-permute-start.10 = (bf16[32,1408]{1,0:T(8,128)(2,1)S(1)}, bf16[32,1408]{1,0:T(8,128)(2,1)S(1)}, u32[]{:S(2)}, u32[]{:S(2)}) collective-permute-start(bf16[32,1408]{1,0:T(8,128)(2,1)S(1)} %get-tuple-element.69), channel_id=1, source_target_pairs={{0,2},{1,3},{2,0},{3,1},{4,6},{5,7},{6,4},{7,5},{8,10},{9,11},{10,... | collective-permute-start | bytes 270344 | tf_op jit(solution)/shard_map/ppermute | solution.py:312
  35.4 1.3 %collective-permute-start.9 = (bf16[32,1408]{1,0:T(8,128)(2,1)S(1)}, bf16[32,1408]{1,0:T(8,128)(2,1)S(1)}, u32[]{:S(2)}, u32[]{:S(2)}) collective-permute-start(bf16[32,1408]{1,0:T(8,128)(2,1)S(1)} %get-tuple-element.69), channel_id=1, source_target_pairs={{0,12},{4,8},{8,4},{12,0},{1,13},{5,9},{9,5},{13,1},{2,14},{6,10},... | collective-permute-start | bytes 270344 | tf_op jit(solution)/shard_map/ppermute | solution.py:312
  36.8 1.5 %collective-permute-done.8 = bf16[32,1408]{1,0:T(8,128)(2,1)S(1)} collective-permute-done((bf16[32,1408]{1,0:T(8,128)(2,1)S(1)}, bf16[32,1408]{1,0:T(8,128)(2,1)S(1)}, u32[]{:S(2)}, u32[]{:S(2)}) %collective-permute-start.8) | collective-permute-done | bytes 90144 | tf_op jit(solution)/shard_map/ppermute | solution.py:312
  38.3 2.5 %collective-permute-start.12 = (bf16[32,1408]{1,0:T(8,128)(2,1)S(1)}, bf16[32,1408]{1,0:T(8,128)(2,1)S(1)}, u32[]{:S(2)}, u32[]{:S(2)}) collective-permute-start(bf16[32,1408]{1,0:T(8,128)(2,1)S(1)} %collective-permute-done.8), channel_id=1, source_target_pairs={{0,2},{1,3},{2,0},{3,1},{4,6},{5,7},{6,4},{7,5},{8,10},{9,11},{10,... | collective-permute-start | bytes 270344 | tf_op jit(solution)/shard_map/ppermute | solution.py:312
  40.8 0.9 %collective-permute-done.9 = bf16[32,1408]{1,0:T(8,128)(2,1)S(1)} collective-permute-done((bf16[32,1408]{1,0:T(8,128)(2,1)S(1)}, bf16[32,1408]{1,0:T(8,128)(2,1)S(1)}, u32[]{:S(2)}, u32[]{:S(2)}) %collective-permute-start.9) | collective-permute-done | bytes 90144 | tf_op jit(solution)/shard_map/ppermute | solution.py:312
  41.8 1.5 %collective-permute-done.12 = bf16[32,1408]{1,0:T(8,128)(2,1)S(1)} collective-permute-done((bf16[32,1408]{1,0:T(8,128)(2,1)S(1)}, bf16[32,1408]{1,0:T(8,128)(2,1)S(1)}, u32[]{:S(2)}, u32[]{:S(2)}) %collective-permute-start.12) | collective-permute-done | bytes 90144 | tf_op jit(solution)/shard_map/ppermute | solution.py:312
  43.3 2.0 %collective-permute-done.11 = bf16[32,1408]{1,0:T(8,128)(2,1)S(1)} collective-permute-done((bf16[32,1408]{1,0:T(8,128)(2,1)S(1)}, bf16[32,1408]{1,0:T(8,128)(2,1)S(1)}, u32[]{:S(2)}, u32[]{:S(2)}) %collective-permute-start.11) | collective-permute-done | bytes 90144 | tf_op jit(solution)/shard_map/ppermute | solution.py:312
  45.5 1.0 %collective-permute-start.14 = (bf16[32,1408]{1,0:T(8,128)(2,1)S(1)}, bf16[32,1408]{1,0:T(8,128)(2,1)S(1)}, u32[]{:S(2)}, u32[]{:S(2)}) collective-permute-start(bf16[32,1408]{1,0:T(8,128)(2,1)S(1)} %collective-permute-done.9), channel_id=1, source_target_pairs={{0,2},{1,3},{2,0},{3,1},{4,6},{5,7},{6,4},{7,5},{8,10},{9,11},{10,... | collective-permute-start | bytes 270344 | tf_op jit(solution)/shard_map/ppermute | solution.py:312
  46.5 0.6 collective-permute-done.13.partner_ref
  47.1 1.8 %experts.2 = (bf16[128,1344]{1,0:T(8,128)(2,1)S(1)}, bf16[128,1344]{1,0:T(8,128)(2,1)S(1)}) custom-call(bf16[1,928,1344]{2,1,0:T(8,128)(2,1)S(1)} %get-tuple-element.57.after_ref.up_ref, bf16[1,928,1344]{2,1,0:T(8,128)(2,1)S(1)} %get-tuple-element.64.down_ref, bf16[128,1408]{1,0:T(8,128)(2,1)S(1)} %constant_dynamic-update-slice_fusion.mine_ref, ...), custom_call_target="tpu_custom_call" | custom-call | tf_op jit(solution)/shard_map/experts/pallas_call | solution.py:29
  49.0 1.5 %collective-permute-done.14 = bf16[32,1408]{1,0:T(8,128)(2,1)S(1)} collective-permute-done((bf16[32,1408]{1,0:T(8,128)(2,1)S(1)}, bf16[32,1408]{1,0:T(8,128)(2,1)S(1)}, u32[]{:S(2)}, u32[]{:S(2)}) %collective-permute-start.14) | collective-permute-done | bytes 90144 | tf_op jit(solution)/shard_map/ppermute | solution.py:312
  50.6 1.7 %collective-permute-done.16.partner_ref = bf16[128,1408]{1,0:T(8,128)(2,1)S(1)} collective-permute-done((bf16[128,1408]{1,0:T(8,128)(2,1)S(1)}, bf16[128,1408]{1,0:T(8,128)(2,1)S(1)}, u32[]{:S(2)}, u32[]{:S(2)}) %collective-permute-start.16) | collective-permute-done | bytes 360480 | tf_op jit(solution)/shard_map/ppermute | solution.py:312
  52.3 1.8 %experts.3 = (bf16[128,1344]{1,0:T(8,128)(2,1)S(1)}, bf16[128,1344]{1,0:T(8,128)(2,1)S(1)}) custom-call(bf16[1,928,1344]{2,1,0:T(8,128)(2,1)S(1)} %get-tuple-element.57.after_ref.up_ref, bf16[1,928,1344]{2,1,0:T(8,128)(2,1)S(1)} %get-tuple-element.64.down_ref, bf16[128,1408]{1,0:T(8,128)(2,1)S(1)} %constant_dynamic-update-slice_fusion.4.mine_ref, ...), custom_call_target="tpu_custom_call" | custom-call | tf_op jit(solution)/shard_map/experts/pallas_call | solution.py:29
  54.3 0.4 collective-permute-start.15
  54.7 1.2 %collective-permute-done.17.got_ref = bf16[128,1344]{1,0:T(8,128)(2,1)S(1)} collective-permute-done((bf16[128,1344]{1,0:T(8,128)(2,1)S(1)}, bf16[128,1344]{1,0:T(8,128)(2,1)S(1)}, u32[]{:S(2)}, u32[]{:S(2)}) %collective-permute-start.17) | collective-permute-done | bytes 344096 | tf_op jit(solution)/shard_map/ppermute | solution.py:312
  56.0 1.0 %collective-permute-start.18 = (bf16[32,1344]{1,0:T(8,128)(2,1)S(1)}, bf16[32,1344]{1,0:T(8,128)(2,1)S(1)}, u32[]{:S(2)}, u32[]{:S(2)}) collective-permute-start(bf16[32,1344]{1,0:T(8,128)(2,1)S(1)} %get-tuple-element.83), channel_id=1, source_target_pairs={{0,2},{1,3},{2,0},{3,1},{4,6},{5,7},{6,4},{7,5},{8,10},{9,11},{10,... | collective-permute-start | bytes 258056 | tf_op jit(solution)/shard_map/ppermute | solution.py:312
  57.0 1.1 %collective-permute-start.20 = (bf16[32,1344]{1,0:T(8,128)(2,1)S(1)}, bf16[32,1344]{1,0:T(8,128)(2,1)S(1)}, u32[]{:S(2)}, u32[]{:S(2)}) collective-permute-start(bf16[32,1344]{1,0:T(8,128)(2,1)S(1)} %get-tuple-element.84), channel_id=1, source_target_pairs={{0,2},{1,3},{2,0},{3,1},{4,6},{5,7},{6,4},{7,5},{8,10},{9,11},{10,... | collective-permute-start | bytes 258056 | tf_op jit(solution)/shard_map/ppermute | solution.py:312
  58.1 1.0 %collective-permute-start.22 = (bf16[32,1344]{1,0:T(8,128)(2,1)S(1)}, bf16[32,1344]{1,0:T(8,128)(2,1)S(1)}, u32[]{:S(2)}, u32[]{:S(2)}) collective-permute-start(bf16[32,1344]{1,0:T(8,128)(2,1)S(1)} %get-tuple-element.85), channel_id=1, source_target_pairs={{0,2},{1,3},{2,0},{3,1},{4,6},{5,7},{6,4},{7,5},{8,10},{9,11},{10,... | collective-permute-start | bytes 258056 | tf_op jit(solution)/shard_map/ppermute | solution.py:312
  59.0 1.1 %collective-permute-start.24 = (bf16[32,1344]{1,0:T(8,128)(2,1)S(1)}, bf16[32,1344]{1,0:T(8,128)(2,1)S(1)}, u32[]{:S(2)}, u32[]{:S(2)}) collective-permute-start(bf16[32,1344]{1,0:T(8,128)(2,1)S(1)} %get-tuple-element.86), channel_id=1, source_target_pairs={{0,2},{1,3},{2,0},{3,1},{4,6},{5,7},{6,4},{7,5},{8,10},{9,11},{10,... | collective-permute-start | bytes 258056 | tf_op jit(solution)/shard_map/ppermute | solution.py:312
  60.1 1.4 %collective-permute-done.18.rest_0_ = bf16[32,1344]{1,0:T(8,128)(2,1)S(1)} collective-permute-done((bf16[32,1344]{1,0:T(8,128)(2,1)S(1)}, bf16[32,1344]{1,0:T(8,128)(2,1)S(1)}, u32[]{:S(2)}, u32[]{:S(2)}) %collective-permute-start.18) | collective-permute-done | bytes 86048 | tf_op jit(solution)/shard_map/ppermute | solution.py:312
  61.5 1.7 %collective-permute-start.19 = (bf16[32,1344]{1,0:T(8,128)(2,1)S(1)}, bf16[32,1344]{1,0:T(8,128)(2,1)S(1)}, u32[]{:S(2)}, u32[]{:S(2)}) collective-permute-start(bf16[32,1344]{1,0:T(8,128)(2,1)S(1)} %piece.4), channel_id=1, source_target_pairs={{0,12},{4,8},{8,4},{12,0},{1,13},{5,9},{9,5},{13,1},{2,14},{6,10},... | collective-permute-start | bytes 258056 | tf_op jit(solution)/shard_map/ppermute | solution.py:312
  63.6 1.8 %collective-permute-done.22.rest_0_ = bf16[32,1344]{1,0:T(8,128)(2,1)S(1)} collective-permute-done((bf16[32,1344]{1,0:T(8,128)(2,1)S(1)}, bf16[32,1344]{1,0:T(8,128)(2,1)S(1)}, u32[]{:S(2)}, u32[]{:S(2)}) %collective-permute-start.22) | collective-permute-done | bytes 86048 | tf_op jit(solution)/shard_map/ppermute | solution.py:312
  65.4 0.8 %collective-permute-start.23 = (bf16[32,1344]{1,0:T(8,128)(2,1)S(1)}, bf16[32,1344]{1,0:T(8,128)(2,1)S(1)}, u32[]{:S(2)}, u32[]{:S(2)}) collective-permute-start(bf16[32,1344]{1,0:T(8,128)(2,1)S(1)} %piece.6), channel_id=1, source_target_pairs={{0,4},{4,0},{8,12},{12,8},{1,5},{5,1},{9,13},{13,9},{2,6},{6,2},{1... | collective-permute-start | bytes 258056 | tf_op jit(solution)/shard_map/ppermute | solution.py:312
  66.2 0.3 collective-permute-done.24.rest_0_
  66.5 2.3 %collective-permute-done.19.rest_0_ = bf16[32,1344]{1,0:T(8,128)(2,1)S(1)} collective-permute-done((bf16[32,1344]{1,0:T(8,128)(2,1)S(1)}, bf16[32,1344]{1,0:T(8,128)(2,1)S(1)}, u32[]{:S(2)}, u32[]{:S(2)}) %collective-permute-start.19) | collective-permute-done | bytes 86048 | tf_op jit(solution)/shard_map/ppermute | solution.py:312
  68.8 1.7 %collective-permute-done.21.rest_1_ = bf16[32,1344]{1,0:T(8,128)(2,1)S(1)} collective-permute-done((bf16[32,1344]{1,0:T(8,128)(2,1)S(1)}, bf16[32,1344]{1,0:T(8,128)(2,1)S(1)}, u32[]{:S(2)}, u32[]{:S(2)}) %collective-permute-start.21) | collective-permute-done | bytes 86048 | tf_op jit(solution)/shard_map/ppermute | solution.py:312
  70.5 0.8 %collective-permute-done.23.rest_2_ = bf16[32,1344]{1,0:T(8,128)(2,1)S(1)} collective-permute-done((bf16[32,1344]{1,0:T(8,128)(2,1)S(1)}, bf16[32,1344]{1,0:T(8,128)(2,1)S(1)}, u32[]{:S(2)}, u32[]{:S(2)}) %collective-permute-start.23) | collective-permute-done | bytes 86048 | tf_op jit(solution)/shard_map/ppermute | solution.py:312
  71.3 0.7 last.1
  (28 shorter events, 1.4 us)
Async XLA Ops:
  1.8 1.5 %collective-permute-start = (bf16[4,144,128]{2,1,0:T(8,128)(2,1)S(1)}, bf16[4,144,128]{2,1,0:T(8,128)(2,1)S(1)}, u32[]{:S(2)}, u32[]{:S(2)}) collective-permute-start(bf16[4,144,128]{2,1,0:T(8,128)(2,1)S(1)} %get-tuple-element.53), channel_id=1, source_target_pairs={{0,1},{1,0},{2,3},{3,2},{4,5},{5,4},{6,7},{7,6},{8,9},{9,8},{10,11... | collective-permute-start | bytes 442376 | tf_op jit(solution)/shard_map/ppermute | solution.py:312
  3.5 7.1 %collective-permute-start.1 = (bf16[4,144,128]{2,1,0:T(8,128)(2,1)S(1)}, bf16[4,144,128]{2,1,0:T(8,128)(2,1)S(1)}, u32[]{:S(2)}, u32[]{:S(2)}) collective-permute-start(bf16[4,144,128]{2,1,0:T(8,128)(2,1)S(1)} %chip_state.1.rest_0_), channel_id=1, source_target_pairs={{0,2},{1,3},{2,0},{3,1},{4,6},{5,7},{6,4},{7,5},{8,10},{9,11},{10,... | collective-permute-start | bytes 442376 | tf_op jit(solution)/shard_map/ppermute | solution.py:312
  10.7 5.5 %collective-permute-start.2 = (bf16[4,144,128]{2,1,0:T(8,128)(2,1)S(1)}, bf16[4,144,128]{2,1,0:T(8,128)(2,1)S(1)}, u32[]{:S(2)}, u32[]{:S(2)}) collective-permute-start(bf16[4,144,128]{2,1,0:T(8,128)(2,1)S(1)} %span.1.rest_2_), channel_id=1, source_target_pairs={{0,16},{16,0},{1,17},{17,1},{2,18},{18,2},{3,19},{19,3},{4,20},{20... | collective-permute-start | bytes 442376 | tf_op jit(solution)/shard_map/ppermute | solution.py:312
  16.4 1.4 %collective-permute-start.3 = (bf16[4,128,128]{2,1,0:T(8,128)(2,1)S(1)}, bf16[4,128,128]{2,1,0:T(8,128)(2,1)S(1)}, u32[]{:S(2)}, u32[]{:S(2)}) collective-permute-start(bf16[4,128,128]{2,1,0:T(8,128)(2,1)S(1)} %get-tuple-element.55), channel_id=1, source_target_pairs={{0,1},{1,0},{2,3},{3,2},{4,5},{5,4},{6,7},{7,6},{8,9},{9,8},{10,11... | collective-permute-start | bytes 393224 | tf_op jit(solution)/shard_map/ppermute | solution.py:312
  19.1 7.3 %collective-permute-start.4 = (bf16[32,1344]{1,0:T(8,128)(2,1)S(1)}, bf16[32,1344]{1,0:T(8,128)(2,1)S(1)}, u32[]{:S(2)}, u32[]{:S(2)}) collective-permute-start(bf16[32,1344]{1,0:T(8,128)(2,1)S(1)} %get-tuple-element.60), channel_id=1, source_target_pairs={{0,12},{4,8},{8,4},{12,0},{1,13},{5,9},{9,5},{13,1},{2,14},{6,10},... | collective-permute-start | bytes 258056 | tf_op jit(solution)/shard_map/ppermute | solution.py:312
  22.8 7.9 %collective-permute-start.5 = (bf16[32,1344]{1,0:T(8,128)(2,1)S(1)}, bf16[32,1344]{1,0:T(8,128)(2,1)S(1)}, u32[]{:S(2)}, u32[]{:S(2)}) collective-permute-start(bf16[32,1344]{1,0:T(8,128)(2,1)S(1)} %get-tuple-element.61), channel_id=1, source_target_pairs={{0,8},{4,12},{8,0},{12,4},{1,9},{5,13},{9,1},{13,5},{2,10},{6,14},... | collective-permute-start | bytes 258056 | tf_op jit(solution)/shard_map/ppermute | solution.py:312
  22.8 7.9 %collective-permute-start.6 = (bf16[32,1344]{1,0:T(8,128)(2,1)S(1)}, bf16[32,1344]{1,0:T(8,128)(2,1)S(1)}, u32[]{:S(2)}, u32[]{:S(2)}) collective-permute-start(bf16[32,1344]{1,0:T(8,128)(2,1)S(1)} %get-tuple-element.62), channel_id=1, source_target_pairs={{0,4},{4,0},{8,12},{12,8},{1,5},{5,1},{9,13},{13,9},{2,6},{6,2},{1... | collective-permute-start | bytes 258056 | tf_op jit(solution)/shard_map/ppermute | solution.py:312
  30.8 7.5 %collective-permute-start.8 = (bf16[32,1408]{1,0:T(8,128)(2,1)S(1)}, bf16[32,1408]{1,0:T(8,128)(2,1)S(1)}, u32[]{:S(2)}, u32[]{:S(2)}) collective-permute-start(bf16[32,1408]{1,0:T(8,128)(2,1)S(1)} %get-tuple-element.69), channel_id=1, source_target_pairs={{0,8},{4,12},{8,0},{12,4},{1,9},{5,13},{9,1},{13,5},{2,10},{6,14},... | collective-permute-start | bytes 270344 | tf_op jit(solution)/shard_map/ppermute | solution.py:312
  31.3 9.4 %collective-permute-start.7 = (bf16[32,1408]{1,0:T(8,128)(2,1)S(1)}, bf16[32,1408]{1,0:T(8,128)(2,1)S(1)}, u32[]{:S(2)}, u32[]{:S(2)}) collective-permute-start(bf16[32,1408]{1,0:T(8,128)(2,1)S(1)} %get-tuple-element.69), channel_id=1, source_target_pairs={{0,4},{4,0},{8,12},{12,8},{1,5},{5,1},{9,13},{13,9},{2,6},{6,2},{1... | collective-permute-start | bytes 270344 | tf_op jit(solution)/shard_map/ppermute | solution.py:312
  33.9 6.9 %collective-permute-start.10 = (bf16[32,1408]{1,0:T(8,128)(2,1)S(1)}, bf16[32,1408]{1,0:T(8,128)(2,1)S(1)}, u32[]{:S(2)}, u32[]{:S(2)}) collective-permute-start(bf16[32,1408]{1,0:T(8,128)(2,1)S(1)} %get-tuple-element.69), channel_id=1, source_target_pairs={{0,2},{1,3},{2,0},{3,1},{4,6},{5,7},{6,4},{7,5},{8,10},{9,11},{10,... | collective-permute-start | bytes 270344 | tf_op jit(solution)/shard_map/ppermute | solution.py:312
  35.4 6.3 %collective-permute-start.9 = (bf16[32,1408]{1,0:T(8,128)(2,1)S(1)}, bf16[32,1408]{1,0:T(8,128)(2,1)S(1)}, u32[]{:S(2)}, u32[]{:S(2)}) collective-permute-start(bf16[32,1408]{1,0:T(8,128)(2,1)S(1)} %get-tuple-element.69), channel_id=1, source_target_pairs={{0,12},{4,8},{8,4},{12,0},{1,13},{5,9},{9,5},{13,1},{2,14},{6,10},... | collective-permute-start | bytes 270344 | tf_op jit(solution)/shard_map/ppermute | solution.py:312
  38.3 5.0 %collective-permute-start.12 = (bf16[32,1408]{1,0:T(8,128)(2,1)S(1)}, bf16[32,1408]{1,0:T(8,128)(2,1)S(1)}, u32[]{:S(2)}, u32[]{:S(2)}) collective-permute-start(bf16[32,1408]{1,0:T(8,128)(2,1)S(1)} %collective-permute-done.8), channel_id=1, source_target_pairs={{0,2},{1,3},{2,0},{3,1},{4,6},{5,7},{6,4},{7,5},{8,10},{9,11},{10,... | collective-permute-start | bytes 270344 | tf_op jit(solution)/shard_map/ppermute | solution.py:312
  40.8 4.5 %collective-permute-start.11 = (bf16[32,1408]{1,0:T(8,128)(2,1)S(1)}, bf16[32,1408]{1,0:T(8,128)(2,1)S(1)}, u32[]{:S(2)}, u32[]{:S(2)}) collective-permute-start(bf16[32,1408]{1,0:T(8,128)(2,1)S(1)} %collective-permute-done.7), channel_id=1, source_target_pairs={{0,2},{1,3},{2,0},{3,1},{4,6},{5,7},{6,4},{7,5},{8,10},{9,11},{10,... | collective-permute-start | bytes 270344 | tf_op jit(solution)/shard_map/ppermute | solution.py:312
  45.4 1.7 %collective-permute-start.13 = (bf16[128,1408]{1,0:T(8,128)(2,1)S(1)}, bf16[128,1408]{1,0:T(8,128)(2,1)S(1)}, u32[]{:S(2)}, u32[]{:S(2)}) collective-permute-start(bf16[128,1408]{1,0:T(8,128)(2,1)S(1)} %constant_dynamic-update-slice_fusion.mine_ref), channel_id=1, source_target_pairs={{0,1},{1,0},{2,3},{3,2},{4,5},{5,4},{6,7},{7,6},{8,9},{9,8},{10,11... | collective-permute-start | bytes 1081352 | tf_op jit(solution)/shard_map/ppermute | solution.py:312
  45.5 5.0 %collective-permute-start.14 = (bf16[32,1408]{1,0:T(8,128)(2,1)S(1)}, bf16[32,1408]{1,0:T(8,128)(2,1)S(1)}, u32[]{:S(2)}, u32[]{:S(2)}) collective-permute-start(bf16[32,1408]{1,0:T(8,128)(2,1)S(1)} %collective-permute-done.9), channel_id=1, source_target_pairs={{0,2},{1,3},{2,0},{3,1},{4,6},{5,7},{6,4},{7,5},{8,10},{9,11},{10,... | collective-permute-start | bytes 270344 | tf_op jit(solution)/shard_map/ppermute | solution.py:312
  50.6 1.7 %collective-permute-start.16 = (bf16[128,1408]{1,0:T(8,128)(2,1)S(1)}, bf16[128,1408]{1,0:T(8,128)(2,1)S(1)}, u32[]{:S(2)}, u32[]{:S(2)}) collective-permute-start(bf16[128,1408]{1,0:T(8,128)(2,1)S(1)} %constant_dynamic-update-slice_fusion.4.mine_ref), channel_id=1, source_target_pairs={{0,1},{1,0},{2,3},{3,2},{4,5},{5,4},{6,7},{7,6},{8,9},{9,8},{10,11... | collective-permute-start | bytes 1081352 | tf_op jit(solution)/shard_map/ppermute | solution.py:312
  54.1 1.7 %collective-permute-start.17 = (bf16[128,1344]{1,0:T(8,128)(2,1)S(1)}, bf16[128,1344]{1,0:T(8,128)(2,1)S(1)}, u32[]{:S(2)}, u32[]{:S(2)}) collective-permute-start(bf16[128,1344]{1,0:T(8,128)(2,1)S(1)} %get-tuple-element.82), channel_id=1, source_target_pairs={{0,1},{1,0},{2,3},{3,2},{4,5},{5,4},{6,7},{7,6},{8,9},{9,8},{10,11... | collective-permute-start | bytes 1032200 | tf_op jit(solution)/shard_map/ppermute | solution.py:312
  54.3 5.8 %collective-permute-start.15 = (bf16[128,1344]{1,0:T(8,128)(2,1)S(1)}, bf16[128,1344]{1,0:T(8,128)(2,1)S(1)}, u32[]{:S(2)}, u32[]{:S(2)}) collective-permute-start(bf16[128,1344]{1,0:T(8,128)(2,1)S(1)} %get-tuple-element.76), channel_id=1, source_target_pairs={{0,1},{1,0},{2,3},{3,2},{4,5},{5,4},{6,7},{7,6},{8,9},{9,8},{10,11... | collective-permute-start | bytes 1032200 | tf_op jit(solution)/shard_map/ppermute | solution.py:312
  56.0 5.5 %collective-permute-start.18 = (bf16[32,1344]{1,0:T(8,128)(2,1)S(1)}, bf16[32,1344]{1,0:T(8,128)(2,1)S(1)}, u32[]{:S(2)}, u32[]{:S(2)}) collective-permute-start(bf16[32,1344]{1,0:T(8,128)(2,1)S(1)} %get-tuple-element.83), channel_id=1, source_target_pairs={{0,2},{1,3},{2,0},{3,1},{4,6},{5,7},{6,4},{7,5},{8,10},{9,11},{10,... | collective-permute-start | bytes 258056 | tf_op jit(solution)/shard_map/ppermute | solution.py:312
  57.0 6.4 %collective-permute-start.20 = (bf16[32,1344]{1,0:T(8,128)(2,1)S(1)}, bf16[32,1344]{1,0:T(8,128)(2,1)S(1)}, u32[]{:S(2)}, u32[]{:S(2)}) collective-permute-start(bf16[32,1344]{1,0:T(8,128)(2,1)S(1)} %get-tuple-element.84), channel_id=1, source_target_pairs={{0,2},{1,3},{2,0},{3,1},{4,6},{5,7},{6,4},{7,5},{8,10},{9,11},{10,... | collective-permute-start | bytes 258056 | tf_op jit(solution)/shard_map/ppermute | solution.py:312
  58.1 7.3 %collective-permute-start.22 = (bf16[32,1344]{1,0:T(8,128)(2,1)S(1)}, bf16[32,1344]{1,0:T(8,128)(2,1)S(1)}, u32[]{:S(2)}, u32[]{:S(2)}) collective-permute-start(bf16[32,1344]{1,0:T(8,128)(2,1)S(1)} %get-tuple-element.85), channel_id=1, source_target_pairs={{0,2},{1,3},{2,0},{3,1},{4,6},{5,7},{6,4},{7,5},{8,10},{9,11},{10,... | collective-permute-start | bytes 258056 | tf_op jit(solution)/shard_map/ppermute | solution.py:312
  59.0 7.5 %collective-permute-start.24 = (bf16[32,1344]{1,0:T(8,128)(2,1)S(1)}, bf16[32,1344]{1,0:T(8,128)(2,1)S(1)}, u32[]{:S(2)}, u32[]{:S(2)}) collective-permute-start(bf16[32,1344]{1,0:T(8,128)(2,1)S(1)} %get-tuple-element.86), channel_id=1, source_target_pairs={{0,2},{1,3},{2,0},{3,1},{4,6},{5,7},{6,4},{7,5},{8,10},{9,11},{10,... | collective-permute-start | bytes 258056 | tf_op jit(solution)/shard_map/ppermute | solution.py:312
  61.5 7.3 %collective-permute-start.19 = (bf16[32,1344]{1,0:T(8,128)(2,1)S(1)}, bf16[32,1344]{1,0:T(8,128)(2,1)S(1)}, u32[]{:S(2)}, u32[]{:S(2)}) collective-permute-start(bf16[32,1344]{1,0:T(8,128)(2,1)S(1)} %piece.4), channel_id=1, source_target_pairs={{0,12},{4,8},{8,4},{12,0},{1,13},{5,9},{9,5},{13,1},{2,14},{6,10},... | collective-permute-start | bytes 258056 | tf_op jit(solution)/shard_map/ppermute | solution.py:312
  63.5 7.0 %collective-permute-start.21 = (bf16[32,1344]{1,0:T(8,128)(2,1)S(1)}, bf16[32,1344]{1,0:T(8,128)(2,1)S(1)}, u32[]{:S(2)}, u32[]{:S(2)}) collective-permute-start(bf16[32,1344]{1,0:T(8,128)(2,1)S(1)} %piece.5), channel_id=1, source_target_pairs={{0,8},{4,12},{8,0},{12,4},{1,9},{5,13},{9,1},{13,5},{2,10},{6,14},... | collective-permute-start | bytes 258056 | tf_op jit(solution)/shard_map/ppermute | solution.py:312
  65.4 5.9 %collective-permute-start.23 = (bf16[32,1344]{1,0:T(8,128)(2,1)S(1)}, bf16[32,1344]{1,0:T(8,128)(2,1)S(1)}, u32[]{:S(2)}, u32[]{:S(2)}) collective-permute-start(bf16[32,1344]{1,0:T(8,128)(2,1)S(1)} %piece.6), channel_id=1, source_target_pairs={{0,4},{4,0},{8,12},{12,8},{1,5},{5,1},{9,13},{13,9},{2,6},{6,2},{1... | collective-permute-start | bytes 258056 | tf_op jit(solution)/shard_map/ppermute | solution.py:312

commit v5 on v4

--- a/solution.py
+++ b/solution.py
@@ -217,7 +217,7 @@
         load.wait()
 
 
-def mixed_kernel(local_ref, grown_ref, c_ref, norm_ref, w_ref, mine_ref, got_ref, *rest):
+def mixed_kernel(after_up, after_down, local_ref, grown_ref, c_ref, norm_ref, w_ref, mine_ref, got_ref, *rest):
     outs, (normed_ref, state_ref) = rest[:-2], rest[-2:]
     half = mine_ref.shape[0]
     pairs = 2 * half
@@ -264,39 +264,34 @@
     rows_ref[:, :width] = (value * scale * gain_ref[...]).astype(BF16)
 
 
-def expert_kernel(experts, up_ref, down_ref, mine_ref, partner_ref, kept_ref, sent_ref):
+def expert_kernel(experts, up_ref, down_ref, other_up_ref, other_down_ref, *rest):
+    count = len(rest) // 2
+    ins, outs = rest[:count], rest[count:]
     width = up_ref.shape[2]
     start = width // LANES * LANES
-    half = mine_ref.shape[0]
-    rows = jnp.concatenate([mine_ref[:, :width], partner_ref[:, :width]], axis=0)
-    up = lax.dot_general(rows, up_ref[0], NT, preferred_element_type=F32)
-    up = jnp.maximum(up, 0.0)
-    activated = (up * up).astype(BF16)
-    tail = jnp.concatenate([mine_ref[:, start:], partner_ref[:, start:]], axis=0).astype(F32)
+    rows = jnp.concatenate([ref[:, :width] for ref in ins], axis=0)
+    tail = jnp.concatenate([ref[:, start:] for ref in ins], axis=0).astype(F32)
     lane = lax.broadcasted_iota(jnp.int32, tail.shape, 1) + start - width
     own = lax.axis_index("head") * lax.axis_size("exp") + lax.axis_index("exp")
-    chosen = (lane == own) | (lane == own + experts)
-    gate = jnp.sum(jnp.where(chosen, tail, 0.0), axis=1, keepdims=True)
-    out = jnp.dot(activated, down_ref[0], preferred_element_type=F32) * gate
-    kept_ref[...] = out[:half].astype(BF16)
-    sent_ref[...] = out[half:].astype(BF16)
-
-
-def split_sum_kernel(kept_ref, got_ref, *outs):
-    rows = outs[0].shape[0]
+    other = own + 1 - 2 * core_index()
+    total = 0.0
+    for expert, up_of, down_of in ((own, up_ref, down_ref), (other, other_up_ref, other_down_ref)):
+        up = lax.dot_general(rows, up_of[0], NT, preferred_element_type=F32)
+        up = jnp.maximum(up, 0.0)
+        activated = (up * up).astype(BF16)
+        chosen = (lane == expert) | (lane == expert + experts)
+        gate = jnp.sum(jnp.where(chosen, tail, 0.0), axis=1, keepdims=True)
+        total = total + jnp.dot(activated, down_of[0], preferred_element_type=F32) * gate
+    size = outs[0].shape[0]
     for at, out in enumerate(outs):
-        span = slice(at * rows, (at + 1) * rows)
-        out[...] = (kept_ref[span].astype(F32) + got_ref[span].astype(F32)).astype(BF16)
-
-
-def piece_kernel(at, kept_ref, got_ref, *rest):
-    parts, out_ref = rest[:-1], rest[-1]
-    rows = out_ref.shape[0]
-    span = slice(at * rows, (at + 1) * rows)
-    total = kept_ref[span].astype(F32) + got_ref[span].astype(F32)
-    for part in parts:
-        total = total + part[...].astype(F32)
-    out_ref[...] = total.astype(BF16)
+        out[...] = total[at * size : (at + 1) * size].astype(BF16)
+
+
+def sum_kernel(*refs):
+    total = refs[0][...].astype(F32)
+    for ref in refs[1:-1]:
+        total = total + ref[...].astype(F32)
+    refs[-1][...] = total.astype(BF16)
 
 
 def last_kernel(hidden_ref, *rest):
@@ -358,6 +353,8 @@
         [pltpu.VMEM(turned[0].shape, jnp.int32), pltpu.VMEM(turned[1].shape, F32), dma((6,))],
         megabytes=16,
     )
+    up_turned = jnp.swapaxes(w_up, 1, 2)
+    other_up, other_down = swap(up_turned, "exp", 1), swap(w_down, "exp", 1)
     got = swap(send, "exp", 1)
     chip = call(chip_state_kernel, "chip_state", packed, [(VMEM, keep), (VMEM, got)])
     along_y = [chip] + [swap(chip, "exp", 2 * d) for d in range(1, chips)]
@@ -382,10 +379,10 @@
         mixed_kernel,
         "mixed",
         [struct((rows, model), BF16)] * head_size,
-        [(VMEM, value) for value in (local, grown, c_held, norm_held, w_held, before, before_got)],
+        [(ANY, other_up), (ANY, other_down)]
+        + [(VMEM, value) for value in (local, grown, c_held, norm_held, w_held, before, before_got)],
         [pltpu.VMEM((length, channels), BF16), pltpu.VMEM((pairs, STATE, LANES), BF16)],
     )
-    up_turned = jnp.swapaxes(w_up, 1, 2)
     up_held, down_held = call(
         weights_kernel,
         "weights",
@@ -402,51 +399,48 @@
         [(ANY, up_held)] + [(VMEM, value) for value in (resid_held, gate_lanes, gain_held, *parts)],
     )
 
-    def through_expert(members):
-        mine = jnp.concatenate(members, axis=0)
-        kept, sent = call(
+    def through_experts(members):
+        produced = call(
             functools.partial(expert_kernel, experts),
             "experts",
-            [struct((head_size * rows, model), BF16)] * 2,
-            [(VMEM, value) for value in (up_held, down_held, mine, swap(mine, "exp", 1))],
+            [struct((rows, model), BF16)] * len(members),
+            [(VMEM, value) for value in (up_held, down_held, other_up, other_down, *members.values())],
             megabytes=16,
         )
-        return kept, sent
-
-    near = [own_rows] + [swap(own_rows, "head", s) for s in reversed(order)]
-    far = [[swap(member, "exp", 2 * d) for member in near] for d in range(1, chips)]
-    near, early = lax.optimization_barrier((near, [members[:-1] for members in far]))
-    far = [members + others[-1:] for members, others in zip(early, far)]
-    near, far = near[::-1], [members[::-1] for members in far]
-    kept, sent = through_expert(near)
-    kept, sent, far = lax.optimization_barrier((kept, sent, far))
-    near_got = swap(sent, "exp", 1)
-    arrived = [[] for _ in near]
-    for d in range(1, chips):
-        far_kept, far_sent = through_expert(far[d - 1])
-        far_got = swap(far_sent, "exp", 1)
-        pieces = call(
-            split_sum_kernel,
-            "split",
-            [struct((rows, model), BF16)] * head_size,
-            [(VMEM, far_kept), (VMEM, far_got)],
-        )
-        for at, piece in enumerate(pieces):
-            arrived[at].append(swap(piece, "exp", 2 * d))
-    final = []
-    for at, mask in enumerate(order + [0]):
-        piece = call(
-            functools.partial(piece_kernel, at),
-            "piece",
-            struct((rows, model), BF16),
-            [(VMEM, value) for value in (kept, near_got, *arrived[at])],
-        )
-        final.append(swap(piece, "head", mask) if mask else piece)
+        return dict(zip(members, produced))
+
+    near = {0: own_rows} | {s: swap(own_rows, "head", s) for s in range(1, head_size)}
+    far = [{s: swap(near[s], "exp", 2 * d) for s in near} for d in range(1, chips)]
+    early = [{s: members[s] for s in members if s != head_size - 1} for members in far]
+    near, early = lax.optimization_barrier((near, early))
+    far = [others | members for others, members in zip(far, early)]
+    back_near = through_experts(near)
+    back_near, far = lax.optimization_barrier((back_near, far))
+    back_far = [through_experts(members) for members in far]
+    relayed, direct = [s for s in order if s % 2 == 0], [s for s in order if s % 2 == 1]
+    later = [0] + direct[1:]
+
+    def diagonal(s):
+        return [swap(members[s], ("head", "exp"), s * exp_size + 2 * d) for d, members in enumerate(back_far, 1)]
+
+    arrived = [swap(back_near[s], "head", s) for s in direct]
+    got = {s: [swap(members[s], "exp", 2 * d) for d, members in enumerate(back_far, 1)] for s in relayed}
+    arrived, got = lax.optimization_barrier((arrived, got))
+    arrived += [part for s in direct[:1] for part in diagonal(s)]
+    totals = {
+        s: call(sum_kernel, "sum", struct((rows, model), BF16), [(VMEM, v) for v in (back_near[s], *got[s])])
+        for s in relayed
+    }
+    totals, rest = lax.optimization_barrier((totals, [{s: members[s] for s in later} for members in back_far]))
+    back_far = rest
+    arrived += [swap(totals[s], "head", s) for s in relayed]
+    for s in later:
+        arrived += diagonal(s)
     return call(
         last_kernel,
         "last",
         struct(resid.shape, BF16),
-        [(VMEM, value) for value in (hidden, *final)],
+        [(VMEM, value) for value in (hidden, back_near[0], *arrived)],
         pinned=False,
     )
 

time: 72.3 us -> 71.1 us (0.983)
  waiting for transfers between devices: 28.4 us -> 23.4 us
  starting transfers between devices: 26.7 us -> 29.1 us
  Pallas kernels: 15.3 us -> 16.8 us
    ppermute x25 -> x23, waiting for transfers between devices: 28.4 us -> 23.4 us  [swap(): return lax.ppermute(value, axis, [(i, i ^ mask) for i in range(size)])]
    ppermute x25 -> x23, starting transfers between devices: 26.7 us -> 29.1 us  [swap(): return lax.ppermute(value, axis, [(i, i ^ mask) for i in range(size)])]
    pallas_call x17 -> x13, Pallas kernels: 15.3 us -> 16.8 us  [call(): pl.pallas_call(kernel, out_shape=jax.tree.map(lambda out: pltpu.VMEM(out....]
  transfers between devices with their start and end apart: 25 -> 23, of which waited for: 21 -> 14; matrix products, arithmetic and copies ran while one was open for 2% -> 2% of each run, Pallas kernels for 12% -> 21%
where the time goes in v5:
time: 71.1 us; the launch traced here: 70.8 us
  starting transfers between devices  29.1 us (41%)
  waiting for transfers between devices  23.4 us (33%)
  Pallas kernels  16.8 us (24%)
  local copies, waits for them, and re-layouts  1.29 us (2%)
    ppermute x23, starting transfers between devices, swap(): return lax.ppermute(value, axis, [(i, i ^ mask) for i in range(size)])  29.1 us
    ppermute x23, waiting for transfers between devices, swap(): return lax.ppermute(value, axis, [(i, i ^ mask) for i in range(size)])  23.4 us
    pallas_call x13, Pallas kernels, call(): pl.pallas_call(kernel, out_shape=jax.tree.map(lambda out: pltpu.VMEM(out....  16.8 us
  transfers between devices with their start and end apart: 23, of which 14 were waited for; matrix products, arithmetic and copies ran while one was open for 2% of the time, Pallas kernels for 21%

profile of v5, /device:TPU:0, one launch (start us, length us, event | category | flops | bytes accessed | tf_op | source)
XLA Modules:
  0.0 70.8 jit_solution(9658387910073880628)
XLA Ops:
  0.0 0.5 collective-permute-start
  0.5 0.1 collective-permute-start.1
  0.5 1.8 %state.1 = (bf16[4,144,128]{2,1,0:T(8,128)(2,1)S(1)}, bf16[4,144,128]{2,1,0:T(8,128)(2,1)S(1)}) custom-call(bf16[128,1024]{1,0:T(8,128)(2,1)} %x_hbm.3, bf16[128,256]{1,0:T(8,128)(2,1)} %b_hbm.3, f32[16,128]{1,0:T(8,128)} %bitcast.11, f32[1,16]{1,0:T(1,128)} %bitcast.16), custom_call_target="tpu_custom_call" | custom-call | tf_op jit(solution)/shard_map/state/pallas_call | solution.py:29
  2.3 0.5 collective-permute-start.2
  2.9 2.5 %collective-permute-done.2.got_ref = bf16[4,144,128]{2,1,0:T(8,128)(2,1)S(1)} collective-permute-done((bf16[4,144,128]{2,1,0:T(8,128)(2,1)S(1)}, bf16[4,144,128]{2,1,0:T(8,128)(2,1)S(1)}, u32[]{:S(2)}, u32[]{:S(2)}) %collective-permute-start.2) | collective-permute-done | bytes 147488 | tf_op jit(solution)/shard_map/ppermute | solution.py:307
  5.4 0.1 chip_state.1.rest_0_
  5.5 3.0 %collective-permute-start.3 = (bf16[4,144,128]{2,1,0:T(8,128)(2,1)S(1)}, bf16[4,144,128]{2,1,0:T(8,128)(2,1)S(1)}, u32[]{:S(2)}, u32[]{:S(2)}) collective-permute-start(bf16[4,144,128]{2,1,0:T(8,128)(2,1)S(1)} %chip_state.1.rest_0_), channel_id=1, source_target_pairs={{0,2},{1,3},{2,0},{3,1},{4,6},{5,7},{6,4},{7,5},{8,10},{9,11},{10,... | collective-permute-start | bytes 442376 | tf_op jit(solution)/shard_map/ppermute | solution.py:307
  8.4 2.4 %inside.1 = (f32[128,1024]{1,0:T(8,128)S(1)}, f32[128,1024]{1,0:T(8,128)S(1)}, bf16[128,256]{1,0:T(8,128)(2,1)S(1)}) custom-call(bf16[128,1024]{1,0:T(8,128)(2,1)} %x_hbm.3, bf16[128,1024]{1,0:T(8,128)(2,1)} %z_hbm.1, bf16[128,256]{1,0:T(8,128)(2,1)} %b_hbm.3, bf16[128,256]{1,0:T(8,128)(2,1)} %c_hbm.1, f32[16,128]{1,0:T(8,128)} %bitcast.12, ...), custom_call_target="tpu_custom_call" | custom-call | tf_op jit(solution)/shard_map/inside/pallas_call | solution.py:29
  10.9 1.7 %collective-permute-done.3.rest_1_ = bf16[4,144,128]{2,1,0:T(8,128)(2,1)S(1)} collective-permute-done((bf16[4,144,128]{2,1,0:T(8,128)(2,1)S(1)}, bf16[4,144,128]{2,1,0:T(8,128)(2,1)S(1)}, u32[]{:S(2)}, u32[]{:S(2)}) %collective-permute-start.3) | collective-permute-done | bytes 147488 | tf_op jit(solution)/shard_map/ppermute | solution.py:307
  12.6 0.1 span.1.rest_2_
  12.7 1.8 %collective-permute-start.4 = (bf16[4,144,128]{2,1,0:T(8,128)(2,1)S(1)}, bf16[4,144,128]{2,1,0:T(8,128)(2,1)S(1)}, u32[]{:S(2)}, u32[]{:S(2)}) collective-permute-start(bf16[4,144,128]{2,1,0:T(8,128)(2,1)S(1)} %span.1.rest_2_), channel_id=1, source_target_pairs={{0,16},{16,0},{1,17},{17,1},{2,18},{18,2},{3,19},{19,3},{4,20},{20... | collective-permute-start | bytes 442376 | tf_op jit(solution)/shard_map/ppermute | solution.py:307
  14.5 1.3 %broadcast_in_dim.14.gain_hbm = f32[1,1344]{1,0:T(1,128)} reshape(f32[1344]{0:T(1024)} %param.27) | data formatting | bytes 10752 | tf_op jit(solution)/shard_map/broadcast_in_dim | solution.py:352
  15.8 1.9 %prep.1 = (bf16[32,128]{1,0:T(8,128)(2,1)S(1)}, bf16[1,32,1344]{2,1,0:T(8,128)(2,1)S(1)}, f32[1,1344]{1,0:T(1,128)S(1)}, f32[1,1024]{1,0:T(1,128)S(1)}, bf16[1344,1024]{1,0:T(8,128)(2,1)S(1)}) custom-call(bf16[1,32,1344]{2,1,0:T(8,128)(2,1)} %resid_hbm.1, s32[6,1,32]{2,1,0:T(1,128)} %bitcast.14, f32[6,1,32]{2,1,0:T(1,128)} %bitcast.15, ...), custom_call_target="tpu_custom_call" | custom-call | tf_op jit(solution)/shard_map/prep/pallas_call | solution.py:29
  17.7 0.4 collective-permute-done.4.rest_3_
  18.1 0.3 before.1
  18.4 0.1 collective-permute-start.5
  18.5 1.3 %collective-permute-done.5.got_ref = bf16[4,128,128]{2,1,0:T(8,128)(2,1)S(1)} collective-permute-done((bf16[4,128,128]{2,1,0:T(8,128)(2,1)S(1)}, bf16[4,128,128]{2,1,0:T(8,128)(2,1)S(1)}, u32[]{:S(2)}, u32[]{:S(2)}) %collective-permute-start.5) | collective-permute-done | bytes 131104 | tf_op jit(solution)/shard_map/ppermute | solution.py:307
  19.8 1.3 %mixed.1 = (bf16[32,1344]{1,0:T(8,128)(2,1)S(1)}, bf16[32,1344]{1,0:T(8,128)(2,1)S(1)}, bf16[32,1344]{1,0:T(8,128)(2,1)S(1)}, bf16[32,1344]{1,0:T(8,128)(2,1)S(1)}) custom-call(bf16[1,928,1344]{2,1,0:T(8,128)(2,1)S(1)} %collective-permute-done.after_up.other_up_ref, bf16[1,928,1344]{2,1,0:T(8,128)(2,1)S(1)} %collective-permute-done.1.after_down.other_down_ref, ...), custom_call_target="tpu_custom_call" | custom-call | tf_op jit(solution)/shard_map/mixed/pallas_call | solution.py:29
  21.2 3.7 %collective-permute-start.6 = (bf16[32,1344]{1,0:T(8,128)(2,1)S(1)}, bf16[32,1344]{1,0:T(8,128)(2,1)S(1)}, u32[]{:S(2)}, u32[]{:S(2)}) collective-permute-start(bf16[32,1344]{1,0:T(8,128)(2,1)S(1)} %get-tuple-element.68), channel_id=1, source_target_pairs={{0,12},{4,8},{8,4},{12,0},{1,13},{5,9},{9,5},{13,1},{2,14},{6,10},... | collective-permute-start | bytes 258056 | tf_op jit(solution)/shard_map/ppermute | solution.py:307
  24.8 0.8 %collective-permute-start.8 = (bf16[32,1344]{1,0:T(8,128)(2,1)S(1)}, bf16[32,1344]{1,0:T(8,128)(2,1)S(1)}, u32[]{:S(2)}, u32[]{:S(2)}) collective-permute-start(bf16[32,1344]{1,0:T(8,128)(2,1)S(1)} %get-tuple-element.70), channel_id=1, source_target_pairs={{0,4},{4,0},{8,12},{12,8},{1,5},{5,1},{9,13},{13,9},{2,6},{6,2},{1... | collective-permute-start | bytes 258056 | tf_op jit(solution)/shard_map/ppermute | solution.py:307
  25.6 2.5 %weights.1 = (bf16[1,928,1344]{2,1,0:T(8,128)(2,1)S(1)}, bf16[1,928,1344]{2,1,0:T(8,128)(2,1)S(1)}) custom-call(bf16[32,1344]{1,0:T(8,128)(2,1)S(1)} %get-tuple-element.64.after_ref.rest_0_, bf16[1,928,1344]{2,1,0:T(8,128)(2,1)} %bitcast.10, bf16[1,928,1344]{2,1,0:T(8,128)(2,1)} %down_hbm.1), custom_call_target="tpu_custom_call" | custom-call | tf_op jit(solution)/shard_map/weights/pallas_call | solution.py:29
  28.2 0.3 collective-permute-done.6.rest_1_
  28.5 4.2 %collective-permute-done.7.rest_2_ = bf16[32,1344]{1,0:T(8,128)(2,1)S(1)} collective-permute-done((bf16[32,1344]{1,0:T(8,128)(2,1)S(1)}, bf16[32,1344]{1,0:T(8,128)(2,1)S(1)}, u32[]{:S(2)}, u32[]{:S(2)}) %collective-permute-start.7) | collective-permute-done | bytes 86048 | tf_op jit(solution)/shard_map/ppermute | solution.py:307
  32.7 0.2 rows.1
  32.9 0.5 collective-permute-start.10
  33.4 2.6 %collective-permute-start.9 = (bf16[32,1408]{1,0:T(8,128)(2,1)S(1)}, bf16[32,1408]{1,0:T(8,128)(2,1)S(1)}, u32[]{:S(2)}, u32[]{:S(2)}) collective-permute-start(bf16[32,1408]{1,0:T(8,128)(2,1)S(1)} %get-tuple-element.74.rest_0_), channel_id=1, source_target_pairs={{0,4},{4,0},{8,12},{12,8},{1,5},{5,1},{9,13},{13,9},{2,6},{6,2},{1... | collective-permute-start | bytes 270344 | tf_op jit(solution)/shard_map/ppermute | solution.py:307
  36.0 1.3 %collective-permute-start.11 = (bf16[32,1408]{1,0:T(8,128)(2,1)S(1)}, bf16[32,1408]{1,0:T(8,128)(2,1)S(1)}, u32[]{:S(2)}, u32[]{:S(2)}) collective-permute-start(bf16[32,1408]{1,0:T(8,128)(2,1)S(1)} %get-tuple-element.74.rest_0_), channel_id=1, source_target_pairs={{0,12},{4,8},{8,4},{12,0},{1,13},{5,9},{9,5},{13,1},{2,14},{6,10},... | collective-permute-start | bytes 270344 | tf_op jit(solution)/shard_map/ppermute | solution.py:307
  37.3 1.5 %collective-permute-start.12 = (bf16[32,1408]{1,0:T(8,128)(2,1)S(1)}, bf16[32,1408]{1,0:T(8,128)(2,1)S(1)}, u32[]{:S(2)}, u32[]{:S(2)}) collective-permute-start(bf16[32,1408]{1,0:T(8,128)(2,1)S(1)} %get-tuple-element.74.rest_0_), channel_id=1, source_target_pairs={{0,2},{1,3},{2,0},{3,1},{4,6},{5,7},{6,4},{7,5},{8,10},{9,11},{10,... | collective-permute-start | bytes 270344 | tf_op jit(solution)/shard_map/ppermute | solution.py:307
  38.8 2.5 %collective-permute-done.10.rest_2_ = bf16[32,1408]{1,0:T(8,128)(2,1)S(1)} collective-permute-done((bf16[32,1408]{1,0:T(8,128)(2,1)S(1)}, bf16[32,1408]{1,0:T(8,128)(2,1)S(1)}, u32[]{:S(2)}, u32[]{:S(2)}) %collective-permute-start.10) | collective-permute-done | bytes 90144 | tf_op jit(solution)/shard_map/ppermute | solution.py:307
  41.3 1.5 %collective-permute-start.14 = (bf16[32,1408]{1,0:T(8,128)(2,1)S(1)}, bf16[32,1408]{1,0:T(8,128)(2,1)S(1)}, u32[]{:S(2)}, u32[]{:S(2)}) collective-permute-start(bf16[32,1408]{1,0:T(8,128)(2,1)S(1)} %collective-permute-done.10.rest_2_), channel_id=1, source_target_pairs={{0,2},{1,3},{2,0},{3,1},{4,6},{5,7},{6,4},{7,5},{8,10},{9,11},{10,... | collective-permute-start | bytes 270344 | tf_op jit(solution)/shard_map/ppermute | solution.py:307
  42.8 0.5 collective-permute-start.13
  43.4 1.5 %collective-permute-start.15 = (bf16[32,1408]{1,0:T(8,128)(2,1)S(1)}, bf16[32,1408]{1,0:T(8,128)(2,1)S(1)}, u32[]{:S(2)}, u32[]{:S(2)}) collective-permute-start(bf16[32,1408]{1,0:T(8,128)(2,1)S(1)} %collective-permute-done.11.rest_3_), channel_id=1, source_target_pairs={{0,2},{1,3},{2,0},{3,1},{4,6},{5,7},{6,4},{7,5},{8,10},{9,11},{10,... | collective-permute-start | bytes 270344 | tf_op jit(solution)/shard_map/ppermute | solution.py:307
  44.9 1.0 %collective-permute-done.14.rest_2_ = bf16[32,1408]{1,0:T(8,128)(2,1)S(1)} collective-permute-done((bf16[32,1408]{1,0:T(8,128)(2,1)S(1)}, bf16[32,1408]{1,0:T(8,128)(2,1)S(1)}, u32[]{:S(2)}, u32[]{:S(2)}) %collective-permute-start.14) | collective-permute-done | bytes 90144 | tf_op jit(solution)/shard_map/ppermute | solution.py:307
  45.9 1.5 %collective-permute-done.13.rest_1_ = bf16[32,1408]{1,0:T(8,128)(2,1)S(1)} collective-permute-done((bf16[32,1408]{1,0:T(8,128)(2,1)S(1)}, bf16[32,1408]{1,0:T(8,128)(2,1)S(1)}, u32[]{:S(2)}, u32[]{:S(2)}) %collective-permute-start.13) | collective-permute-done | bytes 90144 | tf_op jit(solution)/shard_map/ppermute | solution.py:307
  47.4 2.7 %experts.2 = (bf16[32,1344]{1,0:T(8,128)(2,1)S(1)}, bf16[32,1344]{1,0:T(8,128)(2,1)S(1)}, bf16[32,1344]{1,0:T(8,128)(2,1)S(1)}, bf16[32,1344]{1,0:T(8,128)(2,1)S(1)}) custom-call(bf16[1,928,1344]{2,1,0:T(8,128)(2,1)S(1)} %get-tuple-element.65.after_ref.up_ref, bf16[1,928,1344]{2,1,0:T(8,128)(2,1)S(1)} %get-tuple-element.72.down_ref, ...), custom_call_target="tpu_custom_call" | custom-call | tf_op jit(solution)/shard_map/experts/pallas_call | solution.py:29
  50.1 2.7 %collective-permute-start.16 = (bf16[32,1344]{1,0:T(8,128)(2,1)S(1)}, bf16[32,1344]{1,0:T(8,128)(2,1)S(1)}, u32[]{:S(2)}, u32[]{:S(2)}) collective-permute-start(bf16[32,1344]{1,0:T(8,128)(2,1)S(1)} %get-tuple-element.86), channel_id=1, source_target_pairs={{0,12},{4,8},{8,4},{12,0},{1,13},{5,9},{9,5},{13,1},{2,14},{6,10},... | collective-permute-start | bytes 258056 | tf_op jit(solution)/shard_map/ppermute | solution.py:307
  52.7 2.7 %experts.3 = (bf16[32,1344]{1,0:T(8,128)(2,1)S(1)}, bf16[32,1344]{1,0:T(8,128)(2,1)S(1)}, bf16[32,1344]{1,0:T(8,128)(2,1)S(1)}, bf16[32,1344]{1,0:T(8,128)(2,1)S(1)}) custom-call(bf16[1,928,1344]{2,1,0:T(8,128)(2,1)S(1)} %get-tuple-element.65.after_ref.up_ref, bf16[1,928,1344]{2,1,0:T(8,128)(2,1)S(1)} %get-tuple-element.72.down_ref, ...), custom_call_target="tpu_custom_call" | custom-call | tf_op jit(solution)/shard_map/experts/pallas_call | solution.py:29
  55.4 1.0 %collective-permute-start.18 = (bf16[32,1344]{1,0:T(8,128)(2,1)S(1)}, bf16[32,1344]{1,0:T(8,128)(2,1)S(1)}, u32[]{:S(2)}, u32[]{:S(2)}) collective-permute-start(bf16[32,1344]{1,0:T(8,128)(2,1)S(1)} %get-tuple-element.92), channel_id=1, source_target_pairs={{0,2},{1,3},{2,0},{3,1},{4,6},{5,7},{6,4},{7,5},{8,10},{9,11},{10,... | collective-permute-start | bytes 258056 | tf_op jit(solution)/shard_map/ppermute | solution.py:307
  56.5 1.7 %collective-permute-start.19 = (bf16[32,1344]{1,0:T(8,128)(2,1)S(1)}, bf16[32,1344]{1,0:T(8,128)(2,1)S(1)}, u32[]{:S(2)}, u32[]{:S(2)}) collective-permute-start(bf16[32,1344]{1,0:T(8,128)(2,1)S(1)} %get-tuple-element.95), channel_id=1, source_target_pairs={{0,14},{1,15},{2,12},{3,13},{4,10},{5,11},{6,8},{7,9},{8,6},{9,7},... | collective-permute-start | bytes 258056 | tf_op jit(solution)/shard_map/ppermute | solution.py:307
  58.2 0.5 collective-permute-done.17.rest_2_
  58.7 2.0 %collective-permute-done.18.refs_1_ = bf16[32,1344]{1,0:T(8,128)(2,1)S(1)} collective-permute-done((bf16[32,1344]{1,0:T(8,128)(2,1)S(1)}, bf16[32,1344]{1,0:T(8,128)(2,1)S(1)}, u32[]{:S(2)}, u32[]{:S(2)}) %collective-permute-start.18) | collective-permute-done | bytes 86048 | tf_op jit(solution)/shard_map/ppermute | solution.py:307
  60.8 2.9 %collective-permute-start.20 = (bf16[32,1344]{1,0:T(8,128)(2,1)S(1)}, bf16[32,1344]{1,0:T(8,128)(2,1)S(1)}, u32[]{:S(2)}, u32[]{:S(2)}) collective-permute-start(bf16[32,1344]{1,0:T(8,128)(2,1)S(1)} %sum.1), channel_id=1, source_target_pairs={{0,8},{4,12},{8,0},{12,4},{1,9},{5,13},{9,1},{13,5},{2,10},{6,14},... | collective-permute-start | bytes 258056 | tf_op jit(solution)/shard_map/ppermute | solution.py:307
  63.7 0.9 %collective-permute-start.21 = (bf16[32,1344]{1,0:T(8,128)(2,1)S(1)}, bf16[32,1344]{1,0:T(8,128)(2,1)S(1)}, u32[]{:S(2)}, u32[]{:S(2)}) collective-permute-start(bf16[32,1344]{1,0:T(8,128)(2,1)S(1)} %get-tuple-element.101), channel_id=1, source_target_pairs={{0,2},{1,3},{2,0},{3,1},{4,6},{5,7},{6,4},{7,5},{8,10},{9,11},{10,... | collective-permute-start | bytes 258056 | tf_op jit(solution)/shard_map/ppermute | solution.py:307
  64.6 0.1 collective-permute-start.22
  64.7 1.6 %collective-permute-done.20.rest_4_ = bf16[32,1344]{1,0:T(8,128)(2,1)S(1)} collective-permute-done((bf16[32,1344]{1,0:T(8,128)(2,1)S(1)}, bf16[32,1344]{1,0:T(8,128)(2,1)S(1)}, u32[]{:S(2)}, u32[]{:S(2)}) %collective-permute-start.20) | collective-permute-done | bytes 86048 | tf_op jit(solution)/shard_map/ppermute | solution.py:307
  66.3 2.0 %collective-permute-done.21.rest_5_ = bf16[32,1344]{1,0:T(8,128)(2,1)S(1)} collective-permute-done((bf16[32,1344]{1,0:T(8,128)(2,1)S(1)}, bf16[32,1344]{1,0:T(8,128)(2,1)S(1)}, u32[]{:S(2)}, u32[]{:S(2)}) %collective-permute-start.21) | collective-permute-done | bytes 86048 | tf_op jit(solution)/shard_map/ppermute | solution.py:307
  68.2 1.8 %collective-permute-done.22.rest_6_ = bf16[32,1344]{1,0:T(8,128)(2,1)S(1)} collective-permute-done((bf16[32,1344]{1,0:T(8,128)(2,1)S(1)}, bf16[32,1344]{1,0:T(8,128)(2,1)S(1)}, u32[]{:S(2)}, u32[]{:S(2)}) %collective-permute-start.22) | collective-permute-done | bytes 86048 | tf_op jit(solution)/shard_map/ppermute | solution.py:307
  70.0 0.7 %last.1 = bf16[1,32,1344]{2,1,0:T(8,128)(2,1)} custom-call(bf16[32,1344]{1,0:T(8,128)(2,1)S(1)} %get-tuple-element.71.hidden_ref, bf16[32,1344]{1,0:T(8,128)(2,1)S(1)} %get-tuple-element.85.rest_0_, bf16[32,1344]{1,0:T(8,128)(2,1)S(1)} %collective-permute-done.16.rest_1_, bf16[32,1344]{1,0:T(8,128)(2,1)S(1)} %collective-permute-done.17.rest_2_, ...), custom_call_target="tpu_custom_call" | custom-call | tf_op jit(solution)/shard_map/last/pallas_call | solution.py:29
  (12 shorter events, 0.1 us)
Async XLA Ops:
  0.0 19.8 %collective-permute-start = (bf16[1,928,1344]{2,1,0:T(8,128)(2,1)}, bf16[1,928,1344]{2,1,0:T(8,128)(2,1)S(1)}, u32[]{:S(2)}, u32[]{:S(2)}) collective-permute-start(bf16[1,928,1344]{2,1,0:T(8,128)(2,1)} %bitcast.9), channel_id=1, source_target_pairs={{0,1},{1,0},{2,3},{3,2},{4,5},{5,4},{6,7},{7,6},{8,9},{9,8},{10,11... | collective-permute-start | bytes 7483400 | tf_op jit(solution)/shard_map/ppermute | solution.py:307
  0.5 19.4 %collective-permute-start.1 = (bf16[1,928,1344]{2,1,0:T(8,128)(2,1)}, bf16[1,928,1344]{2,1,0:T(8,128)(2,1)S(1)}, u32[]{:S(2)}, u32[]{:S(2)}) collective-permute-start(bf16[1,928,1344]{2,1,0:T(8,128)(2,1)} %down_hbm.1), channel_id=1, source_target_pairs={{0,1},{1,0},{2,3},{3,2},{4,5},{5,4},{6,7},{7,6},{8,9},{9,8},{10,11... | collective-permute-start | bytes 7483400 | tf_op jit(solution)/shard_map/ppermute | solution.py:307
  2.3 3.1 %collective-permute-start.2 = (bf16[4,144,128]{2,1,0:T(8,128)(2,1)S(1)}, bf16[4,144,128]{2,1,0:T(8,128)(2,1)S(1)}, u32[]{:S(2)}, u32[]{:S(2)}) collective-permute-start(bf16[4,144,128]{2,1,0:T(8,128)(2,1)S(1)} %get-tuple-element.61), channel_id=1, source_target_pairs={{0,1},{1,0},{2,3},{3,2},{4,5},{5,4},{6,7},{7,6},{8,9},{9,8},{10,11... | collective-permute-start | bytes 442376 | tf_op jit(solution)/shard_map/ppermute | solution.py:307
  5.5 7.1 %collective-permute-start.3 = (bf16[4,144,128]{2,1,0:T(8,128)(2,1)S(1)}, bf16[4,144,128]{2,1,0:T(8,128)(2,1)S(1)}, u32[]{:S(2)}, u32[]{:S(2)}) collective-permute-start(bf16[4,144,128]{2,1,0:T(8,128)(2,1)S(1)} %chip_state.1.rest_0_), channel_id=1, source_target_pairs={{0,2},{1,3},{2,0},{3,1},{4,6},{5,7},{6,4},{7,5},{8,10},{9,11},{10,... | collective-permute-start | bytes 442376 | tf_op jit(solution)/shard_map/ppermute | solution.py:307
  12.7 5.4 %collective-permute-start.4 = (bf16[4,144,128]{2,1,0:T(8,128)(2,1)S(1)}, bf16[4,144,128]{2,1,0:T(8,128)(2,1)S(1)}, u32[]{:S(2)}, u32[]{:S(2)}) collective-permute-start(bf16[4,144,128]{2,1,0:T(8,128)(2,1)S(1)} %span.1.rest_2_), channel_id=1, source_target_pairs={{0,16},{16,0},{1,17},{17,1},{2,18},{18,2},{3,19},{19,3},{4,20},{20... | collective-permute-start | bytes 442376 | tf_op jit(solution)/shard_map/ppermute | solution.py:307
  18.4 1.4 %collective-permute-start.5 = (bf16[4,128,128]{2,1,0:T(8,128)(2,1)S(1)}, bf16[4,128,128]{2,1,0:T(8,128)(2,1)S(1)}, u32[]{:S(2)}, u32[]{:S(2)}) collective-permute-start(bf16[4,128,128]{2,1,0:T(8,128)(2,1)S(1)} %get-tuple-element.63), channel_id=1, source_target_pairs={{0,1},{1,0},{2,3},{3,2},{4,5},{5,4},{6,7},{7,6},{8,9},{9,8},{10,11... | collective-permute-start | bytes 393224 | tf_op jit(solution)/shard_map/ppermute | solution.py:307
  21.2 7.3 %collective-permute-start.6 = (bf16[32,1344]{1,0:T(8,128)(2,1)S(1)}, bf16[32,1344]{1,0:T(8,128)(2,1)S(1)}, u32[]{:S(2)}, u32[]{:S(2)}) collective-permute-start(bf16[32,1344]{1,0:T(8,128)(2,1)S(1)} %get-tuple-element.68), channel_id=1, source_target_pairs={{0,12},{4,8},{8,4},{12,0},{1,13},{5,9},{9,5},{13,1},{2,14},{6,10},... | collective-permute-start | bytes 258056 | tf_op jit(solution)/shard_map/ppermute | solution.py:307
  24.8 7.9 %collective-permute-start.7 = (bf16[32,1344]{1,0:T(8,128)(2,1)S(1)}, bf16[32,1344]{1,0:T(8,128)(2,1)S(1)}, u32[]{:S(2)}, u32[]{:S(2)}) collective-permute-start(bf16[32,1344]{1,0:T(8,128)(2,1)S(1)} %get-tuple-element.69), channel_id=1, source_target_pairs={{0,8},{4,12},{8,0},{12,4},{1,9},{5,13},{9,1},{13,5},{2,10},{6,14},... | collective-permute-start | bytes 258056 | tf_op jit(solution)/shard_map/ppermute | solution.py:307
  24.8 7.9 %collective-permute-start.8 = (bf16[32,1344]{1,0:T(8,128)(2,1)S(1)}, bf16[32,1344]{1,0:T(8,128)(2,1)S(1)}, u32[]{:S(2)}, u32[]{:S(2)}) collective-permute-start(bf16[32,1344]{1,0:T(8,128)(2,1)S(1)} %get-tuple-element.70), channel_id=1, source_target_pairs={{0,4},{4,0},{8,12},{12,8},{1,5},{5,1},{9,13},{13,9},{2,6},{6,2},{1... | collective-permute-start | bytes 258056 | tf_op jit(solution)/shard_map/ppermute | solution.py:307
  32.9 8.5 %collective-permute-start.10 = (bf16[32,1408]{1,0:T(8,128)(2,1)S(1)}, bf16[32,1408]{1,0:T(8,128)(2,1)S(1)}, u32[]{:S(2)}, u32[]{:S(2)}) collective-permute-start(bf16[32,1408]{1,0:T(8,128)(2,1)S(1)} %get-tuple-element.74.rest_0_), channel_id=1, source_target_pairs={{0,8},{4,12},{8,0},{12,4},{1,9},{5,13},{9,1},{13,5},{2,10},{6,14},... | collective-permute-start | bytes 270344 | tf_op jit(solution)/shard_map/ppermute | solution.py:307
  33.4 9.4 %collective-permute-start.9 = (bf16[32,1408]{1,0:T(8,128)(2,1)S(1)}, bf16[32,1408]{1,0:T(8,128)(2,1)S(1)}, u32[]{:S(2)}, u32[]{:S(2)}) collective-permute-start(bf16[32,1408]{1,0:T(8,128)(2,1)S(1)} %get-tuple-element.74.rest_0_), channel_id=1, source_target_pairs={{0,4},{4,0},{8,12},{12,8},{1,5},{5,1},{9,13},{13,9},{2,6},{6,2},{1... | collective-permute-start | bytes 270344 | tf_op jit(solution)/shard_map/ppermute | solution.py:307
  36.0 7.4 %collective-permute-start.11 = (bf16[32,1408]{1,0:T(8,128)(2,1)S(1)}, bf16[32,1408]{1,0:T(8,128)(2,1)S(1)}, u32[]{:S(2)}, u32[]{:S(2)}) collective-permute-start(bf16[32,1408]{1,0:T(8,128)(2,1)S(1)} %get-tuple-element.74.rest_0_), channel_id=1, source_target_pairs={{0,12},{4,8},{8,4},{12,0},{1,13},{5,9},{9,5},{13,1},{2,14},{6,10},... | collective-permute-start | bytes 270344 | tf_op jit(solution)/shard_map/ppermute | solution.py:307
  37.3 7.6 %collective-permute-start.12 = (bf16[32,1408]{1,0:T(8,128)(2,1)S(1)}, bf16[32,1408]{1,0:T(8,128)(2,1)S(1)}, u32[]{:S(2)}, u32[]{:S(2)}) collective-permute-start(bf16[32,1408]{1,0:T(8,128)(2,1)S(1)} %get-tuple-element.74.rest_0_), channel_id=1, source_target_pairs={{0,2},{1,3},{2,0},{3,1},{4,6},{5,7},{6,4},{7,5},{8,10},{9,11},{10,... | collective-permute-start | bytes 270344 | tf_op jit(solution)/shard_map/ppermute | solution.py:307
  41.3 4.5 %collective-permute-start.14 = (bf16[32,1408]{1,0:T(8,128)(2,1)S(1)}, bf16[32,1408]{1,0:T(8,128)(2,1)S(1)}, u32[]{:S(2)}, u32[]{:S(2)}) collective-permute-start(bf16[32,1408]{1,0:T(8,128)(2,1)S(1)} %collective-permute-done.10.rest_2_), channel_id=1, source_target_pairs={{0,2},{1,3},{2,0},{3,1},{4,6},{5,7},{6,4},{7,5},{8,10},{9,11},{10,... | collective-permute-start | bytes 270344 | tf_op jit(solution)/shard_map/ppermute | solution.py:307
  42.8 4.5 %collective-permute-start.13 = (bf16[32,1408]{1,0:T(8,128)(2,1)S(1)}, bf16[32,1408]{1,0:T(8,128)(2,1)S(1)}, u32[]{:S(2)}, u32[]{:S(2)}) collective-permute-start(bf16[32,1408]{1,0:T(8,128)(2,1)S(1)} %collective-permute-done.9.rest_1_), channel_id=1, source_target_pairs={{0,2},{1,3},{2,0},{3,1},{4,6},{5,7},{6,4},{7,5},{8,10},{9,11},{10,... | collective-permute-start | bytes 270344 | tf_op jit(solution)/shard_map/ppermute | solution.py:307
  43.4 6.7 %collective-permute-start.15 = (bf16[32,1408]{1,0:T(8,128)(2,1)S(1)}, bf16[32,1408]{1,0:T(8,128)(2,1)S(1)}, u32[]{:S(2)}, u32[]{:S(2)}) collective-permute-start(bf16[32,1408]{1,0:T(8,128)(2,1)S(1)} %collective-permute-done.11.rest_3_), channel_id=1, source_target_pairs={{0,2},{1,3},{2,0},{3,1},{4,6},{5,7},{6,4},{7,5},{8,10},{9,11},{10,... | collective-permute-start | bytes 270344 | tf_op jit(solution)/shard_map/ppermute | solution.py:307
  50.1 8.1 %collective-permute-start.16 = (bf16[32,1344]{1,0:T(8,128)(2,1)S(1)}, bf16[32,1344]{1,0:T(8,128)(2,1)S(1)}, u32[]{:S(2)}, u32[]{:S(2)}) collective-permute-start(bf16[32,1344]{1,0:T(8,128)(2,1)S(1)} %get-tuple-element.86), channel_id=1, source_target_pairs={{0,12},{4,8},{8,4},{12,0},{1,13},{5,9},{9,5},{13,1},{2,14},{6,10},... | collective-permute-start | bytes 258056 | tf_op jit(solution)/shard_map/ppermute | solution.py:307
  52.7 6.0 %collective-permute-start.17 = (bf16[32,1344]{1,0:T(8,128)(2,1)S(1)}, bf16[32,1344]{1,0:T(8,128)(2,1)S(1)}, u32[]{:S(2)}, u32[]{:S(2)}) collective-permute-start(bf16[32,1344]{1,0:T(8,128)(2,1)S(1)} %get-tuple-element.87), channel_id=1, source_target_pairs={{0,4},{4,0},{8,12},{12,8},{1,5},{5,1},{9,13},{13,9},{2,6},{6,2},{1... | collective-permute-start | bytes 258056 | tf_op jit(solution)/shard_map/ppermute | solution.py:307
  55.4 5.3 %collective-permute-start.18 = (bf16[32,1344]{1,0:T(8,128)(2,1)S(1)}, bf16[32,1344]{1,0:T(8,128)(2,1)S(1)}, u32[]{:S(2)}, u32[]{:S(2)}) collective-permute-start(bf16[32,1344]{1,0:T(8,128)(2,1)S(1)} %get-tuple-element.92), channel_id=1, source_target_pairs={{0,2},{1,3},{2,0},{3,1},{4,6},{5,7},{6,4},{7,5},{8,10},{9,11},{10,... | collective-permute-start | bytes 258056 | tf_op jit(solution)/shard_map/ppermute | solution.py:307
  56.5 8.2 %collective-permute-start.19 = (bf16[32,1344]{1,0:T(8,128)(2,1)S(1)}, bf16[32,1344]{1,0:T(8,128)(2,1)S(1)}, u32[]{:S(2)}, u32[]{:S(2)}) collective-permute-start(bf16[32,1344]{1,0:T(8,128)(2,1)S(1)} %get-tuple-element.95), channel_id=1, source_target_pairs={{0,14},{1,15},{2,12},{3,13},{4,10},{5,11},{6,8},{7,9},{8,6},{9,7},... | collective-permute-start | bytes 258056 | tf_op jit(solution)/shard_map/ppermute | solution.py:307
  60.8 5.5 %collective-permute-start.20 = (bf16[32,1344]{1,0:T(8,128)(2,1)S(1)}, bf16[32,1344]{1,0:T(8,128)(2,1)S(1)}, u32[]{:S(2)}, u32[]{:S(2)}) collective-permute-start(bf16[32,1344]{1,0:T(8,128)(2,1)S(1)} %sum.1), channel_id=1, source_target_pairs={{0,8},{4,12},{8,0},{12,4},{1,9},{5,13},{9,1},{13,5},{2,10},{6,14},... | collective-permute-start | bytes 258056 | tf_op jit(solution)/shard_map/ppermute | solution.py:307
  63.7 4.5 %collective-permute-start.21 = (bf16[32,1344]{1,0:T(8,128)(2,1)S(1)}, bf16[32,1344]{1,0:T(8,128)(2,1)S(1)}, u32[]{:S(2)}, u32[]{:S(2)}) collective-permute-start(bf16[32,1344]{1,0:T(8,128)(2,1)S(1)} %get-tuple-element.101), channel_id=1, source_target_pairs={{0,2},{1,3},{2,0},{3,1},{4,6},{5,7},{6,4},{7,5},{8,10},{9,11},{10,... | collective-permute-start | bytes 258056 | tf_op jit(solution)/shard_map/ppermute | solution.py:307
  64.6 5.4 %collective-permute-start.22 = (bf16[32,1344]{1,0:T(8,128)(2,1)S(1)}, bf16[32,1344]{1,0:T(8,128)(2,1)S(1)}, u32[]{:S(2)}, u32[]{:S(2)}) collective-permute-start(bf16[32,1344]{1,0:T(8,128)(2,1)S(1)} %get-tuple-element.102), channel_id=1, source_target_pairs={{0,6},{1,7},{2,4},{3,5},{4,2},{5,3},{6,0},{7,1},{8,14},{9,15},{10,... | collective-permute-start | bytes 258056 | tf_op jit(solution)/shard_map/ppermute | solution.py:307

commit v6 on v5

--- a/solution.py
+++ b/solution.py
@@ -11,6 +11,7 @@
 STATE = 128
 LANES = 128
 TILE = 16
+OWN = -1
 FAR = -1e30
 F32 = jnp.float32
 BF16 = jnp.bfloat16
@@ -35,6 +36,16 @@
         name=name,
         compiler_params=pltpu.CompilerParams(vmem_limit_bytes=megabytes << 20),
     )(*args)
+
+
+def offsets(count):
+    down = list(range(count - 1, 0, -1))
+    return [down, down[-1:] + down[:-1]]
+
+
+def head_offset(slot, count):
+    first, second = (order[slot] for order in offsets(count))
+    return jnp.where(core_index() == 0, first, second)
 
 
 def core_index():
@@ -243,7 +254,7 @@
     rows = outs[0].shape[0]
     blocks = []
     for shift in range(len(outs)):
-        owner = lax.axis_index("head") ^ shift
+        owner = lax.axis_index("head") ^ (head_offset(shift - 1, len(outs)) if shift else 0)
         blocks.append(normed_ref[pl.ds(pl.multiple_of(owner * rows, rows), rows), :])
     product = lax.dot_general(jnp.concatenate(blocks, axis=0), w_ref[...], NT, preferred_element_type=F32)
     for shift, out in enumerate(outs):
@@ -307,6 +318,16 @@
     return lax.ppermute(value, axis, [(i, i ^ mask) for i in range(size)])
 
 
+def swap_slot(value, slot, chip_mask=0):
+    heads, size = lax.axis_size("head"), lax.axis_size("exp")
+    order = offsets(heads)
+    pairs = []
+    for i in range(heads * size):
+        head, exp = i // size, i % size
+        pairs.append((i, (head ^ order[exp % 2][slot]) * size + (exp ^ (2 * chip_mask))))
+    return lax.ppermute(value, ("head", "exp"), pairs)
+
+
 def per_device(
     x_in, z_in, b_in, c_in, dt_in, a_log, d_skip, norm_w, w_out, resid, routes, gates, moe_gain, w_up, w_down
 ):
@@ -390,8 +411,8 @@
         [(ANY, mixed[0]), (HBM, up_turned), (HBM, w_down)],
         [dma((2,))],
     )
-    order = list(range(head_size - 1, 0, -1))
-    parts = [mixed[0]] + [swap(mixed[s], "head", s) for s in order]
+    slots = list(range(head_size - 1))
+    parts = [mixed[0]] + [swap_slot(mixed[k + 1], k) for k in slots]
     hidden, own_rows = call(
         rows_kernel,
         "rows",
@@ -409,38 +430,40 @@
         )
         return dict(zip(members, produced))
 
-    near = {0: own_rows} | {s: swap(own_rows, "head", s) for s in range(1, head_size)}
-    far = [{s: swap(near[s], "exp", 2 * d) for s in near} for d in range(1, chips)]
-    early = [{s: members[s] for s in members if s != head_size - 1} for members in far]
+    near = {k: swap_slot(own_rows, slots[-1 - k]) for k in slots} | {OWN: own_rows}
+    far = [{k: swap(near[k], "exp", 2 * d) for k in near} for d in range(1, chips)]
+    early = [{k: members[k] for k in (OWN,)} for members in far]
     near, early = lax.optimization_barrier((near, early))
-    far = [others | members for others, members in zip(far, early)]
+    far = [members | others for members, others in zip(far, early)]
     back_near = through_experts(near)
     back_near, far = lax.optimization_barrier((back_near, far))
     back_far = [through_experts(members) for members in far]
-    relayed, direct = [s for s in order if s % 2 == 0], [s for s in order if s % 2 == 1]
-    later = [0] + direct[1:]
-
-    def diagonal(s):
-        return [swap(members[s], ("head", "exp"), s * exp_size + 2 * d) for d, members in enumerate(back_far, 1)]
-
-    arrived = [swap(back_near[s], "head", s) for s in direct]
-    got = {s: [swap(members[s], "exp", 2 * d) for d, members in enumerate(back_far, 1)] for s in relayed}
+    relayed, direct = slots[1:2], slots[2:] + slots[0:1]
+
+    def diagonal(k):
+        return [swap_slot(members[k], slots[-1 - k], d) for d, members in enumerate(back_far, 1)]
+
+    def across(members, k):
+        return [swap(results[k], "exp", 2 * d) for d, results in enumerate(members, 1)]
+
+    arrived = [swap_slot(back_near[k], slots[-1 - k]) for k in direct]
+    got = {k: across(back_far, k) for k in relayed}
     arrived, got = lax.optimization_barrier((arrived, got))
-    arrived += [part for s in direct[:1] for part in diagonal(s)]
+    arrived += diagonal(direct[0])
     totals = {
-        s: call(sum_kernel, "sum", struct((rows, model), BF16), [(VMEM, v) for v in (back_near[s], *got[s])])
-        for s in relayed
+        k: call(sum_kernel, "sum", struct((rows, model), BF16), [(VMEM, v) for v in (back_near[k], *got[k])])
+        for k in relayed
     }
-    totals, rest = lax.optimization_barrier((totals, [{s: members[s] for s in later} for members in back_far]))
-    back_far = rest
-    arrived += [swap(totals[s], "head", s) for s in relayed]
-    for s in later:
-        arrived += diagonal(s)
+    totals, back_far = lax.optimization_barrier((totals, back_far))
+    arrived += [swap_slot(totals[k], slots[-1 - k]) for k in relayed]
+    for k in direct[1:]:
+        arrived += diagonal(k)
+    arrived += across(back_far, OWN)
     return call(
         last_kernel,
         "last",
         struct(resid.shape, BF16),
-        [(VMEM, value) for value in (hidden, back_near[0], *arrived)],
+        [(VMEM, value) for value in (hidden, back_near[OWN], *arrived)],
         pinned=False,
     )
 

time: 71.1 us -> 69.8 us (0.982)
  waiting for transfers between devices: 23.4 us -> 21.9 us
    ppermute x0 -> x11, starting transfers between devices: none -> 16.1 us  [swap_slot(): return lax.ppermute(value, ('head', 'exp'), pairs)]
    ppermute x23 -> x12, starting transfers between devices: 29.1 us -> 13.1 us  [swap(): return lax.ppermute(value, axis, [(i, i ^ mask) for i in range(size)])]
    ppermute x23 -> x12, waiting for transfers between devices: 23.4 us -> 9.4 us  [swap(): return lax.ppermute(value, axis, [(i, i ^ mask) for i in range(size)])]
    ppermute x0 -> x11, waiting for transfers between devices: none -> 12.5 us  [swap_slot(): return lax.ppermute(value, ('head', 'exp'), pairs)]
  transfers between devices with their start and end apart: 23 -> 23, of which waited for: 14 -> 13; matrix products, arithmetic and copies ran while one was open for 2% -> 2% of each run, Pallas kernels for 21% -> 21%
where the time goes in v6:
time: 69.8 us; the launch traced here: 69.4 us
  starting transfers between devices  29.2 us (42%)
  waiting for transfers between devices  21.9 us (31%)
  Pallas kernels  16.8 us (24%)
  local copies, waits for them, and re-layouts  1.29 us (2%)
    pallas_call x13, Pallas kernels, call(): pl.pallas_call(kernel, out_shape=jax.tree.map(lambda out: pltpu.VMEM(out....  16.8 us
    ppermute x11, starting transfers between devices, swap_slot(): return lax.ppermute(value, ('head', 'exp'), pairs)  16.1 us
    ppermute x12, starting transfers between devices, swap(): return lax.ppermute(value, axis, [(i, i ^ mask) for i in range(size)])  13.1 us
    ppermute x11, waiting for transfers between devices, swap_slot(): return lax.ppermute(value, ('head', 'exp'), pairs)  12.5 us
    ppermute x12, waiting for transfers between devices, swap(): return lax.ppermute(value, axis, [(i, i ^ mask) for i in range(size)])  9.4 us
  transfers between devices with their start and end apart: 23, of which 13 were waited for; matrix products, arithmetic and copies ran while one was open for 2% of the time, Pallas kernels for 21%

profile of v6, /device:TPU:0, one launch (start us, length us, event | category | flops | bytes accessed | tf_op | source)
XLA Modules:
  0.0 69.4 jit_solution(9267269278716467080)
XLA Ops:
  0.0 0.5 collective-permute-start
  0.5 0.1 collective-permute-start.1
  0.5 1.8 %state.1 = (bf16[4,144,128]{2,1,0:T(8,128)(2,1)S(1)}, bf16[4,144,128]{2,1,0:T(8,128)(2,1)S(1)}) custom-call(bf16[128,1024]{1,0:T(8,128)(2,1)} %x_hbm.3, bf16[128,256]{1,0:T(8,128)(2,1)} %b_hbm.3, f32[16,128]{1,0:T(8,128)} %bitcast.11, f32[1,16]{1,0:T(1,128)} %bitcast.16), custom_call_target="tpu_custom_call" | custom-call | tf_op jit(solution)/shard_map/state/pallas_call | solution.py:30
  2.3 0.5 collective-permute-start.2
  2.9 2.5 %collective-permute-done.2.got_ref = bf16[4,144,128]{2,1,0:T(8,128)(2,1)S(1)} collective-permute-done((bf16[4,144,128]{2,1,0:T(8,128)(2,1)S(1)}, bf16[4,144,128]{2,1,0:T(8,128)(2,1)S(1)}, u32[]{:S(2)}, u32[]{:S(2)}) %collective-permute-start.2) | collective-permute-done | bytes 147488 | tf_op jit(solution)/shard_map/ppermute | solution.py:318
  5.4 0.1 chip_state.1.rest_0_
  5.5 3.0 %collective-permute-start.3 = (bf16[4,144,128]{2,1,0:T(8,128)(2,1)S(1)}, bf16[4,144,128]{2,1,0:T(8,128)(2,1)S(1)}, u32[]{:S(2)}, u32[]{:S(2)}) collective-permute-start(bf16[4,144,128]{2,1,0:T(8,128)(2,1)S(1)} %chip_state.1.rest_0_), channel_id=1, source_target_pairs={{0,2},{1,3},{2,0},{3,1},{4,6},{5,7},{6,4},{7,5},{8,10},{9,11},{10,... | collective-permute-start | bytes 442376 | tf_op jit(solution)/shard_map/ppermute | solution.py:318
  8.4 2.4 %inside.1 = (f32[128,1024]{1,0:T(8,128)S(1)}, f32[128,1024]{1,0:T(8,128)S(1)}, bf16[128,256]{1,0:T(8,128)(2,1)S(1)}) custom-call(bf16[128,1024]{1,0:T(8,128)(2,1)} %x_hbm.3, bf16[128,1024]{1,0:T(8,128)(2,1)} %z_hbm.1, bf16[128,256]{1,0:T(8,128)(2,1)} %b_hbm.3, bf16[128,256]{1,0:T(8,128)(2,1)} %c_hbm.1, f32[16,128]{1,0:T(8,128)} %bitcast.12, ...), custom_call_target="tpu_custom_call" | custom-call | tf_op jit(solution)/shard_map/inside/pallas_call | solution.py:30
  10.9 1.7 %collective-permute-done.3.rest_1_ = bf16[4,144,128]{2,1,0:T(8,128)(2,1)S(1)} collective-permute-done((bf16[4,144,128]{2,1,0:T(8,128)(2,1)S(1)}, bf16[4,144,128]{2,1,0:T(8,128)(2,1)S(1)}, u32[]{:S(2)}, u32[]{:S(2)}) %collective-permute-start.3) | collective-permute-done | bytes 147488 | tf_op jit(solution)/shard_map/ppermute | solution.py:318
  12.6 0.1 span.1.rest_2_
  12.7 1.8 %collective-permute-start.4 = (bf16[4,144,128]{2,1,0:T(8,128)(2,1)S(1)}, bf16[4,144,128]{2,1,0:T(8,128)(2,1)S(1)}, u32[]{:S(2)}, u32[]{:S(2)}) collective-permute-start(bf16[4,144,128]{2,1,0:T(8,128)(2,1)S(1)} %span.1.rest_2_), channel_id=1, source_target_pairs={{0,16},{16,0},{1,17},{17,1},{2,18},{18,2},{3,19},{19,3},{4,20},{20... | collective-permute-start | bytes 442376 | tf_op jit(solution)/shard_map/ppermute | solution.py:318
  14.5 1.3 %broadcast_in_dim.14.gain_hbm = f32[1,1344]{1,0:T(1,128)} reshape(f32[1344]{0:T(1024)} %param.27) | data formatting | bytes 10752 | tf_op jit(solution)/shard_map/broadcast_in_dim | solution.py:373
  15.8 1.9 %prep.1 = (bf16[32,128]{1,0:T(8,128)(2,1)S(1)}, bf16[1,32,1344]{2,1,0:T(8,128)(2,1)S(1)}, f32[1,1344]{1,0:T(1,128)S(1)}, f32[1,1024]{1,0:T(1,128)S(1)}, bf16[1344,1024]{1,0:T(8,128)(2,1)S(1)}) custom-call(bf16[1,32,1344]{2,1,0:T(8,128)(2,1)} %resid_hbm.1, s32[6,1,32]{2,1,0:T(1,128)} %bitcast.14, f32[6,1,32]{2,1,0:T(1,128)} %bitcast.15, ...), custom_call_target="tpu_custom_call" | custom-call | tf_op jit(solution)/shard_map/prep/pallas_call | solution.py:30
  17.7 0.4 collective-permute-done.4.rest_3_
  18.1 0.3 before.1
  18.4 0.1 collective-permute-start.5
  18.5 1.3 %collective-permute-done.5.got_ref = bf16[4,128,128]{2,1,0:T(8,128)(2,1)S(1)} collective-permute-done((bf16[4,128,128]{2,1,0:T(8,128)(2,1)S(1)}, bf16[4,128,128]{2,1,0:T(8,128)(2,1)S(1)}, u32[]{:S(2)}, u32[]{:S(2)}) %collective-permute-start.5) | collective-permute-done | bytes 131104 | tf_op jit(solution)/shard_map/ppermute | solution.py:318
  19.8 0.0 collective-permute-done.after_up.other_up_ref
  19.8 1.3 %mixed.1 = (bf16[32,1344]{1,0:T(8,128)(2,1)S(1)}, bf16[32,1344]{1,0:T(8,128)(2,1)S(1)}, bf16[32,1344]{1,0:T(8,128)(2,1)S(1)}, bf16[32,1344]{1,0:T(8,128)(2,1)S(1)}) custom-call(bf16[1,928,1344]{2,1,0:T(8,128)(2,1)S(1)} %collective-permute-done.after_up.other_up_ref, bf16[1,928,1344]{2,1,0:T(8,128)(2,1)S(1)} %collective-permute-done.1.after_down.other_down_ref, ...), custom_call_target="tpu_custom_call" | custom-call | tf_op jit(solution)/shard_map/mixed/pallas_call | solution.py:30
  21.2 3.7 %collective-permute-start.6 = (bf16[32,1344]{1,0:T(8,128)(2,1)S(1)}, bf16[32,1344]{1,0:T(8,128)(2,1)S(1)}, u32[]{:S(2)}, u32[]{:S(2)}) collective-permute-start(bf16[32,1344]{1,0:T(8,128)(2,1)S(1)} %get-tuple-element.66), channel_id=1, source_target_pairs={{0,12},{1,5},{2,14},{3,7},{4,8},{5,1},{6,10},{7,3},{8,4},{9,13},{1... | collective-permute-start | bytes 258056 | tf_op jit(solution)/shard_map/ppermute | solution.py:328
  24.8 0.8 %collective-permute-start.8 = (bf16[32,1344]{1,0:T(8,128)(2,1)S(1)}, bf16[32,1344]{1,0:T(8,128)(2,1)S(1)}, u32[]{:S(2)}, u32[]{:S(2)}) collective-permute-start(bf16[32,1344]{1,0:T(8,128)(2,1)S(1)} %get-tuple-element.68), channel_id=1, source_target_pairs={{0,4},{1,9},{2,6},{3,11},{4,0},{5,13},{6,2},{7,15},{8,12},{9,1},{1... | collective-permute-start | bytes 258056 | tf_op jit(solution)/shard_map/ppermute | solution.py:328
  25.6 2.5 %weights.1 = (bf16[1,928,1344]{2,1,0:T(8,128)(2,1)S(1)}, bf16[1,928,1344]{2,1,0:T(8,128)(2,1)S(1)}) custom-call(bf16[32,1344]{1,0:T(8,128)(2,1)S(1)} %get-tuple-element.62.after_ref.rest_0_, bf16[1,928,1344]{2,1,0:T(8,128)(2,1)} %bitcast.10, bf16[1,928,1344]{2,1,0:T(8,128)(2,1)} %down_hbm.1), custom_call_target="tpu_custom_call" | custom-call | tf_op jit(solution)/shard_map/weights/pallas_call | solution.py:30
  28.2 0.4 collective-permute-done.6.rest_1_
  28.5 4.7 %collective-permute-done.7.rest_2_ = bf16[32,1344]{1,0:T(8,128)(2,1)S(1)} collective-permute-done((bf16[32,1344]{1,0:T(8,128)(2,1)S(1)}, bf16[32,1344]{1,0:T(8,128)(2,1)S(1)}, u32[]{:S(2)}, u32[]{:S(2)}) %collective-permute-start.7) | collective-permute-done | bytes 86048 | tf_op jit(solution)/shard_map/ppermute | solution.py:328
  33.2 0.0 collective-permute-done.8.rest_3_
  33.2 0.2 rows.1
  33.4 2.5 %collective-permute-start.11 = (bf16[32,1408]{1,0:T(8,128)(2,1)S(1)}, bf16[32,1408]{1,0:T(8,128)(2,1)S(1)}, u32[]{:S(2)}, u32[]{:S(2)}) collective-permute-start(bf16[32,1408]{1,0:T(8,128)(2,1)S(1)} %get-tuple-element.72.rest_0_), channel_id=1, source_target_pairs={{0,12},{1,5},{2,14},{3,7},{4,8},{5,1},{6,10},{7,3},{8,4},{9,13},{1... | collective-permute-start | bytes 270344 | tf_op jit(solution)/shard_map/ppermute | solution.py:328
  35.8 2.0 %collective-permute-start.9 = (bf16[32,1408]{1,0:T(8,128)(2,1)S(1)}, bf16[32,1408]{1,0:T(8,128)(2,1)S(1)}, u32[]{:S(2)}, u32[]{:S(2)}) collective-permute-start(bf16[32,1408]{1,0:T(8,128)(2,1)S(1)} %get-tuple-element.72.rest_0_), channel_id=1, source_target_pairs={{0,4},{1,9},{2,6},{3,11},{4,0},{5,13},{6,2},{7,15},{8,12},{9,1},{1... | collective-permute-start | bytes 270344 | tf_op jit(solution)/shard_map/ppermute | solution.py:328
  37.8 1.5 %collective-permute-start.12 = (bf16[32,1408]{1,0:T(8,128)(2,1)S(1)}, bf16[32,1408]{1,0:T(8,128)(2,1)S(1)}, u32[]{:S(2)}, u32[]{:S(2)}) collective-permute-start(bf16[32,1408]{1,0:T(8,128)(2,1)S(1)} %get-tuple-element.72.rest_0_), channel_id=1, source_target_pairs={{0,2},{1,3},{2,0},{3,1},{4,6},{5,7},{6,4},{7,5},{8,10},{9,11},{10,... | collective-permute-start | bytes 270344 | tf_op jit(solution)/shard_map/ppermute | solution.py:318
  39.4 1.2 %collective-permute-done.11.rest_3_ = bf16[32,1408]{1,0:T(8,128)(2,1)S(1)} collective-permute-done((bf16[32,1408]{1,0:T(8,128)(2,1)S(1)}, bf16[32,1408]{1,0:T(8,128)(2,1)S(1)}, u32[]{:S(2)}, u32[]{:S(2)}) %collective-permute-start.11) | collective-permute-done | bytes 90144 | tf_op jit(solution)/shard_map/ppermute | solution.py:328
  40.6 1.5 %collective-permute-start.15 = (bf16[32,1408]{1,0:T(8,128)(2,1)S(1)}, bf16[32,1408]{1,0:T(8,128)(2,1)S(1)}, u32[]{:S(2)}, u32[]{:S(2)}) collective-permute-start(bf16[32,1408]{1,0:T(8,128)(2,1)S(1)} %collective-permute-done.11.rest_3_), channel_id=1, source_target_pairs={{0,2},{1,3},{2,0},{3,1},{4,6},{5,7},{6,4},{7,5},{8,10},{9,11},{10,... | collective-permute-start | bytes 270344 | tf_op jit(solution)/shard_map/ppermute | solution.py:318
  42.1 1.9 %collective-permute-done.10.rest_2_ = bf16[32,1408]{1,0:T(8,128)(2,1)S(1)} collective-permute-done((bf16[32,1408]{1,0:T(8,128)(2,1)S(1)}, bf16[32,1408]{1,0:T(8,128)(2,1)S(1)}, u32[]{:S(2)}, u32[]{:S(2)}) %collective-permute-start.10) | collective-permute-done | bytes 90144 | tf_op jit(solution)/shard_map/ppermute | solution.py:328
  44.0 1.5 %collective-permute-start.14 = (bf16[32,1408]{1,0:T(8,128)(2,1)S(1)}, bf16[32,1408]{1,0:T(8,128)(2,1)S(1)}, u32[]{:S(2)}, u32[]{:S(2)}) collective-permute-start(bf16[32,1408]{1,0:T(8,128)(2,1)S(1)} %collective-permute-done.10.rest_2_), channel_id=1, source_target_pairs={{0,2},{1,3},{2,0},{3,1},{4,6},{5,7},{6,4},{7,5},{8,10},{9,11},{10,... | collective-permute-start | bytes 270344 | tf_op jit(solution)/shard_map/ppermute | solution.py:318
  45.5 0.5 collective-permute-start.13
  46.0 2.7 %experts.2 = (bf16[32,1344]{1,0:T(8,128)(2,1)S(1)}, bf16[32,1344]{1,0:T(8,128)(2,1)S(1)}, bf16[32,1344]{1,0:T(8,128)(2,1)S(1)}, bf16[32,1344]{1,0:T(8,128)(2,1)S(1)}) custom-call(bf16[1,928,1344]{2,1,0:T(8,128)(2,1)S(1)} %get-tuple-element.63.after_ref.up_ref, bf16[1,928,1344]{2,1,0:T(8,128)(2,1)S(1)} %get-tuple-element.70.down_ref, ...), custom_call_target="tpu_custom_call" | custom-call | tf_op jit(solution)/shard_map/experts/pallas_call | solution.py:30
  48.8 1.3 %collective-permute-done.13.rest_1_ = bf16[32,1408]{1,0:T(8,128)(2,1)S(1)} collective-permute-done((bf16[32,1408]{1,0:T(8,128)(2,1)S(1)}, bf16[32,1408]{1,0:T(8,128)(2,1)S(1)}, u32[]{:S(2)}, u32[]{:S(2)}) %collective-permute-start.13) | collective-permute-done | bytes 90144 | tf_op jit(solution)/shard_map/ppermute | solution.py:318
  50.1 2.5 %collective-permute-start.16 = (bf16[32,1344]{1,0:T(8,128)(2,1)S(1)}, bf16[32,1344]{1,0:T(8,128)(2,1)S(1)}, u32[]{:S(2)}, u32[]{:S(2)}) collective-permute-start(bf16[32,1344]{1,0:T(8,128)(2,1)S(1)} %get-tuple-element.82), channel_id=1, source_target_pairs={{0,12},{1,5},{2,14},{3,7},{4,8},{5,1},{6,10},{7,3},{8,4},{9,13},{1... | collective-permute-start | bytes 258056 | tf_op jit(solution)/shard_map/ppermute | solution.py:328
  52.5 2.7 %experts.3 = (bf16[32,1344]{1,0:T(8,128)(2,1)S(1)}, bf16[32,1344]{1,0:T(8,128)(2,1)S(1)}, bf16[32,1344]{1,0:T(8,128)(2,1)S(1)}, bf16[32,1344]{1,0:T(8,128)(2,1)S(1)}) custom-call(bf16[1,928,1344]{2,1,0:T(8,128)(2,1)S(1)} %get-tuple-element.63.after_ref.up_ref, bf16[1,928,1344]{2,1,0:T(8,128)(2,1)S(1)} %get-tuple-element.70.down_ref, ...), custom_call_target="tpu_custom_call" | custom-call | tf_op jit(solution)/shard_map/experts/pallas_call | solution.py:30
  55.2 1.1 %collective-permute-start.18 = (bf16[32,1344]{1,0:T(8,128)(2,1)S(1)}, bf16[32,1344]{1,0:T(8,128)(2,1)S(1)}, u32[]{:S(2)}, u32[]{:S(2)}) collective-permute-start(bf16[32,1344]{1,0:T(8,128)(2,1)S(1)} %get-tuple-element.88), channel_id=1, source_target_pairs={{0,2},{1,3},{2,0},{3,1},{4,6},{5,7},{6,4},{7,5},{8,10},{9,11},{10,... | collective-permute-start | bytes 258056 | tf_op jit(solution)/shard_map/ppermute | solution.py:318
  56.4 1.7 %collective-permute-start.19 = (bf16[32,1344]{1,0:T(8,128)(2,1)S(1)}, bf16[32,1344]{1,0:T(8,128)(2,1)S(1)}, u32[]{:S(2)}, u32[]{:S(2)}) collective-permute-start(bf16[32,1344]{1,0:T(8,128)(2,1)S(1)} %get-tuple-element.91), channel_id=1, source_target_pairs={{0,14},{1,7},{2,12},{3,5},{4,10},{5,3},{6,8},{7,1},{8,6},{9,15},{1... | collective-permute-start | bytes 258056 | tf_op jit(solution)/shard_map/ppermute | solution.py:328
  58.1 1.7 %collective-permute-done.18.refs_1_ = bf16[32,1344]{1,0:T(8,128)(2,1)S(1)} collective-permute-done((bf16[32,1344]{1,0:T(8,128)(2,1)S(1)}, bf16[32,1344]{1,0:T(8,128)(2,1)S(1)}, u32[]{:S(2)}, u32[]{:S(2)}) %collective-permute-start.18) | collective-permute-done | bytes 86048 | tf_op jit(solution)/shard_map/ppermute | solution.py:318
  59.9 2.0 %collective-permute-start.20 = (bf16[32,1344]{1,0:T(8,128)(2,1)S(1)}, bf16[32,1344]{1,0:T(8,128)(2,1)S(1)}, u32[]{:S(2)}, u32[]{:S(2)}) collective-permute-start(bf16[32,1344]{1,0:T(8,128)(2,1)S(1)} %sum.1), channel_id=1, source_target_pairs={{0,8},{1,13},{2,10},{3,15},{4,12},{5,9},{6,14},{7,11},{8,0},{9,5},... | collective-permute-start | bytes 258056 | tf_op jit(solution)/shard_map/ppermute | solution.py:328
  61.8 1.0 %collective-permute-start.21 = (bf16[32,1344]{1,0:T(8,128)(2,1)S(1)}, bf16[32,1344]{1,0:T(8,128)(2,1)S(1)}, u32[]{:S(2)}, u32[]{:S(2)}) collective-permute-start(bf16[32,1344]{1,0:T(8,128)(2,1)S(1)} %get-tuple-element.97), channel_id=1, source_target_pairs={{0,6},{1,11},{2,4},{3,9},{4,2},{5,15},{6,0},{7,13},{8,14},{9,3},{1... | collective-permute-start | bytes 258056 | tf_op jit(solution)/shard_map/ppermute | solution.py:328
  62.9 1.1 %collective-permute-start.22 = (bf16[32,1344]{1,0:T(8,128)(2,1)S(1)}, bf16[32,1344]{1,0:T(8,128)(2,1)S(1)}, u32[]{:S(2)}, u32[]{:S(2)}) collective-permute-start(bf16[32,1344]{1,0:T(8,128)(2,1)S(1)} %get-tuple-element.98), channel_id=1, source_target_pairs={{0,2},{1,3},{2,0},{3,1},{4,6},{5,7},{6,4},{7,5},{8,10},{9,11},{10,... | collective-permute-start | bytes 258056 | tf_op jit(solution)/shard_map/ppermute | solution.py:318
  63.9 0.7 %collective-permute-done.19.rest_3_ = bf16[32,1344]{1,0:T(8,128)(2,1)S(1)} collective-permute-done((bf16[32,1344]{1,0:T(8,128)(2,1)S(1)}, bf16[32,1344]{1,0:T(8,128)(2,1)S(1)}, u32[]{:S(2)}, u32[]{:S(2)}) %collective-permute-start.19) | collective-permute-done | bytes 86048 | tf_op jit(solution)/shard_map/ppermute | solution.py:328
  64.7 3.6 %collective-permute-done.20.rest_4_ = bf16[32,1344]{1,0:T(8,128)(2,1)S(1)} collective-permute-done((bf16[32,1344]{1,0:T(8,128)(2,1)S(1)}, bf16[32,1344]{1,0:T(8,128)(2,1)S(1)}, u32[]{:S(2)}, u32[]{:S(2)}) %collective-permute-start.20) | collective-permute-done | bytes 86048 | tf_op jit(solution)/shard_map/ppermute | solution.py:328
  68.3 0.4 collective-permute-done.22.rest_6_
  68.7 0.7 %last.1 = bf16[1,32,1344]{2,1,0:T(8,128)(2,1)} custom-call(bf16[32,1344]{1,0:T(8,128)(2,1)S(1)} %get-tuple-element.69.hidden_ref, bf16[32,1344]{1,0:T(8,128)(2,1)S(1)} %get-tuple-element.81.rest_0_, bf16[32,1344]{1,0:T(8,128)(2,1)S(1)} %collective-permute-done.16.rest_1_, bf16[32,1344]{1,0:T(8,128)(2,1)S(1)} %collective-permute-done.17.rest_2_, ...), custom_call_target="tpu_custom_call" | custom-call | tf_op jit(solution)/shard_map/last/pallas_call | solution.py:30
  (12 shorter events, 0.1 us)
Async XLA Ops:
  0.0 19.8 %collective-permute-start = (bf16[1,928,1344]{2,1,0:T(8,128)(2,1)}, bf16[1,928,1344]{2,1,0:T(8,128)(2,1)S(1)}, u32[]{:S(2)}, u32[]{:S(2)}) collective-permute-start(bf16[1,928,1344]{2,1,0:T(8,128)(2,1)} %bitcast.9), channel_id=1, source_target_pairs={{0,1},{1,0},{2,3},{3,2},{4,5},{5,4},{6,7},{7,6},{8,9},{9,8},{10,11... | collective-permute-start | bytes 7483400 | tf_op jit(solution)/shard_map/ppermute | solution.py:318
  0.5 19.4 %collective-permute-start.1 = (bf16[1,928,1344]{2,1,0:T(8,128)(2,1)}, bf16[1,928,1344]{2,1,0:T(8,128)(2,1)S(1)}, u32[]{:S(2)}, u32[]{:S(2)}) collective-permute-start(bf16[1,928,1344]{2,1,0:T(8,128)(2,1)} %down_hbm.1), channel_id=1, source_target_pairs={{0,1},{1,0},{2,3},{3,2},{4,5},{5,4},{6,7},{7,6},{8,9},{9,8},{10,11... | collective-permute-start | bytes 7483400 | tf_op jit(solution)/shard_map/ppermute | solution.py:318
  2.3 3.1 %collective-permute-start.2 = (bf16[4,144,128]{2,1,0:T(8,128)(2,1)S(1)}, bf16[4,144,128]{2,1,0:T(8,128)(2,1)S(1)}, u32[]{:S(2)}, u32[]{:S(2)}) collective-permute-start(bf16[4,144,128]{2,1,0:T(8,128)(2,1)S(1)} %get-tuple-element.59), channel_id=1, source_target_pairs={{0,1},{1,0},{2,3},{3,2},{4,5},{5,4},{6,7},{7,6},{8,9},{9,8},{10,11... | collective-permute-start | bytes 442376 | tf_op jit(solution)/shard_map/ppermute | solution.py:318
  5.5 7.1 %collective-permute-start.3 = (bf16[4,144,128]{2,1,0:T(8,128)(2,1)S(1)}, bf16[4,144,128]{2,1,0:T(8,128)(2,1)S(1)}, u32[]{:S(2)}, u32[]{:S(2)}) collective-permute-start(bf16[4,144,128]{2,1,0:T(8,128)(2,1)S(1)} %chip_state.1.rest_0_), channel_id=1, source_target_pairs={{0,2},{1,3},{2,0},{3,1},{4,6},{5,7},{6,4},{7,5},{8,10},{9,11},{10,... | collective-permute-start | bytes 442376 | tf_op jit(solution)/shard_map/ppermute | solution.py:318
  12.7 5.4 %collective-permute-start.4 = (bf16[4,144,128]{2,1,0:T(8,128)(2,1)S(1)}, bf16[4,144,128]{2,1,0:T(8,128)(2,1)S(1)}, u32[]{:S(2)}, u32[]{:S(2)}) collective-permute-start(bf16[4,144,128]{2,1,0:T(8,128)(2,1)S(1)} %span.1.rest_2_), channel_id=1, source_target_pairs={{0,16},{16,0},{1,17},{17,1},{2,18},{18,2},{3,19},{19,3},{4,20},{20... | collective-permute-start | bytes 442376 | tf_op jit(solution)/shard_map/ppermute | solution.py:318
  18.4 1.4 %collective-permute-start.5 = (bf16[4,128,128]{2,1,0:T(8,128)(2,1)S(1)}, bf16[4,128,128]{2,1,0:T(8,128)(2,1)S(1)}, u32[]{:S(2)}, u32[]{:S(2)}) collective-permute-start(bf16[4,128,128]{2,1,0:T(8,128)(2,1)S(1)} %get-tuple-element.61), channel_id=1, source_target_pairs={{0,1},{1,0},{2,3},{3,2},{4,5},{5,4},{6,7},{7,6},{8,9},{9,8},{10,11... | collective-permute-start | bytes 393224 | tf_op jit(solution)/shard_map/ppermute | solution.py:318
  21.2 7.4 %collective-permute-start.6 = (bf16[32,1344]{1,0:T(8,128)(2,1)S(1)}, bf16[32,1344]{1,0:T(8,128)(2,1)S(1)}, u32[]{:S(2)}, u32[]{:S(2)}) collective-permute-start(bf16[32,1344]{1,0:T(8,128)(2,1)S(1)} %get-tuple-element.66), channel_id=1, source_target_pairs={{0,12},{1,5},{2,14},{3,7},{4,8},{5,1},{6,10},{7,3},{8,4},{9,13},{1... | collective-permute-start | bytes 258056 | tf_op jit(solution)/shard_map/ppermute | solution.py:328
  24.8 8.4 %collective-permute-start.7 = (bf16[32,1344]{1,0:T(8,128)(2,1)S(1)}, bf16[32,1344]{1,0:T(8,128)(2,1)S(1)}, u32[]{:S(2)}, u32[]{:S(2)}) collective-permute-start(bf16[32,1344]{1,0:T(8,128)(2,1)S(1)} %get-tuple-element.67), channel_id=1, source_target_pairs={{0,8},{1,13},{2,10},{3,15},{4,12},{5,9},{6,14},{7,11},{8,0},{9,5},... | collective-permute-start | bytes 258056 | tf_op jit(solution)/shard_map/ppermute | solution.py:328
  24.8 8.4 %collective-permute-start.8 = (bf16[32,1344]{1,0:T(8,128)(2,1)S(1)}, bf16[32,1344]{1,0:T(8,128)(2,1)S(1)}, u32[]{:S(2)}, u32[]{:S(2)}) collective-permute-start(bf16[32,1344]{1,0:T(8,128)(2,1)S(1)} %get-tuple-element.68), channel_id=1, source_target_pairs={{0,4},{1,9},{2,6},{3,11},{4,0},{5,13},{6,2},{7,15},{8,12},{9,1},{1... | collective-permute-start | bytes 258056 | tf_op jit(solution)/shard_map/ppermute | solution.py:328
  33.4 7.2 %collective-permute-start.11 = (bf16[32,1408]{1,0:T(8,128)(2,1)S(1)}, bf16[32,1408]{1,0:T(8,128)(2,1)S(1)}, u32[]{:S(2)}, u32[]{:S(2)}) collective-permute-start(bf16[32,1408]{1,0:T(8,128)(2,1)S(1)} %get-tuple-element.72.rest_0_), channel_id=1, source_target_pairs={{0,12},{1,5},{2,14},{3,7},{4,8},{5,1},{6,10},{7,3},{8,4},{9,13},{1... | collective-permute-start | bytes 270344 | tf_op jit(solution)/shard_map/ppermute | solution.py:328
  35.8 8.2 %collective-permute-start.10 = (bf16[32,1408]{1,0:T(8,128)(2,1)S(1)}, bf16[32,1408]{1,0:T(8,128)(2,1)S(1)}, u32[]{:S(2)}, u32[]{:S(2)}) collective-permute-start(bf16[32,1408]{1,0:T(8,128)(2,1)S(1)} %get-tuple-element.72.rest_0_), channel_id=1, source_target_pairs={{0,8},{1,13},{2,10},{3,15},{4,12},{5,9},{6,14},{7,11},{8,0},{9,5},... | collective-permute-start | bytes 270344 | tf_op jit(solution)/shard_map/ppermute | solution.py:328
  35.8 9.7 %collective-permute-start.9 = (bf16[32,1408]{1,0:T(8,128)(2,1)S(1)}, bf16[32,1408]{1,0:T(8,128)(2,1)S(1)}, u32[]{:S(2)}, u32[]{:S(2)}) collective-permute-start(bf16[32,1408]{1,0:T(8,128)(2,1)S(1)} %get-tuple-element.72.rest_0_), channel_id=1, source_target_pairs={{0,4},{1,9},{2,6},{3,11},{4,0},{5,13},{6,2},{7,15},{8,12},{9,1},{1... | collective-permute-start | bytes 270344 | tf_op jit(solution)/shard_map/ppermute | solution.py:328
  37.8 8.2 %collective-permute-start.12 = (bf16[32,1408]{1,0:T(8,128)(2,1)S(1)}, bf16[32,1408]{1,0:T(8,128)(2,1)S(1)}, u32[]{:S(2)}, u32[]{:S(2)}) collective-permute-start(bf16[32,1408]{1,0:T(8,128)(2,1)S(1)} %get-tuple-element.72.rest_0_), channel_id=1, source_target_pairs={{0,2},{1,3},{2,0},{3,1},{4,6},{5,7},{6,4},{7,5},{8,10},{9,11},{10,... | collective-permute-start | bytes 270344 | tf_op jit(solution)/shard_map/ppermute | solution.py:318
  40.6 8.1 %collective-permute-start.15 = (bf16[32,1408]{1,0:T(8,128)(2,1)S(1)}, bf16[32,1408]{1,0:T(8,128)(2,1)S(1)}, u32[]{:S(2)}, u32[]{:S(2)}) collective-permute-start(bf16[32,1408]{1,0:T(8,128)(2,1)S(1)} %collective-permute-done.11.rest_3_), channel_id=1, source_target_pairs={{0,2},{1,3},{2,0},{3,1},{4,6},{5,7},{6,4},{7,5},{8,10},{9,11},{10,... | collective-permute-start | bytes 270344 | tf_op jit(solution)/shard_map/ppermute | solution.py:318
  44.0 4.7 %collective-permute-start.14 = (bf16[32,1408]{1,0:T(8,128)(2,1)S(1)}, bf16[32,1408]{1,0:T(8,128)(2,1)S(1)}, u32[]{:S(2)}, u32[]{:S(2)}) collective-permute-start(bf16[32,1408]{1,0:T(8,128)(2,1)S(1)} %collective-permute-done.10.rest_2_), channel_id=1, source_target_pairs={{0,2},{1,3},{2,0},{3,1},{4,6},{5,7},{6,4},{7,5},{8,10},{9,11},{10,... | collective-permute-start | bytes 270344 | tf_op jit(solution)/shard_map/ppermute | solution.py:318
  45.5 4.5 %collective-permute-start.13 = (bf16[32,1408]{1,0:T(8,128)(2,1)S(1)}, bf16[32,1408]{1,0:T(8,128)(2,1)S(1)}, u32[]{:S(2)}, u32[]{:S(2)}) collective-permute-start(bf16[32,1408]{1,0:T(8,128)(2,1)S(1)} %collective-permute-done.9.rest_1_), channel_id=1, source_target_pairs={{0,2},{1,3},{2,0},{3,1},{4,6},{5,7},{6,4},{7,5},{8,10},{9,11},{10,... | collective-permute-start | bytes 270344 | tf_op jit(solution)/shard_map/ppermute | solution.py:318
  50.1 8.1 %collective-permute-start.16 = (bf16[32,1344]{1,0:T(8,128)(2,1)S(1)}, bf16[32,1344]{1,0:T(8,128)(2,1)S(1)}, u32[]{:S(2)}, u32[]{:S(2)}) collective-permute-start(bf16[32,1344]{1,0:T(8,128)(2,1)S(1)} %get-tuple-element.82), channel_id=1, source_target_pairs={{0,12},{1,5},{2,14},{3,7},{4,8},{5,1},{6,10},{7,3},{8,4},{9,13},{1... | collective-permute-start | bytes 258056 | tf_op jit(solution)/shard_map/ppermute | solution.py:328
  52.5 5.6 %collective-permute-start.17 = (bf16[32,1344]{1,0:T(8,128)(2,1)S(1)}, bf16[32,1344]{1,0:T(8,128)(2,1)S(1)}, u32[]{:S(2)}, u32[]{:S(2)}) collective-permute-start(bf16[32,1344]{1,0:T(8,128)(2,1)S(1)} %get-tuple-element.83), channel_id=1, source_target_pairs={{0,4},{1,9},{2,6},{3,11},{4,0},{5,13},{6,2},{7,15},{8,12},{9,1},{1... | collective-permute-start | bytes 258056 | tf_op jit(solution)/shard_map/ppermute | solution.py:328
  55.2 4.6 %collective-permute-start.18 = (bf16[32,1344]{1,0:T(8,128)(2,1)S(1)}, bf16[32,1344]{1,0:T(8,128)(2,1)S(1)}, u32[]{:S(2)}, u32[]{:S(2)}) collective-permute-start(bf16[32,1344]{1,0:T(8,128)(2,1)S(1)} %get-tuple-element.88), channel_id=1, source_target_pairs={{0,2},{1,3},{2,0},{3,1},{4,6},{5,7},{6,4},{7,5},{8,10},{9,11},{10,... | collective-permute-start | bytes 258056 | tf_op jit(solution)/shard_map/ppermute | solution.py:318
  56.4 8.3 %collective-permute-start.19 = (bf16[32,1344]{1,0:T(8,128)(2,1)S(1)}, bf16[32,1344]{1,0:T(8,128)(2,1)S(1)}, u32[]{:S(2)}, u32[]{:S(2)}) collective-permute-start(bf16[32,1344]{1,0:T(8,128)(2,1)S(1)} %get-tuple-element.91), channel_id=1, source_target_pairs={{0,14},{1,7},{2,12},{3,5},{4,10},{5,3},{6,8},{7,1},{8,6},{9,15},{1... | collective-permute-start | bytes 258056 | tf_op jit(solution)/shard_map/ppermute | solution.py:328
  59.9 8.4 %collective-permute-start.20 = (bf16[32,1344]{1,0:T(8,128)(2,1)S(1)}, bf16[32,1344]{1,0:T(8,128)(2,1)S(1)}, u32[]{:S(2)}, u32[]{:S(2)}) collective-permute-start(bf16[32,1344]{1,0:T(8,128)(2,1)S(1)} %sum.1), channel_id=1, source_target_pairs={{0,8},{1,13},{2,10},{3,15},{4,12},{5,9},{6,14},{7,11},{8,0},{9,5},... | collective-permute-start | bytes 258056 | tf_op jit(solution)/shard_map/ppermute | solution.py:328
  61.8 6.5 %collective-permute-start.21 = (bf16[32,1344]{1,0:T(8,128)(2,1)S(1)}, bf16[32,1344]{1,0:T(8,128)(2,1)S(1)}, u32[]{:S(2)}, u32[]{:S(2)}) collective-permute-start(bf16[32,1344]{1,0:T(8,128)(2,1)S(1)} %get-tuple-element.97), channel_id=1, source_target_pairs={{0,6},{1,11},{2,4},{3,9},{4,2},{5,15},{6,0},{7,13},{8,14},{9,3},{1... | collective-permute-start | bytes 258056 | tf_op jit(solution)/shard_map/ppermute | solution.py:328
  62.9 5.8 %collective-permute-start.22 = (bf16[32,1344]{1,0:T(8,128)(2,1)S(1)}, bf16[32,1344]{1,0:T(8,128)(2,1)S(1)}, u32[]{:S(2)}, u32[]{:S(2)}) collective-permute-start(bf16[32,1344]{1,0:T(8,128)(2,1)S(1)} %get-tuple-element.98), channel_id=1, source_target_pairs={{0,2},{1,3},{2,0},{3,1},{4,6},{5,7},{6,4},{7,5},{8,10},{9,11},{10,... | collective-permute-start | bytes 258056 | tf_op jit(solution)/shard_map/ppermute | solution.py:318

commit v7 on v6

--- a/solution.py
+++ b/solution.py
@@ -11,7 +11,6 @@
 STATE = 128
 LANES = 128
 TILE = 16
-OWN = -1
 FAR = -1e30
 F32 = jnp.float32
 BF16 = jnp.bfloat16
@@ -275,8 +274,7 @@
     rows_ref[:, :width] = (value * scale * gain_ref[...]).astype(BF16)
 
 
-def expert_kernel(experts, up_ref, down_ref, other_up_ref, other_down_ref, *rest):
-    count = len(rest) // 2
+def expert_kernel(experts, count, up_ref, down_ref, other_up_ref, other_down_ref, *rest):
     ins, outs = rest[:count], rest[count:]
     width = up_ref.shape[2]
     start = width // LANES * LANES
@@ -293,9 +291,10 @@
         chosen = (lane == expert) | (lane == expert + experts)
         gate = jnp.sum(jnp.where(chosen, tail, 0.0), axis=1, keepdims=True)
         total = total + jnp.dot(activated, down_of[0], preferred_element_type=F32) * gate
-    size = outs[0].shape[0]
-    for at, out in enumerate(outs):
-        out[...] = total[at * size : (at + 1) * size].astype(BF16)
+    at = 0
+    for out in outs:
+        out[...] = total[at : at + out.shape[0]].astype(BF16)
+        at += out.shape[0]
 
 
 def sum_kernel(*refs):
@@ -420,50 +419,40 @@
         [(ANY, up_held)] + [(VMEM, value) for value in (resid_held, gate_lanes, gain_held, *parts)],
     )
 
-    def through_experts(members):
-        produced = call(
-            functools.partial(expert_kernel, experts),
+    def through_experts(members, sizes):
+        return call(
+            functools.partial(expert_kernel, experts, len(members)),
             "experts",
-            [struct((rows, model), BF16)] * len(members),
-            [(VMEM, value) for value in (up_held, down_held, other_up, other_down, *members.values())],
+            [struct((size * rows, model), BF16) for size in sizes],
+            [(VMEM, value) for value in (up_held, down_held, other_up, other_down, *members)],
             megabytes=16,
         )
-        return dict(zip(members, produced))
-
-    near = {k: swap_slot(own_rows, slots[-1 - k]) for k in slots} | {OWN: own_rows}
-    far = [{k: swap(near[k], "exp", 2 * d) for k in near} for d in range(1, chips)]
-    early = [{k: members[k] for k in (OWN,)} for members in far]
-    near, early = lax.optimization_barrier((near, early))
-    far = [members | others for members, others in zip(far, early)]
-    back_near = through_experts(near)
+
+    near = [swap_slot(own_rows, k) for k in slots]
+    far = [
+        [swap(near[k], "exp", 2 * d) for k in slots[:-1]]
+        + [swap_slot(own_rows, slots[-1], d), swap(own_rows, "exp", 2 * d)]
+        for d in range(1, chips)
+    ]
+    near, whole = lax.optimization_barrier((near + [own_rows], [members[-1] for members in far]))
+    far = [members[:-1] + [last] for members, last in zip(far, whole)]
+    back_near = through_experts(near, [1] * head_size)
     back_near, far = lax.optimization_barrier((back_near, far))
-    back_far = [through_experts(members) for members in far]
-    relayed, direct = slots[1:2], slots[2:] + slots[0:1]
-
-    def diagonal(k):
-        return [swap_slot(members[k], slots[-1 - k], d) for d, members in enumerate(back_far, 1)]
-
-    def across(members, k):
-        return [swap(results[k], "exp", 2 * d) for d, results in enumerate(members, 1)]
-
-    arrived = [swap_slot(back_near[k], slots[-1 - k]) for k in direct]
-    got = {k: across(back_far, k) for k in relayed}
-    arrived, got = lax.optimization_barrier((arrived, got))
-    arrived += diagonal(direct[0])
-    totals = {
-        k: call(sum_kernel, "sum", struct((rows, model), BF16), [(VMEM, v) for v in (back_near[k], *got[k])])
-        for k in relayed
-    }
-    totals, back_far = lax.optimization_barrier((totals, back_far))
-    arrived += [swap_slot(totals[k], slots[-1 - k]) for k in relayed]
-    for k in direct[1:]:
-        arrived += diagonal(k)
-    arrived += across(back_far, OWN)
+    back_far = [through_experts(members, [1] * head_size) for members in far]
+    totals = []
+    for k in slots:
+        got = [swap(pieces[k], "exp", 2 * d) for d, pieces in enumerate(back_far, 1)]
+        totals.append(
+            call(sum_kernel, "sum", struct((rows, model), BF16), [(VMEM, v) for v in (back_near[k], *got)])
+        )
+    totals[1], mine = lax.optimization_barrier((totals[1], [pieces[-1] for pieces in back_far]))
+    arrived = [swap_slot(total, k) for k, total in enumerate(totals)]
+    arrived += [swap(piece, "exp", 2 * d) for d, piece in enumerate(mine, 1)]
     return call(
         last_kernel,
         "last",
         struct(resid.shape, BF16),
-        [(VMEM, value) for value in (hidden, back_near[OWN], *arrived)],
+        [(VMEM, value) for value in (hidden, back_near[-1], *arrived)],
         pinned=False,
     )
 

time: 69.8 us -> 68.7 us (0.984)
  starting transfers between devices: 29.2 us -> 27.8 us
    ppermute x11 -> x10, starting transfers between devices: 16.1 us -> 13.2 us  [swap_slot(): return lax.ppermute(value, ('head', 'exp'), pairs)]
    ppermute x12 -> x13, starting transfers between devices: 13.1 us -> 14.6 us  [swap(): return lax.ppermute(value, axis, [(i, i ^ mask) for i in range(size)])]
    ppermute x12 -> x13, waiting for transfers between devices: 9.4 us -> 10.8 us  [swap(): return lax.ppermute(value, axis, [(i, i ^ mask) for i in range(size)])]
    ppermute x11 -> x10, waiting for transfers between devices: 12.5 us -> 11.6 us  [swap_slot(): return lax.ppermute(value, ('head', 'exp'), pairs)]
    pallas_call x13 -> x15, Pallas kernels: 16.8 us -> 16.9 us  [call(): pl.pallas_call(kernel, out_shape=jax.tree.map(lambda out: pltpu.VMEM(out....]
  transfers between devices with their start and end apart: 23 -> 23, of which waited for: 13 -> 13; matrix products, arithmetic and copies ran while one was open for 2% -> 2% of each run, Pallas kernels for 21% -> 18%
where the time goes in v7:
time: 68.7 us; the launch traced here: 68.4 us
  starting transfers between devices  27.8 us (40%)
  waiting for transfers between devices  22.3 us (32%)
  Pallas kernels  16.9 us (25%)
  local copies, waits for them, and re-layouts  1.29 us (2%)
    pallas_call x15, Pallas kernels, call(): pl.pallas_call(kernel, out_shape=jax.tree.map(lambda out: pltpu.VMEM(out....  16.9 us
    ppermute x13, starting transfers between devices, swap(): return lax.ppermute(value, axis, [(i, i ^ mask) for i in range(size)])  14.6 us
    ppermute x10, starting transfers between devices, swap_slot(): return lax.ppermute(value, ('head', 'exp'), pairs)  13.2 us
    ppermute x10, waiting for transfers between devices, swap_slot(): return lax.ppermute(value, ('head', 'exp'), pairs)  11.6 us
    ppermute x13, waiting for transfers between devices, swap(): return lax.ppermute(value, axis, [(i, i ^ mask) for i in range(size)])  10.8 us
  transfers between devices with their start and end apart: 23, of which 13 were waited for; matrix products, arithmetic and copies ran while one was open for 2% of the time, Pallas kernels for 18%

profile of v7, /device:TPU:0, one launch (start us, length us, event | category | flops | bytes accessed | tf_op | source)
XLA Modules:
  0.0 68.4 jit_solution(16922299699837952433)
XLA Ops:
  0.0 0.5 collective-permute-start
  0.5 0.1 collective-permute-start.1
  0.5 1.8 %state.1 = (bf16[4,144,128]{2,1,0:T(8,128)(2,1)S(1)}, bf16[4,144,128]{2,1,0:T(8,128)(2,1)S(1)}) custom-call(bf16[128,1024]{1,0:T(8,128)(2,1)} %x_hbm.3, bf16[128,256]{1,0:T(8,128)(2,1)} %b_hbm.3, f32[16,128]{1,0:T(8,128)} %bitcast.11, f32[1,16]{1,0:T(1,128)} %bitcast.16), custom_call_target="tpu_custom_call" | custom-call | tf_op jit(solution)/shard_map/state/pallas_call | solution.py:29
  2.3 0.5 collective-permute-start.2
  2.9 2.5 %collective-permute-done.2.got_ref = bf16[4,144,128]{2,1,0:T(8,128)(2,1)S(1)} collective-permute-done((bf16[4,144,128]{2,1,0:T(8,128)(2,1)S(1)}, bf16[4,144,128]{2,1,0:T(8,128)(2,1)S(1)}, u32[]{:S(2)}, u32[]{:S(2)}) %collective-permute-start.2) | collective-permute-done | bytes 147488 | tf_op jit(solution)/shard_map/ppermute | solution.py:317
  5.4 0.1 chip_state.1.rest_0_
  5.5 3.0 %collective-permute-start.3 = (bf16[4,144,128]{2,1,0:T(8,128)(2,1)S(1)}, bf16[4,144,128]{2,1,0:T(8,128)(2,1)S(1)}, u32[]{:S(2)}, u32[]{:S(2)}) collective-permute-start(bf16[4,144,128]{2,1,0:T(8,128)(2,1)S(1)} %chip_state.1.rest_0_), channel_id=1, source_target_pairs={{0,2},{1,3},{2,0},{3,1},{4,6},{5,7},{6,4},{7,5},{8,10},{9,11},{10,... | collective-permute-start | bytes 442376 | tf_op jit(solution)/shard_map/ppermute | solution.py:317
  8.4 2.4 %inside.1 = (f32[128,1024]{1,0:T(8,128)S(1)}, f32[128,1024]{1,0:T(8,128)S(1)}, bf16[128,256]{1,0:T(8,128)(2,1)S(1)}) custom-call(bf16[128,1024]{1,0:T(8,128)(2,1)} %x_hbm.3, bf16[128,1024]{1,0:T(8,128)(2,1)} %z_hbm.1, bf16[128,256]{1,0:T(8,128)(2,1)} %b_hbm.3, bf16[128,256]{1,0:T(8,128)(2,1)} %c_hbm.1, f32[16,128]{1,0:T(8,128)} %bitcast.12, ...), custom_call_target="tpu_custom_call" | custom-call | tf_op jit(solution)/shard_map/inside/pallas_call | solution.py:29
  10.9 1.7 %collective-permute-done.3.rest_1_ = bf16[4,144,128]{2,1,0:T(8,128)(2,1)S(1)} collective-permute-done((bf16[4,144,128]{2,1,0:T(8,128)(2,1)S(1)}, bf16[4,144,128]{2,1,0:T(8,128)(2,1)S(1)}, u32[]{:S(2)}, u32[]{:S(2)}) %collective-permute-start.3) | collective-permute-done | bytes 147488 | tf_op jit(solution)/shard_map/ppermute | solution.py:317
  12.6 0.1 span.1.rest_2_
  12.7 1.8 %collective-permute-start.4 = (bf16[4,144,128]{2,1,0:T(8,128)(2,1)S(1)}, bf16[4,144,128]{2,1,0:T(8,128)(2,1)S(1)}, u32[]{:S(2)}, u32[]{:S(2)}) collective-permute-start(bf16[4,144,128]{2,1,0:T(8,128)(2,1)S(1)} %span.1.rest_2_), channel_id=1, source_target_pairs={{0,16},{16,0},{1,17},{17,1},{2,18},{18,2},{3,19},{19,3},{4,20},{20... | collective-permute-start | bytes 442376 | tf_op jit(solution)/shard_map/ppermute | solution.py:317
  14.5 1.3 %broadcast_in_dim.14.gain_hbm = f32[1,1344]{1,0:T(1,128)} reshape(f32[1344]{0:T(1024)} %param.27) | data formatting | bytes 10752 | tf_op jit(solution)/shard_map/broadcast_in_dim | solution.py:372
  15.8 1.9 %prep.1 = (bf16[32,128]{1,0:T(8,128)(2,1)S(1)}, bf16[1,32,1344]{2,1,0:T(8,128)(2,1)S(1)}, f32[1,1344]{1,0:T(1,128)S(1)}, f32[1,1024]{1,0:T(1,128)S(1)}, bf16[1344,1024]{1,0:T(8,128)(2,1)S(1)}) custom-call(bf16[1,32,1344]{2,1,0:T(8,128)(2,1)} %resid_hbm.1, s32[6,1,32]{2,1,0:T(1,128)} %bitcast.14, f32[6,1,32]{2,1,0:T(1,128)} %bitcast.15, ...), custom_call_target="tpu_custom_call" | custom-call | tf_op jit(solution)/shard_map/prep/pallas_call | solution.py:29
  17.7 0.4 collective-permute-done.4.rest_3_
  18.1 0.3 before.1
  18.4 0.1 collective-permute-start.5
  18.5 1.3 %collective-permute-done.5.got_ref = bf16[4,128,128]{2,1,0:T(8,128)(2,1)S(1)} collective-permute-done((bf16[4,128,128]{2,1,0:T(8,128)(2,1)S(1)}, bf16[4,128,128]{2,1,0:T(8,128)(2,1)S(1)}, u32[]{:S(2)}, u32[]{:S(2)}) %collective-permute-start.5) | collective-permute-done | bytes 131104 | tf_op jit(solution)/shard_map/ppermute | solution.py:317
  19.8 1.3 %mixed.1 = (bf16[32,1344]{1,0:T(8,128)(2,1)S(1)}, bf16[32,1344]{1,0:T(8,128)(2,1)S(1)}, bf16[32,1344]{1,0:T(8,128)(2,1)S(1)}, bf16[32,1344]{1,0:T(8,128)(2,1)S(1)}) custom-call(bf16[1,928,1344]{2,1,0:T(8,128)(2,1)S(1)} %collective-permute-done.after_up.other_up_ref, bf16[1,928,1344]{2,1,0:T(8,128)(2,1)S(1)} %collective-permute-done.1.after_down.other_down_ref, ...), custom_call_target="tpu_custom_call" | custom-call | tf_op jit(solution)/shard_map/mixed/pallas_call | solution.py:29
  21.2 3.7 %collective-permute-start.6 = (bf16[32,1344]{1,0:T(8,128)(2,1)S(1)}, bf16[32,1344]{1,0:T(8,128)(2,1)S(1)}, u32[]{:S(2)}, u32[]{:S(2)}) collective-permute-start(bf16[32,1344]{1,0:T(8,128)(2,1)S(1)} %get-tuple-element.62), channel_id=1, source_target_pairs={{0,12},{1,5},{2,14},{3,7},{4,8},{5,1},{6,10},{7,3},{8,4},{9,13},{1... | collective-permute-start | bytes 258056 | tf_op jit(solution)/shard_map/ppermute | solution.py:327
  24.8 0.8 %collective-permute-start.8 = (bf16[32,1344]{1,0:T(8,128)(2,1)S(1)}, bf16[32,1344]{1,0:T(8,128)(2,1)S(1)}, u32[]{:S(2)}, u32[]{:S(2)}) collective-permute-start(bf16[32,1344]{1,0:T(8,128)(2,1)S(1)} %get-tuple-element.64), channel_id=1, source_target_pairs={{0,4},{1,9},{2,6},{3,11},{4,0},{5,13},{6,2},{7,15},{8,12},{9,1},{1... | collective-permute-start | bytes 258056 | tf_op jit(solution)/shard_map/ppermute | solution.py:327
  25.6 2.5 %weights.1 = (bf16[1,928,1344]{2,1,0:T(8,128)(2,1)S(1)}, bf16[1,928,1344]{2,1,0:T(8,128)(2,1)S(1)}) custom-call(bf16[32,1344]{1,0:T(8,128)(2,1)S(1)} %get-tuple-element.58.after_ref.rest_0_, bf16[1,928,1344]{2,1,0:T(8,128)(2,1)} %bitcast.10, bf16[1,928,1344]{2,1,0:T(8,128)(2,1)} %down_hbm.1), custom_call_target="tpu_custom_call" | custom-call | tf_op jit(solution)/shard_map/weights/pallas_call | solution.py:29
  28.2 0.4 collective-permute-done.6.rest_1_
  28.5 4.7 %collective-permute-done.7.rest_2_ = bf16[32,1344]{1,0:T(8,128)(2,1)S(1)} collective-permute-done((bf16[32,1344]{1,0:T(8,128)(2,1)S(1)}, bf16[32,1344]{1,0:T(8,128)(2,1)S(1)}, u32[]{:S(2)}, u32[]{:S(2)}) %collective-permute-start.7) | collective-permute-done | bytes 86048 | tf_op jit(solution)/shard_map/ppermute | solution.py:327
  33.2 0.2 rows.1
  33.4 0.1 collective-permute-start.10
  33.5 2.5 %collective-permute-start.9 = (bf16[32,1408]{1,0:T(8,128)(2,1)S(1)}, bf16[32,1408]{1,0:T(8,128)(2,1)S(1)}, u32[]{:S(2)}, u32[]{:S(2)}) collective-permute-start(bf16[32,1408]{1,0:T(8,128)(2,1)S(1)} %get-tuple-element.71.rest_3_), channel_id=1, source_target_pairs={{0,12},{1,5},{2,14},{3,7},{4,8},{5,1},{6,10},{7,3},{8,4},{9,13},{1... | collective-permute-start | bytes 270344 | tf_op jit(solution)/shard_map/ppermute | solution.py:327
  35.9 1.5 %collective-permute-start.12 = (bf16[32,1408]{1,0:T(8,128)(2,1)S(1)}, bf16[32,1408]{1,0:T(8,128)(2,1)S(1)}, u32[]{:S(2)}, u32[]{:S(2)}) collective-permute-start(bf16[32,1408]{1,0:T(8,128)(2,1)S(1)} %get-tuple-element.71.rest_3_), channel_id=1, source_target_pairs={{0,2},{1,3},{2,0},{3,1},{4,6},{5,7},{6,4},{7,5},{8,10},{9,11},{10,... | collective-permute-start | bytes 270344 | tf_op jit(solution)/shard_map/ppermute | solution.py:317
  37.4 1.0 %collective-permute-start.11 = (bf16[32,1408]{1,0:T(8,128)(2,1)S(1)}, bf16[32,1408]{1,0:T(8,128)(2,1)S(1)}, u32[]{:S(2)}, u32[]{:S(2)}) collective-permute-start(bf16[32,1408]{1,0:T(8,128)(2,1)S(1)} %get-tuple-element.71.rest_3_), channel_id=1, source_target_pairs={{0,4},{1,9},{2,6},{3,11},{4,0},{5,13},{6,2},{7,15},{8,12},{9,1},{1... | collective-permute-start | bytes 270344 | tf_op jit(solution)/shard_map/ppermute | solution.py:327
  38.5 0.9 %collective-permute-start.15 = (bf16[32,1408]{1,0:T(8,128)(2,1)S(1)}, bf16[32,1408]{1,0:T(8,128)(2,1)S(1)}, u32[]{:S(2)}, u32[]{:S(2)}) collective-permute-start(bf16[32,1408]{1,0:T(8,128)(2,1)S(1)} %get-tuple-element.71.rest_3_), channel_id=1, source_target_pairs={{0,6},{1,11},{2,4},{3,9},{4,2},{5,15},{6,0},{7,13},{8,14},{9,3},{1... | collective-permute-start | bytes 270344 | tf_op jit(solution)/shard_map/ppermute | solution.py:327
  39.4 2.4 %collective-permute-done.10.rest_1_ = bf16[32,1408]{1,0:T(8,128)(2,1)S(1)} collective-permute-done((bf16[32,1408]{1,0:T(8,128)(2,1)S(1)}, bf16[32,1408]{1,0:T(8,128)(2,1)S(1)}, u32[]{:S(2)}, u32[]{:S(2)}) %collective-permute-start.10) | collective-permute-done | bytes 90144 | tf_op jit(solution)/shard_map/ppermute | solution.py:327
  41.8 2.8 %collective-permute-start.14 = (bf16[32,1408]{1,0:T(8,128)(2,1)S(1)}, bf16[32,1408]{1,0:T(8,128)(2,1)S(1)}, u32[]{:S(2)}, u32[]{:S(2)}) collective-permute-start(bf16[32,1408]{1,0:T(8,128)(2,1)S(1)} %collective-permute-done.10.rest_1_), channel_id=1, source_target_pairs={{0,2},{1,3},{2,0},{3,1},{4,6},{5,7},{6,4},{7,5},{8,10},{9,11},{10,... | collective-permute-start | bytes 270344 | tf_op jit(solution)/shard_map/ppermute | solution.py:317
  44.6 0.0 collective-permute-start.13
  44.6 2.7 %experts.2 = (bf16[32,1344]{1,0:T(8,128)(2,1)S(1)}, bf16[32,1344]{1,0:T(8,128)(2,1)S(1)}, bf16[32,1344]{1,0:T(8,128)(2,1)S(1)}, bf16[32,1344]{1,0:T(8,128)(2,1)S(1)}) custom-call(bf16[1,928,1344]{2,1,0:T(8,128)(2,1)S(1)} %get-tuple-element.59.after_ref.up_ref, bf16[1,928,1344]{2,1,0:T(8,128)(2,1)S(1)} %get-tuple-element.66.down_ref, ...), custom_call_target="tpu_custom_call" | custom-call | tf_op jit(solution)/shard_map/experts/pallas_call | solution.py:29
  47.4 1.4 %collective-permute-done.14.rest_1_ = bf16[32,1408]{1,0:T(8,128)(2,1)S(1)} collective-permute-done((bf16[32,1408]{1,0:T(8,128)(2,1)S(1)}, bf16[32,1408]{1,0:T(8,128)(2,1)S(1)}, u32[]{:S(2)}, u32[]{:S(2)}) %collective-permute-start.14) | collective-permute-done | bytes 90144 | tf_op jit(solution)/shard_map/ppermute | solution.py:317
  48.7 1.0 %collective-permute-done.13.rest_0_ = bf16[32,1408]{1,0:T(8,128)(2,1)S(1)} collective-permute-done((bf16[32,1408]{1,0:T(8,128)(2,1)S(1)}, bf16[32,1408]{1,0:T(8,128)(2,1)S(1)}, u32[]{:S(2)}, u32[]{:S(2)}) %collective-permute-start.13) | collective-permute-done | bytes 90144 | tf_op jit(solution)/shard_map/ppermute | solution.py:317
  49.7 2.7 %experts.3 = (bf16[32,1344]{1,0:T(8,128)(2,1)S(1)}, bf16[32,1344]{1,0:T(8,128)(2,1)S(1)}, bf16[32,1344]{1,0:T(8,128)(2,1)S(1)}, bf16[32,1344]{1,0:T(8,128)(2,1)S(1)}) custom-call(bf16[1,928,1344]{2,1,0:T(8,128)(2,1)S(1)} %get-tuple-element.59.after_ref.up_ref, bf16[1,928,1344]{2,1,0:T(8,128)(2,1)S(1)} %get-tuple-element.66.down_ref, ...), custom_call_target="tpu_custom_call" | custom-call | tf_op jit(solution)/shard_map/experts/pallas_call | solution.py:29
  52.4 1.2 %collective-permute-start.16 = (bf16[32,1344]{1,0:T(8,128)(2,1)S(1)}, bf16[32,1344]{1,0:T(8,128)(2,1)S(1)}, u32[]{:S(2)}, u32[]{:S(2)}) collective-permute-start(bf16[32,1344]{1,0:T(8,128)(2,1)S(1)} %get-tuple-element.83), channel_id=1, source_target_pairs={{0,2},{1,3},{2,0},{3,1},{4,6},{5,7},{6,4},{7,5},{8,10},{9,11},{10,... | collective-permute-start | bytes 258056 | tf_op jit(solution)/shard_map/ppermute | solution.py:317
  53.6 0.9 %collective-permute-start.18 = (bf16[32,1344]{1,0:T(8,128)(2,1)S(1)}, bf16[32,1344]{1,0:T(8,128)(2,1)S(1)}, u32[]{:S(2)}, u32[]{:S(2)}) collective-permute-start(bf16[32,1344]{1,0:T(8,128)(2,1)S(1)} %get-tuple-element.85), channel_id=1, source_target_pairs={{0,2},{1,3},{2,0},{3,1},{4,6},{5,7},{6,4},{7,5},{8,10},{9,11},{10,... | collective-permute-start | bytes 258056 | tf_op jit(solution)/shard_map/ppermute | solution.py:317
  54.5 1.1 %collective-permute-start.20 = (bf16[32,1344]{1,0:T(8,128)(2,1)S(1)}, bf16[32,1344]{1,0:T(8,128)(2,1)S(1)}, u32[]{:S(2)}, u32[]{:S(2)}) collective-permute-start(bf16[32,1344]{1,0:T(8,128)(2,1)S(1)} %get-tuple-element.89), channel_id=1, source_target_pairs={{0,2},{1,3},{2,0},{3,1},{4,6},{5,7},{6,4},{7,5},{8,10},{9,11},{10,... | collective-permute-start | bytes 258056 | tf_op jit(solution)/shard_map/ppermute | solution.py:317
  55.6 2.4 %collective-permute-done.16.refs_1_ = bf16[32,1344]{1,0:T(8,128)(2,1)S(1)} collective-permute-done((bf16[32,1344]{1,0:T(8,128)(2,1)S(1)}, bf16[32,1344]{1,0:T(8,128)(2,1)S(1)}, u32[]{:S(2)}, u32[]{:S(2)}) %collective-permute-start.16) | collective-permute-done | bytes 86048 | tf_op jit(solution)/shard_map/ppermute | solution.py:317
  58.0 1.2 %collective-permute-start.17 = (bf16[32,1344]{1,0:T(8,128)(2,1)S(1)}, bf16[32,1344]{1,0:T(8,128)(2,1)S(1)}, u32[]{:S(2)}, u32[]{:S(2)}) collective-permute-start(bf16[32,1344]{1,0:T(8,128)(2,1)S(1)} %sum.3), channel_id=1, source_target_pairs={{0,12},{1,5},{2,14},{3,7},{4,8},{5,1},{6,10},{7,3},{8,4},{9,13},{1... | collective-permute-start | bytes 258056 | tf_op jit(solution)/shard_map/ppermute | solution.py:327
  59.3 1.1 %collective-permute-start.19 = (bf16[32,1344]{1,0:T(8,128)(2,1)S(1)}, bf16[32,1344]{1,0:T(8,128)(2,1)S(1)}, u32[]{:S(2)}, u32[]{:S(2)}) collective-permute-start(bf16[32,1344]{1,0:T(8,128)(2,1)S(1)} %sum.4), channel_id=1, source_target_pairs={{0,8},{1,13},{2,10},{3,15},{4,12},{5,9},{6,14},{7,11},{8,0},{9,5},... | collective-permute-start | bytes 258056 | tf_op jit(solution)/shard_map/ppermute | solution.py:327
  60.3 1.2 %collective-permute-start.22 = (bf16[32,1344]{1,0:T(8,128)(2,1)S(1)}, bf16[32,1344]{1,0:T(8,128)(2,1)S(1)}, u32[]{:S(2)}, u32[]{:S(2)}) collective-permute-start(bf16[32,1344]{1,0:T(8,128)(2,1)S(1)} %get-tuple-element.90), channel_id=1, source_target_pairs={{0,2},{1,3},{2,0},{3,1},{4,6},{5,7},{6,4},{7,5},{8,10},{9,11},{10,... | collective-permute-start | bytes 258056 | tf_op jit(solution)/shard_map/ppermute | solution.py:317
  61.6 2.0 %collective-permute-start.21 = (bf16[32,1344]{1,0:T(8,128)(2,1)S(1)}, bf16[32,1344]{1,0:T(8,128)(2,1)S(1)}, u32[]{:S(2)}, u32[]{:S(2)}) collective-permute-start(bf16[32,1344]{1,0:T(8,128)(2,1)S(1)} %sum.5), channel_id=1, source_target_pairs={{0,4},{1,9},{2,6},{3,11},{4,0},{5,13},{6,2},{7,15},{8,12},{9,1},{1... | collective-permute-start | bytes 258056 | tf_op jit(solution)/shard_map/ppermute | solution.py:327
  63.6 1.0 %collective-permute-done.17.rest_1_ = bf16[32,1344]{1,0:T(8,128)(2,1)S(1)} collective-permute-done((bf16[32,1344]{1,0:T(8,128)(2,1)S(1)}, bf16[32,1344]{1,0:T(8,128)(2,1)S(1)}, u32[]{:S(2)}, u32[]{:S(2)}) %collective-permute-start.17) | collective-permute-done | bytes 86048 | tf_op jit(solution)/shard_map/ppermute | solution.py:327
  64.5 3.1 %collective-permute-done.19.rest_2_ = bf16[32,1344]{1,0:T(8,128)(2,1)S(1)} collective-permute-done((bf16[32,1344]{1,0:T(8,128)(2,1)S(1)}, bf16[32,1344]{1,0:T(8,128)(2,1)S(1)}, u32[]{:S(2)}, u32[]{:S(2)}) %collective-permute-start.19) | collective-permute-done | bytes 86048 | tf_op jit(solution)/shard_map/ppermute | solution.py:327
  67.6 0.1 collective-permute-done.21.rest_3_
  67.7 0.7 %last.1 = bf16[1,32,1344]{2,1,0:T(8,128)(2,1)} custom-call(bf16[32,1344]{1,0:T(8,128)(2,1)S(1)} %get-tuple-element.65.hidden_ref, bf16[32,1344]{1,0:T(8,128)(2,1)S(1)} %get-tuple-element.77.rest_0_, bf16[32,1344]{1,0:T(8,128)(2,1)S(1)} %collective-permute-done.17.rest_1_, bf16[32,1344]{1,0:T(8,128)(2,1)S(1)} %collective-permute-done.19.rest_2_, ...), custom_call_target="tpu_custom_call" | custom-call | tf_op jit(solution)/shard_map/last/pallas_call | solution.py:29
  (14 shorter events, 0.1 us)
Async XLA Ops:
  0.0 19.8 %collective-permute-start = (bf16[1,928,1344]{2,1,0:T(8,128)(2,1)}, bf16[1,928,1344]{2,1,0:T(8,128)(2,1)S(1)}, u32[]{:S(2)}, u32[]{:S(2)}) collective-permute-start(bf16[1,928,1344]{2,1,0:T(8,128)(2,1)} %bitcast.9), channel_id=1, source_target_pairs={{0,1},{1,0},{2,3},{3,2},{4,5},{5,4},{6,7},{7,6},{8,9},{9,8},{10,11... | collective-permute-start | bytes 7483400 | tf_op jit(solution)/shard_map/ppermute | solution.py:317
  0.5 19.4 %collective-permute-start.1 = (bf16[1,928,1344]{2,1,0:T(8,128)(2,1)}, bf16[1,928,1344]{2,1,0:T(8,128)(2,1)S(1)}, u32[]{:S(2)}, u32[]{:S(2)}) collective-permute-start(bf16[1,928,1344]{2,1,0:T(8,128)(2,1)} %down_hbm.1), channel_id=1, source_target_pairs={{0,1},{1,0},{2,3},{3,2},{4,5},{5,4},{6,7},{7,6},{8,9},{9,8},{10,11... | collective-permute-start | bytes 7483400 | tf_op jit(solution)/shard_map/ppermute | solution.py:317
  2.3 3.1 %collective-permute-start.2 = (bf16[4,144,128]{2,1,0:T(8,128)(2,1)S(1)}, bf16[4,144,128]{2,1,0:T(8,128)(2,1)S(1)}, u32[]{:S(2)}, u32[]{:S(2)}) collective-permute-start(bf16[4,144,128]{2,1,0:T(8,128)(2,1)S(1)} %get-tuple-element.55), channel_id=1, source_target_pairs={{0,1},{1,0},{2,3},{3,2},{4,5},{5,4},{6,7},{7,6},{8,9},{9,8},{10,11... | collective-permute-start | bytes 442376 | tf_op jit(solution)/shard_map/ppermute | solution.py:317
  5.5 7.1 %collective-permute-start.3 = (bf16[4,144,128]{2,1,0:T(8,128)(2,1)S(1)}, bf16[4,144,128]{2,1,0:T(8,128)(2,1)S(1)}, u32[]{:S(2)}, u32[]{:S(2)}) collective-permute-start(bf16[4,144,128]{2,1,0:T(8,128)(2,1)S(1)} %chip_state.1.rest_0_), channel_id=1, source_target_pairs={{0,2},{1,3},{2,0},{3,1},{4,6},{5,7},{6,4},{7,5},{8,10},{9,11},{10,... | collective-permute-start | bytes 442376 | tf_op jit(solution)/shard_map/ppermute | solution.py:317
  12.7 5.4 %collective-permute-start.4 = (bf16[4,144,128]{2,1,0:T(8,128)(2,1)S(1)}, bf16[4,144,128]{2,1,0:T(8,128)(2,1)S(1)}, u32[]{:S(2)}, u32[]{:S(2)}) collective-permute-start(bf16[4,144,128]{2,1,0:T(8,128)(2,1)S(1)} %span.1.rest_2_), channel_id=1, source_target_pairs={{0,16},{16,0},{1,17},{17,1},{2,18},{18,2},{3,19},{19,3},{4,20},{20... | collective-permute-start | bytes 442376 | tf_op jit(solution)/shard_map/ppermute | solution.py:317
  18.4 1.4 %collective-permute-start.5 = (bf16[4,128,128]{2,1,0:T(8,128)(2,1)S(1)}, bf16[4,128,128]{2,1,0:T(8,128)(2,1)S(1)}, u32[]{:S(2)}, u32[]{:S(2)}) collective-permute-start(bf16[4,128,128]{2,1,0:T(8,128)(2,1)S(1)} %get-tuple-element.57), channel_id=1, source_target_pairs={{0,1},{1,0},{2,3},{3,2},{4,5},{5,4},{6,7},{7,6},{8,9},{9,8},{10,11... | collective-permute-start | bytes 393224 | tf_op jit(solution)/shard_map/ppermute | solution.py:317
  21.2 7.4 %collective-permute-start.6 = (bf16[32,1344]{1,0:T(8,128)(2,1)S(1)}, bf16[32,1344]{1,0:T(8,128)(2,1)S(1)}, u32[]{:S(2)}, u32[]{:S(2)}) collective-permute-start(bf16[32,1344]{1,0:T(8,128)(2,1)S(1)} %get-tuple-element.62), channel_id=1, source_target_pairs={{0,12},{1,5},{2,14},{3,7},{4,8},{5,1},{6,10},{7,3},{8,4},{9,13},{1... | collective-permute-start | bytes 258056 | tf_op jit(solution)/shard_map/ppermute | solution.py:327
  24.8 8.4 %collective-permute-start.7 = (bf16[32,1344]{1,0:T(8,128)(2,1)S(1)}, bf16[32,1344]{1,0:T(8,128)(2,1)S(1)}, u32[]{:S(2)}, u32[]{:S(2)}) collective-permute-start(bf16[32,1344]{1,0:T(8,128)(2,1)S(1)} %get-tuple-element.63), channel_id=1, source_target_pairs={{0,8},{1,13},{2,10},{3,15},{4,12},{5,9},{6,14},{7,11},{8,0},{9,5},... | collective-permute-start | bytes 258056 | tf_op jit(solution)/shard_map/ppermute | solution.py:327
  24.8 8.4 %collective-permute-start.8 = (bf16[32,1344]{1,0:T(8,128)(2,1)S(1)}, bf16[32,1344]{1,0:T(8,128)(2,1)S(1)}, u32[]{:S(2)}, u32[]{:S(2)}) collective-permute-start(bf16[32,1344]{1,0:T(8,128)(2,1)S(1)} %get-tuple-element.64), channel_id=1, source_target_pairs={{0,4},{1,9},{2,6},{3,11},{4,0},{5,13},{6,2},{7,15},{8,12},{9,1},{1... | collective-permute-start | bytes 258056 | tf_op jit(solution)/shard_map/ppermute | solution.py:327
  33.4 8.4 %collective-permute-start.10 = (bf16[32,1408]{1,0:T(8,128)(2,1)S(1)}, bf16[32,1408]{1,0:T(8,128)(2,1)S(1)}, u32[]{:S(2)}, u32[]{:S(2)}) collective-permute-start(bf16[32,1408]{1,0:T(8,128)(2,1)S(1)} %get-tuple-element.71.rest_3_), channel_id=1, source_target_pairs={{0,8},{1,13},{2,10},{3,15},{4,12},{5,9},{6,14},{7,11},{8,0},{9,5},... | collective-permute-start | bytes 270344 | tf_op jit(solution)/shard_map/ppermute | solution.py:327
  33.5 11.2 %collective-permute-start.9 = (bf16[32,1408]{1,0:T(8,128)(2,1)S(1)}, bf16[32,1408]{1,0:T(8,128)(2,1)S(1)}, u32[]{:S(2)}, u32[]{:S(2)}) collective-permute-start(bf16[32,1408]{1,0:T(8,128)(2,1)S(1)} %get-tuple-element.71.rest_3_), channel_id=1, source_target_pairs={{0,12},{1,5},{2,14},{3,7},{4,8},{5,1},{6,10},{7,3},{8,4},{9,13},{1... | collective-permute-start | bytes 270344 | tf_op jit(solution)/shard_map/ppermute | solution.py:327
  35.9 8.7 %collective-permute-start.12 = (bf16[32,1408]{1,0:T(8,128)(2,1)S(1)}, bf16[32,1408]{1,0:T(8,128)(2,1)S(1)}, u32[]{:S(2)}, u32[]{:S(2)}) collective-permute-start(bf16[32,1408]{1,0:T(8,128)(2,1)S(1)} %get-tuple-element.71.rest_3_), channel_id=1, source_target_pairs={{0,2},{1,3},{2,0},{3,1},{4,6},{5,7},{6,4},{7,5},{8,10},{9,11},{10,... | collective-permute-start | bytes 270344 | tf_op jit(solution)/shard_map/ppermute | solution.py:317
  37.4 7.2 %collective-permute-start.11 = (bf16[32,1408]{1,0:T(8,128)(2,1)S(1)}, bf16[32,1408]{1,0:T(8,128)(2,1)S(1)}, u32[]{:S(2)}, u32[]{:S(2)}) collective-permute-start(bf16[32,1408]{1,0:T(8,128)(2,1)S(1)} %get-tuple-element.71.rest_3_), channel_id=1, source_target_pairs={{0,4},{1,9},{2,6},{3,11},{4,0},{5,13},{6,2},{7,15},{8,12},{9,1},{1... | collective-permute-start | bytes 270344 | tf_op jit(solution)/shard_map/ppermute | solution.py:327
  38.5 8.9 %collective-permute-start.15 = (bf16[32,1408]{1,0:T(8,128)(2,1)S(1)}, bf16[32,1408]{1,0:T(8,128)(2,1)S(1)}, u32[]{:S(2)}, u32[]{:S(2)}) collective-permute-start(bf16[32,1408]{1,0:T(8,128)(2,1)S(1)} %get-tuple-element.71.rest_3_), channel_id=1, source_target_pairs={{0,6},{1,11},{2,4},{3,9},{4,2},{5,15},{6,0},{7,13},{8,14},{9,3},{1... | collective-permute-start | bytes 270344 | tf_op jit(solution)/shard_map/ppermute | solution.py:327
  41.8 6.9 %collective-permute-start.14 = (bf16[32,1408]{1,0:T(8,128)(2,1)S(1)}, bf16[32,1408]{1,0:T(8,128)(2,1)S(1)}, u32[]{:S(2)}, u32[]{:S(2)}) collective-permute-start(bf16[32,1408]{1,0:T(8,128)(2,1)S(1)} %collective-permute-done.10.rest_1_), channel_id=1, source_target_pairs={{0,2},{1,3},{2,0},{3,1},{4,6},{5,7},{6,4},{7,5},{8,10},{9,11},{10,... | collective-permute-start | bytes 270344 | tf_op jit(solution)/shard_map/ppermute | solution.py:317
  44.6 5.1 %collective-permute-start.13 = (bf16[32,1408]{1,0:T(8,128)(2,1)S(1)}, bf16[32,1408]{1,0:T(8,128)(2,1)S(1)}, u32[]{:S(2)}, u32[]{:S(2)}) collective-permute-start(bf16[32,1408]{1,0:T(8,128)(2,1)S(1)} %collective-permute-done.9.rest_0_), channel_id=1, source_target_pairs={{0,2},{1,3},{2,0},{3,1},{4,6},{5,7},{6,4},{7,5},{8,10},{9,11},{10,... | collective-permute-start | bytes 270344 | tf_op jit(solution)/shard_map/ppermute | solution.py:317
  52.4 5.6 %collective-permute-start.16 = (bf16[32,1344]{1,0:T(8,128)(2,1)S(1)}, bf16[32,1344]{1,0:T(8,128)(2,1)S(1)}, u32[]{:S(2)}, u32[]{:S(2)}) collective-permute-start(bf16[32,1344]{1,0:T(8,128)(2,1)S(1)} %get-tuple-element.83), channel_id=1, source_target_pairs={{0,2},{1,3},{2,0},{3,1},{4,6},{5,7},{6,4},{7,5},{8,10},{9,11},{10,... | collective-permute-start | bytes 258056 | tf_op jit(solution)/shard_map/ppermute | solution.py:317
  53.6 5.7 %collective-permute-start.18 = (bf16[32,1344]{1,0:T(8,128)(2,1)S(1)}, bf16[32,1344]{1,0:T(8,128)(2,1)S(1)}, u32[]{:S(2)}, u32[]{:S(2)}) collective-permute-start(bf16[32,1344]{1,0:T(8,128)(2,1)S(1)} %get-tuple-element.85), channel_id=1, source_target_pairs={{0,2},{1,3},{2,0},{3,1},{4,6},{5,7},{6,4},{7,5},{8,10},{9,11},{10,... | collective-permute-start | bytes 258056 | tf_op jit(solution)/shard_map/ppermute | solution.py:317
  54.5 7.0 %collective-permute-start.20 = (bf16[32,1344]{1,0:T(8,128)(2,1)S(1)}, bf16[32,1344]{1,0:T(8,128)(2,1)S(1)}, u32[]{:S(2)}, u32[]{:S(2)}) collective-permute-start(bf16[32,1344]{1,0:T(8,128)(2,1)S(1)} %get-tuple-element.89), channel_id=1, source_target_pairs={{0,2},{1,3},{2,0},{3,1},{4,6},{5,7},{6,4},{7,5},{8,10},{9,11},{10,... | collective-permute-start | bytes 258056 | tf_op jit(solution)/shard_map/ppermute | solution.py:317
  58.0 6.5 %collective-permute-start.17 = (bf16[32,1344]{1,0:T(8,128)(2,1)S(1)}, bf16[32,1344]{1,0:T(8,128)(2,1)S(1)}, u32[]{:S(2)}, u32[]{:S(2)}) collective-permute-start(bf16[32,1344]{1,0:T(8,128)(2,1)S(1)} %sum.3), channel_id=1, source_target_pairs={{0,12},{1,5},{2,14},{3,7},{4,8},{5,1},{6,10},{7,3},{8,4},{9,13},{1... | collective-permute-start | bytes 258056 | tf_op jit(solution)/shard_map/ppermute | solution.py:327
  59.3 8.3 %collective-permute-start.19 = (bf16[32,1344]{1,0:T(8,128)(2,1)S(1)}, bf16[32,1344]{1,0:T(8,128)(2,1)S(1)}, u32[]{:S(2)}, u32[]{:S(2)}) collective-permute-start(bf16[32,1344]{1,0:T(8,128)(2,1)S(1)} %sum.4), channel_id=1, source_target_pairs={{0,8},{1,13},{2,10},{3,15},{4,12},{5,9},{6,14},{7,11},{8,0},{9,5},... | collective-permute-start | bytes 258056 | tf_op jit(solution)/shard_map/ppermute | solution.py:327
  60.3 7.3 %collective-permute-start.22 = (bf16[32,1344]{1,0:T(8,128)(2,1)S(1)}, bf16[32,1344]{1,0:T(8,128)(2,1)S(1)}, u32[]{:S(2)}, u32[]{:S(2)}) collective-permute-start(bf16[32,1344]{1,0:T(8,128)(2,1)S(1)} %get-tuple-element.90), channel_id=1, source_target_pairs={{0,2},{1,3},{2,0},{3,1},{4,6},{5,7},{6,4},{7,5},{8,10},{9,11},{10,... | collective-permute-start | bytes 258056 | tf_op jit(solution)/shard_map/ppermute | solution.py:317
  61.6 6.1 %collective-permute-start.21 = (bf16[32,1344]{1,0:T(8,128)(2,1)S(1)}, bf16[32,1344]{1,0:T(8,128)(2,1)S(1)}, u32[]{:S(2)}, u32[]{:S(2)}) collective-permute-start(bf16[32,1344]{1,0:T(8,128)(2,1)S(1)} %sum.5), channel_id=1, source_target_pairs={{0,4},{1,9},{2,6},{3,11},{4,0},{5,13},{6,2},{7,15},{8,12},{9,1},{1... | collective-permute-start | bytes 258056 | tf_op jit(solution)/shard_map/ppermute | solution.py:327

commit v8 on v7

--- a/solution.py
+++ b/solution.py
@@ -227,19 +227,17 @@
         load.wait()
 
 
-def mixed_kernel(after_up, after_down, local_ref, grown_ref, c_ref, norm_ref, w_ref, mine_ref, got_ref, *rest):
-    outs, (normed_ref, state_ref) = rest[:-2], rest[-2:]
-    half = mine_ref.shape[0]
-    pairs = 2 * half
-    state_ref[pl.ds(core_index() * half, half)] = mine_ref[...]
-    state_ref[pl.ds((1 - core_index()) * half, half)] = got_ref[...]
-    groups = c_ref.shape[1] // STATE
+def half_product(half, local_ref, grown_ref, c_ref, norm_ref, w_ref, state_ref, normed_ref, count):
+    pairs = state_ref.shape[0]
+    width = pairs * LANES
+    base = pl.multiple_of(half * width, width)
+    groups = c_ref.shape[1] // STATE // 2
     per_group = pairs // groups
     for group in range(groups):
-        c_group = c_ref[:, group * STATE : (group + 1) * STATE]
+        c_group = c_ref[:, pl.ds(pl.multiple_of((half * groups + group) * STATE, STATE), STATE)]
         gated, squares = [], 0.0
         for pair in range(group * per_group, (group + 1) * per_group):
-            span = slice(pair * LANES, (pair + 1) * LANES)
+            span = pl.ds(pl.multiple_of(base + pair * LANES, LANES), LANES)
             carried = jnp.dot(c_group, state_ref[pair], preferred_element_type=F32)
             value = local_ref[:, span] + grown_ref[:, span] * carried
             gated.append(value)
@@ -248,14 +246,29 @@
         inverse = lax.rsqrt(mean + 1e-05)
         for offset, value in enumerate(gated):
             pair = group * per_group + offset
-            span = slice(pair * LANES, (pair + 1) * LANES)
-            normed_ref[:, span] = (value * inverse * norm_ref[:, span]).astype(BF16)
+            gain = norm_ref[:, pl.ds(pl.multiple_of(base + pair * LANES, LANES), LANES)]
+            normed_ref[:, pair * LANES : (pair + 1) * LANES] = (value * inverse * gain).astype(BF16)
+    rows = normed_ref.shape[0] // count
+    blocks = []
+    for shift in range(count):
+        owner = lax.axis_index("head") ^ (head_offset(shift - 1, count) if shift else 0)
+        blocks.append(normed_ref[pl.ds(pl.multiple_of(owner * rows, rows), rows), :])
+    weight = w_ref[:, pl.ds(base, width)]
+    return lax.dot_general(jnp.concatenate(blocks, axis=0), weight, NT, preferred_element_type=F32)
+
+
+def first_half_kernel(count, local_ref, grown_ref, c_ref, norm_ref, w_ref, mine_ref, out_ref, normed_ref):
+    out_ref[...] = half_product(
+        core_index(), local_ref, grown_ref, c_ref, norm_ref, w_ref, mine_ref, normed_ref, count
+    )
+
+
+def mixed_kernel(after_up, after_down, local_ref, grown_ref, c_ref, norm_ref, w_ref, got_ref, first_ref, *rest):
+    outs, normed_ref = rest[:-1], rest[-1]
+    product = first_ref[...] + half_product(
+        1 - core_index(), local_ref, grown_ref, c_ref, norm_ref, w_ref, got_ref, normed_ref, len(outs)
+    )
     rows = outs[0].shape[0]
-    blocks = []
-    for shift in range(len(outs)):
-        owner = lax.axis_index("head") ^ (head_offset(shift - 1, len(outs)) if shift else 0)
-        blocks.append(normed_ref[pl.ds(pl.multiple_of(owner * rows, rows), rows), :])
-    product = lax.dot_general(jnp.concatenate(blocks, axis=0), w_ref[...], NT, preferred_element_type=F32)
     for shift, out in enumerate(outs):
         out[...] = product[shift * rows : (shift + 1) * rows].astype(BF16)
 
@@ -374,9 +387,10 @@
         megabytes=16,
     )
     up_turned = jnp.swapaxes(w_up, 1, 2)
-    other_up, other_down = swap(up_turned, "exp", 1), swap(w_down, "exp", 1)
     got = swap(send, "exp", 1)
     chip = call(chip_state_kernel, "chip_state", packed, [(VMEM, keep), (VMEM, got)])
+    chip, up_after, down_after = lax.optimization_barrier((chip, up_turned, w_down))
+    other_up, other_down = swap(up_after, "exp", 1), swap(down_after, "exp", 1)
     along_y = [chip] + [swap(chip, "exp", 2 * d) for d in range(1, chips)]
     span = call(
         span_kernel,
@@ -395,13 +409,21 @@
         megabytes=24,
     )
     before_got = swap(before_send, "exp", 1)
+    shared = [(VMEM, value) for value in (local, grown, c_held, norm_held, w_held)]
+    normed_half = pltpu.VMEM((length, channels // 2), BF16)
+    first = call(
+        functools.partial(first_half_kernel, head_size),
+        "first_half",
+        struct((length, model), F32),
+        shared + [(VMEM, before)],
+        [normed_half],
+    )
     mixed = call(
         mixed_kernel,
         "mixed",
         [struct((rows, model), BF16)] * head_size,
-        [(ANY, other_up), (ANY, other_down)]
-        + [(VMEM, value) for value in (local, grown, c_held, norm_held, w_held, before, before_got)],
-        [pltpu.VMEM((length, channels), BF16), pltpu.VMEM((pairs, STATE, LANES), BF16)],
+        [(ANY, other_up), (ANY, other_down)] + shared + [(VMEM, before_got), (VMEM, first)],
+        [normed_half],
     )
     up_held, down_held = call(
         weights_kernel,
@@ -445,7 +467,7 @@
         totals.append(
             call(sum_kernel, "sum", struct((rows, model), BF16), [(VMEM, v) for v in (back_near[k], *got)])
         )
-    totals[1], mine = lax.optimization_barrier((totals[1], [pieces[-1] for pieces in back_far]))
+    totals[-2], mine = lax.optimization_barrier((totals[-2], [pieces[-1] for pieces in back_far]))
     arrived = [swap_slot(total, k) for k, total in enumerate(totals)]
     arrived += [swap(piece, "exp", 2 * d) for d, piece in enumerate(mine, 1)]
     return call(

time: 68.7 us -> 66.7 us (0.971)
  waiting for transfers between devices: 22.3 us -> 19.9 us
    ppermute x13, waiting for transfers between devices: 10.8 us -> 8.37 us  [swap(): return lax.ppermute(value, axis, [(i, i ^ mask) for i in range(size)])]
    pallas_call x15 -> x16, Pallas kernels: 16.9 us -> 17.3 us  [call(): pl.pallas_call(kernel, out_shape=jax.tree.map(lambda out: pltpu.VMEM(out....]
  transfers between devices with their start and end apart: 23 -> 23, of which waited for: 13 -> 12; matrix products, arithmetic and copies ran while one was open for 2% -> 2% of each run, Pallas kernels for 18% -> 16%
where the time goes in v8:
time: 66.7 us; the launch traced here: 66.4 us
  starting transfers between devices  27.7 us (42%)
  waiting for transfers between devices  19.9 us (30%)
  Pallas kernels  17.3 us (26%)
  local copies, waits for them, and re-layouts  1.29 us (2%)
    pallas_call x16, Pallas kernels, call(): pl.pallas_call(kernel, out_shape=jax.tree.map(lambda out: pltpu.VMEM(out....  17.3 us
    ppermute x13, starting transfers between devices, swap(): return lax.ppermute(value, axis, [(i, i ^ mask) for i in range(size)])  14.5 us
    ppermute x10, starting transfers between devices, swap_slot(): return lax.ppermute(value, ('head', 'exp'), pairs)  13.2 us
    ppermute x10, waiting for transfers between devices, swap_slot(): return lax.ppermute(value, ('head', 'exp'), pairs)  11.6 us
    ppermute x13, waiting for transfers between devices, swap(): return lax.ppermute(value, axis, [(i, i ^ mask) for i in range(size)])  8.37 us
  transfers between devices with their start and end apart: 23, of which 12 were waited for; matrix products, arithmetic and copies ran while one was open for 2% of the time, Pallas kernels for 16%

profile of v8, /device:TPU:0, one launch (start us, length us, event | category | flops | bytes accessed | tf_op | source)
XLA Modules:
  0.0 66.4 jit_solution(9103007895131641485)
XLA Ops:
  0.0 1.8 %state.1 = (bf16[4,144,128]{2,1,0:T(8,128)(2,1)S(1)}, bf16[4,144,128]{2,1,0:T(8,128)(2,1)S(1)}) custom-call(bf16[128,1024]{1,0:T(8,128)(2,1)} %x_hbm.3, bf16[128,256]{1,0:T(8,128)(2,1)} %b_hbm.3, f32[16,128]{1,0:T(8,128)} %bitcast.11, f32[1,16]{1,0:T(1,128)} %bitcast.16), custom_call_target="tpu_custom_call" | custom-call | tf_op jit(solution)/shard_map/state/pallas_call | solution.py:29
  1.8 0.5 collective-permute-start
  2.4 1.0 %collective-permute-done.got_ref = bf16[4,144,128]{2,1,0:T(8,128)(2,1)S(1)} collective-permute-done((bf16[4,144,128]{2,1,0:T(8,128)(2,1)S(1)}, bf16[4,144,128]{2,1,0:T(8,128)(2,1)S(1)}, u32[]{:S(2)}, u32[]{:S(2)}) %collective-permute-start) | collective-permute-done | bytes 147488 | tf_op jit(solution)/shard_map/ppermute | solution.py:330
  3.4 0.1 chip_state.1.rest_0_
  3.5 0.4 collective-permute-start.1
  3.9 0.1 collective-permute-start.2
  4.0 2.9 %collective-permute-start.3 = (bf16[4,144,128]{2,1,0:T(8,128)(2,1)S(1)}, bf16[4,144,128]{2,1,0:T(8,128)(2,1)S(1)}, u32[]{:S(2)}, u32[]{:S(2)}) collective-permute-start(bf16[4,144,128]{2,1,0:T(8,128)(2,1)S(1)} %chip_state.1.rest_0_), channel_id=1, source_target_pairs={{0,2},{1,3},{2,0},{3,1},{4,6},{5,7},{6,4},{7,5},{8,10},{9,11},{10,... | collective-permute-start | bytes 442376 | tf_op jit(solution)/shard_map/ppermute | solution.py:330
  6.9 2.4 %inside.1 = (f32[128,1024]{1,0:T(8,128)S(1)}, f32[128,1024]{1,0:T(8,128)S(1)}, bf16[128,256]{1,0:T(8,128)(2,1)S(1)}) custom-call(bf16[128,1024]{1,0:T(8,128)(2,1)} %x_hbm.3, bf16[128,1024]{1,0:T(8,128)(2,1)} %z_hbm.1, bf16[128,256]{1,0:T(8,128)(2,1)} %b_hbm.3, bf16[128,256]{1,0:T(8,128)(2,1)} %c_hbm.1, f32[16,128]{1,0:T(8,128)} %bitcast.12, ...), custom_call_target="tpu_custom_call" | custom-call | tf_op jit(solution)/shard_map/inside/pallas_call | solution.py:29
  9.4 1.7 %collective-permute-done.3.rest_1_ = bf16[4,144,128]{2,1,0:T(8,128)(2,1)S(1)} collective-permute-done((bf16[4,144,128]{2,1,0:T(8,128)(2,1)S(1)}, bf16[4,144,128]{2,1,0:T(8,128)(2,1)S(1)}, u32[]{:S(2)}, u32[]{:S(2)}) %collective-permute-start.3) | collective-permute-done | bytes 147488 | tf_op jit(solution)/shard_map/ppermute | solution.py:330
  11.1 0.1 span.1.rest_2_
  11.2 1.8 %collective-permute-start.4 = (bf16[4,144,128]{2,1,0:T(8,128)(2,1)S(1)}, bf16[4,144,128]{2,1,0:T(8,128)(2,1)S(1)}, u32[]{:S(2)}, u32[]{:S(2)}) collective-permute-start(bf16[4,144,128]{2,1,0:T(8,128)(2,1)S(1)} %span.1.rest_2_), channel_id=1, source_target_pairs={{0,16},{16,0},{1,17},{17,1},{2,18},{18,2},{3,19},{19,3},{4,20},{20... | collective-permute-start | bytes 442376 | tf_op jit(solution)/shard_map/ppermute | solution.py:330
  12.9 1.3 %broadcast_in_dim.14.gain_hbm = f32[1,1344]{1,0:T(1,128)} reshape(f32[1344]{0:T(1024)} %param.27) | data formatting | bytes 10752 | tf_op jit(solution)/shard_map/broadcast_in_dim | solution.py:385
  14.2 1.9 %prep.1 = (bf16[32,128]{1,0:T(8,128)(2,1)S(1)}, bf16[1,32,1344]{2,1,0:T(8,128)(2,1)S(1)}, f32[1,1344]{1,0:T(1,128)S(1)}, f32[1,1024]{1,0:T(1,128)S(1)}, bf16[1344,1024]{1,0:T(8,128)(2,1)S(1)}) custom-call(bf16[1,32,1344]{2,1,0:T(8,128)(2,1)} %resid_hbm.1, s32[6,1,32]{2,1,0:T(1,128)} %bitcast.14, f32[6,1,32]{2,1,0:T(1,128)} %bitcast.15, ...), custom_call_target="tpu_custom_call" | custom-call | tf_op jit(solution)/shard_map/prep/pallas_call | solution.py:29
  16.2 0.4 collective-permute-done.4.rest_3_
  16.6 0.3 before.1
  16.9 0.1 collective-permute-start.5
  17.0 0.8 %first_half.1.first_ref = f32[128,1344]{1,0:T(8,128)S(1)} custom-call(f32[128,1024]{1,0:T(8,128)S(1)} %get-tuple-element.55.local_ref, f32[128,1024]{1,0:T(8,128)S(1)} %get-tuple-element.56.grown_ref, bf16[128,256]{1,0:T(8,128)(2,1)S(1)} %get-tuple-element.57.after_ref.c_ref, f32[1,1024]{1,0:T(1,128)S(1)} %get-tuple-element.58.norm_ref, ...), custom_call_target="tpu_custom_call" | custom-call | tf_op jit(solution)/shard_map/first_half/pallas_call | solution.py:29
  17.8 0.5 collective-permute-done.5.got_ref
  18.3 0.9 %mixed.1 = (bf16[32,1344]{1,0:T(8,128)(2,1)S(1)}, bf16[32,1344]{1,0:T(8,128)(2,1)S(1)}, bf16[32,1344]{1,0:T(8,128)(2,1)S(1)}, bf16[32,1344]{1,0:T(8,128)(2,1)S(1)}) custom-call(bf16[1,928,1344]{2,1,0:T(8,128)(2,1)S(1)} %collective-permute-done.1.after_up.other_up_ref, bf16[1,928,1344]{2,1,0:T(8,128)(2,1)S(1)} %collective-permute-done.2.after_down.other_down_ref, ...), custom_call_target="tpu_custom_call" | custom-call | tf_op jit(solution)/shard_map/mixed/pallas_call | solution.py:29
  19.2 3.6 %collective-permute-start.6 = (bf16[32,1344]{1,0:T(8,128)(2,1)S(1)}, bf16[32,1344]{1,0:T(8,128)(2,1)S(1)}, u32[]{:S(2)}, u32[]{:S(2)}) collective-permute-start(bf16[32,1344]{1,0:T(8,128)(2,1)S(1)} %get-tuple-element.68), channel_id=1, source_target_pairs={{0,12},{1,5},{2,14},{3,7},{4,8},{5,1},{6,10},{7,3},{8,4},{9,13},{1... | collective-permute-start | bytes 258056 | tf_op jit(solution)/shard_map/ppermute | solution.py:340
  22.8 0.8 %collective-permute-start.8 = (bf16[32,1344]{1,0:T(8,128)(2,1)S(1)}, bf16[32,1344]{1,0:T(8,128)(2,1)S(1)}, u32[]{:S(2)}, u32[]{:S(2)}) collective-permute-start(bf16[32,1344]{1,0:T(8,128)(2,1)S(1)} %get-tuple-element.70), channel_id=1, source_target_pairs={{0,4},{1,9},{2,6},{3,11},{4,0},{5,13},{6,2},{7,15},{8,12},{9,1},{1... | collective-permute-start | bytes 258056 | tf_op jit(solution)/shard_map/ppermute | solution.py:340
  23.6 2.5 %weights.1 = (bf16[1,928,1344]{2,1,0:T(8,128)(2,1)S(1)}, bf16[1,928,1344]{2,1,0:T(8,128)(2,1)S(1)}) custom-call(bf16[32,1344]{1,0:T(8,128)(2,1)S(1)} %get-tuple-element.64.after_ref.rest_0_, bf16[1,928,1344]{2,1,0:T(8,128)(2,1)} %bitcast.10, bf16[1,928,1344]{2,1,0:T(8,128)(2,1)} %down_hbm.1), custom_call_target="tpu_custom_call" | custom-call | tf_op jit(solution)/shard_map/weights/pallas_call | solution.py:29
  26.2 0.4 collective-permute-done.6.rest_1_
  26.5 4.7 %collective-permute-done.7.rest_2_ = bf16[32,1344]{1,0:T(8,128)(2,1)S(1)} collective-permute-done((bf16[32,1344]{1,0:T(8,128)(2,1)S(1)}, bf16[32,1344]{1,0:T(8,128)(2,1)S(1)}, u32[]{:S(2)}, u32[]{:S(2)}) %collective-permute-start.7) | collective-permute-done | bytes 86048 | tf_op jit(solution)/shard_map/ppermute | solution.py:340
  31.2 0.2 rows.1
  31.4 0.1 collective-permute-start.10
  31.5 2.5 %collective-permute-start.9 = (bf16[32,1408]{1,0:T(8,128)(2,1)S(1)}, bf16[32,1408]{1,0:T(8,128)(2,1)S(1)}, u32[]{:S(2)}, u32[]{:S(2)}) collective-permute-start(bf16[32,1408]{1,0:T(8,128)(2,1)S(1)} %get-tuple-element.77.rest_3_), channel_id=1, source_target_pairs={{0,12},{1,5},{2,14},{3,7},{4,8},{5,1},{6,10},{7,3},{8,4},{9,13},{1... | collective-permute-start | bytes 270344 | tf_op jit(solution)/shard_map/ppermute | solution.py:340
  33.9 1.5 %collective-permute-start.12 = (bf16[32,1408]{1,0:T(8,128)(2,1)S(1)}, bf16[32,1408]{1,0:T(8,128)(2,1)S(1)}, u32[]{:S(2)}, u32[]{:S(2)}) collective-permute-start(bf16[32,1408]{1,0:T(8,128)(2,1)S(1)} %get-tuple-element.77.rest_3_), channel_id=1, source_target_pairs={{0,2},{1,3},{2,0},{3,1},{4,6},{5,7},{6,4},{7,5},{8,10},{9,11},{10,... | collective-permute-start | bytes 270344 | tf_op jit(solution)/shard_map/ppermute | solution.py:330
  35.5 1.0 %collective-permute-start.11 = (bf16[32,1408]{1,0:T(8,128)(2,1)S(1)}, bf16[32,1408]{1,0:T(8,128)(2,1)S(1)}, u32[]{:S(2)}, u32[]{:S(2)}) collective-permute-start(bf16[32,1408]{1,0:T(8,128)(2,1)S(1)} %get-tuple-element.77.rest_3_), channel_id=1, source_target_pairs={{0,4},{1,9},{2,6},{3,11},{4,0},{5,13},{6,2},{7,15},{8,12},{9,1},{1... | collective-permute-start | bytes 270344 | tf_op jit(solution)/shard_map/ppermute | solution.py:340
  36.5 1.0 %collective-permute-start.15 = (bf16[32,1408]{1,0:T(8,128)(2,1)S(1)}, bf16[32,1408]{1,0:T(8,128)(2,1)S(1)}, u32[]{:S(2)}, u32[]{:S(2)}) collective-permute-start(bf16[32,1408]{1,0:T(8,128)(2,1)S(1)} %get-tuple-element.77.rest_3_), channel_id=1, source_target_pairs={{0,6},{1,11},{2,4},{3,9},{4,2},{5,15},{6,0},{7,13},{8,14},{9,3},{1... | collective-permute-start | bytes 270344 | tf_op jit(solution)/shard_map/ppermute | solution.py:340
  37.4 2.4 %collective-permute-done.10.rest_1_ = bf16[32,1408]{1,0:T(8,128)(2,1)S(1)} collective-permute-done((bf16[32,1408]{1,0:T(8,128)(2,1)S(1)}, bf16[32,1408]{1,0:T(8,128)(2,1)S(1)}, u32[]{:S(2)}, u32[]{:S(2)}) %collective-permute-start.10) | collective-permute-done | bytes 90144 | tf_op jit(solution)/shard_map/ppermute | solution.py:340
  39.8 2.8 %collective-permute-start.14 = (bf16[32,1408]{1,0:T(8,128)(2,1)S(1)}, bf16[32,1408]{1,0:T(8,128)(2,1)S(1)}, u32[]{:S(2)}, u32[]{:S(2)}) collective-permute-start(bf16[32,1408]{1,0:T(8,128)(2,1)S(1)} %collective-permute-done.10.rest_1_), channel_id=1, source_target_pairs={{0,2},{1,3},{2,0},{3,1},{4,6},{5,7},{6,4},{7,5},{8,10},{9,11},{10,... | collective-permute-start | bytes 270344 | tf_op jit(solution)/shard_map/ppermute | solution.py:330
  42.7 2.7 %experts.2 = (bf16[32,1344]{1,0:T(8,128)(2,1)S(1)}, bf16[32,1344]{1,0:T(8,128)(2,1)S(1)}, bf16[32,1344]{1,0:T(8,128)(2,1)S(1)}, bf16[32,1344]{1,0:T(8,128)(2,1)S(1)}) custom-call(bf16[1,928,1344]{2,1,0:T(8,128)(2,1)S(1)} %get-tuple-element.65.after_ref.up_ref, bf16[1,928,1344]{2,1,0:T(8,128)(2,1)S(1)} %get-tuple-element.72.down_ref, ...), custom_call_target="tpu_custom_call" | custom-call | tf_op jit(solution)/shard_map/experts/pallas_call | solution.py:29
  45.4 1.3 %collective-permute-done.14.rest_1_ = bf16[32,1408]{1,0:T(8,128)(2,1)S(1)} collective-permute-done((bf16[32,1408]{1,0:T(8,128)(2,1)S(1)}, bf16[32,1408]{1,0:T(8,128)(2,1)S(1)}, u32[]{:S(2)}, u32[]{:S(2)}) %collective-permute-start.14) | collective-permute-done | bytes 90144 | tf_op jit(solution)/shard_map/ppermute | solution.py:330
  46.7 1.0 %collective-permute-done.13.rest_0_ = bf16[32,1408]{1,0:T(8,128)(2,1)S(1)} collective-permute-done((bf16[32,1408]{1,0:T(8,128)(2,1)S(1)}, bf16[32,1408]{1,0:T(8,128)(2,1)S(1)}, u32[]{:S(2)}, u32[]{:S(2)}) %collective-permute-start.13) | collective-permute-done | bytes 90144 | tf_op jit(solution)/shard_map/ppermute | solution.py:330
  47.7 2.7 %experts.3 = (bf16[32,1344]{1,0:T(8,128)(2,1)S(1)}, bf16[32,1344]{1,0:T(8,128)(2,1)S(1)}, bf16[32,1344]{1,0:T(8,128)(2,1)S(1)}, bf16[32,1344]{1,0:T(8,128)(2,1)S(1)}) custom-call(bf16[1,928,1344]{2,1,0:T(8,128)(2,1)S(1)} %get-tuple-element.65.after_ref.up_ref, bf16[1,928,1344]{2,1,0:T(8,128)(2,1)S(1)} %get-tuple-element.72.down_ref, ...), custom_call_target="tpu_custom_call" | custom-call | tf_op jit(solution)/shard_map/experts/pallas_call | solution.py:29
  50.4 1.2 %collective-permute-start.16 = (bf16[32,1344]{1,0:T(8,128)(2,1)S(1)}, bf16[32,1344]{1,0:T(8,128)(2,1)S(1)}, u32[]{:S(2)}, u32[]{:S(2)}) collective-permute-start(bf16[32,1344]{1,0:T(8,128)(2,1)S(1)} %get-tuple-element.89), channel_id=1, source_target_pairs={{0,2},{1,3},{2,0},{3,1},{4,6},{5,7},{6,4},{7,5},{8,10},{9,11},{10,... | collective-permute-start | bytes 258056 | tf_op jit(solution)/shard_map/ppermute | solution.py:330
  51.6 0.9 %collective-permute-start.18 = (bf16[32,1344]{1,0:T(8,128)(2,1)S(1)}, bf16[32,1344]{1,0:T(8,128)(2,1)S(1)}, u32[]{:S(2)}, u32[]{:S(2)}) collective-permute-start(bf16[32,1344]{1,0:T(8,128)(2,1)S(1)} %get-tuple-element.91), channel_id=1, source_target_pairs={{0,2},{1,3},{2,0},{3,1},{4,6},{5,7},{6,4},{7,5},{8,10},{9,11},{10,... | collective-permute-start | bytes 258056 | tf_op jit(solution)/shard_map/ppermute | solution.py:330
  52.5 1.1 %collective-permute-start.20 = (bf16[32,1344]{1,0:T(8,128)(2,1)S(1)}, bf16[32,1344]{1,0:T(8,128)(2,1)S(1)}, u32[]{:S(2)}, u32[]{:S(2)}) collective-permute-start(bf16[32,1344]{1,0:T(8,128)(2,1)S(1)} %get-tuple-element.95), channel_id=1, source_target_pairs={{0,2},{1,3},{2,0},{3,1},{4,6},{5,7},{6,4},{7,5},{8,10},{9,11},{10,... | collective-permute-start | bytes 258056 | tf_op jit(solution)/shard_map/ppermute | solution.py:330
  53.6 2.4 %collective-permute-done.16.refs_1_ = bf16[32,1344]{1,0:T(8,128)(2,1)S(1)} collective-permute-done((bf16[32,1344]{1,0:T(8,128)(2,1)S(1)}, bf16[32,1344]{1,0:T(8,128)(2,1)S(1)}, u32[]{:S(2)}, u32[]{:S(2)}) %collective-permute-start.16) | collective-permute-done | bytes 86048 | tf_op jit(solution)/shard_map/ppermute | solution.py:330
  56.1 1.2 %collective-permute-start.17 = (bf16[32,1344]{1,0:T(8,128)(2,1)S(1)}, bf16[32,1344]{1,0:T(8,128)(2,1)S(1)}, u32[]{:S(2)}, u32[]{:S(2)}) collective-permute-start(bf16[32,1344]{1,0:T(8,128)(2,1)S(1)} %sum.3), channel_id=1, source_target_pairs={{0,12},{1,5},{2,14},{3,7},{4,8},{5,1},{6,10},{7,3},{8,4},{9,13},{1... | collective-permute-start | bytes 258056 | tf_op jit(solution)/shard_map/ppermute | solution.py:340
  57.3 1.1 %collective-permute-start.19 = (bf16[32,1344]{1,0:T(8,128)(2,1)S(1)}, bf16[32,1344]{1,0:T(8,128)(2,1)S(1)}, u32[]{:S(2)}, u32[]{:S(2)}) collective-permute-start(bf16[32,1344]{1,0:T(8,128)(2,1)S(1)} %sum.4), channel_id=1, source_target_pairs={{0,8},{1,13},{2,10},{3,15},{4,12},{5,9},{6,14},{7,11},{8,0},{9,5},... | collective-permute-start | bytes 258056 | tf_op jit(solution)/shard_map/ppermute | solution.py:340
  58.4 1.2 %collective-permute-start.22 = (bf16[32,1344]{1,0:T(8,128)(2,1)S(1)}, bf16[32,1344]{1,0:T(8,128)(2,1)S(1)}, u32[]{:S(2)}, u32[]{:S(2)}) collective-permute-start(bf16[32,1344]{1,0:T(8,128)(2,1)S(1)} %get-tuple-element.96), channel_id=1, source_target_pairs={{0,2},{1,3},{2,0},{3,1},{4,6},{5,7},{6,4},{7,5},{8,10},{9,11},{10,... | collective-permute-start | bytes 258056 | tf_op jit(solution)/shard_map/ppermute | solution.py:330
  59.6 2.0 %collective-permute-start.21 = (bf16[32,1344]{1,0:T(8,128)(2,1)S(1)}, bf16[32,1344]{1,0:T(8,128)(2,1)S(1)}, u32[]{:S(2)}, u32[]{:S(2)}) collective-permute-start(bf16[32,1344]{1,0:T(8,128)(2,1)S(1)} %sum.5), channel_id=1, source_target_pairs={{0,4},{1,9},{2,6},{3,11},{4,0},{5,13},{6,2},{7,15},{8,12},{9,1},{1... | collective-permute-start | bytes 258056 | tf_op jit(solution)/shard_map/ppermute | solution.py:340
  61.6 1.0 %collective-permute-done.17.rest_1_ = bf16[32,1344]{1,0:T(8,128)(2,1)S(1)} collective-permute-done((bf16[32,1344]{1,0:T(8,128)(2,1)S(1)}, bf16[32,1344]{1,0:T(8,128)(2,1)S(1)}, u32[]{:S(2)}, u32[]{:S(2)}) %collective-permute-start.17) | collective-permute-done | bytes 86048 | tf_op jit(solution)/shard_map/ppermute | solution.py:340
  62.6 3.1 %collective-permute-done.19.rest_2_ = bf16[32,1344]{1,0:T(8,128)(2,1)S(1)} collective-permute-done((bf16[32,1344]{1,0:T(8,128)(2,1)S(1)}, bf16[32,1344]{1,0:T(8,128)(2,1)S(1)}, u32[]{:S(2)}, u32[]{:S(2)}) %collective-permute-start.19) | collective-permute-done | bytes 86048 | tf_op jit(solution)/shard_map/ppermute | solution.py:340
  65.7 0.0 collective-permute-done.21.rest_3_
  65.7 0.7 %last.1 = bf16[1,32,1344]{2,1,0:T(8,128)(2,1)} custom-call(bf16[32,1344]{1,0:T(8,128)(2,1)S(1)} %get-tuple-element.71.hidden_ref, bf16[32,1344]{1,0:T(8,128)(2,1)S(1)} %get-tuple-element.83.rest_0_, bf16[32,1344]{1,0:T(8,128)(2,1)S(1)} %collective-permute-done.17.rest_1_, bf16[32,1344]{1,0:T(8,128)(2,1)S(1)} %collective-permute-done.19.rest_2_, ...), custom_call_target="tpu_custom_call" | custom-call | tf_op jit(solution)/shard_map/last/pallas_call | solution.py:29
  (15 shorter events, 0.1 us)
Async XLA Ops:
  1.8 1.5 %collective-permute-start = (bf16[4,144,128]{2,1,0:T(8,128)(2,1)S(1)}, bf16[4,144,128]{2,1,0:T(8,128)(2,1)S(1)}, u32[]{:S(2)}, u32[]{:S(2)}) collective-permute-start(bf16[4,144,128]{2,1,0:T(8,128)(2,1)S(1)} %get-tuple-element.52), channel_id=1, source_target_pairs={{0,1},{1,0},{2,3},{3,2},{4,5},{5,4},{6,7},{7,6},{8,9},{9,8},{10,11... | collective-permute-start | bytes 442376 | tf_op jit(solution)/shard_map/ppermute | solution.py:330
  3.5 14.9 %collective-permute-start.1 = (bf16[1,928,1344]{2,1,0:T(8,128)(2,1)}, bf16[1,928,1344]{2,1,0:T(8,128)(2,1)S(1)}, u32[]{:S(2)}, u32[]{:S(2)}) collective-permute-start(bf16[1,928,1344]{2,1,0:T(8,128)(2,1)} %bitcast.9), channel_id=1, source_target_pairs={{0,1},{1,0},{2,3},{3,2},{4,5},{5,4},{6,7},{7,6},{8,9},{9,8},{10,11... | collective-permute-start | bytes 7483400 | tf_op jit(solution)/shard_map/ppermute | solution.py:330
  3.9 14.4 %collective-permute-start.2 = (bf16[1,928,1344]{2,1,0:T(8,128)(2,1)}, bf16[1,928,1344]{2,1,0:T(8,128)(2,1)S(1)}, u32[]{:S(2)}, u32[]{:S(2)}) collective-permute-start(bf16[1,928,1344]{2,1,0:T(8,128)(2,1)} %down_hbm.1), channel_id=1, source_target_pairs={{0,1},{1,0},{2,3},{3,2},{4,5},{5,4},{6,7},{7,6},{8,9},{9,8},{10,11... | collective-permute-start | bytes 7483400 | tf_op jit(solution)/shard_map/ppermute | solution.py:330
  4.0 7.0 %collective-permute-start.3 = (bf16[4,144,128]{2,1,0:T(8,128)(2,1)S(1)}, bf16[4,144,128]{2,1,0:T(8,128)(2,1)S(1)}, u32[]{:S(2)}, u32[]{:S(2)}) collective-permute-start(bf16[4,144,128]{2,1,0:T(8,128)(2,1)S(1)} %chip_state.1.rest_0_), channel_id=1, source_target_pairs={{0,2},{1,3},{2,0},{3,1},{4,6},{5,7},{6,4},{7,5},{8,10},{9,11},{10,... | collective-permute-start | bytes 442376 | tf_op jit(solution)/shard_map/ppermute | solution.py:330
  11.2 5.5 %collective-permute-start.4 = (bf16[4,144,128]{2,1,0:T(8,128)(2,1)S(1)}, bf16[4,144,128]{2,1,0:T(8,128)(2,1)S(1)}, u32[]{:S(2)}, u32[]{:S(2)}) collective-permute-start(bf16[4,144,128]{2,1,0:T(8,128)(2,1)S(1)} %span.1.rest_2_), channel_id=1, source_target_pairs={{0,16},{16,0},{1,17},{17,1},{2,18},{18,2},{3,19},{19,3},{4,20},{20... | collective-permute-start | bytes 442376 | tf_op jit(solution)/shard_map/ppermute | solution.py:330
  16.9 1.4 %collective-permute-start.5 = (bf16[4,128,128]{2,1,0:T(8,128)(2,1)S(1)}, bf16[4,128,128]{2,1,0:T(8,128)(2,1)S(1)}, u32[]{:S(2)}, u32[]{:S(2)}) collective-permute-start(bf16[4,128,128]{2,1,0:T(8,128)(2,1)S(1)} %get-tuple-element.62), channel_id=1, source_target_pairs={{0,1},{1,0},{2,3},{3,2},{4,5},{5,4},{6,7},{7,6},{8,9},{9,8},{10,11... | collective-permute-start | bytes 393224 | tf_op jit(solution)/shard_map/ppermute | solution.py:330
  19.2 7.4 %collective-permute-start.6 = (bf16[32,1344]{1,0:T(8,128)(2,1)S(1)}, bf16[32,1344]{1,0:T(8,128)(2,1)S(1)}, u32[]{:S(2)}, u32[]{:S(2)}) collective-permute-start(bf16[32,1344]{1,0:T(8,128)(2,1)S(1)} %get-tuple-element.68), channel_id=1, source_target_pairs={{0,12},{1,5},{2,14},{3,7},{4,8},{5,1},{6,10},{7,3},{8,4},{9,13},{1... | collective-permute-start | bytes 258056 | tf_op jit(solution)/shard_map/ppermute | solution.py:340
  22.8 8.4 %collective-permute-start.7 = (bf16[32,1344]{1,0:T(8,128)(2,1)S(1)}, bf16[32,1344]{1,0:T(8,128)(2,1)S(1)}, u32[]{:S(2)}, u32[]{:S(2)}) collective-permute-start(bf16[32,1344]{1,0:T(8,128)(2,1)S(1)} %get-tuple-element.69), channel_id=1, source_target_pairs={{0,8},{1,13},{2,10},{3,15},{4,12},{5,9},{6,14},{7,11},{8,0},{9,5},... | collective-permute-start | bytes 258056 | tf_op jit(solution)/shard_map/ppermute | solution.py:340
  22.8 8.4 %collective-permute-start.8 = (bf16[32,1344]{1,0:T(8,128)(2,1)S(1)}, bf16[32,1344]{1,0:T(8,128)(2,1)S(1)}, u32[]{:S(2)}, u32[]{:S(2)}) collective-permute-start(bf16[32,1344]{1,0:T(8,128)(2,1)S(1)} %get-tuple-element.70), channel_id=1, source_target_pairs={{0,4},{1,9},{2,6},{3,11},{4,0},{5,13},{6,2},{7,15},{8,12},{9,1},{1... | collective-permute-start | bytes 258056 | tf_op jit(solution)/shard_map/ppermute | solution.py:340
  31.4 8.5 %collective-permute-start.10 = (bf16[32,1408]{1,0:T(8,128)(2,1)S(1)}, bf16[32,1408]{1,0:T(8,128)(2,1)S(1)}, u32[]{:S(2)}, u32[]{:S(2)}) collective-permute-start(bf16[32,1408]{1,0:T(8,128)(2,1)S(1)} %get-tuple-element.77.rest_3_), channel_id=1, source_target_pairs={{0,8},{1,13},{2,10},{3,15},{4,12},{5,9},{6,14},{7,11},{8,0},{9,5},... | collective-permute-start | bytes 270344 | tf_op jit(solution)/shard_map/ppermute | solution.py:340
  31.5 11.2 %collective-permute-start.9 = (bf16[32,1408]{1,0:T(8,128)(2,1)S(1)}, bf16[32,1408]{1,0:T(8,128)(2,1)S(1)}, u32[]{:S(2)}, u32[]{:S(2)}) collective-permute-start(bf16[32,1408]{1,0:T(8,128)(2,1)S(1)} %get-tuple-element.77.rest_3_), channel_id=1, source_target_pairs={{0,12},{1,5},{2,14},{3,7},{4,8},{5,1},{6,10},{7,3},{8,4},{9,13},{1... | collective-permute-start | bytes 270344 | tf_op jit(solution)/shard_map/ppermute | solution.py:340
  33.9 8.7 %collective-permute-start.12 = (bf16[32,1408]{1,0:T(8,128)(2,1)S(1)}, bf16[32,1408]{1,0:T(8,128)(2,1)S(1)}, u32[]{:S(2)}, u32[]{:S(2)}) collective-permute-start(bf16[32,1408]{1,0:T(8,128)(2,1)S(1)} %get-tuple-element.77.rest_3_), channel_id=1, source_target_pairs={{0,2},{1,3},{2,0},{3,1},{4,6},{5,7},{6,4},{7,5},{8,10},{9,11},{10,... | collective-permute-start | bytes 270344 | tf_op jit(solution)/shard_map/ppermute | solution.py:330
  35.5 7.2 %collective-permute-start.11 = (bf16[32,1408]{1,0:T(8,128)(2,1)S(1)}, bf16[32,1408]{1,0:T(8,128)(2,1)S(1)}, u32[]{:S(2)}, u32[]{:S(2)}) collective-permute-start(bf16[32,1408]{1,0:T(8,128)(2,1)S(1)} %get-tuple-element.77.rest_3_), channel_id=1, source_target_pairs={{0,4},{1,9},{2,6},{3,11},{4,0},{5,13},{6,2},{7,15},{8,12},{9,1},{1... | collective-permute-start | bytes 270344 | tf_op jit(solution)/shard_map/ppermute | solution.py:340
  36.5 8.9 %collective-permute-start.15 = (bf16[32,1408]{1,0:T(8,128)(2,1)S(1)}, bf16[32,1408]{1,0:T(8,128)(2,1)S(1)}, u32[]{:S(2)}, u32[]{:S(2)}) collective-permute-start(bf16[32,1408]{1,0:T(8,128)(2,1)S(1)} %get-tuple-element.77.rest_3_), channel_id=1, source_target_pairs={{0,6},{1,11},{2,4},{3,9},{4,2},{5,15},{6,0},{7,13},{8,14},{9,3},{1... | collective-permute-start | bytes 270344 | tf_op jit(solution)/shard_map/ppermute | solution.py:340
  39.8 6.9 %collective-permute-start.14 = (bf16[32,1408]{1,0:T(8,128)(2,1)S(1)}, bf16[32,1408]{1,0:T(8,128)(2,1)S(1)}, u32[]{:S(2)}, u32[]{:S(2)}) collective-permute-start(bf16[32,1408]{1,0:T(8,128)(2,1)S(1)} %collective-permute-done.10.rest_1_), channel_id=1, source_target_pairs={{0,2},{1,3},{2,0},{3,1},{4,6},{5,7},{6,4},{7,5},{8,10},{9,11},{10,... | collective-permute-start | bytes 270344 | tf_op jit(solution)/shard_map/ppermute | solution.py:330
  42.6 5.1 %collective-permute-start.13 = (bf16[32,1408]{1,0:T(8,128)(2,1)S(1)}, bf16[32,1408]{1,0:T(8,128)(2,1)S(1)}, u32[]{:S(2)}, u32[]{:S(2)}) collective-permute-start(bf16[32,1408]{1,0:T(8,128)(2,1)S(1)} %collective-permute-done.9.rest_0_), channel_id=1, source_target_pairs={{0,2},{1,3},{2,0},{3,1},{4,6},{5,7},{6,4},{7,5},{8,10},{9,11},{10,... | collective-permute-start | bytes 270344 | tf_op jit(solution)/shard_map/ppermute | solution.py:330
  50.4 5.6 %collective-permute-start.16 = (bf16[32,1344]{1,0:T(8,128)(2,1)S(1)}, bf16[32,1344]{1,0:T(8,128)(2,1)S(1)}, u32[]{:S(2)}, u32[]{:S(2)}) collective-permute-start(bf16[32,1344]{1,0:T(8,128)(2,1)S(1)} %get-tuple-element.89), channel_id=1, source_target_pairs={{0,2},{1,3},{2,0},{3,1},{4,6},{5,7},{6,4},{7,5},{8,10},{9,11},{10,... | collective-permute-start | bytes 258056 | tf_op jit(solution)/shard_map/ppermute | solution.py:330
  51.6 5.7 %collective-permute-start.18 = (bf16[32,1344]{1,0:T(8,128)(2,1)S(1)}, bf16[32,1344]{1,0:T(8,128)(2,1)S(1)}, u32[]{:S(2)}, u32[]{:S(2)}) collective-permute-start(bf16[32,1344]{1,0:T(8,128)(2,1)S(1)} %get-tuple-element.91), channel_id=1, source_target_pairs={{0,2},{1,3},{2,0},{3,1},{4,6},{5,7},{6,4},{7,5},{8,10},{9,11},{10,... | collective-permute-start | bytes 258056 | tf_op jit(solution)/shard_map/ppermute | solution.py:330
  52.5 7.1 %collective-permute-start.20 = (bf16[32,1344]{1,0:T(8,128)(2,1)S(1)}, bf16[32,1344]{1,0:T(8,128)(2,1)S(1)}, u32[]{:S(2)}, u32[]{:S(2)}) collective-permute-start(bf16[32,1344]{1,0:T(8,128)(2,1)S(1)} %get-tuple-element.95), channel_id=1, source_target_pairs={{0,2},{1,3},{2,0},{3,1},{4,6},{5,7},{6,4},{7,5},{8,10},{9,11},{10,... | collective-permute-start | bytes 258056 | tf_op jit(solution)/shard_map/ppermute | solution.py:330
  56.1 6.5 %collective-permute-start.17 = (bf16[32,1344]{1,0:T(8,128)(2,1)S(1)}, bf16[32,1344]{1,0:T(8,128)(2,1)S(1)}, u32[]{:S(2)}, u32[]{:S(2)}) collective-permute-start(bf16[32,1344]{1,0:T(8,128)(2,1)S(1)} %sum.3), channel_id=1, source_target_pairs={{0,12},{1,5},{2,14},{3,7},{4,8},{5,1},{6,10},{7,3},{8,4},{9,13},{1... | collective-permute-start | bytes 258056 | tf_op jit(solution)/shard_map/ppermute | solution.py:340
  57.3 8.4 %collective-permute-start.19 = (bf16[32,1344]{1,0:T(8,128)(2,1)S(1)}, bf16[32,1344]{1,0:T(8,128)(2,1)S(1)}, u32[]{:S(2)}, u32[]{:S(2)}) collective-permute-start(bf16[32,1344]{1,0:T(8,128)(2,1)S(1)} %sum.4), channel_id=1, source_target_pairs={{0,8},{1,13},{2,10},{3,15},{4,12},{5,9},{6,14},{7,11},{8,0},{9,5},... | collective-permute-start | bytes 258056 | tf_op jit(solution)/shard_map/ppermute | solution.py:340
  58.4 7.3 %collective-permute-start.22 = (bf16[32,1344]{1,0:T(8,128)(2,1)S(1)}, bf16[32,1344]{1,0:T(8,128)(2,1)S(1)}, u32[]{:S(2)}, u32[]{:S(2)}) collective-permute-start(bf16[32,1344]{1,0:T(8,128)(2,1)S(1)} %get-tuple-element.96), channel_id=1, source_target_pairs={{0,2},{1,3},{2,0},{3,1},{4,6},{5,7},{6,4},{7,5},{8,10},{9,11},{10,... | collective-permute-start | bytes 258056 | tf_op jit(solution)/shard_map/ppermute | solution.py:330
  59.6 6.1 %collective-permute-start.21 = (bf16[32,1344]{1,0:T(8,128)(2,1)S(1)}, bf16[32,1344]{1,0:T(8,128)(2,1)S(1)}, u32[]{:S(2)}, u32[]{:S(2)}) collective-permute-start(bf16[32,1344]{1,0:T(8,128)(2,1)S(1)} %sum.5), channel_id=1, source_target_pairs={{0,4},{1,9},{2,6},{3,11},{4,0},{5,13},{6,2},{7,15},{8,12},{9,1},{1... | collective-permute-start | bytes 258056 | tf_op jit(solution)/shard_map/ppermute | solution.py:340

commit v9 on v8

--- a/solution.py
+++ b/solution.py
@@ -39,7 +39,7 @@
 
 def offsets(count):
     down = list(range(count - 1, 0, -1))
-    return [down, down[-1:] + down[:-1]]
+    return [down, down[-2::-1] + down[-1:]]
 
 
 def head_offset(slot, count):

time: 66.7 us -> 65.7 us (0.985)
  waiting for transfers between devices: 19.9 us -> 17.5 us
  starting transfers between devices: 27.7 us -> 29.2 us
    ppermute x10, starting transfers between devices: 13.2 us -> 14.9 us  [swap_slot(): return lax.ppermute(value, ('head', 'exp'), pairs)]
    ppermute x13, waiting for transfers between devices: 8.37 us -> 6.91 us  [swap(): return lax.ppermute(value, axis, [(i, i ^ mask) for i in range(size)])]
    ppermute x10, waiting for transfers between devices: 11.6 us -> 10.6 us  [swap_slot(): return lax.ppermute(value, ('head', 'exp'), pairs)]
  transfers between devices with their start and end apart: 23 -> 23, of which waited for: 12 -> 13; matrix products, arithmetic and copies ran while one was open for 2% -> 2% of each run, Pallas kernels for 16% -> 17%
where the time goes in v9:
time: 65.7 us; the launch traced here: 65.4 us
  starting transfers between devices  29.2 us (44%)
  waiting for transfers between devices  17.5 us (27%)
  Pallas kernels  17.3 us (26%)
  local copies, waits for them, and re-layouts  1.29 us (2%)
    pallas_call x16, Pallas kernels, call(): pl.pallas_call(kernel, out_shape=jax.tree.map(lambda out: pltpu.VMEM(out....  17.3 us
    ppermute x10, starting transfers between devices, swap_slot(): return lax.ppermute(value, ('head', 'exp'), pairs)  14.9 us
    ppermute x13, starting transfers between devices, swap(): return lax.ppermute(value, axis, [(i, i ^ mask) for i in range(size)])  14.2 us
    ppermute x10, waiting for transfers between devices, swap_slot(): return lax.ppermute(value, ('head', 'exp'), pairs)  10.6 us
    ppermute x13, waiting for transfers between devices, swap(): return lax.ppermute(value, axis, [(i, i ^ mask) for i in range(size)])  6.91 us
  transfers between devices with their start and end apart: 23, of which 13 were waited for; matrix products, arithmetic and copies ran while one was open for 2% of the time, Pallas kernels for 17%

profile of v9, /device:TPU:0, one launch (start us, length us, event | category | flops | bytes accessed | tf_op | source)
XLA Modules:
  0.0 65.4 jit_solution(6288171077994224795)
XLA Ops:
  0.0 1.8 %state.1 = (bf16[4,144,128]{2,1,0:T(8,128)(2,1)S(1)}, bf16[4,144,128]{2,1,0:T(8,128)(2,1)S(1)}) custom-call(bf16[128,1024]{1,0:T(8,128)(2,1)} %x_hbm.3, bf16[128,256]{1,0:T(8,128)(2,1)} %b_hbm.3, f32[16,128]{1,0:T(8,128)} %bitcast.11, f32[1,16]{1,0:T(1,128)} %bitcast.16), custom_call_target="tpu_custom_call" | custom-call | tf_op jit(solution)/shard_map/state/pallas_call | solution.py:29
  1.8 0.5 collective-permute-start
  2.4 1.0 %collective-permute-done.got_ref = bf16[4,144,128]{2,1,0:T(8,128)(2,1)S(1)} collective-permute-done((bf16[4,144,128]{2,1,0:T(8,128)(2,1)S(1)}, bf16[4,144,128]{2,1,0:T(8,128)(2,1)S(1)}, u32[]{:S(2)}, u32[]{:S(2)}) %collective-permute-start) | collective-permute-done | bytes 147488 | tf_op jit(solution)/shard_map/ppermute | solution.py:330
  3.4 0.1 chip_state.1.rest_0_
  3.5 0.4 collective-permute-start.1
  3.9 0.1 collective-permute-start.2
  4.0 2.9 %collective-permute-start.3 = (bf16[4,144,128]{2,1,0:T(8,128)(2,1)S(1)}, bf16[4,144,128]{2,1,0:T(8,128)(2,1)S(1)}, u32[]{:S(2)}, u32[]{:S(2)}) collective-permute-start(bf16[4,144,128]{2,1,0:T(8,128)(2,1)S(1)} %chip_state.1.rest_0_), channel_id=1, source_target_pairs={{0,2},{1,3},{2,0},{3,1},{4,6},{5,7},{6,4},{7,5},{8,10},{9,11},{10,... | collective-permute-start | bytes 442376 | tf_op jit(solution)/shard_map/ppermute | solution.py:330
  6.9 2.4 %inside.1 = (f32[128,1024]{1,0:T(8,128)S(1)}, f32[128,1024]{1,0:T(8,128)S(1)}, bf16[128,256]{1,0:T(8,128)(2,1)S(1)}) custom-call(bf16[128,1024]{1,0:T(8,128)(2,1)} %x_hbm.3, bf16[128,1024]{1,0:T(8,128)(2,1)} %z_hbm.1, bf16[128,256]{1,0:T(8,128)(2,1)} %b_hbm.3, bf16[128,256]{1,0:T(8,128)(2,1)} %c_hbm.1, f32[16,128]{1,0:T(8,128)} %bitcast.12, ...), custom_call_target="tpu_custom_call" | custom-call | tf_op jit(solution)/shard_map/inside/pallas_call | solution.py:29
  9.4 1.7 %collective-permute-done.3.rest_1_ = bf16[4,144,128]{2,1,0:T(8,128)(2,1)S(1)} collective-permute-done((bf16[4,144,128]{2,1,0:T(8,128)(2,1)S(1)}, bf16[4,144,128]{2,1,0:T(8,128)(2,1)S(1)}, u32[]{:S(2)}, u32[]{:S(2)}) %collective-permute-start.3) | collective-permute-done | bytes 147488 | tf_op jit(solution)/shard_map/ppermute | solution.py:330
  11.1 0.1 span.1.rest_2_
  11.2 1.8 %collective-permute-start.4 = (bf16[4,144,128]{2,1,0:T(8,128)(2,1)S(1)}, bf16[4,144,128]{2,1,0:T(8,128)(2,1)S(1)}, u32[]{:S(2)}, u32[]{:S(2)}) collective-permute-start(bf16[4,144,128]{2,1,0:T(8,128)(2,1)S(1)} %span.1.rest_2_), channel_id=1, source_target_pairs={{0,16},{16,0},{1,17},{17,1},{2,18},{18,2},{3,19},{19,3},{4,20},{20... | collective-permute-start | bytes 442376 | tf_op jit(solution)/shard_map/ppermute | solution.py:330
  12.9 1.3 %broadcast_in_dim.14.gain_hbm = f32[1,1344]{1,0:T(1,128)} reshape(f32[1344]{0:T(1024)} %param.27) | data formatting | bytes 10752 | tf_op jit(solution)/shard_map/broadcast_in_dim | solution.py:385
  14.2 1.9 %prep.1 = (bf16[32,128]{1,0:T(8,128)(2,1)S(1)}, bf16[1,32,1344]{2,1,0:T(8,128)(2,1)S(1)}, f32[1,1344]{1,0:T(1,128)S(1)}, f32[1,1024]{1,0:T(1,128)S(1)}, bf16[1344,1024]{1,0:T(8,128)(2,1)S(1)}) custom-call(bf16[1,32,1344]{2,1,0:T(8,128)(2,1)} %resid_hbm.1, s32[6,1,32]{2,1,0:T(1,128)} %bitcast.14, f32[6,1,32]{2,1,0:T(1,128)} %bitcast.15, ...), custom_call_target="tpu_custom_call" | custom-call | tf_op jit(solution)/shard_map/prep/pallas_call | solution.py:29
  16.2 0.4 collective-permute-done.4.rest_3_
  16.6 0.3 before.1
  16.9 0.1 collective-permute-start.5
  17.0 0.8 %first_half.1.first_ref = f32[128,1344]{1,0:T(8,128)S(1)} custom-call(f32[128,1024]{1,0:T(8,128)S(1)} %get-tuple-element.55.local_ref, f32[128,1024]{1,0:T(8,128)S(1)} %get-tuple-element.56.grown_ref, bf16[128,256]{1,0:T(8,128)(2,1)S(1)} %get-tuple-element.57.after_ref.c_ref, f32[1,1024]{1,0:T(1,128)S(1)} %get-tuple-element.58.norm_ref, ...), custom_call_target="tpu_custom_call" | custom-call | tf_op jit(solution)/shard_map/first_half/pallas_call | solution.py:29
  17.8 0.5 collective-permute-done.5.got_ref
  18.3 0.9 %mixed.1 = (bf16[32,1344]{1,0:T(8,128)(2,1)S(1)}, bf16[32,1344]{1,0:T(8,128)(2,1)S(1)}, bf16[32,1344]{1,0:T(8,128)(2,1)S(1)}, bf16[32,1344]{1,0:T(8,128)(2,1)S(1)}) custom-call(bf16[1,928,1344]{2,1,0:T(8,128)(2,1)S(1)} %collective-permute-done.1.after_up.other_up_ref, bf16[1,928,1344]{2,1,0:T(8,128)(2,1)S(1)} %collective-permute-done.2.after_down.other_down_ref, ...), custom_call_target="tpu_custom_call" | custom-call | tf_op jit(solution)/shard_map/mixed/pallas_call | solution.py:29
  19.2 3.6 %collective-permute-start.6 = (bf16[32,1344]{1,0:T(8,128)(2,1)S(1)}, bf16[32,1344]{1,0:T(8,128)(2,1)S(1)}, u32[]{:S(2)}, u32[]{:S(2)}) collective-permute-start(bf16[32,1344]{1,0:T(8,128)(2,1)S(1)} %get-tuple-element.68), channel_id=1, source_target_pairs={{0,12},{1,9},{2,14},{3,11},{4,8},{5,13},{6,10},{7,15},{8,4},{9,1},... | collective-permute-start | bytes 258056 | tf_op jit(solution)/shard_map/ppermute | solution.py:340
  22.8 0.8 %collective-permute-start.8 = (bf16[32,1344]{1,0:T(8,128)(2,1)S(1)}, bf16[32,1344]{1,0:T(8,128)(2,1)S(1)}, u32[]{:S(2)}, u32[]{:S(2)}) collective-permute-start(bf16[32,1344]{1,0:T(8,128)(2,1)S(1)} %get-tuple-element.70), channel_id=1, source_target_pairs={{0,4},{1,5},{2,6},{3,7},{4,0},{5,1},{6,2},{7,3},{8,12},{9,13},{10,... | collective-permute-start | bytes 258056 | tf_op jit(solution)/shard_map/ppermute | solution.py:340
  23.6 2.5 %weights.1 = (bf16[1,928,1344]{2,1,0:T(8,128)(2,1)S(1)}, bf16[1,928,1344]{2,1,0:T(8,128)(2,1)S(1)}) custom-call(bf16[32,1344]{1,0:T(8,128)(2,1)S(1)} %get-tuple-element.64.after_ref.rest_0_, bf16[1,928,1344]{2,1,0:T(8,128)(2,1)} %bitcast.10, bf16[1,928,1344]{2,1,0:T(8,128)(2,1)} %down_hbm.1), custom_call_target="tpu_custom_call" | custom-call | tf_op jit(solution)/shard_map/weights/pallas_call | solution.py:29
  26.2 4.4 %collective-permute-done.7.rest_2_ = bf16[32,1344]{1,0:T(8,128)(2,1)S(1)} collective-permute-done((bf16[32,1344]{1,0:T(8,128)(2,1)S(1)}, bf16[32,1344]{1,0:T(8,128)(2,1)S(1)}, u32[]{:S(2)}, u32[]{:S(2)}) %collective-permute-start.7) | collective-permute-done | bytes 86048 | tf_op jit(solution)/shard_map/ppermute | solution.py:340
  30.6 0.2 rows.1
  30.8 0.5 collective-permute-start.10
  31.3 2.9 %collective-permute-start.9 = (bf16[32,1408]{1,0:T(8,128)(2,1)S(1)}, bf16[32,1408]{1,0:T(8,128)(2,1)S(1)}, u32[]{:S(2)}, u32[]{:S(2)}) collective-permute-start(bf16[32,1408]{1,0:T(8,128)(2,1)S(1)} %get-tuple-element.77.rest_3_), channel_id=1, source_target_pairs={{0,12},{1,9},{2,14},{3,11},{4,8},{5,13},{6,10},{7,15},{8,4},{9,1},... | collective-permute-start | bytes 270344 | tf_op jit(solution)/shard_map/ppermute | solution.py:340
  34.2 1.5 %collective-permute-start.12 = (bf16[32,1408]{1,0:T(8,128)(2,1)S(1)}, bf16[32,1408]{1,0:T(8,128)(2,1)S(1)}, u32[]{:S(2)}, u32[]{:S(2)}) collective-permute-start(bf16[32,1408]{1,0:T(8,128)(2,1)S(1)} %get-tuple-element.77.rest_3_), channel_id=1, source_target_pairs={{0,2},{1,3},{2,0},{3,1},{4,6},{5,7},{6,4},{7,5},{8,10},{9,11},{10,... | collective-permute-start | bytes 270344 | tf_op jit(solution)/shard_map/ppermute | solution.py:330
  35.7 0.5 collective-permute-start.11
  36.2 1.5 %collective-permute-start.15 = (bf16[32,1408]{1,0:T(8,128)(2,1)S(1)}, bf16[32,1408]{1,0:T(8,128)(2,1)S(1)}, u32[]{:S(2)}, u32[]{:S(2)}) collective-permute-start(bf16[32,1408]{1,0:T(8,128)(2,1)S(1)} %get-tuple-element.77.rest_3_), channel_id=1, source_target_pairs={{0,6},{1,7},{2,4},{3,5},{4,2},{5,3},{6,0},{7,1},{8,14},{9,15},{10,... | collective-permute-start | bytes 270344 | tf_op jit(solution)/shard_map/ppermute | solution.py:340
  37.6 2.4 %collective-permute-done.10.rest_1_ = bf16[32,1408]{1,0:T(8,128)(2,1)S(1)} collective-permute-done((bf16[32,1408]{1,0:T(8,128)(2,1)S(1)}, bf16[32,1408]{1,0:T(8,128)(2,1)S(1)}, u32[]{:S(2)}, u32[]{:S(2)}) %collective-permute-start.10) | collective-permute-done | bytes 90144 | tf_op jit(solution)/shard_map/ppermute | solution.py:340
  40.0 1.5 %collective-permute-start.14 = (bf16[32,1408]{1,0:T(8,128)(2,1)S(1)}, bf16[32,1408]{1,0:T(8,128)(2,1)S(1)}, u32[]{:S(2)}, u32[]{:S(2)}) collective-permute-start(bf16[32,1408]{1,0:T(8,128)(2,1)S(1)} %collective-permute-done.10.rest_1_), channel_id=1, source_target_pairs={{0,2},{1,3},{2,0},{3,1},{4,6},{5,7},{6,4},{7,5},{8,10},{9,11},{10,... | collective-permute-start | bytes 270344 | tf_op jit(solution)/shard_map/ppermute | solution.py:330
  41.5 0.5 collective-permute-start.13
  42.0 0.2 collective-permute-done.11.rest_2_
  42.3 2.7 %experts.2 = (bf16[32,1344]{1,0:T(8,128)(2,1)S(1)}, bf16[32,1344]{1,0:T(8,128)(2,1)S(1)}, bf16[32,1344]{1,0:T(8,128)(2,1)S(1)}, bf16[32,1344]{1,0:T(8,128)(2,1)S(1)}) custom-call(bf16[1,928,1344]{2,1,0:T(8,128)(2,1)S(1)} %get-tuple-element.65.after_ref.up_ref, bf16[1,928,1344]{2,1,0:T(8,128)(2,1)S(1)} %get-tuple-element.72.down_ref, ...), custom_call_target="tpu_custom_call" | custom-call | tf_op jit(solution)/shard_map/experts/pallas_call | solution.py:29
  45.0 0.3 collective-permute-done.14.rest_1_
  45.3 1.0 %collective-permute-done.13.rest_0_ = bf16[32,1408]{1,0:T(8,128)(2,1)S(1)} collective-permute-done((bf16[32,1408]{1,0:T(8,128)(2,1)S(1)}, bf16[32,1408]{1,0:T(8,128)(2,1)S(1)}, u32[]{:S(2)}, u32[]{:S(2)}) %collective-permute-start.13) | collective-permute-done | bytes 90144 | tf_op jit(solution)/shard_map/ppermute | solution.py:330
  46.3 2.7 %experts.3 = (bf16[32,1344]{1,0:T(8,128)(2,1)S(1)}, bf16[32,1344]{1,0:T(8,128)(2,1)S(1)}, bf16[32,1344]{1,0:T(8,128)(2,1)S(1)}, bf16[32,1344]{1,0:T(8,128)(2,1)S(1)}) custom-call(bf16[1,928,1344]{2,1,0:T(8,128)(2,1)S(1)} %get-tuple-element.65.after_ref.up_ref, bf16[1,928,1344]{2,1,0:T(8,128)(2,1)S(1)} %get-tuple-element.72.down_ref, ...), custom_call_target="tpu_custom_call" | custom-call | tf_op jit(solution)/shard_map/experts/pallas_call | solution.py:29
  49.0 1.4 %collective-permute-start.16 = (bf16[32,1344]{1,0:T(8,128)(2,1)S(1)}, bf16[32,1344]{1,0:T(8,128)(2,1)S(1)}, u32[]{:S(2)}, u32[]{:S(2)}) collective-permute-start(bf16[32,1344]{1,0:T(8,128)(2,1)S(1)} %get-tuple-element.89), channel_id=1, source_target_pairs={{0,2},{1,3},{2,0},{3,1},{4,6},{5,7},{6,4},{7,5},{8,10},{9,11},{10,... | collective-permute-start | bytes 258056 | tf_op jit(solution)/shard_map/ppermute | solution.py:330
  50.4 0.7 %collective-permute-start.18 = (bf16[32,1344]{1,0:T(8,128)(2,1)S(1)}, bf16[32,1344]{1,0:T(8,128)(2,1)S(1)}, u32[]{:S(2)}, u32[]{:S(2)}) collective-permute-start(bf16[32,1344]{1,0:T(8,128)(2,1)S(1)} %get-tuple-element.91), channel_id=1, source_target_pairs={{0,2},{1,3},{2,0},{3,1},{4,6},{5,7},{6,4},{7,5},{8,10},{9,11},{10,... | collective-permute-start | bytes 258056 | tf_op jit(solution)/shard_map/ppermute | solution.py:330
  51.1 1.4 %collective-permute-start.20 = (bf16[32,1344]{1,0:T(8,128)(2,1)S(1)}, bf16[32,1344]{1,0:T(8,128)(2,1)S(1)}, u32[]{:S(2)}, u32[]{:S(2)}) collective-permute-start(bf16[32,1344]{1,0:T(8,128)(2,1)S(1)} %get-tuple-element.95), channel_id=1, source_target_pairs={{0,2},{1,3},{2,0},{3,1},{4,6},{5,7},{6,4},{7,5},{8,10},{9,11},{10,... | collective-permute-start | bytes 258056 | tf_op jit(solution)/shard_map/ppermute | solution.py:330
  52.4 2.0 %collective-permute-done.16.refs_1_ = bf16[32,1344]{1,0:T(8,128)(2,1)S(1)} collective-permute-done((bf16[32,1344]{1,0:T(8,128)(2,1)S(1)}, bf16[32,1344]{1,0:T(8,128)(2,1)S(1)}, u32[]{:S(2)}, u32[]{:S(2)}) %collective-permute-start.16) | collective-permute-done | bytes 86048 | tf_op jit(solution)/shard_map/ppermute | solution.py:330
  54.5 3.1 %collective-permute-start.17 = (bf16[32,1344]{1,0:T(8,128)(2,1)S(1)}, bf16[32,1344]{1,0:T(8,128)(2,1)S(1)}, u32[]{:S(2)}, u32[]{:S(2)}) collective-permute-start(bf16[32,1344]{1,0:T(8,128)(2,1)S(1)} %sum.3), channel_id=1, source_target_pairs={{0,12},{1,9},{2,14},{3,11},{4,8},{5,13},{6,10},{7,15},{8,4},{9,1},... | collective-permute-start | bytes 258056 | tf_op jit(solution)/shard_map/ppermute | solution.py:340
  57.6 1.4 %collective-permute-start.22 = (bf16[32,1344]{1,0:T(8,128)(2,1)S(1)}, bf16[32,1344]{1,0:T(8,128)(2,1)S(1)}, u32[]{:S(2)}, u32[]{:S(2)}) collective-permute-start(bf16[32,1344]{1,0:T(8,128)(2,1)S(1)} %get-tuple-element.96), channel_id=1, source_target_pairs={{0,2},{1,3},{2,0},{3,1},{4,6},{5,7},{6,4},{7,5},{8,10},{9,11},{10,... | collective-permute-start | bytes 258056 | tf_op jit(solution)/shard_map/ppermute | solution.py:330
  59.1 2.0 %collective-permute-start.21 = (bf16[32,1344]{1,0:T(8,128)(2,1)S(1)}, bf16[32,1344]{1,0:T(8,128)(2,1)S(1)}, u32[]{:S(2)}, u32[]{:S(2)}) collective-permute-start(bf16[32,1344]{1,0:T(8,128)(2,1)S(1)} %sum.5), channel_id=1, source_target_pairs={{0,4},{1,5},{2,6},{3,7},{4,0},{5,1},{6,2},{7,3},{8,12},{9,13},{10,... | collective-permute-start | bytes 258056 | tf_op jit(solution)/shard_map/ppermute | solution.py:340
  61.1 0.7 %collective-permute-done.17.rest_1_ = bf16[32,1344]{1,0:T(8,128)(2,1)S(1)} collective-permute-done((bf16[32,1344]{1,0:T(8,128)(2,1)S(1)}, bf16[32,1344]{1,0:T(8,128)(2,1)S(1)}, u32[]{:S(2)}, u32[]{:S(2)}) %collective-permute-start.17) | collective-permute-done | bytes 86048 | tf_op jit(solution)/shard_map/ppermute | solution.py:340
  61.8 2.1 %collective-permute-done.19.rest_2_ = bf16[32,1344]{1,0:T(8,128)(2,1)S(1)} collective-permute-done((bf16[32,1344]{1,0:T(8,128)(2,1)S(1)}, bf16[32,1344]{1,0:T(8,128)(2,1)S(1)}, u32[]{:S(2)}, u32[]{:S(2)}) %collective-permute-start.19) | collective-permute-done | bytes 86048 | tf_op jit(solution)/shard_map/ppermute | solution.py:340
  63.9 0.8 %collective-permute-done.21.rest_3_ = bf16[32,1344]{1,0:T(8,128)(2,1)S(1)} collective-permute-done((bf16[32,1344]{1,0:T(8,128)(2,1)S(1)}, bf16[32,1344]{1,0:T(8,128)(2,1)S(1)}, u32[]{:S(2)}, u32[]{:S(2)}) %collective-permute-start.21) | collective-permute-done | bytes 86048 | tf_op jit(solution)/shard_map/ppermute | solution.py:340
  64.7 0.7 %last.1 = bf16[1,32,1344]{2,1,0:T(8,128)(2,1)} custom-call(bf16[32,1344]{1,0:T(8,128)(2,1)S(1)} %get-tuple-element.71.hidden_ref, bf16[32,1344]{1,0:T(8,128)(2,1)S(1)} %get-tuple-element.83.rest_0_, bf16[32,1344]{1,0:T(8,128)(2,1)S(1)} %collective-permute-done.17.rest_1_, bf16[32,1344]{1,0:T(8,128)(2,1)S(1)} %collective-permute-done.19.rest_2_, ...), custom_call_target="tpu_custom_call" | custom-call | tf_op jit(solution)/shard_map/last/pallas_call | solution.py:29
  (15 shorter events, 0.2 us)
Async XLA Ops:
  1.8 1.5 %collective-permute-start = (bf16[4,144,128]{2,1,0:T(8,128)(2,1)S(1)}, bf16[4,144,128]{2,1,0:T(8,128)(2,1)S(1)}, u32[]{:S(2)}, u32[]{:S(2)}) collective-permute-start(bf16[4,144,128]{2,1,0:T(8,128)(2,1)S(1)} %get-tuple-element.52), channel_id=1, source_target_pairs={{0,1},{1,0},{2,3},{3,2},{4,5},{5,4},{6,7},{7,6},{8,9},{9,8},{10,11... | collective-permute-start | bytes 442376 | tf_op jit(solution)/shard_map/ppermute | solution.py:330
  3.5 14.9 %collective-permute-start.1 = (bf16[1,928,1344]{2,1,0:T(8,128)(2,1)}, bf16[1,928,1344]{2,1,0:T(8,128)(2,1)S(1)}, u32[]{:S(2)}, u32[]{:S(2)}) collective-permute-start(bf16[1,928,1344]{2,1,0:T(8,128)(2,1)} %bitcast.9), channel_id=1, source_target_pairs={{0,1},{1,0},{2,3},{3,2},{4,5},{5,4},{6,7},{7,6},{8,9},{9,8},{10,11... | collective-permute-start | bytes 7483400 | tf_op jit(solution)/shard_map/ppermute | solution.py:330
  3.9 14.4 %collective-permute-start.2 = (bf16[1,928,1344]{2,1,0:T(8,128)(2,1)}, bf16[1,928,1344]{2,1,0:T(8,128)(2,1)S(1)}, u32[]{:S(2)}, u32[]{:S(2)}) collective-permute-start(bf16[1,928,1344]{2,1,0:T(8,128)(2,1)} %down_hbm.1), channel_id=1, source_target_pairs={{0,1},{1,0},{2,3},{3,2},{4,5},{5,4},{6,7},{7,6},{8,9},{9,8},{10,11... | collective-permute-start | bytes 7483400 | tf_op jit(solution)/shard_map/ppermute | solution.py:330
  4.0 7.0 %collective-permute-start.3 = (bf16[4,144,128]{2,1,0:T(8,128)(2,1)S(1)}, bf16[4,144,128]{2,1,0:T(8,128)(2,1)S(1)}, u32[]{:S(2)}, u32[]{:S(2)}) collective-permute-start(bf16[4,144,128]{2,1,0:T(8,128)(2,1)S(1)} %chip_state.1.rest_0_), channel_id=1, source_target_pairs={{0,2},{1,3},{2,0},{3,1},{4,6},{5,7},{6,4},{7,5},{8,10},{9,11},{10,... | collective-permute-start | bytes 442376 | tf_op jit(solution)/shard_map/ppermute | solution.py:330
  11.2 5.5 %collective-permute-start.4 = (bf16[4,144,128]{2,1,0:T(8,128)(2,1)S(1)}, bf16[4,144,128]{2,1,0:T(8,128)(2,1)S(1)}, u32[]{:S(2)}, u32[]{:S(2)}) collective-permute-start(bf16[4,144,128]{2,1,0:T(8,128)(2,1)S(1)} %span.1.rest_2_), channel_id=1, source_target_pairs={{0,16},{16,0},{1,17},{17,1},{2,18},{18,2},{3,19},{19,3},{4,20},{20... | collective-permute-start | bytes 442376 | tf_op jit(solution)/shard_map/ppermute | solution.py:330
  16.9 1.4 %collective-permute-start.5 = (bf16[4,128,128]{2,1,0:T(8,128)(2,1)S(1)}, bf16[4,128,128]{2,1,0:T(8,128)(2,1)S(1)}, u32[]{:S(2)}, u32[]{:S(2)}) collective-permute-start(bf16[4,128,128]{2,1,0:T(8,128)(2,1)S(1)} %get-tuple-element.62), channel_id=1, source_target_pairs={{0,1},{1,0},{2,3},{3,2},{4,5},{5,4},{6,7},{7,6},{8,9},{9,8},{10,11... | collective-permute-start | bytes 393224 | tf_op jit(solution)/shard_map/ppermute | solution.py:330
  19.2 7.0 %collective-permute-start.6 = (bf16[32,1344]{1,0:T(8,128)(2,1)S(1)}, bf16[32,1344]{1,0:T(8,128)(2,1)S(1)}, u32[]{:S(2)}, u32[]{:S(2)}) collective-permute-start(bf16[32,1344]{1,0:T(8,128)(2,1)S(1)} %get-tuple-element.68), channel_id=1, source_target_pairs={{0,12},{1,9},{2,14},{3,11},{4,8},{5,13},{6,10},{7,15},{8,4},{9,1},... | collective-permute-start | bytes 258056 | tf_op jit(solution)/shard_map/ppermute | solution.py:340
  22.8 7.8 %collective-permute-start.7 = (bf16[32,1344]{1,0:T(8,128)(2,1)S(1)}, bf16[32,1344]{1,0:T(8,128)(2,1)S(1)}, u32[]{:S(2)}, u32[]{:S(2)}) collective-permute-start(bf16[32,1344]{1,0:T(8,128)(2,1)S(1)} %get-tuple-element.69), channel_id=1, source_target_pairs={{0,8},{1,13},{2,10},{3,15},{4,12},{5,9},{6,14},{7,11},{8,0},{9,5},... | collective-permute-start | bytes 258056 | tf_op jit(solution)/shard_map/ppermute | solution.py:340
  22.8 7.8 %collective-permute-start.8 = (bf16[32,1344]{1,0:T(8,128)(2,1)S(1)}, bf16[32,1344]{1,0:T(8,128)(2,1)S(1)}, u32[]{:S(2)}, u32[]{:S(2)}) collective-permute-start(bf16[32,1344]{1,0:T(8,128)(2,1)S(1)} %get-tuple-element.70), channel_id=1, source_target_pairs={{0,4},{1,5},{2,6},{3,7},{4,0},{5,1},{6,2},{7,3},{8,12},{9,13},{10,... | collective-permute-start | bytes 258056 | tf_op jit(solution)/shard_map/ppermute | solution.py:340
  30.8 9.2 %collective-permute-start.10 = (bf16[32,1408]{1,0:T(8,128)(2,1)S(1)}, bf16[32,1408]{1,0:T(8,128)(2,1)S(1)}, u32[]{:S(2)}, u32[]{:S(2)}) collective-permute-start(bf16[32,1408]{1,0:T(8,128)(2,1)S(1)} %get-tuple-element.77.rest_3_), channel_id=1, source_target_pairs={{0,8},{1,13},{2,10},{3,15},{4,12},{5,9},{6,14},{7,11},{8,0},{9,5},... | collective-permute-start | bytes 270344 | tf_op jit(solution)/shard_map/ppermute | solution.py:340
  31.3 10.3 %collective-permute-start.9 = (bf16[32,1408]{1,0:T(8,128)(2,1)S(1)}, bf16[32,1408]{1,0:T(8,128)(2,1)S(1)}, u32[]{:S(2)}, u32[]{:S(2)}) collective-permute-start(bf16[32,1408]{1,0:T(8,128)(2,1)S(1)} %get-tuple-element.77.rest_3_), channel_id=1, source_target_pairs={{0,12},{1,9},{2,14},{3,11},{4,8},{5,13},{6,10},{7,15},{8,4},{9,1},... | collective-permute-start | bytes 270344 | tf_op jit(solution)/shard_map/ppermute | solution.py:340
  34.2 7.9 %collective-permute-start.12 = (bf16[32,1408]{1,0:T(8,128)(2,1)S(1)}, bf16[32,1408]{1,0:T(8,128)(2,1)S(1)}, u32[]{:S(2)}, u32[]{:S(2)}) collective-permute-start(bf16[32,1408]{1,0:T(8,128)(2,1)S(1)} %get-tuple-element.77.rest_3_), channel_id=1, source_target_pairs={{0,2},{1,3},{2,0},{3,1},{4,6},{5,7},{6,4},{7,5},{8,10},{9,11},{10,... | collective-permute-start | bytes 270344 | tf_op jit(solution)/shard_map/ppermute | solution.py:330
  35.7 6.6 %collective-permute-start.11 = (bf16[32,1408]{1,0:T(8,128)(2,1)S(1)}, bf16[32,1408]{1,0:T(8,128)(2,1)S(1)}, u32[]{:S(2)}, u32[]{:S(2)}) collective-permute-start(bf16[32,1408]{1,0:T(8,128)(2,1)S(1)} %get-tuple-element.77.rest_3_), channel_id=1, source_target_pairs={{0,4},{1,5},{2,6},{3,7},{4,0},{5,1},{6,2},{7,3},{8,12},{9,13},{10,... | collective-permute-start | bytes 270344 | tf_op jit(solution)/shard_map/ppermute | solution.py:340
  36.2 8.8 %collective-permute-start.15 = (bf16[32,1408]{1,0:T(8,128)(2,1)S(1)}, bf16[32,1408]{1,0:T(8,128)(2,1)S(1)}, u32[]{:S(2)}, u32[]{:S(2)}) collective-permute-start(bf16[32,1408]{1,0:T(8,128)(2,1)S(1)} %get-tuple-element.77.rest_3_), channel_id=1, source_target_pairs={{0,6},{1,7},{2,4},{3,5},{4,2},{5,3},{6,0},{7,1},{8,14},{9,15},{10,... | collective-permute-start | bytes 270344 | tf_op jit(solution)/shard_map/ppermute | solution.py:340
  40.0 5.3 %collective-permute-start.14 = (bf16[32,1408]{1,0:T(8,128)(2,1)S(1)}, bf16[32,1408]{1,0:T(8,128)(2,1)S(1)}, u32[]{:S(2)}, u32[]{:S(2)}) collective-permute-start(bf16[32,1408]{1,0:T(8,128)(2,1)S(1)} %collective-permute-done.10.rest_1_), channel_id=1, source_target_pairs={{0,2},{1,3},{2,0},{3,1},{4,6},{5,7},{6,4},{7,5},{8,10},{9,11},{10,... | collective-permute-start | bytes 270344 | tf_op jit(solution)/shard_map/ppermute | solution.py:330
  41.5 4.7 %collective-permute-start.13 = (bf16[32,1408]{1,0:T(8,128)(2,1)S(1)}, bf16[32,1408]{1,0:T(8,128)(2,1)S(1)}, u32[]{:S(2)}, u32[]{:S(2)}) collective-permute-start(bf16[32,1408]{1,0:T(8,128)(2,1)S(1)} %collective-permute-done.9.rest_0_), channel_id=1, source_target_pairs={{0,2},{1,3},{2,0},{3,1},{4,6},{5,7},{6,4},{7,5},{8,10},{9,11},{10,... | collective-permute-start | bytes 270344 | tf_op jit(solution)/shard_map/ppermute | solution.py:330
  49.0 5.5 %collective-permute-start.16 = (bf16[32,1344]{1,0:T(8,128)(2,1)S(1)}, bf16[32,1344]{1,0:T(8,128)(2,1)S(1)}, u32[]{:S(2)}, u32[]{:S(2)}) collective-permute-start(bf16[32,1344]{1,0:T(8,128)(2,1)S(1)} %get-tuple-element.89), channel_id=1, source_target_pairs={{0,2},{1,3},{2,0},{3,1},{4,6},{5,7},{6,4},{7,5},{8,10},{9,11},{10,... | collective-permute-start | bytes 258056 | tf_op jit(solution)/shard_map/ppermute | solution.py:330
  50.4 7.1 %collective-permute-start.18 = (bf16[32,1344]{1,0:T(8,128)(2,1)S(1)}, bf16[32,1344]{1,0:T(8,128)(2,1)S(1)}, u32[]{:S(2)}, u32[]{:S(2)}) collective-permute-start(bf16[32,1344]{1,0:T(8,128)(2,1)S(1)} %get-tuple-element.91), channel_id=1, source_target_pairs={{0,2},{1,3},{2,0},{3,1},{4,6},{5,7},{6,4},{7,5},{8,10},{9,11},{10,... | collective-permute-start | bytes 258056 | tf_op jit(solution)/shard_map/ppermute | solution.py:330
  51.1 8.0 %collective-permute-start.20 = (bf16[32,1344]{1,0:T(8,128)(2,1)S(1)}, bf16[32,1344]{1,0:T(8,128)(2,1)S(1)}, u32[]{:S(2)}, u32[]{:S(2)}) collective-permute-start(bf16[32,1344]{1,0:T(8,128)(2,1)S(1)} %get-tuple-element.95), channel_id=1, source_target_pairs={{0,2},{1,3},{2,0},{3,1},{4,6},{5,7},{6,4},{7,5},{8,10},{9,11},{10,... | collective-permute-start | bytes 258056 | tf_op jit(solution)/shard_map/ppermute | solution.py:330
  54.5 7.3 %collective-permute-start.17 = (bf16[32,1344]{1,0:T(8,128)(2,1)S(1)}, bf16[32,1344]{1,0:T(8,128)(2,1)S(1)}, u32[]{:S(2)}, u32[]{:S(2)}) collective-permute-start(bf16[32,1344]{1,0:T(8,128)(2,1)S(1)} %sum.3), channel_id=1, source_target_pairs={{0,12},{1,9},{2,14},{3,11},{4,8},{5,13},{6,10},{7,15},{8,4},{9,1},... | collective-permute-start | bytes 258056 | tf_op jit(solution)/shard_map/ppermute | solution.py:340
  57.6 6.3 %collective-permute-start.19 = (bf16[32,1344]{1,0:T(8,128)(2,1)S(1)}, bf16[32,1344]{1,0:T(8,128)(2,1)S(1)}, u32[]{:S(2)}, u32[]{:S(2)}) collective-permute-start(bf16[32,1344]{1,0:T(8,128)(2,1)S(1)} %sum.4), channel_id=1, source_target_pairs={{0,8},{1,13},{2,10},{3,15},{4,12},{5,9},{6,14},{7,11},{8,0},{9,5},... | collective-permute-start | bytes 258056 | tf_op jit(solution)/shard_map/ppermute | solution.py:340
  57.6 6.2 %collective-permute-start.22 = (bf16[32,1344]{1,0:T(8,128)(2,1)S(1)}, bf16[32,1344]{1,0:T(8,128)(2,1)S(1)}, u32[]{:S(2)}, u32[]{:S(2)}) collective-permute-start(bf16[32,1344]{1,0:T(8,128)(2,1)S(1)} %get-tuple-element.96), channel_id=1, source_target_pairs={{0,2},{1,3},{2,0},{3,1},{4,6},{5,7},{6,4},{7,5},{8,10},{9,11},{10,... | collective-permute-start | bytes 258056 | tf_op jit(solution)/shard_map/ppermute | solution.py:330
  59.1 5.6 %collective-permute-start.21 = (bf16[32,1344]{1,0:T(8,128)(2,1)S(1)}, bf16[32,1344]{1,0:T(8,128)(2,1)S(1)}, u32[]{:S(2)}, u32[]{:S(2)}) collective-permute-start(bf16[32,1344]{1,0:T(8,128)(2,1)S(1)} %sum.5), channel_id=1, source_target_pairs={{0,4},{1,5},{2,6},{3,7},{4,0},{5,1},{6,2},{7,3},{8,12},{9,13},{10,... | collective-permute-start | bytes 258056 | tf_op jit(solution)/shard_map/ppermute | solution.py:340

commit v10 on v9

--- a/solution.py
+++ b/solution.py
@@ -461,14 +461,16 @@
     back_near = through_experts(near, [1] * head_size)
     back_near, far = lax.optimization_barrier((back_near, far))
     back_far = [through_experts(members, [1] * head_size) for members in far]
-    totals = []
-    for k in slots:
-        got = [swap(pieces[k], "exp", 2 * d) for d, pieces in enumerate(back_far, 1)]
-        totals.append(
-            call(sum_kernel, "sum", struct((rows, model), BF16), [(VMEM, v) for v in (back_near[k], *got)])
-        )
-    totals[-2], mine = lax.optimization_barrier((totals[-2], [pieces[-1] for pieces in back_far]))
-    arrived = [swap_slot(total, k) for k, total in enumerate(totals)]
+    arrived = [swap_slot(back_near[0], 0)]
+    got = {k: [swap(pieces[k], "exp", 2 * d) for d, pieces in enumerate(back_far, 1)] for k in slots[1:]}
+    arrived, got[1] = lax.optimization_barrier((arrived, got[1]))
+    arrived += [swap_slot(pieces[0], 0, d) for d, pieces in enumerate(back_far, 1)]
+    mine = [pieces[-1] for pieces in back_far]
+    for k in slots[1:]:
+        total = call(sum_kernel, "sum", struct((rows, model), BF16), [(VMEM, v) for v in (back_near[k], *got[k])])
+        if k == 1:
+            total, mine = lax.optimization_barrier((total, mine))
+        arrived.append(swap_slot(total, k))
     arrived += [swap(piece, "exp", 2 * d) for d, piece in enumerate(mine, 1)]
     return call(
         last_kernel,

time: 65.7 us -> 64.9 us (0.988)
    ppermute x13 -> x12, starting transfers between devices: 14.2 us -> 12.4 us  [swap(): return lax.ppermute(value, axis, [(i, i ^ mask) for i in range(size)])]
    ppermute x10 -> x11, starting transfers between devices: 14.9 us -> 16.6 us  [swap_slot(): return lax.ppermute(value, ('head', 'exp'), pairs)]
    ppermute x13 -> x12, waiting for transfers between devices: 6.91 us -> 6.16 us  [swap(): return lax.ppermute(value, axis, [(i, i ^ mask) for i in range(size)])]
    ppermute x10 -> x11, waiting for transfers between devices: 10.6 us -> 10.8 us  [swap_slot(): return lax.ppermute(value, ('head', 'exp'), pairs)]
    pallas_call x16 -> x15, Pallas kernels: 17.3 us -> 17.3 us  [call(): pl.pallas_call(kernel, out_shape=jax.tree.map(lambda out: pltpu.VMEM(out....]
  transfers between devices with their start and end apart: 23 -> 23, of which waited for: 13 -> 12; matrix products, arithmetic and copies ran while one was open for 2% -> 2% of each run, Pallas kernels for 17% -> 21%
where the time goes in v10:
time: 64.9 us; the launch traced here: 64.6 us
  starting transfers between devices  28.9 us (45%)
  Pallas kernels  17.3 us (27%)
  waiting for transfers between devices  16.9 us (26%)
  local copies, waits for them, and re-layouts  1.29 us (2%)
    pallas_call x15, Pallas kernels, call(): pl.pallas_call(kernel, out_shape=jax.tree.map(lambda out: pltpu.VMEM(out....  17.3 us
    ppermute x11, starting transfers between devices, swap_slot(): return lax.ppermute(value, ('head', 'exp'), pairs)  16.6 us
    ppermute x12, starting transfers between devices, swap(): return lax.ppermute(value, axis, [(i, i ^ mask) for i in range(size)])  12.4 us
    ppermute x11, waiting for transfers between devices, swap_slot(): return lax.ppermute(value, ('head', 'exp'), pairs)  10.8 us
    ppermute x12, waiting for transfers between devices, swap(): return lax.ppermute(value, axis, [(i, i ^ mask) for i in range(size)])  6.16 us
  transfers between devices with their start and end apart: 23, of which 12 were waited for; matrix products, arithmetic and copies ran while one was open for 2% of the time, Pallas kernels for 21%

profile of v10, /device:TPU:0, one launch (start us, length us, event | category | flops | bytes accessed | tf_op | source)
XLA Modules:
  0.0 64.6 jit_solution(5387248791332144508)
XLA Ops:
  0.0 1.8 %state.1 = (bf16[4,144,128]{2,1,0:T(8,128)(2,1)S(1)}, bf16[4,144,128]{2,1,0:T(8,128)(2,1)S(1)}) custom-call(bf16[128,1024]{1,0:T(8,128)(2,1)} %x_hbm.3, bf16[128,256]{1,0:T(8,128)(2,1)} %b_hbm.3, f32[16,128]{1,0:T(8,128)} %bitcast.11, f32[1,16]{1,0:T(1,128)} %bitcast.16), custom_call_target="tpu_custom_call" | custom-call | tf_op jit(solution)/shard_map/state/pallas_call | solution.py:29
  1.8 0.5 collective-permute-start
  2.4 1.0 %collective-permute-done.got_ref = bf16[4,144,128]{2,1,0:T(8,128)(2,1)S(1)} collective-permute-done((bf16[4,144,128]{2,1,0:T(8,128)(2,1)S(1)}, bf16[4,144,128]{2,1,0:T(8,128)(2,1)S(1)}, u32[]{:S(2)}, u32[]{:S(2)}) %collective-permute-start) | collective-permute-done | bytes 147488 | tf_op jit(solution)/shard_map/ppermute | solution.py:330
  3.4 0.1 chip_state.1.rest_0_
  3.5 0.4 collective-permute-start.1
  3.9 0.1 collective-permute-start.2
  4.0 2.9 %collective-permute-start.3 = (bf16[4,144,128]{2,1,0:T(8,128)(2,1)S(1)}, bf16[4,144,128]{2,1,0:T(8,128)(2,1)S(1)}, u32[]{:S(2)}, u32[]{:S(2)}) collective-permute-start(bf16[4,144,128]{2,1,0:T(8,128)(2,1)S(1)} %chip_state.1.rest_0_), channel_id=1, source_target_pairs={{0,2},{1,3},{2,0},{3,1},{4,6},{5,7},{6,4},{7,5},{8,10},{9,11},{10,... | collective-permute-start | bytes 442376 | tf_op jit(solution)/shard_map/ppermute | solution.py:330
  6.9 2.4 %inside.1 = (f32[128,1024]{1,0:T(8,128)S(1)}, f32[128,1024]{1,0:T(8,128)S(1)}, bf16[128,256]{1,0:T(8,128)(2,1)S(1)}) custom-call(bf16[128,1024]{1,0:T(8,128)(2,1)} %x_hbm.3, bf16[128,1024]{1,0:T(8,128)(2,1)} %z_hbm.1, bf16[128,256]{1,0:T(8,128)(2,1)} %b_hbm.3, bf16[128,256]{1,0:T(8,128)(2,1)} %c_hbm.1, f32[16,128]{1,0:T(8,128)} %bitcast.12, ...), custom_call_target="tpu_custom_call" | custom-call | tf_op jit(solution)/shard_map/inside/pallas_call | solution.py:29
  9.4 1.7 %collective-permute-done.3.rest_1_ = bf16[4,144,128]{2,1,0:T(8,128)(2,1)S(1)} collective-permute-done((bf16[4,144,128]{2,1,0:T(8,128)(2,1)S(1)}, bf16[4,144,128]{2,1,0:T(8,128)(2,1)S(1)}, u32[]{:S(2)}, u32[]{:S(2)}) %collective-permute-start.3) | collective-permute-done | bytes 147488 | tf_op jit(solution)/shard_map/ppermute | solution.py:330
  11.1 0.1 span.1.rest_2_
  11.2 1.8 %collective-permute-start.4 = (bf16[4,144,128]{2,1,0:T(8,128)(2,1)S(1)}, bf16[4,144,128]{2,1,0:T(8,128)(2,1)S(1)}, u32[]{:S(2)}, u32[]{:S(2)}) collective-permute-start(bf16[4,144,128]{2,1,0:T(8,128)(2,1)S(1)} %span.1.rest_2_), channel_id=1, source_target_pairs={{0,16},{16,0},{1,17},{17,1},{2,18},{18,2},{3,19},{19,3},{4,20},{20... | collective-permute-start | bytes 442376 | tf_op jit(solution)/shard_map/ppermute | solution.py:330
  12.9 1.3 %broadcast_in_dim.14.gain_hbm = f32[1,1344]{1,0:T(1,128)} reshape(f32[1344]{0:T(1024)} %param.27) | data formatting | bytes 10752 | tf_op jit(solution)/shard_map/broadcast_in_dim | solution.py:385
  14.2 1.9 %prep.1 = (bf16[32,128]{1,0:T(8,128)(2,1)S(1)}, bf16[1,32,1344]{2,1,0:T(8,128)(2,1)S(1)}, f32[1,1344]{1,0:T(1,128)S(1)}, f32[1,1024]{1,0:T(1,128)S(1)}, bf16[1344,1024]{1,0:T(8,128)(2,1)S(1)}) custom-call(bf16[1,32,1344]{2,1,0:T(8,128)(2,1)} %resid_hbm.1, s32[6,1,32]{2,1,0:T(1,128)} %bitcast.14, f32[6,1,32]{2,1,0:T(1,128)} %bitcast.15, ...), custom_call_target="tpu_custom_call" | custom-call | tf_op jit(solution)/shard_map/prep/pallas_call | solution.py:29
  16.2 0.4 collective-permute-done.4.rest_3_
  16.6 0.3 before.1
  16.9 0.1 collective-permute-start.5
  17.0 0.8 %first_half.1.first_ref = f32[128,1344]{1,0:T(8,128)S(1)} custom-call(f32[128,1024]{1,0:T(8,128)S(1)} %get-tuple-element.57.local_ref, f32[128,1024]{1,0:T(8,128)S(1)} %get-tuple-element.58.grown_ref, bf16[128,256]{1,0:T(8,128)(2,1)S(1)} %get-tuple-element.59.after_ref.c_ref, f32[1,1024]{1,0:T(1,128)S(1)} %get-tuple-element.60.norm_ref, ...), custom_call_target="tpu_custom_call" | custom-call | tf_op jit(solution)/shard_map/first_half/pallas_call | solution.py:29
  17.8 0.5 collective-permute-done.5.got_ref
  18.3 0.9 %mixed.1 = (bf16[32,1344]{1,0:T(8,128)(2,1)S(1)}, bf16[32,1344]{1,0:T(8,128)(2,1)S(1)}, bf16[32,1344]{1,0:T(8,128)(2,1)S(1)}, bf16[32,1344]{1,0:T(8,128)(2,1)S(1)}) custom-call(bf16[1,928,1344]{2,1,0:T(8,128)(2,1)S(1)} %collective-permute-done.1.after_up.other_up_ref, bf16[1,928,1344]{2,1,0:T(8,128)(2,1)S(1)} %collective-permute-done.2.after_down.other_down_ref, ...), custom_call_target="tpu_custom_call" | custom-call | tf_op jit(solution)/shard_map/mixed/pallas_call | solution.py:29
  19.2 3.6 %collective-permute-start.6 = (bf16[32,1344]{1,0:T(8,128)(2,1)S(1)}, bf16[32,1344]{1,0:T(8,128)(2,1)S(1)}, u32[]{:S(2)}, u32[]{:S(2)}) collective-permute-start(bf16[32,1344]{1,0:T(8,128)(2,1)S(1)} %get-tuple-element.70), channel_id=1, source_target_pairs={{0,12},{1,9},{2,14},{3,11},{4,8},{5,13},{6,10},{7,15},{8,4},{9,1},... | collective-permute-start | bytes 258056 | tf_op jit(solution)/shard_map/ppermute | solution.py:340
  22.8 0.8 %collective-permute-start.8 = (bf16[32,1344]{1,0:T(8,128)(2,1)S(1)}, bf16[32,1344]{1,0:T(8,128)(2,1)S(1)}, u32[]{:S(2)}, u32[]{:S(2)}) collective-permute-start(bf16[32,1344]{1,0:T(8,128)(2,1)S(1)} %get-tuple-element.72), channel_id=1, source_target_pairs={{0,4},{1,5},{2,6},{3,7},{4,0},{5,1},{6,2},{7,3},{8,12},{9,13},{10,... | collective-permute-start | bytes 258056 | tf_op jit(solution)/shard_map/ppermute | solution.py:340
  23.6 2.5 %weights.1 = (bf16[1,928,1344]{2,1,0:T(8,128)(2,1)S(1)}, bf16[1,928,1344]{2,1,0:T(8,128)(2,1)S(1)}) custom-call(bf16[32,1344]{1,0:T(8,128)(2,1)S(1)} %get-tuple-element.66.after_ref.rest_0_, bf16[1,928,1344]{2,1,0:T(8,128)(2,1)} %bitcast.10, bf16[1,928,1344]{2,1,0:T(8,128)(2,1)} %down_hbm.1), custom_call_target="tpu_custom_call" | custom-call | tf_op jit(solution)/shard_map/weights/pallas_call | solution.py:29
  26.2 4.4 %collective-permute-done.7.rest_2_ = bf16[32,1344]{1,0:T(8,128)(2,1)S(1)} collective-permute-done((bf16[32,1344]{1,0:T(8,128)(2,1)S(1)}, bf16[32,1344]{1,0:T(8,128)(2,1)S(1)}, u32[]{:S(2)}, u32[]{:S(2)}) %collective-permute-start.7) | collective-permute-done | bytes 86048 | tf_op jit(solution)/shard_map/ppermute | solution.py:340
  30.6 0.2 rows.1
  30.8 0.5 collective-permute-start.10
  31.3 2.9 %collective-permute-start.9 = (bf16[32,1408]{1,0:T(8,128)(2,1)S(1)}, bf16[32,1408]{1,0:T(8,128)(2,1)S(1)}, u32[]{:S(2)}, u32[]{:S(2)}) collective-permute-start(bf16[32,1408]{1,0:T(8,128)(2,1)S(1)} %get-tuple-element.79.rest_3_), channel_id=1, source_target_pairs={{0,12},{1,9},{2,14},{3,11},{4,8},{5,13},{6,10},{7,15},{8,4},{9,1},... | collective-permute-start | bytes 270344 | tf_op jit(solution)/shard_map/ppermute | solution.py:340
  34.2 1.5 %collective-permute-start.12 = (bf16[32,1408]{1,0:T(8,128)(2,1)S(1)}, bf16[32,1408]{1,0:T(8,128)(2,1)S(1)}, u32[]{:S(2)}, u32[]{:S(2)}) collective-permute-start(bf16[32,1408]{1,0:T(8,128)(2,1)S(1)} %get-tuple-element.79.rest_3_), channel_id=1, source_target_pairs={{0,2},{1,3},{2,0},{3,1},{4,6},{5,7},{6,4},{7,5},{8,10},{9,11},{10,... | collective-permute-start | bytes 270344 | tf_op jit(solution)/shard_map/ppermute | solution.py:330
  35.7 0.5 collective-permute-start.11
  36.2 1.5 %collective-permute-start.15 = (bf16[32,1408]{1,0:T(8,128)(2,1)S(1)}, bf16[32,1408]{1,0:T(8,128)(2,1)S(1)}, u32[]{:S(2)}, u32[]{:S(2)}) collective-permute-start(bf16[32,1408]{1,0:T(8,128)(2,1)S(1)} %get-tuple-element.79.rest_3_), channel_id=1, source_target_pairs={{0,6},{1,7},{2,4},{3,5},{4,2},{5,3},{6,0},{7,1},{8,14},{9,15},{10,... | collective-permute-start | bytes 270344 | tf_op jit(solution)/shard_map/ppermute | solution.py:340
  37.6 2.4 %collective-permute-done.10.rest_1_ = bf16[32,1408]{1,0:T(8,128)(2,1)S(1)} collective-permute-done((bf16[32,1408]{1,0:T(8,128)(2,1)S(1)}, bf16[32,1408]{1,0:T(8,128)(2,1)S(1)}, u32[]{:S(2)}, u32[]{:S(2)}) %collective-permute-start.10) | collective-permute-done | bytes 90144 | tf_op jit(solution)/shard_map/ppermute | solution.py:340
  40.0 1.5 %collective-permute-start.14 = (bf16[32,1408]{1,0:T(8,128)(2,1)S(1)}, bf16[32,1408]{1,0:T(8,128)(2,1)S(1)}, u32[]{:S(2)}, u32[]{:S(2)}) collective-permute-start(bf16[32,1408]{1,0:T(8,128)(2,1)S(1)} %collective-permute-done.10.rest_1_), channel_id=1, source_target_pairs={{0,2},{1,3},{2,0},{3,1},{4,6},{5,7},{6,4},{7,5},{8,10},{9,11},{10,... | collective-permute-start | bytes 270344 | tf_op jit(solution)/shard_map/ppermute | solution.py:330
  41.5 0.5 collective-permute-start.13
  42.0 0.2 collective-permute-done.11.rest_2_
  42.3 2.7 %experts.2 = (bf16[32,1344]{1,0:T(8,128)(2,1)S(1)}, bf16[32,1344]{1,0:T(8,128)(2,1)S(1)}, bf16[32,1344]{1,0:T(8,128)(2,1)S(1)}, bf16[32,1344]{1,0:T(8,128)(2,1)S(1)}) custom-call(bf16[1,928,1344]{2,1,0:T(8,128)(2,1)S(1)} %get-tuple-element.67.after_ref.up_ref, bf16[1,928,1344]{2,1,0:T(8,128)(2,1)S(1)} %get-tuple-element.74.down_ref, ...), custom_call_target="tpu_custom_call" | custom-call | tf_op jit(solution)/shard_map/experts/pallas_call | solution.py:29
  45.0 0.3 collective-permute-done.14.rest_1_
  45.3 1.0 %collective-permute-done.13.rest_0_ = bf16[32,1408]{1,0:T(8,128)(2,1)S(1)} collective-permute-done((bf16[32,1408]{1,0:T(8,128)(2,1)S(1)}, bf16[32,1408]{1,0:T(8,128)(2,1)S(1)}, u32[]{:S(2)}, u32[]{:S(2)}) %collective-permute-start.13) | collective-permute-done | bytes 90144 | tf_op jit(solution)/shard_map/ppermute | solution.py:330
  46.3 3.0 %collective-permute-start.16 = (bf16[32,1344]{1,0:T(8,128)(2,1)S(1)}, bf16[32,1344]{1,0:T(8,128)(2,1)S(1)}, u32[]{:S(2)}, u32[]{:S(2)}) collective-permute-start(bf16[32,1344]{1,0:T(8,128)(2,1)S(1)} %get-tuple-element.86), channel_id=1, source_target_pairs={{0,12},{1,9},{2,14},{3,11},{4,8},{5,13},{6,10},{7,15},{8,4},{9,1},... | collective-permute-start | bytes 258056 | tf_op jit(solution)/shard_map/ppermute | solution.py:340
  49.2 2.7 %experts.3 = (bf16[32,1344]{1,0:T(8,128)(2,1)S(1)}, bf16[32,1344]{1,0:T(8,128)(2,1)S(1)}, bf16[32,1344]{1,0:T(8,128)(2,1)S(1)}, bf16[32,1344]{1,0:T(8,128)(2,1)S(1)}) custom-call(bf16[1,928,1344]{2,1,0:T(8,128)(2,1)S(1)} %get-tuple-element.67.after_ref.up_ref, bf16[1,928,1344]{2,1,0:T(8,128)(2,1)S(1)} %get-tuple-element.74.down_ref, ...), custom_call_target="tpu_custom_call" | custom-call | tf_op jit(solution)/shard_map/experts/pallas_call | solution.py:29
  52.0 1.3 %collective-permute-start.17 = (bf16[32,1344]{1,0:T(8,128)(2,1)S(1)}, bf16[32,1344]{1,0:T(8,128)(2,1)S(1)}, u32[]{:S(2)}, u32[]{:S(2)}) collective-permute-start(bf16[32,1344]{1,0:T(8,128)(2,1)S(1)} %get-tuple-element.91), channel_id=1, source_target_pairs={{0,2},{1,3},{2,0},{3,1},{4,6},{5,7},{6,4},{7,5},{8,10},{9,11},{10,... | collective-permute-start | bytes 258056 | tf_op jit(solution)/shard_map/ppermute | solution.py:330
  53.3 0.8 %collective-permute-start.20 = (bf16[32,1344]{1,0:T(8,128)(2,1)S(1)}, bf16[32,1344]{1,0:T(8,128)(2,1)S(1)}, u32[]{:S(2)}, u32[]{:S(2)}) collective-permute-start(bf16[32,1344]{1,0:T(8,128)(2,1)S(1)} %get-tuple-element.99), channel_id=1, source_target_pairs={{0,2},{1,3},{2,0},{3,1},{4,6},{5,7},{6,4},{7,5},{8,10},{9,11},{10,... | collective-permute-start | bytes 258056 | tf_op jit(solution)/shard_map/ppermute | solution.py:330
  54.1 1.6 %collective-permute-start.18 = (bf16[32,1344]{1,0:T(8,128)(2,1)S(1)}, bf16[32,1344]{1,0:T(8,128)(2,1)S(1)}, u32[]{:S(2)}, u32[]{:S(2)}) collective-permute-start(bf16[32,1344]{1,0:T(8,128)(2,1)S(1)} %get-tuple-element.93), channel_id=1, source_target_pairs={{0,14},{1,11},{2,12},{3,9},{4,10},{5,15},{6,8},{7,13},{8,6},{9,3},... | collective-permute-start | bytes 258056 | tf_op jit(solution)/shard_map/ppermute | solution.py:340
  55.7 1.3 %collective-permute-done.17.refs_1_ = bf16[32,1344]{1,0:T(8,128)(2,1)S(1)} collective-permute-done((bf16[32,1344]{1,0:T(8,128)(2,1)S(1)}, bf16[32,1344]{1,0:T(8,128)(2,1)S(1)}, u32[]{:S(2)}, u32[]{:S(2)}) %collective-permute-start.17) | collective-permute-done | bytes 86048 | tf_op jit(solution)/shard_map/ppermute | solution.py:330
  57.0 0.1 collective-permute-start.19
  57.0 0.9 %collective-permute-start.22 = (bf16[32,1344]{1,0:T(8,128)(2,1)S(1)}, bf16[32,1344]{1,0:T(8,128)(2,1)S(1)}, u32[]{:S(2)}, u32[]{:S(2)}) collective-permute-start(bf16[32,1344]{1,0:T(8,128)(2,1)S(1)} %get-tuple-element.100), channel_id=1, source_target_pairs={{0,2},{1,3},{2,0},{3,1},{4,6},{5,7},{6,4},{7,5},{8,10},{9,11},{10,... | collective-permute-start | bytes 258056 | tf_op jit(solution)/shard_map/ppermute | solution.py:330
  58.0 2.1 %collective-permute-start.21 = (bf16[32,1344]{1,0:T(8,128)(2,1)S(1)}, bf16[32,1344]{1,0:T(8,128)(2,1)S(1)}, u32[]{:S(2)}, u32[]{:S(2)}) collective-permute-start(bf16[32,1344]{1,0:T(8,128)(2,1)S(1)} %sum.3), channel_id=1, source_target_pairs={{0,4},{1,5},{2,6},{3,7},{4,0},{5,1},{6,2},{7,3},{8,12},{9,13},{10,... | collective-permute-start | bytes 258056 | tf_op jit(solution)/shard_map/ppermute | solution.py:340
  60.1 1.9 %collective-permute-done.18.rest_2_ = bf16[32,1344]{1,0:T(8,128)(2,1)S(1)} collective-permute-done((bf16[32,1344]{1,0:T(8,128)(2,1)S(1)}, bf16[32,1344]{1,0:T(8,128)(2,1)S(1)}, u32[]{:S(2)}, u32[]{:S(2)}) %collective-permute-start.18) | collective-permute-done | bytes 86048 | tf_op jit(solution)/shard_map/ppermute | solution.py:340
  62.0 1.8 %collective-permute-done.19.rest_3_ = bf16[32,1344]{1,0:T(8,128)(2,1)S(1)} collective-permute-done((bf16[32,1344]{1,0:T(8,128)(2,1)S(1)}, bf16[32,1344]{1,0:T(8,128)(2,1)S(1)}, u32[]{:S(2)}, u32[]{:S(2)}) %collective-permute-start.19) | collective-permute-done | bytes 86048 | tf_op jit(solution)/shard_map/ppermute | solution.py:340
  63.9 0.7 %last.1 = bf16[1,32,1344]{2,1,0:T(8,128)(2,1)} custom-call(bf16[32,1344]{1,0:T(8,128)(2,1)S(1)} %get-tuple-element.73.hidden_ref, bf16[32,1344]{1,0:T(8,128)(2,1)S(1)} %get-tuple-element.85.rest_0_, bf16[32,1344]{1,0:T(8,128)(2,1)S(1)} %collective-permute-done.16.rest_1_, bf16[32,1344]{1,0:T(8,128)(2,1)S(1)} %collective-permute-done.18.rest_2_, ...), custom_call_target="tpu_custom_call" | custom-call | tf_op jit(solution)/shard_map/last/pallas_call | solution.py:29
  (14 shorter events, 0.1 us)
Async XLA Ops:
  1.8 1.5 %collective-permute-start = (bf16[4,144,128]{2,1,0:T(8,128)(2,1)S(1)}, bf16[4,144,128]{2,1,0:T(8,128)(2,1)S(1)}, u32[]{:S(2)}, u32[]{:S(2)}) collective-permute-start(bf16[4,144,128]{2,1,0:T(8,128)(2,1)S(1)} %get-tuple-element.54), channel_id=1, source_target_pairs={{0,1},{1,0},{2,3},{3,2},{4,5},{5,4},{6,7},{7,6},{8,9},{9,8},{10,11... | collective-permute-start | bytes 442376 | tf_op jit(solution)/shard_map/ppermute | solution.py:330
  3.5 14.9 %collective-permute-start.1 = (bf16[1,928,1344]{2,1,0:T(8,128)(2,1)}, bf16[1,928,1344]{2,1,0:T(8,128)(2,1)S(1)}, u32[]{:S(2)}, u32[]{:S(2)}) collective-permute-start(bf16[1,928,1344]{2,1,0:T(8,128)(2,1)} %bitcast.9), channel_id=1, source_target_pairs={{0,1},{1,0},{2,3},{3,2},{4,5},{5,4},{6,7},{7,6},{8,9},{9,8},{10,11... | collective-permute-start | bytes 7483400 | tf_op jit(solution)/shard_map/ppermute | solution.py:330
  3.9 14.4 %collective-permute-start.2 = (bf16[1,928,1344]{2,1,0:T(8,128)(2,1)}, bf16[1,928,1344]{2,1,0:T(8,128)(2,1)S(1)}, u32[]{:S(2)}, u32[]{:S(2)}) collective-permute-start(bf16[1,928,1344]{2,1,0:T(8,128)(2,1)} %down_hbm.1), channel_id=1, source_target_pairs={{0,1},{1,0},{2,3},{3,2},{4,5},{5,4},{6,7},{7,6},{8,9},{9,8},{10,11... | collective-permute-start | bytes 7483400 | tf_op jit(solution)/shard_map/ppermute | solution.py:330
  4.0 7.0 %collective-permute-start.3 = (bf16[4,144,128]{2,1,0:T(8,128)(2,1)S(1)}, bf16[4,144,128]{2,1,0:T(8,128)(2,1)S(1)}, u32[]{:S(2)}, u32[]{:S(2)}) collective-permute-start(bf16[4,144,128]{2,1,0:T(8,128)(2,1)S(1)} %chip_state.1.rest_0_), channel_id=1, source_target_pairs={{0,2},{1,3},{2,0},{3,1},{4,6},{5,7},{6,4},{7,5},{8,10},{9,11},{10,... | collective-permute-start | bytes 442376 | tf_op jit(solution)/shard_map/ppermute | solution.py:330
  11.2 5.5 %collective-permute-start.4 = (bf16[4,144,128]{2,1,0:T(8,128)(2,1)S(1)}, bf16[4,144,128]{2,1,0:T(8,128)(2,1)S(1)}, u32[]{:S(2)}, u32[]{:S(2)}) collective-permute-start(bf16[4,144,128]{2,1,0:T(8,128)(2,1)S(1)} %span.1.rest_2_), channel_id=1, source_target_pairs={{0,16},{16,0},{1,17},{17,1},{2,18},{18,2},{3,19},{19,3},{4,20},{20... | collective-permute-start | bytes 442376 | tf_op jit(solution)/shard_map/ppermute | solution.py:330
  16.9 1.4 %collective-permute-start.5 = (bf16[4,128,128]{2,1,0:T(8,128)(2,1)S(1)}, bf16[4,128,128]{2,1,0:T(8,128)(2,1)S(1)}, u32[]{:S(2)}, u32[]{:S(2)}) collective-permute-start(bf16[4,128,128]{2,1,0:T(8,128)(2,1)S(1)} %get-tuple-element.64), channel_id=1, source_target_pairs={{0,1},{1,0},{2,3},{3,2},{4,5},{5,4},{6,7},{7,6},{8,9},{9,8},{10,11... | collective-permute-start | bytes 393224 | tf_op jit(solution)/shard_map/ppermute | solution.py:330
  19.2 7.0 %collective-permute-start.6 = (bf16[32,1344]{1,0:T(8,128)(2,1)S(1)}, bf16[32,1344]{1,0:T(8,128)(2,1)S(1)}, u32[]{:S(2)}, u32[]{:S(2)}) collective-permute-start(bf16[32,1344]{1,0:T(8,128)(2,1)S(1)} %get-tuple-element.70), channel_id=1, source_target_pairs={{0,12},{1,9},{2,14},{3,11},{4,8},{5,13},{6,10},{7,15},{8,4},{9,1},... | collective-permute-start | bytes 258056 | tf_op jit(solution)/shard_map/ppermute | solution.py:340
  22.8 7.8 %collective-permute-start.7 = (bf16[32,1344]{1,0:T(8,128)(2,1)S(1)}, bf16[32,1344]{1,0:T(8,128)(2,1)S(1)}, u32[]{:S(2)}, u32[]{:S(2)}) collective-permute-start(bf16[32,1344]{1,0:T(8,128)(2,1)S(1)} %get-tuple-element.71), channel_id=1, source_target_pairs={{0,8},{1,13},{2,10},{3,15},{4,12},{5,9},{6,14},{7,11},{8,0},{9,5},... | collective-permute-start | bytes 258056 | tf_op jit(solution)/shard_map/ppermute | solution.py:340
  22.8 7.8 %collective-permute-start.8 = (bf16[32,1344]{1,0:T(8,128)(2,1)S(1)}, bf16[32,1344]{1,0:T(8,128)(2,1)S(1)}, u32[]{:S(2)}, u32[]{:S(2)}) collective-permute-start(bf16[32,1344]{1,0:T(8,128)(2,1)S(1)} %get-tuple-element.72), channel_id=1, source_target_pairs={{0,4},{1,5},{2,6},{3,7},{4,0},{5,1},{6,2},{7,3},{8,12},{9,13},{10,... | collective-permute-start | bytes 258056 | tf_op jit(solution)/shard_map/ppermute | solution.py:340
  30.8 9.2 %collective-permute-start.10 = (bf16[32,1408]{1,0:T(8,128)(2,1)S(1)}, bf16[32,1408]{1,0:T(8,128)(2,1)S(1)}, u32[]{:S(2)}, u32[]{:S(2)}) collective-permute-start(bf16[32,1408]{1,0:T(8,128)(2,1)S(1)} %get-tuple-element.79.rest_3_), channel_id=1, source_target_pairs={{0,8},{1,13},{2,10},{3,15},{4,12},{5,9},{6,14},{7,11},{8,0},{9,5},... | collective-permute-start | bytes 270344 | tf_op jit(solution)/shard_map/ppermute | solution.py:340
  31.3 10.3 %collective-permute-start.9 = (bf16[32,1408]{1,0:T(8,128)(2,1)S(1)}, bf16[32,1408]{1,0:T(8,128)(2,1)S(1)}, u32[]{:S(2)}, u32[]{:S(2)}) collective-permute-start(bf16[32,1408]{1,0:T(8,128)(2,1)S(1)} %get-tuple-element.79.rest_3_), channel_id=1, source_target_pairs={{0,12},{1,9},{2,14},{3,11},{4,8},{5,13},{6,10},{7,15},{8,4},{9,1},... | collective-permute-start | bytes 270344 | tf_op jit(solution)/shard_map/ppermute | solution.py:340
  34.2 7.9 %collective-permute-start.12 = (bf16[32,1408]{1,0:T(8,128)(2,1)S(1)}, bf16[32,1408]{1,0:T(8,128)(2,1)S(1)}, u32[]{:S(2)}, u32[]{:S(2)}) collective-permute-start(bf16[32,1408]{1,0:T(8,128)(2,1)S(1)} %get-tuple-element.79.rest_3_), channel_id=1, source_target_pairs={{0,2},{1,3},{2,0},{3,1},{4,6},{5,7},{6,4},{7,5},{8,10},{9,11},{10,... | collective-permute-start | bytes 270344 | tf_op jit(solution)/shard_map/ppermute | solution.py:330
  35.7 6.6 %collective-permute-start.11 = (bf16[32,1408]{1,0:T(8,128)(2,1)S(1)}, bf16[32,1408]{1,0:T(8,128)(2,1)S(1)}, u32[]{:S(2)}, u32[]{:S(2)}) collective-permute-start(bf16[32,1408]{1,0:T(8,128)(2,1)S(1)} %get-tuple-element.79.rest_3_), channel_id=1, source_target_pairs={{0,4},{1,5},{2,6},{3,7},{4,0},{5,1},{6,2},{7,3},{8,12},{9,13},{10,... | collective-permute-start | bytes 270344 | tf_op jit(solution)/shard_map/ppermute | solution.py:340
  36.2 8.8 %collective-permute-start.15 = (bf16[32,1408]{1,0:T(8,128)(2,1)S(1)}, bf16[32,1408]{1,0:T(8,128)(2,1)S(1)}, u32[]{:S(2)}, u32[]{:S(2)}) collective-permute-start(bf16[32,1408]{1,0:T(8,128)(2,1)S(1)} %get-tuple-element.79.rest_3_), channel_id=1, source_target_pairs={{0,6},{1,7},{2,4},{3,5},{4,2},{5,3},{6,0},{7,1},{8,14},{9,15},{10,... | collective-permute-start | bytes 270344 | tf_op jit(solution)/shard_map/ppermute | solution.py:340
  40.0 5.3 %collective-permute-start.14 = (bf16[32,1408]{1,0:T(8,128)(2,1)S(1)}, bf16[32,1408]{1,0:T(8,128)(2,1)S(1)}, u32[]{:S(2)}, u32[]{:S(2)}) collective-permute-start(bf16[32,1408]{1,0:T(8,128)(2,1)S(1)} %collective-permute-done.10.rest_1_), channel_id=1, source_target_pairs={{0,2},{1,3},{2,0},{3,1},{4,6},{5,7},{6,4},{7,5},{8,10},{9,11},{10,... | collective-permute-start | bytes 270344 | tf_op jit(solution)/shard_map/ppermute | solution.py:330
  41.5 4.7 %collective-permute-start.13 = (bf16[32,1408]{1,0:T(8,128)(2,1)S(1)}, bf16[32,1408]{1,0:T(8,128)(2,1)S(1)}, u32[]{:S(2)}, u32[]{:S(2)}) collective-permute-start(bf16[32,1408]{1,0:T(8,128)(2,1)S(1)} %collective-permute-done.9.rest_0_), channel_id=1, source_target_pairs={{0,2},{1,3},{2,0},{3,1},{4,6},{5,7},{6,4},{7,5},{8,10},{9,11},{10,... | collective-permute-start | bytes 270344 | tf_op jit(solution)/shard_map/ppermute | solution.py:330
  46.3 9.4 %collective-permute-start.16 = (bf16[32,1344]{1,0:T(8,128)(2,1)S(1)}, bf16[32,1344]{1,0:T(8,128)(2,1)S(1)}, u32[]{:S(2)}, u32[]{:S(2)}) collective-permute-start(bf16[32,1344]{1,0:T(8,128)(2,1)S(1)} %get-tuple-element.86), channel_id=1, source_target_pairs={{0,12},{1,9},{2,14},{3,11},{4,8},{5,13},{6,10},{7,15},{8,4},{9,1},... | collective-permute-start | bytes 258056 | tf_op jit(solution)/shard_map/ppermute | solution.py:340
  52.0 5.0 %collective-permute-start.17 = (bf16[32,1344]{1,0:T(8,128)(2,1)S(1)}, bf16[32,1344]{1,0:T(8,128)(2,1)S(1)}, u32[]{:S(2)}, u32[]{:S(2)}) collective-permute-start(bf16[32,1344]{1,0:T(8,128)(2,1)S(1)} %get-tuple-element.91), channel_id=1, source_target_pairs={{0,2},{1,3},{2,0},{3,1},{4,6},{5,7},{6,4},{7,5},{8,10},{9,11},{10,... | collective-permute-start | bytes 258056 | tf_op jit(solution)/shard_map/ppermute | solution.py:330
  53.3 4.7 %collective-permute-start.20 = (bf16[32,1344]{1,0:T(8,128)(2,1)S(1)}, bf16[32,1344]{1,0:T(8,128)(2,1)S(1)}, u32[]{:S(2)}, u32[]{:S(2)}) collective-permute-start(bf16[32,1344]{1,0:T(8,128)(2,1)S(1)} %get-tuple-element.99), channel_id=1, source_target_pairs={{0,2},{1,3},{2,0},{3,1},{4,6},{5,7},{6,4},{7,5},{8,10},{9,11},{10,... | collective-permute-start | bytes 258056 | tf_op jit(solution)/shard_map/ppermute | solution.py:330
  54.1 8.0 %collective-permute-start.18 = (bf16[32,1344]{1,0:T(8,128)(2,1)S(1)}, bf16[32,1344]{1,0:T(8,128)(2,1)S(1)}, u32[]{:S(2)}, u32[]{:S(2)}) collective-permute-start(bf16[32,1344]{1,0:T(8,128)(2,1)S(1)} %get-tuple-element.93), channel_id=1, source_target_pairs={{0,14},{1,11},{2,12},{3,9},{4,10},{5,15},{6,8},{7,13},{8,6},{9,3},... | collective-permute-start | bytes 258056 | tf_op jit(solution)/shard_map/ppermute | solution.py:340
  57.0 6.9 %collective-permute-start.19 = (bf16[32,1344]{1,0:T(8,128)(2,1)S(1)}, bf16[32,1344]{1,0:T(8,128)(2,1)S(1)}, u32[]{:S(2)}, u32[]{:S(2)}) collective-permute-start(bf16[32,1344]{1,0:T(8,128)(2,1)S(1)} %sum.2), channel_id=1, source_target_pairs={{0,8},{1,13},{2,10},{3,15},{4,12},{5,9},{6,14},{7,11},{8,0},{9,5},... | collective-permute-start | bytes 258056 | tf_op jit(solution)/shard_map/ppermute | solution.py:340
  57.0 6.8 %collective-permute-start.22 = (bf16[32,1344]{1,0:T(8,128)(2,1)S(1)}, bf16[32,1344]{1,0:T(8,128)(2,1)S(1)}, u32[]{:S(2)}, u32[]{:S(2)}) collective-permute-start(bf16[32,1344]{1,0:T(8,128)(2,1)S(1)} %get-tuple-element.100), channel_id=1, source_target_pairs={{0,2},{1,3},{2,0},{3,1},{4,6},{5,7},{6,4},{7,5},{8,10},{9,11},{10,... | collective-permute-start | bytes 258056 | tf_op jit(solution)/shard_map/ppermute | solution.py:330
  58.0 5.9 %collective-permute-start.21 = (bf16[32,1344]{1,0:T(8,128)(2,1)S(1)}, bf16[32,1344]{1,0:T(8,128)(2,1)S(1)}, u32[]{:S(2)}, u32[]{:S(2)}) collective-permute-start(bf16[32,1344]{1,0:T(8,128)(2,1)S(1)} %sum.3), channel_id=1, source_target_pairs={{0,4},{1,5},{2,6},{3,7},{4,0},{5,1},{6,2},{7,3},{8,12},{9,13},{10,... | collective-permute-start | bytes 258056 | tf_op jit(solution)/shard_map/ppermute | solution.py:340

commit v11 on v9

--- a/solution.py
+++ b/solution.py
@@ -441,40 +441,36 @@
         [(ANY, up_held)] + [(VMEM, value) for value in (resid_held, gate_lanes, gain_held, *parts)],
     )
 
-    def through_experts(members, sizes):
+    def through_experts(members):
         return call(
             functools.partial(expert_kernel, experts, len(members)),
             "experts",
-            [struct((size * rows, model), BF16) for size in sizes],
+            [struct((rows, model), BF16)] * len(members),
             [(VMEM, value) for value in (up_held, down_held, other_up, other_down, *members)],
             megabytes=16,
         )
 
-    near = [swap_slot(own_rows, k) for k in slots]
-    far = [
-        [swap(near[k], "exp", 2 * d) for k in slots[:-1]]
-        + [swap_slot(own_rows, slots[-1], d), swap(own_rows, "exp", 2 * d)]
-        for d in range(1, chips)
-    ]
-    near, whole = lax.optimization_barrier((near + [own_rows], [members[-1] for members in far]))
-    far = [members[:-1] + [last] for members, last in zip(far, whole)]
-    back_near = through_experts(near, [1] * head_size)
-    back_near, far = lax.optimization_barrier((back_near, far))
-    back_far = [through_experts(members, [1] * head_size) for members in far]
-    totals = []
-    for k in slots:
-        got = [swap(pieces[k], "exp", 2 * d) for d, pieces in enumerate(back_far, 1)]
-        totals.append(
-            call(sum_kernel, "sum", struct((rows, model), BF16), [(VMEM, v) for v in (back_near[k], *got)])
-        )
-    totals[-2], mine = lax.optimization_barrier((totals[-2], [pieces[-1] for pieces in back_far]))
-    arrived = [swap_slot(total, k) for k, total in enumerate(totals)]
-    arrived += [swap(piece, "exp", 2 * d) for d, piece in enumerate(mine, 1)]
+    both = ("head", "exp")
+    group = [z * exp_size + 2 * d for z in (1, 0) for d in reversed(range(chips))][:-1]
+
+    def spread(block):
+        return [block] + [swap(block, both, mask) for mask in group]
+
+    sets = [spread(swap(own_rows, "head", high)) for high in range(2, head_size, 2)]
+    near = through_experts(spread(own_rows))
+    near, sets = lax.optimization_barrier((near, sets))
+    far = [through_experts(members) for members in sets]
+    arrived = []
+    for high, pieces in zip(range(2, head_size, 2), far):
+        got = [swap(piece, both, mask) for piece, mask in zip(pieces[1:], group)]
+        total = call(sum_kernel, "sum", struct((rows, model), BF16), [(VMEM, v) for v in (pieces[0], *got)])
+        arrived.append(swap(total, "head", high))
+    arrived += [swap(piece, both, mask) for piece, mask in zip(near[1:], group)]
     return call(
         last_kernel,
         "last",
         struct(resid.shape, BF16),
-        [(VMEM, value) for value in (hidden, back_near[-1], *arrived)],
+        [(VMEM, value) for value in (hidden, near[0], *arrived)],
         pinned=False,
     )
 

time: 65.7 us -> 64.7 us (0.985)
  starting transfers between devices: 29.2 us -> 27.9 us
    ppermute x10 -> x3, starting transfers between devices: 14.9 us -> 4.45 us  [swap_slot(): return lax.ppermute(value, ('head', 'exp'), pairs)]
    ppermute x13 -> x20, starting transfers between devices: 14.2 us -> 23.4 us  [swap(): return lax.ppermute(value, axis, [(i, i ^ mask) for i in range(size)])]
    ppermute x13 -> x20, waiting for transfers between devices: 6.91 us -> 13.5 us  [swap(): return lax.ppermute(value, axis, [(i, i ^ mask) for i in range(size)])]
    ppermute x10 -> x3, waiting for transfers between devices: 10.6 us -> 4.42 us  [swap_slot(): return lax.ppermute(value, ('head', 'exp'), pairs)]
    pallas_call x16 -> x14, Pallas kernels: 17.3 us -> 17.3 us  [call(): pl.pallas_call(kernel, out_shape=jax.tree.map(lambda out: pltpu.VMEM(out....]
  transfers between devices with their start and end apart: 23 -> 23, of which waited for: 13 -> 12; matrix products, arithmetic and copies ran while one was open for 2% -> 2% of each run, Pallas kernels for 17% -> 17%
where the time goes in v11:
time: 64.7 us; the launch traced here: 64.4 us
  starting transfers between devices  27.9 us (43%)
  waiting for transfers between devices  17.9 us (28%)
  Pallas kernels  17.3 us (27%)
  local copies, waits for them, and re-layouts  1.29 us (2%)
    ppermute x20, starting transfers between devices, swap(): return lax.ppermute(value, axis, [(i, i ^ mask) for i in range(size)])  23.4 us
    pallas_call x14, Pallas kernels, call(): pl.pallas_call(kernel, out_shape=jax.tree.map(lambda out: pltpu.VMEM(out....  17.3 us
    ppermute x20, waiting for transfers between devices, swap(): return lax.ppermute(value, axis, [(i, i ^ mask) for i in range(size)])  13.5 us
    ppermute x3, starting transfers between devices, swap_slot(): return lax.ppermute(value, ('head', 'exp'), pairs)  4.45 us
    ppermute x3, waiting for transfers between devices, swap_slot(): return lax.ppermute(value, ('head', 'exp'), pairs)  4.42 us
  transfers between devices with their start and end apart: 23, of which 12 were waited for; matrix products, arithmetic and copies ran while one was open for 2% of the time, Pallas kernels for 17%

profile of v11, /device:TPU:0, one launch (start us, length us, event | category | flops | bytes accessed | tf_op | source)
XLA Modules:
  0.0 64.4 jit_solution(16144938430966586173)
XLA Ops:
  0.0 1.8 %state.1 = (bf16[4,144,128]{2,1,0:T(8,128)(2,1)S(1)}, bf16[4,144,128]{2,1,0:T(8,128)(2,1)S(1)}) custom-call(bf16[128,1024]{1,0:T(8,128)(2,1)} %x_hbm.3, bf16[128,256]{1,0:T(8,128)(2,1)} %b_hbm.3, f32[16,128]{1,0:T(8,128)} %bitcast.11, f32[1,16]{1,0:T(1,128)} %bitcast.16), custom_call_target="tpu_custom_call" | custom-call | tf_op jit(solution)/shard_map/state/pallas_call | solution.py:29
  1.8 0.5 collective-permute-start
  2.4 1.0 %collective-permute-done.got_ref = bf16[4,144,128]{2,1,0:T(8,128)(2,1)S(1)} collective-permute-done((bf16[4,144,128]{2,1,0:T(8,128)(2,1)S(1)}, bf16[4,144,128]{2,1,0:T(8,128)(2,1)S(1)}, u32[]{:S(2)}, u32[]{:S(2)}) %collective-permute-start) | collective-permute-done | bytes 147488 | tf_op jit(solution)/shard_map/ppermute | solution.py:330
  3.4 0.1 chip_state.1.rest_0_
  3.5 0.4 collective-permute-start.1
  3.9 0.1 collective-permute-start.2
  4.0 2.9 %collective-permute-start.3 = (bf16[4,144,128]{2,1,0:T(8,128)(2,1)S(1)}, bf16[4,144,128]{2,1,0:T(8,128)(2,1)S(1)}, u32[]{:S(2)}, u32[]{:S(2)}) collective-permute-start(bf16[4,144,128]{2,1,0:T(8,128)(2,1)S(1)} %chip_state.1.rest_0_), channel_id=1, source_target_pairs={{0,2},{1,3},{2,0},{3,1},{4,6},{5,7},{6,4},{7,5},{8,10},{9,11},{10,... | collective-permute-start | bytes 442376 | tf_op jit(solution)/shard_map/ppermute | solution.py:330
  6.9 2.4 %inside.1 = (f32[128,1024]{1,0:T(8,128)S(1)}, f32[128,1024]{1,0:T(8,128)S(1)}, bf16[128,256]{1,0:T(8,128)(2,1)S(1)}) custom-call(bf16[128,1024]{1,0:T(8,128)(2,1)} %x_hbm.3, bf16[128,1024]{1,0:T(8,128)(2,1)} %z_hbm.1, bf16[128,256]{1,0:T(8,128)(2,1)} %b_hbm.3, bf16[128,256]{1,0:T(8,128)(2,1)} %c_hbm.1, f32[16,128]{1,0:T(8,128)} %bitcast.12, ...), custom_call_target="tpu_custom_call" | custom-call | tf_op jit(solution)/shard_map/inside/pallas_call | solution.py:29
  9.4 1.7 %collective-permute-done.3.rest_1_ = bf16[4,144,128]{2,1,0:T(8,128)(2,1)S(1)} collective-permute-done((bf16[4,144,128]{2,1,0:T(8,128)(2,1)S(1)}, bf16[4,144,128]{2,1,0:T(8,128)(2,1)S(1)}, u32[]{:S(2)}, u32[]{:S(2)}) %collective-permute-start.3) | collective-permute-done | bytes 147488 | tf_op jit(solution)/shard_map/ppermute | solution.py:330
  11.1 0.1 span.1.rest_2_
  11.2 1.8 %collective-permute-start.4 = (bf16[4,144,128]{2,1,0:T(8,128)(2,1)S(1)}, bf16[4,144,128]{2,1,0:T(8,128)(2,1)S(1)}, u32[]{:S(2)}, u32[]{:S(2)}) collective-permute-start(bf16[4,144,128]{2,1,0:T(8,128)(2,1)S(1)} %span.1.rest_2_), channel_id=1, source_target_pairs={{0,16},{16,0},{1,17},{17,1},{2,18},{18,2},{3,19},{19,3},{4,20},{20... | collective-permute-start | bytes 442376 | tf_op jit(solution)/shard_map/ppermute | solution.py:330
  12.9 1.3 %broadcast_in_dim.14.gain_hbm = f32[1,1344]{1,0:T(1,128)} reshape(f32[1344]{0:T(1024)} %param.27) | data formatting | bytes 10752 | tf_op jit(solution)/shard_map/broadcast_in_dim | solution.py:385
  14.2 1.9 %prep.1 = (bf16[32,128]{1,0:T(8,128)(2,1)S(1)}, bf16[1,32,1344]{2,1,0:T(8,128)(2,1)S(1)}, f32[1,1344]{1,0:T(1,128)S(1)}, f32[1,1024]{1,0:T(1,128)S(1)}, bf16[1344,1024]{1,0:T(8,128)(2,1)S(1)}) custom-call(bf16[1,32,1344]{2,1,0:T(8,128)(2,1)} %resid_hbm.1, s32[6,1,32]{2,1,0:T(1,128)} %bitcast.14, f32[6,1,32]{2,1,0:T(1,128)} %bitcast.15, ...), custom_call_target="tpu_custom_call" | custom-call | tf_op jit(solution)/shard_map/prep/pallas_call | solution.py:29
  16.2 0.4 collective-permute-done.4.rest_3_
  16.6 0.3 before.1
  16.9 0.1 collective-permute-start.5
  17.0 0.8 %first_half.1.first_ref = f32[128,1344]{1,0:T(8,128)S(1)} custom-call(f32[128,1024]{1,0:T(8,128)S(1)} %get-tuple-element.48.local_ref, f32[128,1024]{1,0:T(8,128)S(1)} %get-tuple-element.49.grown_ref, bf16[128,256]{1,0:T(8,128)(2,1)S(1)} %get-tuple-element.50.after_ref.c_ref, f32[1,1024]{1,0:T(1,128)S(1)} %get-tuple-element.51.norm_ref, ...), custom_call_target="tpu_custom_call" | custom-call | tf_op jit(solution)/shard_map/first_half/pallas_call | solution.py:29
  17.8 0.5 collective-permute-done.5.got_ref
  18.3 0.9 %mixed.1 = (bf16[32,1344]{1,0:T(8,128)(2,1)S(1)}, bf16[32,1344]{1,0:T(8,128)(2,1)S(1)}, bf16[32,1344]{1,0:T(8,128)(2,1)S(1)}, bf16[32,1344]{1,0:T(8,128)(2,1)S(1)}) custom-call(bf16[1,928,1344]{2,1,0:T(8,128)(2,1)S(1)} %collective-permute-done.1.after_up.other_up_ref, bf16[1,928,1344]{2,1,0:T(8,128)(2,1)S(1)} %collective-permute-done.2.after_down.other_down_ref, ...), custom_call_target="tpu_custom_call" | custom-call | tf_op jit(solution)/shard_map/mixed/pallas_call | solution.py:29
  19.2 3.6 %collective-permute-start.6 = (bf16[32,1344]{1,0:T(8,128)(2,1)S(1)}, bf16[32,1344]{1,0:T(8,128)(2,1)S(1)}, u32[]{:S(2)}, u32[]{:S(2)}) collective-permute-start(bf16[32,1344]{1,0:T(8,128)(2,1)S(1)} %get-tuple-element.61), channel_id=1, source_target_pairs={{0,12},{1,9},{2,14},{3,11},{4,8},{5,13},{6,10},{7,15},{8,4},{9,1},... | collective-permute-start | bytes 258056 | tf_op jit(solution)/shard_map/ppermute | solution.py:340
  22.8 0.8 %collective-permute-start.8 = (bf16[32,1344]{1,0:T(8,128)(2,1)S(1)}, bf16[32,1344]{1,0:T(8,128)(2,1)S(1)}, u32[]{:S(2)}, u32[]{:S(2)}) collective-permute-start(bf16[32,1344]{1,0:T(8,128)(2,1)S(1)} %get-tuple-element.63), channel_id=1, source_target_pairs={{0,4},{1,5},{2,6},{3,7},{4,0},{5,1},{6,2},{7,3},{8,12},{9,13},{10,... | collective-permute-start | bytes 258056 | tf_op jit(solution)/shard_map/ppermute | solution.py:340
  23.6 2.5 %weights.1 = (bf16[1,928,1344]{2,1,0:T(8,128)(2,1)S(1)}, bf16[1,928,1344]{2,1,0:T(8,128)(2,1)S(1)}) custom-call(bf16[32,1344]{1,0:T(8,128)(2,1)S(1)} %get-tuple-element.57.after_ref.rest_0_, bf16[1,928,1344]{2,1,0:T(8,128)(2,1)} %bitcast.10, bf16[1,928,1344]{2,1,0:T(8,128)(2,1)} %down_hbm.1), custom_call_target="tpu_custom_call" | custom-call | tf_op jit(solution)/shard_map/weights/pallas_call | solution.py:29
  26.2 4.4 %collective-permute-done.7.rest_2_ = bf16[32,1344]{1,0:T(8,128)(2,1)S(1)} collective-permute-done((bf16[32,1344]{1,0:T(8,128)(2,1)S(1)}, bf16[32,1344]{1,0:T(8,128)(2,1)S(1)}, u32[]{:S(2)}, u32[]{:S(2)}) %collective-permute-start.7) | collective-permute-done | bytes 86048 | tf_op jit(solution)/shard_map/ppermute | solution.py:340
  30.6 0.2 rows.1
  30.8 0.5 collective-permute-start.12
  31.3 1.5 %collective-permute-start.11 = (bf16[32,1408]{1,0:T(8,128)(2,1)S(1)}, bf16[32,1408]{1,0:T(8,128)(2,1)S(1)}, u32[]{:S(2)}, u32[]{:S(2)}) collective-permute-start(bf16[32,1408]{1,0:T(8,128)(2,1)S(1)} %get-tuple-element.66.rest_0_), channel_id=1, source_target_pairs={{0,2},{1,3},{2,0},{3,1},{4,6},{5,7},{6,4},{7,5},{8,10},{9,11},{10,... | collective-permute-start | bytes 270344 | tf_op jit(solution)/shard_map/ppermute | solution.py:330
  32.8 3.4 %collective-permute-start.10 = (bf16[32,1408]{1,0:T(8,128)(2,1)S(1)}, bf16[32,1408]{1,0:T(8,128)(2,1)S(1)}, u32[]{:S(2)}, u32[]{:S(2)}) collective-permute-start(bf16[32,1408]{1,0:T(8,128)(2,1)S(1)} %get-tuple-element.66.rest_0_), channel_id=1, source_target_pairs={{0,4},{1,5},{2,6},{3,7},{4,0},{5,1},{6,2},{7,3},{8,12},{9,13},{10,... | collective-permute-start | bytes 270344 | tf_op jit(solution)/shard_map/ppermute | solution.py:330
  36.2 1.8 %collective-permute-done.12.rest_0_ = bf16[32,1408]{1,0:T(8,128)(2,1)S(1)} collective-permute-done((bf16[32,1408]{1,0:T(8,128)(2,1)S(1)}, bf16[32,1408]{1,0:T(8,128)(2,1)S(1)}, u32[]{:S(2)}, u32[]{:S(2)}) %collective-permute-start.12) | collective-permute-done | bytes 90144 | tf_op jit(solution)/shard_map/ppermute | solution.py:330
  38.0 1.5 %collective-permute-start.15 = (bf16[32,1408]{1,0:T(8,128)(2,1)S(1)}, bf16[32,1408]{1,0:T(8,128)(2,1)S(1)}, u32[]{:S(2)}, u32[]{:S(2)}) collective-permute-start(bf16[32,1408]{1,0:T(8,128)(2,1)S(1)} %collective-permute-done.12.rest_0_), channel_id=1, source_target_pairs={{0,2},{1,3},{2,0},{3,1},{4,6},{5,7},{6,4},{7,5},{8,10},{9,11},{10,... | collective-permute-start | bytes 270344 | tf_op jit(solution)/shard_map/ppermute | solution.py:330
  39.5 0.1 collective-permute-start.14
  39.7 2.9 %collective-permute-start.13 = (bf16[32,1408]{1,0:T(8,128)(2,1)S(1)}, bf16[32,1408]{1,0:T(8,128)(2,1)S(1)}, u32[]{:S(2)}, u32[]{:S(2)}) collective-permute-start(bf16[32,1408]{1,0:T(8,128)(2,1)S(1)} %collective-permute-done.12.rest_0_), channel_id=1, source_target_pairs={{0,6},{1,7},{2,4},{3,5},{4,2},{5,3},{6,0},{7,1},{8,14},{9,15},{10,... | collective-permute-start | bytes 270344 | tf_op jit(solution)/shard_map/ppermute | solution.py:330
  42.6 2.7 %experts.2 = (bf16[32,1344]{1,0:T(8,128)(2,1)S(1)}, bf16[32,1344]{1,0:T(8,128)(2,1)S(1)}, bf16[32,1344]{1,0:T(8,128)(2,1)S(1)}, bf16[32,1344]{1,0:T(8,128)(2,1)S(1)}) custom-call(bf16[1,928,1344]{2,1,0:T(8,128)(2,1)S(1)} %get-tuple-element.58.after_ref.up_ref, bf16[1,928,1344]{2,1,0:T(8,128)(2,1)S(1)} %get-tuple-element.65.down_ref, ...), custom_call_target="tpu_custom_call" | custom-call | tf_op jit(solution)/shard_map/experts/pallas_call | solution.py:29
  45.3 0.4 collective-permute-done.13.rest_1_
  45.6 2.7 %experts.3 = (bf16[32,1344]{1,0:T(8,128)(2,1)S(1)}, bf16[32,1344]{1,0:T(8,128)(2,1)S(1)}, bf16[32,1344]{1,0:T(8,128)(2,1)S(1)}, bf16[32,1344]{1,0:T(8,128)(2,1)S(1)}) custom-call(bf16[1,928,1344]{2,1,0:T(8,128)(2,1)S(1)} %get-tuple-element.58.after_ref.up_ref, bf16[1,928,1344]{2,1,0:T(8,128)(2,1)S(1)} %get-tuple-element.65.down_ref, ...), custom_call_target="tpu_custom_call" | custom-call | tf_op jit(solution)/shard_map/experts/pallas_call | solution.py:29
  48.4 2.4 %collective-permute-start.16 = (bf16[32,1344]{1,0:T(8,128)(2,1)S(1)}, bf16[32,1344]{1,0:T(8,128)(2,1)S(1)}, u32[]{:S(2)}, u32[]{:S(2)}) collective-permute-start(bf16[32,1344]{1,0:T(8,128)(2,1)S(1)} %get-tuple-element.77), channel_id=1, source_target_pairs={{0,6},{1,7},{2,4},{3,5},{4,2},{5,3},{6,0},{7,1},{8,14},{9,15},{10,... | collective-permute-start | bytes 258056 | tf_op jit(solution)/shard_map/ppermute | solution.py:330
  50.8 0.6 collective-permute-start.17
  51.4 0.5 collective-permute-start.18
  51.9 2.3 %collective-permute-start.20 = (bf16[32,1344]{1,0:T(8,128)(2,1)S(1)}, bf16[32,1344]{1,0:T(8,128)(2,1)S(1)}, u32[]{:S(2)}, u32[]{:S(2)}) collective-permute-start(bf16[32,1344]{1,0:T(8,128)(2,1)S(1)} %get-tuple-element.80), channel_id=1, source_target_pairs={{0,6},{1,7},{2,4},{3,5},{4,2},{5,3},{6,0},{7,1},{8,14},{9,15},{10,... | collective-permute-start | bytes 258056 | tf_op jit(solution)/shard_map/ppermute | solution.py:330
  54.2 0.6 collective-permute-start.21
  54.9 0.9 %collective-permute-start.22 = (bf16[32,1344]{1,0:T(8,128)(2,1)S(1)}, bf16[32,1344]{1,0:T(8,128)(2,1)S(1)}, u32[]{:S(2)}, u32[]{:S(2)}) collective-permute-start(bf16[32,1344]{1,0:T(8,128)(2,1)S(1)} %get-tuple-element.82), channel_id=1, source_target_pairs={{0,2},{1,3},{2,0},{3,1},{4,6},{5,7},{6,4},{7,5},{8,10},{9,11},{10,... | collective-permute-start | bytes 258056 | tf_op jit(solution)/shard_map/ppermute | solution.py:330
  55.8 0.4 collective-permute-done.17.refs_2_
  56.2 1.8 %collective-permute-done.18.refs_3_ = bf16[32,1344]{1,0:T(8,128)(2,1)S(1)} collective-permute-done((bf16[32,1344]{1,0:T(8,128)(2,1)S(1)}, bf16[32,1344]{1,0:T(8,128)(2,1)S(1)}, u32[]{:S(2)}, u32[]{:S(2)}) %collective-permute-start.18) | collective-permute-done | bytes 86048 | tf_op jit(solution)/shard_map/ppermute | solution.py:330
  58.0 0.1 sum.1
  58.1 0.2 collective-permute-start.19
  58.3 0.5 collective-permute-done.21.rest_3_
  58.8 0.6 collective-permute-done.22.rest_4_
  59.4 4.3 %collective-permute-done.19.rest_1_ = bf16[32,1344]{1,0:T(8,128)(2,1)S(1)} collective-permute-done((bf16[32,1344]{1,0:T(8,128)(2,1)S(1)}, bf16[32,1344]{1,0:T(8,128)(2,1)S(1)}, u32[]{:S(2)}, u32[]{:S(2)}) %collective-permute-start.19) | collective-permute-done | bytes 86048 | tf_op jit(solution)/shard_map/ppermute | solution.py:330
  63.7 0.7 %last.1 = bf16[1,32,1344]{2,1,0:T(8,128)(2,1)} custom-call(bf16[32,1344]{1,0:T(8,128)(2,1)S(1)} %get-tuple-element.64.hidden_ref, bf16[32,1344]{1,0:T(8,128)(2,1)S(1)} %get-tuple-element.71.rest_0_, bf16[32,1344]{1,0:T(8,128)(2,1)S(1)} %collective-permute-done.19.rest_1_, bf16[32,1344]{1,0:T(8,128)(2,1)S(1)} %collective-permute-done.20.rest_2_, ...), custom_call_target="tpu_custom_call" | custom-call | tf_op jit(solution)/shard_map/last/pallas_call | solution.py:29
  (13 shorter events, 0.0 us)
Async XLA Ops:
  1.8 1.5 %collective-permute-start = (bf16[4,144,128]{2,1,0:T(8,128)(2,1)S(1)}, bf16[4,144,128]{2,1,0:T(8,128)(2,1)S(1)}, u32[]{:S(2)}, u32[]{:S(2)}) collective-permute-start(bf16[4,144,128]{2,1,0:T(8,128)(2,1)S(1)} %get-tuple-element.45), channel_id=1, source_target_pairs={{0,1},{1,0},{2,3},{3,2},{4,5},{5,4},{6,7},{7,6},{8,9},{9,8},{10,11... | collective-permute-start | bytes 442376 | tf_op jit(solution)/shard_map/ppermute | solution.py:330
  3.5 14.9 %collective-permute-start.1 = (bf16[1,928,1344]{2,1,0:T(8,128)(2,1)}, bf16[1,928,1344]{2,1,0:T(8,128)(2,1)S(1)}, u32[]{:S(2)}, u32[]{:S(2)}) collective-permute-start(bf16[1,928,1344]{2,1,0:T(8,128)(2,1)} %bitcast.9), channel_id=1, source_target_pairs={{0,1},{1,0},{2,3},{3,2},{4,5},{5,4},{6,7},{7,6},{8,9},{9,8},{10,11... | collective-permute-start | bytes 7483400 | tf_op jit(solution)/shard_map/ppermute | solution.py:330
  3.9 14.4 %collective-permute-start.2 = (bf16[1,928,1344]{2,1,0:T(8,128)(2,1)}, bf16[1,928,1344]{2,1,0:T(8,128)(2,1)S(1)}, u32[]{:S(2)}, u32[]{:S(2)}) collective-permute-start(bf16[1,928,1344]{2,1,0:T(8,128)(2,1)} %down_hbm.1), channel_id=1, source_target_pairs={{0,1},{1,0},{2,3},{3,2},{4,5},{5,4},{6,7},{7,6},{8,9},{9,8},{10,11... | collective-permute-start | bytes 7483400 | tf_op jit(solution)/shard_map/ppermute | solution.py:330
  4.0 7.0 %collective-permute-start.3 = (bf16[4,144,128]{2,1,0:T(8,128)(2,1)S(1)}, bf16[4,144,128]{2,1,0:T(8,128)(2,1)S(1)}, u32[]{:S(2)}, u32[]{:S(2)}) collective-permute-start(bf16[4,144,128]{2,1,0:T(8,128)(2,1)S(1)} %chip_state.1.rest_0_), channel_id=1, source_target_pairs={{0,2},{1,3},{2,0},{3,1},{4,6},{5,7},{6,4},{7,5},{8,10},{9,11},{10,... | collective-permute-start | bytes 442376 | tf_op jit(solution)/shard_map/ppermute | solution.py:330
  11.2 5.5 %collective-permute-start.4 = (bf16[4,144,128]{2,1,0:T(8,128)(2,1)S(1)}, bf16[4,144,128]{2,1,0:T(8,128)(2,1)S(1)}, u32[]{:S(2)}, u32[]{:S(2)}) collective-permute-start(bf16[4,144,128]{2,1,0:T(8,128)(2,1)S(1)} %span.1.rest_2_), channel_id=1, source_target_pairs={{0,16},{16,0},{1,17},{17,1},{2,18},{18,2},{3,19},{19,3},{4,20},{20... | collective-permute-start | bytes 442376 | tf_op jit(solution)/shard_map/ppermute | solution.py:330
  16.9 1.4 %collective-permute-start.5 = (bf16[4,128,128]{2,1,0:T(8,128)(2,1)S(1)}, bf16[4,128,128]{2,1,0:T(8,128)(2,1)S(1)}, u32[]{:S(2)}, u32[]{:S(2)}) collective-permute-start(bf16[4,128,128]{2,1,0:T(8,128)(2,1)S(1)} %get-tuple-element.55), channel_id=1, source_target_pairs={{0,1},{1,0},{2,3},{3,2},{4,5},{5,4},{6,7},{7,6},{8,9},{9,8},{10,11... | collective-permute-start | bytes 393224 | tf_op jit(solution)/shard_map/ppermute | solution.py:330
  19.2 7.0 %collective-permute-start.6 = (bf16[32,1344]{1,0:T(8,128)(2,1)S(1)}, bf16[32,1344]{1,0:T(8,128)(2,1)S(1)}, u32[]{:S(2)}, u32[]{:S(2)}) collective-permute-start(bf16[32,1344]{1,0:T(8,128)(2,1)S(1)} %get-tuple-element.61), channel_id=1, source_target_pairs={{0,12},{1,9},{2,14},{3,11},{4,8},{5,13},{6,10},{7,15},{8,4},{9,1},... | collective-permute-start | bytes 258056 | tf_op jit(solution)/shard_map/ppermute | solution.py:340
  22.8 7.8 %collective-permute-start.7 = (bf16[32,1344]{1,0:T(8,128)(2,1)S(1)}, bf16[32,1344]{1,0:T(8,128)(2,1)S(1)}, u32[]{:S(2)}, u32[]{:S(2)}) collective-permute-start(bf16[32,1344]{1,0:T(8,128)(2,1)S(1)} %get-tuple-element.62), channel_id=1, source_target_pairs={{0,8},{1,13},{2,10},{3,15},{4,12},{5,9},{6,14},{7,11},{8,0},{9,5},... | collective-permute-start | bytes 258056 | tf_op jit(solution)/shard_map/ppermute | solution.py:340
  22.8 7.8 %collective-permute-start.8 = (bf16[32,1344]{1,0:T(8,128)(2,1)S(1)}, bf16[32,1344]{1,0:T(8,128)(2,1)S(1)}, u32[]{:S(2)}, u32[]{:S(2)}) collective-permute-start(bf16[32,1344]{1,0:T(8,128)(2,1)S(1)} %get-tuple-element.63), channel_id=1, source_target_pairs={{0,4},{1,5},{2,6},{3,7},{4,0},{5,1},{6,2},{7,3},{8,12},{9,13},{10,... | collective-permute-start | bytes 258056 | tf_op jit(solution)/shard_map/ppermute | solution.py:340
  30.8 7.2 %collective-permute-start.12 = (bf16[32,1408]{1,0:T(8,128)(2,1)S(1)}, bf16[32,1408]{1,0:T(8,128)(2,1)S(1)}, u32[]{:S(2)}, u32[]{:S(2)}) collective-permute-start(bf16[32,1408]{1,0:T(8,128)(2,1)S(1)} %get-tuple-element.66.rest_0_), channel_id=1, source_target_pairs={{0,8},{4,12},{8,0},{12,4},{1,9},{5,13},{9,1},{13,5},{2,10},{6,14},... | collective-permute-start | bytes 270344 | tf_op jit(solution)/shard_map/ppermute | solution.py:330
  31.3 8.4 %collective-permute-start.11 = (bf16[32,1408]{1,0:T(8,128)(2,1)S(1)}, bf16[32,1408]{1,0:T(8,128)(2,1)S(1)}, u32[]{:S(2)}, u32[]{:S(2)}) collective-permute-start(bf16[32,1408]{1,0:T(8,128)(2,1)S(1)} %get-tuple-element.66.rest_0_), channel_id=1, source_target_pairs={{0,2},{1,3},{2,0},{3,1},{4,6},{5,7},{6,4},{7,5},{8,10},{9,11},{10,... | collective-permute-start | bytes 270344 | tf_op jit(solution)/shard_map/ppermute | solution.py:330
  32.8 9.8 %collective-permute-start.10 = (bf16[32,1408]{1,0:T(8,128)(2,1)S(1)}, bf16[32,1408]{1,0:T(8,128)(2,1)S(1)}, u32[]{:S(2)}, u32[]{:S(2)}) collective-permute-start(bf16[32,1408]{1,0:T(8,128)(2,1)S(1)} %get-tuple-element.66.rest_0_), channel_id=1, source_target_pairs={{0,4},{1,5},{2,6},{3,7},{4,0},{5,1},{6,2},{7,3},{8,12},{9,13},{10,... | collective-permute-start | bytes 270344 | tf_op jit(solution)/shard_map/ppermute | solution.py:330
  36.2 6.4 %collective-permute-start.9 = (bf16[32,1408]{1,0:T(8,128)(2,1)S(1)}, bf16[32,1408]{1,0:T(8,128)(2,1)S(1)}, u32[]{:S(2)}, u32[]{:S(2)}) collective-permute-start(bf16[32,1408]{1,0:T(8,128)(2,1)S(1)} %get-tuple-element.66.rest_0_), channel_id=1, source_target_pairs={{0,6},{1,7},{2,4},{3,5},{4,2},{5,3},{6,0},{7,1},{8,14},{9,15},{10,... | collective-permute-start | bytes 270344 | tf_op jit(solution)/shard_map/ppermute | solution.py:330
  38.0 7.3 %collective-permute-start.15 = (bf16[32,1408]{1,0:T(8,128)(2,1)S(1)}, bf16[32,1408]{1,0:T(8,128)(2,1)S(1)}, u32[]{:S(2)}, u32[]{:S(2)}) collective-permute-start(bf16[32,1408]{1,0:T(8,128)(2,1)S(1)} %collective-permute-done.12.rest_0_), channel_id=1, source_target_pairs={{0,2},{1,3},{2,0},{3,1},{4,6},{5,7},{6,4},{7,5},{8,10},{9,11},{10,... | collective-permute-start | bytes 270344 | tf_op jit(solution)/shard_map/ppermute | solution.py:330
  39.5 5.8 %collective-permute-start.14 = (bf16[32,1408]{1,0:T(8,128)(2,1)S(1)}, bf16[32,1408]{1,0:T(8,128)(2,1)S(1)}, u32[]{:S(2)}, u32[]{:S(2)}) collective-permute-start(bf16[32,1408]{1,0:T(8,128)(2,1)S(1)} %collective-permute-done.12.rest_0_), channel_id=1, source_target_pairs={{0,4},{1,5},{2,6},{3,7},{4,0},{5,1},{6,2},{7,3},{8,12},{9,13},{10,... | collective-permute-start | bytes 270344 | tf_op jit(solution)/shard_map/ppermute | solution.py:330
  39.7 6.0 %collective-permute-start.13 = (bf16[32,1408]{1,0:T(8,128)(2,1)S(1)}, bf16[32,1408]{1,0:T(8,128)(2,1)S(1)}, u32[]{:S(2)}, u32[]{:S(2)}) collective-permute-start(bf16[32,1408]{1,0:T(8,128)(2,1)S(1)} %collective-permute-done.12.rest_0_), channel_id=1, source_target_pairs={{0,6},{1,7},{2,4},{3,5},{4,2},{5,3},{6,0},{7,1},{8,14},{9,15},{10,... | collective-permute-start | bytes 270344 | tf_op jit(solution)/shard_map/ppermute | solution.py:330
  48.4 6.5 %collective-permute-start.16 = (bf16[32,1344]{1,0:T(8,128)(2,1)S(1)}, bf16[32,1344]{1,0:T(8,128)(2,1)S(1)}, u32[]{:S(2)}, u32[]{:S(2)}) collective-permute-start(bf16[32,1344]{1,0:T(8,128)(2,1)S(1)} %get-tuple-element.77), channel_id=1, source_target_pairs={{0,6},{1,7},{2,4},{3,5},{4,2},{5,3},{6,0},{7,1},{8,14},{9,15},{10,... | collective-permute-start | bytes 258056 | tf_op jit(solution)/shard_map/ppermute | solution.py:330
  50.8 5.5 %collective-permute-start.17 = (bf16[32,1344]{1,0:T(8,128)(2,1)S(1)}, bf16[32,1344]{1,0:T(8,128)(2,1)S(1)}, u32[]{:S(2)}, u32[]{:S(2)}) collective-permute-start(bf16[32,1344]{1,0:T(8,128)(2,1)S(1)} %get-tuple-element.78), channel_id=1, source_target_pairs={{0,4},{1,5},{2,6},{3,7},{4,0},{5,1},{6,2},{7,3},{8,12},{9,13},{10,... | collective-permute-start | bytes 258056 | tf_op jit(solution)/shard_map/ppermute | solution.py:330
  51.4 6.6 %collective-permute-start.18 = (bf16[32,1344]{1,0:T(8,128)(2,1)S(1)}, bf16[32,1344]{1,0:T(8,128)(2,1)S(1)}, u32[]{:S(2)}, u32[]{:S(2)}) collective-permute-start(bf16[32,1344]{1,0:T(8,128)(2,1)S(1)} %get-tuple-element.79), channel_id=1, source_target_pairs={{0,2},{1,3},{2,0},{3,1},{4,6},{5,7},{6,4},{7,5},{8,10},{9,11},{10,... | collective-permute-start | bytes 258056 | tf_op jit(solution)/shard_map/ppermute | solution.py:330
  51.9 6.4 %collective-permute-start.20 = (bf16[32,1344]{1,0:T(8,128)(2,1)S(1)}, bf16[32,1344]{1,0:T(8,128)(2,1)S(1)}, u32[]{:S(2)}, u32[]{:S(2)}) collective-permute-start(bf16[32,1344]{1,0:T(8,128)(2,1)S(1)} %get-tuple-element.80), channel_id=1, source_target_pairs={{0,6},{1,7},{2,4},{3,5},{4,2},{5,3},{6,0},{7,1},{8,14},{9,15},{10,... | collective-permute-start | bytes 258056 | tf_op jit(solution)/shard_map/ppermute | solution.py:330
  54.2 4.5 %collective-permute-start.21 = (bf16[32,1344]{1,0:T(8,128)(2,1)S(1)}, bf16[32,1344]{1,0:T(8,128)(2,1)S(1)}, u32[]{:S(2)}, u32[]{:S(2)}) collective-permute-start(bf16[32,1344]{1,0:T(8,128)(2,1)S(1)} %get-tuple-element.81), channel_id=1, source_target_pairs={{0,4},{1,5},{2,6},{3,7},{4,0},{5,1},{6,2},{7,3},{8,12},{9,13},{10,... | collective-permute-start | bytes 258056 | tf_op jit(solution)/shard_map/ppermute | solution.py:330
  54.9 4.5 %collective-permute-start.22 = (bf16[32,1344]{1,0:T(8,128)(2,1)S(1)}, bf16[32,1344]{1,0:T(8,128)(2,1)S(1)}, u32[]{:S(2)}, u32[]{:S(2)}) collective-permute-start(bf16[32,1344]{1,0:T(8,128)(2,1)S(1)} %get-tuple-element.82), channel_id=1, source_target_pairs={{0,2},{1,3},{2,0},{3,1},{4,6},{5,7},{6,4},{7,5},{8,10},{9,11},{10,... | collective-permute-start | bytes 258056 | tf_op jit(solution)/shard_map/ppermute | solution.py:330
  58.1 5.6 %collective-permute-start.19 = (bf16[32,1344]{1,0:T(8,128)(2,1)S(1)}, bf16[32,1344]{1,0:T(8,128)(2,1)S(1)}, u32[]{:S(2)}, u32[]{:S(2)}) collective-permute-start(bf16[32,1344]{1,0:T(8,128)(2,1)S(1)} %sum.1), channel_id=1, source_target_pairs={{0,8},{4,12},{8,0},{12,4},{1,9},{5,13},{9,1},{13,5},{2,10},{6,14},... | collective-permute-start | bytes 258056 | tf_op jit(solution)/shard_map/ppermute | solution.py:330

commit v12 on v11

--- a/solution.py
+++ b/solution.py
@@ -454,18 +454,20 @@
     group = [z * exp_size + 2 * d for z in (1, 0) for d in reversed(range(chips))][:-1]
 
     def spread(block):
-        return [block] + [swap(block, both, mask) for mask in group]
+        return [block] + [swap(block, both, mask) for mask in reversed(group)]
 
     sets = [spread(swap(own_rows, "head", high)) for high in range(2, head_size, 2)]
     near = through_experts(spread(own_rows))
     near, sets = lax.optimization_barrier((near, sets))
     far = [through_experts(members) for members in sets]
-    arrived = []
+    arrived, near = [], list(near)
     for high, pieces in zip(range(2, head_size, 2), far):
-        got = [swap(piece, both, mask) for piece, mask in zip(pieces[1:], group)]
+        got = [swap(piece, both, mask) for piece, mask in zip(pieces[:0:-1], group)]
         total = call(sum_kernel, "sum", struct((rows, model), BF16), [(VMEM, v) for v in (pieces[0], *got)])
+        if high == 2:
+            total, near[1:-1] = lax.optimization_barrier((total, near[1:-1]))
         arrived.append(swap(total, "head", high))
-    arrived += [swap(piece, both, mask) for piece, mask in zip(near[1:], group)]
+    arrived += [swap(piece, both, mask) for piece, mask in zip(near[:0:-1], group)]
     return call(
         last_kernel,
         "last",

time: 64.7 us -> 63.9 us (0.988)
  starting transfers between devices: 27.9 us -> 26.7 us
    ppermute x20, starting transfers between devices: 23.4 us -> 22.2 us  [swap(): return lax.ppermute(value, axis, [(i, i ^ mask) for i in range(size)])]
  transfers between devices with their start and end apart: 23 -> 23, of which waited for: 12 -> 14; matrix products, arithmetic and copies ran while one was open for 2% -> 2% of each run, Pallas kernels for 17% -> 17%
where the time goes in v12:
time: 63.9 us; the launch traced here: 63.6 us
  starting transfers between devices  26.7 us (42%)
  waiting for transfers between devices  18.3 us (29%)
  Pallas kernels  17.3 us (27%)
  local copies, waits for them, and re-layouts  1.29 us (2%)
    ppermute x20, starting transfers between devices, swap(): return lax.ppermute(value, axis, [(i, i ^ mask) for i in range(size)])  22.2 us
    pallas_call x14, Pallas kernels, call(): pl.pallas_call(kernel, out_shape=jax.tree.map(lambda out: pltpu.VMEM(out....  17.3 us
    ppermute x20, waiting for transfers between devices, swap(): return lax.ppermute(value, axis, [(i, i ^ mask) for i in range(size)])  13.9 us
    ppermute x3, starting transfers between devices, swap_slot(): return lax.ppermute(value, ('head', 'exp'), pairs)  4.45 us
    ppermute x3, waiting for transfers between devices, swap_slot(): return lax.ppermute(value, ('head', 'exp'), pairs)  4.42 us
    broadcast_in_dim x1, local copies, waits for them, and re-layouts, per_device(): moe_gain[None]  1.29 us
  transfers between devices with their start and end apart: 23, of which 14 were waited for; matrix products, arithmetic and copies ran while one was open for 2% of the time, Pallas kernels for 17%

profile of v12, /device:TPU:0, one launch (start us, length us, event | category | flops | bytes accessed | tf_op | source)
XLA Modules:
  0.0 63.6 jit_solution(4902528480662004956)
XLA Ops:
  0.0 1.8 %state.1 = (bf16[4,144,128]{2,1,0:T(8,128)(2,1)S(1)}, bf16[4,144,128]{2,1,0:T(8,128)(2,1)S(1)}) custom-call(bf16[128,1024]{1,0:T(8,128)(2,1)} %x_hbm.3, bf16[128,256]{1,0:T(8,128)(2,1)} %b_hbm.3, f32[16,128]{1,0:T(8,128)} %bitcast.11, f32[1,16]{1,0:T(1,128)} %bitcast.16), custom_call_target="tpu_custom_call" | custom-call | tf_op jit(solution)/shard_map/state/pallas_call | solution.py:29
  1.8 0.5 collective-permute-start
  2.4 1.0 %collective-permute-done.got_ref = bf16[4,144,128]{2,1,0:T(8,128)(2,1)S(1)} collective-permute-done((bf16[4,144,128]{2,1,0:T(8,128)(2,1)S(1)}, bf16[4,144,128]{2,1,0:T(8,128)(2,1)S(1)}, u32[]{:S(2)}, u32[]{:S(2)}) %collective-permute-start) | collective-permute-done | bytes 147488 | tf_op jit(solution)/shard_map/ppermute | solution.py:330
  3.4 0.1 chip_state.1.rest_0_
  3.5 0.4 collective-permute-start.1
  3.9 0.1 collective-permute-start.2
  4.0 2.9 %collective-permute-start.3 = (bf16[4,144,128]{2,1,0:T(8,128)(2,1)S(1)}, bf16[4,144,128]{2,1,0:T(8,128)(2,1)S(1)}, u32[]{:S(2)}, u32[]{:S(2)}) collective-permute-start(bf16[4,144,128]{2,1,0:T(8,128)(2,1)S(1)} %chip_state.1.rest_0_), channel_id=1, source_target_pairs={{0,2},{1,3},{2,0},{3,1},{4,6},{5,7},{6,4},{7,5},{8,10},{9,11},{10,... | collective-permute-start | bytes 442376 | tf_op jit(solution)/shard_map/ppermute | solution.py:330
  6.9 2.4 %inside.1 = (f32[128,1024]{1,0:T(8,128)S(1)}, f32[128,1024]{1,0:T(8,128)S(1)}, bf16[128,256]{1,0:T(8,128)(2,1)S(1)}) custom-call(bf16[128,1024]{1,0:T(8,128)(2,1)} %x_hbm.3, bf16[128,1024]{1,0:T(8,128)(2,1)} %z_hbm.1, bf16[128,256]{1,0:T(8,128)(2,1)} %b_hbm.3, bf16[128,256]{1,0:T(8,128)(2,1)} %c_hbm.1, f32[16,128]{1,0:T(8,128)} %bitcast.12, ...), custom_call_target="tpu_custom_call" | custom-call | tf_op jit(solution)/shard_map/inside/pallas_call | solution.py:29
  9.4 1.7 %collective-permute-done.3.rest_1_ = bf16[4,144,128]{2,1,0:T(8,128)(2,1)S(1)} collective-permute-done((bf16[4,144,128]{2,1,0:T(8,128)(2,1)S(1)}, bf16[4,144,128]{2,1,0:T(8,128)(2,1)S(1)}, u32[]{:S(2)}, u32[]{:S(2)}) %collective-permute-start.3) | collective-permute-done | bytes 147488 | tf_op jit(solution)/shard_map/ppermute | solution.py:330
  11.1 0.1 span.1.rest_2_
  11.2 1.8 %collective-permute-start.4 = (bf16[4,144,128]{2,1,0:T(8,128)(2,1)S(1)}, bf16[4,144,128]{2,1,0:T(8,128)(2,1)S(1)}, u32[]{:S(2)}, u32[]{:S(2)}) collective-permute-start(bf16[4,144,128]{2,1,0:T(8,128)(2,1)S(1)} %span.1.rest_2_), channel_id=1, source_target_pairs={{0,16},{16,0},{1,17},{17,1},{2,18},{18,2},{3,19},{19,3},{4,20},{20... | collective-permute-start | bytes 442376 | tf_op jit(solution)/shard_map/ppermute | solution.py:330
  12.9 1.3 %broadcast_in_dim.14.gain_hbm = f32[1,1344]{1,0:T(1,128)} reshape(f32[1344]{0:T(1024)} %param.27) | data formatting | bytes 10752 | tf_op jit(solution)/shard_map/broadcast_in_dim | solution.py:385
  14.2 1.9 %prep.1 = (bf16[32,128]{1,0:T(8,128)(2,1)S(1)}, bf16[1,32,1344]{2,1,0:T(8,128)(2,1)S(1)}, f32[1,1344]{1,0:T(1,128)S(1)}, f32[1,1024]{1,0:T(1,128)S(1)}, bf16[1344,1024]{1,0:T(8,128)(2,1)S(1)}) custom-call(bf16[1,32,1344]{2,1,0:T(8,128)(2,1)} %resid_hbm.1, s32[6,1,32]{2,1,0:T(1,128)} %bitcast.14, f32[6,1,32]{2,1,0:T(1,128)} %bitcast.15, ...), custom_call_target="tpu_custom_call" | custom-call | tf_op jit(solution)/shard_map/prep/pallas_call | solution.py:29
  16.2 0.4 collective-permute-done.4.rest_3_
  16.6 0.3 before.1
  17.0 0.8 %first_half.1.first_ref = f32[128,1344]{1,0:T(8,128)S(1)} custom-call(f32[128,1024]{1,0:T(8,128)S(1)} %get-tuple-element.51.local_ref, f32[128,1024]{1,0:T(8,128)S(1)} %get-tuple-element.52.grown_ref, bf16[128,256]{1,0:T(8,128)(2,1)S(1)} %get-tuple-element.53.after_ref.c_ref, f32[1,1024]{1,0:T(1,128)S(1)} %get-tuple-element.54.norm_ref, ...), custom_call_target="tpu_custom_call" | custom-call | tf_op jit(solution)/shard_map/first_half/pallas_call | solution.py:29
  17.8 0.5 collective-permute-done.5.got_ref
  18.3 0.9 %mixed.1 = (bf16[32,1344]{1,0:T(8,128)(2,1)S(1)}, bf16[32,1344]{1,0:T(8,128)(2,1)S(1)}, bf16[32,1344]{1,0:T(8,128)(2,1)S(1)}, bf16[32,1344]{1,0:T(8,128)(2,1)S(1)}) custom-call(bf16[1,928,1344]{2,1,0:T(8,128)(2,1)S(1)} %collective-permute-done.1.after_up.other_up_ref, bf16[1,928,1344]{2,1,0:T(8,128)(2,1)S(1)} %collective-permute-done.2.after_down.other_down_ref, ...), custom_call_target="tpu_custom_call" | custom-call | tf_op jit(solution)/shard_map/mixed/pallas_call | solution.py:29
  19.2 3.6 %collective-permute-start.6 = (bf16[32,1344]{1,0:T(8,128)(2,1)S(1)}, bf16[32,1344]{1,0:T(8,128)(2,1)S(1)}, u32[]{:S(2)}, u32[]{:S(2)}) collective-permute-start(bf16[32,1344]{1,0:T(8,128)(2,1)S(1)} %get-tuple-element.64), channel_id=1, source_target_pairs={{0,12},{1,9},{2,14},{3,11},{4,8},{5,13},{6,10},{7,15},{8,4},{9,1},... | collective-permute-start | bytes 258056 | tf_op jit(solution)/shard_map/ppermute | solution.py:340
  22.8 0.8 %collective-permute-start.8 = (bf16[32,1344]{1,0:T(8,128)(2,1)S(1)}, bf16[32,1344]{1,0:T(8,128)(2,1)S(1)}, u32[]{:S(2)}, u32[]{:S(2)}) collective-permute-start(bf16[32,1344]{1,0:T(8,128)(2,1)S(1)} %get-tuple-element.66), channel_id=1, source_target_pairs={{0,4},{1,5},{2,6},{3,7},{4,0},{5,1},{6,2},{7,3},{8,12},{9,13},{10,... | collective-permute-start | bytes 258056 | tf_op jit(solution)/shard_map/ppermute | solution.py:340
  23.6 2.5 %weights.1 = (bf16[1,928,1344]{2,1,0:T(8,128)(2,1)S(1)}, bf16[1,928,1344]{2,1,0:T(8,128)(2,1)S(1)}) custom-call(bf16[32,1344]{1,0:T(8,128)(2,1)S(1)} %get-tuple-element.60.after_ref.rest_0_, bf16[1,928,1344]{2,1,0:T(8,128)(2,1)} %bitcast.10, bf16[1,928,1344]{2,1,0:T(8,128)(2,1)} %down_hbm.1), custom_call_target="tpu_custom_call" | custom-call | tf_op jit(solution)/shard_map/weights/pallas_call | solution.py:29
  26.2 4.4 %collective-permute-done.7.rest_2_ = bf16[32,1344]{1,0:T(8,128)(2,1)S(1)} collective-permute-done((bf16[32,1344]{1,0:T(8,128)(2,1)S(1)}, bf16[32,1344]{1,0:T(8,128)(2,1)S(1)}, u32[]{:S(2)}, u32[]{:S(2)}) %collective-permute-start.7) | collective-permute-done | bytes 86048 | tf_op jit(solution)/shard_map/ppermute | solution.py:340
  30.6 0.2 rows.1
  30.8 0.5 collective-permute-start.12
  31.3 4.3 %collective-permute-start.11 = (bf16[32,1408]{1,0:T(8,128)(2,1)S(1)}, bf16[32,1408]{1,0:T(8,128)(2,1)S(1)}, u32[]{:S(2)}, u32[]{:S(2)}) collective-permute-start(bf16[32,1408]{1,0:T(8,128)(2,1)S(1)} %get-tuple-element.69.rest_0_), channel_id=1, source_target_pairs={{0,6},{1,7},{2,4},{3,5},{4,2},{5,3},{6,0},{7,1},{8,14},{9,15},{10,... | collective-permute-start | bytes 270344 | tf_op jit(solution)/shard_map/ppermute | solution.py:330
  35.6 0.6 collective-permute-start.9
  36.2 1.7 %collective-permute-done.12.rest_0_ = bf16[32,1408]{1,0:T(8,128)(2,1)S(1)} collective-permute-done((bf16[32,1408]{1,0:T(8,128)(2,1)S(1)}, bf16[32,1408]{1,0:T(8,128)(2,1)S(1)}, u32[]{:S(2)}, u32[]{:S(2)}) %collective-permute-start.12) | collective-permute-done | bytes 90144 | tf_op jit(solution)/shard_map/ppermute | solution.py:330
  37.9 1.2 %collective-permute-start.15 = (bf16[32,1408]{1,0:T(8,128)(2,1)S(1)}, bf16[32,1408]{1,0:T(8,128)(2,1)S(1)}, u32[]{:S(2)}, u32[]{:S(2)}) collective-permute-start(bf16[32,1408]{1,0:T(8,128)(2,1)S(1)} %collective-permute-done.12.rest_0_), channel_id=1, source_target_pairs={{0,6},{1,7},{2,4},{3,5},{4,2},{5,3},{6,0},{7,1},{8,14},{9,15},{10,... | collective-permute-start | bytes 270344 | tf_op jit(solution)/shard_map/ppermute | solution.py:330
  39.1 1.8 %collective-permute-start.14 = (bf16[32,1408]{1,0:T(8,128)(2,1)S(1)}, bf16[32,1408]{1,0:T(8,128)(2,1)S(1)}, u32[]{:S(2)}, u32[]{:S(2)}) collective-permute-start(bf16[32,1408]{1,0:T(8,128)(2,1)S(1)} %collective-permute-done.12.rest_0_), channel_id=1, source_target_pairs={{0,4},{1,5},{2,6},{3,7},{4,0},{5,1},{6,2},{7,3},{8,12},{9,13},{10,... | collective-permute-start | bytes 270344 | tf_op jit(solution)/shard_map/ppermute | solution.py:330
  40.9 0.5 collective-permute-start.13
  41.4 2.7 %experts.2 = (bf16[32,1344]{1,0:T(8,128)(2,1)S(1)}, bf16[32,1344]{1,0:T(8,128)(2,1)S(1)}, bf16[32,1344]{1,0:T(8,128)(2,1)S(1)}, bf16[32,1344]{1,0:T(8,128)(2,1)S(1)}) custom-call(bf16[1,928,1344]{2,1,0:T(8,128)(2,1)S(1)} %get-tuple-element.61.after_ref.up_ref, bf16[1,928,1344]{2,1,0:T(8,128)(2,1)S(1)} %get-tuple-element.68.down_ref, ...), custom_call_target="tpu_custom_call" | custom-call | tf_op jit(solution)/shard_map/experts/pallas_call | solution.py:29
  44.1 0.2 collective-permute-done.15.rest_3_
  44.4 0.9 %collective-permute-done.14.rest_2_ = bf16[32,1408]{1,0:T(8,128)(2,1)S(1)} collective-permute-done((bf16[32,1408]{1,0:T(8,128)(2,1)S(1)}, bf16[32,1408]{1,0:T(8,128)(2,1)S(1)}, u32[]{:S(2)}, u32[]{:S(2)}) %collective-permute-start.14) | collective-permute-done | bytes 90144 | tf_op jit(solution)/shard_map/ppermute | solution.py:330
  45.2 0.2 collective-permute-done.13.rest_1_
  45.5 2.7 %experts.3 = (bf16[32,1344]{1,0:T(8,128)(2,1)S(1)}, bf16[32,1344]{1,0:T(8,128)(2,1)S(1)}, bf16[32,1344]{1,0:T(8,128)(2,1)S(1)}, bf16[32,1344]{1,0:T(8,128)(2,1)S(1)}) custom-call(bf16[1,928,1344]{2,1,0:T(8,128)(2,1)S(1)} %get-tuple-element.61.after_ref.up_ref, bf16[1,928,1344]{2,1,0:T(8,128)(2,1)S(1)} %get-tuple-element.68.down_ref, ...), custom_call_target="tpu_custom_call" | custom-call | tf_op jit(solution)/shard_map/experts/pallas_call | solution.py:29
  48.2 0.6 collective-permute-start.16
  48.8 2.1 %collective-permute-start.17 = (bf16[32,1344]{1,0:T(8,128)(2,1)S(1)}, bf16[32,1344]{1,0:T(8,128)(2,1)S(1)}, u32[]{:S(2)}, u32[]{:S(2)}) collective-permute-start(bf16[32,1344]{1,0:T(8,128)(2,1)S(1)} %get-tuple-element.81), channel_id=1, source_target_pairs={{0,4},{1,5},{2,6},{3,7},{4,0},{5,1},{6,2},{7,3},{8,12},{9,13},{10,... | collective-permute-start | bytes 258056 | tf_op jit(solution)/shard_map/ppermute | solution.py:330
  50.9 0.8 %collective-permute-start.18 = (bf16[32,1344]{1,0:T(8,128)(2,1)S(1)}, bf16[32,1344]{1,0:T(8,128)(2,1)S(1)}, u32[]{:S(2)}, u32[]{:S(2)}) collective-permute-start(bf16[32,1344]{1,0:T(8,128)(2,1)S(1)} %get-tuple-element.82), channel_id=1, source_target_pairs={{0,2},{1,3},{2,0},{3,1},{4,6},{5,7},{6,4},{7,5},{8,10},{9,11},{10,... | collective-permute-start | bytes 258056 | tf_op jit(solution)/shard_map/ppermute | solution.py:330
  51.7 0.9 %collective-permute-start.20 = (bf16[32,1344]{1,0:T(8,128)(2,1)S(1)}, bf16[32,1344]{1,0:T(8,128)(2,1)S(1)}, u32[]{:S(2)}, u32[]{:S(2)}) collective-permute-start(bf16[32,1344]{1,0:T(8,128)(2,1)S(1)} %get-tuple-element.86), channel_id=1, source_target_pairs={{0,6},{1,7},{2,4},{3,5},{4,2},{5,3},{6,0},{7,1},{8,14},{9,15},{10,... | collective-permute-start | bytes 258056 | tf_op jit(solution)/shard_map/ppermute | solution.py:330
  52.7 1.5 %collective-permute-done.16.refs_1_ = bf16[32,1344]{1,0:T(8,128)(2,1)S(1)} collective-permute-done((bf16[32,1344]{1,0:T(8,128)(2,1)S(1)}, bf16[32,1344]{1,0:T(8,128)(2,1)S(1)}, u32[]{:S(2)}, u32[]{:S(2)}) %collective-permute-start.16) | collective-permute-done | bytes 86048 | tf_op jit(solution)/shard_map/ppermute | solution.py:330
  54.1 1.6 %collective-permute-done.17.refs_2_ = bf16[32,1344]{1,0:T(8,128)(2,1)S(1)} collective-permute-done((bf16[32,1344]{1,0:T(8,128)(2,1)S(1)}, bf16[32,1344]{1,0:T(8,128)(2,1)S(1)}, u32[]{:S(2)}, u32[]{:S(2)}) %collective-permute-start.17) | collective-permute-done | bytes 86048 | tf_op jit(solution)/shard_map/ppermute | solution.py:330
  55.7 0.5 collective-permute-done.18.refs_3_
  56.3 0.7 %collective-permute-start.19 = (bf16[32,1344]{1,0:T(8,128)(2,1)S(1)}, bf16[32,1344]{1,0:T(8,128)(2,1)S(1)}, u32[]{:S(2)}, u32[]{:S(2)}) collective-permute-start(bf16[32,1344]{1,0:T(8,128)(2,1)S(1)} %sum.1), channel_id=1, source_target_pairs={{0,8},{4,12},{8,0},{12,4},{1,9},{5,13},{9,1},{13,5},{2,10},{6,14},... | collective-permute-start | bytes 258056 | tf_op jit(solution)/shard_map/ppermute | solution.py:330
  57.0 1.4 %collective-permute-start.21 = (bf16[32,1344]{1,0:T(8,128)(2,1)S(1)}, bf16[32,1344]{1,0:T(8,128)(2,1)S(1)}, u32[]{:S(2)}, u32[]{:S(2)}) collective-permute-start(bf16[32,1344]{1,0:T(8,128)(2,1)S(1)} %get-tuple-element.87), channel_id=1, source_target_pairs={{0,4},{1,5},{2,6},{3,7},{4,0},{5,1},{6,2},{7,3},{8,12},{9,13},{10,... | collective-permute-start | bytes 258056 | tf_op jit(solution)/shard_map/ppermute | solution.py:330
  58.4 0.9 %collective-permute-start.22 = (bf16[32,1344]{1,0:T(8,128)(2,1)S(1)}, bf16[32,1344]{1,0:T(8,128)(2,1)S(1)}, u32[]{:S(2)}, u32[]{:S(2)}) collective-permute-start(bf16[32,1344]{1,0:T(8,128)(2,1)S(1)} %get-tuple-element.88), channel_id=1, source_target_pairs={{0,2},{1,3},{2,0},{3,1},{4,6},{5,7},{6,4},{7,5},{8,10},{9,11},{10,... | collective-permute-start | bytes 258056 | tf_op jit(solution)/shard_map/ppermute | solution.py:330
  59.3 3.4 %collective-permute-done.19.rest_1_ = bf16[32,1344]{1,0:T(8,128)(2,1)S(1)} collective-permute-done((bf16[32,1344]{1,0:T(8,128)(2,1)S(1)}, bf16[32,1344]{1,0:T(8,128)(2,1)S(1)}, u32[]{:S(2)}, u32[]{:S(2)}) %collective-permute-start.19) | collective-permute-done | bytes 86048 | tf_op jit(solution)/shard_map/ppermute | solution.py:330
  62.7 0.2 collective-permute-done.22.rest_4_
  62.9 0.7 %last.1 = bf16[1,32,1344]{2,1,0:T(8,128)(2,1)} custom-call(bf16[32,1344]{1,0:T(8,128)(2,1)S(1)} %get-tuple-element.67.hidden_ref, bf16[32,1344]{1,0:T(8,128)(2,1)S(1)} %get-tuple-element.74.rest_0_, bf16[32,1344]{1,0:T(8,128)(2,1)S(1)} %collective-permute-done.19.rest_1_, bf16[32,1344]{1,0:T(8,128)(2,1)S(1)} %collective-permute-done.20.rest_2_, ...), custom_call_target="tpu_custom_call" | custom-call | tf_op jit(solution)/shard_map/last/pallas_call | solution.py:29
  (13 shorter events, 0.1 us)
Async XLA Ops:
  1.8 1.5 %collective-permute-start = (bf16[4,144,128]{2,1,0:T(8,128)(2,1)S(1)}, bf16[4,144,128]{2,1,0:T(8,128)(2,1)S(1)}, u32[]{:S(2)}, u32[]{:S(2)}) collective-permute-start(bf16[4,144,128]{2,1,0:T(8,128)(2,1)S(1)} %get-tuple-element.48), channel_id=1, source_target_pairs={{0,1},{1,0},{2,3},{3,2},{4,5},{5,4},{6,7},{7,6},{8,9},{9,8},{10,11... | collective-permute-start | bytes 442376 | tf_op jit(solution)/shard_map/ppermute | solution.py:330
  3.5 14.9 %collective-permute-start.1 = (bf16[1,928,1344]{2,1,0:T(8,128)(2,1)}, bf16[1,928,1344]{2,1,0:T(8,128)(2,1)S(1)}, u32[]{:S(2)}, u32[]{:S(2)}) collective-permute-start(bf16[1,928,1344]{2,1,0:T(8,128)(2,1)} %bitcast.9), channel_id=1, source_target_pairs={{0,1},{1,0},{2,3},{3,2},{4,5},{5,4},{6,7},{7,6},{8,9},{9,8},{10,11... | collective-permute-start | bytes 7483400 | tf_op jit(solution)/shard_map/ppermute | solution.py:330
  3.9 14.4 %collective-permute-start.2 = (bf16[1,928,1344]{2,1,0:T(8,128)(2,1)}, bf16[1,928,1344]{2,1,0:T(8,128)(2,1)S(1)}, u32[]{:S(2)}, u32[]{:S(2)}) collective-permute-start(bf16[1,928,1344]{2,1,0:T(8,128)(2,1)} %down_hbm.1), channel_id=1, source_target_pairs={{0,1},{1,0},{2,3},{3,2},{4,5},{5,4},{6,7},{7,6},{8,9},{9,8},{10,11... | collective-permute-start | bytes 7483400 | tf_op jit(solution)/shard_map/ppermute | solution.py:330
  4.0 7.0 %collective-permute-start.3 = (bf16[4,144,128]{2,1,0:T(8,128)(2,1)S(1)}, bf16[4,144,128]{2,1,0:T(8,128)(2,1)S(1)}, u32[]{:S(2)}, u32[]{:S(2)}) collective-permute-start(bf16[4,144,128]{2,1,0:T(8,128)(2,1)S(1)} %chip_state.1.rest_0_), channel_id=1, source_target_pairs={{0,2},{1,3},{2,0},{3,1},{4,6},{5,7},{6,4},{7,5},{8,10},{9,11},{10,... | collective-permute-start | bytes 442376 | tf_op jit(solution)/shard_map/ppermute | solution.py:330
  11.2 5.5 %collective-permute-start.4 = (bf16[4,144,128]{2,1,0:T(8,128)(2,1)S(1)}, bf16[4,144,128]{2,1,0:T(8,128)(2,1)S(1)}, u32[]{:S(2)}, u32[]{:S(2)}) collective-permute-start(bf16[4,144,128]{2,1,0:T(8,128)(2,1)S(1)} %span.1.rest_2_), channel_id=1, source_target_pairs={{0,16},{16,0},{1,17},{17,1},{2,18},{18,2},{3,19},{19,3},{4,20},{20... | collective-permute-start | bytes 442376 | tf_op jit(solution)/shard_map/ppermute | solution.py:330
  16.9 1.4 %collective-permute-start.5 = (bf16[4,128,128]{2,1,0:T(8,128)(2,1)S(1)}, bf16[4,128,128]{2,1,0:T(8,128)(2,1)S(1)}, u32[]{:S(2)}, u32[]{:S(2)}) collective-permute-start(bf16[4,128,128]{2,1,0:T(8,128)(2,1)S(1)} %get-tuple-element.58), channel_id=1, source_target_pairs={{0,1},{1,0},{2,3},{3,2},{4,5},{5,4},{6,7},{7,6},{8,9},{9,8},{10,11... | collective-permute-start | bytes 393224 | tf_op jit(solution)/shard_map/ppermute | solution.py:330
  19.2 7.0 %collective-permute-start.6 = (bf16[32,1344]{1,0:T(8,128)(2,1)S(1)}, bf16[32,1344]{1,0:T(8,128)(2,1)S(1)}, u32[]{:S(2)}, u32[]{:S(2)}) collective-permute-start(bf16[32,1344]{1,0:T(8,128)(2,1)S(1)} %get-tuple-element.64), channel_id=1, source_target_pairs={{0,12},{1,9},{2,14},{3,11},{4,8},{5,13},{6,10},{7,15},{8,4},{9,1},... | collective-permute-start | bytes 258056 | tf_op jit(solution)/shard_map/ppermute | solution.py:340
  22.8 7.8 %collective-permute-start.7 = (bf16[32,1344]{1,0:T(8,128)(2,1)S(1)}, bf16[32,1344]{1,0:T(8,128)(2,1)S(1)}, u32[]{:S(2)}, u32[]{:S(2)}) collective-permute-start(bf16[32,1344]{1,0:T(8,128)(2,1)S(1)} %get-tuple-element.65), channel_id=1, source_target_pairs={{0,8},{1,13},{2,10},{3,15},{4,12},{5,9},{6,14},{7,11},{8,0},{9,5},... | collective-permute-start | bytes 258056 | tf_op jit(solution)/shard_map/ppermute | solution.py:340
  22.8 7.8 %collective-permute-start.8 = (bf16[32,1344]{1,0:T(8,128)(2,1)S(1)}, bf16[32,1344]{1,0:T(8,128)(2,1)S(1)}, u32[]{:S(2)}, u32[]{:S(2)}) collective-permute-start(bf16[32,1344]{1,0:T(8,128)(2,1)S(1)} %get-tuple-element.66), channel_id=1, source_target_pairs={{0,4},{1,5},{2,6},{3,7},{4,0},{5,1},{6,2},{7,3},{8,12},{9,13},{10,... | collective-permute-start | bytes 258056 | tf_op jit(solution)/shard_map/ppermute | solution.py:340
  30.8 7.1 %collective-permute-start.12 = (bf16[32,1408]{1,0:T(8,128)(2,1)S(1)}, bf16[32,1408]{1,0:T(8,128)(2,1)S(1)}, u32[]{:S(2)}, u32[]{:S(2)}) collective-permute-start(bf16[32,1408]{1,0:T(8,128)(2,1)S(1)} %get-tuple-element.69.rest_0_), channel_id=1, source_target_pairs={{0,8},{4,12},{8,0},{12,4},{1,9},{5,13},{9,1},{13,5},{2,10},{6,14},... | collective-permute-start | bytes 270344 | tf_op jit(solution)/shard_map/ppermute | solution.py:330
  31.3 9.6 %collective-permute-start.11 = (bf16[32,1408]{1,0:T(8,128)(2,1)S(1)}, bf16[32,1408]{1,0:T(8,128)(2,1)S(1)}, u32[]{:S(2)}, u32[]{:S(2)}) collective-permute-start(bf16[32,1408]{1,0:T(8,128)(2,1)S(1)} %get-tuple-element.69.rest_0_), channel_id=1, source_target_pairs={{0,6},{1,7},{2,4},{3,5},{4,2},{5,3},{6,0},{7,1},{8,14},{9,15},{10,... | collective-permute-start | bytes 270344 | tf_op jit(solution)/shard_map/ppermute | solution.py:330
  35.6 5.8 %collective-permute-start.10 = (bf16[32,1408]{1,0:T(8,128)(2,1)S(1)}, bf16[32,1408]{1,0:T(8,128)(2,1)S(1)}, u32[]{:S(2)}, u32[]{:S(2)}) collective-permute-start(bf16[32,1408]{1,0:T(8,128)(2,1)S(1)} %get-tuple-element.69.rest_0_), channel_id=1, source_target_pairs={{0,4},{1,5},{2,6},{3,7},{4,0},{5,1},{6,2},{7,3},{8,12},{9,13},{10,... | collective-permute-start | bytes 270344 | tf_op jit(solution)/shard_map/ppermute | solution.py:330
  35.6 5.8 %collective-permute-start.9 = (bf16[32,1408]{1,0:T(8,128)(2,1)S(1)}, bf16[32,1408]{1,0:T(8,128)(2,1)S(1)}, u32[]{:S(2)}, u32[]{:S(2)}) collective-permute-start(bf16[32,1408]{1,0:T(8,128)(2,1)S(1)} %get-tuple-element.69.rest_0_), channel_id=1, source_target_pairs={{0,2},{1,3},{2,0},{3,1},{4,6},{5,7},{6,4},{7,5},{8,10},{9,11},{10,... | collective-permute-start | bytes 270344 | tf_op jit(solution)/shard_map/ppermute | solution.py:330
  37.9 6.5 %collective-permute-start.15 = (bf16[32,1408]{1,0:T(8,128)(2,1)S(1)}, bf16[32,1408]{1,0:T(8,128)(2,1)S(1)}, u32[]{:S(2)}, u32[]{:S(2)}) collective-permute-start(bf16[32,1408]{1,0:T(8,128)(2,1)S(1)} %collective-permute-done.12.rest_0_), channel_id=1, source_target_pairs={{0,6},{1,7},{2,4},{3,5},{4,2},{5,3},{6,0},{7,1},{8,14},{9,15},{10,... | collective-permute-start | bytes 270344 | tf_op jit(solution)/shard_map/ppermute | solution.py:330
  39.1 6.1 %collective-permute-start.14 = (bf16[32,1408]{1,0:T(8,128)(2,1)S(1)}, bf16[32,1408]{1,0:T(8,128)(2,1)S(1)}, u32[]{:S(2)}, u32[]{:S(2)}) collective-permute-start(bf16[32,1408]{1,0:T(8,128)(2,1)S(1)} %collective-permute-done.12.rest_0_), channel_id=1, source_target_pairs={{0,4},{1,5},{2,6},{3,7},{4,0},{5,1},{6,2},{7,3},{8,12},{9,13},{10,... | collective-permute-start | bytes 270344 | tf_op jit(solution)/shard_map/ppermute | solution.py:330
  40.9 4.6 %collective-permute-start.13 = (bf16[32,1408]{1,0:T(8,128)(2,1)S(1)}, bf16[32,1408]{1,0:T(8,128)(2,1)S(1)}, u32[]{:S(2)}, u32[]{:S(2)}) collective-permute-start(bf16[32,1408]{1,0:T(8,128)(2,1)S(1)} %collective-permute-done.12.rest_0_), channel_id=1, source_target_pairs={{0,2},{1,3},{2,0},{3,1},{4,6},{5,7},{6,4},{7,5},{8,10},{9,11},{10,... | collective-permute-start | bytes 270344 | tf_op jit(solution)/shard_map/ppermute | solution.py:330
  48.2 6.0 %collective-permute-start.16 = (bf16[32,1344]{1,0:T(8,128)(2,1)S(1)}, bf16[32,1344]{1,0:T(8,128)(2,1)S(1)}, u32[]{:S(2)}, u32[]{:S(2)}) collective-permute-start(bf16[32,1344]{1,0:T(8,128)(2,1)S(1)} %get-tuple-element.80), channel_id=1, source_target_pairs={{0,6},{1,7},{2,4},{3,5},{4,2},{5,3},{6,0},{7,1},{8,14},{9,15},{10,... | collective-permute-start | bytes 258056 | tf_op jit(solution)/shard_map/ppermute | solution.py:330
  48.8 6.9 %collective-permute-start.17 = (bf16[32,1344]{1,0:T(8,128)(2,1)S(1)}, bf16[32,1344]{1,0:T(8,128)(2,1)S(1)}, u32[]{:S(2)}, u32[]{:S(2)}) collective-permute-start(bf16[32,1344]{1,0:T(8,128)(2,1)S(1)} %get-tuple-element.81), channel_id=1, source_target_pairs={{0,4},{1,5},{2,6},{3,7},{4,0},{5,1},{6,2},{7,3},{8,12},{9,13},{10,... | collective-permute-start | bytes 258056 | tf_op jit(solution)/shard_map/ppermute | solution.py:330
  50.9 5.3 %collective-permute-start.18 = (bf16[32,1344]{1,0:T(8,128)(2,1)S(1)}, bf16[32,1344]{1,0:T(8,128)(2,1)S(1)}, u32[]{:S(2)}, u32[]{:S(2)}) collective-permute-start(bf16[32,1344]{1,0:T(8,128)(2,1)S(1)} %get-tuple-element.82), channel_id=1, source_target_pairs={{0,2},{1,3},{2,0},{3,1},{4,6},{5,7},{6,4},{7,5},{8,10},{9,11},{10,... | collective-permute-start | bytes 258056 | tf_op jit(solution)/shard_map/ppermute | solution.py:330
  51.7 7.6 %collective-permute-start.20 = (bf16[32,1344]{1,0:T(8,128)(2,1)S(1)}, bf16[32,1344]{1,0:T(8,128)(2,1)S(1)}, u32[]{:S(2)}, u32[]{:S(2)}) collective-permute-start(bf16[32,1344]{1,0:T(8,128)(2,1)S(1)} %get-tuple-element.86), channel_id=1, source_target_pairs={{0,6},{1,7},{2,4},{3,5},{4,2},{5,3},{6,0},{7,1},{8,14},{9,15},{10,... | collective-permute-start | bytes 258056 | tf_op jit(solution)/shard_map/ppermute | solution.py:330
  56.3 6.5 %collective-permute-start.19 = (bf16[32,1344]{1,0:T(8,128)(2,1)S(1)}, bf16[32,1344]{1,0:T(8,128)(2,1)S(1)}, u32[]{:S(2)}, u32[]{:S(2)}) collective-permute-start(bf16[32,1344]{1,0:T(8,128)(2,1)S(1)} %sum.1), channel_id=1, source_target_pairs={{0,8},{4,12},{8,0},{12,4},{1,9},{5,13},{9,1},{13,5},{2,10},{6,14},... | collective-permute-start | bytes 258056 | tf_op jit(solution)/shard_map/ppermute | solution.py:330
  57.0 5.7 %collective-permute-start.21 = (bf16[32,1344]{1,0:T(8,128)(2,1)S(1)}, bf16[32,1344]{1,0:T(8,128)(2,1)S(1)}, u32[]{:S(2)}, u32[]{:S(2)}) collective-permute-start(bf16[32,1344]{1,0:T(8,128)(2,1)S(1)} %get-tuple-element.87), channel_id=1, source_target_pairs={{0,4},{1,5},{2,6},{3,7},{4,0},{5,1},{6,2},{7,3},{8,12},{9,13},{10,... | collective-permute-start | bytes 258056 | tf_op jit(solution)/shard_map/ppermute | solution.py:330
  58.4 4.5 %collective-permute-start.22 = (bf16[32,1344]{1,0:T(8,128)(2,1)S(1)}, bf16[32,1344]{1,0:T(8,128)(2,1)S(1)}, u32[]{:S(2)}, u32[]{:S(2)}) collective-permute-start(bf16[32,1344]{1,0:T(8,128)(2,1)S(1)} %get-tuple-element.88), channel_id=1, source_target_pairs={{0,2},{1,3},{2,0},{3,1},{4,6},{5,7},{6,4},{7,5},{8,10},{9,11},{10,... | collective-permute-start | bytes 258056 | tf_op jit(solution)/shard_map/ppermute | solution.py:330

commit v13 on v12

--- a/solution.py
+++ b/solution.py
@@ -39,7 +39,11 @@
 
 def offsets(count):
     down = list(range(count - 1, 0, -1))
-    return [down, down[-2::-1] + down[-1:]]
+    return [[2, 3, 1], [3, 1, 2]] if count == 4 else [down, down]
+
+
+def targets(count):
+    return [[2, 3, 1], [1, 1, 2]] if count == 4 else offsets(count)
 
 
 def head_offset(slot, count):
@@ -84,16 +88,22 @@
 
 
 def unpacked(block):
-    block = block.astype(F32)
-    return block[:, STATE : STATE + 1, :] + block[:, STATE + 1 : STATE + 2, :], block[:, 0:STATE, :]
+    pairs = block.shape[0] // STATE
+    tail = block[pairs * STATE :].astype(F32)
+    totals = [tail[pair : pair + 1] + tail[pairs + pair : pairs + pair + 1] for pair in range(pairs)]
+    return jnp.stack(totals), block[: pairs * STATE].astype(F32).reshape(pairs, STATE, LANES)
 
 
 def pack(ref, total, state):
-    ref[:, 0:STATE, :] = state.astype(BF16)
-    wide = jnp.broadcast_to(total, (ref.shape[0], TILE, LANES))
-    high = wide.astype(BF16).astype(F32)
-    row = lax.broadcasted_iota(jnp.int32, wide.shape, 1)
-    ref[:, STATE : STATE + TILE, :] = jnp.where(row == 0, high, wide - high).astype(BF16)
+    pairs = state.shape[0]
+    ref[0 : pairs * STATE, :] = state.reshape(pairs * STATE, LANES).astype(BF16)
+    row = lax.broadcasted_iota(jnp.int32, (TILE, LANES), 0)
+    tail = jnp.zeros((TILE, LANES), F32)
+    for pair in range(pairs):
+        wide = jnp.broadcast_to(total[pair], (TILE, LANES))
+        high = wide.astype(BF16).astype(F32)
+        tail = jnp.where(row == pair, high, jnp.where(row == pairs + pair, wide - high, tail))
+    ref[pairs * STATE :, :] = tail.astype(BF16)
 
 
 def state_kernel(x_hbm, b_hbm, dt_hbm, a_hbm, keep_ref, send_ref, *scratch):
@@ -108,18 +118,23 @@
     total = jnp.broadcast_to(total, cum.shape).T[0:1]
     loads[2].wait()
     loads[3].wait()
-    pairs = packed_ref.shape[0]
+    pairs = x_ref.shape[1] // LANES
+    half = pairs // 2
     groups = b_ref.shape[1] // STATE
+    totals, states = [], []
     for group in range(groups):
         turned = b_ref[:, group * STATE : (group + 1) * STATE].T
         for pair in range(group * pairs // groups, (group + 1) * pairs // groups):
             x_pair = x_ref[:, pair * LANES : (pair + 1) * LANES].astype(F32)
             weighted = (pair_lanes(tail, pair) * x_pair).astype(BF16)
             state = jnp.dot(turned, weighted, preferred_element_type=F32)
-            pack(packed_ref.at[pair : pair + 1], pair_lanes(total, pair)[None], state[None])
-    half = pairs // 2
-    keep_ref[...] = packed_ref[pl.ds(core_index() * half, half)]
-    send_ref[...] = packed_ref[pl.ds((1 - core_index()) * half, half)]
+            totals.append(pair_lanes(total, pair))
+            states.append(state)
+    for at in range(2):
+        span = slice(at * half, (at + 1) * half)
+        pack(packed_ref.at[at], totals[span], jnp.stack(states[span]))
+    keep_ref[...] = packed_ref[core_index()]
+    send_ref[...] = packed_ref[1 - core_index()]
 
 
 def chip_state_kernel(keep_ref, got_ref, out_ref):
@@ -273,11 +288,19 @@
         out[...] = product[shift * rows : (shift + 1) * rows].astype(BF16)
 
 
+def relay_kernel(own_ref, got_ref, out_ref):
+    got = jnp.where(core_index() == 1, got_ref[...].astype(F32), 0.0)
+    out_ref[...] = (own_ref[...].astype(F32) + got).astype(BF16)
+
+
 def rows_kernel(after_ref, resid_ref, gate_ref, gain_ref, *rest):
     parts, hidden_ref, rows_ref = rest[:-2], rest[-2], rest[-1]
     mixed = parts[0][...].astype(F32)
-    for part in parts[1:]:
-        mixed = mixed + part[...].astype(F32)
+    for at, part in enumerate(parts[1:]):
+        value = part[...].astype(F32)
+        if at == 0 and len(parts) == 4:
+            value = jnp.where(core_index() == 0, value, 0.0)
+        mixed = mixed + value
     hidden = (resid_ref[0].astype(F32) + mixed).astype(BF16)
     hidden_ref[...] = hidden
     value = hidden.astype(F32)
@@ -330,13 +353,13 @@
     return lax.ppermute(value, axis, [(i, i ^ mask) for i in range(size)])
 
 
-def swap_slot(value, slot, chip_mask=0):
+def swap_slot(value, slot):
     heads, size = lax.axis_size("head"), lax.axis_size("exp")
-    order = offsets(heads)
+    order = targets(heads)
     pairs = []
     for i in range(heads * size):
         head, exp = i // size, i % size
-        pairs.append((i, (head ^ order[exp % 2][slot]) * size + (exp ^ (2 * chip_mask))))
+        pairs.append((i, (head ^ order[exp % 2][slot]) * size + exp))
     return lax.ppermute(value, ("head", "exp"), pairs)
 
 
@@ -355,7 +378,7 @@
     half = pairs // 2
     dt_rows, a_row, d_row = dt_in.T, a_log[None], d_skip[None]
     dma = pltpu.SemaphoreType.DMA
-    packed = struct((half, STATE + TILE, LANES), BF16)
+    packed = struct((half * STATE + TILE, LANES), BF16)
 
     keep, send = call(
         state_kernel,
@@ -363,7 +386,7 @@
         [packed, packed],
         [(HBM, x_in), (HBM, b_in), (HBM, dt_rows), (HBM, a_row)],
         [pltpu.VMEM(x_in.shape, BF16), pltpu.VMEM(b_in.shape, BF16), pltpu.VMEM(dt_rows.shape, F32),
-         pltpu.VMEM(a_row.shape, F32), pltpu.VMEM((pairs, STATE + TILE, LANES), BF16), dma((4,))],
+         pltpu.VMEM(a_row.shape, F32), pltpu.VMEM((2, half * STATE + TILE, LANES), BF16), dma((4,))],
         megabytes=16,
     )
     local, grown, c_held = call(
@@ -433,7 +456,10 @@
         [dma((2,))],
     )
     slots = list(range(head_size - 1))
-    parts = [mixed[0]] + [swap_slot(mixed[k + 1], k) for k in slots]
+    parts, last = [swap_slot(mixed[k + 1], k) for k in slots[:-1]], mixed[-1]
+    if head_size == 4:
+        last = call(relay_kernel, "relay", struct((rows, model), BF16), [(VMEM, last), (VMEM, parts[0])])
+    parts = [mixed[0]] + parts + [swap_slot(last, slots[-1])]
     hidden, own_rows = call(
         rows_kernel,
         "rows",

time: 63.9 us -> 66.5 us (1.041)
  starting transfers between devices: 26.7 us -> 35.3 us
  waiting for transfers between devices: 18.3 us -> 12.1 us
    ppermute x20, starting transfers between devices: 22.2 us -> 28.3 us  [swap(): return lax.ppermute(value, axis, [(i, i ^ mask) for i in range(size)])]
    ppermute x20, waiting for transfers between devices: 13.9 us -> 10 us  [swap(): return lax.ppermute(value, axis, [(i, i ^ mask) for i in range(size)])]
    ppermute x3, starting transfers between devices: 4.45 us -> 7.05 us  [swap_slot(): return lax.ppermute(value, ('head', 'exp'), pairs)]
    ppermute x3, waiting for transfers between devices: 4.42 us -> 2.06 us  [swap_slot(): return lax.ppermute(value, ('head', 'exp'), pairs)]
    pallas_call x14 -> x15, Pallas kernels: 17.3 us -> 17.3 us  [call(): pl.pallas_call(kernel, out_shape=jax.tree.map(lambda out: pltpu.VMEM(out....]
  transfers between devices with their start and end apart: 23 -> 23, of which waited for: 14 -> 11; matrix products, arithmetic and copies ran while one was open for 2% -> 2% of each run, Pallas kernels for 17% -> 17%
where the time goes in v13:
time: 66.5 us; the launch traced here: 66.1 us
  starting transfers between devices  35.3 us (53%)
  Pallas kernels  17.3 us (26%)
  waiting for transfers between devices  12.1 us (18%)
  local copies, waits for them, and re-layouts  1.29 us (2%)
    ppermute x20, starting transfers between devices, swap(): return lax.ppermute(value, axis, [(i, i ^ mask) for i in range(size)])  28.3 us
    pallas_call x15, Pallas kernels, call(): pl.pallas_call(kernel, out_shape=jax.tree.map(lambda out: pltpu.VMEM(out....  17.3 us
    ppermute x20, waiting for transfers between devices, swap(): return lax.ppermute(value, axis, [(i, i ^ mask) for i in range(size)])  10 us
    ppermute x3, starting transfers between devices, swap_slot(): return lax.ppermute(value, ('head', 'exp'), pairs)  7.05 us
    ppermute x3, waiting for transfers between devices, swap_slot(): return lax.ppermute(value, ('head', 'exp'), pairs)  2.06 us
  transfers between devices with their start and end apart: 23, of which 11 were waited for; matrix products, arithmetic and copies ran while one was open for 2% of the time, Pallas kernels for 17%

profile of v13, /device:TPU:0, one launch (start us, length us, event | category | flops | bytes accessed | tf_op | source)
XLA Modules:
  0.0 66.1 jit_solution(15455965728081588528)
XLA Ops:
  0.0 1.8 %state.1 = (bf16[528,128]{1,0:T(8,128)(2,1)S(1)}, bf16[528,128]{1,0:T(8,128)(2,1)S(1)}) custom-call(bf16[128,1024]{1,0:T(8,128)(2,1)} %x_hbm.3, bf16[128,256]{1,0:T(8,128)(2,1)} %b_hbm.3, f32[16,128]{1,0:T(8,128)} %bitcast.11, f32[1,16]{1,0:T(1,128)} %bitcast.16), custom_call_target="tpu_custom_call" | custom-call | tf_op jit(solution)/shard_map/state/pallas_call | solution.py:29
  1.8 0.5 collective-permute-start
  2.3 1.0 %collective-permute-done.got_ref = bf16[528,128]{1,0:T(8,128)(2,1)S(1)} collective-permute-done((bf16[528,128]{1,0:T(8,128)(2,1)S(1)}, bf16[528,128]{1,0:T(8,128)(2,1)S(1)}, u32[]{:S(2)}, u32[]{:S(2)}) %collective-permute-start) | collective-permute-done | bytes 135200 | tf_op jit(solution)/shard_map/ppermute | solution.py:353
  3.3 0.1 chip_state.1.rest_0_
  3.4 0.4 collective-permute-start.1
  3.9 0.1 collective-permute-start.2
  4.0 2.9 %collective-permute-start.3 = (bf16[528,128]{1,0:T(8,128)(2,1)S(1)}, bf16[528,128]{1,0:T(8,128)(2,1)S(1)}, u32[]{:S(2)}, u32[]{:S(2)}) collective-permute-start(bf16[528,128]{1,0:T(8,128)(2,1)S(1)} %chip_state.1.rest_0_), channel_id=1, source_target_pairs={{0,2},{1,3},{2,0},{3,1},{4,6},{5,7},{6,4},{7,5},{8,10},{9,11},{10,... | collective-permute-start | bytes 405512 | tf_op jit(solution)/shard_map/ppermute | solution.py:353
  6.9 2.4 %inside.1 = (f32[128,1024]{1,0:T(8,128)S(1)}, f32[128,1024]{1,0:T(8,128)S(1)}, bf16[128,256]{1,0:T(8,128)(2,1)S(1)}) custom-call(bf16[128,1024]{1,0:T(8,128)(2,1)} %x_hbm.3, bf16[128,1024]{1,0:T(8,128)(2,1)} %z_hbm.1, bf16[128,256]{1,0:T(8,128)(2,1)} %b_hbm.3, bf16[128,256]{1,0:T(8,128)(2,1)} %c_hbm.1, f32[16,128]{1,0:T(8,128)} %bitcast.12, ...), custom_call_target="tpu_custom_call" | custom-call | tf_op jit(solution)/shard_map/inside/pallas_call | solution.py:29
  9.3 1.4 %collective-permute-done.3.rest_1_ = bf16[528,128]{1,0:T(8,128)(2,1)S(1)} collective-permute-done((bf16[528,128]{1,0:T(8,128)(2,1)S(1)}, bf16[528,128]{1,0:T(8,128)(2,1)S(1)}, u32[]{:S(2)}, u32[]{:S(2)}) %collective-permute-start.3) | collective-permute-done | bytes 135200 | tf_op jit(solution)/shard_map/ppermute | solution.py:353
  10.8 0.1 span.1.rest_2_
  10.9 1.8 %collective-permute-start.4 = (bf16[528,128]{1,0:T(8,128)(2,1)S(1)}, bf16[528,128]{1,0:T(8,128)(2,1)S(1)}, u32[]{:S(2)}, u32[]{:S(2)}) collective-permute-start(bf16[528,128]{1,0:T(8,128)(2,1)S(1)} %span.1.rest_2_), channel_id=1, source_target_pairs={{0,16},{16,0},{1,17},{17,1},{2,18},{18,2},{3,19},{19,3},{4,20},{20... | collective-permute-start | bytes 405512 | tf_op jit(solution)/shard_map/ppermute | solution.py:353
  12.7 1.3 %broadcast_in_dim.14.gain_hbm = f32[1,1344]{1,0:T(1,128)} reshape(f32[1344]{0:T(1024)} %param.27) | data formatting | bytes 10752 | tf_op jit(solution)/shard_map/broadcast_in_dim | solution.py:408
  14.0 1.9 %prep.1 = (bf16[32,128]{1,0:T(8,128)(2,1)S(1)}, bf16[1,32,1344]{2,1,0:T(8,128)(2,1)S(1)}, f32[1,1344]{1,0:T(1,128)S(1)}, f32[1,1024]{1,0:T(1,128)S(1)}, bf16[1344,1024]{1,0:T(8,128)(2,1)S(1)}) custom-call(bf16[1,32,1344]{2,1,0:T(8,128)(2,1)} %resid_hbm.1, s32[6,1,32]{2,1,0:T(1,128)} %bitcast.14, f32[6,1,32]{2,1,0:T(1,128)} %bitcast.15, ...), custom_call_target="tpu_custom_call" | custom-call | tf_op jit(solution)/shard_map/prep/pallas_call | solution.py:29
  15.9 0.2 collective-permute-done.4.rest_3_
  16.1 0.3 before.1
  16.4 0.1 collective-permute-start.5
  16.4 0.8 %first_half.1.first_ref = f32[128,1344]{1,0:T(8,128)S(1)} custom-call(f32[128,1024]{1,0:T(8,128)S(1)} %get-tuple-element.51.local_ref, f32[128,1024]{1,0:T(8,128)S(1)} %get-tuple-element.52.grown_ref, bf16[128,256]{1,0:T(8,128)(2,1)S(1)} %get-tuple-element.53.after_ref.c_ref, f32[1,1024]{1,0:T(1,128)S(1)} %get-tuple-element.54.norm_ref, ...), custom_call_target="tpu_custom_call" | custom-call | tf_op jit(solution)/shard_map/first_half/pallas_call | solution.py:29
  17.3 0.5 collective-permute-done.5.got_ref
  17.8 0.9 %mixed.1 = (bf16[32,1344]{1,0:T(8,128)(2,1)S(1)}, bf16[32,1344]{1,0:T(8,128)(2,1)S(1)}, bf16[32,1344]{1,0:T(8,128)(2,1)S(1)}, bf16[32,1344]{1,0:T(8,128)(2,1)S(1)}) custom-call(bf16[1,928,1344]{2,1,0:T(8,128)(2,1)S(1)} %collective-permute-done.1.after_up.other_up_ref, bf16[1,928,1344]{2,1,0:T(8,128)(2,1)S(1)} %collective-permute-done.2.after_down.other_down_ref, ...), custom_call_target="tpu_custom_call" | custom-call | tf_op jit(solution)/shard_map/mixed/pallas_call | solution.py:29
  18.6 2.8 %collective-permute-start.6 = (bf16[32,1344]{1,0:T(8,128)(2,1)S(1)}, bf16[32,1344]{1,0:T(8,128)(2,1)S(1)}, u32[]{:S(2)}, u32[]{:S(2)}) collective-permute-start(bf16[32,1344]{1,0:T(8,128)(2,1)S(1)} %get-tuple-element.64), channel_id=1, source_target_pairs={{0,8},{1,5},{2,10},{3,7},{4,12},{5,1},{6,14},{7,3},{8,0},{9,13},{1... | collective-permute-start | bytes 258056 | tf_op jit(solution)/shard_map/ppermute | solution.py:363
  21.4 1.4 %collective-permute-start.7 = (bf16[32,1344]{1,0:T(8,128)(2,1)S(1)}, bf16[32,1344]{1,0:T(8,128)(2,1)S(1)}, u32[]{:S(2)}, u32[]{:S(2)}) collective-permute-start(bf16[32,1344]{1,0:T(8,128)(2,1)S(1)} %get-tuple-element.65), channel_id=1, source_target_pairs={{0,12},{1,5},{2,14},{3,7},{4,8},{5,1},{6,10},{7,3},{8,4},{9,13},{1... | collective-permute-start | bytes 258056 | tf_op jit(solution)/shard_map/ppermute | solution.py:363
  22.8 1.5 %collective-permute-done.6.got_ref.rest_1_ = bf16[32,1344]{1,0:T(8,128)(2,1)S(1)} collective-permute-done((bf16[32,1344]{1,0:T(8,128)(2,1)S(1)}, bf16[32,1344]{1,0:T(8,128)(2,1)S(1)}, u32[]{:S(2)}, u32[]{:S(2)}) %collective-permute-start.6) | collective-permute-done | bytes 86048 | tf_op jit(solution)/shard_map/ppermute | solution.py:363
  24.3 2.9 %collective-permute-start.8 = (bf16[32,1344]{1,0:T(8,128)(2,1)S(1)}, bf16[32,1344]{1,0:T(8,128)(2,1)S(1)}, u32[]{:S(2)}, u32[]{:S(2)}) collective-permute-start(bf16[32,1344]{1,0:T(8,128)(2,1)S(1)} %relay.1), channel_id=1, source_target_pairs={{0,4},{1,9},{2,6},{3,11},{4,0},{5,13},{6,2},{7,15},{8,12},{9,1},{1... | collective-permute-start | bytes 258056 | tf_op jit(solution)/shard_map/ppermute | solution.py:363
  27.2 2.5 %weights.1 = (bf16[1,928,1344]{2,1,0:T(8,128)(2,1)S(1)}, bf16[1,928,1344]{2,1,0:T(8,128)(2,1)S(1)}) custom-call(bf16[32,1344]{1,0:T(8,128)(2,1)S(1)} %get-tuple-element.60.after_ref.rest_0_, bf16[1,928,1344]{2,1,0:T(8,128)(2,1)} %bitcast.10, bf16[1,928,1344]{2,1,0:T(8,128)(2,1)} %down_hbm.1), custom_call_target="tpu_custom_call" | custom-call | tf_op jit(solution)/shard_map/weights/pallas_call | solution.py:29
  29.8 0.6 collective-permute-done.8.rest_3_
  30.4 0.2 rows.1
  30.6 3.8 %collective-permute-start.12 = (bf16[32,1408]{1,0:T(8,128)(2,1)S(1)}, bf16[32,1408]{1,0:T(8,128)(2,1)S(1)}, u32[]{:S(2)}, u32[]{:S(2)}) collective-permute-start(bf16[32,1408]{1,0:T(8,128)(2,1)S(1)} %get-tuple-element.69.rest_0_), channel_id=1, source_target_pairs={{0,8},{4,12},{8,0},{12,4},{1,9},{5,13},{9,1},{13,5},{2,10},{6,14},... | collective-permute-start | bytes 270344 | tf_op jit(solution)/shard_map/ppermute | solution.py:353
  34.4 3.2 %collective-permute-start.11 = (bf16[32,1408]{1,0:T(8,128)(2,1)S(1)}, bf16[32,1408]{1,0:T(8,128)(2,1)S(1)}, u32[]{:S(2)}, u32[]{:S(2)}) collective-permute-start(bf16[32,1408]{1,0:T(8,128)(2,1)S(1)} %get-tuple-element.69.rest_0_), channel_id=1, source_target_pairs={{0,6},{1,7},{2,4},{3,5},{4,2},{5,3},{6,0},{7,1},{8,14},{9,15},{10,... | collective-permute-start | bytes 270344 | tf_op jit(solution)/shard_map/ppermute | solution.py:353
  37.6 0.6 collective-permute-start.9
  38.2 2.9 %collective-permute-start.15 = (bf16[32,1408]{1,0:T(8,128)(2,1)S(1)}, bf16[32,1408]{1,0:T(8,128)(2,1)S(1)}, u32[]{:S(2)}, u32[]{:S(2)}) collective-permute-start(bf16[32,1408]{1,0:T(8,128)(2,1)S(1)} %collective-permute-done.12.rest_0_), channel_id=1, source_target_pairs={{0,6},{1,7},{2,4},{3,5},{4,2},{5,3},{6,0},{7,1},{8,14},{9,15},{10,... | collective-permute-start | bytes 270344 | tf_op jit(solution)/shard_map/ppermute | solution.py:353
  41.1 1.3 %collective-permute-start.13 = (bf16[32,1408]{1,0:T(8,128)(2,1)S(1)}, bf16[32,1408]{1,0:T(8,128)(2,1)S(1)}, u32[]{:S(2)}, u32[]{:S(2)}) collective-permute-start(bf16[32,1408]{1,0:T(8,128)(2,1)S(1)} %collective-permute-done.12.rest_0_), channel_id=1, source_target_pairs={{0,2},{1,3},{2,0},{3,1},{4,6},{5,7},{6,4},{7,5},{8,10},{9,11},{10,... | collective-permute-start | bytes 270344 | tf_op jit(solution)/shard_map/ppermute | solution.py:353
  42.4 0.4 collective-permute-done.10.rest_2_
  42.7 2.7 %experts.2 = (bf16[32,1344]{1,0:T(8,128)(2,1)S(1)}, bf16[32,1344]{1,0:T(8,128)(2,1)S(1)}, bf16[32,1344]{1,0:T(8,128)(2,1)S(1)}, bf16[32,1344]{1,0:T(8,128)(2,1)S(1)}) custom-call(bf16[1,928,1344]{2,1,0:T(8,128)(2,1)S(1)} %get-tuple-element.61.after_ref.up_ref, bf16[1,928,1344]{2,1,0:T(8,128)(2,1)S(1)} %get-tuple-element.68.down_ref, ...), custom_call_target="tpu_custom_call" | custom-call | tf_op jit(solution)/shard_map/experts/pallas_call | solution.py:29
  45.5 0.2 collective-permute-done.14.rest_2_
  45.6 0.0 collective-permute-done.13.rest_1_
  45.6 2.7 %experts.3 = (bf16[32,1344]{1,0:T(8,128)(2,1)S(1)}, bf16[32,1344]{1,0:T(8,128)(2,1)S(1)}, bf16[32,1344]{1,0:T(8,128)(2,1)S(1)}, bf16[32,1344]{1,0:T(8,128)(2,1)S(1)}) custom-call(bf16[1,928,1344]{2,1,0:T(8,128)(2,1)S(1)} %get-tuple-element.61.after_ref.up_ref, bf16[1,928,1344]{2,1,0:T(8,128)(2,1)S(1)} %get-tuple-element.68.down_ref, ...), custom_call_target="tpu_custom_call" | custom-call | tf_op jit(solution)/shard_map/experts/pallas_call | solution.py:29
  48.4 2.5 %collective-permute-start.16 = (bf16[32,1344]{1,0:T(8,128)(2,1)S(1)}, bf16[32,1344]{1,0:T(8,128)(2,1)S(1)}, u32[]{:S(2)}, u32[]{:S(2)}) collective-permute-start(bf16[32,1344]{1,0:T(8,128)(2,1)S(1)} %get-tuple-element.80), channel_id=1, source_target_pairs={{0,6},{1,7},{2,4},{3,5},{4,2},{5,3},{6,0},{7,1},{8,14},{9,15},{10,... | collective-permute-start | bytes 258056 | tf_op jit(solution)/shard_map/ppermute | solution.py:353
  50.8 0.4 collective-permute-start.17
  51.2 0.7 %collective-permute-start.18 = (bf16[32,1344]{1,0:T(8,128)(2,1)S(1)}, bf16[32,1344]{1,0:T(8,128)(2,1)S(1)}, u32[]{:S(2)}, u32[]{:S(2)}) collective-permute-start(bf16[32,1344]{1,0:T(8,128)(2,1)S(1)} %get-tuple-element.82), channel_id=1, source_target_pairs={{0,2},{1,3},{2,0},{3,1},{4,6},{5,7},{6,4},{7,5},{8,10},{9,11},{10,... | collective-permute-start | bytes 258056 | tf_op jit(solution)/shard_map/ppermute | solution.py:353
  51.9 2.4 %collective-permute-start.20 = (bf16[32,1344]{1,0:T(8,128)(2,1)S(1)}, bf16[32,1344]{1,0:T(8,128)(2,1)S(1)}, u32[]{:S(2)}, u32[]{:S(2)}) collective-permute-start(bf16[32,1344]{1,0:T(8,128)(2,1)S(1)} %get-tuple-element.86), channel_id=1, source_target_pairs={{0,6},{1,7},{2,4},{3,5},{4,2},{5,3},{6,0},{7,1},{8,14},{9,15},{10,... | collective-permute-start | bytes 258056 | tf_op jit(solution)/shard_map/ppermute | solution.py:353
  54.3 2.8 %collective-permute-done.17.refs_2_ = bf16[32,1344]{1,0:T(8,128)(2,1)S(1)} collective-permute-done((bf16[32,1344]{1,0:T(8,128)(2,1)S(1)}, bf16[32,1344]{1,0:T(8,128)(2,1)S(1)}, u32[]{:S(2)}, u32[]{:S(2)}) %collective-permute-start.17) | collective-permute-done | bytes 86048 | tf_op jit(solution)/shard_map/ppermute | solution.py:353
  57.1 0.1 sum.1
  57.2 1.7 %collective-permute-start.19 = (bf16[32,1344]{1,0:T(8,128)(2,1)S(1)}, bf16[32,1344]{1,0:T(8,128)(2,1)S(1)}, u32[]{:S(2)}, u32[]{:S(2)}) collective-permute-start(bf16[32,1344]{1,0:T(8,128)(2,1)S(1)} %sum.1), channel_id=1, source_target_pairs={{0,8},{4,12},{8,0},{12,4},{1,9},{5,13},{9,1},{13,5},{2,10},{6,14},... | collective-permute-start | bytes 258056 | tf_op jit(solution)/shard_map/ppermute | solution.py:353
  58.9 2.0 %collective-permute-start.21 = (bf16[32,1344]{1,0:T(8,128)(2,1)S(1)}, bf16[32,1344]{1,0:T(8,128)(2,1)S(1)}, u32[]{:S(2)}, u32[]{:S(2)}) collective-permute-start(bf16[32,1344]{1,0:T(8,128)(2,1)S(1)} %get-tuple-element.87), channel_id=1, source_target_pairs={{0,4},{1,5},{2,6},{3,7},{4,0},{5,1},{6,2},{7,3},{8,12},{9,13},{10,... | collective-permute-start | bytes 258056 | tf_op jit(solution)/shard_map/ppermute | solution.py:353
  60.9 1.0 %collective-permute-start.22 = (bf16[32,1344]{1,0:T(8,128)(2,1)S(1)}, bf16[32,1344]{1,0:T(8,128)(2,1)S(1)}, u32[]{:S(2)}, u32[]{:S(2)}) collective-permute-start(bf16[32,1344]{1,0:T(8,128)(2,1)S(1)} %get-tuple-element.88), channel_id=1, source_target_pairs={{0,2},{1,3},{2,0},{3,1},{4,6},{5,7},{6,4},{7,5},{8,10},{9,11},{10,... | collective-permute-start | bytes 258056 | tf_op jit(solution)/shard_map/ppermute | solution.py:353
  61.9 1.8 %collective-permute-done.19.rest_1_ = bf16[32,1344]{1,0:T(8,128)(2,1)S(1)} collective-permute-done((bf16[32,1344]{1,0:T(8,128)(2,1)S(1)}, bf16[32,1344]{1,0:T(8,128)(2,1)S(1)}, u32[]{:S(2)}, u32[]{:S(2)}) %collective-permute-start.19) | collective-permute-done | bytes 86048 | tf_op jit(solution)/shard_map/ppermute | solution.py:353
  63.6 1.8 %collective-permute-done.22.rest_4_ = bf16[32,1344]{1,0:T(8,128)(2,1)S(1)} collective-permute-done((bf16[32,1344]{1,0:T(8,128)(2,1)S(1)}, bf16[32,1344]{1,0:T(8,128)(2,1)S(1)}, u32[]{:S(2)}, u32[]{:S(2)}) %collective-permute-start.22) | collective-permute-done | bytes 86048 | tf_op jit(solution)/shard_map/ppermute | solution.py:353
  65.4 0.7 %last.1 = bf16[1,32,1344]{2,1,0:T(8,128)(2,1)} custom-call(bf16[32,1344]{1,0:T(8,128)(2,1)S(1)} %get-tuple-element.67.hidden_ref, bf16[32,1344]{1,0:T(8,128)(2,1)S(1)} %get-tuple-element.74.rest_0_, bf16[32,1344]{1,0:T(8,128)(2,1)S(1)} %collective-permute-done.19.rest_1_, bf16[32,1344]{1,0:T(8,128)(2,1)S(1)} %collective-permute-done.20.rest_2_, ...), custom_call_target="tpu_custom_call" | custom-call | tf_op jit(solution)/shard_map/last/pallas_call | solution.py:29
  (14 shorter events, 0.1 us)
Async XLA Ops:
  1.8 1.5 %collective-permute-start = (bf16[528,128]{1,0:T(8,128)(2,1)S(1)}, bf16[528,128]{1,0:T(8,128)(2,1)S(1)}, u32[]{:S(2)}, u32[]{:S(2)}) collective-permute-start(bf16[528,128]{1,0:T(8,128)(2,1)S(1)} %get-tuple-element.48), channel_id=1, source_target_pairs={{0,1},{1,0},{2,3},{3,2},{4,5},{5,4},{6,7},{7,6},{8,9},{9,8},{10,11... | collective-permute-start | bytes 405512 | tf_op jit(solution)/shard_map/ppermute | solution.py:353
  3.4 14.3 %collective-permute-start.1 = (bf16[1,928,1344]{2,1,0:T(8,128)(2,1)}, bf16[1,928,1344]{2,1,0:T(8,128)(2,1)S(1)}, u32[]{:S(2)}, u32[]{:S(2)}) collective-permute-start(bf16[1,928,1344]{2,1,0:T(8,128)(2,1)} %bitcast.9), channel_id=1, source_target_pairs={{0,1},{1,0},{2,3},{3,2},{4,5},{5,4},{6,7},{7,6},{8,9},{9,8},{10,11... | collective-permute-start | bytes 7483400 | tf_op jit(solution)/shard_map/ppermute | solution.py:353
  3.9 13.9 %collective-permute-start.2 = (bf16[1,928,1344]{2,1,0:T(8,128)(2,1)}, bf16[1,928,1344]{2,1,0:T(8,128)(2,1)S(1)}, u32[]{:S(2)}, u32[]{:S(2)}) collective-permute-start(bf16[1,928,1344]{2,1,0:T(8,128)(2,1)} %down_hbm.1), channel_id=1, source_target_pairs={{0,1},{1,0},{2,3},{3,2},{4,5},{5,4},{6,7},{7,6},{8,9},{9,8},{10,11... | collective-permute-start | bytes 7483400 | tf_op jit(solution)/shard_map/ppermute | solution.py:353
  4.0 6.8 %collective-permute-start.3 = (bf16[528,128]{1,0:T(8,128)(2,1)S(1)}, bf16[528,128]{1,0:T(8,128)(2,1)S(1)}, u32[]{:S(2)}, u32[]{:S(2)}) collective-permute-start(bf16[528,128]{1,0:T(8,128)(2,1)S(1)} %chip_state.1.rest_0_), channel_id=1, source_target_pairs={{0,2},{1,3},{2,0},{3,1},{4,6},{5,7},{6,4},{7,5},{8,10},{9,11},{10,... | collective-permute-start | bytes 405512 | tf_op jit(solution)/shard_map/ppermute | solution.py:353
  10.9 5.2 %collective-permute-start.4 = (bf16[528,128]{1,0:T(8,128)(2,1)S(1)}, bf16[528,128]{1,0:T(8,128)(2,1)S(1)}, u32[]{:S(2)}, u32[]{:S(2)}) collective-permute-start(bf16[528,128]{1,0:T(8,128)(2,1)S(1)} %span.1.rest_2_), channel_id=1, source_target_pairs={{0,16},{16,0},{1,17},{17,1},{2,18},{18,2},{3,19},{19,3},{4,20},{20... | collective-permute-start | bytes 405512 | tf_op jit(solution)/shard_map/ppermute | solution.py:353
  16.4 1.4 %collective-permute-start.5 = (bf16[4,128,128]{2,1,0:T(8,128)(2,1)S(1)}, bf16[4,128,128]{2,1,0:T(8,128)(2,1)S(1)}, u32[]{:S(2)}, u32[]{:S(2)}) collective-permute-start(bf16[4,128,128]{2,1,0:T(8,128)(2,1)S(1)} %get-tuple-element.58), channel_id=1, source_target_pairs={{0,1},{1,0},{2,3},{3,2},{4,5},{5,4},{6,7},{7,6},{8,9},{9,8},{10,11... | collective-permute-start | bytes 393224 | tf_op jit(solution)/shard_map/ppermute | solution.py:353
  18.6 5.6 %collective-permute-start.6 = (bf16[32,1344]{1,0:T(8,128)(2,1)S(1)}, bf16[32,1344]{1,0:T(8,128)(2,1)S(1)}, u32[]{:S(2)}, u32[]{:S(2)}) collective-permute-start(bf16[32,1344]{1,0:T(8,128)(2,1)S(1)} %get-tuple-element.64), channel_id=1, source_target_pairs={{0,8},{1,5},{2,10},{3,7},{4,12},{5,1},{6,14},{7,3},{8,0},{9,13},{1... | collective-permute-start | bytes 258056 | tf_op jit(solution)/shard_map/ppermute | solution.py:363
  21.4 8.4 %collective-permute-start.7 = (bf16[32,1344]{1,0:T(8,128)(2,1)S(1)}, bf16[32,1344]{1,0:T(8,128)(2,1)S(1)}, u32[]{:S(2)}, u32[]{:S(2)}) collective-permute-start(bf16[32,1344]{1,0:T(8,128)(2,1)S(1)} %get-tuple-element.65), channel_id=1, source_target_pairs={{0,12},{1,5},{2,14},{3,7},{4,8},{5,1},{6,10},{7,3},{8,4},{9,13},{1... | collective-permute-start | bytes 258056 | tf_op jit(solution)/shard_map/ppermute | solution.py:363
  24.3 6.1 %collective-permute-start.8 = (bf16[32,1344]{1,0:T(8,128)(2,1)S(1)}, bf16[32,1344]{1,0:T(8,128)(2,1)S(1)}, u32[]{:S(2)}, u32[]{:S(2)}) collective-permute-start(bf16[32,1344]{1,0:T(8,128)(2,1)S(1)} %relay.1), channel_id=1, source_target_pairs={{0,4},{1,9},{2,6},{3,11},{4,0},{5,13},{6,2},{7,15},{8,12},{9,1},{1... | collective-permute-start | bytes 258056 | tf_op jit(solution)/shard_map/ppermute | solution.py:363
  30.6 7.6 %collective-permute-start.12 = (bf16[32,1408]{1,0:T(8,128)(2,1)S(1)}, bf16[32,1408]{1,0:T(8,128)(2,1)S(1)}, u32[]{:S(2)}, u32[]{:S(2)}) collective-permute-start(bf16[32,1408]{1,0:T(8,128)(2,1)S(1)} %get-tuple-element.69.rest_0_), channel_id=1, source_target_pairs={{0,8},{4,12},{8,0},{12,4},{1,9},{5,13},{9,1},{13,5},{2,10},{6,14},... | collective-permute-start | bytes 270344 | tf_op jit(solution)/shard_map/ppermute | solution.py:353
  34.4 6.7 %collective-permute-start.11 = (bf16[32,1408]{1,0:T(8,128)(2,1)S(1)}, bf16[32,1408]{1,0:T(8,128)(2,1)S(1)}, u32[]{:S(2)}, u32[]{:S(2)}) collective-permute-start(bf16[32,1408]{1,0:T(8,128)(2,1)S(1)} %get-tuple-element.69.rest_0_), channel_id=1, source_target_pairs={{0,6},{1,7},{2,4},{3,5},{4,2},{5,3},{6,0},{7,1},{8,14},{9,15},{10,... | collective-permute-start | bytes 270344 | tf_op jit(solution)/shard_map/ppermute | solution.py:353
  37.6 5.1 %collective-permute-start.10 = (bf16[32,1408]{1,0:T(8,128)(2,1)S(1)}, bf16[32,1408]{1,0:T(8,128)(2,1)S(1)}, u32[]{:S(2)}, u32[]{:S(2)}) collective-permute-start(bf16[32,1408]{1,0:T(8,128)(2,1)S(1)} %get-tuple-element.69.rest_0_), channel_id=1, source_target_pairs={{0,4},{1,5},{2,6},{3,7},{4,0},{5,1},{6,2},{7,3},{8,12},{9,13},{10,... | collective-permute-start | bytes 270344 | tf_op jit(solution)/shard_map/ppermute | solution.py:353
  37.6 5.1 %collective-permute-start.9 = (bf16[32,1408]{1,0:T(8,128)(2,1)S(1)}, bf16[32,1408]{1,0:T(8,128)(2,1)S(1)}, u32[]{:S(2)}, u32[]{:S(2)}) collective-permute-start(bf16[32,1408]{1,0:T(8,128)(2,1)S(1)} %get-tuple-element.69.rest_0_), channel_id=1, source_target_pairs={{0,2},{1,3},{2,0},{3,1},{4,6},{5,7},{6,4},{7,5},{8,10},{9,11},{10,... | collective-permute-start | bytes 270344 | tf_op jit(solution)/shard_map/ppermute | solution.py:353
  38.2 7.2 %collective-permute-start.15 = (bf16[32,1408]{1,0:T(8,128)(2,1)S(1)}, bf16[32,1408]{1,0:T(8,128)(2,1)S(1)}, u32[]{:S(2)}, u32[]{:S(2)}) collective-permute-start(bf16[32,1408]{1,0:T(8,128)(2,1)S(1)} %collective-permute-done.12.rest_0_), channel_id=1, source_target_pairs={{0,6},{1,7},{2,4},{3,5},{4,2},{5,3},{6,0},{7,1},{8,14},{9,15},{10,... | collective-permute-start | bytes 270344 | tf_op jit(solution)/shard_map/ppermute | solution.py:353
  41.1 4.5 %collective-permute-start.14 = (bf16[32,1408]{1,0:T(8,128)(2,1)S(1)}, bf16[32,1408]{1,0:T(8,128)(2,1)S(1)}, u32[]{:S(2)}, u32[]{:S(2)}) collective-permute-start(bf16[32,1408]{1,0:T(8,128)(2,1)S(1)} %collective-permute-done.12.rest_0_), channel_id=1, source_target_pairs={{0,4},{1,5},{2,6},{3,7},{4,0},{5,1},{6,2},{7,3},{8,12},{9,13},{10,... | collective-permute-start | bytes 270344 | tf_op jit(solution)/shard_map/ppermute | solution.py:353
  41.1 4.5 %collective-permute-start.13 = (bf16[32,1408]{1,0:T(8,128)(2,1)S(1)}, bf16[32,1408]{1,0:T(8,128)(2,1)S(1)}, u32[]{:S(2)}, u32[]{:S(2)}) collective-permute-start(bf16[32,1408]{1,0:T(8,128)(2,1)S(1)} %collective-permute-done.12.rest_0_), channel_id=1, source_target_pairs={{0,2},{1,3},{2,0},{3,1},{4,6},{5,7},{6,4},{7,5},{8,10},{9,11},{10,... | collective-permute-start | bytes 270344 | tf_op jit(solution)/shard_map/ppermute | solution.py:353
  48.4 6.0 %collective-permute-start.16 = (bf16[32,1344]{1,0:T(8,128)(2,1)S(1)}, bf16[32,1344]{1,0:T(8,128)(2,1)S(1)}, u32[]{:S(2)}, u32[]{:S(2)}) collective-permute-start(bf16[32,1344]{1,0:T(8,128)(2,1)S(1)} %get-tuple-element.80), channel_id=1, source_target_pairs={{0,6},{1,7},{2,4},{3,5},{4,2},{5,3},{6,0},{7,1},{8,14},{9,15},{10,... | collective-permute-start | bytes 258056 | tf_op jit(solution)/shard_map/ppermute | solution.py:353
  50.8 6.3 %collective-permute-start.17 = (bf16[32,1344]{1,0:T(8,128)(2,1)S(1)}, bf16[32,1344]{1,0:T(8,128)(2,1)S(1)}, u32[]{:S(2)}, u32[]{:S(2)}) collective-permute-start(bf16[32,1344]{1,0:T(8,128)(2,1)S(1)} %get-tuple-element.81), channel_id=1, source_target_pairs={{0,4},{1,5},{2,6},{3,7},{4,0},{5,1},{6,2},{7,3},{8,12},{9,13},{10,... | collective-permute-start | bytes 258056 | tf_op jit(solution)/shard_map/ppermute | solution.py:353
  51.2 5.9 %collective-permute-start.18 = (bf16[32,1344]{1,0:T(8,128)(2,1)S(1)}, bf16[32,1344]{1,0:T(8,128)(2,1)S(1)}, u32[]{:S(2)}, u32[]{:S(2)}) collective-permute-start(bf16[32,1344]{1,0:T(8,128)(2,1)S(1)} %get-tuple-element.82), channel_id=1, source_target_pairs={{0,2},{1,3},{2,0},{3,1},{4,6},{5,7},{6,4},{7,5},{8,10},{9,11},{10,... | collective-permute-start | bytes 258056 | tf_op jit(solution)/shard_map/ppermute | solution.py:353
  51.9 10.0 %collective-permute-start.20 = (bf16[32,1344]{1,0:T(8,128)(2,1)S(1)}, bf16[32,1344]{1,0:T(8,128)(2,1)S(1)}, u32[]{:S(2)}, u32[]{:S(2)}) collective-permute-start(bf16[32,1344]{1,0:T(8,128)(2,1)S(1)} %get-tuple-element.86), channel_id=1, source_target_pairs={{0,6},{1,7},{2,4},{3,5},{4,2},{5,3},{6,0},{7,1},{8,14},{9,15},{10,... | collective-permute-start | bytes 258056 | tf_op jit(solution)/shard_map/ppermute | solution.py:353
  57.2 6.5 %collective-permute-start.19 = (bf16[32,1344]{1,0:T(8,128)(2,1)S(1)}, bf16[32,1344]{1,0:T(8,128)(2,1)S(1)}, u32[]{:S(2)}, u32[]{:S(2)}) collective-permute-start(bf16[32,1344]{1,0:T(8,128)(2,1)S(1)} %sum.1), channel_id=1, source_target_pairs={{0,8},{4,12},{8,0},{12,4},{1,9},{5,13},{9,1},{13,5},{2,10},{6,14},... | collective-permute-start | bytes 258056 | tf_op jit(solution)/shard_map/ppermute | solution.py:353
  58.9 4.8 %collective-permute-start.21 = (bf16[32,1344]{1,0:T(8,128)(2,1)S(1)}, bf16[32,1344]{1,0:T(8,128)(2,1)S(1)}, u32[]{:S(2)}, u32[]{:S(2)}) collective-permute-start(bf16[32,1344]{1,0:T(8,128)(2,1)S(1)} %get-tuple-element.87), channel_id=1, source_target_pairs={{0,4},{1,5},{2,6},{3,7},{4,0},{5,1},{6,2},{7,3},{8,12},{9,13},{10,... | collective-permute-start | bytes 258056 | tf_op jit(solution)/shard_map/ppermute | solution.py:353
  60.9 4.5 %collective-permute-start.22 = (bf16[32,1344]{1,0:T(8,128)(2,1)S(1)}, bf16[32,1344]{1,0:T(8,128)(2,1)S(1)}, u32[]{:S(2)}, u32[]{:S(2)}) collective-permute-start(bf16[32,1344]{1,0:T(8,128)(2,1)S(1)} %get-tuple-element.88), channel_id=1, source_target_pairs={{0,2},{1,3},{2,0},{3,1},{4,6},{5,7},{6,4},{7,5},{8,10},{9,11},{10,... | collective-permute-start | bytes 258056 | tf_op jit(solution)/shard_map/ppermute | solution.py:353

commit v14 on v13

--- a/solution.py
+++ b/solution.py
@@ -39,11 +39,11 @@
 
 def offsets(count):
     down = list(range(count - 1, 0, -1))
-    return [[2, 3, 1], [3, 1, 2]] if count == 4 else [down, down]
+    return [[3, 1, 2], [2, 3, 1]] if count == 4 else [down, down]
 
 
 def targets(count):
-    return [[2, 3, 1], [1, 1, 2]] if count == 4 else offsets(count)
+    return [[1, 1, 2], [2, 3, 1]] if count == 4 else offsets(count)
 
 
 def head_offset(slot, count):
@@ -289,7 +289,7 @@
 
 
 def relay_kernel(own_ref, got_ref, out_ref):
-    got = jnp.where(core_index() == 1, got_ref[...].astype(F32), 0.0)
+    got = jnp.where(core_index() == 0, got_ref[...].astype(F32), 0.0)
     out_ref[...] = (own_ref[...].astype(F32) + got).astype(BF16)
 
 
@@ -299,7 +299,7 @@
     for at, part in enumerate(parts[1:]):
         value = part[...].astype(F32)
         if at == 0 and len(parts) == 4:
-            value = jnp.where(core_index() == 0, value, 0.0)
+            value = jnp.where(core_index() == 1, value, 0.0)
         mixed = mixed + value
     hidden = (resid_ref[0].astype(F32) + mixed).astype(BF16)
     hidden_ref[...] = hidden

time: 66.5 us -> 62.7 us (0.943)
  starting transfers between devices: 35.3 us -> 29.3 us
  waiting for transfers between devices: 12.1 us -> 14.2 us
    ppermute x3, starting transfers between devices: 7.05 us -> 3.92 us  [swap_slot(): return lax.ppermute(value, ('head', 'exp'), pairs)]
    ppermute x20, starting transfers between devices: 28.3 us -> 25.4 us  [swap(): return lax.ppermute(value, axis, [(i, i ^ mask) for i in range(size)])]
    ppermute x3, waiting for transfers between devices: 2.06 us -> 4.58 us  [swap_slot(): return lax.ppermute(value, ('head', 'exp'), pairs)]
  transfers between devices with their start and end apart: 23 -> 23, of which waited for: 11 -> 14; matrix products, arithmetic and copies ran while one was open for 2% -> 2% of each run, Pallas kernels for 17% -> 18%
where the time goes in v14:
time: 62.7 us; the launch traced here: 62.3 us
  starting transfers between devices  29.3 us (47%)
  Pallas kernels  17.3 us (28%)
  waiting for transfers between devices  14.2 us (23%)
  local copies, waits for them, and re-layouts  1.29 us (2%)
    ppermute x20, starting transfers between devices, swap(): return lax.ppermute(value, axis, [(i, i ^ mask) for i in range(size)])  25.4 us
    pallas_call x15, Pallas kernels, call(): pl.pallas_call(kernel, out_shape=jax.tree.map(lambda out: pltpu.VMEM(out....  17.3 us
    ppermute x20, waiting for transfers between devices, swap(): return lax.ppermute(value, axis, [(i, i ^ mask) for i in range(size)])  9.65 us
    ppermute x3, waiting for transfers between devices, swap_slot(): return lax.ppermute(value, ('head', 'exp'), pairs)  4.58 us
    ppermute x3, starting transfers between devices, swap_slot(): return lax.ppermute(value, ('head', 'exp'), pairs)  3.92 us
    broadcast_in_dim x1, local copies, waits for them, and re-layouts, per_device(): moe_gain[None]  1.29 us
  transfers between devices with their start and end apart: 23, of which 14 were waited for; matrix products, arithmetic and copies ran while one was open for 2% of the time, Pallas kernels for 18%

profile of v14, /device:TPU:0, one launch (start us, length us, event | category | flops | bytes accessed | tf_op | source)
XLA Modules:
  0.0 62.3 jit_solution(15659412757720081683)
XLA Ops:
  0.0 1.8 %state.1 = (bf16[528,128]{1,0:T(8,128)(2,1)S(1)}, bf16[528,128]{1,0:T(8,128)(2,1)S(1)}) custom-call(bf16[128,1024]{1,0:T(8,128)(2,1)} %x_hbm.3, bf16[128,256]{1,0:T(8,128)(2,1)} %b_hbm.3, f32[16,128]{1,0:T(8,128)} %bitcast.11, f32[1,16]{1,0:T(1,128)} %bitcast.16), custom_call_target="tpu_custom_call" | custom-call | tf_op jit(solution)/shard_map/state/pallas_call | solution.py:29
  1.8 0.5 collective-permute-start
  2.3 1.0 %collective-permute-done.got_ref = bf16[528,128]{1,0:T(8,128)(2,1)S(1)} collective-permute-done((bf16[528,128]{1,0:T(8,128)(2,1)S(1)}, bf16[528,128]{1,0:T(8,128)(2,1)S(1)}, u32[]{:S(2)}, u32[]{:S(2)}) %collective-permute-start) | collective-permute-done | bytes 135200 | tf_op jit(solution)/shard_map/ppermute | solution.py:353
  3.3 0.1 chip_state.1.rest_0_
  3.4 0.4 collective-permute-start.1
  3.9 0.1 collective-permute-start.2
  4.0 2.9 %collective-permute-start.3 = (bf16[528,128]{1,0:T(8,128)(2,1)S(1)}, bf16[528,128]{1,0:T(8,128)(2,1)S(1)}, u32[]{:S(2)}, u32[]{:S(2)}) collective-permute-start(bf16[528,128]{1,0:T(8,128)(2,1)S(1)} %chip_state.1.rest_0_), channel_id=1, source_target_pairs={{0,2},{1,3},{2,0},{3,1},{4,6},{5,7},{6,4},{7,5},{8,10},{9,11},{10,... | collective-permute-start | bytes 405512 | tf_op jit(solution)/shard_map/ppermute | solution.py:353
  6.9 2.4 %inside.1 = (f32[128,1024]{1,0:T(8,128)S(1)}, f32[128,1024]{1,0:T(8,128)S(1)}, bf16[128,256]{1,0:T(8,128)(2,1)S(1)}) custom-call(bf16[128,1024]{1,0:T(8,128)(2,1)} %x_hbm.3, bf16[128,1024]{1,0:T(8,128)(2,1)} %z_hbm.1, bf16[128,256]{1,0:T(8,128)(2,1)} %b_hbm.3, bf16[128,256]{1,0:T(8,128)(2,1)} %c_hbm.1, f32[16,128]{1,0:T(8,128)} %bitcast.12, ...), custom_call_target="tpu_custom_call" | custom-call | tf_op jit(solution)/shard_map/inside/pallas_call | solution.py:29
  9.3 1.4 %collective-permute-done.3.rest_1_ = bf16[528,128]{1,0:T(8,128)(2,1)S(1)} collective-permute-done((bf16[528,128]{1,0:T(8,128)(2,1)S(1)}, bf16[528,128]{1,0:T(8,128)(2,1)S(1)}, u32[]{:S(2)}, u32[]{:S(2)}) %collective-permute-start.3) | collective-permute-done | bytes 135200 | tf_op jit(solution)/shard_map/ppermute | solution.py:353
  10.8 0.1 span.1.rest_2_
  10.9 1.8 %collective-permute-start.4 = (bf16[528,128]{1,0:T(8,128)(2,1)S(1)}, bf16[528,128]{1,0:T(8,128)(2,1)S(1)}, u32[]{:S(2)}, u32[]{:S(2)}) collective-permute-start(bf16[528,128]{1,0:T(8,128)(2,1)S(1)} %span.1.rest_2_), channel_id=1, source_target_pairs={{0,16},{16,0},{1,17},{17,1},{2,18},{18,2},{3,19},{19,3},{4,20},{20... | collective-permute-start | bytes 405512 | tf_op jit(solution)/shard_map/ppermute | solution.py:353
  12.7 1.3 %broadcast_in_dim.14.gain_hbm = f32[1,1344]{1,0:T(1,128)} reshape(f32[1344]{0:T(1024)} %param.27) | data formatting | bytes 10752 | tf_op jit(solution)/shard_map/broadcast_in_dim | solution.py:408
  14.0 1.9 %prep.1 = (bf16[32,128]{1,0:T(8,128)(2,1)S(1)}, bf16[1,32,1344]{2,1,0:T(8,128)(2,1)S(1)}, f32[1,1344]{1,0:T(1,128)S(1)}, f32[1,1024]{1,0:T(1,128)S(1)}, bf16[1344,1024]{1,0:T(8,128)(2,1)S(1)}) custom-call(bf16[1,32,1344]{2,1,0:T(8,128)(2,1)} %resid_hbm.1, s32[6,1,32]{2,1,0:T(1,128)} %bitcast.14, f32[6,1,32]{2,1,0:T(1,128)} %bitcast.15, ...), custom_call_target="tpu_custom_call" | custom-call | tf_op jit(solution)/shard_map/prep/pallas_call | solution.py:29
  15.9 0.2 collective-permute-done.4.rest_3_
  16.1 0.3 before.1
  16.4 0.8 %first_half.1.first_ref = f32[128,1344]{1,0:T(8,128)S(1)} custom-call(f32[128,1024]{1,0:T(8,128)S(1)} %get-tuple-element.51.local_ref, f32[128,1024]{1,0:T(8,128)S(1)} %get-tuple-element.52.grown_ref, bf16[128,256]{1,0:T(8,128)(2,1)S(1)} %get-tuple-element.53.after_ref.c_ref, f32[1,1024]{1,0:T(1,128)S(1)} %get-tuple-element.54.norm_ref, ...), custom_call_target="tpu_custom_call" | custom-call | tf_op jit(solution)/shard_map/first_half/pallas_call | solution.py:29
  17.3 0.5 collective-permute-done.5.got_ref
  17.8 0.9 %mixed.1 = (bf16[32,1344]{1,0:T(8,128)(2,1)S(1)}, bf16[32,1344]{1,0:T(8,128)(2,1)S(1)}, bf16[32,1344]{1,0:T(8,128)(2,1)S(1)}, bf16[32,1344]{1,0:T(8,128)(2,1)S(1)}) custom-call(bf16[1,928,1344]{2,1,0:T(8,128)(2,1)S(1)} %collective-permute-done.1.after_up.other_up_ref, bf16[1,928,1344]{2,1,0:T(8,128)(2,1)S(1)} %collective-permute-done.2.after_down.other_down_ref, ...), custom_call_target="tpu_custom_call" | custom-call | tf_op jit(solution)/shard_map/mixed/pallas_call | solution.py:29
  18.6 1.8 %collective-permute-start.6 = (bf16[32,1344]{1,0:T(8,128)(2,1)S(1)}, bf16[32,1344]{1,0:T(8,128)(2,1)S(1)}, u32[]{:S(2)}, u32[]{:S(2)}) collective-permute-start(bf16[32,1344]{1,0:T(8,128)(2,1)S(1)} %get-tuple-element.64), channel_id=1, source_target_pairs={{0,4},{1,9},{2,6},{3,11},{4,0},{5,13},{6,2},{7,15},{8,12},{9,1},{1... | collective-permute-start | bytes 258056 | tf_op jit(solution)/shard_map/ppermute | solution.py:363
  20.4 0.3 collective-permute-start.7
  20.7 3.5 %collective-permute-done.6.got_ref.rest_1_ = bf16[32,1344]{1,0:T(8,128)(2,1)S(1)} collective-permute-done((bf16[32,1344]{1,0:T(8,128)(2,1)S(1)}, bf16[32,1344]{1,0:T(8,128)(2,1)S(1)}, u32[]{:S(2)}, u32[]{:S(2)}) %collective-permute-start.6) | collective-permute-done | bytes 86048 | tf_op jit(solution)/shard_map/ppermute | solution.py:363
  24.3 1.8 %collective-permute-start.8 = (bf16[32,1344]{1,0:T(8,128)(2,1)S(1)}, bf16[32,1344]{1,0:T(8,128)(2,1)S(1)}, u32[]{:S(2)}, u32[]{:S(2)}) collective-permute-start(bf16[32,1344]{1,0:T(8,128)(2,1)S(1)} %relay.1), channel_id=1, source_target_pairs={{0,8},{1,5},{2,10},{3,7},{4,12},{5,1},{6,14},{7,3},{8,0},{9,13},{1... | collective-permute-start | bytes 258056 | tf_op jit(solution)/shard_map/ppermute | solution.py:363
  26.1 2.5 %weights.1 = (bf16[1,928,1344]{2,1,0:T(8,128)(2,1)S(1)}, bf16[1,928,1344]{2,1,0:T(8,128)(2,1)S(1)}) custom-call(bf16[32,1344]{1,0:T(8,128)(2,1)S(1)} %get-tuple-element.60.after_ref.rest_0_, bf16[1,928,1344]{2,1,0:T(8,128)(2,1)} %bitcast.10, bf16[1,928,1344]{2,1,0:T(8,128)(2,1)} %down_hbm.1), custom_call_target="tpu_custom_call" | custom-call | tf_op jit(solution)/shard_map/weights/pallas_call | solution.py:29
  28.6 1.1 %collective-permute-done.8.rest_3_ = bf16[32,1344]{1,0:T(8,128)(2,1)S(1)} collective-permute-done((bf16[32,1344]{1,0:T(8,128)(2,1)S(1)}, bf16[32,1344]{1,0:T(8,128)(2,1)S(1)}, u32[]{:S(2)}, u32[]{:S(2)}) %collective-permute-start.8) | collective-permute-done | bytes 86048 | tf_op jit(solution)/shard_map/ppermute | solution.py:363
  29.8 0.2 rows.1
  29.9 1.8 %collective-permute-start.12 = (bf16[32,1408]{1,0:T(8,128)(2,1)S(1)}, bf16[32,1408]{1,0:T(8,128)(2,1)S(1)}, u32[]{:S(2)}, u32[]{:S(2)}) collective-permute-start(bf16[32,1408]{1,0:T(8,128)(2,1)S(1)} %get-tuple-element.69.rest_0_), channel_id=1, source_target_pairs={{0,8},{4,12},{8,0},{12,4},{1,9},{5,13},{9,1},{13,5},{2,10},{6,14},... | collective-permute-start | bytes 270344 | tf_op jit(solution)/shard_map/ppermute | solution.py:353
  31.8 3.4 %collective-permute-start.11 = (bf16[32,1408]{1,0:T(8,128)(2,1)S(1)}, bf16[32,1408]{1,0:T(8,128)(2,1)S(1)}, u32[]{:S(2)}, u32[]{:S(2)}) collective-permute-start(bf16[32,1408]{1,0:T(8,128)(2,1)S(1)} %get-tuple-element.69.rest_0_), channel_id=1, source_target_pairs={{0,6},{1,7},{2,4},{3,5},{4,2},{5,3},{6,0},{7,1},{8,14},{9,15},{10,... | collective-permute-start | bytes 270344 | tf_op jit(solution)/shard_map/ppermute | solution.py:353
  35.2 0.5 collective-permute-start.9
  35.7 3.0 %collective-permute-start.15 = (bf16[32,1408]{1,0:T(8,128)(2,1)S(1)}, bf16[32,1408]{1,0:T(8,128)(2,1)S(1)}, u32[]{:S(2)}, u32[]{:S(2)}) collective-permute-start(bf16[32,1408]{1,0:T(8,128)(2,1)S(1)} %collective-permute-done.12.rest_0_), channel_id=1, source_target_pairs={{0,6},{1,7},{2,4},{3,5},{4,2},{5,3},{6,0},{7,1},{8,14},{9,15},{10,... | collective-permute-start | bytes 270344 | tf_op jit(solution)/shard_map/ppermute | solution.py:353
  38.7 1.1 %collective-permute-start.14 = (bf16[32,1408]{1,0:T(8,128)(2,1)S(1)}, bf16[32,1408]{1,0:T(8,128)(2,1)S(1)}, u32[]{:S(2)}, u32[]{:S(2)}) collective-permute-start(bf16[32,1408]{1,0:T(8,128)(2,1)S(1)} %collective-permute-done.12.rest_0_), channel_id=1, source_target_pairs={{0,4},{1,5},{2,6},{3,7},{4,0},{5,1},{6,2},{7,3},{8,12},{9,13},{10,... | collective-permute-start | bytes 270344 | tf_op jit(solution)/shard_map/ppermute | solution.py:353
  39.8 1.0 %collective-permute-done.10.rest_2_ = bf16[32,1408]{1,0:T(8,128)(2,1)S(1)} collective-permute-done((bf16[32,1408]{1,0:T(8,128)(2,1)S(1)}, bf16[32,1408]{1,0:T(8,128)(2,1)S(1)}, u32[]{:S(2)}, u32[]{:S(2)}) %collective-permute-start.10) | collective-permute-done | bytes 90144 | tf_op jit(solution)/shard_map/ppermute | solution.py:353
  40.7 1.4 %collective-permute-done.9.rest_1_ = bf16[32,1408]{1,0:T(8,128)(2,1)S(1)} collective-permute-done((bf16[32,1408]{1,0:T(8,128)(2,1)S(1)}, bf16[32,1408]{1,0:T(8,128)(2,1)S(1)}, u32[]{:S(2)}, u32[]{:S(2)}) %collective-permute-start.9) | collective-permute-done | bytes 90144 | tf_op jit(solution)/shard_map/ppermute | solution.py:353
  42.1 2.7 %experts.2 = (bf16[32,1344]{1,0:T(8,128)(2,1)S(1)}, bf16[32,1344]{1,0:T(8,128)(2,1)S(1)}, bf16[32,1344]{1,0:T(8,128)(2,1)S(1)}, bf16[32,1344]{1,0:T(8,128)(2,1)S(1)}) custom-call(bf16[1,928,1344]{2,1,0:T(8,128)(2,1)S(1)} %get-tuple-element.61.after_ref.up_ref, bf16[1,928,1344]{2,1,0:T(8,128)(2,1)S(1)} %get-tuple-element.68.down_ref, ...), custom_call_target="tpu_custom_call" | custom-call | tf_op jit(solution)/shard_map/experts/pallas_call | solution.py:29
  44.9 2.7 %experts.3 = (bf16[32,1344]{1,0:T(8,128)(2,1)S(1)}, bf16[32,1344]{1,0:T(8,128)(2,1)S(1)}, bf16[32,1344]{1,0:T(8,128)(2,1)S(1)}, bf16[32,1344]{1,0:T(8,128)(2,1)S(1)}) custom-call(bf16[1,928,1344]{2,1,0:T(8,128)(2,1)S(1)} %get-tuple-element.61.after_ref.up_ref, bf16[1,928,1344]{2,1,0:T(8,128)(2,1)S(1)} %get-tuple-element.68.down_ref, ...), custom_call_target="tpu_custom_call" | custom-call | tf_op jit(solution)/shard_map/experts/pallas_call | solution.py:29
  47.6 1.4 %collective-permute-start.16 = (bf16[32,1344]{1,0:T(8,128)(2,1)S(1)}, bf16[32,1344]{1,0:T(8,128)(2,1)S(1)}, u32[]{:S(2)}, u32[]{:S(2)}) collective-permute-start(bf16[32,1344]{1,0:T(8,128)(2,1)S(1)} %get-tuple-element.80), channel_id=1, source_target_pairs={{0,6},{1,7},{2,4},{3,5},{4,2},{5,3},{6,0},{7,1},{8,14},{9,15},{10,... | collective-permute-start | bytes 258056 | tf_op jit(solution)/shard_map/ppermute | solution.py:353
  48.9 0.1 collective-permute-start.17
  49.1 2.1 %collective-permute-start.18 = (bf16[32,1344]{1,0:T(8,128)(2,1)S(1)}, bf16[32,1344]{1,0:T(8,128)(2,1)S(1)}, u32[]{:S(2)}, u32[]{:S(2)}) collective-permute-start(bf16[32,1344]{1,0:T(8,128)(2,1)S(1)} %get-tuple-element.82), channel_id=1, source_target_pairs={{0,2},{1,3},{2,0},{3,1},{4,6},{5,7},{6,4},{7,5},{8,10},{9,11},{10,... | collective-permute-start | bytes 258056 | tf_op jit(solution)/shard_map/ppermute | solution.py:353
  51.1 1.3 %collective-permute-start.20 = (bf16[32,1344]{1,0:T(8,128)(2,1)S(1)}, bf16[32,1344]{1,0:T(8,128)(2,1)S(1)}, u32[]{:S(2)}, u32[]{:S(2)}) collective-permute-start(bf16[32,1344]{1,0:T(8,128)(2,1)S(1)} %get-tuple-element.86), channel_id=1, source_target_pairs={{0,6},{1,7},{2,4},{3,5},{4,2},{5,3},{6,0},{7,1},{8,14},{9,15},{10,... | collective-permute-start | bytes 258056 | tf_op jit(solution)/shard_map/ppermute | solution.py:353
  52.4 0.8 %collective-permute-done.16.refs_1_ = bf16[32,1344]{1,0:T(8,128)(2,1)S(1)} collective-permute-done((bf16[32,1344]{1,0:T(8,128)(2,1)S(1)}, bf16[32,1344]{1,0:T(8,128)(2,1)S(1)}, u32[]{:S(2)}, u32[]{:S(2)}) %collective-permute-start.16) | collective-permute-done | bytes 86048 | tf_op jit(solution)/shard_map/ppermute | solution.py:353
  53.2 0.6 %collective-permute-done.17.refs_2_ = bf16[32,1344]{1,0:T(8,128)(2,1)S(1)} collective-permute-done((bf16[32,1344]{1,0:T(8,128)(2,1)S(1)}, bf16[32,1344]{1,0:T(8,128)(2,1)S(1)}, u32[]{:S(2)}, u32[]{:S(2)}) %collective-permute-start.17) | collective-permute-done | bytes 86048 | tf_op jit(solution)/shard_map/ppermute | solution.py:353
  53.9 0.3 collective-permute-done.18.refs_3_
  54.2 1.4 %collective-permute-start.19 = (bf16[32,1344]{1,0:T(8,128)(2,1)S(1)}, bf16[32,1344]{1,0:T(8,128)(2,1)S(1)}, u32[]{:S(2)}, u32[]{:S(2)}) collective-permute-start(bf16[32,1344]{1,0:T(8,128)(2,1)S(1)} %sum.1), channel_id=1, source_target_pairs={{0,8},{4,12},{8,0},{12,4},{1,9},{5,13},{9,1},{13,5},{2,10},{6,14},... | collective-permute-start | bytes 258056 | tf_op jit(solution)/shard_map/ppermute | solution.py:353
  55.6 1.4 %collective-permute-start.21 = (bf16[32,1344]{1,0:T(8,128)(2,1)S(1)}, bf16[32,1344]{1,0:T(8,128)(2,1)S(1)}, u32[]{:S(2)}, u32[]{:S(2)}) collective-permute-start(bf16[32,1344]{1,0:T(8,128)(2,1)S(1)} %get-tuple-element.87), channel_id=1, source_target_pairs={{0,4},{1,5},{2,6},{3,7},{4,0},{5,1},{6,2},{7,3},{8,12},{9,13},{10,... | collective-permute-start | bytes 258056 | tf_op jit(solution)/shard_map/ppermute | solution.py:353
  57.0 2.1 %collective-permute-start.22 = (bf16[32,1344]{1,0:T(8,128)(2,1)S(1)}, bf16[32,1344]{1,0:T(8,128)(2,1)S(1)}, u32[]{:S(2)}, u32[]{:S(2)}) collective-permute-start(bf16[32,1344]{1,0:T(8,128)(2,1)S(1)} %get-tuple-element.88), channel_id=1, source_target_pairs={{0,2},{1,3},{2,0},{3,1},{4,6},{5,7},{6,4},{7,5},{8,10},{9,11},{10,... | collective-permute-start | bytes 258056 | tf_op jit(solution)/shard_map/ppermute | solution.py:353
  59.1 0.6 collective-permute-done.19.rest_1_
  59.7 0.9 %collective-permute-done.21.rest_3_ = bf16[32,1344]{1,0:T(8,128)(2,1)S(1)} collective-permute-done((bf16[32,1344]{1,0:T(8,128)(2,1)S(1)}, bf16[32,1344]{1,0:T(8,128)(2,1)S(1)}, u32[]{:S(2)}, u32[]{:S(2)}) %collective-permute-start.21) | collective-permute-done | bytes 86048 | tf_op jit(solution)/shard_map/ppermute | solution.py:353
  60.7 1.0 %collective-permute-done.22.rest_4_ = bf16[32,1344]{1,0:T(8,128)(2,1)S(1)} collective-permute-done((bf16[32,1344]{1,0:T(8,128)(2,1)S(1)}, bf16[32,1344]{1,0:T(8,128)(2,1)S(1)}, u32[]{:S(2)}, u32[]{:S(2)}) %collective-permute-start.22) | collective-permute-done | bytes 86048 | tf_op jit(solution)/shard_map/ppermute | solution.py:353
  61.6 0.7 %last.1 = bf16[1,32,1344]{2,1,0:T(8,128)(2,1)} custom-call(bf16[32,1344]{1,0:T(8,128)(2,1)S(1)} %get-tuple-element.67.hidden_ref, bf16[32,1344]{1,0:T(8,128)(2,1)S(1)} %get-tuple-element.74.rest_0_, bf16[32,1344]{1,0:T(8,128)(2,1)S(1)} %collective-permute-done.19.rest_1_, bf16[32,1344]{1,0:T(8,128)(2,1)S(1)} %collective-permute-done.20.rest_2_, ...), custom_call_target="tpu_custom_call" | custom-call | tf_op jit(solution)/shard_map/last/pallas_call | solution.py:29
  (14 shorter events, 0.2 us)
Async XLA Ops:
  1.8 1.5 %collective-permute-start = (bf16[528,128]{1,0:T(8,128)(2,1)S(1)}, bf16[528,128]{1,0:T(8,128)(2,1)S(1)}, u32[]{:S(2)}, u32[]{:S(2)}) collective-permute-start(bf16[528,128]{1,0:T(8,128)(2,1)S(1)} %get-tuple-element.48), channel_id=1, source_target_pairs={{0,1},{1,0},{2,3},{3,2},{4,5},{5,4},{6,7},{7,6},{8,9},{9,8},{10,11... | collective-permute-start | bytes 405512 | tf_op jit(solution)/shard_map/ppermute | solution.py:353
  3.4 14.3 %collective-permute-start.1 = (bf16[1,928,1344]{2,1,0:T(8,128)(2,1)}, bf16[1,928,1344]{2,1,0:T(8,128)(2,1)S(1)}, u32[]{:S(2)}, u32[]{:S(2)}) collective-permute-start(bf16[1,928,1344]{2,1,0:T(8,128)(2,1)} %bitcast.9), channel_id=1, source_target_pairs={{0,1},{1,0},{2,3},{3,2},{4,5},{5,4},{6,7},{7,6},{8,9},{9,8},{10,11... | collective-permute-start | bytes 7483400 | tf_op jit(solution)/shard_map/ppermute | solution.py:353
  3.9 13.9 %collective-permute-start.2 = (bf16[1,928,1344]{2,1,0:T(8,128)(2,1)}, bf16[1,928,1344]{2,1,0:T(8,128)(2,1)S(1)}, u32[]{:S(2)}, u32[]{:S(2)}) collective-permute-start(bf16[1,928,1344]{2,1,0:T(8,128)(2,1)} %down_hbm.1), channel_id=1, source_target_pairs={{0,1},{1,0},{2,3},{3,2},{4,5},{5,4},{6,7},{7,6},{8,9},{9,8},{10,11... | collective-permute-start | bytes 7483400 | tf_op jit(solution)/shard_map/ppermute | solution.py:353
  4.0 6.8 %collective-permute-start.3 = (bf16[528,128]{1,0:T(8,128)(2,1)S(1)}, bf16[528,128]{1,0:T(8,128)(2,1)S(1)}, u32[]{:S(2)}, u32[]{:S(2)}) collective-permute-start(bf16[528,128]{1,0:T(8,128)(2,1)S(1)} %chip_state.1.rest_0_), channel_id=1, source_target_pairs={{0,2},{1,3},{2,0},{3,1},{4,6},{5,7},{6,4},{7,5},{8,10},{9,11},{10,... | collective-permute-start | bytes 405512 | tf_op jit(solution)/shard_map/ppermute | solution.py:353
  10.9 5.2 %collective-permute-start.4 = (bf16[528,128]{1,0:T(8,128)(2,1)S(1)}, bf16[528,128]{1,0:T(8,128)(2,1)S(1)}, u32[]{:S(2)}, u32[]{:S(2)}) collective-permute-start(bf16[528,128]{1,0:T(8,128)(2,1)S(1)} %span.1.rest_2_), channel_id=1, source_target_pairs={{0,16},{16,0},{1,17},{17,1},{2,18},{18,2},{3,19},{19,3},{4,20},{20... | collective-permute-start | bytes 405512 | tf_op jit(solution)/shard_map/ppermute | solution.py:353
  16.4 1.4 %collective-permute-start.5 = (bf16[4,128,128]{2,1,0:T(8,128)(2,1)S(1)}, bf16[4,128,128]{2,1,0:T(8,128)(2,1)S(1)}, u32[]{:S(2)}, u32[]{:S(2)}) collective-permute-start(bf16[4,128,128]{2,1,0:T(8,128)(2,1)S(1)} %get-tuple-element.58), channel_id=1, source_target_pairs={{0,1},{1,0},{2,3},{3,2},{4,5},{5,4},{6,7},{7,6},{8,9},{9,8},{10,11... | collective-permute-start | bytes 393224 | tf_op jit(solution)/shard_map/ppermute | solution.py:353
  18.6 5.6 %collective-permute-start.6 = (bf16[32,1344]{1,0:T(8,128)(2,1)S(1)}, bf16[32,1344]{1,0:T(8,128)(2,1)S(1)}, u32[]{:S(2)}, u32[]{:S(2)}) collective-permute-start(bf16[32,1344]{1,0:T(8,128)(2,1)S(1)} %get-tuple-element.64), channel_id=1, source_target_pairs={{0,4},{1,9},{2,6},{3,11},{4,0},{5,13},{6,2},{7,15},{8,12},{9,1},{1... | collective-permute-start | bytes 258056 | tf_op jit(solution)/shard_map/ppermute | solution.py:363
  20.4 8.2 %collective-permute-start.7 = (bf16[32,1344]{1,0:T(8,128)(2,1)S(1)}, bf16[32,1344]{1,0:T(8,128)(2,1)S(1)}, u32[]{:S(2)}, u32[]{:S(2)}) collective-permute-start(bf16[32,1344]{1,0:T(8,128)(2,1)S(1)} %get-tuple-element.65), channel_id=1, source_target_pairs={{0,4},{1,13},{2,6},{3,15},{4,0},{5,9},{6,2},{7,11},{8,12},{9,5},{1... | collective-permute-start | bytes 258056 | tf_op jit(solution)/shard_map/ppermute | solution.py:363
  24.3 5.5 %collective-permute-start.8 = (bf16[32,1344]{1,0:T(8,128)(2,1)S(1)}, bf16[32,1344]{1,0:T(8,128)(2,1)S(1)}, u32[]{:S(2)}, u32[]{:S(2)}) collective-permute-start(bf16[32,1344]{1,0:T(8,128)(2,1)S(1)} %relay.1), channel_id=1, source_target_pairs={{0,8},{1,5},{2,10},{3,7},{4,12},{5,1},{6,14},{7,3},{8,0},{9,13},{1... | collective-permute-start | bytes 258056 | tf_op jit(solution)/shard_map/ppermute | solution.py:363
  29.9 5.8 %collective-permute-start.12 = (bf16[32,1408]{1,0:T(8,128)(2,1)S(1)}, bf16[32,1408]{1,0:T(8,128)(2,1)S(1)}, u32[]{:S(2)}, u32[]{:S(2)}) collective-permute-start(bf16[32,1408]{1,0:T(8,128)(2,1)S(1)} %get-tuple-element.69.rest_0_), channel_id=1, source_target_pairs={{0,8},{4,12},{8,0},{12,4},{1,9},{5,13},{9,1},{13,5},{2,10},{6,14},... | collective-permute-start | bytes 270344 | tf_op jit(solution)/shard_map/ppermute | solution.py:353
  31.8 8.0 %collective-permute-start.11 = (bf16[32,1408]{1,0:T(8,128)(2,1)S(1)}, bf16[32,1408]{1,0:T(8,128)(2,1)S(1)}, u32[]{:S(2)}, u32[]{:S(2)}) collective-permute-start(bf16[32,1408]{1,0:T(8,128)(2,1)S(1)} %get-tuple-element.69.rest_0_), channel_id=1, source_target_pairs={{0,6},{1,7},{2,4},{3,5},{4,2},{5,3},{6,0},{7,1},{8,14},{9,15},{10,... | collective-permute-start | bytes 270344 | tf_op jit(solution)/shard_map/ppermute | solution.py:353
  35.2 5.6 %collective-permute-start.10 = (bf16[32,1408]{1,0:T(8,128)(2,1)S(1)}, bf16[32,1408]{1,0:T(8,128)(2,1)S(1)}, u32[]{:S(2)}, u32[]{:S(2)}) collective-permute-start(bf16[32,1408]{1,0:T(8,128)(2,1)S(1)} %get-tuple-element.69.rest_0_), channel_id=1, source_target_pairs={{0,4},{1,5},{2,6},{3,7},{4,0},{5,1},{6,2},{7,3},{8,12},{9,13},{10,... | collective-permute-start | bytes 270344 | tf_op jit(solution)/shard_map/ppermute | solution.py:353
  35.2 6.9 %collective-permute-start.9 = (bf16[32,1408]{1,0:T(8,128)(2,1)S(1)}, bf16[32,1408]{1,0:T(8,128)(2,1)S(1)}, u32[]{:S(2)}, u32[]{:S(2)}) collective-permute-start(bf16[32,1408]{1,0:T(8,128)(2,1)S(1)} %get-tuple-element.69.rest_0_), channel_id=1, source_target_pairs={{0,2},{1,3},{2,0},{3,1},{4,6},{5,7},{6,4},{7,5},{8,10},{9,11},{10,... | collective-permute-start | bytes 270344 | tf_op jit(solution)/shard_map/ppermute | solution.py:353
  35.7 9.1 %collective-permute-start.15 = (bf16[32,1408]{1,0:T(8,128)(2,1)S(1)}, bf16[32,1408]{1,0:T(8,128)(2,1)S(1)}, u32[]{:S(2)}, u32[]{:S(2)}) collective-permute-start(bf16[32,1408]{1,0:T(8,128)(2,1)S(1)} %collective-permute-done.12.rest_0_), channel_id=1, source_target_pairs={{0,6},{1,7},{2,4},{3,5},{4,2},{5,3},{6,0},{7,1},{8,14},{9,15},{10,... | collective-permute-start | bytes 270344 | tf_op jit(solution)/shard_map/ppermute | solution.py:353
  38.7 6.2 %collective-permute-start.14 = (bf16[32,1408]{1,0:T(8,128)(2,1)S(1)}, bf16[32,1408]{1,0:T(8,128)(2,1)S(1)}, u32[]{:S(2)}, u32[]{:S(2)}) collective-permute-start(bf16[32,1408]{1,0:T(8,128)(2,1)S(1)} %collective-permute-done.12.rest_0_), channel_id=1, source_target_pairs={{0,4},{1,5},{2,6},{3,7},{4,0},{5,1},{6,2},{7,3},{8,12},{9,13},{10,... | collective-permute-start | bytes 270344 | tf_op jit(solution)/shard_map/ppermute | solution.py:353
  39.8 5.1 %collective-permute-start.13 = (bf16[32,1408]{1,0:T(8,128)(2,1)S(1)}, bf16[32,1408]{1,0:T(8,128)(2,1)S(1)}, u32[]{:S(2)}, u32[]{:S(2)}) collective-permute-start(bf16[32,1408]{1,0:T(8,128)(2,1)S(1)} %collective-permute-done.12.rest_0_), channel_id=1, source_target_pairs={{0,2},{1,3},{2,0},{3,1},{4,6},{5,7},{6,4},{7,5},{8,10},{9,11},{10,... | collective-permute-start | bytes 270344 | tf_op jit(solution)/shard_map/ppermute | solution.py:353
  47.6 5.7 %collective-permute-start.16 = (bf16[32,1344]{1,0:T(8,128)(2,1)S(1)}, bf16[32,1344]{1,0:T(8,128)(2,1)S(1)}, u32[]{:S(2)}, u32[]{:S(2)}) collective-permute-start(bf16[32,1344]{1,0:T(8,128)(2,1)S(1)} %get-tuple-element.80), channel_id=1, source_target_pairs={{0,6},{1,7},{2,4},{3,5},{4,2},{5,3},{6,0},{7,1},{8,14},{9,15},{10,... | collective-permute-start | bytes 258056 | tf_op jit(solution)/shard_map/ppermute | solution.py:353
  48.9 4.9 %collective-permute-start.17 = (bf16[32,1344]{1,0:T(8,128)(2,1)S(1)}, bf16[32,1344]{1,0:T(8,128)(2,1)S(1)}, u32[]{:S(2)}, u32[]{:S(2)}) collective-permute-start(bf16[32,1344]{1,0:T(8,128)(2,1)S(1)} %get-tuple-element.81), channel_id=1, source_target_pairs={{0,4},{1,5},{2,6},{3,7},{4,0},{5,1},{6,2},{7,3},{8,12},{9,13},{10,... | collective-permute-start | bytes 258056 | tf_op jit(solution)/shard_map/ppermute | solution.py:353
  49.1 5.1 %collective-permute-start.18 = (bf16[32,1344]{1,0:T(8,128)(2,1)S(1)}, bf16[32,1344]{1,0:T(8,128)(2,1)S(1)}, u32[]{:S(2)}, u32[]{:S(2)}) collective-permute-start(bf16[32,1344]{1,0:T(8,128)(2,1)S(1)} %get-tuple-element.82), channel_id=1, source_target_pairs={{0,2},{1,3},{2,0},{3,1},{4,6},{5,7},{6,4},{7,5},{8,10},{9,11},{10,... | collective-permute-start | bytes 258056 | tf_op jit(solution)/shard_map/ppermute | solution.py:353
  51.1 8.0 %collective-permute-start.20 = (bf16[32,1344]{1,0:T(8,128)(2,1)S(1)}, bf16[32,1344]{1,0:T(8,128)(2,1)S(1)}, u32[]{:S(2)}, u32[]{:S(2)}) collective-permute-start(bf16[32,1344]{1,0:T(8,128)(2,1)S(1)} %get-tuple-element.86), channel_id=1, source_target_pairs={{0,6},{1,7},{2,4},{3,5},{4,2},{5,3},{6,0},{7,1},{8,14},{9,15},{10,... | collective-permute-start | bytes 258056 | tf_op jit(solution)/shard_map/ppermute | solution.py:353
  54.2 5.5 %collective-permute-start.19 = (bf16[32,1344]{1,0:T(8,128)(2,1)S(1)}, bf16[32,1344]{1,0:T(8,128)(2,1)S(1)}, u32[]{:S(2)}, u32[]{:S(2)}) collective-permute-start(bf16[32,1344]{1,0:T(8,128)(2,1)S(1)} %sum.1), channel_id=1, source_target_pairs={{0,8},{4,12},{8,0},{12,4},{1,9},{5,13},{9,1},{13,5},{2,10},{6,14},... | collective-permute-start | bytes 258056 | tf_op jit(solution)/shard_map/ppermute | solution.py:353
  55.6 5.1 %collective-permute-start.21 = (bf16[32,1344]{1,0:T(8,128)(2,1)S(1)}, bf16[32,1344]{1,0:T(8,128)(2,1)S(1)}, u32[]{:S(2)}, u32[]{:S(2)}) collective-permute-start(bf16[32,1344]{1,0:T(8,128)(2,1)S(1)} %get-tuple-element.87), channel_id=1, source_target_pairs={{0,4},{1,5},{2,6},{3,7},{4,0},{5,1},{6,2},{7,3},{8,12},{9,13},{10,... | collective-permute-start | bytes 258056 | tf_op jit(solution)/shard_map/ppermute | solution.py:353
  57.0 4.6 %collective-permute-start.22 = (bf16[32,1344]{1,0:T(8,128)(2,1)S(1)}, bf16[32,1344]{1,0:T(8,128)(2,1)S(1)}, u32[]{:S(2)}, u32[]{:S(2)}) collective-permute-start(bf16[32,1344]{1,0:T(8,128)(2,1)S(1)} %get-tuple-element.88), channel_id=1, source_target_pairs={{0,2},{1,3},{2,0},{3,1},{4,6},{5,7},{6,4},{7,5},{8,10},{9,11},{10,... | collective-permute-start | bytes 258056 | tf_op jit(solution)/shard_map/ppermute | solution.py:353

commit v15 on v13

--- a/solution.py
+++ b/solution.py
@@ -40,10 +40,6 @@
 def offsets(count):
     down = list(range(count - 1, 0, -1))
     return [[2, 3, 1], [3, 1, 2]] if count == 4 else [down, down]
-
-
-def targets(count):
-    return [[2, 3, 1], [1, 1, 2]] if count == 4 else offsets(count)
 
 
 def head_offset(slot, count):
@@ -288,17 +284,12 @@
         out[...] = product[shift * rows : (shift + 1) * rows].astype(BF16)
 
 
-def relay_kernel(own_ref, got_ref, out_ref):
-    got = jnp.where(core_index() == 1, got_ref[...].astype(F32), 0.0)
-    out_ref[...] = (own_ref[...].astype(F32) + got).astype(BF16)
-
-
-def rows_kernel(after_ref, resid_ref, gate_ref, gain_ref, *rest):
+def rows_kernel(relay, after_ref, resid_ref, gate_ref, gain_ref, *rest):
     parts, hidden_ref, rows_ref = rest[:-2], rest[-2], rest[-1]
     mixed = parts[0][...].astype(F32)
     for at, part in enumerate(parts[1:]):
         value = part[...].astype(F32)
-        if at == 0 and len(parts) == 4:
+        if at == 0 and relay:
             value = jnp.where(core_index() == 0, value, 0.0)
         mixed = mixed + value
     hidden = (resid_ref[0].astype(F32) + mixed).astype(BF16)
@@ -353,14 +344,25 @@
     return lax.ppermute(value, axis, [(i, i ^ mask) for i in range(size)])
 
 
-def swap_slot(value, slot):
+def swap_by_core(value, masks):
     heads, size = lax.axis_size("head"), lax.axis_size("exp")
-    order = targets(heads)
     pairs = []
     for i in range(heads * size):
-        head, exp = i // size, i % size
-        pairs.append((i, (head ^ order[exp % 2][slot]) * size + exp))
+        mask = masks[i % size % 2]
+        if mask:
+            pairs.append((i, i ^ (mask * size)))
     return lax.ppermute(value, ("head", "exp"), pairs)
+
+
+def projection_parts(pieces):
+    orders = list(zip(*offsets(len(pieces))))
+    if len(pieces) != 4:
+        return [pieces[0]] + [swap_by_core(piece, masks) for piece, masks in zip(pieces[1:], orders)]
+    first = swap_by_core(pieces[1], (2, 1))
+    second = swap_by_core(pieces[2], orders[1])
+    third = swap_by_core(pieces[3], (1, 0))
+    relayed = call(sum_kernel, "relay", struct(pieces[3].shape, BF16), [(VMEM, pieces[3]), (VMEM, first)])
+    return [pieces[0], first, second, third, swap_by_core(relayed, (0, 2))]
 
 
 def per_device(
@@ -455,13 +457,9 @@
         [(ANY, mixed[0]), (HBM, up_turned), (HBM, w_down)],
         [dma((2,))],
     )
-    slots = list(range(head_size - 1))
-    parts, last = [swap_slot(mixed[k + 1], k) for k in slots[:-1]], mixed[-1]
-    if head_size == 4:
-        last = call(relay_kernel, "relay", struct((rows, model), BF16), [(VMEM, last), (VMEM, parts[0])])
-    parts = [mixed[0]] + parts + [swap_slot(last, slots[-1])]
+    parts = projection_parts(mixed)
     hidden, own_rows = call(
-        rows_kernel,
+        functools.partial(rows_kernel, head_size == 4),
         "rows",
         [struct((rows, model), BF16), struct((rows, wide), BF16)],
         [(ANY, up_held)] + [(VMEM, value) for value in (resid_held, gate_lanes, gain_held, *parts)],

time: 66.5 us -> 65.9 us (level)
  starting transfers between devices: 35.3 us -> 31.5 us
  waiting for transfers between devices: 12.1 us -> 15.3 us
    ppermute x20, starting transfers between devices: 28.3 us -> 24.6 us  [swap(): return lax.ppermute(value, axis, [(i, i ^ mask) for i in range(size)])]
    ppermute x20, waiting for transfers between devices: 10 us -> 13.5 us  [swap(): return lax.ppermute(value, axis, [(i, i ^ mask) for i in range(size)])]
    ppermute x3 -> x4, waiting for transfers between devices: 2.06 us -> 1.77 us  [swap_by_core(): return lax.ppermute(value, ('head', 'exp'), pairs)]
    ppermute x3 -> x4, starting transfers between devices: 7.05 us -> 6.9 us  [swap_by_core(): return lax.ppermute(value, ('head', 'exp'), pairs)]
  transfers between devices with their start and end apart: 23 -> 24, of which waited for: 11 -> 14; matrix products, arithmetic and copies ran while one was open for 2% -> 2% of each run, Pallas kernels for 17% -> 17%
where the time goes in v15:
time: 65.9 us; the launch traced here: 65.5 us
  starting transfers between devices  31.5 us (48%)
  Pallas kernels  17.3 us (26%)
  waiting for transfers between devices  15.3 us (23%)
  local copies, waits for them, and re-layouts  1.29 us (2%)
    ppermute x20, starting transfers between devices, swap(): return lax.ppermute(value, axis, [(i, i ^ mask) for i in range(size)])  24.6 us
    pallas_call x15, Pallas kernels, call(): pl.pallas_call(kernel, out_shape=jax.tree.map(lambda out: pltpu.VMEM(out....  17.3 us
    ppermute x20, waiting for transfers between devices, swap(): return lax.ppermute(value, axis, [(i, i ^ mask) for i in range(size)])  13.5 us
    ppermute x4, starting transfers between devices, swap_by_core(): return lax.ppermute(value, ('head', 'exp'), pairs)  6.9 us
    ppermute x4, waiting for transfers between devices, swap_by_core(): return lax.ppermute(value, ('head', 'exp'), pairs)  1.77 us
  transfers between devices with their start and end apart: 24, of which 14 were waited for; matrix products, arithmetic and copies ran while one was open for 2% of the time, Pallas kernels for 17%

profile of v15, /device:TPU:0, one launch (start us, length us, event | category | flops | bytes accessed | tf_op | source)
XLA Modules:
  0.0 65.5 jit_solution(1116598231554962166)
XLA Ops:
  0.0 1.8 %state.1 = (bf16[528,128]{1,0:T(8,128)(2,1)S(1)}, bf16[528,128]{1,0:T(8,128)(2,1)S(1)}) custom-call(bf16[128,1024]{1,0:T(8,128)(2,1)} %x_hbm.3, bf16[128,256]{1,0:T(8,128)(2,1)} %b_hbm.3, f32[16,128]{1,0:T(8,128)} %bitcast.11, f32[1,16]{1,0:T(1,128)} %bitcast.16), custom_call_target="tpu_custom_call" | custom-call | tf_op jit(solution)/shard_map/state/pallas_call | solution.py:29
  1.8 0.5 collective-permute-start
  2.3 1.0 %collective-permute-done.got_ref = bf16[528,128]{1,0:T(8,128)(2,1)S(1)} collective-permute-done((bf16[528,128]{1,0:T(8,128)(2,1)S(1)}, bf16[528,128]{1,0:T(8,128)(2,1)S(1)}, u32[]{:S(2)}, u32[]{:S(2)}) %collective-permute-start) | collective-permute-done | bytes 135200 | tf_op jit(solution)/shard_map/ppermute | solution.py:344
  3.4 0.4 collective-permute-start.1
  3.9 0.1 collective-permute-start.2
  4.0 2.9 %collective-permute-start.3 = (bf16[528,128]{1,0:T(8,128)(2,1)S(1)}, bf16[528,128]{1,0:T(8,128)(2,1)S(1)}, u32[]{:S(2)}, u32[]{:S(2)}) collective-permute-start(bf16[528,128]{1,0:T(8,128)(2,1)S(1)} %chip_state.1.rest_0_), channel_id=1, source_target_pairs={{0,2},{1,3},{2,0},{3,1},{4,6},{5,7},{6,4},{7,5},{8,10},{9,11},{10,... | collective-permute-start | bytes 405512 | tf_op jit(solution)/shard_map/ppermute | solution.py:344
  6.9 2.4 %inside.1 = (f32[128,1024]{1,0:T(8,128)S(1)}, f32[128,1024]{1,0:T(8,128)S(1)}, bf16[128,256]{1,0:T(8,128)(2,1)S(1)}) custom-call(bf16[128,1024]{1,0:T(8,128)(2,1)} %x_hbm.3, bf16[128,1024]{1,0:T(8,128)(2,1)} %z_hbm.1, bf16[128,256]{1,0:T(8,128)(2,1)} %b_hbm.3, bf16[128,256]{1,0:T(8,128)(2,1)} %c_hbm.1, f32[16,128]{1,0:T(8,128)} %bitcast.12, ...), custom_call_target="tpu_custom_call" | custom-call | tf_op jit(solution)/shard_map/inside/pallas_call | solution.py:29
  9.3 1.4 %collective-permute-done.3.rest_1_ = bf16[528,128]{1,0:T(8,128)(2,1)S(1)} collective-permute-done((bf16[528,128]{1,0:T(8,128)(2,1)S(1)}, bf16[528,128]{1,0:T(8,128)(2,1)S(1)}, u32[]{:S(2)}, u32[]{:S(2)}) %collective-permute-start.3) | collective-permute-done | bytes 135200 | tf_op jit(solution)/shard_map/ppermute | solution.py:344
  10.8 0.1 span.1.rest_2_
  10.9 1.8 %collective-permute-start.4 = (bf16[528,128]{1,0:T(8,128)(2,1)S(1)}, bf16[528,128]{1,0:T(8,128)(2,1)S(1)}, u32[]{:S(2)}, u32[]{:S(2)}) collective-permute-start(bf16[528,128]{1,0:T(8,128)(2,1)S(1)} %span.1.rest_2_), channel_id=1, source_target_pairs={{0,16},{16,0},{1,17},{17,1},{2,18},{18,2},{3,19},{19,3},{4,20},{20... | collective-permute-start | bytes 405512 | tf_op jit(solution)/shard_map/ppermute | solution.py:344
  12.7 1.3 %broadcast_in_dim.14.gain_hbm = f32[1,1344]{1,0:T(1,128)} reshape(f32[1344]{0:T(1024)} %param.27) | data formatting | bytes 10752 | tf_op jit(solution)/shard_map/broadcast_in_dim | solution.py:410
  14.0 1.9 %prep.1 = (bf16[32,128]{1,0:T(8,128)(2,1)S(1)}, bf16[1,32,1344]{2,1,0:T(8,128)(2,1)S(1)}, f32[1,1344]{1,0:T(1,128)S(1)}, f32[1,1024]{1,0:T(1,128)S(1)}, bf16[1344,1024]{1,0:T(8,128)(2,1)S(1)}) custom-call(bf16[1,32,1344]{2,1,0:T(8,128)(2,1)} %resid_hbm.1, s32[6,1,32]{2,1,0:T(1,128)} %bitcast.14, f32[6,1,32]{2,1,0:T(1,128)} %bitcast.15, ...), custom_call_target="tpu_custom_call" | custom-call | tf_op jit(solution)/shard_map/prep/pallas_call | solution.py:29
  15.9 0.2 collective-permute-done.4.rest_3_
  16.1 0.3 before.1
  16.4 0.8 %first_half.1.first_ref = f32[128,1344]{1,0:T(8,128)S(1)} custom-call(f32[128,1024]{1,0:T(8,128)S(1)} %get-tuple-element.51.local_ref, f32[128,1024]{1,0:T(8,128)S(1)} %get-tuple-element.52.grown_ref, bf16[128,256]{1,0:T(8,128)(2,1)S(1)} %get-tuple-element.53.after_ref.c_ref, f32[1,1024]{1,0:T(1,128)S(1)} %get-tuple-element.54.norm_ref, ...), custom_call_target="tpu_custom_call" | custom-call | tf_op jit(solution)/shard_map/first_half/pallas_call | solution.py:29
  17.3 0.5 collective-permute-done.5.got_ref
  17.8 0.9 %mixed.1 = (bf16[32,1344]{1,0:T(8,128)(2,1)S(1)}, bf16[32,1344]{1,0:T(8,128)(2,1)S(1)}, bf16[32,1344]{1,0:T(8,128)(2,1)S(1)}, bf16[32,1344]{1,0:T(8,128)(2,1)S(1)}) custom-call(bf16[1,928,1344]{2,1,0:T(8,128)(2,1)S(1)} %collective-permute-done.1.after_up.other_up_ref, bf16[1,928,1344]{2,1,0:T(8,128)(2,1)S(1)} %collective-permute-done.2.after_down.other_down_ref, ...), custom_call_target="tpu_custom_call" | custom-call | tf_op jit(solution)/shard_map/mixed/pallas_call | solution.py:29
  18.6 2.8 %collective-permute-start.6 = (bf16[32,1344]{1,0:T(8,128)(2,1)S(1)}, bf16[32,1344]{1,0:T(8,128)(2,1)S(1)}, u32[]{:S(2)}, u32[]{:S(2)}) collective-permute-start(bf16[32,1344]{1,0:T(8,128)(2,1)S(1)} %get-tuple-element.64), channel_id=1, source_target_pairs={{0,8},{1,5},{2,10},{3,7},{4,12},{5,1},{6,14},{7,3},{8,0},{9,13},{1... | collective-permute-start | bytes 258056 | tf_op jit(solution)/shard_map/ppermute | solution.py:354
  21.4 1.4 %collective-permute-start.7 = (bf16[32,1344]{1,0:T(8,128)(2,1)S(1)}, bf16[32,1344]{1,0:T(8,128)(2,1)S(1)}, u32[]{:S(2)}, u32[]{:S(2)}) collective-permute-start(bf16[32,1344]{1,0:T(8,128)(2,1)S(1)} %get-tuple-element.65), channel_id=1, source_target_pairs={{0,12},{1,5},{2,14},{3,7},{4,8},{5,1},{6,10},{7,3},{8,4},{9,13},{1... | collective-permute-start | bytes 258056 | tf_op jit(solution)/shard_map/ppermute | solution.py:354
  22.8 2.1 %collective-permute-start.8 = (bf16[32,1344]{1,0:T(8,128)(2,1)S(1)}, bf16[32,1344]{1,0:T(8,128)(2,1)S(1)}, u32[]{:S(2)}, u32[]{:S(2)}) collective-permute-start(bf16[32,1344]{1,0:T(8,128)(2,1)S(1)} %get-tuple-element.66.refs_0_), channel_id=1, source_target_pairs={{0,4},{2,6},{4,0},{6,2},{8,12},{10,14},{12,8},{14,10},{16,20},{18,... | collective-permute-start | bytes 258056 | tf_op jit(solution)/shard_map/ppermute | solution.py:354
  24.9 0.7 %collective-permute-start.9 = (bf16[32,1344]{1,0:T(8,128)(2,1)S(1)}, bf16[32,1344]{1,0:T(8,128)(2,1)S(1)}, u32[]{:S(2)}, u32[]{:S(2)}) collective-permute-start(bf16[32,1344]{1,0:T(8,128)(2,1)S(1)} %relay.1), channel_id=1, source_target_pairs={{1,9},{3,11},{5,13},{7,15},{9,1},{11,3},{13,5},{15,7},{17,25},{19,... | collective-permute-start | bytes 258056 | tf_op jit(solution)/shard_map/ppermute | solution.py:354
  25.6 2.5 %weights.1 = (bf16[1,928,1344]{2,1,0:T(8,128)(2,1)S(1)}, bf16[1,928,1344]{2,1,0:T(8,128)(2,1)S(1)}) custom-call(bf16[32,1344]{1,0:T(8,128)(2,1)S(1)} %get-tuple-element.60.after_ref.rest_0_, bf16[1,928,1344]{2,1,0:T(8,128)(2,1)} %bitcast.10, bf16[1,928,1344]{2,1,0:T(8,128)(2,1)} %down_hbm.1), custom_call_target="tpu_custom_call" | custom-call | tf_op jit(solution)/shard_map/weights/pallas_call | solution.py:29
  28.2 1.8 %collective-permute-done.8.rest_3_ = bf16[32,1344]{1,0:T(8,128)(2,1)S(1)} collective-permute-done((bf16[32,1344]{1,0:T(8,128)(2,1)S(1)}, bf16[32,1344]{1,0:T(8,128)(2,1)S(1)}, u32[]{:S(2)}, u32[]{:S(2)}) %collective-permute-start.8) | collective-permute-done | bytes 86048 | tf_op jit(solution)/shard_map/ppermute | solution.py:354
  29.9 0.2 rows.1
  30.1 1.4 %collective-permute-start.13 = (bf16[32,1408]{1,0:T(8,128)(2,1)S(1)}, bf16[32,1408]{1,0:T(8,128)(2,1)S(1)}, u32[]{:S(2)}, u32[]{:S(2)}) collective-permute-start(bf16[32,1408]{1,0:T(8,128)(2,1)S(1)} %get-tuple-element.69.rest_0_), channel_id=1, source_target_pairs={{0,8},{4,12},{8,0},{12,4},{1,9},{5,13},{9,1},{13,5},{2,10},{6,14},... | collective-permute-start | bytes 270344 | tf_op jit(solution)/shard_map/ppermute | solution.py:344
  31.5 3.3 %collective-permute-start.12 = (bf16[32,1408]{1,0:T(8,128)(2,1)S(1)}, bf16[32,1408]{1,0:T(8,128)(2,1)S(1)}, u32[]{:S(2)}, u32[]{:S(2)}) collective-permute-start(bf16[32,1408]{1,0:T(8,128)(2,1)S(1)} %get-tuple-element.69.rest_0_), channel_id=1, source_target_pairs={{0,6},{1,7},{2,4},{3,5},{4,2},{5,3},{6,0},{7,1},{8,14},{9,15},{10,... | collective-permute-start | bytes 270344 | tf_op jit(solution)/shard_map/ppermute | solution.py:344
  34.8 0.6 collective-permute-start.10
  35.4 1.8 %collective-permute-done.13.rest_0_ = bf16[32,1408]{1,0:T(8,128)(2,1)S(1)} collective-permute-done((bf16[32,1408]{1,0:T(8,128)(2,1)S(1)}, bf16[32,1408]{1,0:T(8,128)(2,1)S(1)}, u32[]{:S(2)}, u32[]{:S(2)}) %collective-permute-start.13) | collective-permute-done | bytes 90144 | tf_op jit(solution)/shard_map/ppermute | solution.py:344
  37.2 1.1 %collective-permute-start.16 = (bf16[32,1408]{1,0:T(8,128)(2,1)S(1)}, bf16[32,1408]{1,0:T(8,128)(2,1)S(1)}, u32[]{:S(2)}, u32[]{:S(2)}) collective-permute-start(bf16[32,1408]{1,0:T(8,128)(2,1)S(1)} %collective-permute-done.13.rest_0_), channel_id=1, source_target_pairs={{0,6},{1,7},{2,4},{3,5},{4,2},{5,3},{6,0},{7,1},{8,14},{9,15},{10,... | collective-permute-start | bytes 270344 | tf_op jit(solution)/shard_map/ppermute | solution.py:344
  38.3 1.9 %collective-permute-start.15 = (bf16[32,1408]{1,0:T(8,128)(2,1)S(1)}, bf16[32,1408]{1,0:T(8,128)(2,1)S(1)}, u32[]{:S(2)}, u32[]{:S(2)}) collective-permute-start(bf16[32,1408]{1,0:T(8,128)(2,1)S(1)} %collective-permute-done.13.rest_0_), channel_id=1, source_target_pairs={{0,4},{1,5},{2,6},{3,7},{4,0},{5,1},{6,2},{7,3},{8,12},{9,13},{10,... | collective-permute-start | bytes 270344 | tf_op jit(solution)/shard_map/ppermute | solution.py:344
  40.2 0.5 collective-permute-start.14
  40.7 2.7 %experts.2 = (bf16[32,1344]{1,0:T(8,128)(2,1)S(1)}, bf16[32,1344]{1,0:T(8,128)(2,1)S(1)}, bf16[32,1344]{1,0:T(8,128)(2,1)S(1)}, bf16[32,1344]{1,0:T(8,128)(2,1)S(1)}) custom-call(bf16[1,928,1344]{2,1,0:T(8,128)(2,1)S(1)} %get-tuple-element.61.after_ref.up_ref, bf16[1,928,1344]{2,1,0:T(8,128)(2,1)S(1)} %get-tuple-element.68.down_ref, ...), custom_call_target="tpu_custom_call" | custom-call | tf_op jit(solution)/shard_map/experts/pallas_call | solution.py:29
  43.4 0.3 collective-permute-done.15.rest_2_
  43.7 1.0 %collective-permute-done.14.rest_1_ = bf16[32,1408]{1,0:T(8,128)(2,1)S(1)} collective-permute-done((bf16[32,1408]{1,0:T(8,128)(2,1)S(1)}, bf16[32,1408]{1,0:T(8,128)(2,1)S(1)}, u32[]{:S(2)}, u32[]{:S(2)}) %collective-permute-start.14) | collective-permute-done | bytes 90144 | tf_op jit(solution)/shard_map/ppermute | solution.py:344
  44.7 2.7 %experts.3 = (bf16[32,1344]{1,0:T(8,128)(2,1)S(1)}, bf16[32,1344]{1,0:T(8,128)(2,1)S(1)}, bf16[32,1344]{1,0:T(8,128)(2,1)S(1)}, bf16[32,1344]{1,0:T(8,128)(2,1)S(1)}) custom-call(bf16[1,928,1344]{2,1,0:T(8,128)(2,1)S(1)} %get-tuple-element.61.after_ref.up_ref, bf16[1,928,1344]{2,1,0:T(8,128)(2,1)S(1)} %get-tuple-element.68.down_ref, ...), custom_call_target="tpu_custom_call" | custom-call | tf_op jit(solution)/shard_map/experts/pallas_call | solution.py:29
  47.5 1.1 %collective-permute-start.17 = (bf16[32,1344]{1,0:T(8,128)(2,1)S(1)}, bf16[32,1344]{1,0:T(8,128)(2,1)S(1)}, u32[]{:S(2)}, u32[]{:S(2)}) collective-permute-start(bf16[32,1344]{1,0:T(8,128)(2,1)S(1)} %get-tuple-element.80), channel_id=1, source_target_pairs={{0,6},{1,7},{2,4},{3,5},{4,2},{5,3},{6,0},{7,1},{8,14},{9,15},{10,... | collective-permute-start | bytes 258056 | tf_op jit(solution)/shard_map/ppermute | solution.py:344
  48.6 0.9 %collective-permute-start.18 = (bf16[32,1344]{1,0:T(8,128)(2,1)S(1)}, bf16[32,1344]{1,0:T(8,128)(2,1)S(1)}, u32[]{:S(2)}, u32[]{:S(2)}) collective-permute-start(bf16[32,1344]{1,0:T(8,128)(2,1)S(1)} %get-tuple-element.81), channel_id=1, source_target_pairs={{0,4},{1,5},{2,6},{3,7},{4,0},{5,1},{6,2},{7,3},{8,12},{9,13},{10,... | collective-permute-start | bytes 258056 | tf_op jit(solution)/shard_map/ppermute | solution.py:344
  49.5 1.5 %collective-permute-start.19 = (bf16[32,1344]{1,0:T(8,128)(2,1)S(1)}, bf16[32,1344]{1,0:T(8,128)(2,1)S(1)}, u32[]{:S(2)}, u32[]{:S(2)}) collective-permute-start(bf16[32,1344]{1,0:T(8,128)(2,1)S(1)} %get-tuple-element.82), channel_id=1, source_target_pairs={{0,2},{1,3},{2,0},{3,1},{4,6},{5,7},{6,4},{7,5},{8,10},{9,11},{10,... | collective-permute-start | bytes 258056 | tf_op jit(solution)/shard_map/ppermute | solution.py:344
  51.0 1.1 %collective-permute-start.21 = (bf16[32,1344]{1,0:T(8,128)(2,1)S(1)}, bf16[32,1344]{1,0:T(8,128)(2,1)S(1)}, u32[]{:S(2)}, u32[]{:S(2)}) collective-permute-start(bf16[32,1344]{1,0:T(8,128)(2,1)S(1)} %get-tuple-element.86), channel_id=1, source_target_pairs={{0,6},{1,7},{2,4},{3,5},{4,2},{5,3},{6,0},{7,1},{8,14},{9,15},{10,... | collective-permute-start | bytes 258056 | tf_op jit(solution)/shard_map/ppermute | solution.py:344
  52.1 1.9 %collective-permute-done.17.refs_1_ = bf16[32,1344]{1,0:T(8,128)(2,1)S(1)} collective-permute-done((bf16[32,1344]{1,0:T(8,128)(2,1)S(1)}, bf16[32,1344]{1,0:T(8,128)(2,1)S(1)}, u32[]{:S(2)}, u32[]{:S(2)}) %collective-permute-start.17) | collective-permute-done | bytes 86048 | tf_op jit(solution)/shard_map/ppermute | solution.py:344
  54.0 0.1 collective-permute-done.18.refs_2_
  54.1 0.7 %collective-permute-done.19.refs_3_ = bf16[32,1344]{1,0:T(8,128)(2,1)S(1)} collective-permute-done((bf16[32,1344]{1,0:T(8,128)(2,1)S(1)}, bf16[32,1344]{1,0:T(8,128)(2,1)S(1)}, u32[]{:S(2)}, u32[]{:S(2)}) %collective-permute-start.19) | collective-permute-done | bytes 86048 | tf_op jit(solution)/shard_map/ppermute | solution.py:344
  54.9 3.7 %collective-permute-start.20 = (bf16[32,1344]{1,0:T(8,128)(2,1)S(1)}, bf16[32,1344]{1,0:T(8,128)(2,1)S(1)}, u32[]{:S(2)}, u32[]{:S(2)}) collective-permute-start(bf16[32,1344]{1,0:T(8,128)(2,1)S(1)} %sum.1), channel_id=1, source_target_pairs={{0,8},{4,12},{8,0},{12,4},{1,9},{5,13},{9,1},{13,5},{2,10},{6,14},... | collective-permute-start | bytes 258056 | tf_op jit(solution)/shard_map/ppermute | solution.py:344
  58.5 1.7 %collective-permute-start.22 = (bf16[32,1344]{1,0:T(8,128)(2,1)S(1)}, bf16[32,1344]{1,0:T(8,128)(2,1)S(1)}, u32[]{:S(2)}, u32[]{:S(2)}) collective-permute-start(bf16[32,1344]{1,0:T(8,128)(2,1)S(1)} %get-tuple-element.87), channel_id=1, source_target_pairs={{0,4},{1,5},{2,6},{3,7},{4,0},{5,1},{6,2},{7,3},{8,12},{9,13},{10,... | collective-permute-start | bytes 258056 | tf_op jit(solution)/shard_map/ppermute | solution.py:344
  60.3 0.9 %collective-permute-done.20.rest_1_ = bf16[32,1344]{1,0:T(8,128)(2,1)S(1)} collective-permute-done((bf16[32,1344]{1,0:T(8,128)(2,1)S(1)}, bf16[32,1344]{1,0:T(8,128)(2,1)S(1)}, u32[]{:S(2)}, u32[]{:S(2)}) %collective-permute-start.20) | collective-permute-done | bytes 86048 | tf_op jit(solution)/shard_map/ppermute | solution.py:344
  61.2 1.9 %collective-permute-done.22.rest_3_ = bf16[32,1344]{1,0:T(8,128)(2,1)S(1)} collective-permute-done((bf16[32,1344]{1,0:T(8,128)(2,1)S(1)}, bf16[32,1344]{1,0:T(8,128)(2,1)S(1)}, u32[]{:S(2)}, u32[]{:S(2)}) %collective-permute-start.22) | collective-permute-done | bytes 86048 | tf_op jit(solution)/shard_map/ppermute | solution.py:344
  63.1 1.7 %collective-permute-done.23.rest_4_ = bf16[32,1344]{1,0:T(8,128)(2,1)S(1)} collective-permute-done((bf16[32,1344]{1,0:T(8,128)(2,1)S(1)}, bf16[32,1344]{1,0:T(8,128)(2,1)S(1)}, u32[]{:S(2)}, u32[]{:S(2)}) %collective-permute-start.23) | collective-permute-done | bytes 86048 | tf_op jit(solution)/shard_map/ppermute | solution.py:344
  64.8 0.7 %last.1 = bf16[1,32,1344]{2,1,0:T(8,128)(2,1)} custom-call(bf16[32,1344]{1,0:T(8,128)(2,1)S(1)} %get-tuple-element.67.hidden_ref, bf16[32,1344]{1,0:T(8,128)(2,1)S(1)} %get-tuple-element.74.rest_0_, bf16[32,1344]{1,0:T(8,128)(2,1)S(1)} %collective-permute-done.20.rest_1_, bf16[32,1344]{1,0:T(8,128)(2,1)S(1)} %collective-permute-done.21.rest_2_, ...), custom_call_target="tpu_custom_call" | custom-call | tf_op jit(solution)/shard_map/last/pallas_call | solution.py:29
  (16 shorter events, 0.3 us)
Async XLA Ops:
  1.8 1.5 %collective-permute-start = (bf16[528,128]{1,0:T(8,128)(2,1)S(1)}, bf16[528,128]{1,0:T(8,128)(2,1)S(1)}, u32[]{:S(2)}, u32[]{:S(2)}) collective-permute-start(bf16[528,128]{1,0:T(8,128)(2,1)S(1)} %get-tuple-element.48), channel_id=1, source_target_pairs={{0,1},{1,0},{2,3},{3,2},{4,5},{5,4},{6,7},{7,6},{8,9},{9,8},{10,11... | collective-permute-start | bytes 405512 | tf_op jit(solution)/shard_map/ppermute | solution.py:344
  3.4 14.3 %collective-permute-start.1 = (bf16[1,928,1344]{2,1,0:T(8,128)(2,1)}, bf16[1,928,1344]{2,1,0:T(8,128)(2,1)S(1)}, u32[]{:S(2)}, u32[]{:S(2)}) collective-permute-start(bf16[1,928,1344]{2,1,0:T(8,128)(2,1)} %bitcast.9), channel_id=1, source_target_pairs={{0,1},{1,0},{2,3},{3,2},{4,5},{5,4},{6,7},{7,6},{8,9},{9,8},{10,11... | collective-permute-start | bytes 7483400 | tf_op jit(solution)/shard_map/ppermute | solution.py:344
  3.9 13.9 %collective-permute-start.2 = (bf16[1,928,1344]{2,1,0:T(8,128)(2,1)}, bf16[1,928,1344]{2,1,0:T(8,128)(2,1)S(1)}, u32[]{:S(2)}, u32[]{:S(2)}) collective-permute-start(bf16[1,928,1344]{2,1,0:T(8,128)(2,1)} %down_hbm.1), channel_id=1, source_target_pairs={{0,1},{1,0},{2,3},{3,2},{4,5},{5,4},{6,7},{7,6},{8,9},{9,8},{10,11... | collective-permute-start | bytes 7483400 | tf_op jit(solution)/shard_map/ppermute | solution.py:344
  4.0 6.8 %collective-permute-start.3 = (bf16[528,128]{1,0:T(8,128)(2,1)S(1)}, bf16[528,128]{1,0:T(8,128)(2,1)S(1)}, u32[]{:S(2)}, u32[]{:S(2)}) collective-permute-start(bf16[528,128]{1,0:T(8,128)(2,1)S(1)} %chip_state.1.rest_0_), channel_id=1, source_target_pairs={{0,2},{1,3},{2,0},{3,1},{4,6},{5,7},{6,4},{7,5},{8,10},{9,11},{10,... | collective-permute-start | bytes 405512 | tf_op jit(solution)/shard_map/ppermute | solution.py:344
  10.9 5.2 %collective-permute-start.4 = (bf16[528,128]{1,0:T(8,128)(2,1)S(1)}, bf16[528,128]{1,0:T(8,128)(2,1)S(1)}, u32[]{:S(2)}, u32[]{:S(2)}) collective-permute-start(bf16[528,128]{1,0:T(8,128)(2,1)S(1)} %span.1.rest_2_), channel_id=1, source_target_pairs={{0,16},{16,0},{1,17},{17,1},{2,18},{18,2},{3,19},{19,3},{4,20},{20... | collective-permute-start | bytes 405512 | tf_op jit(solution)/shard_map/ppermute | solution.py:344
  16.4 1.4 %collective-permute-start.5 = (bf16[4,128,128]{2,1,0:T(8,128)(2,1)S(1)}, bf16[4,128,128]{2,1,0:T(8,128)(2,1)S(1)}, u32[]{:S(2)}, u32[]{:S(2)}) collective-permute-start(bf16[4,128,128]{2,1,0:T(8,128)(2,1)S(1)} %get-tuple-element.58), channel_id=1, source_target_pairs={{0,1},{1,0},{2,3},{3,2},{4,5},{5,4},{6,7},{7,6},{8,9},{9,8},{10,11... | collective-permute-start | bytes 393224 | tf_op jit(solution)/shard_map/ppermute | solution.py:344
  18.6 6.2 %collective-permute-start.6 = (bf16[32,1344]{1,0:T(8,128)(2,1)S(1)}, bf16[32,1344]{1,0:T(8,128)(2,1)S(1)}, u32[]{:S(2)}, u32[]{:S(2)}) collective-permute-start(bf16[32,1344]{1,0:T(8,128)(2,1)S(1)} %get-tuple-element.64), channel_id=1, source_target_pairs={{0,8},{1,5},{2,10},{3,7},{4,12},{5,1},{6,14},{7,3},{8,0},{9,13},{1... | collective-permute-start | bytes 258056 | tf_op jit(solution)/shard_map/ppermute | solution.py:354
  21.4 6.8 %collective-permute-start.7 = (bf16[32,1344]{1,0:T(8,128)(2,1)S(1)}, bf16[32,1344]{1,0:T(8,128)(2,1)S(1)}, u32[]{:S(2)}, u32[]{:S(2)}) collective-permute-start(bf16[32,1344]{1,0:T(8,128)(2,1)S(1)} %get-tuple-element.65), channel_id=1, source_target_pairs={{0,12},{1,5},{2,14},{3,7},{4,8},{5,1},{6,10},{7,3},{8,4},{9,13},{1... | collective-permute-start | bytes 258056 | tf_op jit(solution)/shard_map/ppermute | solution.py:354
  22.8 7.2 %collective-permute-start.8 = (bf16[32,1344]{1,0:T(8,128)(2,1)S(1)}, bf16[32,1344]{1,0:T(8,128)(2,1)S(1)}, u32[]{:S(2)}, u32[]{:S(2)}) collective-permute-start(bf16[32,1344]{1,0:T(8,128)(2,1)S(1)} %get-tuple-element.66.refs_0_), channel_id=1, source_target_pairs={{0,4},{2,6},{4,0},{6,2},{8,12},{10,14},{12,8},{14,10},{16,20},{18,... | collective-permute-start | bytes 258056 | tf_op jit(solution)/shard_map/ppermute | solution.py:354
  24.9 5.0 %collective-permute-start.9 = (bf16[32,1344]{1,0:T(8,128)(2,1)S(1)}, bf16[32,1344]{1,0:T(8,128)(2,1)S(1)}, u32[]{:S(2)}, u32[]{:S(2)}) collective-permute-start(bf16[32,1344]{1,0:T(8,128)(2,1)S(1)} %relay.1), channel_id=1, source_target_pairs={{1,9},{3,11},{5,13},{7,15},{9,1},{11,3},{13,5},{15,7},{17,25},{19,... | collective-permute-start | bytes 258056 | tf_op jit(solution)/shard_map/ppermute | solution.py:354
  30.1 7.1 %collective-permute-start.13 = (bf16[32,1408]{1,0:T(8,128)(2,1)S(1)}, bf16[32,1408]{1,0:T(8,128)(2,1)S(1)}, u32[]{:S(2)}, u32[]{:S(2)}) collective-permute-start(bf16[32,1408]{1,0:T(8,128)(2,1)S(1)} %get-tuple-element.69.rest_0_), channel_id=1, source_target_pairs={{0,8},{4,12},{8,0},{12,4},{1,9},{5,13},{9,1},{13,5},{2,10},{6,14},... | collective-permute-start | bytes 270344 | tf_op jit(solution)/shard_map/ppermute | solution.py:344
  31.5 8.7 %collective-permute-start.12 = (bf16[32,1408]{1,0:T(8,128)(2,1)S(1)}, bf16[32,1408]{1,0:T(8,128)(2,1)S(1)}, u32[]{:S(2)}, u32[]{:S(2)}) collective-permute-start(bf16[32,1408]{1,0:T(8,128)(2,1)S(1)} %get-tuple-element.69.rest_0_), channel_id=1, source_target_pairs={{0,6},{1,7},{2,4},{3,5},{4,2},{5,3},{6,0},{7,1},{8,14},{9,15},{10,... | collective-permute-start | bytes 270344 | tf_op jit(solution)/shard_map/ppermute | solution.py:344
  34.8 5.9 %collective-permute-start.11 = (bf16[32,1408]{1,0:T(8,128)(2,1)S(1)}, bf16[32,1408]{1,0:T(8,128)(2,1)S(1)}, u32[]{:S(2)}, u32[]{:S(2)}) collective-permute-start(bf16[32,1408]{1,0:T(8,128)(2,1)S(1)} %get-tuple-element.69.rest_0_), channel_id=1, source_target_pairs={{0,4},{1,5},{2,6},{3,7},{4,0},{5,1},{6,2},{7,3},{8,12},{9,13},{10,... | collective-permute-start | bytes 270344 | tf_op jit(solution)/shard_map/ppermute | solution.py:344
  34.8 5.9 %collective-permute-start.10 = (bf16[32,1408]{1,0:T(8,128)(2,1)S(1)}, bf16[32,1408]{1,0:T(8,128)(2,1)S(1)}, u32[]{:S(2)}, u32[]{:S(2)}) collective-permute-start(bf16[32,1408]{1,0:T(8,128)(2,1)S(1)} %get-tuple-element.69.rest_0_), channel_id=1, source_target_pairs={{0,2},{1,3},{2,0},{3,1},{4,6},{5,7},{6,4},{7,5},{8,10},{9,11},{10,... | collective-permute-start | bytes 270344 | tf_op jit(solution)/shard_map/ppermute | solution.py:344
  37.2 6.2 %collective-permute-start.16 = (bf16[32,1408]{1,0:T(8,128)(2,1)S(1)}, bf16[32,1408]{1,0:T(8,128)(2,1)S(1)}, u32[]{:S(2)}, u32[]{:S(2)}) collective-permute-start(bf16[32,1408]{1,0:T(8,128)(2,1)S(1)} %collective-permute-done.13.rest_0_), channel_id=1, source_target_pairs={{0,6},{1,7},{2,4},{3,5},{4,2},{5,3},{6,0},{7,1},{8,14},{9,15},{10,... | collective-permute-start | bytes 270344 | tf_op jit(solution)/shard_map/ppermute | solution.py:344
  38.3 5.4 %collective-permute-start.15 = (bf16[32,1408]{1,0:T(8,128)(2,1)S(1)}, bf16[32,1408]{1,0:T(8,128)(2,1)S(1)}, u32[]{:S(2)}, u32[]{:S(2)}) collective-permute-start(bf16[32,1408]{1,0:T(8,128)(2,1)S(1)} %collective-permute-done.13.rest_0_), channel_id=1, source_target_pairs={{0,4},{1,5},{2,6},{3,7},{4,0},{5,1},{6,2},{7,3},{8,12},{9,13},{10,... | collective-permute-start | bytes 270344 | tf_op jit(solution)/shard_map/ppermute | solution.py:344
  40.2 4.5 %collective-permute-start.14 = (bf16[32,1408]{1,0:T(8,128)(2,1)S(1)}, bf16[32,1408]{1,0:T(8,128)(2,1)S(1)}, u32[]{:S(2)}, u32[]{:S(2)}) collective-permute-start(bf16[32,1408]{1,0:T(8,128)(2,1)S(1)} %collective-permute-done.13.rest_0_), channel_id=1, source_target_pairs={{0,2},{1,3},{2,0},{3,1},{4,6},{5,7},{6,4},{7,5},{8,10},{9,11},{10,... | collective-permute-start | bytes 270344 | tf_op jit(solution)/shard_map/ppermute | solution.py:344
  47.5 6.5 %collective-permute-start.17 = (bf16[32,1344]{1,0:T(8,128)(2,1)S(1)}, bf16[32,1344]{1,0:T(8,128)(2,1)S(1)}, u32[]{:S(2)}, u32[]{:S(2)}) collective-permute-start(bf16[32,1344]{1,0:T(8,128)(2,1)S(1)} %get-tuple-element.80), channel_id=1, source_target_pairs={{0,6},{1,7},{2,4},{3,5},{4,2},{5,3},{6,0},{7,1},{8,14},{9,15},{10,... | collective-permute-start | bytes 258056 | tf_op jit(solution)/shard_map/ppermute | solution.py:344
  48.6 5.5 %collective-permute-start.18 = (bf16[32,1344]{1,0:T(8,128)(2,1)S(1)}, bf16[32,1344]{1,0:T(8,128)(2,1)S(1)}, u32[]{:S(2)}, u32[]{:S(2)}) collective-permute-start(bf16[32,1344]{1,0:T(8,128)(2,1)S(1)} %get-tuple-element.81), channel_id=1, source_target_pairs={{0,4},{1,5},{2,6},{3,7},{4,0},{5,1},{6,2},{7,3},{8,12},{9,13},{10,... | collective-permute-start | bytes 258056 | tf_op jit(solution)/shard_map/ppermute | solution.py:344
  49.5 5.3 %collective-permute-start.19 = (bf16[32,1344]{1,0:T(8,128)(2,1)S(1)}, bf16[32,1344]{1,0:T(8,128)(2,1)S(1)}, u32[]{:S(2)}, u32[]{:S(2)}) collective-permute-start(bf16[32,1344]{1,0:T(8,128)(2,1)S(1)} %get-tuple-element.82), channel_id=1, source_target_pairs={{0,2},{1,3},{2,0},{3,1},{4,6},{5,7},{6,4},{7,5},{8,10},{9,11},{10,... | collective-permute-start | bytes 258056 | tf_op jit(solution)/shard_map/ppermute | solution.py:344
  51.0 9.3 %collective-permute-start.21 = (bf16[32,1344]{1,0:T(8,128)(2,1)S(1)}, bf16[32,1344]{1,0:T(8,128)(2,1)S(1)}, u32[]{:S(2)}, u32[]{:S(2)}) collective-permute-start(bf16[32,1344]{1,0:T(8,128)(2,1)S(1)} %get-tuple-element.86), channel_id=1, source_target_pairs={{0,6},{1,7},{2,4},{3,5},{4,2},{5,3},{6,0},{7,1},{8,14},{9,15},{10,... | collective-permute-start | bytes 258056 | tf_op jit(solution)/shard_map/ppermute | solution.py:344
  54.9 6.3 %collective-permute-start.20 = (bf16[32,1344]{1,0:T(8,128)(2,1)S(1)}, bf16[32,1344]{1,0:T(8,128)(2,1)S(1)}, u32[]{:S(2)}, u32[]{:S(2)}) collective-permute-start(bf16[32,1344]{1,0:T(8,128)(2,1)S(1)} %sum.1), channel_id=1, source_target_pairs={{0,8},{4,12},{8,0},{12,4},{1,9},{5,13},{9,1},{13,5},{2,10},{6,14},... | collective-permute-start | bytes 258056 | tf_op jit(solution)/shard_map/ppermute | solution.py:344
  58.5 4.5 %collective-permute-start.22 = (bf16[32,1344]{1,0:T(8,128)(2,1)S(1)}, bf16[32,1344]{1,0:T(8,128)(2,1)S(1)}, u32[]{:S(2)}, u32[]{:S(2)}) collective-permute-start(bf16[32,1344]{1,0:T(8,128)(2,1)S(1)} %get-tuple-element.87), channel_id=1, source_target_pairs={{0,4},{1,5},{2,6},{3,7},{4,0},{5,1},{6,2},{7,3},{8,12},{9,13},{10,... | collective-permute-start | bytes 258056 | tf_op jit(solution)/shard_map/ppermute | solution.py:344
  60.3 4.5 %collective-permute-start.23 = (bf16[32,1344]{1,0:T(8,128)(2,1)S(1)}, bf16[32,1344]{1,0:T(8,128)(2,1)S(1)}, u32[]{:S(2)}, u32[]{:S(2)}) collective-permute-start(bf16[32,1344]{1,0:T(8,128)(2,1)S(1)} %get-tuple-element.88), channel_id=1, source_target_pairs={{0,2},{1,3},{2,0},{3,1},{4,6},{5,7},{6,4},{7,5},{8,10},{9,11},{10,... | collective-permute-start | bytes 258056 | tf_op jit(solution)/shard_map/ppermute | solution.py:344

commit v16 on v14

--- a/solution.py
+++ b/solution.py
@@ -310,8 +310,8 @@
     rows_ref[:, :width] = (value * scale * gain_ref[...]).astype(BF16)
 
 
-def expert_kernel(experts, count, up_ref, down_ref, other_up_ref, other_down_ref, *rest):
-    ins, outs = rest[:count], rest[count:]
+def expert_kernel(experts, count, carried, up_ref, down_ref, other_up_ref, other_down_ref, *rest):
+    ins, done, outs = rest[:count], rest[count : count + len(carried)], rest[count + len(carried) :]
     width = up_ref.shape[2]
     start = width // LANES * LANES
     rows = jnp.concatenate([ref[:, :width] for ref in ins], axis=0)
@@ -327,24 +327,27 @@
         chosen = (lane == expert) | (lane == expert + experts)
         gate = jnp.sum(jnp.where(chosen, tail, 0.0), axis=1, keepdims=True)
         total = total + jnp.dot(activated, down_of[0], preferred_element_type=F32) * gate
-    at = 0
-    for out in outs:
-        out[...] = total[at : at + out.shape[0]].astype(BF16)
-        at += out.shape[0]
+    size = ins[0].shape[0]
+    for at, out in enumerate(outs):
+        out[0:size] = total[at * size : (at + 1) * size].astype(BF16)
+    for at, ref in zip(carried, done):
+        outs[at][size:] = ref[...]
 
 
 def sum_kernel(*refs):
+    rows = refs[-1].shape[0]
     total = refs[0][...].astype(F32)
     for ref in refs[1:-1]:
-        total = total + ref[...].astype(F32)
+        total = total + ref[0:rows].astype(F32)
     refs[-1][...] = total.astype(BF16)
 
 
 def last_kernel(hidden_ref, *rest):
     parts, out_ref = rest[:-1], rest[-1]
+    rows = out_ref.shape[1]
     total = parts[0][...].astype(F32)
     for part in parts[1:]:
-        total = total + part[...].astype(F32)
+        total = total + part[part.shape[0] - rows :].astype(F32)
     out_ref[0] = (hidden_ref[...].astype(F32) + total).astype(BF16)
 
 
@@ -467,33 +470,38 @@
         [(ANY, up_held)] + [(VMEM, value) for value in (resid_held, gate_lanes, gain_held, *parts)],
     )
 
-    def through_experts(members):
+    def through_experts(members, carried=()):
+        places = [at for at, _ in carried]
         return call(
-            functools.partial(expert_kernel, experts, len(members)),
+            functools.partial(expert_kernel, experts, len(members), places),
             "experts",
-            [struct((rows, model), BF16)] * len(members),
-            [(VMEM, value) for value in (up_held, down_held, other_up, other_down, *members)],
+            [struct((rows * (2 if at in places else 1), model), BF16) for at in range(len(members))],
+            [(VMEM, value) for value in (up_held, down_held, other_up, other_down, *members)]
+            + [(VMEM, value) for _, value in carried],
             megabytes=16,
         )
 
     both = ("head", "exp")
-    group = [z * exp_size + 2 * d for z in (1, 0) for d in reversed(range(chips))][:-1]
+    group = [z * exp_size + 2 * d for z in (0, 1) for d in range(chips)][1:]
 
     def spread(block):
-        return [block] + [swap(block, both, mask) for mask in reversed(group)]
+        return [block] + [swap(block, both, mask) for mask in group]
 
     sets = [spread(swap(own_rows, "head", high)) for high in range(2, head_size, 2)]
     near = through_experts(spread(own_rows))
     near, sets = lax.optimization_barrier((near, sets))
-    far = [through_experts(members) for members in sets]
-    arrived, near = [], list(near)
-    for high, pieces in zip(range(2, head_size, 2), far):
-        got = [swap(piece, both, mask) for piece, mask in zip(pieces[:0:-1], group)]
+    joined = [at for at, mask in enumerate(group, 1) if mask >= exp_size]
+    arrived, later = [], [at for at in range(1, len(near)) if at not in joined]
+    apart = [near[at] for at in later]
+    for high, members in zip(range(2, head_size, 2), sets):
+        pieces = through_experts(members, [(at, near[at]) for at in joined] if high == 2 else ())
+        got = [swap(piece, both, mask) for piece, mask in zip(pieces[:0:-1], group[::-1])]
         total = call(sum_kernel, "sum", struct((rows, model), BF16), [(VMEM, v) for v in (pieces[0], *got)])
         if high == 2:
-            total, near[1:-1] = lax.optimization_barrier((total, near[1:-1]))
+            total, apart = lax.optimization_barrier((total, apart))
+            arrived += [part for part, mask in zip(got, group[::-1]) if mask >= exp_size]
         arrived.append(swap(total, "head", high))
-    arrived += [swap(piece, both, mask) for piece, mask in zip(near[:0:-1], group)]
+    arrived += [swap(piece, both, group[at - 1]) for piece, at in zip(apart, later)]
     return call(
         last_kernel,
         "last",

time: 62.7 us -> 62.1 us (level)
  starting transfers between devices: 29.3 us -> 26.2 us
  waiting for transfers between devices: 14.2 us -> 16.8 us
    ppermute x20 -> x18, starting transfers between devices: 25.4 us -> 22.3 us  [swap(): return lax.ppermute(value, axis, [(i, i ^ mask) for i in range(size)])]
    ppermute x20 -> x18, waiting for transfers between devices: 9.65 us -> 12.2 us  [swap(): return lax.ppermute(value, axis, [(i, i ^ mask) for i in range(size)])]
  transfers between devices with their start and end apart: 23 -> 21, of which waited for: 14 -> 12; matrix products, arithmetic and copies ran while one was open for 2% -> 2% of each run, Pallas kernels for 18% -> 18%
where the time goes in v16:
time: 62.1 us; the launch traced here: 61.8 us
  starting transfers between devices  26.2 us (42%)
  Pallas kernels  17.3 us (28%)
  waiting for transfers between devices  16.8 us (27%)
  local copies, waits for them, and re-layouts  1.29 us (2%)
    ppermute x18, starting transfers between devices, swap(): return lax.ppermute(value, axis, [(i, i ^ mask) for i in range(size)])  22.3 us
    pallas_call x15, Pallas kernels, call(): pl.pallas_call(kernel, out_shape=jax.tree.map(lambda out: pltpu.VMEM(out....  17.3 us
    ppermute x18, waiting for transfers between devices, swap(): return lax.ppermute(value, axis, [(i, i ^ mask) for i in range(size)])  12.2 us
    ppermute x3, waiting for transfers between devices, swap_slot(): return lax.ppermute(value, ('head', 'exp'), pairs)  4.58 us
    ppermute x3, starting transfers between devices, swap_slot(): return lax.ppermute(value, ('head', 'exp'), pairs)  3.92 us
    broadcast_in_dim x1, local copies, waits for them, and re-layouts, per_device(): moe_gain[None]  1.29 us
  transfers between devices with their start and end apart: 21, of which 12 were waited for; matrix products, arithmetic and copies ran while one was open for 2% of the time, Pallas kernels for 18%

profile of v16, /device:TPU:0, one launch (start us, length us, event | category | flops | bytes accessed | tf_op | source)
XLA Modules:
  0.0 61.8 jit_solution(9777246481764708034)
XLA Ops:
  0.0 1.8 %state.1 = (bf16[528,128]{1,0:T(8,128)(2,1)S(1)}, bf16[528,128]{1,0:T(8,128)(2,1)S(1)}) custom-call(bf16[128,1024]{1,0:T(8,128)(2,1)} %x_hbm.3, bf16[128,256]{1,0:T(8,128)(2,1)} %b_hbm.3, f32[16,128]{1,0:T(8,128)} %bitcast.11, f32[1,16]{1,0:T(1,128)} %bitcast.16), custom_call_target="tpu_custom_call" | custom-call | tf_op jit(solution)/shard_map/state/pallas_call | solution.py:29
  1.8 0.5 collective-permute-start
  2.3 1.0 %collective-permute-done.got_ref = bf16[528,128]{1,0:T(8,128)(2,1)S(1)} collective-permute-done((bf16[528,128]{1,0:T(8,128)(2,1)S(1)}, bf16[528,128]{1,0:T(8,128)(2,1)S(1)}, u32[]{:S(2)}, u32[]{:S(2)}) %collective-permute-start) | collective-permute-done | bytes 135200 | tf_op jit(solution)/shard_map/ppermute | solution.py:356
  3.3 0.1 chip_state.1.rest_0_
  3.4 0.4 collective-permute-start.1
  3.9 0.1 collective-permute-start.2
  4.0 2.9 %collective-permute-start.3 = (bf16[528,128]{1,0:T(8,128)(2,1)S(1)}, bf16[528,128]{1,0:T(8,128)(2,1)S(1)}, u32[]{:S(2)}, u32[]{:S(2)}) collective-permute-start(bf16[528,128]{1,0:T(8,128)(2,1)S(1)} %chip_state.1.rest_0_), channel_id=1, source_target_pairs={{0,2},{1,3},{2,0},{3,1},{4,6},{5,7},{6,4},{7,5},{8,10},{9,11},{10,... | collective-permute-start | bytes 405512 | tf_op jit(solution)/shard_map/ppermute | solution.py:356
  6.9 2.4 %inside.1 = (f32[128,1024]{1,0:T(8,128)S(1)}, f32[128,1024]{1,0:T(8,128)S(1)}, bf16[128,256]{1,0:T(8,128)(2,1)S(1)}) custom-call(bf16[128,1024]{1,0:T(8,128)(2,1)} %x_hbm.3, bf16[128,1024]{1,0:T(8,128)(2,1)} %z_hbm.1, bf16[128,256]{1,0:T(8,128)(2,1)} %b_hbm.3, bf16[128,256]{1,0:T(8,128)(2,1)} %c_hbm.1, f32[16,128]{1,0:T(8,128)} %bitcast.12, ...), custom_call_target="tpu_custom_call" | custom-call | tf_op jit(solution)/shard_map/inside/pallas_call | solution.py:29
  9.3 1.4 %collective-permute-done.3.rest_1_ = bf16[528,128]{1,0:T(8,128)(2,1)S(1)} collective-permute-done((bf16[528,128]{1,0:T(8,128)(2,1)S(1)}, bf16[528,128]{1,0:T(8,128)(2,1)S(1)}, u32[]{:S(2)}, u32[]{:S(2)}) %collective-permute-start.3) | collective-permute-done | bytes 135200 | tf_op jit(solution)/shard_map/ppermute | solution.py:356
  10.8 0.1 span.1.rest_2_
  10.9 1.8 %collective-permute-start.4 = (bf16[528,128]{1,0:T(8,128)(2,1)S(1)}, bf16[528,128]{1,0:T(8,128)(2,1)S(1)}, u32[]{:S(2)}, u32[]{:S(2)}) collective-permute-start(bf16[528,128]{1,0:T(8,128)(2,1)S(1)} %span.1.rest_2_), channel_id=1, source_target_pairs={{0,16},{16,0},{1,17},{17,1},{2,18},{18,2},{3,19},{19,3},{4,20},{20... | collective-permute-start | bytes 405512 | tf_op jit(solution)/shard_map/ppermute | solution.py:356
  12.7 1.3 %broadcast_in_dim.14.gain_hbm = f32[1,1344]{1,0:T(1,128)} reshape(f32[1344]{0:T(1024)} %param.27) | data formatting | bytes 10752 | tf_op jit(solution)/shard_map/broadcast_in_dim | solution.py:411
  14.0 1.9 %prep.1 = (bf16[32,128]{1,0:T(8,128)(2,1)S(1)}, bf16[1,32,1344]{2,1,0:T(8,128)(2,1)S(1)}, f32[1,1344]{1,0:T(1,128)S(1)}, f32[1,1024]{1,0:T(1,128)S(1)}, bf16[1344,1024]{1,0:T(8,128)(2,1)S(1)}) custom-call(bf16[1,32,1344]{2,1,0:T(8,128)(2,1)} %resid_hbm.1, s32[6,1,32]{2,1,0:T(1,128)} %bitcast.14, f32[6,1,32]{2,1,0:T(1,128)} %bitcast.15, ...), custom_call_target="tpu_custom_call" | custom-call | tf_op jit(solution)/shard_map/prep/pallas_call | solution.py:29
  15.9 0.2 collective-permute-done.4.rest_3_
  16.1 0.3 before.1
  16.4 0.1 collective-permute-start.5
  16.4 0.8 %first_half.1.first_ref = f32[128,1344]{1,0:T(8,128)S(1)} custom-call(f32[128,1024]{1,0:T(8,128)S(1)} %get-tuple-element.50.local_ref, f32[128,1024]{1,0:T(8,128)S(1)} %get-tuple-element.51.grown_ref, bf16[128,256]{1,0:T(8,128)(2,1)S(1)} %get-tuple-element.52.after_ref.c_ref, f32[1,1024]{1,0:T(1,128)S(1)} %get-tuple-element.53.norm_ref, ...), custom_call_target="tpu_custom_call" | custom-call | tf_op jit(solution)/shard_map/first_half/pallas_call | solution.py:29
  17.3 0.5 collective-permute-done.5.got_ref
  17.8 0.9 %mixed.1 = (bf16[32,1344]{1,0:T(8,128)(2,1)S(1)}, bf16[32,1344]{1,0:T(8,128)(2,1)S(1)}, bf16[32,1344]{1,0:T(8,128)(2,1)S(1)}, bf16[32,1344]{1,0:T(8,128)(2,1)S(1)}) custom-call(bf16[1,928,1344]{2,1,0:T(8,128)(2,1)S(1)} %collective-permute-done.1.after_up.other_up_ref, bf16[1,928,1344]{2,1,0:T(8,128)(2,1)S(1)} %collective-permute-done.2.after_down.other_down_ref, ...), custom_call_target="tpu_custom_call" | custom-call | tf_op jit(solution)/shard_map/mixed/pallas_call | solution.py:29
  18.6 1.8 %collective-permute-start.6 = (bf16[32,1344]{1,0:T(8,128)(2,1)S(1)}, bf16[32,1344]{1,0:T(8,128)(2,1)S(1)}, u32[]{:S(2)}, u32[]{:S(2)}) collective-permute-start(bf16[32,1344]{1,0:T(8,128)(2,1)S(1)} %get-tuple-element.63), channel_id=1, source_target_pairs={{0,4},{1,9},{2,6},{3,11},{4,0},{5,13},{6,2},{7,15},{8,12},{9,1},{1... | collective-permute-start | bytes 258056 | tf_op jit(solution)/shard_map/ppermute | solution.py:366
  20.4 0.3 collective-permute-start.7
  20.7 3.5 %collective-permute-done.6.got_ref.rest_1_ = bf16[32,1344]{1,0:T(8,128)(2,1)S(1)} collective-permute-done((bf16[32,1344]{1,0:T(8,128)(2,1)S(1)}, bf16[32,1344]{1,0:T(8,128)(2,1)S(1)}, u32[]{:S(2)}, u32[]{:S(2)}) %collective-permute-start.6) | collective-permute-done | bytes 86048 | tf_op jit(solution)/shard_map/ppermute | solution.py:366
  24.3 1.8 %collective-permute-start.8 = (bf16[32,1344]{1,0:T(8,128)(2,1)S(1)}, bf16[32,1344]{1,0:T(8,128)(2,1)S(1)}, u32[]{:S(2)}, u32[]{:S(2)}) collective-permute-start(bf16[32,1344]{1,0:T(8,128)(2,1)S(1)} %relay.1), channel_id=1, source_target_pairs={{0,8},{1,5},{2,10},{3,7},{4,12},{5,1},{6,14},{7,3},{8,0},{9,13},{1... | collective-permute-start | bytes 258056 | tf_op jit(solution)/shard_map/ppermute | solution.py:366
  26.1 2.5 %weights.1 = (bf16[1,928,1344]{2,1,0:T(8,128)(2,1)S(1)}, bf16[1,928,1344]{2,1,0:T(8,128)(2,1)S(1)}) custom-call(bf16[32,1344]{1,0:T(8,128)(2,1)S(1)} %get-tuple-element.59.after_ref.rest_0_, bf16[1,928,1344]{2,1,0:T(8,128)(2,1)} %bitcast.10, bf16[1,928,1344]{2,1,0:T(8,128)(2,1)} %down_hbm.1), custom_call_target="tpu_custom_call" | custom-call | tf_op jit(solution)/shard_map/weights/pallas_call | solution.py:29
  28.6 0.0 collective-permute-done.7.rest_2_
  28.6 1.1 %collective-permute-done.8.rest_3_ = bf16[32,1344]{1,0:T(8,128)(2,1)S(1)} collective-permute-done((bf16[32,1344]{1,0:T(8,128)(2,1)S(1)}, bf16[32,1344]{1,0:T(8,128)(2,1)S(1)}, u32[]{:S(2)}, u32[]{:S(2)}) %collective-permute-start.8) | collective-permute-done | bytes 86048 | tf_op jit(solution)/shard_map/ppermute | solution.py:366
  29.8 0.2 rows.1
  29.9 1.8 %collective-permute-start.12 = (bf16[32,1408]{1,0:T(8,128)(2,1)S(1)}, bf16[32,1408]{1,0:T(8,128)(2,1)S(1)}, u32[]{:S(2)}, u32[]{:S(2)}) collective-permute-start(bf16[32,1408]{1,0:T(8,128)(2,1)S(1)} %get-tuple-element.68.rest_0_), channel_id=1, source_target_pairs={{0,8},{4,12},{8,0},{12,4},{1,9},{5,13},{9,1},{13,5},{2,10},{6,14},... | collective-permute-start | bytes 270344 | tf_op jit(solution)/shard_map/ppermute | solution.py:356
  31.8 3.4 %collective-permute-start.11 = (bf16[32,1408]{1,0:T(8,128)(2,1)S(1)}, bf16[32,1408]{1,0:T(8,128)(2,1)S(1)}, u32[]{:S(2)}, u32[]{:S(2)}) collective-permute-start(bf16[32,1408]{1,0:T(8,128)(2,1)S(1)} %get-tuple-element.68.rest_0_), channel_id=1, source_target_pairs={{0,6},{1,7},{2,4},{3,5},{4,2},{5,3},{6,0},{7,1},{8,14},{9,15},{10,... | collective-permute-start | bytes 270344 | tf_op jit(solution)/shard_map/ppermute | solution.py:356
  35.2 0.0 collective-permute-start.10
  35.2 0.5 collective-permute-start.9
  35.7 3.0 %collective-permute-start.15 = (bf16[32,1408]{1,0:T(8,128)(2,1)S(1)}, bf16[32,1408]{1,0:T(8,128)(2,1)S(1)}, u32[]{:S(2)}, u32[]{:S(2)}) collective-permute-start(bf16[32,1408]{1,0:T(8,128)(2,1)S(1)} %collective-permute-done.12.rest_0_), channel_id=1, source_target_pairs={{0,6},{1,7},{2,4},{3,5},{4,2},{5,3},{6,0},{7,1},{8,14},{9,15},{10,... | collective-permute-start | bytes 270344 | tf_op jit(solution)/shard_map/ppermute | solution.py:356
  38.7 1.1 %collective-permute-start.14 = (bf16[32,1408]{1,0:T(8,128)(2,1)S(1)}, bf16[32,1408]{1,0:T(8,128)(2,1)S(1)}, u32[]{:S(2)}, u32[]{:S(2)}) collective-permute-start(bf16[32,1408]{1,0:T(8,128)(2,1)S(1)} %collective-permute-done.12.rest_0_), channel_id=1, source_target_pairs={{0,4},{1,5},{2,6},{3,7},{4,0},{5,1},{6,2},{7,3},{8,12},{9,13},{10,... | collective-permute-start | bytes 270344 | tf_op jit(solution)/shard_map/ppermute | solution.py:356
  39.8 1.0 %collective-permute-done.10.rest_2_ = bf16[32,1408]{1,0:T(8,128)(2,1)S(1)} collective-permute-done((bf16[32,1408]{1,0:T(8,128)(2,1)S(1)}, bf16[32,1408]{1,0:T(8,128)(2,1)S(1)}, u32[]{:S(2)}, u32[]{:S(2)}) %collective-permute-start.10) | collective-permute-done | bytes 90144 | tf_op jit(solution)/shard_map/ppermute | solution.py:356
  40.7 1.4 %collective-permute-done.9.rest_1_ = bf16[32,1408]{1,0:T(8,128)(2,1)S(1)} collective-permute-done((bf16[32,1408]{1,0:T(8,128)(2,1)S(1)}, bf16[32,1408]{1,0:T(8,128)(2,1)S(1)}, u32[]{:S(2)}, u32[]{:S(2)}) %collective-permute-start.9) | collective-permute-done | bytes 90144 | tf_op jit(solution)/shard_map/ppermute | solution.py:356
  42.1 2.7 %experts.2 = (bf16[32,1344]{1,0:T(8,128)(2,1)S(1)}, bf16[32,1344]{1,0:T(8,128)(2,1)S(1)}, bf16[32,1344]{1,0:T(8,128)(2,1)S(1)}, bf16[32,1344]{1,0:T(8,128)(2,1)S(1)}) custom-call(bf16[1,928,1344]{2,1,0:T(8,128)(2,1)S(1)} %get-tuple-element.60.after_ref.up_ref, bf16[1,928,1344]{2,1,0:T(8,128)(2,1)S(1)} %get-tuple-element.67.down_ref, ...), custom_call_target="tpu_custom_call" | custom-call | tf_op jit(solution)/shard_map/experts/pallas_call | solution.py:29
  44.9 2.7 %experts.3 = (bf16[32,1344]{1,0:T(8,128)(2,1)S(1)}, bf16[32,1344]{1,0:T(8,128)(2,1)S(1)}, bf16[64,1344]{1,0:T(8,128)(2,1)S(1)}, bf16[64,1344]{1,0:T(8,128)(2,1)S(1)}) custom-call(bf16[1,928,1344]{2,1,0:T(8,128)(2,1)S(1)} %get-tuple-element.60.after_ref.up_ref, bf16[1,928,1344]{2,1,0:T(8,128)(2,1)S(1)} %get-tuple-element.67.down_ref, ...), custom_call_target="tpu_custom_call" | custom-call | tf_op jit(solution)/shard_map/experts/pallas_call | solution.py:29
  47.6 1.4 %collective-permute-start.16 = (bf16[64,1344]{1,0:T(8,128)(2,1)S(1)}, bf16[64,1344]{1,0:T(8,128)(2,1)S(1)}, u32[]{:S(2)}, u32[]{:S(2)}) collective-permute-start(bf16[64,1344]{1,0:T(8,128)(2,1)S(1)} %get-tuple-element.80), channel_id=1, source_target_pairs={{0,6},{1,7},{2,4},{3,5},{4,2},{5,3},{6,0},{7,1},{8,14},{9,15},{10,... | collective-permute-start | bytes 516104 | tf_op jit(solution)/shard_map/ppermute | solution.py:356
  48.9 0.1 collective-permute-start.17
  49.1 2.1 %collective-permute-start.18 = (bf16[32,1344]{1,0:T(8,128)(2,1)S(1)}, bf16[32,1344]{1,0:T(8,128)(2,1)S(1)}, u32[]{:S(2)}, u32[]{:S(2)}) collective-permute-start(bf16[32,1344]{1,0:T(8,128)(2,1)S(1)} %get-tuple-element.83), channel_id=1, source_target_pairs={{0,2},{1,3},{2,0},{3,1},{4,6},{5,7},{6,4},{7,5},{8,10},{9,11},{10,... | collective-permute-start | bytes 258056 | tf_op jit(solution)/shard_map/ppermute | solution.py:356
  51.1 4.2 %collective-permute-done.18.refs_3_ = bf16[32,1344]{1,0:T(8,128)(2,1)S(1)} collective-permute-done((bf16[32,1344]{1,0:T(8,128)(2,1)S(1)}, bf16[32,1344]{1,0:T(8,128)(2,1)S(1)}, u32[]{:S(2)}, u32[]{:S(2)}) %collective-permute-start.18) | collective-permute-done | bytes 86048 | tf_op jit(solution)/shard_map/ppermute | solution.py:356
  55.3 0.1 collective-permute-done.17.refs_2_.rest_2_
  55.4 0.1 sum.1
  55.5 0.9 %collective-permute-start.19 = (bf16[32,1344]{1,0:T(8,128)(2,1)S(1)}, bf16[32,1344]{1,0:T(8,128)(2,1)S(1)}, u32[]{:S(2)}, u32[]{:S(2)}) collective-permute-start(bf16[32,1344]{1,0:T(8,128)(2,1)S(1)} %sum.1), channel_id=1, source_target_pairs={{0,8},{4,12},{8,0},{12,4},{1,9},{5,13},{9,1},{13,5},{2,10},{6,14},... | collective-permute-start | bytes 258056 | tf_op jit(solution)/shard_map/ppermute | solution.py:356
  56.4 2.1 %collective-permute-start.20 = (bf16[32,1344]{1,0:T(8,128)(2,1)S(1)}, bf16[32,1344]{1,0:T(8,128)(2,1)S(1)}, u32[]{:S(2)}, u32[]{:S(2)}) collective-permute-start(bf16[32,1344]{1,0:T(8,128)(2,1)S(1)} %get-tuple-element.86), channel_id=1, source_target_pairs={{0,2},{1,3},{2,0},{3,1},{4,6},{5,7},{6,4},{7,5},{8,10},{9,11},{10,... | collective-permute-start | bytes 258056 | tf_op jit(solution)/shard_map/ppermute | solution.py:356
  58.5 2.4 %collective-permute-done.19.rest_3_ = bf16[32,1344]{1,0:T(8,128)(2,1)S(1)} collective-permute-done((bf16[32,1344]{1,0:T(8,128)(2,1)S(1)}, bf16[32,1344]{1,0:T(8,128)(2,1)S(1)}, u32[]{:S(2)}, u32[]{:S(2)}) %collective-permute-start.19) | collective-permute-done | bytes 86048 | tf_op jit(solution)/shard_map/ppermute | solution.py:356
  61.0 0.1 collective-permute-done.20.rest_4_
  61.0 0.7 %last.1 = bf16[1,32,1344]{2,1,0:T(8,128)(2,1)} custom-call(bf16[32,1344]{1,0:T(8,128)(2,1)S(1)} %get-tuple-element.66.hidden_ref, bf16[32,1344]{1,0:T(8,128)(2,1)S(1)} %get-tuple-element.73.rest_0_, bf16[64,1344]{1,0:T(8,128)(2,1)S(1)} %collective-permute-done.16.refs_1_.rest_1_, bf16[64,1344]{1,0:T(8,128)(2,1)S(1)} %collective-permute-done.17.refs_2_.rest_2_, ...), custom_call_target="tpu_custom_call" | custom-call | tf_op jit(solution)/shard_map/last/pallas_call | solution.py:29
  (10 shorter events, 0.1 us)
Async XLA Ops:
  1.8 1.5 %collective-permute-start = (bf16[528,128]{1,0:T(8,128)(2,1)S(1)}, bf16[528,128]{1,0:T(8,128)(2,1)S(1)}, u32[]{:S(2)}, u32[]{:S(2)}) collective-permute-start(bf16[528,128]{1,0:T(8,128)(2,1)S(1)} %get-tuple-element.47), channel_id=1, source_target_pairs={{0,1},{1,0},{2,3},{3,2},{4,5},{5,4},{6,7},{7,6},{8,9},{9,8},{10,11... | collective-permute-start | bytes 405512 | tf_op jit(solution)/shard_map/ppermute | solution.py:356
  3.4 14.3 %collective-permute-start.1 = (bf16[1,928,1344]{2,1,0:T(8,128)(2,1)}, bf16[1,928,1344]{2,1,0:T(8,128)(2,1)S(1)}, u32[]{:S(2)}, u32[]{:S(2)}) collective-permute-start(bf16[1,928,1344]{2,1,0:T(8,128)(2,1)} %bitcast.9), channel_id=1, source_target_pairs={{0,1},{1,0},{2,3},{3,2},{4,5},{5,4},{6,7},{7,6},{8,9},{9,8},{10,11... | collective-permute-start | bytes 7483400 | tf_op jit(solution)/shard_map/ppermute | solution.py:356
  3.9 13.9 %collective-permute-start.2 = (bf16[1,928,1344]{2,1,0:T(8,128)(2,1)}, bf16[1,928,1344]{2,1,0:T(8,128)(2,1)S(1)}, u32[]{:S(2)}, u32[]{:S(2)}) collective-permute-start(bf16[1,928,1344]{2,1,0:T(8,128)(2,1)} %down_hbm.1), channel_id=1, source_target_pairs={{0,1},{1,0},{2,3},{3,2},{4,5},{5,4},{6,7},{7,6},{8,9},{9,8},{10,11... | collective-permute-start | bytes 7483400 | tf_op jit(solution)/shard_map/ppermute | solution.py:356
  4.0 6.8 %collective-permute-start.3 = (bf16[528,128]{1,0:T(8,128)(2,1)S(1)}, bf16[528,128]{1,0:T(8,128)(2,1)S(1)}, u32[]{:S(2)}, u32[]{:S(2)}) collective-permute-start(bf16[528,128]{1,0:T(8,128)(2,1)S(1)} %chip_state.1.rest_0_), channel_id=1, source_target_pairs={{0,2},{1,3},{2,0},{3,1},{4,6},{5,7},{6,4},{7,5},{8,10},{9,11},{10,... | collective-permute-start | bytes 405512 | tf_op jit(solution)/shard_map/ppermute | solution.py:356
  10.9 5.2 %collective-permute-start.4 = (bf16[528,128]{1,0:T(8,128)(2,1)S(1)}, bf16[528,128]{1,0:T(8,128)(2,1)S(1)}, u32[]{:S(2)}, u32[]{:S(2)}) collective-permute-start(bf16[528,128]{1,0:T(8,128)(2,1)S(1)} %span.1.rest_2_), channel_id=1, source_target_pairs={{0,16},{16,0},{1,17},{17,1},{2,18},{18,2},{3,19},{19,3},{4,20},{20... | collective-permute-start | bytes 405512 | tf_op jit(solution)/shard_map/ppermute | solution.py:356
  16.4 1.4 %collective-permute-start.5 = (bf16[4,128,128]{2,1,0:T(8,128)(2,1)S(1)}, bf16[4,128,128]{2,1,0:T(8,128)(2,1)S(1)}, u32[]{:S(2)}, u32[]{:S(2)}) collective-permute-start(bf16[4,128,128]{2,1,0:T(8,128)(2,1)S(1)} %get-tuple-element.57), channel_id=1, source_target_pairs={{0,1},{1,0},{2,3},{3,2},{4,5},{5,4},{6,7},{7,6},{8,9},{9,8},{10,11... | collective-permute-start | bytes 393224 | tf_op jit(solution)/shard_map/ppermute | solution.py:356
  18.6 5.6 %collective-permute-start.6 = (bf16[32,1344]{1,0:T(8,128)(2,1)S(1)}, bf16[32,1344]{1,0:T(8,128)(2,1)S(1)}, u32[]{:S(2)}, u32[]{:S(2)}) collective-permute-start(bf16[32,1344]{1,0:T(8,128)(2,1)S(1)} %get-tuple-element.63), channel_id=1, source_target_pairs={{0,4},{1,9},{2,6},{3,11},{4,0},{5,13},{6,2},{7,15},{8,12},{9,1},{1... | collective-permute-start | bytes 258056 | tf_op jit(solution)/shard_map/ppermute | solution.py:366
  20.4 8.2 %collective-permute-start.7 = (bf16[32,1344]{1,0:T(8,128)(2,1)S(1)}, bf16[32,1344]{1,0:T(8,128)(2,1)S(1)}, u32[]{:S(2)}, u32[]{:S(2)}) collective-permute-start(bf16[32,1344]{1,0:T(8,128)(2,1)S(1)} %get-tuple-element.64), channel_id=1, source_target_pairs={{0,4},{1,13},{2,6},{3,15},{4,0},{5,9},{6,2},{7,11},{8,12},{9,5},{1... | collective-permute-start | bytes 258056 | tf_op jit(solution)/shard_map/ppermute | solution.py:366
  24.3 5.5 %collective-permute-start.8 = (bf16[32,1344]{1,0:T(8,128)(2,1)S(1)}, bf16[32,1344]{1,0:T(8,128)(2,1)S(1)}, u32[]{:S(2)}, u32[]{:S(2)}) collective-permute-start(bf16[32,1344]{1,0:T(8,128)(2,1)S(1)} %relay.1), channel_id=1, source_target_pairs={{0,8},{1,5},{2,10},{3,7},{4,12},{5,1},{6,14},{7,3},{8,0},{9,13},{1... | collective-permute-start | bytes 258056 | tf_op jit(solution)/shard_map/ppermute | solution.py:366
  29.9 5.8 %collective-permute-start.12 = (bf16[32,1408]{1,0:T(8,128)(2,1)S(1)}, bf16[32,1408]{1,0:T(8,128)(2,1)S(1)}, u32[]{:S(2)}, u32[]{:S(2)}) collective-permute-start(bf16[32,1408]{1,0:T(8,128)(2,1)S(1)} %get-tuple-element.68.rest_0_), channel_id=1, source_target_pairs={{0,8},{4,12},{8,0},{12,4},{1,9},{5,13},{9,1},{13,5},{2,10},{6,14},... | collective-permute-start | bytes 270344 | tf_op jit(solution)/shard_map/ppermute | solution.py:356
  31.8 8.0 %collective-permute-start.11 = (bf16[32,1408]{1,0:T(8,128)(2,1)S(1)}, bf16[32,1408]{1,0:T(8,128)(2,1)S(1)}, u32[]{:S(2)}, u32[]{:S(2)}) collective-permute-start(bf16[32,1408]{1,0:T(8,128)(2,1)S(1)} %get-tuple-element.68.rest_0_), channel_id=1, source_target_pairs={{0,6},{1,7},{2,4},{3,5},{4,2},{5,3},{6,0},{7,1},{8,14},{9,15},{10,... | collective-permute-start | bytes 270344 | tf_op jit(solution)/shard_map/ppermute | solution.py:356
  35.2 5.6 %collective-permute-start.10 = (bf16[32,1408]{1,0:T(8,128)(2,1)S(1)}, bf16[32,1408]{1,0:T(8,128)(2,1)S(1)}, u32[]{:S(2)}, u32[]{:S(2)}) collective-permute-start(bf16[32,1408]{1,0:T(8,128)(2,1)S(1)} %get-tuple-element.68.rest_0_), channel_id=1, source_target_pairs={{0,4},{1,5},{2,6},{3,7},{4,0},{5,1},{6,2},{7,3},{8,12},{9,13},{10,... | collective-permute-start | bytes 270344 | tf_op jit(solution)/shard_map/ppermute | solution.py:356
  35.2 6.9 %collective-permute-start.9 = (bf16[32,1408]{1,0:T(8,128)(2,1)S(1)}, bf16[32,1408]{1,0:T(8,128)(2,1)S(1)}, u32[]{:S(2)}, u32[]{:S(2)}) collective-permute-start(bf16[32,1408]{1,0:T(8,128)(2,1)S(1)} %get-tuple-element.68.rest_0_), channel_id=1, source_target_pairs={{0,2},{1,3},{2,0},{3,1},{4,6},{5,7},{6,4},{7,5},{8,10},{9,11},{10,... | collective-permute-start | bytes 270344 | tf_op jit(solution)/shard_map/ppermute | solution.py:356
  35.7 9.1 %collective-permute-start.15 = (bf16[32,1408]{1,0:T(8,128)(2,1)S(1)}, bf16[32,1408]{1,0:T(8,128)(2,1)S(1)}, u32[]{:S(2)}, u32[]{:S(2)}) collective-permute-start(bf16[32,1408]{1,0:T(8,128)(2,1)S(1)} %collective-permute-done.12.rest_0_), channel_id=1, source_target_pairs={{0,6},{1,7},{2,4},{3,5},{4,2},{5,3},{6,0},{7,1},{8,14},{9,15},{10,... | collective-permute-start | bytes 270344 | tf_op jit(solution)/shard_map/ppermute | solution.py:356
  38.7 6.2 %collective-permute-start.14 = (bf16[32,1408]{1,0:T(8,128)(2,1)S(1)}, bf16[32,1408]{1,0:T(8,128)(2,1)S(1)}, u32[]{:S(2)}, u32[]{:S(2)}) collective-permute-start(bf16[32,1408]{1,0:T(8,128)(2,1)S(1)} %collective-permute-done.12.rest_0_), channel_id=1, source_target_pairs={{0,4},{1,5},{2,6},{3,7},{4,0},{5,1},{6,2},{7,3},{8,12},{9,13},{10,... | collective-permute-start | bytes 270344 | tf_op jit(solution)/shard_map/ppermute | solution.py:356
  39.8 5.1 %collective-permute-start.13 = (bf16[32,1408]{1,0:T(8,128)(2,1)S(1)}, bf16[32,1408]{1,0:T(8,128)(2,1)S(1)}, u32[]{:S(2)}, u32[]{:S(2)}) collective-permute-start(bf16[32,1408]{1,0:T(8,128)(2,1)S(1)} %collective-permute-done.12.rest_0_), channel_id=1, source_target_pairs={{0,2},{1,3},{2,0},{3,1},{4,6},{5,7},{6,4},{7,5},{8,10},{9,11},{10,... | collective-permute-start | bytes 270344 | tf_op jit(solution)/shard_map/ppermute | solution.py:356
  47.6 7.7 %collective-permute-start.16 = (bf16[64,1344]{1,0:T(8,128)(2,1)S(1)}, bf16[64,1344]{1,0:T(8,128)(2,1)S(1)}, u32[]{:S(2)}, u32[]{:S(2)}) collective-permute-start(bf16[64,1344]{1,0:T(8,128)(2,1)S(1)} %get-tuple-element.80), channel_id=1, source_target_pairs={{0,6},{1,7},{2,4},{3,5},{4,2},{5,3},{6,0},{7,1},{8,14},{9,15},{10,... | collective-permute-start | bytes 516104 | tf_op jit(solution)/shard_map/ppermute | solution.py:356
  48.9 6.5 %collective-permute-start.17 = (bf16[64,1344]{1,0:T(8,128)(2,1)S(1)}, bf16[64,1344]{1,0:T(8,128)(2,1)S(1)}, u32[]{:S(2)}, u32[]{:S(2)}) collective-permute-start(bf16[64,1344]{1,0:T(8,128)(2,1)S(1)} %get-tuple-element.81), channel_id=1, source_target_pairs={{0,4},{1,5},{2,6},{3,7},{4,0},{5,1},{6,2},{7,3},{8,12},{9,13},{10,... | collective-permute-start | bytes 516104 | tf_op jit(solution)/shard_map/ppermute | solution.py:356
  49.1 6.3 %collective-permute-start.18 = (bf16[32,1344]{1,0:T(8,128)(2,1)S(1)}, bf16[32,1344]{1,0:T(8,128)(2,1)S(1)}, u32[]{:S(2)}, u32[]{:S(2)}) collective-permute-start(bf16[32,1344]{1,0:T(8,128)(2,1)S(1)} %get-tuple-element.83), channel_id=1, source_target_pairs={{0,2},{1,3},{2,0},{3,1},{4,6},{5,7},{6,4},{7,5},{8,10},{9,11},{10,... | collective-permute-start | bytes 258056 | tf_op jit(solution)/shard_map/ppermute | solution.py:356
  55.5 5.5 %collective-permute-start.19 = (bf16[32,1344]{1,0:T(8,128)(2,1)S(1)}, bf16[32,1344]{1,0:T(8,128)(2,1)S(1)}, u32[]{:S(2)}, u32[]{:S(2)}) collective-permute-start(bf16[32,1344]{1,0:T(8,128)(2,1)S(1)} %sum.1), channel_id=1, source_target_pairs={{0,8},{4,12},{8,0},{12,4},{1,9},{5,13},{9,1},{13,5},{2,10},{6,14},... | collective-permute-start | bytes 258056 | tf_op jit(solution)/shard_map/ppermute | solution.py:356
  56.4 4.6 %collective-permute-start.20 = (bf16[32,1344]{1,0:T(8,128)(2,1)S(1)}, bf16[32,1344]{1,0:T(8,128)(2,1)S(1)}, u32[]{:S(2)}, u32[]{:S(2)}) collective-permute-start(bf16[32,1344]{1,0:T(8,128)(2,1)S(1)} %get-tuple-element.86), channel_id=1, source_target_pairs={{0,2},{1,3},{2,0},{3,1},{4,6},{5,7},{6,4},{7,5},{8,10},{9,11},{10,... | collective-permute-start | bytes 258056 | tf_op jit(solution)/shard_map/ppermute | solution.py:356

commit v17 on v16

--- a/solution.py
+++ b/solution.py
@@ -137,12 +137,15 @@
     send_ref[...] = packed_ref[1 - core_index()]
 
 
-def chip_state_kernel(keep_ref, got_ref, out_ref):
+def chip_state_kernel(after_ref, keep_ref, got_ref, *outs):
     first = core_index() == 0
     keep, got = unpacked(keep_ref[...]), unpacked(got_ref[...])
     early = [jnp.where(first, mine, other) for mine, other in zip(keep, got)]
     late = [jnp.where(first, other, mine) for mine, other in zip(keep, got)]
-    pack(out_ref, early[0] + late[0], jnp.exp(late[0]) * early[1] + late[1])
+    total, state = early[0] + late[0], jnp.exp(late[0]) * early[1] + late[1]
+    size = total.shape[0] // len(outs)
+    for at, out in enumerate(outs):
+        pack(out, total[at * size : (at + 1) * size], state[at * size : (at + 1) * size])
 
 
 def weights_kernel(after_ref, up_hbm, down_hbm, up_ref, down_ref, sems):
@@ -161,23 +164,27 @@
     pack(out_ref, total, state)
 
 
-def before_kernel(chips, after_ref, keep_ref, got_ref, *rest):
+def before_kernel(chips, parts, after_ref, keep_ref, got_ref, *rest):
     ins, (mine_ref, send_ref, chip_ref, part_ref) = rest[:-4], rest[-4:]
-    for mask in range(chips):
-        chip_ref[chip_index() ^ mask] = ins[mask][...]
-    parts = len(ins) - chips
-    for mask in range(parts):
-        part_ref[lax.axis_index("seq") ^ mask] = ins[chips + mask][...]
-    carry = jnp.zeros(mine_ref.shape, F32)
-    for ref, count, own in ((part_ref, parts, lax.axis_index("seq")), (chip_ref, chips, chip_index())):
-        for index in range(count - 1):
-            total, state = unpacked(ref[index])
-            carry = jnp.where(index < own, jnp.exp(total) * carry + state, carry)
     first = core_index() == 0
-    total, state = (jnp.where(first, k, g) for k, g in zip(unpacked(keep_ref[...]), unpacked(got_ref[...])))
-    later = jnp.exp(total) * carry + state
-    mine_ref[...] = jnp.where(first, carry, later).astype(BF16)
-    send_ref[...] = jnp.where(first, later, carry).astype(BF16)
+    totals, states = (jnp.where(first, k, g) for k, g in zip(unpacked(keep_ref[...]), unpacked(got_ref[...])))
+    each = chips + parts
+    chunks = len(ins) // each
+    size = totals.shape[0] // chunks
+    for chunk in range(chunks):
+        span = slice(chunk * size, (chunk + 1) * size)
+        for mask in range(chips):
+            chip_ref[chip_index() ^ mask] = ins[chunk * each + mask][...]
+        for mask in range(parts):
+            part_ref[lax.axis_index("seq") ^ mask] = ins[chunk * each + chips + mask][...]
+        carry = jnp.zeros(states[span].shape, F32)
+        for ref, count, own in ((part_ref, parts, lax.axis_index("seq")), (chip_ref, chips, chip_index())):
+            for index in range(count - 1):
+                total, state = unpacked(ref[index])
+                carry = jnp.where(index < own, jnp.exp(total) * carry + state, carry)
+        later = jnp.exp(totals[span]) * carry + states[span]
+        mine_ref[span] = jnp.where(first, carry, later).astype(BF16)
+        send_ref[span] = jnp.where(first, later, carry).astype(BF16)
 
 
 def inside_kernel(x_hbm, z_hbm, b_hbm, c_hbm, dt_hbm, a_hbm, d_hbm, local_ref, grown_ref, c_ref, *scratch):
@@ -219,12 +226,17 @@
             grown_ref[:, at] = pair_lanes(grown, pair) * gate
 
 
-def prep_kernel(experts, width, resid_hbm, routes_hbm, gates_hbm, gain_hbm, norm_hbm, w_hbm, *rest):
-    gate_ref, resid_ref, gain_ref, norm_ref, w_ref, routes_ref, gates_ref, sems = rest
+def projection_kernel(norm_hbm, w_hbm, norm_ref, w_ref, sems):
+    for load in copies(sems, (norm_hbm, w_hbm), (norm_ref, w_ref)):
+        load.wait()
+
+
+def prep_kernel(experts, width, after_ref, resid_hbm, routes_hbm, gates_hbm, gain_hbm, *rest):
+    gate_ref, resid_ref, gain_ref, routes_ref, gates_ref, sems = rest
     loads = copies(
         sems,
-        (routes_hbm, gates_hbm, resid_hbm, gain_hbm, norm_hbm, w_hbm),
-        (routes_ref, gates_ref, resid_ref, gain_ref, norm_ref, w_ref),
+        (routes_hbm, gates_hbm, resid_hbm, gain_hbm),
+        (routes_ref, gates_ref, resid_ref, gain_ref.at[0]),
     )
     loads[0].wait()
     loads[1].wait()
@@ -403,34 +415,44 @@
     )
     wide = -(-(model + 2 * experts) // LANES) * LANES
     turned = [jnp.transpose(value, (2, 0, 1)) for value in (routes, gates)]
-    gate_lanes, resid_held, gain_held, norm_held, w_held = call(
+    norm_held, w_held = call(
+        projection_kernel,
+        "projection",
+        [struct((1, channels), F32), struct((model, channels), BF16)],
+        [(HBM, norm_w[None]), (HBM, w_out.T)],
+        [dma((2,))],
+    )
+    gate_lanes, resid_held, gain_held = call(
         functools.partial(prep_kernel, experts, model),
         "prep",
-        [struct((rows, wide - model // LANES * LANES), BF16), struct(resid.shape, BF16), struct((1, model), F32),
-         struct((1, channels), F32), struct((model, channels), BF16)],
-        [(HBM, value) for value in (resid, *turned, moe_gain[None], norm_w[None], w_out.T)],
-        [pltpu.VMEM(turned[0].shape, jnp.int32), pltpu.VMEM(turned[1].shape, F32), dma((6,))],
+        [struct((rows, wide - model // LANES * LANES), BF16), struct(resid.shape, BF16), struct((1, model), F32)],
+        [(ANY, keep)] + [(HBM, value) for value in (resid, *turned, moe_gain)],
+        [pltpu.VMEM(turned[0].shape, jnp.int32), pltpu.VMEM(turned[1].shape, F32), dma((4,))],
         megabytes=16,
     )
     up_turned = jnp.swapaxes(w_up, 1, 2)
     got = swap(send, "exp", 1)
-    chip = call(chip_state_kernel, "chip_state", packed, [(VMEM, keep), (VMEM, got)])
+    chunks = 2 if half % 2 == 0 else 1
+    packed = struct((half // chunks * STATE + TILE, LANES), BF16)
+    chip = call(chip_state_kernel, "chip_state", [packed] * chunks, [(ANY, gate_lanes), (VMEM, keep), (VMEM, got)])
     chip, up_after, down_after = lax.optimization_barrier((chip, up_turned, w_down))
     other_up, other_down = swap(up_after, "exp", 1), swap(down_after, "exp", 1)
-    along_y = [chip] + [swap(chip, "exp", 2 * d) for d in range(1, chips)]
-    span = call(
-        span_kernel,
-        "span",
-        packed,
-        [(ANY, c_held)] + [(VMEM, value) for value in along_y],
-        [pltpu.VMEM((chips, *packed.shape), BF16)],
-    )
-    along_x = [span] + [swap(span, "seq", d) for d in range(1, seq_size)]
+    exchanged = []
+    for own in chip:
+        along_y = [own] + [swap(own, "exp", 2 * d) for d in range(1, chips)]
+        span = call(
+            span_kernel,
+            "span",
+            packed,
+            [(ANY, c_held)] + [(VMEM, value) for value in along_y],
+            [pltpu.VMEM((chips, *packed.shape), BF16)],
+        )
+        exchanged += along_y + [span] + [swap(span, "seq", d) for d in range(1, seq_size)]
     before, before_send = call(
-        functools.partial(before_kernel, chips),
+        functools.partial(before_kernel, chips, seq_size),
         "before",
         [struct((half, STATE, LANES), BF16)] * 2,
-        [(ANY, gate_lanes)] + [(VMEM, value) for value in (keep, got, *along_y, *along_x)],
+        [(ANY, norm_held)] + [(VMEM, value) for value in (keep, got, *exchanged)],
         [pltpu.VMEM((chips, *packed.shape), BF16), pltpu.VMEM((seq_size, *packed.shape), BF16)],
         megabytes=24,
     )

time: 62.1 us -> 62.4 us (level)
  local copies, waits for them, and re-layouts: 1.29 us -> 0 us
  starting transfers between devices: 26.2 us -> 27.4 us
  Pallas kernels: 17.3 us -> 18.1 us
    ppermute x18 -> x20, starting transfers between devices: 22.3 us -> 23.5 us  [swap(): return lax.ppermute(value, axis, [(i, i ^ mask) for i in range(size)])]
    broadcast_in_dim x1 -> x0, local copies, waits for them, and re-layouts: 1.29 us -> none  [per_device(): moe_gain[None]]
    pallas_call x15 -> x17, Pallas kernels: 17.3 us -> 18.1 us  [call(): pl.pallas_call(kernel, out_shape=jax.tree.map(lambda out: pltpu.VMEM(out....]
    ppermute x18 -> x20, waiting for transfers between devices: 12.2 us -> 11.6 us  [swap(): return lax.ppermute(value, axis, [(i, i ^ mask) for i in range(size)])]
  transfers between devices with their start and end apart: 21 -> 23, of which waited for: 12 -> 8; matrix products, arithmetic and copies ran while one was open for 2% -> 0% of each run, Pallas kernels for 18% -> 19%
where the time goes in v17:
time: 62.4 us; the launch traced here: 62.1 us
  starting transfers between devices  27.4 us (44%)
  Pallas kernels  18.1 us (29%)
  waiting for transfers between devices  16.5 us (26%)
    ppermute x20, starting transfers between devices, swap(): return lax.ppermute(value, axis, [(i, i ^ mask) for i in range(size)])  23.5 us
    pallas_call x17, Pallas kernels, call(): pl.pallas_call(kernel, out_shape=jax.tree.map(lambda out: pltpu.VMEM(out....  18.1 us
    ppermute x20, waiting for transfers between devices, swap(): return lax.ppermute(value, axis, [(i, i ^ mask) for i in range(size)])  11.6 us
    ppermute x3, waiting for transfers between devices, swap_slot(): return lax.ppermute(value, ('head', 'exp'), pairs)  4.87 us
    ppermute x3, starting transfers between devices, swap_slot(): return lax.ppermute(value, ('head', 'exp'), pairs)  3.81 us
  transfers between devices with their start and end apart: 23, of which 8 were waited for; matrix products, arithmetic and copies ran while one was open for 0% of the time, Pallas kernels for 19%

profile of v17, /device:TPU:0, one launch (start us, length us, event | category | flops | bytes accessed | tf_op | source)
XLA Modules:
  0.0 62.1 jit_solution(9031598428186326794)
XLA Ops:
  0.0 1.8 %state.1 = (bf16[528,128]{1,0:T(8,128)(2,1)S(1)}, bf16[528,128]{1,0:T(8,128)(2,1)S(1)}) custom-call(bf16[128,1024]{1,0:T(8,128)(2,1)} %x_hbm.3, bf16[128,256]{1,0:T(8,128)(2,1)} %b_hbm.3, f32[16,128]{1,0:T(8,128)} %bitcast.11, f32[1,16]{1,0:T(1,128)} %bitcast.16), custom_call_target="tpu_custom_call" | custom-call | tf_op jit(solution)/shard_map/state/pallas_call | solution.py:29
  1.8 0.5 collective-permute-start
  2.4 1.0 %prep.1 = (bf16[32,128]{1,0:T(8,128)(2,1)S(1)}, bf16[1,32,1344]{2,1,0:T(8,128)(2,1)S(1)}, f32[1,1344]{1,0:T(1,128)S(1)}) custom-call(bf16[528,128]{1,0:T(8,128)(2,1)S(1)} %get-tuple-element.49.after_ref.keep_ref, bf16[1,32,1344]{2,1,0:T(8,128)(2,1)} %resid_hbm.1, s32[6,1,32]{2,1,0:T(1,128)} %bitcast.14, f32[6,1,32]{2,1,0:T(1,128)} %bitcast.15, f32[1344]{0:T(1024)} %gain_hbm.1), custom_call_target="tpu_custom_call" | custom-call | tf_op jit(solution)/shard_map/prep/pallas_call | solution.py:29
  3.3 0.0 collective-permute-done.got_ref
  3.3 0.1 chip_state.1
  3.4 0.4 collective-permute-start.1
  3.9 0.1 collective-permute-start.2
  4.0 2.9 %collective-permute-start.3 = (bf16[272,128]{1,0:T(8,128)(2,1)S(1)}, bf16[272,128]{1,0:T(8,128)(2,1)S(1)}, u32[]{:S(2)}, u32[]{:S(2)}) collective-permute-start(bf16[272,128]{1,0:T(8,128)(2,1)S(1)} %get-tuple-element.61.rest_0_), channel_id=1, source_target_pairs={{0,2},{1,3},{2,0},{3,1},{4,6},{5,7},{6,4},{7,5},{8,10},{9,11},{10,... | collective-permute-start | bytes 208904 | tf_op jit(solution)/shard_map/ppermute | solution.py:368
  6.9 0.0 collective-permute-start.5
  6.9 2.4 %inside.1 = (f32[128,1024]{1,0:T(8,128)S(1)}, f32[128,1024]{1,0:T(8,128)S(1)}, bf16[128,256]{1,0:T(8,128)(2,1)S(1)}) custom-call(bf16[128,1024]{1,0:T(8,128)(2,1)} %x_hbm.3, bf16[128,1024]{1,0:T(8,128)(2,1)} %z_hbm.1, bf16[128,256]{1,0:T(8,128)(2,1)} %b_hbm.3, bf16[128,256]{1,0:T(8,128)(2,1)} %c_hbm.1, f32[16,128]{1,0:T(8,128)} %bitcast.12, ...), custom_call_target="tpu_custom_call" | custom-call | tf_op jit(solution)/shard_map/inside/pallas_call | solution.py:29
  9.4 0.0 collective-permute-done.3.rest_1_
  9.4 0.1 span.2.rest_2_
  9.5 2.2 %collective-permute-start.4 = (bf16[272,128]{1,0:T(8,128)(2,1)S(1)}, bf16[272,128]{1,0:T(8,128)(2,1)S(1)}, u32[]{:S(2)}, u32[]{:S(2)}) collective-permute-start(bf16[272,128]{1,0:T(8,128)(2,1)S(1)} %span.2.rest_2_), channel_id=1, source_target_pairs={{0,16},{16,0},{1,17},{17,1},{2,18},{18,2},{3,19},{19,3},{4,20},{20... | collective-permute-start | bytes 208904 | tf_op jit(solution)/shard_map/ppermute | solution.py:368
  11.7 0.0 collective-permute-done.5.rest_1_.rest_5_
  11.7 0.1 span.3.rest_6_
  11.8 1.1 %collective-permute-start.6 = (bf16[272,128]{1,0:T(8,128)(2,1)S(1)}, bf16[272,128]{1,0:T(8,128)(2,1)S(1)}, u32[]{:S(2)}, u32[]{:S(2)}) collective-permute-start(bf16[272,128]{1,0:T(8,128)(2,1)S(1)} %span.3.rest_6_), channel_id=1, source_target_pairs={{0,16},{16,0},{1,17},{17,1},{2,18},{18,2},{3,19},{19,3},{4,20},{20... | collective-permute-start | bytes 208904 | tf_op jit(solution)/shard_map/ppermute | solution.py:368
  12.8 1.8 %projection.1 = (f32[1,1024]{1,0:T(1,128)S(1)}, bf16[1344,1024]{1,0:T(8,128)(2,1)S(1)}) custom-call(f32[1,1024]{1,0:T(1,128)} %bitcast.13, bf16[1344,1024]{1,0:T(8,128)(2,1)} %bitcast.8), custom_call_target="tpu_custom_call" | custom-call | tf_op jit(solution)/shard_map/projection/pallas_call | solution.py:29
  14.7 1.5 %collective-permute-done.6.rest_7_ = bf16[272,128]{1,0:T(8,128)(2,1)S(1)} collective-permute-done((bf16[272,128]{1,0:T(8,128)(2,1)S(1)}, bf16[272,128]{1,0:T(8,128)(2,1)S(1)}, u32[]{:S(2)}, u32[]{:S(2)}) %collective-permute-start.6) | collective-permute-done | bytes 69664 | tf_op jit(solution)/shard_map/ppermute | solution.py:368
  16.1 0.2 before.1
  16.3 0.1 collective-permute-start.7
  16.4 0.8 %first_half.1.first_ref = f32[128,1344]{1,0:T(8,128)S(1)} custom-call(f32[128,1024]{1,0:T(8,128)S(1)} %get-tuple-element.56.local_ref, f32[128,1024]{1,0:T(8,128)S(1)} %get-tuple-element.57.grown_ref, bf16[128,256]{1,0:T(8,128)(2,1)S(1)} %get-tuple-element.58.after_ref.c_ref, f32[1,1024]{1,0:T(1,128)S(1)} %get-tuple-element.59.after_ref.norm_ref, ...), custom_call_target="tpu_custom_call" | custom-call | tf_op jit(solution)/shard_map/first_half/pallas_call | solution.py:29
  17.3 0.5 collective-permute-done.7.got_ref
  17.8 0.9 %mixed.1 = (bf16[32,1344]{1,0:T(8,128)(2,1)S(1)}, bf16[32,1344]{1,0:T(8,128)(2,1)S(1)}, bf16[32,1344]{1,0:T(8,128)(2,1)S(1)}, bf16[32,1344]{1,0:T(8,128)(2,1)S(1)}) custom-call(bf16[1,928,1344]{2,1,0:T(8,128)(2,1)S(1)} %collective-permute-done.1.after_up.other_up_ref, bf16[1,928,1344]{2,1,0:T(8,128)(2,1)S(1)} %collective-permute-done.2.after_down.other_down_ref, ...), custom_call_target="tpu_custom_call" | custom-call | tf_op jit(solution)/shard_map/mixed/pallas_call | solution.py:29
  18.6 1.6 %collective-permute-start.8 = (bf16[32,1344]{1,0:T(8,128)(2,1)S(1)}, bf16[32,1344]{1,0:T(8,128)(2,1)S(1)}, u32[]{:S(2)}, u32[]{:S(2)}) collective-permute-start(bf16[32,1344]{1,0:T(8,128)(2,1)S(1)} %get-tuple-element.69), channel_id=1, source_target_pairs={{0,4},{1,9},{2,6},{3,11},{4,0},{5,13},{6,2},{7,15},{8,12},{9,1},{1... | collective-permute-start | bytes 258056 | tf_op jit(solution)/shard_map/ppermute | solution.py:378
  20.3 0.5 collective-permute-start.9
  20.7 3.5 %collective-permute-done.8.got_ref.rest_1_ = bf16[32,1344]{1,0:T(8,128)(2,1)S(1)} collective-permute-done((bf16[32,1344]{1,0:T(8,128)(2,1)S(1)}, bf16[32,1344]{1,0:T(8,128)(2,1)S(1)}, u32[]{:S(2)}, u32[]{:S(2)}) %collective-permute-start.8) | collective-permute-done | bytes 86048 | tf_op jit(solution)/shard_map/ppermute | solution.py:378
  24.2 1.7 %collective-permute-start.10 = (bf16[32,1344]{1,0:T(8,128)(2,1)S(1)}, bf16[32,1344]{1,0:T(8,128)(2,1)S(1)}, u32[]{:S(2)}, u32[]{:S(2)}) collective-permute-start(bf16[32,1344]{1,0:T(8,128)(2,1)S(1)} %relay.1), channel_id=1, source_target_pairs={{0,8},{1,5},{2,10},{3,7},{4,12},{5,1},{6,14},{7,3},{8,0},{9,13},{1... | collective-permute-start | bytes 258056 | tf_op jit(solution)/shard_map/ppermute | solution.py:378
  25.9 2.5 %weights.1 = (bf16[1,928,1344]{2,1,0:T(8,128)(2,1)S(1)}, bf16[1,928,1344]{2,1,0:T(8,128)(2,1)S(1)}) custom-call(bf16[32,1344]{1,0:T(8,128)(2,1)S(1)} %get-tuple-element.65.after_ref.rest_0_, bf16[1,928,1344]{2,1,0:T(8,128)(2,1)} %bitcast.10, bf16[1,928,1344]{2,1,0:T(8,128)(2,1)} %down_hbm.1), custom_call_target="tpu_custom_call" | custom-call | tf_op jit(solution)/shard_map/weights/pallas_call | solution.py:29
  28.5 1.4 %collective-permute-done.10.rest_3_ = bf16[32,1344]{1,0:T(8,128)(2,1)S(1)} collective-permute-done((bf16[32,1344]{1,0:T(8,128)(2,1)S(1)}, bf16[32,1344]{1,0:T(8,128)(2,1)S(1)}, u32[]{:S(2)}, u32[]{:S(2)}) %collective-permute-start.10) | collective-permute-done | bytes 86048 | tf_op jit(solution)/shard_map/ppermute | solution.py:378
  29.9 0.2 rows.1
  30.1 1.5 %collective-permute-start.14 = (bf16[32,1408]{1,0:T(8,128)(2,1)S(1)}, bf16[32,1408]{1,0:T(8,128)(2,1)S(1)}, u32[]{:S(2)}, u32[]{:S(2)}) collective-permute-start(bf16[32,1408]{1,0:T(8,128)(2,1)S(1)} %get-tuple-element.74.rest_0_), channel_id=1, source_target_pairs={{0,8},{4,12},{8,0},{12,4},{1,9},{5,13},{9,1},{13,5},{2,10},{6,14},... | collective-permute-start | bytes 270344 | tf_op jit(solution)/shard_map/ppermute | solution.py:368
  31.6 3.6 %collective-permute-start.13 = (bf16[32,1408]{1,0:T(8,128)(2,1)S(1)}, bf16[32,1408]{1,0:T(8,128)(2,1)S(1)}, u32[]{:S(2)}, u32[]{:S(2)}) collective-permute-start(bf16[32,1408]{1,0:T(8,128)(2,1)S(1)} %get-tuple-element.74.rest_0_), channel_id=1, source_target_pairs={{0,6},{1,7},{2,4},{3,5},{4,2},{5,3},{6,0},{7,1},{8,14},{9,15},{10,... | collective-permute-start | bytes 270344 | tf_op jit(solution)/shard_map/ppermute | solution.py:368
  35.3 0.6 collective-permute-start.11
  35.8 2.9 %collective-permute-start.17 = (bf16[32,1408]{1,0:T(8,128)(2,1)S(1)}, bf16[32,1408]{1,0:T(8,128)(2,1)S(1)}, u32[]{:S(2)}, u32[]{:S(2)}) collective-permute-start(bf16[32,1408]{1,0:T(8,128)(2,1)S(1)} %collective-permute-done.14.rest_0_), channel_id=1, source_target_pairs={{0,6},{1,7},{2,4},{3,5},{4,2},{5,3},{6,0},{7,1},{8,14},{9,15},{10,... | collective-permute-start | bytes 270344 | tf_op jit(solution)/shard_map/ppermute | solution.py:368
  38.8 1.1 %collective-permute-start.16 = (bf16[32,1408]{1,0:T(8,128)(2,1)S(1)}, bf16[32,1408]{1,0:T(8,128)(2,1)S(1)}, u32[]{:S(2)}, u32[]{:S(2)}) collective-permute-start(bf16[32,1408]{1,0:T(8,128)(2,1)S(1)} %collective-permute-done.14.rest_0_), channel_id=1, source_target_pairs={{0,4},{1,5},{2,6},{3,7},{4,0},{5,1},{6,2},{7,3},{8,12},{9,13},{10,... | collective-permute-start | bytes 270344 | tf_op jit(solution)/shard_map/ppermute | solution.py:368
  39.9 0.9 %collective-permute-done.12.rest_2_ = bf16[32,1408]{1,0:T(8,128)(2,1)S(1)} collective-permute-done((bf16[32,1408]{1,0:T(8,128)(2,1)S(1)}, bf16[32,1408]{1,0:T(8,128)(2,1)S(1)}, u32[]{:S(2)}, u32[]{:S(2)}) %collective-permute-start.12) | collective-permute-done | bytes 90144 | tf_op jit(solution)/shard_map/ppermute | solution.py:368
  40.8 0.9 %collective-permute-done.11.rest_1_ = bf16[32,1408]{1,0:T(8,128)(2,1)S(1)} collective-permute-done((bf16[32,1408]{1,0:T(8,128)(2,1)S(1)}, bf16[32,1408]{1,0:T(8,128)(2,1)S(1)}, u32[]{:S(2)}, u32[]{:S(2)}) %collective-permute-start.11) | collective-permute-done | bytes 90144 | tf_op jit(solution)/shard_map/ppermute | solution.py:368
  41.7 2.7 %experts.2 = (bf16[32,1344]{1,0:T(8,128)(2,1)S(1)}, bf16[32,1344]{1,0:T(8,128)(2,1)S(1)}, bf16[32,1344]{1,0:T(8,128)(2,1)S(1)}, bf16[32,1344]{1,0:T(8,128)(2,1)S(1)}) custom-call(bf16[1,928,1344]{2,1,0:T(8,128)(2,1)S(1)} %get-tuple-element.66.after_ref.up_ref, bf16[1,928,1344]{2,1,0:T(8,128)(2,1)S(1)} %get-tuple-element.73.down_ref, ...), custom_call_target="tpu_custom_call" | custom-call | tf_op jit(solution)/shard_map/experts/pallas_call | solution.py:29
  44.4 2.7 %experts.3 = (bf16[32,1344]{1,0:T(8,128)(2,1)S(1)}, bf16[32,1344]{1,0:T(8,128)(2,1)S(1)}, bf16[64,1344]{1,0:T(8,128)(2,1)S(1)}, bf16[64,1344]{1,0:T(8,128)(2,1)S(1)}) custom-call(bf16[1,928,1344]{2,1,0:T(8,128)(2,1)S(1)} %get-tuple-element.66.after_ref.up_ref, bf16[1,928,1344]{2,1,0:T(8,128)(2,1)S(1)} %get-tuple-element.73.down_ref, ...), custom_call_target="tpu_custom_call" | custom-call | tf_op jit(solution)/shard_map/experts/pallas_call | solution.py:29
  47.2 1.7 %collective-permute-start.18 = (bf16[64,1344]{1,0:T(8,128)(2,1)S(1)}, bf16[64,1344]{1,0:T(8,128)(2,1)S(1)}, u32[]{:S(2)}, u32[]{:S(2)}) collective-permute-start(bf16[64,1344]{1,0:T(8,128)(2,1)S(1)} %get-tuple-element.86), channel_id=1, source_target_pairs={{0,6},{1,7},{2,4},{3,5},{4,2},{5,3},{6,0},{7,1},{8,14},{9,15},{10,... | collective-permute-start | bytes 516104 | tf_op jit(solution)/shard_map/ppermute | solution.py:368
  48.9 0.2 collective-permute-start.19
  49.1 1.6 %collective-permute-start.20 = (bf16[32,1344]{1,0:T(8,128)(2,1)S(1)}, bf16[32,1344]{1,0:T(8,128)(2,1)S(1)}, u32[]{:S(2)}, u32[]{:S(2)}) collective-permute-start(bf16[32,1344]{1,0:T(8,128)(2,1)S(1)} %get-tuple-element.89), channel_id=1, source_target_pairs={{0,2},{1,3},{2,0},{3,1},{4,6},{5,7},{6,4},{7,5},{8,10},{9,11},{10,... | collective-permute-start | bytes 258056 | tf_op jit(solution)/shard_map/ppermute | solution.py:368
  50.7 5.1 %collective-permute-done.20.refs_3_ = bf16[32,1344]{1,0:T(8,128)(2,1)S(1)} collective-permute-done((bf16[32,1344]{1,0:T(8,128)(2,1)S(1)}, bf16[32,1344]{1,0:T(8,128)(2,1)S(1)}, u32[]{:S(2)}, u32[]{:S(2)}) %collective-permute-start.20) | collective-permute-done | bytes 86048 | tf_op jit(solution)/shard_map/ppermute | solution.py:368
  55.8 0.1 sum.1
  55.9 0.5 collective-permute-start.21
  56.4 2.3 %collective-permute-start.22 = (bf16[32,1344]{1,0:T(8,128)(2,1)S(1)}, bf16[32,1344]{1,0:T(8,128)(2,1)S(1)}, u32[]{:S(2)}, u32[]{:S(2)}) collective-permute-start(bf16[32,1344]{1,0:T(8,128)(2,1)S(1)} %get-tuple-element.92), channel_id=1, source_target_pairs={{0,2},{1,3},{2,0},{3,1},{4,6},{5,7},{6,4},{7,5},{8,10},{9,11},{10,... | collective-permute-start | bytes 258056 | tf_op jit(solution)/shard_map/ppermute | solution.py:368
  58.7 2.7 %collective-permute-done.21.rest_3_ = bf16[32,1344]{1,0:T(8,128)(2,1)S(1)} collective-permute-done((bf16[32,1344]{1,0:T(8,128)(2,1)S(1)}, bf16[32,1344]{1,0:T(8,128)(2,1)S(1)}, u32[]{:S(2)}, u32[]{:S(2)}) %collective-permute-start.21) | collective-permute-done | bytes 86048 | tf_op jit(solution)/shard_map/ppermute | solution.py:368
  61.4 0.7 %last.1 = bf16[1,32,1344]{2,1,0:T(8,128)(2,1)} custom-call(bf16[32,1344]{1,0:T(8,128)(2,1)S(1)} %get-tuple-element.72.hidden_ref, bf16[32,1344]{1,0:T(8,128)(2,1)S(1)} %get-tuple-element.79.rest_0_, bf16[64,1344]{1,0:T(8,128)(2,1)S(1)} %collective-permute-done.18.refs_1_.rest_1_, bf16[64,1344]{1,0:T(8,128)(2,1)S(1)} %collective-permute-done.19.refs_2_.rest_2_, ...), custom_call_target="tpu_custom_call" | custom-call | tf_op jit(solution)/shard_map/last/pallas_call | solution.py:29
  (15 shorter events, 0.1 us)
Async XLA Ops:
  1.8 1.5 %collective-permute-start = (bf16[528,128]{1,0:T(8,128)(2,1)S(1)}, bf16[528,128]{1,0:T(8,128)(2,1)S(1)}, u32[]{:S(2)}, u32[]{:S(2)}) collective-permute-start(bf16[528,128]{1,0:T(8,128)(2,1)S(1)} %get-tuple-element.51), channel_id=1, source_target_pairs={{0,1},{1,0},{2,3},{3,2},{4,5},{5,4},{6,7},{7,6},{8,9},{9,8},{10,11... | collective-permute-start | bytes 405512 | tf_op jit(solution)/shard_map/ppermute | solution.py:368
  3.4 14.3 %collective-permute-start.1 = (bf16[1,928,1344]{2,1,0:T(8,128)(2,1)}, bf16[1,928,1344]{2,1,0:T(8,128)(2,1)S(1)}, u32[]{:S(2)}, u32[]{:S(2)}) collective-permute-start(bf16[1,928,1344]{2,1,0:T(8,128)(2,1)} %bitcast.9), channel_id=1, source_target_pairs={{0,1},{1,0},{2,3},{3,2},{4,5},{5,4},{6,7},{7,6},{8,9},{9,8},{10,11... | collective-permute-start | bytes 7483400 | tf_op jit(solution)/shard_map/ppermute | solution.py:368
  3.9 13.9 %collective-permute-start.2 = (bf16[1,928,1344]{2,1,0:T(8,128)(2,1)}, bf16[1,928,1344]{2,1,0:T(8,128)(2,1)S(1)}, u32[]{:S(2)}, u32[]{:S(2)}) collective-permute-start(bf16[1,928,1344]{2,1,0:T(8,128)(2,1)} %down_hbm.1), channel_id=1, source_target_pairs={{0,1},{1,0},{2,3},{3,2},{4,5},{5,4},{6,7},{7,6},{8,9},{9,8},{10,11... | collective-permute-start | bytes 7483400 | tf_op jit(solution)/shard_map/ppermute | solution.py:368
  4.0 5.4 %collective-permute-start.3 = (bf16[272,128]{1,0:T(8,128)(2,1)S(1)}, bf16[272,128]{1,0:T(8,128)(2,1)S(1)}, u32[]{:S(2)}, u32[]{:S(2)}) collective-permute-start(bf16[272,128]{1,0:T(8,128)(2,1)S(1)} %get-tuple-element.61.rest_0_), channel_id=1, source_target_pairs={{0,2},{1,3},{2,0},{3,1},{4,6},{5,7},{6,4},{7,5},{8,10},{9,11},{10,... | collective-permute-start | bytes 208904 | tf_op jit(solution)/shard_map/ppermute | solution.py:368
  6.9 4.8 %collective-permute-start.5 = (bf16[272,128]{1,0:T(8,128)(2,1)S(1)}, bf16[272,128]{1,0:T(8,128)(2,1)S(1)}, u32[]{:S(2)}, u32[]{:S(2)}) collective-permute-start(bf16[272,128]{1,0:T(8,128)(2,1)S(1)} %get-tuple-element.62.rest_0_.rest_4_), channel_id=1, source_target_pairs={{0,2},{1,3},{2,0},{3,1},{4,6},{5,7},{6,4},{7,5},{8,10},{9,11},{10,... | collective-permute-start | bytes 208904 | tf_op jit(solution)/shard_map/ppermute | solution.py:368
  9.5 5.2 %collective-permute-start.4 = (bf16[272,128]{1,0:T(8,128)(2,1)S(1)}, bf16[272,128]{1,0:T(8,128)(2,1)S(1)}, u32[]{:S(2)}, u32[]{:S(2)}) collective-permute-start(bf16[272,128]{1,0:T(8,128)(2,1)S(1)} %span.2.rest_2_), channel_id=1, source_target_pairs={{0,16},{16,0},{1,17},{17,1},{2,18},{18,2},{3,19},{19,3},{4,20},{20... | collective-permute-start | bytes 208904 | tf_op jit(solution)/shard_map/ppermute | solution.py:368
  11.8 4.4 %collective-permute-start.6 = (bf16[272,128]{1,0:T(8,128)(2,1)S(1)}, bf16[272,128]{1,0:T(8,128)(2,1)S(1)}, u32[]{:S(2)}, u32[]{:S(2)}) collective-permute-start(bf16[272,128]{1,0:T(8,128)(2,1)S(1)} %span.3.rest_6_), channel_id=1, source_target_pairs={{0,16},{16,0},{1,17},{17,1},{2,18},{18,2},{3,19},{19,3},{4,20},{20... | collective-permute-start | bytes 208904 | tf_op jit(solution)/shard_map/ppermute | solution.py:368
  16.3 1.4 %collective-permute-start.7 = (bf16[4,128,128]{2,1,0:T(8,128)(2,1)S(1)}, bf16[4,128,128]{2,1,0:T(8,128)(2,1)S(1)}, u32[]{:S(2)}, u32[]{:S(2)}) collective-permute-start(bf16[4,128,128]{2,1,0:T(8,128)(2,1)S(1)} %get-tuple-element.63), channel_id=1, source_target_pairs={{0,1},{1,0},{2,3},{3,2},{4,5},{5,4},{6,7},{7,6},{8,9},{9,8},{10,11... | collective-permute-start | bytes 393224 | tf_op jit(solution)/shard_map/ppermute | solution.py:368
  18.6 5.6 %collective-permute-start.8 = (bf16[32,1344]{1,0:T(8,128)(2,1)S(1)}, bf16[32,1344]{1,0:T(8,128)(2,1)S(1)}, u32[]{:S(2)}, u32[]{:S(2)}) collective-permute-start(bf16[32,1344]{1,0:T(8,128)(2,1)S(1)} %get-tuple-element.69), channel_id=1, source_target_pairs={{0,4},{1,9},{2,6},{3,11},{4,0},{5,13},{6,2},{7,15},{8,12},{9,1},{1... | collective-permute-start | bytes 258056 | tf_op jit(solution)/shard_map/ppermute | solution.py:378
  20.3 8.2 %collective-permute-start.9 = (bf16[32,1344]{1,0:T(8,128)(2,1)S(1)}, bf16[32,1344]{1,0:T(8,128)(2,1)S(1)}, u32[]{:S(2)}, u32[]{:S(2)}) collective-permute-start(bf16[32,1344]{1,0:T(8,128)(2,1)S(1)} %get-tuple-element.70), channel_id=1, source_target_pairs={{0,4},{1,13},{2,6},{3,15},{4,0},{5,9},{6,2},{7,11},{8,12},{9,5},{1... | collective-permute-start | bytes 258056 | tf_op jit(solution)/shard_map/ppermute | solution.py:378
  24.2 5.7 %collective-permute-start.10 = (bf16[32,1344]{1,0:T(8,128)(2,1)S(1)}, bf16[32,1344]{1,0:T(8,128)(2,1)S(1)}, u32[]{:S(2)}, u32[]{:S(2)}) collective-permute-start(bf16[32,1344]{1,0:T(8,128)(2,1)S(1)} %relay.1), channel_id=1, source_target_pairs={{0,8},{1,5},{2,10},{3,7},{4,12},{5,1},{6,14},{7,3},{8,0},{9,13},{1... | collective-permute-start | bytes 258056 | tf_op jit(solution)/shard_map/ppermute | solution.py:378
  30.1 5.7 %collective-permute-start.14 = (bf16[32,1408]{1,0:T(8,128)(2,1)S(1)}, bf16[32,1408]{1,0:T(8,128)(2,1)S(1)}, u32[]{:S(2)}, u32[]{:S(2)}) collective-permute-start(bf16[32,1408]{1,0:T(8,128)(2,1)S(1)} %get-tuple-element.74.rest_0_), channel_id=1, source_target_pairs={{0,8},{4,12},{8,0},{12,4},{1,9},{5,13},{9,1},{13,5},{2,10},{6,14},... | collective-permute-start | bytes 270344 | tf_op jit(solution)/shard_map/ppermute | solution.py:368
  31.6 8.3 %collective-permute-start.13 = (bf16[32,1408]{1,0:T(8,128)(2,1)S(1)}, bf16[32,1408]{1,0:T(8,128)(2,1)S(1)}, u32[]{:S(2)}, u32[]{:S(2)}) collective-permute-start(bf16[32,1408]{1,0:T(8,128)(2,1)S(1)} %get-tuple-element.74.rest_0_), channel_id=1, source_target_pairs={{0,6},{1,7},{2,4},{3,5},{4,2},{5,3},{6,0},{7,1},{8,14},{9,15},{10,... | collective-permute-start | bytes 270344 | tf_op jit(solution)/shard_map/ppermute | solution.py:368
  35.3 5.6 %collective-permute-start.12 = (bf16[32,1408]{1,0:T(8,128)(2,1)S(1)}, bf16[32,1408]{1,0:T(8,128)(2,1)S(1)}, u32[]{:S(2)}, u32[]{:S(2)}) collective-permute-start(bf16[32,1408]{1,0:T(8,128)(2,1)S(1)} %get-tuple-element.74.rest_0_), channel_id=1, source_target_pairs={{0,4},{1,5},{2,6},{3,7},{4,0},{5,1},{6,2},{7,3},{8,12},{9,13},{10,... | collective-permute-start | bytes 270344 | tf_op jit(solution)/shard_map/ppermute | solution.py:368
  35.3 6.4 %collective-permute-start.11 = (bf16[32,1408]{1,0:T(8,128)(2,1)S(1)}, bf16[32,1408]{1,0:T(8,128)(2,1)S(1)}, u32[]{:S(2)}, u32[]{:S(2)}) collective-permute-start(bf16[32,1408]{1,0:T(8,128)(2,1)S(1)} %get-tuple-element.74.rest_0_), channel_id=1, source_target_pairs={{0,2},{1,3},{2,0},{3,1},{4,6},{5,7},{6,4},{7,5},{8,10},{9,11},{10,... | collective-permute-start | bytes 270344 | tf_op jit(solution)/shard_map/ppermute | solution.py:368
  35.8 8.6 %collective-permute-start.17 = (bf16[32,1408]{1,0:T(8,128)(2,1)S(1)}, bf16[32,1408]{1,0:T(8,128)(2,1)S(1)}, u32[]{:S(2)}, u32[]{:S(2)}) collective-permute-start(bf16[32,1408]{1,0:T(8,128)(2,1)S(1)} %collective-permute-done.14.rest_0_), channel_id=1, source_target_pairs={{0,6},{1,7},{2,4},{3,5},{4,2},{5,3},{6,0},{7,1},{8,14},{9,15},{10,... | collective-permute-start | bytes 270344 | tf_op jit(solution)/shard_map/ppermute | solution.py:368
  38.8 5.7 %collective-permute-start.16 = (bf16[32,1408]{1,0:T(8,128)(2,1)S(1)}, bf16[32,1408]{1,0:T(8,128)(2,1)S(1)}, u32[]{:S(2)}, u32[]{:S(2)}) collective-permute-start(bf16[32,1408]{1,0:T(8,128)(2,1)S(1)} %collective-permute-done.14.rest_0_), channel_id=1, source_target_pairs={{0,4},{1,5},{2,6},{3,7},{4,0},{5,1},{6,2},{7,3},{8,12},{9,13},{10,... | collective-permute-start | bytes 270344 | tf_op jit(solution)/shard_map/ppermute | solution.py:368
  39.9 4.5 %collective-permute-start.15 = (bf16[32,1408]{1,0:T(8,128)(2,1)S(1)}, bf16[32,1408]{1,0:T(8,128)(2,1)S(1)}, u32[]{:S(2)}, u32[]{:S(2)}) collective-permute-start(bf16[32,1408]{1,0:T(8,128)(2,1)S(1)} %collective-permute-done.14.rest_0_), channel_id=1, source_target_pairs={{0,2},{1,3},{2,0},{3,1},{4,6},{5,7},{6,4},{7,5},{8,10},{9,11},{10,... | collective-permute-start | bytes 270344 | tf_op jit(solution)/shard_map/ppermute | solution.py:368
  47.2 8.6 %collective-permute-start.18 = (bf16[64,1344]{1,0:T(8,128)(2,1)S(1)}, bf16[64,1344]{1,0:T(8,128)(2,1)S(1)}, u32[]{:S(2)}, u32[]{:S(2)}) collective-permute-start(bf16[64,1344]{1,0:T(8,128)(2,1)S(1)} %get-tuple-element.86), channel_id=1, source_target_pairs={{0,6},{1,7},{2,4},{3,5},{4,2},{5,3},{6,0},{7,1},{8,14},{9,15},{10,... | collective-permute-start | bytes 516104 | tf_op jit(solution)/shard_map/ppermute | solution.py:368
  48.9 6.9 %collective-permute-start.19 = (bf16[64,1344]{1,0:T(8,128)(2,1)S(1)}, bf16[64,1344]{1,0:T(8,128)(2,1)S(1)}, u32[]{:S(2)}, u32[]{:S(2)}) collective-permute-start(bf16[64,1344]{1,0:T(8,128)(2,1)S(1)} %get-tuple-element.87), channel_id=1, source_target_pairs={{0,4},{1,5},{2,6},{3,7},{4,0},{5,1},{6,2},{7,3},{8,12},{9,13},{10,... | collective-permute-start | bytes 516104 | tf_op jit(solution)/shard_map/ppermute | solution.py:368
  49.1 6.7 %collective-permute-start.20 = (bf16[32,1344]{1,0:T(8,128)(2,1)S(1)}, bf16[32,1344]{1,0:T(8,128)(2,1)S(1)}, u32[]{:S(2)}, u32[]{:S(2)}) collective-permute-start(bf16[32,1344]{1,0:T(8,128)(2,1)S(1)} %get-tuple-element.89), channel_id=1, source_target_pairs={{0,2},{1,3},{2,0},{3,1},{4,6},{5,7},{6,4},{7,5},{8,10},{9,11},{10,... | collective-permute-start | bytes 258056 | tf_op jit(solution)/shard_map/ppermute | solution.py:368
  55.9 5.5 %collective-permute-start.21 = (bf16[32,1344]{1,0:T(8,128)(2,1)S(1)}, bf16[32,1344]{1,0:T(8,128)(2,1)S(1)}, u32[]{:S(2)}, u32[]{:S(2)}) collective-permute-start(bf16[32,1344]{1,0:T(8,128)(2,1)S(1)} %sum.1), channel_id=1, source_target_pairs={{0,8},{4,12},{8,0},{12,4},{1,9},{5,13},{9,1},{13,5},{2,10},{6,14},... | collective-permute-start | bytes 258056 | tf_op jit(solution)/shard_map/ppermute | solution.py:368
  56.4 5.0 %collective-permute-start.22 = (bf16[32,1344]{1,0:T(8,128)(2,1)S(1)}, bf16[32,1344]{1,0:T(8,128)(2,1)S(1)}, u32[]{:S(2)}, u32[]{:S(2)}) collective-permute-start(bf16[32,1344]{1,0:T(8,128)(2,1)S(1)} %get-tuple-element.92), channel_id=1, source_target_pairs={{0,2},{1,3},{2,0},{3,1},{4,6},{5,7},{6,4},{7,5},{8,10},{9,11},{10,... | collective-permute-start | bytes 258056 | tf_op jit(solution)/shard_map/ppermute | solution.py:368

commit v18 on v17

--- a/solution.py
+++ b/solution.py
@@ -322,8 +322,8 @@
     rows_ref[:, :width] = (value * scale * gain_ref[...]).astype(BF16)
 
 
-def expert_kernel(experts, count, carried, up_ref, down_ref, other_up_ref, other_down_ref, *rest):
-    ins, done, outs = rest[:count], rest[count : count + len(carried)], rest[count + len(carried) :]
+def expert_kernel(experts, count, up_ref, down_ref, other_up_ref, other_down_ref, *rest):
+    ins, outs = rest[:count], rest[count:]
     width = up_ref.shape[2]
     start = width // LANES * LANES
     rows = jnp.concatenate([ref[:, :width] for ref in ins], axis=0)
@@ -341,25 +341,21 @@
         total = total + jnp.dot(activated, down_of[0], preferred_element_type=F32) * gate
     size = ins[0].shape[0]
     for at, out in enumerate(outs):
-        out[0:size] = total[at * size : (at + 1) * size].astype(BF16)
-    for at, ref in zip(carried, done):
-        outs[at][size:] = ref[...]
+        out[...] = total[at * size : (at + 1) * size].astype(BF16)
 
 
 def sum_kernel(*refs):
-    rows = refs[-1].shape[0]
     total = refs[0][...].astype(F32)
     for ref in refs[1:-1]:
-        total = total + ref[0:rows].astype(F32)
+        total = total + ref[...].astype(F32)
     refs[-1][...] = total.astype(BF16)
 
 
 def last_kernel(hidden_ref, *rest):
     parts, out_ref = rest[:-1], rest[-1]
-    rows = out_ref.shape[1]
     total = parts[0][...].astype(F32)
     for part in parts[1:]:
-        total = total + part[part.shape[0] - rows :].astype(F32)
+        total = total + part[...].astype(F32)
     out_ref[0] = (hidden_ref[...].astype(F32) + total).astype(BF16)
 
 
@@ -492,14 +488,12 @@
         [(ANY, up_held)] + [(VMEM, value) for value in (resid_held, gate_lanes, gain_held, *parts)],
     )
 
-    def through_experts(members, carried=()):
-        places = [at for at, _ in carried]
+    def through_experts(members):
         return call(
-            functools.partial(expert_kernel, experts, len(members), places),
+            functools.partial(expert_kernel, experts, len(members)),
             "experts",
-            [struct((rows * (2 if at in places else 1), model), BF16) for at in range(len(members))],
-            [(VMEM, value) for value in (up_held, down_held, other_up, other_down, *members)]
-            + [(VMEM, value) for _, value in carried],
+            [struct((rows, model), BF16)] * len(members),
+            [(VMEM, value) for value in (up_held, down_held, other_up, other_down, *members)],
             megabytes=16,
         )
 
@@ -512,18 +506,13 @@
     sets = [spread(swap(own_rows, "head", high)) for high in range(2, head_size, 2)]
     near = through_experts(spread(own_rows))
     near, sets = lax.optimization_barrier((near, sets))
-    joined = [at for at, mask in enumerate(group, 1) if mask >= exp_size]
-    arrived, later = [], [at for at in range(1, len(near)) if at not in joined]
-    apart = [near[at] for at in later]
+    arrived = []
     for high, members in zip(range(2, head_size, 2), sets):
-        pieces = through_experts(members, [(at, near[at]) for at in joined] if high == 2 else ())
+        pieces = through_experts(members)
         got = [swap(piece, both, mask) for piece, mask in zip(pieces[:0:-1], group[::-1])]
         total = call(sum_kernel, "sum", struct((rows, model), BF16), [(VMEM, v) for v in (pieces[0], *got)])
-        if high == 2:
-            total, apart = lax.optimization_barrier((total, apart))
-            arrived += [part for part, mask in zip(got, group[::-1]) if mask >= exp_size]
         arrived.append(swap(total, "head", high))
-    arrived += [swap(piece, both, group[at - 1]) for piece, at in zip(apart, later)]
+    arrived += [swap(piece, both, mask) for piece, mask in zip(near[:0:-1], group[::-1])]
     return call(
         last_kernel,
         "last",

time: 62.4 us -> 62.2 us (level)
  waiting for transfers between devices: 16.5 us -> 15.6 us
  starting transfers between devices: 27.4 us -> 28.1 us
    ppermute x20 -> x22, waiting for transfers between devices: 11.6 us -> 10.7 us  [swap(): return lax.ppermute(value, axis, [(i, i ^ mask) for i in range(size)])]
    ppermute x20 -> x22, starting transfers between devices: 23.5 us -> 24.3 us  [swap(): return lax.ppermute(value, axis, [(i, i ^ mask) for i in range(size)])]
  transfers between devices with their start and end apart: 23 -> 25, of which waited for: 8 -> 12; matrix products, arithmetic and copies ran while one was open for 0% -> 0% of each run, Pallas kernels for 19% -> 19%
where the time goes in v18:
time: 62.2 us; the launch traced here: 61.9 us
  starting transfers between devices  28.1 us (45%)
  Pallas kernels  18.1 us (29%)
  waiting for transfers between devices  15.6 us (25%)
    ppermute x22, starting transfers between devices, swap(): return lax.ppermute(value, axis, [(i, i ^ mask) for i in range(size)])  24.3 us
    pallas_call x17, Pallas kernels, call(): pl.pallas_call(kernel, out_shape=jax.tree.map(lambda out: pltpu.VMEM(out....  18.1 us
    ppermute x22, waiting for transfers between devices, swap(): return lax.ppermute(value, axis, [(i, i ^ mask) for i in range(size)])  10.7 us
    ppermute x3, waiting for transfers between devices, swap_slot(): return lax.ppermute(value, ('head', 'exp'), pairs)  4.87 us
    ppermute x3, starting transfers between devices, swap_slot(): return lax.ppermute(value, ('head', 'exp'), pairs)  3.81 us
  transfers between devices with their start and end apart: 25, of which 12 were waited for; matrix products, arithmetic and copies ran while one was open for 0% of the time, Pallas kernels for 19%

profile of v18, /device:TPU:0, one launch (start us, length us, event | category | flops | bytes accessed | tf_op | source)
XLA Modules:
  0.0 61.9 jit_solution(12385813245239630251)
XLA Ops:
  0.0 1.8 %state.1 = (bf16[528,128]{1,0:T(8,128)(2,1)S(1)}, bf16[528,128]{1,0:T(8,128)(2,1)S(1)}) custom-call(bf16[128,1024]{1,0:T(8,128)(2,1)} %x_hbm.3, bf16[128,256]{1,0:T(8,128)(2,1)} %b_hbm.3, f32[16,128]{1,0:T(8,128)} %bitcast.11, f32[1,16]{1,0:T(1,128)} %bitcast.16), custom_call_target="tpu_custom_call" | custom-call | tf_op jit(solution)/shard_map/state/pallas_call | solution.py:29
  1.8 0.5 collective-permute-start
  2.4 1.0 %prep.1 = (bf16[32,128]{1,0:T(8,128)(2,1)S(1)}, bf16[1,32,1344]{2,1,0:T(8,128)(2,1)S(1)}, f32[1,1344]{1,0:T(1,128)S(1)}) custom-call(bf16[528,128]{1,0:T(8,128)(2,1)S(1)} %get-tuple-element.47.after_ref.keep_ref, bf16[1,32,1344]{2,1,0:T(8,128)(2,1)} %resid_hbm.1, s32[6,1,32]{2,1,0:T(1,128)} %bitcast.14, f32[6,1,32]{2,1,0:T(1,128)} %bitcast.15, f32[1344]{0:T(1024)} %gain_hbm.1), custom_call_target="tpu_custom_call" | custom-call | tf_op jit(solution)/shard_map/prep/pallas_call | solution.py:29
  3.3 0.1 chip_state.1
  3.4 0.4 collective-permute-start.1
  3.9 0.1 collective-permute-start.2
  4.0 2.9 %collective-permute-start.3 = (bf16[272,128]{1,0:T(8,128)(2,1)S(1)}, bf16[272,128]{1,0:T(8,128)(2,1)S(1)}, u32[]{:S(2)}, u32[]{:S(2)}) collective-permute-start(bf16[272,128]{1,0:T(8,128)(2,1)S(1)} %get-tuple-element.59.rest_0_), channel_id=1, source_target_pairs={{0,2},{1,3},{2,0},{3,1},{4,6},{5,7},{6,4},{7,5},{8,10},{9,11},{10,... | collective-permute-start | bytes 208904 | tf_op jit(solution)/shard_map/ppermute | solution.py:364
  6.9 2.4 %inside.1 = (f32[128,1024]{1,0:T(8,128)S(1)}, f32[128,1024]{1,0:T(8,128)S(1)}, bf16[128,256]{1,0:T(8,128)(2,1)S(1)}) custom-call(bf16[128,1024]{1,0:T(8,128)(2,1)} %x_hbm.3, bf16[128,1024]{1,0:T(8,128)(2,1)} %z_hbm.1, bf16[128,256]{1,0:T(8,128)(2,1)} %b_hbm.3, bf16[128,256]{1,0:T(8,128)(2,1)} %c_hbm.1, f32[16,128]{1,0:T(8,128)} %bitcast.12, ...), custom_call_target="tpu_custom_call" | custom-call | tf_op jit(solution)/shard_map/inside/pallas_call | solution.py:29
  9.5 2.2 %collective-permute-start.4 = (bf16[272,128]{1,0:T(8,128)(2,1)S(1)}, bf16[272,128]{1,0:T(8,128)(2,1)S(1)}, u32[]{:S(2)}, u32[]{:S(2)}) collective-permute-start(bf16[272,128]{1,0:T(8,128)(2,1)S(1)} %span.2.rest_2_), channel_id=1, source_target_pairs={{0,16},{16,0},{1,17},{17,1},{2,18},{18,2},{3,19},{19,3},{4,20},{20... | collective-permute-start | bytes 208904 | tf_op jit(solution)/shard_map/ppermute | solution.py:364
  11.7 0.1 span.3.rest_6_
  11.8 1.1 %collective-permute-start.6 = (bf16[272,128]{1,0:T(8,128)(2,1)S(1)}, bf16[272,128]{1,0:T(8,128)(2,1)S(1)}, u32[]{:S(2)}, u32[]{:S(2)}) collective-permute-start(bf16[272,128]{1,0:T(8,128)(2,1)S(1)} %span.3.rest_6_), channel_id=1, source_target_pairs={{0,16},{16,0},{1,17},{17,1},{2,18},{18,2},{3,19},{19,3},{4,20},{20... | collective-permute-start | bytes 208904 | tf_op jit(solution)/shard_map/ppermute | solution.py:364
  12.8 1.8 %projection.1 = (f32[1,1024]{1,0:T(1,128)S(1)}, bf16[1344,1024]{1,0:T(8,128)(2,1)S(1)}) custom-call(f32[1,1024]{1,0:T(1,128)} %bitcast.13, bf16[1344,1024]{1,0:T(8,128)(2,1)} %bitcast.8), custom_call_target="tpu_custom_call" | custom-call | tf_op jit(solution)/shard_map/projection/pallas_call | solution.py:29
  14.7 1.5 %collective-permute-done.6.rest_7_ = bf16[272,128]{1,0:T(8,128)(2,1)S(1)} collective-permute-done((bf16[272,128]{1,0:T(8,128)(2,1)S(1)}, bf16[272,128]{1,0:T(8,128)(2,1)S(1)}, u32[]{:S(2)}, u32[]{:S(2)}) %collective-permute-start.6) | collective-permute-done | bytes 69664 | tf_op jit(solution)/shard_map/ppermute | solution.py:364
  16.1 0.2 before.1
  16.3 0.1 collective-permute-start.7
  16.4 0.8 %first_half.1.first_ref = f32[128,1344]{1,0:T(8,128)S(1)} custom-call(f32[128,1024]{1,0:T(8,128)S(1)} %get-tuple-element.54.local_ref, f32[128,1024]{1,0:T(8,128)S(1)} %get-tuple-element.55.grown_ref, bf16[128,256]{1,0:T(8,128)(2,1)S(1)} %get-tuple-element.56.after_ref.c_ref, f32[1,1024]{1,0:T(1,128)S(1)} %get-tuple-element.57.after_ref.norm_ref, ...), custom_call_target="tpu_custom_call" | custom-call | tf_op jit(solution)/shard_map/first_half/pallas_call | solution.py:29
  17.3 0.5 collective-permute-done.7.got_ref
  17.8 0.9 %mixed.1 = (bf16[32,1344]{1,0:T(8,128)(2,1)S(1)}, bf16[32,1344]{1,0:T(8,128)(2,1)S(1)}, bf16[32,1344]{1,0:T(8,128)(2,1)S(1)}, bf16[32,1344]{1,0:T(8,128)(2,1)S(1)}) custom-call(bf16[1,928,1344]{2,1,0:T(8,128)(2,1)S(1)} %collective-permute-done.1.after_up.other_up_ref, bf16[1,928,1344]{2,1,0:T(8,128)(2,1)S(1)} %collective-permute-done.2.after_down.other_down_ref, ...), custom_call_target="tpu_custom_call" | custom-call | tf_op jit(solution)/shard_map/mixed/pallas_call | solution.py:29
  18.6 1.6 %collective-permute-start.8 = (bf16[32,1344]{1,0:T(8,128)(2,1)S(1)}, bf16[32,1344]{1,0:T(8,128)(2,1)S(1)}, u32[]{:S(2)}, u32[]{:S(2)}) collective-permute-start(bf16[32,1344]{1,0:T(8,128)(2,1)S(1)} %get-tuple-element.67), channel_id=1, source_target_pairs={{0,4},{1,9},{2,6},{3,11},{4,0},{5,13},{6,2},{7,15},{8,12},{9,1},{1... | collective-permute-start | bytes 258056 | tf_op jit(solution)/shard_map/ppermute | solution.py:374
  20.3 0.5 collective-permute-start.9
  20.7 3.5 %collective-permute-done.8.got_ref.rest_1_ = bf16[32,1344]{1,0:T(8,128)(2,1)S(1)} collective-permute-done((bf16[32,1344]{1,0:T(8,128)(2,1)S(1)}, bf16[32,1344]{1,0:T(8,128)(2,1)S(1)}, u32[]{:S(2)}, u32[]{:S(2)}) %collective-permute-start.8) | collective-permute-done | bytes 86048 | tf_op jit(solution)/shard_map/ppermute | solution.py:374
  24.2 1.7 %collective-permute-start.10 = (bf16[32,1344]{1,0:T(8,128)(2,1)S(1)}, bf16[32,1344]{1,0:T(8,128)(2,1)S(1)}, u32[]{:S(2)}, u32[]{:S(2)}) collective-permute-start(bf16[32,1344]{1,0:T(8,128)(2,1)S(1)} %relay.1), channel_id=1, source_target_pairs={{0,8},{1,5},{2,10},{3,7},{4,12},{5,1},{6,14},{7,3},{8,0},{9,13},{1... | collective-permute-start | bytes 258056 | tf_op jit(solution)/shard_map/ppermute | solution.py:374
  25.9 2.5 %weights.1 = (bf16[1,928,1344]{2,1,0:T(8,128)(2,1)S(1)}, bf16[1,928,1344]{2,1,0:T(8,128)(2,1)S(1)}) custom-call(bf16[32,1344]{1,0:T(8,128)(2,1)S(1)} %get-tuple-element.63.after_ref.rest_0_, bf16[1,928,1344]{2,1,0:T(8,128)(2,1)} %bitcast.10, bf16[1,928,1344]{2,1,0:T(8,128)(2,1)} %down_hbm.1), custom_call_target="tpu_custom_call" | custom-call | tf_op jit(solution)/shard_map/weights/pallas_call | solution.py:29
  28.5 1.4 %collective-permute-done.10.rest_3_ = bf16[32,1344]{1,0:T(8,128)(2,1)S(1)} collective-permute-done((bf16[32,1344]{1,0:T(8,128)(2,1)S(1)}, bf16[32,1344]{1,0:T(8,128)(2,1)S(1)}, u32[]{:S(2)}, u32[]{:S(2)}) %collective-permute-start.10) | collective-permute-done | bytes 86048 | tf_op jit(solution)/shard_map/ppermute | solution.py:374
  29.9 0.2 rows.1
  30.1 1.5 %collective-permute-start.14 = (bf16[32,1408]{1,0:T(8,128)(2,1)S(1)}, bf16[32,1408]{1,0:T(8,128)(2,1)S(1)}, u32[]{:S(2)}, u32[]{:S(2)}) collective-permute-start(bf16[32,1408]{1,0:T(8,128)(2,1)S(1)} %get-tuple-element.72.rest_0_), channel_id=1, source_target_pairs={{0,8},{4,12},{8,0},{12,4},{1,9},{5,13},{9,1},{13,5},{2,10},{6,14},... | collective-permute-start | bytes 270344 | tf_op jit(solution)/shard_map/ppermute | solution.py:364
  31.6 3.6 %collective-permute-start.13 = (bf16[32,1408]{1,0:T(8,128)(2,1)S(1)}, bf16[32,1408]{1,0:T(8,128)(2,1)S(1)}, u32[]{:S(2)}, u32[]{:S(2)}) collective-permute-start(bf16[32,1408]{1,0:T(8,128)(2,1)S(1)} %get-tuple-element.72.rest_0_), channel_id=1, source_target_pairs={{0,6},{1,7},{2,4},{3,5},{4,2},{5,3},{6,0},{7,1},{8,14},{9,15},{10,... | collective-permute-start | bytes 270344 | tf_op jit(solution)/shard_map/ppermute | solution.py:364
  35.3 0.6 collective-permute-start.11
  35.8 2.9 %collective-permute-start.17 = (bf16[32,1408]{1,0:T(8,128)(2,1)S(1)}, bf16[32,1408]{1,0:T(8,128)(2,1)S(1)}, u32[]{:S(2)}, u32[]{:S(2)}) collective-permute-start(bf16[32,1408]{1,0:T(8,128)(2,1)S(1)} %collective-permute-done.14.rest_0_), channel_id=1, source_target_pairs={{0,6},{1,7},{2,4},{3,5},{4,2},{5,3},{6,0},{7,1},{8,14},{9,15},{10,... | collective-permute-start | bytes 270344 | tf_op jit(solution)/shard_map/ppermute | solution.py:364
  38.8 1.1 %collective-permute-start.16 = (bf16[32,1408]{1,0:T(8,128)(2,1)S(1)}, bf16[32,1408]{1,0:T(8,128)(2,1)S(1)}, u32[]{:S(2)}, u32[]{:S(2)}) collective-permute-start(bf16[32,1408]{1,0:T(8,128)(2,1)S(1)} %collective-permute-done.14.rest_0_), channel_id=1, source_target_pairs={{0,4},{1,5},{2,6},{3,7},{4,0},{5,1},{6,2},{7,3},{8,12},{9,13},{10,... | collective-permute-start | bytes 270344 | tf_op jit(solution)/shard_map/ppermute | solution.py:364
  39.9 0.9 %collective-permute-done.12.rest_2_ = bf16[32,1408]{1,0:T(8,128)(2,1)S(1)} collective-permute-done((bf16[32,1408]{1,0:T(8,128)(2,1)S(1)}, bf16[32,1408]{1,0:T(8,128)(2,1)S(1)}, u32[]{:S(2)}, u32[]{:S(2)}) %collective-permute-start.12) | collective-permute-done | bytes 90144 | tf_op jit(solution)/shard_map/ppermute | solution.py:364
  40.8 0.9 %collective-permute-done.11.rest_1_ = bf16[32,1408]{1,0:T(8,128)(2,1)S(1)} collective-permute-done((bf16[32,1408]{1,0:T(8,128)(2,1)S(1)}, bf16[32,1408]{1,0:T(8,128)(2,1)S(1)}, u32[]{:S(2)}, u32[]{:S(2)}) %collective-permute-start.11) | collective-permute-done | bytes 90144 | tf_op jit(solution)/shard_map/ppermute | solution.py:364
  41.7 2.7 %experts.2 = (bf16[32,1344]{1,0:T(8,128)(2,1)S(1)}, bf16[32,1344]{1,0:T(8,128)(2,1)S(1)}, bf16[32,1344]{1,0:T(8,128)(2,1)S(1)}, bf16[32,1344]{1,0:T(8,128)(2,1)S(1)}) custom-call(bf16[1,928,1344]{2,1,0:T(8,128)(2,1)S(1)} %get-tuple-element.64.after_ref.up_ref, bf16[1,928,1344]{2,1,0:T(8,128)(2,1)S(1)} %get-tuple-element.71.down_ref, ...), custom_call_target="tpu_custom_call" | custom-call | tf_op jit(solution)/shard_map/experts/pallas_call | solution.py:29
  44.4 2.7 %experts.3 = (bf16[32,1344]{1,0:T(8,128)(2,1)S(1)}, bf16[32,1344]{1,0:T(8,128)(2,1)S(1)}, bf16[32,1344]{1,0:T(8,128)(2,1)S(1)}, bf16[32,1344]{1,0:T(8,128)(2,1)S(1)}) custom-call(bf16[1,928,1344]{2,1,0:T(8,128)(2,1)S(1)} %get-tuple-element.64.after_ref.up_ref, bf16[1,928,1344]{2,1,0:T(8,128)(2,1)S(1)} %get-tuple-element.71.down_ref, ...), custom_call_target="tpu_custom_call" | custom-call | tf_op jit(solution)/shard_map/experts/pallas_call | solution.py:29
  47.2 1.7 %collective-permute-start.18 = (bf16[32,1344]{1,0:T(8,128)(2,1)S(1)}, bf16[32,1344]{1,0:T(8,128)(2,1)S(1)}, u32[]{:S(2)}, u32[]{:S(2)}) collective-permute-start(bf16[32,1344]{1,0:T(8,128)(2,1)S(1)} %get-tuple-element.83), channel_id=1, source_target_pairs={{0,6},{1,7},{2,4},{3,5},{4,2},{5,3},{6,0},{7,1},{8,14},{9,15},{10,... | collective-permute-start | bytes 258056 | tf_op jit(solution)/shard_map/ppermute | solution.py:364
  48.9 0.2 collective-permute-start.19
  49.1 1.6 %collective-permute-start.20 = (bf16[32,1344]{1,0:T(8,128)(2,1)S(1)}, bf16[32,1344]{1,0:T(8,128)(2,1)S(1)}, u32[]{:S(2)}, u32[]{:S(2)}) collective-permute-start(bf16[32,1344]{1,0:T(8,128)(2,1)S(1)} %get-tuple-element.85), channel_id=1, source_target_pairs={{0,2},{1,3},{2,0},{3,1},{4,6},{5,7},{6,4},{7,5},{8,10},{9,11},{10,... | collective-permute-start | bytes 258056 | tf_op jit(solution)/shard_map/ppermute | solution.py:364
  50.7 1.7 %collective-permute-start.22 = (bf16[32,1344]{1,0:T(8,128)(2,1)S(1)}, bf16[32,1344]{1,0:T(8,128)(2,1)S(1)}, u32[]{:S(2)}, u32[]{:S(2)}) collective-permute-start(bf16[32,1344]{1,0:T(8,128)(2,1)S(1)} %get-tuple-element.86), channel_id=1, source_target_pairs={{0,6},{1,7},{2,4},{3,5},{4,2},{5,3},{6,0},{7,1},{8,14},{9,15},{10,... | collective-permute-start | bytes 258056 | tf_op jit(solution)/shard_map/ppermute | solution.py:364
  52.4 0.2 collective-permute-start.23
  52.6 1.0 %collective-permute-done.18.refs_1_ = bf16[32,1344]{1,0:T(8,128)(2,1)S(1)} collective-permute-done((bf16[32,1344]{1,0:T(8,128)(2,1)S(1)}, bf16[32,1344]{1,0:T(8,128)(2,1)S(1)}, u32[]{:S(2)}, u32[]{:S(2)}) %collective-permute-start.18) | collective-permute-done | bytes 86048 | tf_op jit(solution)/shard_map/ppermute | solution.py:364
  53.6 0.6 collective-permute-start.24
  54.2 0.5 collective-permute-done.20.refs_3_
  54.7 1.1 %collective-permute-start.21 = (bf16[32,1344]{1,0:T(8,128)(2,1)S(1)}, bf16[32,1344]{1,0:T(8,128)(2,1)S(1)}, u32[]{:S(2)}, u32[]{:S(2)}) collective-permute-start(bf16[32,1344]{1,0:T(8,128)(2,1)S(1)} %sum.1), channel_id=1, source_target_pairs={{0,8},{4,12},{8,0},{12,4},{1,9},{5,13},{9,1},{13,5},{2,10},{6,14},... | collective-permute-start | bytes 258056 | tf_op jit(solution)/shard_map/ppermute | solution.py:364
  55.8 0.8 %collective-permute-done.22.rest_2_ = bf16[32,1344]{1,0:T(8,128)(2,1)S(1)} collective-permute-done((bf16[32,1344]{1,0:T(8,128)(2,1)S(1)}, bf16[32,1344]{1,0:T(8,128)(2,1)S(1)}, u32[]{:S(2)}, u32[]{:S(2)}) %collective-permute-start.22) | collective-permute-done | bytes 86048 | tf_op jit(solution)/shard_map/ppermute | solution.py:364
  56.6 0.3 collective-permute-done.23.rest_3_
  56.9 1.2 %collective-permute-done.24.rest_4_ = bf16[32,1344]{1,0:T(8,128)(2,1)S(1)} collective-permute-done((bf16[32,1344]{1,0:T(8,128)(2,1)S(1)}, bf16[32,1344]{1,0:T(8,128)(2,1)S(1)}, u32[]{:S(2)}, u32[]{:S(2)}) %collective-permute-start.24) | collective-permute-done | bytes 86048 | tf_op jit(solution)/shard_map/ppermute | solution.py:364
  58.1 3.1 %collective-permute-done.21.rest_1_ = bf16[32,1344]{1,0:T(8,128)(2,1)S(1)} collective-permute-done((bf16[32,1344]{1,0:T(8,128)(2,1)S(1)}, bf16[32,1344]{1,0:T(8,128)(2,1)S(1)}, u32[]{:S(2)}, u32[]{:S(2)}) %collective-permute-start.21) | collective-permute-done | bytes 86048 | tf_op jit(solution)/shard_map/ppermute | solution.py:364
  61.2 0.7 %last.1 = bf16[1,32,1344]{2,1,0:T(8,128)(2,1)} custom-call(bf16[32,1344]{1,0:T(8,128)(2,1)S(1)} %get-tuple-element.70.hidden_ref, bf16[32,1344]{1,0:T(8,128)(2,1)S(1)} %get-tuple-element.77.rest_0_, bf16[32,1344]{1,0:T(8,128)(2,1)S(1)} %collective-permute-done.21.rest_1_, bf16[32,1344]{1,0:T(8,128)(2,1)S(1)} %collective-permute-done.22.rest_2_, ...), custom_call_target="tpu_custom_call" | custom-call | tf_op jit(solution)/shard_map/last/pallas_call | solution.py:29
  (19 shorter events, 0.3 us)
Async XLA Ops:
  1.8 1.5 %collective-permute-start = (bf16[528,128]{1,0:T(8,128)(2,1)S(1)}, bf16[528,128]{1,0:T(8,128)(2,1)S(1)}, u32[]{:S(2)}, u32[]{:S(2)}) collective-permute-start(bf16[528,128]{1,0:T(8,128)(2,1)S(1)} %get-tuple-element.49), channel_id=1, source_target_pairs={{0,1},{1,0},{2,3},{3,2},{4,5},{5,4},{6,7},{7,6},{8,9},{9,8},{10,11... | collective-permute-start | bytes 405512 | tf_op jit(solution)/shard_map/ppermute | solution.py:364
  3.4 14.3 %collective-permute-start.1 = (bf16[1,928,1344]{2,1,0:T(8,128)(2,1)}, bf16[1,928,1344]{2,1,0:T(8,128)(2,1)S(1)}, u32[]{:S(2)}, u32[]{:S(2)}) collective-permute-start(bf16[1,928,1344]{2,1,0:T(8,128)(2,1)} %bitcast.9), channel_id=1, source_target_pairs={{0,1},{1,0},{2,3},{3,2},{4,5},{5,4},{6,7},{7,6},{8,9},{9,8},{10,11... | collective-permute-start | bytes 7483400 | tf_op jit(solution)/shard_map/ppermute | solution.py:364
  3.9 13.9 %collective-permute-start.2 = (bf16[1,928,1344]{2,1,0:T(8,128)(2,1)}, bf16[1,928,1344]{2,1,0:T(8,128)(2,1)S(1)}, u32[]{:S(2)}, u32[]{:S(2)}) collective-permute-start(bf16[1,928,1344]{2,1,0:T(8,128)(2,1)} %down_hbm.1), channel_id=1, source_target_pairs={{0,1},{1,0},{2,3},{3,2},{4,5},{5,4},{6,7},{7,6},{8,9},{9,8},{10,11... | collective-permute-start | bytes 7483400 | tf_op jit(solution)/shard_map/ppermute | solution.py:364
  4.0 5.4 %collective-permute-start.3 = (bf16[272,128]{1,0:T(8,128)(2,1)S(1)}, bf16[272,128]{1,0:T(8,128)(2,1)S(1)}, u32[]{:S(2)}, u32[]{:S(2)}) collective-permute-start(bf16[272,128]{1,0:T(8,128)(2,1)S(1)} %get-tuple-element.59.rest_0_), channel_id=1, source_target_pairs={{0,2},{1,3},{2,0},{3,1},{4,6},{5,7},{6,4},{7,5},{8,10},{9,11},{10,... | collective-permute-start | bytes 208904 | tf_op jit(solution)/shard_map/ppermute | solution.py:364
  6.9 4.8 %collective-permute-start.5 = (bf16[272,128]{1,0:T(8,128)(2,1)S(1)}, bf16[272,128]{1,0:T(8,128)(2,1)S(1)}, u32[]{:S(2)}, u32[]{:S(2)}) collective-permute-start(bf16[272,128]{1,0:T(8,128)(2,1)S(1)} %get-tuple-element.60.rest_0_.rest_4_), channel_id=1, source_target_pairs={{0,2},{1,3},{2,0},{3,1},{4,6},{5,7},{6,4},{7,5},{8,10},{9,11},{10,... | collective-permute-start | bytes 208904 | tf_op jit(solution)/shard_map/ppermute | solution.py:364
  9.5 5.2 %collective-permute-start.4 = (bf16[272,128]{1,0:T(8,128)(2,1)S(1)}, bf16[272,128]{1,0:T(8,128)(2,1)S(1)}, u32[]{:S(2)}, u32[]{:S(2)}) collective-permute-start(bf16[272,128]{1,0:T(8,128)(2,1)S(1)} %span.2.rest_2_), channel_id=1, source_target_pairs={{0,16},{16,0},{1,17},{17,1},{2,18},{18,2},{3,19},{19,3},{4,20},{20... | collective-permute-start | bytes 208904 | tf_op jit(solution)/shard_map/ppermute | solution.py:364
  11.8 4.4 %collective-permute-start.6 = (bf16[272,128]{1,0:T(8,128)(2,1)S(1)}, bf16[272,128]{1,0:T(8,128)(2,1)S(1)}, u32[]{:S(2)}, u32[]{:S(2)}) collective-permute-start(bf16[272,128]{1,0:T(8,128)(2,1)S(1)} %span.3.rest_6_), channel_id=1, source_target_pairs={{0,16},{16,0},{1,17},{17,1},{2,18},{18,2},{3,19},{19,3},{4,20},{20... | collective-permute-start | bytes 208904 | tf_op jit(solution)/shard_map/ppermute | solution.py:364
  16.3 1.4 %collective-permute-start.7 = (bf16[4,128,128]{2,1,0:T(8,128)(2,1)S(1)}, bf16[4,128,128]{2,1,0:T(8,128)(2,1)S(1)}, u32[]{:S(2)}, u32[]{:S(2)}) collective-permute-start(bf16[4,128,128]{2,1,0:T(8,128)(2,1)S(1)} %get-tuple-element.61), channel_id=1, source_target_pairs={{0,1},{1,0},{2,3},{3,2},{4,5},{5,4},{6,7},{7,6},{8,9},{9,8},{10,11... | collective-permute-start | bytes 393224 | tf_op jit(solution)/shard_map/ppermute | solution.py:364
  18.6 5.6 %collective-permute-start.8 = (bf16[32,1344]{1,0:T(8,128)(2,1)S(1)}, bf16[32,1344]{1,0:T(8,128)(2,1)S(1)}, u32[]{:S(2)}, u32[]{:S(2)}) collective-permute-start(bf16[32,1344]{1,0:T(8,128)(2,1)S(1)} %get-tuple-element.67), channel_id=1, source_target_pairs={{0,4},{1,9},{2,6},{3,11},{4,0},{5,13},{6,2},{7,15},{8,12},{9,1},{1... | collective-permute-start | bytes 258056 | tf_op jit(solution)/shard_map/ppermute | solution.py:374
  20.3 8.2 %collective-permute-start.9 = (bf16[32,1344]{1,0:T(8,128)(2,1)S(1)}, bf16[32,1344]{1,0:T(8,128)(2,1)S(1)}, u32[]{:S(2)}, u32[]{:S(2)}) collective-permute-start(bf16[32,1344]{1,0:T(8,128)(2,1)S(1)} %get-tuple-element.68), channel_id=1, source_target_pairs={{0,4},{1,13},{2,6},{3,15},{4,0},{5,9},{6,2},{7,11},{8,12},{9,5},{1... | collective-permute-start | bytes 258056 | tf_op jit(solution)/shard_map/ppermute | solution.py:374
  24.2 5.7 %collective-permute-start.10 = (bf16[32,1344]{1,0:T(8,128)(2,1)S(1)}, bf16[32,1344]{1,0:T(8,128)(2,1)S(1)}, u32[]{:S(2)}, u32[]{:S(2)}) collective-permute-start(bf16[32,1344]{1,0:T(8,128)(2,1)S(1)} %relay.1), channel_id=1, source_target_pairs={{0,8},{1,5},{2,10},{3,7},{4,12},{5,1},{6,14},{7,3},{8,0},{9,13},{1... | collective-permute-start | bytes 258056 | tf_op jit(solution)/shard_map/ppermute | solution.py:374
  30.1 5.7 %collective-permute-start.14 = (bf16[32,1408]{1,0:T(8,128)(2,1)S(1)}, bf16[32,1408]{1,0:T(8,128)(2,1)S(1)}, u32[]{:S(2)}, u32[]{:S(2)}) collective-permute-start(bf16[32,1408]{1,0:T(8,128)(2,1)S(1)} %get-tuple-element.72.rest_0_), channel_id=1, source_target_pairs={{0,8},{4,12},{8,0},{12,4},{1,9},{5,13},{9,1},{13,5},{2,10},{6,14},... | collective-permute-start | bytes 270344 | tf_op jit(solution)/shard_map/ppermute | solution.py:364
  31.6 8.3 %collective-permute-start.13 = (bf16[32,1408]{1,0:T(8,128)(2,1)S(1)}, bf16[32,1408]{1,0:T(8,128)(2,1)S(1)}, u32[]{:S(2)}, u32[]{:S(2)}) collective-permute-start(bf16[32,1408]{1,0:T(8,128)(2,1)S(1)} %get-tuple-element.72.rest_0_), channel_id=1, source_target_pairs={{0,6},{1,7},{2,4},{3,5},{4,2},{5,3},{6,0},{7,1},{8,14},{9,15},{10,... | collective-permute-start | bytes 270344 | tf_op jit(solution)/shard_map/ppermute | solution.py:364
  35.3 5.6 %collective-permute-start.12 = (bf16[32,1408]{1,0:T(8,128)(2,1)S(1)}, bf16[32,1408]{1,0:T(8,128)(2,1)S(1)}, u32[]{:S(2)}, u32[]{:S(2)}) collective-permute-start(bf16[32,1408]{1,0:T(8,128)(2,1)S(1)} %get-tuple-element.72.rest_0_), channel_id=1, source_target_pairs={{0,4},{1,5},{2,6},{3,7},{4,0},{5,1},{6,2},{7,3},{8,12},{9,13},{10,... | collective-permute-start | bytes 270344 | tf_op jit(solution)/shard_map/ppermute | solution.py:364
  35.3 6.4 %collective-permute-start.11 = (bf16[32,1408]{1,0:T(8,128)(2,1)S(1)}, bf16[32,1408]{1,0:T(8,128)(2,1)S(1)}, u32[]{:S(2)}, u32[]{:S(2)}) collective-permute-start(bf16[32,1408]{1,0:T(8,128)(2,1)S(1)} %get-tuple-element.72.rest_0_), channel_id=1, source_target_pairs={{0,2},{1,3},{2,0},{3,1},{4,6},{5,7},{6,4},{7,5},{8,10},{9,11},{10,... | collective-permute-start | bytes 270344 | tf_op jit(solution)/shard_map/ppermute | solution.py:364
  35.8 8.6 %collective-permute-start.17 = (bf16[32,1408]{1,0:T(8,128)(2,1)S(1)}, bf16[32,1408]{1,0:T(8,128)(2,1)S(1)}, u32[]{:S(2)}, u32[]{:S(2)}) collective-permute-start(bf16[32,1408]{1,0:T(8,128)(2,1)S(1)} %collective-permute-done.14.rest_0_), channel_id=1, source_target_pairs={{0,6},{1,7},{2,4},{3,5},{4,2},{5,3},{6,0},{7,1},{8,14},{9,15},{10,... | collective-permute-start | bytes 270344 | tf_op jit(solution)/shard_map/ppermute | solution.py:364
  38.8 5.7 %collective-permute-start.16 = (bf16[32,1408]{1,0:T(8,128)(2,1)S(1)}, bf16[32,1408]{1,0:T(8,128)(2,1)S(1)}, u32[]{:S(2)}, u32[]{:S(2)}) collective-permute-start(bf16[32,1408]{1,0:T(8,128)(2,1)S(1)} %collective-permute-done.14.rest_0_), channel_id=1, source_target_pairs={{0,4},{1,5},{2,6},{3,7},{4,0},{5,1},{6,2},{7,3},{8,12},{9,13},{10,... | collective-permute-start | bytes 270344 | tf_op jit(solution)/shard_map/ppermute | solution.py:364
  39.9 4.5 %collective-permute-start.15 = (bf16[32,1408]{1,0:T(8,128)(2,1)S(1)}, bf16[32,1408]{1,0:T(8,128)(2,1)S(1)}, u32[]{:S(2)}, u32[]{:S(2)}) collective-permute-start(bf16[32,1408]{1,0:T(8,128)(2,1)S(1)} %collective-permute-done.14.rest_0_), channel_id=1, source_target_pairs={{0,2},{1,3},{2,0},{3,1},{4,6},{5,7},{6,4},{7,5},{8,10},{9,11},{10,... | collective-permute-start | bytes 270344 | tf_op jit(solution)/shard_map/ppermute | solution.py:364
  47.2 6.4 %collective-permute-start.18 = (bf16[32,1344]{1,0:T(8,128)(2,1)S(1)}, bf16[32,1344]{1,0:T(8,128)(2,1)S(1)}, u32[]{:S(2)}, u32[]{:S(2)}) collective-permute-start(bf16[32,1344]{1,0:T(8,128)(2,1)S(1)} %get-tuple-element.83), channel_id=1, source_target_pairs={{0,6},{1,7},{2,4},{3,5},{4,2},{5,3},{6,0},{7,1},{8,14},{9,15},{10,... | collective-permute-start | bytes 258056 | tf_op jit(solution)/shard_map/ppermute | solution.py:364
  48.9 5.3 %collective-permute-start.19 = (bf16[32,1344]{1,0:T(8,128)(2,1)S(1)}, bf16[32,1344]{1,0:T(8,128)(2,1)S(1)}, u32[]{:S(2)}, u32[]{:S(2)}) collective-permute-start(bf16[32,1344]{1,0:T(8,128)(2,1)S(1)} %get-tuple-element.84), channel_id=1, source_target_pairs={{0,4},{1,5},{2,6},{3,7},{4,0},{5,1},{6,2},{7,3},{8,12},{9,13},{10,... | collective-permute-start | bytes 258056 | tf_op jit(solution)/shard_map/ppermute | solution.py:364
  49.1 5.6 %collective-permute-start.20 = (bf16[32,1344]{1,0:T(8,128)(2,1)S(1)}, bf16[32,1344]{1,0:T(8,128)(2,1)S(1)}, u32[]{:S(2)}, u32[]{:S(2)}) collective-permute-start(bf16[32,1344]{1,0:T(8,128)(2,1)S(1)} %get-tuple-element.85), channel_id=1, source_target_pairs={{0,2},{1,3},{2,0},{3,1},{4,6},{5,7},{6,4},{7,5},{8,10},{9,11},{10,... | collective-permute-start | bytes 258056 | tf_op jit(solution)/shard_map/ppermute | solution.py:364
  50.7 5.9 %collective-permute-start.22 = (bf16[32,1344]{1,0:T(8,128)(2,1)S(1)}, bf16[32,1344]{1,0:T(8,128)(2,1)S(1)}, u32[]{:S(2)}, u32[]{:S(2)}) collective-permute-start(bf16[32,1344]{1,0:T(8,128)(2,1)S(1)} %get-tuple-element.86), channel_id=1, source_target_pairs={{0,6},{1,7},{2,4},{3,5},{4,2},{5,3},{6,0},{7,1},{8,14},{9,15},{10,... | collective-permute-start | bytes 258056 | tf_op jit(solution)/shard_map/ppermute | solution.py:364
  52.4 4.5 %collective-permute-start.23 = (bf16[32,1344]{1,0:T(8,128)(2,1)S(1)}, bf16[32,1344]{1,0:T(8,128)(2,1)S(1)}, u32[]{:S(2)}, u32[]{:S(2)}) collective-permute-start(bf16[32,1344]{1,0:T(8,128)(2,1)S(1)} %get-tuple-element.87), channel_id=1, source_target_pairs={{0,4},{1,5},{2,6},{3,7},{4,0},{5,1},{6,2},{7,3},{8,12},{9,13},{10,... | collective-permute-start | bytes 258056 | tf_op jit(solution)/shard_map/ppermute | solution.py:364
  53.6 4.5 %collective-permute-start.24 = (bf16[32,1344]{1,0:T(8,128)(2,1)S(1)}, bf16[32,1344]{1,0:T(8,128)(2,1)S(1)}, u32[]{:S(2)}, u32[]{:S(2)}) collective-permute-start(bf16[32,1344]{1,0:T(8,128)(2,1)S(1)} %get-tuple-element.88), channel_id=1, source_target_pairs={{0,2},{1,3},{2,0},{3,1},{4,6},{5,7},{6,4},{7,5},{8,10},{9,11},{10,... | collective-permute-start | bytes 258056 | tf_op jit(solution)/shard_map/ppermute | solution.py:364
  54.7 6.5 %collective-permute-start.21 = (bf16[32,1344]{1,0:T(8,128)(2,1)S(1)}, bf16[32,1344]{1,0:T(8,128)(2,1)S(1)}, u32[]{:S(2)}, u32[]{:S(2)}) collective-permute-start(bf16[32,1344]{1,0:T(8,128)(2,1)S(1)} %sum.1), channel_id=1, source_target_pairs={{0,8},{4,12},{8,0},{12,4},{1,9},{5,13},{9,1},{13,5},{2,10},{6,14},... | collective-permute-start | bytes 258056 | tf_op jit(solution)/shard_map/ppermute | solution.py:364

commit v19 on v18

--- a/solution.py
+++ b/solution.py
@@ -339,16 +339,19 @@
         chosen = (lane == expert) | (lane == expert + experts)
         gate = jnp.sum(jnp.where(chosen, tail, 0.0), axis=1, keepdims=True)
         total = total + jnp.dot(activated, down_of[0], preferred_element_type=F32) * gate
-    size = ins[0].shape[0]
-    for at, out in enumerate(outs):
-        out[...] = total[at * size : (at + 1) * size].astype(BF16)
-
-
-def sum_kernel(*refs):
-    total = refs[0][...].astype(F32)
-    for ref in refs[1:-1]:
-        total = total + ref[...].astype(F32)
-    refs[-1][...] = total.astype(BF16)
+    at = 0
+    for out in outs:
+        out[...] = total[at : at + out.shape[0]].astype(BF16)
+        at += out.shape[0]
+
+
+def sum_kernel(block, own_ref, *rest):
+    parts, out_ref = rest[:-1], rest[-1]
+    rows = out_ref.shape[0]
+    total = own_ref[...].astype(F32)
+    for part in parts:
+        total = total + part[block * rows : (block + 1) * rows].astype(F32)
+    out_ref[...] = total.astype(BF16)
 
 
 def last_kernel(hidden_ref, *rest):
@@ -488,30 +491,37 @@
         [(ANY, up_held)] + [(VMEM, value) for value in (resid_held, gate_lanes, gain_held, *parts)],
     )
 
-    def through_experts(members):
+    def through_experts(members, sizes):
         return call(
             functools.partial(expert_kernel, experts, len(members)),
             "experts",
-            [struct((rows, model), BF16)] * len(members),
+            [struct((size * rows, model), BF16) for size in sizes],
             [(VMEM, value) for value in (up_held, down_held, other_up, other_down, *members)],
             megabytes=16,
         )
 
     both = ("head", "exp")
     group = [z * exp_size + 2 * d for z in (0, 1) for d in range(chips)][1:]
-
-    def spread(block):
-        return [block] + [swap(block, both, mask) for mask in group]
-
-    sets = [spread(swap(own_rows, "head", high)) for high in range(2, head_size, 2)]
-    near = through_experts(spread(own_rows))
+    paired = [z * exp_size + 2 * d for d in range(chips) for z in (0, 1)][1:]
+
+    def spread(block, masks):
+        return [block] + [swap(block, both, mask) for mask in masks]
+
+    sets = [spread(swap(own_rows, "head", high), paired) for high in range(2, head_size, 2)]
+    near = through_experts(spread(own_rows, group), [1] * (1 + len(group)))
     near, sets = lax.optimization_barrier((near, sets))
     arrived = []
     for high, members in zip(range(2, head_size, 2), sets):
-        pieces = through_experts(members)
-        got = [swap(piece, both, mask) for piece, mask in zip(pieces[:0:-1], group[::-1])]
-        total = call(sum_kernel, "sum", struct((rows, model), BF16), [(VMEM, v) for v in (pieces[0], *got)])
-        arrived.append(swap(total, "head", high))
+        pieces = through_experts(members, [1, 1] + [2] * (chips - 1))
+        got = [swap(piece, "exp", 2 * d) for d, piece in enumerate(pieces[2:], 1)]
+        for z in (1, 0):
+            total = call(
+                functools.partial(sum_kernel, z),
+                "sum",
+                struct((rows, model), BF16),
+                [(VMEM, value) for value in (pieces[z], *got)],
+            )
+            arrived.append(swap(total, "head", high + z))
     arrived += [swap(piece, both, mask) for piece, mask in zip(near[:0:-1], group[::-1])]
     return call(
         last_kernel,

time: 62.2 us -> 63.1 us (1.014)
  waiting for transfers between devices: 15.6 us -> 17.6 us
  starting transfers between devices: 28.1 us -> 26.9 us
    ppermute x22 -> x21, waiting for transfers between devices: 10.7 us -> 12.7 us  [swap(): return lax.ppermute(value, axis, [(i, i ^ mask) for i in range(size)])]
    ppermute x22 -> x21, starting transfers between devices: 24.3 us -> 23.1 us  [swap(): return lax.ppermute(value, axis, [(i, i ^ mask) for i in range(size)])]
    pallas_call x17 -> x18, Pallas kernels: 18.1 us -> 18.1 us  [call(): pl.pallas_call(kernel, out_shape=jax.tree.map(lambda out: pltpu.VMEM(out....]
  transfers between devices with their start and end apart: 25 -> 24, of which waited for: 12 -> 10; matrix products, arithmetic and copies ran while one was open for 0% -> 0% of each run, Pallas kernels for 19% -> 19%
where the time goes in v19:
time: 63.1 us; the launch traced here: 62.8 us
  starting transfers between devices  26.9 us (43%)
  Pallas kernels  18.1 us (29%)
  waiting for transfers between devices  17.6 us (28%)
    ppermute x21, starting transfers between devices, swap(): return lax.ppermute(value, axis, [(i, i ^ mask) for i in range(size)])  23.1 us
    pallas_call x18, Pallas kernels, call(): pl.pallas_call(kernel, out_shape=jax.tree.map(lambda out: pltpu.VMEM(out....  18.1 us
    ppermute x21, waiting for transfers between devices, swap(): return lax.ppermute(value, axis, [(i, i ^ mask) for i in range(size)])  12.7 us
    ppermute x3, waiting for transfers between devices, swap_slot(): return lax.ppermute(value, ('head', 'exp'), pairs)  4.87 us
    ppermute x3, starting transfers between devices, swap_slot(): return lax.ppermute(value, ('head', 'exp'), pairs)  3.81 us
  transfers between devices with their start and end apart: 24, of which 10 were waited for; matrix products, arithmetic and copies ran while one was open for 0% of the time, Pallas kernels for 19%

profile of v19, /device:TPU:0, one launch (start us, length us, event | category | flops | bytes accessed | tf_op | source)
XLA Modules:
  0.0 62.8 jit_solution(3988984022572947490)
XLA Ops:
  0.0 1.8 %state.1 = (bf16[528,128]{1,0:T(8,128)(2,1)S(1)}, bf16[528,128]{1,0:T(8,128)(2,1)S(1)}) custom-call(bf16[128,1024]{1,0:T(8,128)(2,1)} %x_hbm.3, bf16[128,256]{1,0:T(8,128)(2,1)} %b_hbm.3, f32[16,128]{1,0:T(8,128)} %bitcast.11, f32[1,16]{1,0:T(1,128)} %bitcast.16), custom_call_target="tpu_custom_call" | custom-call | tf_op jit(solution)/shard_map/state/pallas_call | solution.py:29
  1.8 0.5 collective-permute-start
  2.4 1.0 %prep.1 = (bf16[32,128]{1,0:T(8,128)(2,1)S(1)}, bf16[1,32,1344]{2,1,0:T(8,128)(2,1)S(1)}, f32[1,1344]{1,0:T(1,128)S(1)}) custom-call(bf16[528,128]{1,0:T(8,128)(2,1)S(1)} %get-tuple-element.46.after_ref.keep_ref, bf16[1,32,1344]{2,1,0:T(8,128)(2,1)} %resid_hbm.1, s32[6,1,32]{2,1,0:T(1,128)} %bitcast.14, f32[6,1,32]{2,1,0:T(1,128)} %bitcast.15, f32[1344]{0:T(1024)} %gain_hbm.1), custom_call_target="tpu_custom_call" | custom-call | tf_op jit(solution)/shard_map/prep/pallas_call | solution.py:29
  3.3 0.1 chip_state.1
  3.4 0.4 collective-permute-start.1
  3.9 0.1 collective-permute-start.2
  4.0 2.9 %collective-permute-start.3 = (bf16[272,128]{1,0:T(8,128)(2,1)S(1)}, bf16[272,128]{1,0:T(8,128)(2,1)S(1)}, u32[]{:S(2)}, u32[]{:S(2)}) collective-permute-start(bf16[272,128]{1,0:T(8,128)(2,1)S(1)} %get-tuple-element.58.rest_0_), channel_id=1, source_target_pairs={{0,2},{1,3},{2,0},{3,1},{4,6},{5,7},{6,4},{7,5},{8,10},{9,11},{10,... | collective-permute-start | bytes 208904 | tf_op jit(solution)/shard_map/ppermute | solution.py:367
  6.9 2.4 %inside.1 = (f32[128,1024]{1,0:T(8,128)S(1)}, f32[128,1024]{1,0:T(8,128)S(1)}, bf16[128,256]{1,0:T(8,128)(2,1)S(1)}) custom-call(bf16[128,1024]{1,0:T(8,128)(2,1)} %x_hbm.3, bf16[128,1024]{1,0:T(8,128)(2,1)} %z_hbm.1, bf16[128,256]{1,0:T(8,128)(2,1)} %b_hbm.3, bf16[128,256]{1,0:T(8,128)(2,1)} %c_hbm.1, f32[16,128]{1,0:T(8,128)} %bitcast.12, ...), custom_call_target="tpu_custom_call" | custom-call | tf_op jit(solution)/shard_map/inside/pallas_call | solution.py:29
  9.4 0.0 collective-permute-done.3.rest_1_
  9.4 0.1 span.2.rest_2_
  9.5 2.2 %collective-permute-start.4 = (bf16[272,128]{1,0:T(8,128)(2,1)S(1)}, bf16[272,128]{1,0:T(8,128)(2,1)S(1)}, u32[]{:S(2)}, u32[]{:S(2)}) collective-permute-start(bf16[272,128]{1,0:T(8,128)(2,1)S(1)} %span.2.rest_2_), channel_id=1, source_target_pairs={{0,16},{16,0},{1,17},{17,1},{2,18},{18,2},{3,19},{19,3},{4,20},{20... | collective-permute-start | bytes 208904 | tf_op jit(solution)/shard_map/ppermute | solution.py:367
  11.7 0.1 span.3.rest_6_
  11.8 1.1 %collective-permute-start.6 = (bf16[272,128]{1,0:T(8,128)(2,1)S(1)}, bf16[272,128]{1,0:T(8,128)(2,1)S(1)}, u32[]{:S(2)}, u32[]{:S(2)}) collective-permute-start(bf16[272,128]{1,0:T(8,128)(2,1)S(1)} %span.3.rest_6_), channel_id=1, source_target_pairs={{0,16},{16,0},{1,17},{17,1},{2,18},{18,2},{3,19},{19,3},{4,20},{20... | collective-permute-start | bytes 208904 | tf_op jit(solution)/shard_map/ppermute | solution.py:367
  12.8 1.8 %projection.1 = (f32[1,1024]{1,0:T(1,128)S(1)}, bf16[1344,1024]{1,0:T(8,128)(2,1)S(1)}) custom-call(f32[1,1024]{1,0:T(1,128)} %bitcast.13, bf16[1344,1024]{1,0:T(8,128)(2,1)} %bitcast.8), custom_call_target="tpu_custom_call" | custom-call | tf_op jit(solution)/shard_map/projection/pallas_call | solution.py:29
  14.7 1.5 %collective-permute-done.6.rest_7_ = bf16[272,128]{1,0:T(8,128)(2,1)S(1)} collective-permute-done((bf16[272,128]{1,0:T(8,128)(2,1)S(1)}, bf16[272,128]{1,0:T(8,128)(2,1)S(1)}, u32[]{:S(2)}, u32[]{:S(2)}) %collective-permute-start.6) | collective-permute-done | bytes 69664 | tf_op jit(solution)/shard_map/ppermute | solution.py:367
  16.1 0.2 before.1
  16.3 0.1 collective-permute-start.7
  16.4 0.8 %first_half.1.first_ref = f32[128,1344]{1,0:T(8,128)S(1)} custom-call(f32[128,1024]{1,0:T(8,128)S(1)} %get-tuple-element.53.local_ref, f32[128,1024]{1,0:T(8,128)S(1)} %get-tuple-element.54.grown_ref, bf16[128,256]{1,0:T(8,128)(2,1)S(1)} %get-tuple-element.55.after_ref.c_ref, f32[1,1024]{1,0:T(1,128)S(1)} %get-tuple-element.56.after_ref.norm_ref, ...), custom_call_target="tpu_custom_call" | custom-call | tf_op jit(solution)/shard_map/first_half/pallas_call | solution.py:29
  17.3 0.5 collective-permute-done.7.got_ref
  17.8 0.9 %mixed.1 = (bf16[32,1344]{1,0:T(8,128)(2,1)S(1)}, bf16[32,1344]{1,0:T(8,128)(2,1)S(1)}, bf16[32,1344]{1,0:T(8,128)(2,1)S(1)}, bf16[32,1344]{1,0:T(8,128)(2,1)S(1)}) custom-call(bf16[1,928,1344]{2,1,0:T(8,128)(2,1)S(1)} %collective-permute-done.1.after_up.other_up_ref, bf16[1,928,1344]{2,1,0:T(8,128)(2,1)S(1)} %collective-permute-done.2.after_down.other_down_ref, ...), custom_call_target="tpu_custom_call" | custom-call | tf_op jit(solution)/shard_map/mixed/pallas_call | solution.py:29
  18.6 1.6 %collective-permute-start.8 = (bf16[32,1344]{1,0:T(8,128)(2,1)S(1)}, bf16[32,1344]{1,0:T(8,128)(2,1)S(1)}, u32[]{:S(2)}, u32[]{:S(2)}) collective-permute-start(bf16[32,1344]{1,0:T(8,128)(2,1)S(1)} %get-tuple-element.66), channel_id=1, source_target_pairs={{0,4},{1,9},{2,6},{3,11},{4,0},{5,13},{6,2},{7,15},{8,12},{9,1},{1... | collective-permute-start | bytes 258056 | tf_op jit(solution)/shard_map/ppermute | solution.py:377
  20.3 0.5 collective-permute-start.9
  20.7 3.5 %collective-permute-done.8.got_ref.rest_1_ = bf16[32,1344]{1,0:T(8,128)(2,1)S(1)} collective-permute-done((bf16[32,1344]{1,0:T(8,128)(2,1)S(1)}, bf16[32,1344]{1,0:T(8,128)(2,1)S(1)}, u32[]{:S(2)}, u32[]{:S(2)}) %collective-permute-start.8) | collective-permute-done | bytes 86048 | tf_op jit(solution)/shard_map/ppermute | solution.py:377
  24.2 1.7 %collective-permute-start.10 = (bf16[32,1344]{1,0:T(8,128)(2,1)S(1)}, bf16[32,1344]{1,0:T(8,128)(2,1)S(1)}, u32[]{:S(2)}, u32[]{:S(2)}) collective-permute-start(bf16[32,1344]{1,0:T(8,128)(2,1)S(1)} %relay.1), channel_id=1, source_target_pairs={{0,8},{1,5},{2,10},{3,7},{4,12},{5,1},{6,14},{7,3},{8,0},{9,13},{1... | collective-permute-start | bytes 258056 | tf_op jit(solution)/shard_map/ppermute | solution.py:377
  25.9 2.5 %weights.1 = (bf16[1,928,1344]{2,1,0:T(8,128)(2,1)S(1)}, bf16[1,928,1344]{2,1,0:T(8,128)(2,1)S(1)}) custom-call(bf16[32,1344]{1,0:T(8,128)(2,1)S(1)} %get-tuple-element.62.after_ref.rest_0_, bf16[1,928,1344]{2,1,0:T(8,128)(2,1)} %bitcast.10, bf16[1,928,1344]{2,1,0:T(8,128)(2,1)} %down_hbm.1), custom_call_target="tpu_custom_call" | custom-call | tf_op jit(solution)/shard_map/weights/pallas_call | solution.py:29
  28.5 1.4 %collective-permute-done.10.rest_3_ = bf16[32,1344]{1,0:T(8,128)(2,1)S(1)} collective-permute-done((bf16[32,1344]{1,0:T(8,128)(2,1)S(1)}, bf16[32,1344]{1,0:T(8,128)(2,1)S(1)}, u32[]{:S(2)}, u32[]{:S(2)}) %collective-permute-start.10) | collective-permute-done | bytes 86048 | tf_op jit(solution)/shard_map/ppermute | solution.py:377
  29.9 0.2 rows.1
  30.1 1.5 %collective-permute-start.14 = (bf16[32,1408]{1,0:T(8,128)(2,1)S(1)}, bf16[32,1408]{1,0:T(8,128)(2,1)S(1)}, u32[]{:S(2)}, u32[]{:S(2)}) collective-permute-start(bf16[32,1408]{1,0:T(8,128)(2,1)S(1)} %get-tuple-element.71.rest_0_), channel_id=1, source_target_pairs={{0,8},{4,12},{8,0},{12,4},{1,9},{5,13},{9,1},{13,5},{2,10},{6,14},... | collective-permute-start | bytes 270344 | tf_op jit(solution)/shard_map/ppermute | solution.py:367
  31.6 3.6 %collective-permute-start.13 = (bf16[32,1408]{1,0:T(8,128)(2,1)S(1)}, bf16[32,1408]{1,0:T(8,128)(2,1)S(1)}, u32[]{:S(2)}, u32[]{:S(2)}) collective-permute-start(bf16[32,1408]{1,0:T(8,128)(2,1)S(1)} %get-tuple-element.71.rest_0_), channel_id=1, source_target_pairs={{0,6},{1,7},{2,4},{3,5},{4,2},{5,3},{6,0},{7,1},{8,14},{9,15},{10,... | collective-permute-start | bytes 270344 | tf_op jit(solution)/shard_map/ppermute | solution.py:367
  35.3 0.6 collective-permute-start.11
  35.8 2.9 %collective-permute-start.17 = (bf16[32,1408]{1,0:T(8,128)(2,1)S(1)}, bf16[32,1408]{1,0:T(8,128)(2,1)S(1)}, u32[]{:S(2)}, u32[]{:S(2)}) collective-permute-start(bf16[32,1408]{1,0:T(8,128)(2,1)S(1)} %collective-permute-done.14.rest_0_), channel_id=1, source_target_pairs={{0,6},{1,7},{2,4},{3,5},{4,2},{5,3},{6,0},{7,1},{8,14},{9,15},{10,... | collective-permute-start | bytes 270344 | tf_op jit(solution)/shard_map/ppermute | solution.py:367
  38.8 0.5 collective-permute-start.16
  39.3 1.4 %collective-permute-start.15 = (bf16[32,1408]{1,0:T(8,128)(2,1)S(1)}, bf16[32,1408]{1,0:T(8,128)(2,1)S(1)}, u32[]{:S(2)}, u32[]{:S(2)}) collective-permute-start(bf16[32,1408]{1,0:T(8,128)(2,1)S(1)} %collective-permute-done.14.rest_0_), channel_id=1, source_target_pairs={{0,4},{1,5},{2,6},{3,7},{4,0},{5,1},{6,2},{7,3},{8,12},{9,13},{10,... | collective-permute-start | bytes 270344 | tf_op jit(solution)/shard_map/ppermute | solution.py:367
  40.6 0.2 collective-permute-done.12.rest_2_
  40.9 1.2 %collective-permute-done.11.rest_1_ = bf16[32,1408]{1,0:T(8,128)(2,1)S(1)} collective-permute-done((bf16[32,1408]{1,0:T(8,128)(2,1)S(1)}, bf16[32,1408]{1,0:T(8,128)(2,1)S(1)}, u32[]{:S(2)}, u32[]{:S(2)}) %collective-permute-start.11) | collective-permute-done | bytes 90144 | tf_op jit(solution)/shard_map/ppermute | solution.py:367
  42.1 2.7 %experts.2 = (bf16[32,1344]{1,0:T(8,128)(2,1)S(1)}, bf16[32,1344]{1,0:T(8,128)(2,1)S(1)}, bf16[32,1344]{1,0:T(8,128)(2,1)S(1)}, bf16[32,1344]{1,0:T(8,128)(2,1)S(1)}) custom-call(bf16[1,928,1344]{2,1,0:T(8,128)(2,1)S(1)} %get-tuple-element.63.after_ref.up_ref, bf16[1,928,1344]{2,1,0:T(8,128)(2,1)S(1)} %get-tuple-element.70.down_ref, ...), custom_call_target="tpu_custom_call" | custom-call | tf_op jit(solution)/shard_map/experts/pallas_call | solution.py:29
  44.8 2.7 %experts.3 = (bf16[32,1344]{1,0:T(8,128)(2,1)S(1)}, bf16[32,1344]{1,0:T(8,128)(2,1)S(1)}, bf16[64,1344]{1,0:T(8,128)(2,1)S(1)}) custom-call(bf16[1,928,1344]{2,1,0:T(8,128)(2,1)S(1)} %get-tuple-element.63.after_ref.up_ref, bf16[1,928,1344]{2,1,0:T(8,128)(2,1)S(1)} %get-tuple-element.70.down_ref, ...), custom_call_target="tpu_custom_call" | custom-call | tf_op jit(solution)/shard_map/experts/pallas_call | solution.py:29
  47.5 0.6 collective-permute-start.18
  48.1 1.6 %collective-permute-start.21 = (bf16[32,1344]{1,0:T(8,128)(2,1)S(1)}, bf16[32,1344]{1,0:T(8,128)(2,1)S(1)}, u32[]{:S(2)}, u32[]{:S(2)}) collective-permute-start(bf16[32,1344]{1,0:T(8,128)(2,1)S(1)} %get-tuple-element.84), channel_id=1, source_target_pairs={{0,6},{1,7},{2,4},{3,5},{4,2},{5,3},{6,0},{7,1},{8,14},{9,15},{10,... | collective-permute-start | bytes 258056 | tf_op jit(solution)/shard_map/ppermute | solution.py:367
  49.7 1.4 %collective-permute-start.22 = (bf16[32,1344]{1,0:T(8,128)(2,1)S(1)}, bf16[32,1344]{1,0:T(8,128)(2,1)S(1)}, u32[]{:S(2)}, u32[]{:S(2)}) collective-permute-start(bf16[32,1344]{1,0:T(8,128)(2,1)S(1)} %get-tuple-element.85), channel_id=1, source_target_pairs={{0,4},{1,5},{2,6},{3,7},{4,0},{5,1},{6,2},{7,3},{8,12},{9,13},{10,... | collective-permute-start | bytes 258056 | tf_op jit(solution)/shard_map/ppermute | solution.py:367
  51.1 0.5 collective-permute-start.23
  51.6 2.5 %collective-permute-done.18.rest_0_ = bf16[64,1344]{1,0:T(8,128)(2,1)S(1)} collective-permute-done((bf16[64,1344]{1,0:T(8,128)(2,1)S(1)}, bf16[64,1344]{1,0:T(8,128)(2,1)S(1)}, u32[]{:S(2)}, u32[]{:S(2)}) %collective-permute-start.18) | collective-permute-done | bytes 172064 | tf_op jit(solution)/shard_map/ppermute | solution.py:367
  54.2 0.4 collective-permute-start.19
  54.7 0.8 %collective-permute-start.20 = (bf16[32,1344]{1,0:T(8,128)(2,1)S(1)}, bf16[32,1344]{1,0:T(8,128)(2,1)S(1)}, u32[]{:S(2)}, u32[]{:S(2)}) collective-permute-start(bf16[32,1344]{1,0:T(8,128)(2,1)S(1)} %sum.3), channel_id=1, source_target_pairs={{0,8},{4,12},{8,0},{12,4},{1,9},{5,13},{9,1},{13,5},{2,10},{6,14},... | collective-permute-start | bytes 258056 | tf_op jit(solution)/shard_map/ppermute | solution.py:367
  55.4 1.1 %collective-permute-done.22.rest_4_ = bf16[32,1344]{1,0:T(8,128)(2,1)S(1)} collective-permute-done((bf16[32,1344]{1,0:T(8,128)(2,1)S(1)}, bf16[32,1344]{1,0:T(8,128)(2,1)S(1)}, u32[]{:S(2)}, u32[]{:S(2)}) %collective-permute-start.22) | collective-permute-done | bytes 86048 | tf_op jit(solution)/shard_map/ppermute | solution.py:367
  56.5 4.2 %collective-permute-done.19.rest_1_ = bf16[32,1344]{1,0:T(8,128)(2,1)S(1)} collective-permute-done((bf16[32,1344]{1,0:T(8,128)(2,1)S(1)}, bf16[32,1344]{1,0:T(8,128)(2,1)S(1)}, u32[]{:S(2)}, u32[]{:S(2)}) %collective-permute-start.19) | collective-permute-done | bytes 86048 | tf_op jit(solution)/shard_map/ppermute | solution.py:367
  60.7 1.4 %collective-permute-done.20.rest_2_ = bf16[32,1344]{1,0:T(8,128)(2,1)S(1)} collective-permute-done((bf16[32,1344]{1,0:T(8,128)(2,1)S(1)}, bf16[32,1344]{1,0:T(8,128)(2,1)S(1)}, u32[]{:S(2)}, u32[]{:S(2)}) %collective-permute-start.20) | collective-permute-done | bytes 86048 | tf_op jit(solution)/shard_map/ppermute | solution.py:367
  62.1 0.7 %last.1 = bf16[1,32,1344]{2,1,0:T(8,128)(2,1)} custom-call(bf16[32,1344]{1,0:T(8,128)(2,1)S(1)} %get-tuple-element.69.hidden_ref, bf16[32,1344]{1,0:T(8,128)(2,1)S(1)} %get-tuple-element.76.rest_0_, bf16[32,1344]{1,0:T(8,128)(2,1)S(1)} %collective-permute-done.19.rest_1_, bf16[32,1344]{1,0:T(8,128)(2,1)S(1)} %collective-permute-done.20.rest_2_, ...), custom_call_target="tpu_custom_call" | custom-call | tf_op jit(solution)/shard_map/last/pallas_call | solution.py:29
  (18 shorter events, 0.2 us)
Async XLA Ops:
  1.8 1.5 %collective-permute-start = (bf16[528,128]{1,0:T(8,128)(2,1)S(1)}, bf16[528,128]{1,0:T(8,128)(2,1)S(1)}, u32[]{:S(2)}, u32[]{:S(2)}) collective-permute-start(bf16[528,128]{1,0:T(8,128)(2,1)S(1)} %get-tuple-element.48), channel_id=1, source_target_pairs={{0,1},{1,0},{2,3},{3,2},{4,5},{5,4},{6,7},{7,6},{8,9},{9,8},{10,11... | collective-permute-start | bytes 405512 | tf_op jit(solution)/shard_map/ppermute | solution.py:367
  3.4 14.3 %collective-permute-start.1 = (bf16[1,928,1344]{2,1,0:T(8,128)(2,1)}, bf16[1,928,1344]{2,1,0:T(8,128)(2,1)S(1)}, u32[]{:S(2)}, u32[]{:S(2)}) collective-permute-start(bf16[1,928,1344]{2,1,0:T(8,128)(2,1)} %bitcast.9), channel_id=1, source_target_pairs={{0,1},{1,0},{2,3},{3,2},{4,5},{5,4},{6,7},{7,6},{8,9},{9,8},{10,11... | collective-permute-start | bytes 7483400 | tf_op jit(solution)/shard_map/ppermute | solution.py:367
  3.9 13.9 %collective-permute-start.2 = (bf16[1,928,1344]{2,1,0:T(8,128)(2,1)}, bf16[1,928,1344]{2,1,0:T(8,128)(2,1)S(1)}, u32[]{:S(2)}, u32[]{:S(2)}) collective-permute-start(bf16[1,928,1344]{2,1,0:T(8,128)(2,1)} %down_hbm.1), channel_id=1, source_target_pairs={{0,1},{1,0},{2,3},{3,2},{4,5},{5,4},{6,7},{7,6},{8,9},{9,8},{10,11... | collective-permute-start | bytes 7483400 | tf_op jit(solution)/shard_map/ppermute | solution.py:367
  4.0 5.4 %collective-permute-start.3 = (bf16[272,128]{1,0:T(8,128)(2,1)S(1)}, bf16[272,128]{1,0:T(8,128)(2,1)S(1)}, u32[]{:S(2)}, u32[]{:S(2)}) collective-permute-start(bf16[272,128]{1,0:T(8,128)(2,1)S(1)} %get-tuple-element.58.rest_0_), channel_id=1, source_target_pairs={{0,2},{1,3},{2,0},{3,1},{4,6},{5,7},{6,4},{7,5},{8,10},{9,11},{10,... | collective-permute-start | bytes 208904 | tf_op jit(solution)/shard_map/ppermute | solution.py:367
  6.9 4.8 %collective-permute-start.5 = (bf16[272,128]{1,0:T(8,128)(2,1)S(1)}, bf16[272,128]{1,0:T(8,128)(2,1)S(1)}, u32[]{:S(2)}, u32[]{:S(2)}) collective-permute-start(bf16[272,128]{1,0:T(8,128)(2,1)S(1)} %get-tuple-element.59.rest_0_.rest_4_), channel_id=1, source_target_pairs={{0,2},{1,3},{2,0},{3,1},{4,6},{5,7},{6,4},{7,5},{8,10},{9,11},{10,... | collective-permute-start | bytes 208904 | tf_op jit(solution)/shard_map/ppermute | solution.py:367
  9.5 5.2 %collective-permute-start.4 = (bf16[272,128]{1,0:T(8,128)(2,1)S(1)}, bf16[272,128]{1,0:T(8,128)(2,1)S(1)}, u32[]{:S(2)}, u32[]{:S(2)}) collective-permute-start(bf16[272,128]{1,0:T(8,128)(2,1)S(1)} %span.2.rest_2_), channel_id=1, source_target_pairs={{0,16},{16,0},{1,17},{17,1},{2,18},{18,2},{3,19},{19,3},{4,20},{20... | collective-permute-start | bytes 208904 | tf_op jit(solution)/shard_map/ppermute | solution.py:367
  11.8 4.4 %collective-permute-start.6 = (bf16[272,128]{1,0:T(8,128)(2,1)S(1)}, bf16[272,128]{1,0:T(8,128)(2,1)S(1)}, u32[]{:S(2)}, u32[]{:S(2)}) collective-permute-start(bf16[272,128]{1,0:T(8,128)(2,1)S(1)} %span.3.rest_6_), channel_id=1, source_target_pairs={{0,16},{16,0},{1,17},{17,1},{2,18},{18,2},{3,19},{19,3},{4,20},{20... | collective-permute-start | bytes 208904 | tf_op jit(solution)/shard_map/ppermute | solution.py:367
  16.3 1.4 %collective-permute-start.7 = (bf16[4,128,128]{2,1,0:T(8,128)(2,1)S(1)}, bf16[4,128,128]{2,1,0:T(8,128)(2,1)S(1)}, u32[]{:S(2)}, u32[]{:S(2)}) collective-permute-start(bf16[4,128,128]{2,1,0:T(8,128)(2,1)S(1)} %get-tuple-element.60), channel_id=1, source_target_pairs={{0,1},{1,0},{2,3},{3,2},{4,5},{5,4},{6,7},{7,6},{8,9},{9,8},{10,11... | collective-permute-start | bytes 393224 | tf_op jit(solution)/shard_map/ppermute | solution.py:367
  18.6 5.6 %collective-permute-start.8 = (bf16[32,1344]{1,0:T(8,128)(2,1)S(1)}, bf16[32,1344]{1,0:T(8,128)(2,1)S(1)}, u32[]{:S(2)}, u32[]{:S(2)}) collective-permute-start(bf16[32,1344]{1,0:T(8,128)(2,1)S(1)} %get-tuple-element.66), channel_id=1, source_target_pairs={{0,4},{1,9},{2,6},{3,11},{4,0},{5,13},{6,2},{7,15},{8,12},{9,1},{1... | collective-permute-start | bytes 258056 | tf_op jit(solution)/shard_map/ppermute | solution.py:377
  20.3 8.2 %collective-permute-start.9 = (bf16[32,1344]{1,0:T(8,128)(2,1)S(1)}, bf16[32,1344]{1,0:T(8,128)(2,1)S(1)}, u32[]{:S(2)}, u32[]{:S(2)}) collective-permute-start(bf16[32,1344]{1,0:T(8,128)(2,1)S(1)} %get-tuple-element.67), channel_id=1, source_target_pairs={{0,4},{1,13},{2,6},{3,15},{4,0},{5,9},{6,2},{7,11},{8,12},{9,5},{1... | collective-permute-start | bytes 258056 | tf_op jit(solution)/shard_map/ppermute | solution.py:377
  24.2 5.7 %collective-permute-start.10 = (bf16[32,1344]{1,0:T(8,128)(2,1)S(1)}, bf16[32,1344]{1,0:T(8,128)(2,1)S(1)}, u32[]{:S(2)}, u32[]{:S(2)}) collective-permute-start(bf16[32,1344]{1,0:T(8,128)(2,1)S(1)} %relay.1), channel_id=1, source_target_pairs={{0,8},{1,5},{2,10},{3,7},{4,12},{5,1},{6,14},{7,3},{8,0},{9,13},{1... | collective-permute-start | bytes 258056 | tf_op jit(solution)/shard_map/ppermute | solution.py:377
  30.1 5.7 %collective-permute-start.14 = (bf16[32,1408]{1,0:T(8,128)(2,1)S(1)}, bf16[32,1408]{1,0:T(8,128)(2,1)S(1)}, u32[]{:S(2)}, u32[]{:S(2)}) collective-permute-start(bf16[32,1408]{1,0:T(8,128)(2,1)S(1)} %get-tuple-element.71.rest_0_), channel_id=1, source_target_pairs={{0,8},{4,12},{8,0},{12,4},{1,9},{5,13},{9,1},{13,5},{2,10},{6,14},... | collective-permute-start | bytes 270344 | tf_op jit(solution)/shard_map/ppermute | solution.py:367
  31.6 7.6 %collective-permute-start.13 = (bf16[32,1408]{1,0:T(8,128)(2,1)S(1)}, bf16[32,1408]{1,0:T(8,128)(2,1)S(1)}, u32[]{:S(2)}, u32[]{:S(2)}) collective-permute-start(bf16[32,1408]{1,0:T(8,128)(2,1)S(1)} %get-tuple-element.71.rest_0_), channel_id=1, source_target_pairs={{0,6},{1,7},{2,4},{3,5},{4,2},{5,3},{6,0},{7,1},{8,14},{9,15},{10,... | collective-permute-start | bytes 270344 | tf_op jit(solution)/shard_map/ppermute | solution.py:367
  35.3 5.6 %collective-permute-start.12 = (bf16[32,1408]{1,0:T(8,128)(2,1)S(1)}, bf16[32,1408]{1,0:T(8,128)(2,1)S(1)}, u32[]{:S(2)}, u32[]{:S(2)}) collective-permute-start(bf16[32,1408]{1,0:T(8,128)(2,1)S(1)} %get-tuple-element.71.rest_0_), channel_id=1, source_target_pairs={{0,4},{1,5},{2,6},{3,7},{4,0},{5,1},{6,2},{7,3},{8,12},{9,13},{10,... | collective-permute-start | bytes 270344 | tf_op jit(solution)/shard_map/ppermute | solution.py:367
  35.3 6.8 %collective-permute-start.11 = (bf16[32,1408]{1,0:T(8,128)(2,1)S(1)}, bf16[32,1408]{1,0:T(8,128)(2,1)S(1)}, u32[]{:S(2)}, u32[]{:S(2)}) collective-permute-start(bf16[32,1408]{1,0:T(8,128)(2,1)S(1)} %get-tuple-element.71.rest_0_), channel_id=1, source_target_pairs={{0,2},{1,3},{2,0},{3,1},{4,6},{5,7},{6,4},{7,5},{8,10},{9,11},{10,... | collective-permute-start | bytes 270344 | tf_op jit(solution)/shard_map/ppermute | solution.py:367
  35.8 8.9 %collective-permute-start.17 = (bf16[32,1408]{1,0:T(8,128)(2,1)S(1)}, bf16[32,1408]{1,0:T(8,128)(2,1)S(1)}, u32[]{:S(2)}, u32[]{:S(2)}) collective-permute-start(bf16[32,1408]{1,0:T(8,128)(2,1)S(1)} %collective-permute-done.14.rest_0_), channel_id=1, source_target_pairs={{0,6},{1,7},{2,4},{3,5},{4,2},{5,3},{6,0},{7,1},{8,14},{9,15},{10,... | collective-permute-start | bytes 270344 | tf_op jit(solution)/shard_map/ppermute | solution.py:367
  38.8 6.0 %collective-permute-start.16 = (bf16[32,1408]{1,0:T(8,128)(2,1)S(1)}, bf16[32,1408]{1,0:T(8,128)(2,1)S(1)}, u32[]{:S(2)}, u32[]{:S(2)}) collective-permute-start(bf16[32,1408]{1,0:T(8,128)(2,1)S(1)} %collective-permute-done.14.rest_0_), channel_id=1, source_target_pairs={{0,2},{1,3},{2,0},{3,1},{4,6},{5,7},{6,4},{7,5},{8,10},{9,11},{10,... | collective-permute-start | bytes 270344 | tf_op jit(solution)/shard_map/ppermute | solution.py:367
  39.3 5.5 %collective-permute-start.15 = (bf16[32,1408]{1,0:T(8,128)(2,1)S(1)}, bf16[32,1408]{1,0:T(8,128)(2,1)S(1)}, u32[]{:S(2)}, u32[]{:S(2)}) collective-permute-start(bf16[32,1408]{1,0:T(8,128)(2,1)S(1)} %collective-permute-done.14.rest_0_), channel_id=1, source_target_pairs={{0,4},{1,5},{2,6},{3,7},{4,0},{5,1},{6,2},{7,3},{8,12},{9,13},{10,... | collective-permute-start | bytes 270344 | tf_op jit(solution)/shard_map/ppermute | solution.py:367
  47.5 6.6 %collective-permute-start.18 = (bf16[64,1344]{1,0:T(8,128)(2,1)S(1)}, bf16[64,1344]{1,0:T(8,128)(2,1)S(1)}, u32[]{:S(2)}, u32[]{:S(2)}) collective-permute-start(bf16[64,1344]{1,0:T(8,128)(2,1)S(1)} %get-tuple-element.82), channel_id=1, source_target_pairs={{0,2},{1,3},{2,0},{3,1},{4,6},{5,7},{6,4},{7,5},{8,10},{9,11},{10,... | collective-permute-start | bytes 516104 | tf_op jit(solution)/shard_map/ppermute | solution.py:367
  48.1 7.3 %collective-permute-start.21 = (bf16[32,1344]{1,0:T(8,128)(2,1)S(1)}, bf16[32,1344]{1,0:T(8,128)(2,1)S(1)}, u32[]{:S(2)}, u32[]{:S(2)}) collective-permute-start(bf16[32,1344]{1,0:T(8,128)(2,1)S(1)} %get-tuple-element.84), channel_id=1, source_target_pairs={{0,6},{1,7},{2,4},{3,5},{4,2},{5,3},{6,0},{7,1},{8,14},{9,15},{10,... | collective-permute-start | bytes 258056 | tf_op jit(solution)/shard_map/ppermute | solution.py:367
  49.7 6.8 %collective-permute-start.22 = (bf16[32,1344]{1,0:T(8,128)(2,1)S(1)}, bf16[32,1344]{1,0:T(8,128)(2,1)S(1)}, u32[]{:S(2)}, u32[]{:S(2)}) collective-permute-start(bf16[32,1344]{1,0:T(8,128)(2,1)S(1)} %get-tuple-element.85), channel_id=1, source_target_pairs={{0,4},{1,5},{2,6},{3,7},{4,0},{5,1},{6,2},{7,3},{8,12},{9,13},{10,... | collective-permute-start | bytes 258056 | tf_op jit(solution)/shard_map/ppermute | solution.py:367
  51.1 5.4 %collective-permute-start.23 = (bf16[32,1344]{1,0:T(8,128)(2,1)S(1)}, bf16[32,1344]{1,0:T(8,128)(2,1)S(1)}, u32[]{:S(2)}, u32[]{:S(2)}) collective-permute-start(bf16[32,1344]{1,0:T(8,128)(2,1)S(1)} %get-tuple-element.86), channel_id=1, source_target_pairs={{0,2},{1,3},{2,0},{3,1},{4,6},{5,7},{6,4},{7,5},{8,10},{9,11},{10,... | collective-permute-start | bytes 258056 | tf_op jit(solution)/shard_map/ppermute | solution.py:367
  54.2 6.5 %collective-permute-start.19 = (bf16[32,1344]{1,0:T(8,128)(2,1)S(1)}, bf16[32,1344]{1,0:T(8,128)(2,1)S(1)}, u32[]{:S(2)}, u32[]{:S(2)}) collective-permute-start(bf16[32,1344]{1,0:T(8,128)(2,1)S(1)} %sum.2), channel_id=1, source_target_pairs={{0,12},{4,8},{8,4},{12,0},{1,13},{5,9},{9,5},{13,1},{2,14},{6,10},... | collective-permute-start | bytes 258056 | tf_op jit(solution)/shard_map/ppermute | solution.py:367
  54.7 7.4 %collective-permute-start.20 = (bf16[32,1344]{1,0:T(8,128)(2,1)S(1)}, bf16[32,1344]{1,0:T(8,128)(2,1)S(1)}, u32[]{:S(2)}, u32[]{:S(2)}) collective-permute-start(bf16[32,1344]{1,0:T(8,128)(2,1)S(1)} %sum.3), channel_id=1, source_target_pairs={{0,8},{4,12},{8,0},{12,4},{1,9},{5,13},{9,1},{13,5},{2,10},{6,14},... | collective-permute-start | bytes 258056 | tf_op jit(solution)/shard_map/ppermute | solution.py:367

commit v20 on v17

--- a/solution.py
+++ b/solution.py
@@ -137,15 +137,12 @@
     send_ref[...] = packed_ref[1 - core_index()]
 
 
-def chip_state_kernel(after_ref, keep_ref, got_ref, *outs):
+def chip_state_kernel(after_ref, keep_ref, got_ref, out_ref):
     first = core_index() == 0
     keep, got = unpacked(keep_ref[...]), unpacked(got_ref[...])
     early = [jnp.where(first, mine, other) for mine, other in zip(keep, got)]
     late = [jnp.where(first, other, mine) for mine, other in zip(keep, got)]
-    total, state = early[0] + late[0], jnp.exp(late[0]) * early[1] + late[1]
-    size = total.shape[0] // len(outs)
-    for at, out in enumerate(outs):
-        pack(out, total[at * size : (at + 1) * size], state[at * size : (at + 1) * size])
+    pack(out_ref, early[0] + late[0], jnp.exp(late[0]) * early[1] + late[1])
 
 
 def weights_kernel(after_ref, up_hbm, down_hbm, up_ref, down_ref, sems):
@@ -153,7 +150,7 @@
         load.wait()
 
 
-def span_kernel(after_ref, *rest):
+def span_kernel(*rest):
     ins, out_ref, block_ref = rest[:-2], rest[-2], rest[-1]
     for mask, part in enumerate(ins):
         block_ref[chip_index() ^ mask] = part[...]
@@ -164,27 +161,25 @@
     pack(out_ref, total, state)
 
 
-def before_kernel(chips, parts, after_ref, keep_ref, got_ref, *rest):
+def before_kernel(chips, parts, flat, after_a, after_b, keep_ref, got_ref, *rest):
     ins, (mine_ref, send_ref, chip_ref, part_ref) = rest[:-4], rest[-4:]
     first = core_index() == 0
     totals, states = (jnp.where(first, k, g) for k, g in zip(unpacked(keep_ref[...]), unpacked(got_ref[...])))
-    each = chips + parts
-    chunks = len(ins) // each
-    size = totals.shape[0] // chunks
-    for chunk in range(chunks):
-        span = slice(chunk * size, (chunk + 1) * size)
-        for mask in range(chips):
-            chip_ref[chip_index() ^ mask] = ins[chunk * each + mask][...]
-        for mask in range(parts):
-            part_ref[lax.axis_index("seq") ^ mask] = ins[chunk * each + chips + mask][...]
-        carry = jnp.zeros(states[span].shape, F32)
-        for ref, count, own in ((part_ref, parts, lax.axis_index("seq")), (chip_ref, chips, chip_index())):
-            for index in range(count - 1):
-                total, state = unpacked(ref[index])
-                carry = jnp.where(index < own, jnp.exp(total) * carry + state, carry)
-        later = jnp.exp(totals[span]) * carry + states[span]
-        mine_ref[span] = jnp.where(first, carry, later).astype(BF16)
-        send_ref[span] = jnp.where(first, later, carry).astype(BF16)
+    place = chip_index()
+    if flat:
+        place = lax.axis_index("seq") * (lax.axis_size("exp") // 2) + place
+    for mask in range(chips):
+        chip_ref[place ^ mask] = ins[mask][...]
+    for mask in range(parts):
+        part_ref[lax.axis_index("seq") ^ mask] = ins[chips + mask][...]
+    carry = jnp.zeros(states.shape, F32)
+    for ref, count, own in ((part_ref, parts, lax.axis_index("seq")), (chip_ref, chips, place)):
+        for index in range(count - 1):
+            total, state = unpacked(ref[index])
+            carry = jnp.where(index < own, jnp.exp(total) * carry + state, carry)
+    later = jnp.exp(totals) * carry + states
+    mine_ref[...] = jnp.where(first, carry, later).astype(BF16)
+    send_ref[...] = jnp.where(first, later, carry).astype(BF16)
 
 
 def inside_kernel(x_hbm, z_hbm, b_hbm, c_hbm, dt_hbm, a_hbm, d_hbm, local_ref, grown_ref, c_ref, *scratch):
@@ -432,28 +427,31 @@
     )
     up_turned = jnp.swapaxes(w_up, 1, 2)
     got = swap(send, "exp", 1)
-    chunks = 2 if half % 2 == 0 else 1
-    packed = struct((half // chunks * STATE + TILE, LANES), BF16)
-    chip = call(chip_state_kernel, "chip_state", [packed] * chunks, [(ANY, gate_lanes), (VMEM, keep), (VMEM, got)])
+    chip = call(chip_state_kernel, "chip_state", packed, [(ANY, gate_lanes), (VMEM, keep), (VMEM, got)])
     chip, up_after, down_after = lax.optimization_barrier((chip, up_turned, w_down))
     other_up, other_down = swap(up_after, "exp", 1), swap(down_after, "exp", 1)
-    exchanged = []
-    for own in chip:
-        along_y = [own] + [swap(own, "exp", 2 * d) for d in range(1, chips)]
+    flat = seq_size * chips <= 8
+    if flat:
+        masks = [x * exp_size + 2 * y for x in range(seq_size) for y in range(chips)]
+        exchanged = [chip] + [swap(chip, ("seq", "exp"), mask) for mask in masks[1:]]
+        counts = (seq_size * chips, 0)
+    else:
+        along_y = [chip] + [swap(chip, "exp", 2 * d) for d in range(1, chips)]
         span = call(
             span_kernel,
             "span",
             packed,
-            [(ANY, c_held)] + [(VMEM, value) for value in along_y],
+            [(VMEM, value) for value in along_y],
             [pltpu.VMEM((chips, *packed.shape), BF16)],
         )
-        exchanged += along_y + [span] + [swap(span, "seq", d) for d in range(1, seq_size)]
+        exchanged = along_y + [span] + [swap(span, "seq", d) for d in range(1, seq_size)]
+        counts = (chips, seq_size)
     before, before_send = call(
-        functools.partial(before_kernel, chips, seq_size),
+        functools.partial(before_kernel, *counts, flat),
         "before",
         [struct((half, STATE, LANES), BF16)] * 2,
-        [(ANY, norm_held)] + [(VMEM, value) for value in (keep, got, *exchanged)],
-        [pltpu.VMEM((chips, *packed.shape), BF16), pltpu.VMEM((seq_size, *packed.shape), BF16)],
+        [(ANY, norm_held), (ANY, c_held)] + [(VMEM, value) for value in (keep, got, *exchanged)],
+        [pltpu.VMEM((counts[0], *packed.shape), BF16), pltpu.VMEM((max(1, counts[1]), *packed.shape), BF16)],
         megabytes=24,
     )
     before_got = swap(before_send, "exp", 1)

time: 62.4 us -> 60.8 us (0.974)
  starting transfers between devices: 27.4 us -> 25.1 us
    ppermute x20 -> x19, starting transfers between devices: 23.5 us -> 21.3 us  [swap(): return lax.ppermute(value, axis, [(i, i ^ mask) for i in range(size)])]
    ppermute x20 -> x19, waiting for transfers between devices: 11.6 us -> 12.2 us  [swap(): return lax.ppermute(value, axis, [(i, i ^ mask) for i in range(size)])]
    pallas_call x17 -> x15, Pallas kernels: 18.1 us -> 18.1 us  [call(): pl.pallas_call(kernel, out_shape=jax.tree.map(lambda out: pltpu.VMEM(out....]
  transfers between devices with their start and end apart: 23 -> 22, of which waited for: 8 -> 10; matrix products, arithmetic and copies ran while one was open for 0% -> 0% of each run, Pallas kernels for 19% -> 19%
where the time goes in v20:
time: 60.8 us; the launch traced here: 60.4 us
  starting transfers between devices  25.1 us (41%)
  Pallas kernels  18.1 us (30%)
  waiting for transfers between devices  17.1 us (28%)
    ppermute x19, starting transfers between devices, swap(): return lax.ppermute(value, axis, [(i, i ^ mask) for i in range(size)])  21.3 us
    pallas_call x15, Pallas kernels, call(): pl.pallas_call(kernel, out_shape=jax.tree.map(lambda out: pltpu.VMEM(out....  18.1 us
    ppermute x19, waiting for transfers between devices, swap(): return lax.ppermute(value, axis, [(i, i ^ mask) for i in range(size)])  12.2 us
    ppermute x3, waiting for transfers between devices, swap_slot(): return lax.ppermute(value, ('head', 'exp'), pairs)  4.89 us
    ppermute x3, starting transfers between devices, swap_slot(): return lax.ppermute(value, ('head', 'exp'), pairs)  3.79 us
  transfers between devices with their start and end apart: 22, of which 10 were waited for; matrix products, arithmetic and copies ran while one was open for 0% of the time, Pallas kernels for 19%

profile of v20, /device:TPU:0, one launch (start us, length us, event | category | flops | bytes accessed | tf_op | source)
XLA Modules:
  0.0 60.4 jit_solution(12707985813861877217)
XLA Ops:
  0.0 1.8 %state.1 = (bf16[528,128]{1,0:T(8,128)(2,1)S(1)}, bf16[528,128]{1,0:T(8,128)(2,1)S(1)}) custom-call(bf16[128,1024]{1,0:T(8,128)(2,1)} %x_hbm.3, bf16[128,256]{1,0:T(8,128)(2,1)} %b_hbm.3, f32[16,128]{1,0:T(8,128)} %bitcast.11, f32[1,16]{1,0:T(1,128)} %bitcast.16), custom_call_target="tpu_custom_call" | custom-call | tf_op jit(solution)/shard_map/state/pallas_call | solution.py:29
  1.8 0.5 collective-permute-start
  2.4 1.0 %prep.1 = (bf16[32,128]{1,0:T(8,128)(2,1)S(1)}, bf16[1,32,1344]{2,1,0:T(8,128)(2,1)S(1)}, f32[1,1344]{1,0:T(1,128)S(1)}) custom-call(bf16[528,128]{1,0:T(8,128)(2,1)S(1)} %get-tuple-element.46.after_ref.keep_ref, bf16[1,32,1344]{2,1,0:T(8,128)(2,1)} %resid_hbm.1, s32[6,1,32]{2,1,0:T(1,128)} %bitcast.14, f32[6,1,32]{2,1,0:T(1,128)} %bitcast.15, f32[1344]{0:T(1024)} %gain_hbm.1), custom_call_target="tpu_custom_call" | custom-call | tf_op jit(solution)/shard_map/prep/pallas_call | solution.py:29
  3.3 0.0 collective-permute-done.got_ref
  3.3 0.1 chip_state.1.rest_0_
  3.4 0.4 collective-permute-start.1
  3.9 0.1 collective-permute-start.2
  4.0 3.8 %collective-permute-start.5 = (bf16[528,128]{1,0:T(8,128)(2,1)S(1)}, bf16[528,128]{1,0:T(8,128)(2,1)S(1)}, u32[]{:S(2)}, u32[]{:S(2)}) collective-permute-start(bf16[528,128]{1,0:T(8,128)(2,1)S(1)} %chip_state.1.rest_0_), channel_id=1, source_target_pairs={{0,18},{1,19},{2,16},{3,17},{16,2},{17,3},{18,0},{19,1},{4,22},{5,... | collective-permute-start | bytes 405512 | tf_op jit(solution)/shard_map/ppermute | solution.py:363
  7.8 0.5 collective-permute-start.4
  8.4 0.0 collective-permute-start.3
  8.4 1.8 %projection.1 = (f32[1,1024]{1,0:T(1,128)S(1)}, bf16[1344,1024]{1,0:T(8,128)(2,1)S(1)}) custom-call(f32[1,1024]{1,0:T(1,128)} %bitcast.13, bf16[1344,1024]{1,0:T(8,128)(2,1)} %bitcast.8), custom_call_target="tpu_custom_call" | custom-call | tf_op jit(solution)/shard_map/projection/pallas_call | solution.py:29
  10.2 2.4 %inside.1 = (f32[128,1024]{1,0:T(8,128)S(1)}, f32[128,1024]{1,0:T(8,128)S(1)}, bf16[128,256]{1,0:T(8,128)(2,1)S(1)}) custom-call(bf16[128,1024]{1,0:T(8,128)(2,1)} %x_hbm.3, bf16[128,1024]{1,0:T(8,128)(2,1)} %z_hbm.1, bf16[128,256]{1,0:T(8,128)(2,1)} %b_hbm.3, bf16[128,256]{1,0:T(8,128)(2,1)} %c_hbm.1, f32[16,128]{1,0:T(8,128)} %bitcast.12, ...), custom_call_target="tpu_custom_call" | custom-call | tf_op jit(solution)/shard_map/inside/pallas_call | solution.py:29
  12.7 0.0 collective-permute-done.5.rest_3_
  12.7 2.2 %collective-permute-done.4.rest_2_ = bf16[528,128]{1,0:T(8,128)(2,1)S(1)} collective-permute-done((bf16[528,128]{1,0:T(8,128)(2,1)S(1)}, bf16[528,128]{1,0:T(8,128)(2,1)S(1)}, u32[]{:S(2)}, u32[]{:S(2)}) %collective-permute-start.4) | collective-permute-done | bytes 135200 | tf_op jit(solution)/shard_map/ppermute | solution.py:363
  14.9 0.3 before.1
  15.2 0.1 collective-permute-start.6
  15.3 0.8 %first_half.1.first_ref = f32[128,1344]{1,0:T(8,128)S(1)} custom-call(f32[128,1024]{1,0:T(8,128)S(1)} %get-tuple-element.51.local_ref, f32[128,1024]{1,0:T(8,128)S(1)} %get-tuple-element.52.grown_ref, bf16[128,256]{1,0:T(8,128)(2,1)S(1)} %get-tuple-element.53.after_b.c_ref, f32[1,1024]{1,0:T(1,128)S(1)} %get-tuple-element.54.after_a.norm_ref, ...), custom_call_target="tpu_custom_call" | custom-call | tf_op jit(solution)/shard_map/first_half/pallas_call | solution.py:29
  16.1 0.5 collective-permute-done.6.got_ref
  16.6 0.9 %mixed.1 = (bf16[32,1344]{1,0:T(8,128)(2,1)S(1)}, bf16[32,1344]{1,0:T(8,128)(2,1)S(1)}, bf16[32,1344]{1,0:T(8,128)(2,1)S(1)}, bf16[32,1344]{1,0:T(8,128)(2,1)S(1)}) custom-call(bf16[1,928,1344]{2,1,0:T(8,128)(2,1)S(1)} %collective-permute-done.1.after_up.other_up_ref, bf16[1,928,1344]{2,1,0:T(8,128)(2,1)S(1)} %collective-permute-done.2.after_down.other_down_ref, ...), custom_call_target="tpu_custom_call" | custom-call | tf_op jit(solution)/shard_map/mixed/pallas_call | solution.py:29
  17.5 1.6 %collective-permute-start.7 = (bf16[32,1344]{1,0:T(8,128)(2,1)S(1)}, bf16[32,1344]{1,0:T(8,128)(2,1)S(1)}, u32[]{:S(2)}, u32[]{:S(2)}) collective-permute-start(bf16[32,1344]{1,0:T(8,128)(2,1)S(1)} %get-tuple-element.63), channel_id=1, source_target_pairs={{0,4},{1,9},{2,6},{3,11},{4,0},{5,13},{6,2},{7,15},{8,12},{9,1},{1... | collective-permute-start | bytes 258056 | tf_op jit(solution)/shard_map/ppermute | solution.py:373
  19.1 0.5 collective-permute-start.8
  19.6 3.5 %collective-permute-done.7.got_ref.rest_1_ = bf16[32,1344]{1,0:T(8,128)(2,1)S(1)} collective-permute-done((bf16[32,1344]{1,0:T(8,128)(2,1)S(1)}, bf16[32,1344]{1,0:T(8,128)(2,1)S(1)}, u32[]{:S(2)}, u32[]{:S(2)}) %collective-permute-start.7) | collective-permute-done | bytes 86048 | tf_op jit(solution)/shard_map/ppermute | solution.py:373
  23.1 1.7 %collective-permute-start.9 = (bf16[32,1344]{1,0:T(8,128)(2,1)S(1)}, bf16[32,1344]{1,0:T(8,128)(2,1)S(1)}, u32[]{:S(2)}, u32[]{:S(2)}) collective-permute-start(bf16[32,1344]{1,0:T(8,128)(2,1)S(1)} %relay.1), channel_id=1, source_target_pairs={{0,8},{1,5},{2,10},{3,7},{4,12},{5,1},{6,14},{7,3},{8,0},{9,13},{1... | collective-permute-start | bytes 258056 | tf_op jit(solution)/shard_map/ppermute | solution.py:373
  24.8 2.5 %weights.1 = (bf16[1,928,1344]{2,1,0:T(8,128)(2,1)S(1)}, bf16[1,928,1344]{2,1,0:T(8,128)(2,1)S(1)}) custom-call(bf16[32,1344]{1,0:T(8,128)(2,1)S(1)} %get-tuple-element.59.after_ref.rest_0_, bf16[1,928,1344]{2,1,0:T(8,128)(2,1)} %bitcast.10, bf16[1,928,1344]{2,1,0:T(8,128)(2,1)} %down_hbm.1), custom_call_target="tpu_custom_call" | custom-call | tf_op jit(solution)/shard_map/weights/pallas_call | solution.py:29
  27.4 1.4 %collective-permute-done.9.rest_3_ = bf16[32,1344]{1,0:T(8,128)(2,1)S(1)} collective-permute-done((bf16[32,1344]{1,0:T(8,128)(2,1)S(1)}, bf16[32,1344]{1,0:T(8,128)(2,1)S(1)}, u32[]{:S(2)}, u32[]{:S(2)}) %collective-permute-start.9) | collective-permute-done | bytes 86048 | tf_op jit(solution)/shard_map/ppermute | solution.py:373
  28.8 0.2 rows.1
  29.0 1.5 %collective-permute-start.13 = (bf16[32,1408]{1,0:T(8,128)(2,1)S(1)}, bf16[32,1408]{1,0:T(8,128)(2,1)S(1)}, u32[]{:S(2)}, u32[]{:S(2)}) collective-permute-start(bf16[32,1408]{1,0:T(8,128)(2,1)S(1)} %get-tuple-element.68.rest_0_), channel_id=1, source_target_pairs={{0,8},{4,12},{8,0},{12,4},{1,9},{5,13},{9,1},{13,5},{2,10},{6,14},... | collective-permute-start | bytes 270344 | tf_op jit(solution)/shard_map/ppermute | solution.py:363
  30.5 3.3 %collective-permute-start.12 = (bf16[32,1408]{1,0:T(8,128)(2,1)S(1)}, bf16[32,1408]{1,0:T(8,128)(2,1)S(1)}, u32[]{:S(2)}, u32[]{:S(2)}) collective-permute-start(bf16[32,1408]{1,0:T(8,128)(2,1)S(1)} %get-tuple-element.68.rest_0_), channel_id=1, source_target_pairs={{0,6},{1,7},{2,4},{3,5},{4,2},{5,3},{6,0},{7,1},{8,14},{9,15},{10,... | collective-permute-start | bytes 270344 | tf_op jit(solution)/shard_map/ppermute | solution.py:363
  33.8 0.6 %collective-permute-start.10 = (bf16[32,1408]{1,0:T(8,128)(2,1)S(1)}, bf16[32,1408]{1,0:T(8,128)(2,1)S(1)}, u32[]{:S(2)}, u32[]{:S(2)}) collective-permute-start(bf16[32,1408]{1,0:T(8,128)(2,1)S(1)} %get-tuple-element.68.rest_0_), channel_id=1, source_target_pairs={{0,2},{1,3},{2,0},{3,1},{4,6},{5,7},{6,4},{7,5},{8,10},{9,11},{10,... | collective-permute-start | bytes 270344 | tf_op jit(solution)/shard_map/ppermute | solution.py:363
  34.4 0.1 collective-permute-done.13.rest_0_
  34.6 2.7 %collective-permute-start.16 = (bf16[32,1408]{1,0:T(8,128)(2,1)S(1)}, bf16[32,1408]{1,0:T(8,128)(2,1)S(1)}, u32[]{:S(2)}, u32[]{:S(2)}) collective-permute-start(bf16[32,1408]{1,0:T(8,128)(2,1)S(1)} %collective-permute-done.13.rest_0_), channel_id=1, source_target_pairs={{0,6},{1,7},{2,4},{3,5},{4,2},{5,3},{6,0},{7,1},{8,14},{9,15},{10,... | collective-permute-start | bytes 270344 | tf_op jit(solution)/shard_map/ppermute | solution.py:363
  37.3 1.1 %collective-permute-start.15 = (bf16[32,1408]{1,0:T(8,128)(2,1)S(1)}, bf16[32,1408]{1,0:T(8,128)(2,1)S(1)}, u32[]{:S(2)}, u32[]{:S(2)}) collective-permute-start(bf16[32,1408]{1,0:T(8,128)(2,1)S(1)} %collective-permute-done.13.rest_0_), channel_id=1, source_target_pairs={{0,4},{1,5},{2,6},{3,7},{4,0},{5,1},{6,2},{7,3},{8,12},{9,13},{10,... | collective-permute-start | bytes 270344 | tf_op jit(solution)/shard_map/ppermute | solution.py:363
  38.4 0.0 collective-permute-done.12.rest_3_
  38.4 0.0 collective-permute-start.14
  38.4 0.9 %collective-permute-done.11.rest_2_ = bf16[32,1408]{1,0:T(8,128)(2,1)S(1)} collective-permute-done((bf16[32,1408]{1,0:T(8,128)(2,1)S(1)}, bf16[32,1408]{1,0:T(8,128)(2,1)S(1)}, u32[]{:S(2)}, u32[]{:S(2)}) %collective-permute-start.11) | collective-permute-done | bytes 90144 | tf_op jit(solution)/shard_map/ppermute | solution.py:363
  39.4 1.5 %collective-permute-done.10.rest_1_ = bf16[32,1408]{1,0:T(8,128)(2,1)S(1)} collective-permute-done((bf16[32,1408]{1,0:T(8,128)(2,1)S(1)}, bf16[32,1408]{1,0:T(8,128)(2,1)S(1)}, u32[]{:S(2)}, u32[]{:S(2)}) %collective-permute-start.10) | collective-permute-done | bytes 90144 | tf_op jit(solution)/shard_map/ppermute | solution.py:363
  40.9 2.7 %experts.2 = (bf16[32,1344]{1,0:T(8,128)(2,1)S(1)}, bf16[32,1344]{1,0:T(8,128)(2,1)S(1)}, bf16[32,1344]{1,0:T(8,128)(2,1)S(1)}, bf16[32,1344]{1,0:T(8,128)(2,1)S(1)}) custom-call(bf16[1,928,1344]{2,1,0:T(8,128)(2,1)S(1)} %get-tuple-element.60.after_ref.up_ref, bf16[1,928,1344]{2,1,0:T(8,128)(2,1)S(1)} %get-tuple-element.67.down_ref, ...), custom_call_target="tpu_custom_call" | custom-call | tf_op jit(solution)/shard_map/experts/pallas_call | solution.py:29
  43.7 2.7 %experts.3 = (bf16[32,1344]{1,0:T(8,128)(2,1)S(1)}, bf16[32,1344]{1,0:T(8,128)(2,1)S(1)}, bf16[64,1344]{1,0:T(8,128)(2,1)S(1)}, bf16[64,1344]{1,0:T(8,128)(2,1)S(1)}) custom-call(bf16[1,928,1344]{2,1,0:T(8,128)(2,1)S(1)} %get-tuple-element.60.after_ref.up_ref, bf16[1,928,1344]{2,1,0:T(8,128)(2,1)S(1)} %get-tuple-element.67.down_ref, ...), custom_call_target="tpu_custom_call" | custom-call | tf_op jit(solution)/shard_map/experts/pallas_call | solution.py:29
  46.4 1.2 %collective-permute-start.17 = (bf16[64,1344]{1,0:T(8,128)(2,1)S(1)}, bf16[64,1344]{1,0:T(8,128)(2,1)S(1)}, u32[]{:S(2)}, u32[]{:S(2)}) collective-permute-start(bf16[64,1344]{1,0:T(8,128)(2,1)S(1)} %get-tuple-element.80), channel_id=1, source_target_pairs={{0,6},{1,7},{2,4},{3,5},{4,2},{5,3},{6,0},{7,1},{8,14},{9,15},{10,... | collective-permute-start | bytes 516104 | tf_op jit(solution)/shard_map/ppermute | solution.py:363
  47.6 0.2 collective-permute-start.18
  47.8 2.2 %collective-permute-start.19 = (bf16[32,1344]{1,0:T(8,128)(2,1)S(1)}, bf16[32,1344]{1,0:T(8,128)(2,1)S(1)}, u32[]{:S(2)}, u32[]{:S(2)}) collective-permute-start(bf16[32,1344]{1,0:T(8,128)(2,1)S(1)} %get-tuple-element.83), channel_id=1, source_target_pairs={{0,2},{1,3},{2,0},{3,1},{4,6},{5,7},{6,4},{7,5},{8,10},{9,11},{10,... | collective-permute-start | bytes 258056 | tf_op jit(solution)/shard_map/ppermute | solution.py:363
  49.9 4.2 %collective-permute-done.19.refs_3_ = bf16[32,1344]{1,0:T(8,128)(2,1)S(1)} collective-permute-done((bf16[32,1344]{1,0:T(8,128)(2,1)S(1)}, bf16[32,1344]{1,0:T(8,128)(2,1)S(1)}, u32[]{:S(2)}, u32[]{:S(2)}) %collective-permute-start.19) | collective-permute-done | bytes 86048 | tf_op jit(solution)/shard_map/ppermute | solution.py:363
  54.1 0.1 collective-permute-done.18.refs_2_.rest_2_
  54.2 0.1 sum.1
  54.2 0.9 %collective-permute-start.20 = (bf16[32,1344]{1,0:T(8,128)(2,1)S(1)}, bf16[32,1344]{1,0:T(8,128)(2,1)S(1)}, u32[]{:S(2)}, u32[]{:S(2)}) collective-permute-start(bf16[32,1344]{1,0:T(8,128)(2,1)S(1)} %sum.1), channel_id=1, source_target_pairs={{0,8},{4,12},{8,0},{12,4},{1,9},{5,13},{9,1},{13,5},{2,10},{6,14},... | collective-permute-start | bytes 258056 | tf_op jit(solution)/shard_map/ppermute | solution.py:363
  55.2 2.0 %collective-permute-start.21 = (bf16[32,1344]{1,0:T(8,128)(2,1)S(1)}, bf16[32,1344]{1,0:T(8,128)(2,1)S(1)}, u32[]{:S(2)}, u32[]{:S(2)}) collective-permute-start(bf16[32,1344]{1,0:T(8,128)(2,1)S(1)} %get-tuple-element.86), channel_id=1, source_target_pairs={{0,2},{1,3},{2,0},{3,1},{4,6},{5,7},{6,4},{7,5},{8,10},{9,11},{10,... | collective-permute-start | bytes 258056 | tf_op jit(solution)/shard_map/ppermute | solution.py:363
  57.2 2.5 %collective-permute-done.20.rest_3_ = bf16[32,1344]{1,0:T(8,128)(2,1)S(1)} collective-permute-done((bf16[32,1344]{1,0:T(8,128)(2,1)S(1)}, bf16[32,1344]{1,0:T(8,128)(2,1)S(1)}, u32[]{:S(2)}, u32[]{:S(2)}) %collective-permute-start.20) | collective-permute-done | bytes 86048 | tf_op jit(solution)/shard_map/ppermute | solution.py:363
  59.7 0.7 %last.1 = bf16[1,32,1344]{2,1,0:T(8,128)(2,1)} custom-call(bf16[32,1344]{1,0:T(8,128)(2,1)S(1)} %get-tuple-element.66.hidden_ref, bf16[32,1344]{1,0:T(8,128)(2,1)S(1)} %get-tuple-element.73.rest_0_, bf16[64,1344]{1,0:T(8,128)(2,1)S(1)} %collective-permute-done.17.refs_1_.rest_1_, bf16[64,1344]{1,0:T(8,128)(2,1)S(1)} %collective-permute-done.18.refs_2_.rest_2_, ...), custom_call_target="tpu_custom_call" | custom-call | tf_op jit(solution)/shard_map/last/pallas_call | solution.py:29
  (11 shorter events, 0.1 us)
Async XLA Ops:
  1.8 1.5 %collective-permute-start = (bf16[528,128]{1,0:T(8,128)(2,1)S(1)}, bf16[528,128]{1,0:T(8,128)(2,1)S(1)}, u32[]{:S(2)}, u32[]{:S(2)}) collective-permute-start(bf16[528,128]{1,0:T(8,128)(2,1)S(1)} %get-tuple-element.48), channel_id=1, source_target_pairs={{0,1},{1,0},{2,3},{3,2},{4,5},{5,4},{6,7},{7,6},{8,9},{9,8},{10,11... | collective-permute-start | bytes 405512 | tf_op jit(solution)/shard_map/ppermute | solution.py:363
  3.4 13.2 %collective-permute-start.1 = (bf16[1,928,1344]{2,1,0:T(8,128)(2,1)}, bf16[1,928,1344]{2,1,0:T(8,128)(2,1)S(1)}, u32[]{:S(2)}, u32[]{:S(2)}) collective-permute-start(bf16[1,928,1344]{2,1,0:T(8,128)(2,1)} %bitcast.9), channel_id=1, source_target_pairs={{0,1},{1,0},{2,3},{3,2},{4,5},{5,4},{6,7},{7,6},{8,9},{9,8},{10,11... | collective-permute-start | bytes 7483400 | tf_op jit(solution)/shard_map/ppermute | solution.py:363
  3.9 12.8 %collective-permute-start.2 = (bf16[1,928,1344]{2,1,0:T(8,128)(2,1)}, bf16[1,928,1344]{2,1,0:T(8,128)(2,1)S(1)}, u32[]{:S(2)}, u32[]{:S(2)}) collective-permute-start(bf16[1,928,1344]{2,1,0:T(8,128)(2,1)} %down_hbm.1), channel_id=1, source_target_pairs={{0,1},{1,0},{2,3},{3,2},{4,5},{5,4},{6,7},{7,6},{8,9},{9,8},{10,11... | collective-permute-start | bytes 7483400 | tf_op jit(solution)/shard_map/ppermute | solution.py:363
  4.0 8.6 %collective-permute-start.5 = (bf16[528,128]{1,0:T(8,128)(2,1)S(1)}, bf16[528,128]{1,0:T(8,128)(2,1)S(1)}, u32[]{:S(2)}, u32[]{:S(2)}) collective-permute-start(bf16[528,128]{1,0:T(8,128)(2,1)S(1)} %chip_state.1.rest_0_), channel_id=1, source_target_pairs={{0,18},{1,19},{2,16},{3,17},{16,2},{17,3},{18,0},{19,1},{4,22},{5,... | collective-permute-start | bytes 405512 | tf_op jit(solution)/shard_map/ppermute | solution.py:363
  7.8 7.1 %collective-permute-start.4 = (bf16[528,128]{1,0:T(8,128)(2,1)S(1)}, bf16[528,128]{1,0:T(8,128)(2,1)S(1)}, u32[]{:S(2)}, u32[]{:S(2)}) collective-permute-start(bf16[528,128]{1,0:T(8,128)(2,1)S(1)} %chip_state.1.rest_0_), channel_id=1, source_target_pairs={{0,16},{1,17},{2,18},{3,19},{16,0},{17,1},{18,2},{19,3},{4,20},{5,... | collective-permute-start | bytes 405512 | tf_op jit(solution)/shard_map/ppermute | solution.py:363
  8.4 6.5 %collective-permute-start.3 = (bf16[528,128]{1,0:T(8,128)(2,1)S(1)}, bf16[528,128]{1,0:T(8,128)(2,1)S(1)}, u32[]{:S(2)}, u32[]{:S(2)}) collective-permute-start(bf16[528,128]{1,0:T(8,128)(2,1)S(1)} %chip_state.1.rest_0_), channel_id=1, source_target_pairs={{0,2},{1,3},{2,0},{3,1},{16,18},{17,19},{18,16},{19,17},{4,6},{5,7... | collective-permute-start | bytes 405512 | tf_op jit(solution)/shard_map/ppermute | solution.py:363
  15.2 1.4 %collective-permute-start.6 = (bf16[4,128,128]{2,1,0:T(8,128)(2,1)S(1)}, bf16[4,128,128]{2,1,0:T(8,128)(2,1)S(1)}, u32[]{:S(2)}, u32[]{:S(2)}) collective-permute-start(bf16[4,128,128]{2,1,0:T(8,128)(2,1)S(1)} %get-tuple-element.57), channel_id=1, source_target_pairs={{0,1},{1,0},{2,3},{3,2},{4,5},{5,4},{6,7},{7,6},{8,9},{9,8},{10,11... | collective-permute-start | bytes 393224 | tf_op jit(solution)/shard_map/ppermute | solution.py:363
  17.5 5.6 %collective-permute-start.7 = (bf16[32,1344]{1,0:T(8,128)(2,1)S(1)}, bf16[32,1344]{1,0:T(8,128)(2,1)S(1)}, u32[]{:S(2)}, u32[]{:S(2)}) collective-permute-start(bf16[32,1344]{1,0:T(8,128)(2,1)S(1)} %get-tuple-element.63), channel_id=1, source_target_pairs={{0,4},{1,9},{2,6},{3,11},{4,0},{5,13},{6,2},{7,15},{8,12},{9,1},{1... | collective-permute-start | bytes 258056 | tf_op jit(solution)/shard_map/ppermute | solution.py:373
  19.1 8.2 %collective-permute-start.8 = (bf16[32,1344]{1,0:T(8,128)(2,1)S(1)}, bf16[32,1344]{1,0:T(8,128)(2,1)S(1)}, u32[]{:S(2)}, u32[]{:S(2)}) collective-permute-start(bf16[32,1344]{1,0:T(8,128)(2,1)S(1)} %get-tuple-element.64), channel_id=1, source_target_pairs={{0,4},{1,13},{2,6},{3,15},{4,0},{5,9},{6,2},{7,11},{8,12},{9,5},{1... | collective-permute-start | bytes 258056 | tf_op jit(solution)/shard_map/ppermute | solution.py:373
  23.1 5.7 %collective-permute-start.9 = (bf16[32,1344]{1,0:T(8,128)(2,1)S(1)}, bf16[32,1344]{1,0:T(8,128)(2,1)S(1)}, u32[]{:S(2)}, u32[]{:S(2)}) collective-permute-start(bf16[32,1344]{1,0:T(8,128)(2,1)S(1)} %relay.1), channel_id=1, source_target_pairs={{0,8},{1,5},{2,10},{3,7},{4,12},{5,1},{6,14},{7,3},{8,0},{9,13},{1... | collective-permute-start | bytes 258056 | tf_op jit(solution)/shard_map/ppermute | solution.py:373
  29.0 5.6 %collective-permute-start.13 = (bf16[32,1408]{1,0:T(8,128)(2,1)S(1)}, bf16[32,1408]{1,0:T(8,128)(2,1)S(1)}, u32[]{:S(2)}, u32[]{:S(2)}) collective-permute-start(bf16[32,1408]{1,0:T(8,128)(2,1)S(1)} %get-tuple-element.68.rest_0_), channel_id=1, source_target_pairs={{0,8},{4,12},{8,0},{12,4},{1,9},{5,13},{9,1},{13,5},{2,10},{6,14},... | collective-permute-start | bytes 270344 | tf_op jit(solution)/shard_map/ppermute | solution.py:363
  30.5 7.9 %collective-permute-start.12 = (bf16[32,1408]{1,0:T(8,128)(2,1)S(1)}, bf16[32,1408]{1,0:T(8,128)(2,1)S(1)}, u32[]{:S(2)}, u32[]{:S(2)}) collective-permute-start(bf16[32,1408]{1,0:T(8,128)(2,1)S(1)} %get-tuple-element.68.rest_0_), channel_id=1, source_target_pairs={{0,6},{1,7},{2,4},{3,5},{4,2},{5,3},{6,0},{7,1},{8,14},{9,15},{10,... | collective-permute-start | bytes 270344 | tf_op jit(solution)/shard_map/ppermute | solution.py:363
  33.8 5.6 %collective-permute-start.11 = (bf16[32,1408]{1,0:T(8,128)(2,1)S(1)}, bf16[32,1408]{1,0:T(8,128)(2,1)S(1)}, u32[]{:S(2)}, u32[]{:S(2)}) collective-permute-start(bf16[32,1408]{1,0:T(8,128)(2,1)S(1)} %get-tuple-element.68.rest_0_), channel_id=1, source_target_pairs={{0,4},{1,5},{2,6},{3,7},{4,0},{5,1},{6,2},{7,3},{8,12},{9,13},{10,... | collective-permute-start | bytes 270344 | tf_op jit(solution)/shard_map/ppermute | solution.py:363
  33.8 7.1 %collective-permute-start.10 = (bf16[32,1408]{1,0:T(8,128)(2,1)S(1)}, bf16[32,1408]{1,0:T(8,128)(2,1)S(1)}, u32[]{:S(2)}, u32[]{:S(2)}) collective-permute-start(bf16[32,1408]{1,0:T(8,128)(2,1)S(1)} %get-tuple-element.68.rest_0_), channel_id=1, source_target_pairs={{0,2},{1,3},{2,0},{3,1},{4,6},{5,7},{6,4},{7,5},{8,10},{9,11},{10,... | collective-permute-start | bytes 270344 | tf_op jit(solution)/shard_map/ppermute | solution.py:363
  34.6 9.1 %collective-permute-start.16 = (bf16[32,1408]{1,0:T(8,128)(2,1)S(1)}, bf16[32,1408]{1,0:T(8,128)(2,1)S(1)}, u32[]{:S(2)}, u32[]{:S(2)}) collective-permute-start(bf16[32,1408]{1,0:T(8,128)(2,1)S(1)} %collective-permute-done.13.rest_0_), channel_id=1, source_target_pairs={{0,6},{1,7},{2,4},{3,5},{4,2},{5,3},{6,0},{7,1},{8,14},{9,15},{10,... | collective-permute-start | bytes 270344 | tf_op jit(solution)/shard_map/ppermute | solution.py:363
  37.3 6.3 %collective-permute-start.15 = (bf16[32,1408]{1,0:T(8,128)(2,1)S(1)}, bf16[32,1408]{1,0:T(8,128)(2,1)S(1)}, u32[]{:S(2)}, u32[]{:S(2)}) collective-permute-start(bf16[32,1408]{1,0:T(8,128)(2,1)S(1)} %collective-permute-done.13.rest_0_), channel_id=1, source_target_pairs={{0,4},{1,5},{2,6},{3,7},{4,0},{5,1},{6,2},{7,3},{8,12},{9,13},{10,... | collective-permute-start | bytes 270344 | tf_op jit(solution)/shard_map/ppermute | solution.py:363
  38.4 5.2 %collective-permute-start.14 = (bf16[32,1408]{1,0:T(8,128)(2,1)S(1)}, bf16[32,1408]{1,0:T(8,128)(2,1)S(1)}, u32[]{:S(2)}, u32[]{:S(2)}) collective-permute-start(bf16[32,1408]{1,0:T(8,128)(2,1)S(1)} %collective-permute-done.13.rest_0_), channel_id=1, source_target_pairs={{0,2},{1,3},{2,0},{3,1},{4,6},{5,7},{6,4},{7,5},{8,10},{9,11},{10,... | collective-permute-start | bytes 270344 | tf_op jit(solution)/shard_map/ppermute | solution.py:363
  46.4 7.7 %collective-permute-start.17 = (bf16[64,1344]{1,0:T(8,128)(2,1)S(1)}, bf16[64,1344]{1,0:T(8,128)(2,1)S(1)}, u32[]{:S(2)}, u32[]{:S(2)}) collective-permute-start(bf16[64,1344]{1,0:T(8,128)(2,1)S(1)} %get-tuple-element.80), channel_id=1, source_target_pairs={{0,6},{1,7},{2,4},{3,5},{4,2},{5,3},{6,0},{7,1},{8,14},{9,15},{10,... | collective-permute-start | bytes 516104 | tf_op jit(solution)/shard_map/ppermute | solution.py:363
  47.6 6.6 %collective-permute-start.18 = (bf16[64,1344]{1,0:T(8,128)(2,1)S(1)}, bf16[64,1344]{1,0:T(8,128)(2,1)S(1)}, u32[]{:S(2)}, u32[]{:S(2)}) collective-permute-start(bf16[64,1344]{1,0:T(8,128)(2,1)S(1)} %get-tuple-element.81), channel_id=1, source_target_pairs={{0,4},{1,5},{2,6},{3,7},{4,0},{5,1},{6,2},{7,3},{8,12},{9,13},{10,... | collective-permute-start | bytes 516104 | tf_op jit(solution)/shard_map/ppermute | solution.py:363
  47.8 6.3 %collective-permute-start.19 = (bf16[32,1344]{1,0:T(8,128)(2,1)S(1)}, bf16[32,1344]{1,0:T(8,128)(2,1)S(1)}, u32[]{:S(2)}, u32[]{:S(2)}) collective-permute-start(bf16[32,1344]{1,0:T(8,128)(2,1)S(1)} %get-tuple-element.83), channel_id=1, source_target_pairs={{0,2},{1,3},{2,0},{3,1},{4,6},{5,7},{6,4},{7,5},{8,10},{9,11},{10,... | collective-permute-start | bytes 258056 | tf_op jit(solution)/shard_map/ppermute | solution.py:363
  54.2 5.5 %collective-permute-start.20 = (bf16[32,1344]{1,0:T(8,128)(2,1)S(1)}, bf16[32,1344]{1,0:T(8,128)(2,1)S(1)}, u32[]{:S(2)}, u32[]{:S(2)}) collective-permute-start(bf16[32,1344]{1,0:T(8,128)(2,1)S(1)} %sum.1), channel_id=1, source_target_pairs={{0,8},{4,12},{8,0},{12,4},{1,9},{5,13},{9,1},{13,5},{2,10},{6,14},... | collective-permute-start | bytes 258056 | tf_op jit(solution)/shard_map/ppermute | solution.py:363
  55.2 4.6 %collective-permute-start.21 = (bf16[32,1344]{1,0:T(8,128)(2,1)S(1)}, bf16[32,1344]{1,0:T(8,128)(2,1)S(1)}, u32[]{:S(2)}, u32[]{:S(2)}) collective-permute-start(bf16[32,1344]{1,0:T(8,128)(2,1)S(1)} %get-tuple-element.86), channel_id=1, source_target_pairs={{0,2},{1,3},{2,0},{3,1},{4,6},{5,7},{6,4},{7,5},{8,10},{9,11},{10,... | collective-permute-start | bytes 258056 | tf_op jit(solution)/shard_map/ppermute | solution.py:363

commit v21 on v20

--- a/solution.py
+++ b/solution.py
@@ -510,18 +510,15 @@
     sets = [spread(swap(own_rows, "head", high)) for high in range(2, head_size, 2)]
     near = through_experts(spread(own_rows))
     near, sets = lax.optimization_barrier((near, sets))
-    joined = [at for at, mask in enumerate(group, 1) if mask >= exp_size]
-    arrived, later = [], [at for at in range(1, len(near)) if at not in joined]
-    apart = [near[at] for at in later]
+    joined = list(range(1, len(near)))
+    arrived = []
     for high, members in zip(range(2, head_size, 2), sets):
         pieces = through_experts(members, [(at, near[at]) for at in joined] if high == 2 else ())
         got = [swap(piece, both, mask) for piece, mask in zip(pieces[:0:-1], group[::-1])]
         total = call(sum_kernel, "sum", struct((rows, model), BF16), [(VMEM, v) for v in (pieces[0], *got)])
         if high == 2:
-            total, apart = lax.optimization_barrier((total, apart))
-            arrived += [part for part, mask in zip(got, group[::-1]) if mask >= exp_size]
+            arrived += got
         arrived.append(swap(total, "head", high))
-    arrived += [swap(piece, both, group[at - 1]) for piece, at in zip(apart, later)]
     return call(
         last_kernel,
         "last",

time: 60.8 us -> 61.8 us (1.016)
  starting transfers between devices: 25.1 us -> 26.9 us
  waiting for transfers between devices: 17.1 us -> 16.4 us
    ppermute x19 -> x18, starting transfers between devices: 21.3 us -> 22.8 us  [swap(): return lax.ppermute(value, axis, [(i, i ^ mask) for i in range(size)])]
    ppermute x19 -> x18, waiting for transfers between devices: 12.2 us -> 11.9 us  [swap(): return lax.ppermute(value, axis, [(i, i ^ mask) for i in range(size)])]
  transfers between devices with their start and end apart: 22 -> 21, of which waited for: 10 -> 10; matrix products, arithmetic and copies ran while one was open for 0% -> 0% of each run, Pallas kernels for 19% -> 19%
where the time goes in v21:
time: 61.8 us; the launch traced here: 61.5 us
  starting transfers between devices  26.9 us (44%)
  Pallas kernels  18.1 us (29%)
  waiting for transfers between devices  16.4 us (27%)
    ppermute x18, starting transfers between devices, swap(): return lax.ppermute(value, axis, [(i, i ^ mask) for i in range(size)])  22.8 us
    pallas_call x15, Pallas kernels, call(): pl.pallas_call(kernel, out_shape=jax.tree.map(lambda out: pltpu.VMEM(out....  18.1 us
    ppermute x18, waiting for transfers between devices, swap(): return lax.ppermute(value, axis, [(i, i ^ mask) for i in range(size)])  11.9 us
    ppermute x3, waiting for transfers between devices, swap_slot(): return lax.ppermute(value, ('head', 'exp'), pairs)  4.45 us
    ppermute x3, starting transfers between devices, swap_slot(): return lax.ppermute(value, ('head', 'exp'), pairs)  4.04 us
  transfers between devices with their start and end apart: 21, of which 10 were waited for; matrix products, arithmetic and copies ran while one was open for 0% of the time, Pallas kernels for 19%

profile of v21, /device:TPU:0, one launch (start us, length us, event | category | flops | bytes accessed | tf_op | source)
XLA Modules:
  0.0 61.5 jit_solution(2444325668741595523)
XLA Ops:
  0.0 1.8 %state.1 = (bf16[528,128]{1,0:T(8,128)(2,1)S(1)}, bf16[528,128]{1,0:T(8,128)(2,1)S(1)}) custom-call(bf16[128,1024]{1,0:T(8,128)(2,1)} %x_hbm.3, bf16[128,256]{1,0:T(8,128)(2,1)} %b_hbm.3, f32[16,128]{1,0:T(8,128)} %bitcast.11, f32[1,16]{1,0:T(1,128)} %bitcast.16), custom_call_target="tpu_custom_call" | custom-call | tf_op jit(solution)/shard_map/state/pallas_call | solution.py:29
  1.8 0.5 collective-permute-start
  2.4 1.0 %prep.1 = (bf16[32,128]{1,0:T(8,128)(2,1)S(1)}, bf16[1,32,1344]{2,1,0:T(8,128)(2,1)S(1)}, f32[1,1344]{1,0:T(1,128)S(1)}) custom-call(bf16[528,128]{1,0:T(8,128)(2,1)S(1)} %get-tuple-element.44.after_ref.keep_ref, bf16[1,32,1344]{2,1,0:T(8,128)(2,1)} %resid_hbm.1, s32[6,1,32]{2,1,0:T(1,128)} %bitcast.14, f32[6,1,32]{2,1,0:T(1,128)} %bitcast.15, f32[1344]{0:T(1024)} %gain_hbm.1), custom_call_target="tpu_custom_call" | custom-call | tf_op jit(solution)/shard_map/prep/pallas_call | solution.py:29
  3.3 0.0 collective-permute-done.got_ref
  3.3 0.1 chip_state.1.rest_0_
  3.4 0.4 collective-permute-start.1
  3.9 0.1 collective-permute-start.2
  4.0 2.9 %collective-permute-start.3 = (bf16[528,128]{1,0:T(8,128)(2,1)S(1)}, bf16[528,128]{1,0:T(8,128)(2,1)S(1)}, u32[]{:S(2)}, u32[]{:S(2)}) collective-permute-start(bf16[528,128]{1,0:T(8,128)(2,1)S(1)} %chip_state.1.rest_0_), channel_id=1, source_target_pairs={{0,2},{1,3},{2,0},{3,1},{16,18},{17,19},{18,16},{19,17},{4,6},{5,7... | collective-permute-start | bytes 405512 | tf_op jit(solution)/shard_map/ppermute | solution.py:363
  6.9 1.5 %collective-permute-start.4 = (bf16[528,128]{1,0:T(8,128)(2,1)S(1)}, bf16[528,128]{1,0:T(8,128)(2,1)S(1)}, u32[]{:S(2)}, u32[]{:S(2)}) collective-permute-start(bf16[528,128]{1,0:T(8,128)(2,1)S(1)} %chip_state.1.rest_0_), channel_id=1, source_target_pairs={{0,16},{1,17},{2,18},{3,19},{16,0},{17,1},{18,2},{19,3},{4,20},{5,... | collective-permute-start | bytes 405512 | tf_op jit(solution)/shard_map/ppermute | solution.py:363
  8.4 1.8 %projection.1 = (f32[1,1024]{1,0:T(1,128)S(1)}, bf16[1344,1024]{1,0:T(8,128)(2,1)S(1)}) custom-call(f32[1,1024]{1,0:T(1,128)} %bitcast.13, bf16[1344,1024]{1,0:T(8,128)(2,1)} %bitcast.8), custom_call_target="tpu_custom_call" | custom-call | tf_op jit(solution)/shard_map/projection/pallas_call | solution.py:29
  10.2 2.4 %inside.1 = (f32[128,1024]{1,0:T(8,128)S(1)}, f32[128,1024]{1,0:T(8,128)S(1)}, bf16[128,256]{1,0:T(8,128)(2,1)S(1)}) custom-call(bf16[128,1024]{1,0:T(8,128)(2,1)} %x_hbm.3, bf16[128,1024]{1,0:T(8,128)(2,1)} %z_hbm.1, bf16[128,256]{1,0:T(8,128)(2,1)} %b_hbm.3, bf16[128,256]{1,0:T(8,128)(2,1)} %c_hbm.1, f32[16,128]{1,0:T(8,128)} %bitcast.12, ...), custom_call_target="tpu_custom_call" | custom-call | tf_op jit(solution)/shard_map/inside/pallas_call | solution.py:29
  12.7 0.7 %collective-permute-done.4.rest_2_ = bf16[528,128]{1,0:T(8,128)(2,1)S(1)} collective-permute-done((bf16[528,128]{1,0:T(8,128)(2,1)S(1)}, bf16[528,128]{1,0:T(8,128)(2,1)S(1)}, u32[]{:S(2)}, u32[]{:S(2)}) %collective-permute-start.4) | collective-permute-done | bytes 135200 | tf_op jit(solution)/shard_map/ppermute | solution.py:363
  13.4 1.5 %collective-permute-done.5.rest_3_ = bf16[528,128]{1,0:T(8,128)(2,1)S(1)} collective-permute-done((bf16[528,128]{1,0:T(8,128)(2,1)S(1)}, bf16[528,128]{1,0:T(8,128)(2,1)S(1)}, u32[]{:S(2)}, u32[]{:S(2)}) %collective-permute-start.5) | collective-permute-done | bytes 135200 | tf_op jit(solution)/shard_map/ppermute | solution.py:363
  14.9 0.3 before.1
  15.2 0.1 collective-permute-start.6
  15.3 0.8 %first_half.1.first_ref = f32[128,1344]{1,0:T(8,128)S(1)} custom-call(f32[128,1024]{1,0:T(8,128)S(1)} %get-tuple-element.49.local_ref, f32[128,1024]{1,0:T(8,128)S(1)} %get-tuple-element.50.grown_ref, bf16[128,256]{1,0:T(8,128)(2,1)S(1)} %get-tuple-element.51.after_b.c_ref, f32[1,1024]{1,0:T(1,128)S(1)} %get-tuple-element.52.after_a.norm_ref, ...), custom_call_target="tpu_custom_call" | custom-call | tf_op jit(solution)/shard_map/first_half/pallas_call | solution.py:29
  16.1 0.5 collective-permute-done.6.got_ref
  16.6 0.0 collective-permute-done.1.after_up.other_up_ref
  16.6 0.0 collective-permute-done.2.after_down.other_down_ref
  16.6 0.9 %mixed.1 = (bf16[32,1344]{1,0:T(8,128)(2,1)S(1)}, bf16[32,1344]{1,0:T(8,128)(2,1)S(1)}, bf16[32,1344]{1,0:T(8,128)(2,1)S(1)}, bf16[32,1344]{1,0:T(8,128)(2,1)S(1)}) custom-call(bf16[1,928,1344]{2,1,0:T(8,128)(2,1)S(1)} %collective-permute-done.1.after_up.other_up_ref, bf16[1,928,1344]{2,1,0:T(8,128)(2,1)S(1)} %collective-permute-done.2.after_down.other_down_ref, ...), custom_call_target="tpu_custom_call" | custom-call | tf_op jit(solution)/shard_map/mixed/pallas_call | solution.py:29
  17.5 1.9 %collective-permute-start.7 = (bf16[32,1344]{1,0:T(8,128)(2,1)S(1)}, bf16[32,1344]{1,0:T(8,128)(2,1)S(1)}, u32[]{:S(2)}, u32[]{:S(2)}) collective-permute-start(bf16[32,1344]{1,0:T(8,128)(2,1)S(1)} %get-tuple-element.61), channel_id=1, source_target_pairs={{0,4},{1,9},{2,6},{3,11},{4,0},{5,13},{6,2},{7,15},{8,12},{9,1},{1... | collective-permute-start | bytes 258056 | tf_op jit(solution)/shard_map/ppermute | solution.py:373
  19.3 0.2 collective-permute-start.8
  19.6 3.5 %collective-permute-done.7.got_ref.rest_1_ = bf16[32,1344]{1,0:T(8,128)(2,1)S(1)} collective-permute-done((bf16[32,1344]{1,0:T(8,128)(2,1)S(1)}, bf16[32,1344]{1,0:T(8,128)(2,1)S(1)}, u32[]{:S(2)}, u32[]{:S(2)}) %collective-permute-start.7) | collective-permute-done | bytes 86048 | tf_op jit(solution)/shard_map/ppermute | solution.py:373
  23.1 2.0 %collective-permute-start.9 = (bf16[32,1344]{1,0:T(8,128)(2,1)S(1)}, bf16[32,1344]{1,0:T(8,128)(2,1)S(1)}, u32[]{:S(2)}, u32[]{:S(2)}) collective-permute-start(bf16[32,1344]{1,0:T(8,128)(2,1)S(1)} %relay.1), channel_id=1, source_target_pairs={{0,8},{1,5},{2,10},{3,7},{4,12},{5,1},{6,14},{7,3},{8,0},{9,13},{1... | collective-permute-start | bytes 258056 | tf_op jit(solution)/shard_map/ppermute | solution.py:373
  25.0 2.5 %weights.1 = (bf16[1,928,1344]{2,1,0:T(8,128)(2,1)S(1)}, bf16[1,928,1344]{2,1,0:T(8,128)(2,1)S(1)}) custom-call(bf16[32,1344]{1,0:T(8,128)(2,1)S(1)} %get-tuple-element.57.after_ref.rest_0_, bf16[1,928,1344]{2,1,0:T(8,128)(2,1)} %bitcast.10, bf16[1,928,1344]{2,1,0:T(8,128)(2,1)} %down_hbm.1), custom_call_target="tpu_custom_call" | custom-call | tf_op jit(solution)/shard_map/weights/pallas_call | solution.py:29
  27.6 0.0 collective-permute-done.8.rest_2_
  27.6 1.0 %collective-permute-done.9.rest_3_ = bf16[32,1344]{1,0:T(8,128)(2,1)S(1)} collective-permute-done((bf16[32,1344]{1,0:T(8,128)(2,1)S(1)}, bf16[32,1344]{1,0:T(8,128)(2,1)S(1)}, u32[]{:S(2)}, u32[]{:S(2)}) %collective-permute-start.9) | collective-permute-done | bytes 86048 | tf_op jit(solution)/shard_map/ppermute | solution.py:373
  28.6 0.2 rows.1
  28.8 2.0 %collective-permute-start.13 = (bf16[32,1408]{1,0:T(8,128)(2,1)S(1)}, bf16[32,1408]{1,0:T(8,128)(2,1)S(1)}, u32[]{:S(2)}, u32[]{:S(2)}) collective-permute-start(bf16[32,1408]{1,0:T(8,128)(2,1)S(1)} %get-tuple-element.66.rest_0_), channel_id=1, source_target_pairs={{0,8},{4,12},{8,0},{12,4},{1,9},{5,13},{9,1},{13,5},{2,10},{6,14},... | collective-permute-start | bytes 270344 | tf_op jit(solution)/shard_map/ppermute | solution.py:363
  30.7 1.5 %collective-permute-start.10 = (bf16[32,1408]{1,0:T(8,128)(2,1)S(1)}, bf16[32,1408]{1,0:T(8,128)(2,1)S(1)}, u32[]{:S(2)}, u32[]{:S(2)}) collective-permute-start(bf16[32,1408]{1,0:T(8,128)(2,1)S(1)} %get-tuple-element.66.rest_0_), channel_id=1, source_target_pairs={{0,2},{1,3},{2,0},{3,1},{4,6},{5,7},{6,4},{7,5},{8,10},{9,11},{10,... | collective-permute-start | bytes 270344 | tf_op jit(solution)/shard_map/ppermute | solution.py:363
  32.2 2.4 %collective-permute-start.11 = (bf16[32,1408]{1,0:T(8,128)(2,1)S(1)}, bf16[32,1408]{1,0:T(8,128)(2,1)S(1)}, u32[]{:S(2)}, u32[]{:S(2)}) collective-permute-start(bf16[32,1408]{1,0:T(8,128)(2,1)S(1)} %get-tuple-element.66.rest_0_), channel_id=1, source_target_pairs={{0,4},{1,5},{2,6},{3,7},{4,0},{5,1},{6,2},{7,3},{8,12},{9,13},{10,... | collective-permute-start | bytes 270344 | tf_op jit(solution)/shard_map/ppermute | solution.py:363
  34.7 0.0 collective-permute-start.12
  34.7 0.0 collective-permute-done.13.rest_0_
  34.7 1.7 %collective-permute-start.14 = (bf16[32,1408]{1,0:T(8,128)(2,1)S(1)}, bf16[32,1408]{1,0:T(8,128)(2,1)S(1)}, u32[]{:S(2)}, u32[]{:S(2)}) collective-permute-start(bf16[32,1408]{1,0:T(8,128)(2,1)S(1)} %collective-permute-done.13.rest_0_), channel_id=1, source_target_pairs={{0,2},{1,3},{2,0},{3,1},{4,6},{5,7},{6,4},{7,5},{8,10},{9,11},{10,... | collective-permute-start | bytes 270344 | tf_op jit(solution)/shard_map/ppermute | solution.py:363
  36.4 1.8 %collective-permute-start.15 = (bf16[32,1408]{1,0:T(8,128)(2,1)S(1)}, bf16[32,1408]{1,0:T(8,128)(2,1)S(1)}, u32[]{:S(2)}, u32[]{:S(2)}) collective-permute-start(bf16[32,1408]{1,0:T(8,128)(2,1)S(1)} %collective-permute-done.13.rest_0_), channel_id=1, source_target_pairs={{0,4},{1,5},{2,6},{3,7},{4,0},{5,1},{6,2},{7,3},{8,12},{9,13},{10,... | collective-permute-start | bytes 270344 | tf_op jit(solution)/shard_map/ppermute | solution.py:363
  38.2 2.4 %collective-permute-start.16 = (bf16[32,1408]{1,0:T(8,128)(2,1)S(1)}, bf16[32,1408]{1,0:T(8,128)(2,1)S(1)}, u32[]{:S(2)}, u32[]{:S(2)}) collective-permute-start(bf16[32,1408]{1,0:T(8,128)(2,1)S(1)} %collective-permute-done.13.rest_0_), channel_id=1, source_target_pairs={{0,6},{1,7},{2,4},{3,5},{4,2},{5,3},{6,0},{7,1},{8,14},{9,15},{10,... | collective-permute-start | bytes 270344 | tf_op jit(solution)/shard_map/ppermute | solution.py:363
  40.5 0.1 collective-permute-done.12.rest_3_
  40.7 2.7 %experts.2 = (bf16[32,1344]{1,0:T(8,128)(2,1)S(1)}, bf16[32,1344]{1,0:T(8,128)(2,1)S(1)}, bf16[32,1344]{1,0:T(8,128)(2,1)S(1)}, bf16[32,1344]{1,0:T(8,128)(2,1)S(1)}) custom-call(bf16[1,928,1344]{2,1,0:T(8,128)(2,1)S(1)} %get-tuple-element.58.after_ref.up_ref, bf16[1,928,1344]{2,1,0:T(8,128)(2,1)S(1)} %get-tuple-element.65.down_ref, ...), custom_call_target="tpu_custom_call" | custom-call | tf_op jit(solution)/shard_map/experts/pallas_call | solution.py:29
  43.4 0.2 collective-permute-done.16.rest_3_
  43.6 2.7 %experts.3 = (bf16[32,1344]{1,0:T(8,128)(2,1)S(1)}, bf16[64,1344]{1,0:T(8,128)(2,1)S(1)}, bf16[64,1344]{1,0:T(8,128)(2,1)S(1)}, bf16[64,1344]{1,0:T(8,128)(2,1)S(1)}) custom-call(bf16[1,928,1344]{2,1,0:T(8,128)(2,1)S(1)} %get-tuple-element.58.after_ref.up_ref, bf16[1,928,1344]{2,1,0:T(8,128)(2,1)S(1)} %get-tuple-element.65.down_ref, ...), custom_call_target="tpu_custom_call" | custom-call | tf_op jit(solution)/shard_map/experts/pallas_call | solution.py:29
  46.3 2.4 %collective-permute-start.17 = (bf16[64,1344]{1,0:T(8,128)(2,1)S(1)}, bf16[64,1344]{1,0:T(8,128)(2,1)S(1)}, u32[]{:S(2)}, u32[]{:S(2)}) collective-permute-start(bf16[64,1344]{1,0:T(8,128)(2,1)S(1)} %get-tuple-element.79), channel_id=1, source_target_pairs={{0,6},{1,7},{2,4},{3,5},{4,2},{5,3},{6,0},{7,1},{8,14},{9,15},{10,... | collective-permute-start | bytes 516104 | tf_op jit(solution)/shard_map/ppermute | solution.py:363
  48.8 1.1 %collective-permute-start.19 = (bf16[64,1344]{1,0:T(8,128)(2,1)S(1)}, bf16[64,1344]{1,0:T(8,128)(2,1)S(1)}, u32[]{:S(2)}, u32[]{:S(2)}) collective-permute-start(bf16[64,1344]{1,0:T(8,128)(2,1)S(1)} %get-tuple-element.81), channel_id=1, source_target_pairs={{0,2},{1,3},{2,0},{3,1},{4,6},{5,7},{6,4},{7,5},{8,10},{9,11},{10,... | collective-permute-start | bytes 516104 | tf_op jit(solution)/shard_map/ppermute | solution.py:363
  49.9 3.0 %collective-permute-done.17.refs_1_.rest_1_ = bf16[64,1344]{1,0:T(8,128)(2,1)S(1)} collective-permute-done((bf16[64,1344]{1,0:T(8,128)(2,1)S(1)}, bf16[64,1344]{1,0:T(8,128)(2,1)S(1)}, u32[]{:S(2)}, u32[]{:S(2)}) %collective-permute-start.17) | collective-permute-done | bytes 172064 | tf_op jit(solution)/shard_map/ppermute | solution.py:363
  52.8 2.4 %collective-permute-done.18.refs_2_.rest_2_ = bf16[64,1344]{1,0:T(8,128)(2,1)S(1)} collective-permute-done((bf16[64,1344]{1,0:T(8,128)(2,1)S(1)}, bf16[64,1344]{1,0:T(8,128)(2,1)S(1)}, u32[]{:S(2)}, u32[]{:S(2)}) %collective-permute-start.18) | collective-permute-done | bytes 172064 | tf_op jit(solution)/shard_map/ppermute | solution.py:363
  55.2 0.1 sum.1
  55.3 2.0 %collective-permute-start.20 = (bf16[32,1344]{1,0:T(8,128)(2,1)S(1)}, bf16[32,1344]{1,0:T(8,128)(2,1)S(1)}, u32[]{:S(2)}, u32[]{:S(2)}) collective-permute-start(bf16[32,1344]{1,0:T(8,128)(2,1)S(1)} %sum.1), channel_id=1, source_target_pairs={{0,8},{4,12},{8,0},{12,4},{1,9},{5,13},{9,1},{13,5},{2,10},{6,14},... | collective-permute-start | bytes 258056 | tf_op jit(solution)/shard_map/ppermute | solution.py:363
  57.2 3.5 %collective-permute-done.20.rest_4_ = bf16[32,1344]{1,0:T(8,128)(2,1)S(1)} collective-permute-done((bf16[32,1344]{1,0:T(8,128)(2,1)S(1)}, bf16[32,1344]{1,0:T(8,128)(2,1)S(1)}, u32[]{:S(2)}, u32[]{:S(2)}) %collective-permute-start.20) | collective-permute-done | bytes 86048 | tf_op jit(solution)/shard_map/ppermute | solution.py:363
  60.8 0.7 %last.1 = bf16[1,32,1344]{2,1,0:T(8,128)(2,1)} custom-call(bf16[32,1344]{1,0:T(8,128)(2,1)S(1)} %get-tuple-element.64.hidden_ref, bf16[32,1344]{1,0:T(8,128)(2,1)S(1)} %get-tuple-element.71.rest_0_, bf16[64,1344]{1,0:T(8,128)(2,1)S(1)} %collective-permute-done.17.refs_1_.rest_1_, bf16[64,1344]{1,0:T(8,128)(2,1)S(1)} %collective-permute-done.18.refs_2_.rest_2_, ...), custom_call_target="tpu_custom_call" | custom-call | tf_op jit(solution)/shard_map/last/pallas_call | solution.py:29
  (9 shorter events, 0.1 us)
Async XLA Ops:
  1.8 1.5 %collective-permute-start = (bf16[528,128]{1,0:T(8,128)(2,1)S(1)}, bf16[528,128]{1,0:T(8,128)(2,1)S(1)}, u32[]{:S(2)}, u32[]{:S(2)}) collective-permute-start(bf16[528,128]{1,0:T(8,128)(2,1)S(1)} %get-tuple-element.46), channel_id=1, source_target_pairs={{0,1},{1,0},{2,3},{3,2},{4,5},{5,4},{6,7},{7,6},{8,9},{9,8},{10,11... | collective-permute-start | bytes 405512 | tf_op jit(solution)/shard_map/ppermute | solution.py:363
  3.4 13.2 %collective-permute-start.1 = (bf16[1,928,1344]{2,1,0:T(8,128)(2,1)}, bf16[1,928,1344]{2,1,0:T(8,128)(2,1)S(1)}, u32[]{:S(2)}, u32[]{:S(2)}) collective-permute-start(bf16[1,928,1344]{2,1,0:T(8,128)(2,1)} %bitcast.9), channel_id=1, source_target_pairs={{0,1},{1,0},{2,3},{3,2},{4,5},{5,4},{6,7},{7,6},{8,9},{9,8},{10,11... | collective-permute-start | bytes 7483400 | tf_op jit(solution)/shard_map/ppermute | solution.py:363
  3.9 12.7 %collective-permute-start.2 = (bf16[1,928,1344]{2,1,0:T(8,128)(2,1)}, bf16[1,928,1344]{2,1,0:T(8,128)(2,1)S(1)}, u32[]{:S(2)}, u32[]{:S(2)}) collective-permute-start(bf16[1,928,1344]{2,1,0:T(8,128)(2,1)} %down_hbm.1), channel_id=1, source_target_pairs={{0,1},{1,0},{2,3},{3,2},{4,5},{5,4},{6,7},{7,6},{8,9},{9,8},{10,11... | collective-permute-start | bytes 7483400 | tf_op jit(solution)/shard_map/ppermute | solution.py:363
  4.0 8.6 %collective-permute-start.3 = (bf16[528,128]{1,0:T(8,128)(2,1)S(1)}, bf16[528,128]{1,0:T(8,128)(2,1)S(1)}, u32[]{:S(2)}, u32[]{:S(2)}) collective-permute-start(bf16[528,128]{1,0:T(8,128)(2,1)S(1)} %chip_state.1.rest_0_), channel_id=1, source_target_pairs={{0,2},{1,3},{2,0},{3,1},{16,18},{17,19},{18,16},{19,17},{4,6},{5,7... | collective-permute-start | bytes 405512 | tf_op jit(solution)/shard_map/ppermute | solution.py:363
  6.9 6.5 %collective-permute-start.4 = (bf16[528,128]{1,0:T(8,128)(2,1)S(1)}, bf16[528,128]{1,0:T(8,128)(2,1)S(1)}, u32[]{:S(2)}, u32[]{:S(2)}) collective-permute-start(bf16[528,128]{1,0:T(8,128)(2,1)S(1)} %chip_state.1.rest_0_), channel_id=1, source_target_pairs={{0,16},{1,17},{2,18},{3,19},{16,0},{17,1},{18,2},{19,3},{4,20},{5,... | collective-permute-start | bytes 405512 | tf_op jit(solution)/shard_map/ppermute | solution.py:363
  8.4 6.5 %collective-permute-start.5 = (bf16[528,128]{1,0:T(8,128)(2,1)S(1)}, bf16[528,128]{1,0:T(8,128)(2,1)S(1)}, u32[]{:S(2)}, u32[]{:S(2)}) collective-permute-start(bf16[528,128]{1,0:T(8,128)(2,1)S(1)} %chip_state.1.rest_0_), channel_id=1, source_target_pairs={{0,18},{1,19},{2,16},{3,17},{16,2},{17,3},{18,0},{19,1},{4,22},{5,... | collective-permute-start | bytes 405512 | tf_op jit(solution)/shard_map/ppermute | solution.py:363
  15.2 1.4 %collective-permute-start.6 = (bf16[4,128,128]{2,1,0:T(8,128)(2,1)S(1)}, bf16[4,128,128]{2,1,0:T(8,128)(2,1)S(1)}, u32[]{:S(2)}, u32[]{:S(2)}) collective-permute-start(bf16[4,128,128]{2,1,0:T(8,128)(2,1)S(1)} %get-tuple-element.55), channel_id=1, source_target_pairs={{0,1},{1,0},{2,3},{3,2},{4,5},{5,4},{6,7},{7,6},{8,9},{9,8},{10,11... | collective-permute-start | bytes 393224 | tf_op jit(solution)/shard_map/ppermute | solution.py:363
  17.5 5.6 %collective-permute-start.7 = (bf16[32,1344]{1,0:T(8,128)(2,1)S(1)}, bf16[32,1344]{1,0:T(8,128)(2,1)S(1)}, u32[]{:S(2)}, u32[]{:S(2)}) collective-permute-start(bf16[32,1344]{1,0:T(8,128)(2,1)S(1)} %get-tuple-element.61), channel_id=1, source_target_pairs={{0,4},{1,9},{2,6},{3,11},{4,0},{5,13},{6,2},{7,15},{8,12},{9,1},{1... | collective-permute-start | bytes 258056 | tf_op jit(solution)/shard_map/ppermute | solution.py:373
  19.3 8.2 %collective-permute-start.8 = (bf16[32,1344]{1,0:T(8,128)(2,1)S(1)}, bf16[32,1344]{1,0:T(8,128)(2,1)S(1)}, u32[]{:S(2)}, u32[]{:S(2)}) collective-permute-start(bf16[32,1344]{1,0:T(8,128)(2,1)S(1)} %get-tuple-element.62), channel_id=1, source_target_pairs={{0,4},{1,13},{2,6},{3,15},{4,0},{5,9},{6,2},{7,11},{8,12},{9,5},{1... | collective-permute-start | bytes 258056 | tf_op jit(solution)/shard_map/ppermute | solution.py:373
  23.1 5.5 %collective-permute-start.9 = (bf16[32,1344]{1,0:T(8,128)(2,1)S(1)}, bf16[32,1344]{1,0:T(8,128)(2,1)S(1)}, u32[]{:S(2)}, u32[]{:S(2)}) collective-permute-start(bf16[32,1344]{1,0:T(8,128)(2,1)S(1)} %relay.1), channel_id=1, source_target_pairs={{0,8},{1,5},{2,10},{3,7},{4,12},{5,1},{6,14},{7,3},{8,0},{9,13},{1... | collective-permute-start | bytes 258056 | tf_op jit(solution)/shard_map/ppermute | solution.py:373
  28.8 5.9 %collective-permute-start.13 = (bf16[32,1408]{1,0:T(8,128)(2,1)S(1)}, bf16[32,1408]{1,0:T(8,128)(2,1)S(1)}, u32[]{:S(2)}, u32[]{:S(2)}) collective-permute-start(bf16[32,1408]{1,0:T(8,128)(2,1)S(1)} %get-tuple-element.66.rest_0_), channel_id=1, source_target_pairs={{0,8},{4,12},{8,0},{12,4},{1,9},{5,13},{9,1},{13,5},{2,10},{6,14},... | collective-permute-start | bytes 270344 | tf_op jit(solution)/shard_map/ppermute | solution.py:363
  30.7 7.5 %collective-permute-start.10 = (bf16[32,1408]{1,0:T(8,128)(2,1)S(1)}, bf16[32,1408]{1,0:T(8,128)(2,1)S(1)}, u32[]{:S(2)}, u32[]{:S(2)}) collective-permute-start(bf16[32,1408]{1,0:T(8,128)(2,1)S(1)} %get-tuple-element.66.rest_0_), channel_id=1, source_target_pairs={{0,2},{1,3},{2,0},{3,1},{4,6},{5,7},{6,4},{7,5},{8,10},{9,11},{10,... | collective-permute-start | bytes 270344 | tf_op jit(solution)/shard_map/ppermute | solution.py:363
  32.2 8.3 %collective-permute-start.11 = (bf16[32,1408]{1,0:T(8,128)(2,1)S(1)}, bf16[32,1408]{1,0:T(8,128)(2,1)S(1)}, u32[]{:S(2)}, u32[]{:S(2)}) collective-permute-start(bf16[32,1408]{1,0:T(8,128)(2,1)S(1)} %get-tuple-element.66.rest_0_), channel_id=1, source_target_pairs={{0,4},{1,5},{2,6},{3,7},{4,0},{5,1},{6,2},{7,3},{8,12},{9,13},{10,... | collective-permute-start | bytes 270344 | tf_op jit(solution)/shard_map/ppermute | solution.py:363
  34.7 6.0 %collective-permute-start.12 = (bf16[32,1408]{1,0:T(8,128)(2,1)S(1)}, bf16[32,1408]{1,0:T(8,128)(2,1)S(1)}, u32[]{:S(2)}, u32[]{:S(2)}) collective-permute-start(bf16[32,1408]{1,0:T(8,128)(2,1)S(1)} %get-tuple-element.66.rest_0_), channel_id=1, source_target_pairs={{0,6},{1,7},{2,4},{3,5},{4,2},{5,3},{6,0},{7,1},{8,14},{9,15},{10,... | collective-permute-start | bytes 270344 | tf_op jit(solution)/shard_map/ppermute | solution.py:363
  34.7 8.7 %collective-permute-start.14 = (bf16[32,1408]{1,0:T(8,128)(2,1)S(1)}, bf16[32,1408]{1,0:T(8,128)(2,1)S(1)}, u32[]{:S(2)}, u32[]{:S(2)}) collective-permute-start(bf16[32,1408]{1,0:T(8,128)(2,1)S(1)} %collective-permute-done.13.rest_0_), channel_id=1, source_target_pairs={{0,2},{1,3},{2,0},{3,1},{4,6},{5,7},{6,4},{7,5},{8,10},{9,11},{10,... | collective-permute-start | bytes 270344 | tf_op jit(solution)/shard_map/ppermute | solution.py:363
  36.4 7.0 %collective-permute-start.15 = (bf16[32,1408]{1,0:T(8,128)(2,1)S(1)}, bf16[32,1408]{1,0:T(8,128)(2,1)S(1)}, u32[]{:S(2)}, u32[]{:S(2)}) collective-permute-start(bf16[32,1408]{1,0:T(8,128)(2,1)S(1)} %collective-permute-done.13.rest_0_), channel_id=1, source_target_pairs={{0,4},{1,5},{2,6},{3,7},{4,0},{5,1},{6,2},{7,3},{8,12},{9,13},{10,... | collective-permute-start | bytes 270344 | tf_op jit(solution)/shard_map/ppermute | solution.py:363
  38.2 5.4 %collective-permute-start.16 = (bf16[32,1408]{1,0:T(8,128)(2,1)S(1)}, bf16[32,1408]{1,0:T(8,128)(2,1)S(1)}, u32[]{:S(2)}, u32[]{:S(2)}) collective-permute-start(bf16[32,1408]{1,0:T(8,128)(2,1)S(1)} %collective-permute-done.13.rest_0_), channel_id=1, source_target_pairs={{0,6},{1,7},{2,4},{3,5},{4,2},{5,3},{6,0},{7,1},{8,14},{9,15},{10,... | collective-permute-start | bytes 270344 | tf_op jit(solution)/shard_map/ppermute | solution.py:363
  46.3 6.5 %collective-permute-start.17 = (bf16[64,1344]{1,0:T(8,128)(2,1)S(1)}, bf16[64,1344]{1,0:T(8,128)(2,1)S(1)}, u32[]{:S(2)}, u32[]{:S(2)}) collective-permute-start(bf16[64,1344]{1,0:T(8,128)(2,1)S(1)} %get-tuple-element.79), channel_id=1, source_target_pairs={{0,6},{1,7},{2,4},{3,5},{4,2},{5,3},{6,0},{7,1},{8,14},{9,15},{10,... | collective-permute-start | bytes 516104 | tf_op jit(solution)/shard_map/ppermute | solution.py:363
  48.8 6.5 %collective-permute-start.18 = (bf16[64,1344]{1,0:T(8,128)(2,1)S(1)}, bf16[64,1344]{1,0:T(8,128)(2,1)S(1)}, u32[]{:S(2)}, u32[]{:S(2)}) collective-permute-start(bf16[64,1344]{1,0:T(8,128)(2,1)S(1)} %get-tuple-element.80), channel_id=1, source_target_pairs={{0,4},{1,5},{2,6},{3,7},{4,0},{5,1},{6,2},{7,3},{8,12},{9,13},{10,... | collective-permute-start | bytes 516104 | tf_op jit(solution)/shard_map/ppermute | solution.py:363
  48.8 6.5 %collective-permute-start.19 = (bf16[64,1344]{1,0:T(8,128)(2,1)S(1)}, bf16[64,1344]{1,0:T(8,128)(2,1)S(1)}, u32[]{:S(2)}, u32[]{:S(2)}) collective-permute-start(bf16[64,1344]{1,0:T(8,128)(2,1)S(1)} %get-tuple-element.81), channel_id=1, source_target_pairs={{0,2},{1,3},{2,0},{3,1},{4,6},{5,7},{6,4},{7,5},{8,10},{9,11},{10,... | collective-permute-start | bytes 516104 | tf_op jit(solution)/shard_map/ppermute | solution.py:363
  55.3 5.5 %collective-permute-start.20 = (bf16[32,1344]{1,0:T(8,128)(2,1)S(1)}, bf16[32,1344]{1,0:T(8,128)(2,1)S(1)}, u32[]{:S(2)}, u32[]{:S(2)}) collective-permute-start(bf16[32,1344]{1,0:T(8,128)(2,1)S(1)} %sum.1), channel_id=1, source_target_pairs={{0,8},{4,12},{8,0},{12,4},{1,9},{5,13},{9,1},{13,5},{2,10},{6,14},... | collective-permute-start | bytes 258056 | tf_op jit(solution)/shard_map/ppermute | solution.py:363

commit v22 on v20

--- a/solution.py
+++ b/solution.py
@@ -510,8 +510,8 @@
     sets = [spread(swap(own_rows, "head", high)) for high in range(2, head_size, 2)]
     near = through_experts(spread(own_rows))
     near, sets = lax.optimization_barrier((near, sets))
-    joined = [at for at, mask in enumerate(group, 1) if mask >= exp_size]
-    arrived, later = [], [at for at in range(1, len(near)) if at not in joined]
+    joined = [at for at, mask in enumerate(group, 1) if mask == exp_size]
+    arrived, later = [], [at for at, mask in enumerate(group, 1) if mask < exp_size]
     apart = [near[at] for at in later]
     for high, members in zip(range(2, head_size, 2), sets):
         pieces = through_experts(members, [(at, near[at]) for at in joined] if high == 2 else ())
@@ -519,8 +519,9 @@
         total = call(sum_kernel, "sum", struct((rows, model), BF16), [(VMEM, v) for v in (pieces[0], *got)])
         if high == 2:
             total, apart = lax.optimization_barrier((total, apart))
-            arrived += [part for part, mask in zip(got, group[::-1]) if mask >= exp_size]
+            arrived += [part for part, mask in zip(got, group[::-1]) if mask == exp_size]
         arrived.append(swap(total, "head", high))
+    arrived += [swap(near[at], both, mask) for at, mask in enumerate(group, 1) if mask > exp_size]
     arrived += [swap(piece, both, group[at - 1]) for piece, at in zip(apart, later)]
     return call(
         last_kernel,

time: 60.8 us -> 60.8 us (level)
  waiting for transfers between devices: 17.1 us -> 15.5 us
  starting transfers between devices: 25.1 us -> 26.7 us
    ppermute x19 -> x20, starting transfers between devices: 21.3 us -> 22.9 us  [swap(): return lax.ppermute(value, axis, [(i, i ^ mask) for i in range(size)])]
    ppermute x19 -> x20, waiting for transfers between devices: 12.2 us -> 10.6 us  [swap(): return lax.ppermute(value, axis, [(i, i ^ mask) for i in range(size)])]
  transfers between devices with their start and end apart: 22 -> 23, of which waited for: 10 -> 11; matrix products, arithmetic and copies ran while one was open for 0% -> 0% of each run, Pallas kernels for 19% -> 19%
where the time goes in v22:
time: 60.8 us; the launch traced here: 60.4 us
  starting transfers between devices  26.7 us (44%)
  Pallas kernels  18.1 us (30%)
  waiting for transfers between devices  15.5 us (25%)
    ppermute x20, starting transfers between devices, swap(): return lax.ppermute(value, axis, [(i, i ^ mask) for i in range(size)])  22.9 us
    pallas_call x15, Pallas kernels, call(): pl.pallas_call(kernel, out_shape=jax.tree.map(lambda out: pltpu.VMEM(out....  18.1 us
    ppermute x20, waiting for transfers between devices, swap(): return lax.ppermute(value, axis, [(i, i ^ mask) for i in range(size)])  10.6 us
    ppermute x3, waiting for transfers between devices, swap_slot(): return lax.ppermute(value, ('head', 'exp'), pairs)  4.89 us
    ppermute x3, starting transfers between devices, swap_slot(): return lax.ppermute(value, ('head', 'exp'), pairs)  3.79 us
  transfers between devices with their start and end apart: 23, of which 11 were waited for; matrix products, arithmetic and copies ran while one was open for 0% of the time, Pallas kernels for 19%

profile of v22, /device:TPU:0, one launch (start us, length us, event | category | flops | bytes accessed | tf_op | source)
XLA Modules:
  0.0 60.4 jit_solution(12359267409057910227)
XLA Ops:
  0.0 1.8 %state.1 = (bf16[528,128]{1,0:T(8,128)(2,1)S(1)}, bf16[528,128]{1,0:T(8,128)(2,1)S(1)}) custom-call(bf16[128,1024]{1,0:T(8,128)(2,1)} %x_hbm.3, bf16[128,256]{1,0:T(8,128)(2,1)} %b_hbm.3, f32[16,128]{1,0:T(8,128)} %bitcast.11, f32[1,16]{1,0:T(1,128)} %bitcast.16), custom_call_target="tpu_custom_call" | custom-call | tf_op jit(solution)/shard_map/state/pallas_call | solution.py:29
  1.8 0.5 collective-permute-start
  2.4 1.0 %prep.1 = (bf16[32,128]{1,0:T(8,128)(2,1)S(1)}, bf16[1,32,1344]{2,1,0:T(8,128)(2,1)S(1)}, f32[1,1344]{1,0:T(1,128)S(1)}) custom-call(bf16[528,128]{1,0:T(8,128)(2,1)S(1)} %get-tuple-element.46.after_ref.keep_ref, bf16[1,32,1344]{2,1,0:T(8,128)(2,1)} %resid_hbm.1, s32[6,1,32]{2,1,0:T(1,128)} %bitcast.14, f32[6,1,32]{2,1,0:T(1,128)} %bitcast.15, f32[1344]{0:T(1024)} %gain_hbm.1), custom_call_target="tpu_custom_call" | custom-call | tf_op jit(solution)/shard_map/prep/pallas_call | solution.py:29
  3.3 0.0 collective-permute-done.got_ref
  3.3 0.1 chip_state.1.rest_0_
  3.4 0.4 collective-permute-start.1
  3.9 0.1 collective-permute-start.2
  4.0 3.8 %collective-permute-start.5 = (bf16[528,128]{1,0:T(8,128)(2,1)S(1)}, bf16[528,128]{1,0:T(8,128)(2,1)S(1)}, u32[]{:S(2)}, u32[]{:S(2)}) collective-permute-start(bf16[528,128]{1,0:T(8,128)(2,1)S(1)} %chip_state.1.rest_0_), channel_id=1, source_target_pairs={{0,18},{1,19},{2,16},{3,17},{16,2},{17,3},{18,0},{19,1},{4,22},{5,... | collective-permute-start | bytes 405512 | tf_op jit(solution)/shard_map/ppermute | solution.py:363
  7.8 0.5 collective-permute-start.4
  8.4 0.0 collective-permute-start.3
  8.4 1.8 %projection.1 = (f32[1,1024]{1,0:T(1,128)S(1)}, bf16[1344,1024]{1,0:T(8,128)(2,1)S(1)}) custom-call(f32[1,1024]{1,0:T(1,128)} %bitcast.13, bf16[1344,1024]{1,0:T(8,128)(2,1)} %bitcast.8), custom_call_target="tpu_custom_call" | custom-call | tf_op jit(solution)/shard_map/projection/pallas_call | solution.py:29
  10.2 2.4 %inside.1 = (f32[128,1024]{1,0:T(8,128)S(1)}, f32[128,1024]{1,0:T(8,128)S(1)}, bf16[128,256]{1,0:T(8,128)(2,1)S(1)}) custom-call(bf16[128,1024]{1,0:T(8,128)(2,1)} %x_hbm.3, bf16[128,1024]{1,0:T(8,128)(2,1)} %z_hbm.1, bf16[128,256]{1,0:T(8,128)(2,1)} %b_hbm.3, bf16[128,256]{1,0:T(8,128)(2,1)} %c_hbm.1, f32[16,128]{1,0:T(8,128)} %bitcast.12, ...), custom_call_target="tpu_custom_call" | custom-call | tf_op jit(solution)/shard_map/inside/pallas_call | solution.py:29
  12.7 0.0 collective-permute-done.5.rest_3_
  12.7 2.2 %collective-permute-done.4.rest_2_ = bf16[528,128]{1,0:T(8,128)(2,1)S(1)} collective-permute-done((bf16[528,128]{1,0:T(8,128)(2,1)S(1)}, bf16[528,128]{1,0:T(8,128)(2,1)S(1)}, u32[]{:S(2)}, u32[]{:S(2)}) %collective-permute-start.4) | collective-permute-done | bytes 135200 | tf_op jit(solution)/shard_map/ppermute | solution.py:363
  14.9 0.3 before.1
  15.2 0.1 collective-permute-start.6
  15.3 0.8 %first_half.1.first_ref = f32[128,1344]{1,0:T(8,128)S(1)} custom-call(f32[128,1024]{1,0:T(8,128)S(1)} %get-tuple-element.51.local_ref, f32[128,1024]{1,0:T(8,128)S(1)} %get-tuple-element.52.grown_ref, bf16[128,256]{1,0:T(8,128)(2,1)S(1)} %get-tuple-element.53.after_b.c_ref, f32[1,1024]{1,0:T(1,128)S(1)} %get-tuple-element.54.after_a.norm_ref, ...), custom_call_target="tpu_custom_call" | custom-call | tf_op jit(solution)/shard_map/first_half/pallas_call | solution.py:29
  16.1 0.5 collective-permute-done.6.got_ref
  16.6 0.9 %mixed.1 = (bf16[32,1344]{1,0:T(8,128)(2,1)S(1)}, bf16[32,1344]{1,0:T(8,128)(2,1)S(1)}, bf16[32,1344]{1,0:T(8,128)(2,1)S(1)}, bf16[32,1344]{1,0:T(8,128)(2,1)S(1)}) custom-call(bf16[1,928,1344]{2,1,0:T(8,128)(2,1)S(1)} %collective-permute-done.1.after_up.other_up_ref, bf16[1,928,1344]{2,1,0:T(8,128)(2,1)S(1)} %collective-permute-done.2.after_down.other_down_ref, ...), custom_call_target="tpu_custom_call" | custom-call | tf_op jit(solution)/shard_map/mixed/pallas_call | solution.py:29
  17.5 1.6 %collective-permute-start.7 = (bf16[32,1344]{1,0:T(8,128)(2,1)S(1)}, bf16[32,1344]{1,0:T(8,128)(2,1)S(1)}, u32[]{:S(2)}, u32[]{:S(2)}) collective-permute-start(bf16[32,1344]{1,0:T(8,128)(2,1)S(1)} %get-tuple-element.63), channel_id=1, source_target_pairs={{0,4},{1,9},{2,6},{3,11},{4,0},{5,13},{6,2},{7,15},{8,12},{9,1},{1... | collective-permute-start | bytes 258056 | tf_op jit(solution)/shard_map/ppermute | solution.py:373
  19.1 0.5 collective-permute-start.8
  19.6 3.5 %collective-permute-done.7.got_ref.rest_1_ = bf16[32,1344]{1,0:T(8,128)(2,1)S(1)} collective-permute-done((bf16[32,1344]{1,0:T(8,128)(2,1)S(1)}, bf16[32,1344]{1,0:T(8,128)(2,1)S(1)}, u32[]{:S(2)}, u32[]{:S(2)}) %collective-permute-start.7) | collective-permute-done | bytes 86048 | tf_op jit(solution)/shard_map/ppermute | solution.py:373
  23.1 1.7 %collective-permute-start.9 = (bf16[32,1344]{1,0:T(8,128)(2,1)S(1)}, bf16[32,1344]{1,0:T(8,128)(2,1)S(1)}, u32[]{:S(2)}, u32[]{:S(2)}) collective-permute-start(bf16[32,1344]{1,0:T(8,128)(2,1)S(1)} %relay.1), channel_id=1, source_target_pairs={{0,8},{1,5},{2,10},{3,7},{4,12},{5,1},{6,14},{7,3},{8,0},{9,13},{1... | collective-permute-start | bytes 258056 | tf_op jit(solution)/shard_map/ppermute | solution.py:373
  24.8 2.5 %weights.1 = (bf16[1,928,1344]{2,1,0:T(8,128)(2,1)S(1)}, bf16[1,928,1344]{2,1,0:T(8,128)(2,1)S(1)}) custom-call(bf16[32,1344]{1,0:T(8,128)(2,1)S(1)} %get-tuple-element.59.after_ref.rest_0_, bf16[1,928,1344]{2,1,0:T(8,128)(2,1)} %bitcast.10, bf16[1,928,1344]{2,1,0:T(8,128)(2,1)} %down_hbm.1), custom_call_target="tpu_custom_call" | custom-call | tf_op jit(solution)/shard_map/weights/pallas_call | solution.py:29
  27.4 1.4 %collective-permute-done.9.rest_3_ = bf16[32,1344]{1,0:T(8,128)(2,1)S(1)} collective-permute-done((bf16[32,1344]{1,0:T(8,128)(2,1)S(1)}, bf16[32,1344]{1,0:T(8,128)(2,1)S(1)}, u32[]{:S(2)}, u32[]{:S(2)}) %collective-permute-start.9) | collective-permute-done | bytes 86048 | tf_op jit(solution)/shard_map/ppermute | solution.py:373
  28.8 0.2 rows.1
  29.0 1.5 %collective-permute-start.13 = (bf16[32,1408]{1,0:T(8,128)(2,1)S(1)}, bf16[32,1408]{1,0:T(8,128)(2,1)S(1)}, u32[]{:S(2)}, u32[]{:S(2)}) collective-permute-start(bf16[32,1408]{1,0:T(8,128)(2,1)S(1)} %get-tuple-element.68.rest_0_), channel_id=1, source_target_pairs={{0,8},{4,12},{8,0},{12,4},{1,9},{5,13},{9,1},{13,5},{2,10},{6,14},... | collective-permute-start | bytes 270344 | tf_op jit(solution)/shard_map/ppermute | solution.py:363
  30.5 3.3 %collective-permute-start.12 = (bf16[32,1408]{1,0:T(8,128)(2,1)S(1)}, bf16[32,1408]{1,0:T(8,128)(2,1)S(1)}, u32[]{:S(2)}, u32[]{:S(2)}) collective-permute-start(bf16[32,1408]{1,0:T(8,128)(2,1)S(1)} %get-tuple-element.68.rest_0_), channel_id=1, source_target_pairs={{0,6},{1,7},{2,4},{3,5},{4,2},{5,3},{6,0},{7,1},{8,14},{9,15},{10,... | collective-permute-start | bytes 270344 | tf_op jit(solution)/shard_map/ppermute | solution.py:363
  33.8 0.6 %collective-permute-start.10 = (bf16[32,1408]{1,0:T(8,128)(2,1)S(1)}, bf16[32,1408]{1,0:T(8,128)(2,1)S(1)}, u32[]{:S(2)}, u32[]{:S(2)}) collective-permute-start(bf16[32,1408]{1,0:T(8,128)(2,1)S(1)} %get-tuple-element.68.rest_0_), channel_id=1, source_target_pairs={{0,2},{1,3},{2,0},{3,1},{4,6},{5,7},{6,4},{7,5},{8,10},{9,11},{10,... | collective-permute-start | bytes 270344 | tf_op jit(solution)/shard_map/ppermute | solution.py:363
  34.4 0.1 collective-permute-done.13.rest_0_
  34.6 2.7 %collective-permute-start.16 = (bf16[32,1408]{1,0:T(8,128)(2,1)S(1)}, bf16[32,1408]{1,0:T(8,128)(2,1)S(1)}, u32[]{:S(2)}, u32[]{:S(2)}) collective-permute-start(bf16[32,1408]{1,0:T(8,128)(2,1)S(1)} %collective-permute-done.13.rest_0_), channel_id=1, source_target_pairs={{0,6},{1,7},{2,4},{3,5},{4,2},{5,3},{6,0},{7,1},{8,14},{9,15},{10,... | collective-permute-start | bytes 270344 | tf_op jit(solution)/shard_map/ppermute | solution.py:363
  37.3 1.1 %collective-permute-start.15 = (bf16[32,1408]{1,0:T(8,128)(2,1)S(1)}, bf16[32,1408]{1,0:T(8,128)(2,1)S(1)}, u32[]{:S(2)}, u32[]{:S(2)}) collective-permute-start(bf16[32,1408]{1,0:T(8,128)(2,1)S(1)} %collective-permute-done.13.rest_0_), channel_id=1, source_target_pairs={{0,4},{1,5},{2,6},{3,7},{4,0},{5,1},{6,2},{7,3},{8,12},{9,13},{10,... | collective-permute-start | bytes 270344 | tf_op jit(solution)/shard_map/ppermute | solution.py:363
  38.4 0.9 %collective-permute-done.11.rest_2_ = bf16[32,1408]{1,0:T(8,128)(2,1)S(1)} collective-permute-done((bf16[32,1408]{1,0:T(8,128)(2,1)S(1)}, bf16[32,1408]{1,0:T(8,128)(2,1)S(1)}, u32[]{:S(2)}, u32[]{:S(2)}) %collective-permute-start.11) | collective-permute-done | bytes 90144 | tf_op jit(solution)/shard_map/ppermute | solution.py:363
  39.4 1.5 %collective-permute-done.10.rest_1_ = bf16[32,1408]{1,0:T(8,128)(2,1)S(1)} collective-permute-done((bf16[32,1408]{1,0:T(8,128)(2,1)S(1)}, bf16[32,1408]{1,0:T(8,128)(2,1)S(1)}, u32[]{:S(2)}, u32[]{:S(2)}) %collective-permute-start.10) | collective-permute-done | bytes 90144 | tf_op jit(solution)/shard_map/ppermute | solution.py:363
  40.9 2.7 %experts.2 = (bf16[32,1344]{1,0:T(8,128)(2,1)S(1)}, bf16[32,1344]{1,0:T(8,128)(2,1)S(1)}, bf16[32,1344]{1,0:T(8,128)(2,1)S(1)}, bf16[32,1344]{1,0:T(8,128)(2,1)S(1)}) custom-call(bf16[1,928,1344]{2,1,0:T(8,128)(2,1)S(1)} %get-tuple-element.60.after_ref.up_ref, bf16[1,928,1344]{2,1,0:T(8,128)(2,1)S(1)} %get-tuple-element.67.down_ref, ...), custom_call_target="tpu_custom_call" | custom-call | tf_op jit(solution)/shard_map/experts/pallas_call | solution.py:29
  43.7 2.7 %experts.3 = (bf16[32,1344]{1,0:T(8,128)(2,1)S(1)}, bf16[32,1344]{1,0:T(8,128)(2,1)S(1)}, bf16[64,1344]{1,0:T(8,128)(2,1)S(1)}, bf16[32,1344]{1,0:T(8,128)(2,1)S(1)}) custom-call(bf16[1,928,1344]{2,1,0:T(8,128)(2,1)S(1)} %get-tuple-element.60.after_ref.up_ref, bf16[1,928,1344]{2,1,0:T(8,128)(2,1)S(1)} %get-tuple-element.67.down_ref, ...), custom_call_target="tpu_custom_call" | custom-call | tf_op jit(solution)/shard_map/experts/pallas_call | solution.py:29
  46.4 0.3 collective-permute-start.17
  46.7 1.0 %collective-permute-start.18 = (bf16[32,1344]{1,0:T(8,128)(2,1)S(1)}, bf16[32,1344]{1,0:T(8,128)(2,1)S(1)}, u32[]{:S(2)}, u32[]{:S(2)}) collective-permute-start(bf16[32,1344]{1,0:T(8,128)(2,1)S(1)} %get-tuple-element.81), channel_id=1, source_target_pairs={{0,6},{1,7},{2,4},{3,5},{4,2},{5,3},{6,0},{7,1},{8,14},{9,15},{10,... | collective-permute-start | bytes 258056 | tf_op jit(solution)/shard_map/ppermute | solution.py:363
  47.8 2.2 %collective-permute-start.19 = (bf16[32,1344]{1,0:T(8,128)(2,1)S(1)}, bf16[32,1344]{1,0:T(8,128)(2,1)S(1)}, u32[]{:S(2)}, u32[]{:S(2)}) collective-permute-start(bf16[32,1344]{1,0:T(8,128)(2,1)S(1)} %get-tuple-element.82), channel_id=1, source_target_pairs={{0,2},{1,3},{2,0},{3,1},{4,6},{5,7},{6,4},{7,5},{8,10},{9,11},{10,... | collective-permute-start | bytes 258056 | tf_op jit(solution)/shard_map/ppermute | solution.py:363
  49.9 1.1 %collective-permute-start.21 = (bf16[32,1344]{1,0:T(8,128)(2,1)S(1)}, bf16[32,1344]{1,0:T(8,128)(2,1)S(1)}, u32[]{:S(2)}, u32[]{:S(2)}) collective-permute-start(bf16[32,1344]{1,0:T(8,128)(2,1)S(1)} %get-tuple-element.85), channel_id=1, source_target_pairs={{0,6},{1,7},{2,4},{3,5},{4,2},{5,3},{6,0},{7,1},{8,14},{9,15},{10,... | collective-permute-start | bytes 258056 | tf_op jit(solution)/shard_map/ppermute | solution.py:363
  51.1 2.2 %collective-permute-done.18.refs_1_ = bf16[32,1344]{1,0:T(8,128)(2,1)S(1)} collective-permute-done((bf16[32,1344]{1,0:T(8,128)(2,1)S(1)}, bf16[32,1344]{1,0:T(8,128)(2,1)S(1)}, u32[]{:S(2)}, u32[]{:S(2)}) %collective-permute-start.18) | collective-permute-done | bytes 86048 | tf_op jit(solution)/shard_map/ppermute | solution.py:363
  53.3 0.5 collective-permute-done.19.refs_3_
  53.8 0.1 sum.1
  53.8 1.0 %collective-permute-start.20 = (bf16[32,1344]{1,0:T(8,128)(2,1)S(1)}, bf16[32,1344]{1,0:T(8,128)(2,1)S(1)}, u32[]{:S(2)}, u32[]{:S(2)}) collective-permute-start(bf16[32,1344]{1,0:T(8,128)(2,1)S(1)} %sum.1), channel_id=1, source_target_pairs={{0,8},{4,12},{8,0},{12,4},{1,9},{5,13},{9,1},{13,5},{2,10},{6,14},... | collective-permute-start | bytes 258056 | tf_op jit(solution)/shard_map/ppermute | solution.py:363
  54.8 2.4 %collective-permute-start.22 = (bf16[32,1344]{1,0:T(8,128)(2,1)S(1)}, bf16[32,1344]{1,0:T(8,128)(2,1)S(1)}, u32[]{:S(2)}, u32[]{:S(2)}) collective-permute-start(bf16[32,1344]{1,0:T(8,128)(2,1)S(1)} %get-tuple-element.86), channel_id=1, source_target_pairs={{0,2},{1,3},{2,0},{3,1},{4,6},{5,7},{6,4},{7,5},{8,10},{9,11},{10,... | collective-permute-start | bytes 258056 | tf_op jit(solution)/shard_map/ppermute | solution.py:363
  57.2 2.1 %collective-permute-done.20.rest_2_ = bf16[32,1344]{1,0:T(8,128)(2,1)S(1)} collective-permute-done((bf16[32,1344]{1,0:T(8,128)(2,1)S(1)}, bf16[32,1344]{1,0:T(8,128)(2,1)S(1)}, u32[]{:S(2)}, u32[]{:S(2)}) %collective-permute-start.20) | collective-permute-done | bytes 86048 | tf_op jit(solution)/shard_map/ppermute | solution.py:363
  59.3 0.4 collective-permute-done.22.rest_4_
  59.7 0.7 %last.1 = bf16[1,32,1344]{2,1,0:T(8,128)(2,1)} custom-call(bf16[32,1344]{1,0:T(8,128)(2,1)S(1)} %get-tuple-element.66.hidden_ref, bf16[32,1344]{1,0:T(8,128)(2,1)S(1)} %get-tuple-element.73.rest_0_, bf16[64,1344]{1,0:T(8,128)(2,1)S(1)} %collective-permute-done.17.refs_2_.rest_1_, bf16[32,1344]{1,0:T(8,128)(2,1)S(1)} %collective-permute-done.20.rest_2_, ...), custom_call_target="tpu_custom_call" | custom-call | tf_op jit(solution)/shard_map/last/pallas_call | solution.py:29
  (13 shorter events, 0.1 us)
Async XLA Ops:
  1.8 1.5 %collective-permute-start = (bf16[528,128]{1,0:T(8,128)(2,1)S(1)}, bf16[528,128]{1,0:T(8,128)(2,1)S(1)}, u32[]{:S(2)}, u32[]{:S(2)}) collective-permute-start(bf16[528,128]{1,0:T(8,128)(2,1)S(1)} %get-tuple-element.48), channel_id=1, source_target_pairs={{0,1},{1,0},{2,3},{3,2},{4,5},{5,4},{6,7},{7,6},{8,9},{9,8},{10,11... | collective-permute-start | bytes 405512 | tf_op jit(solution)/shard_map/ppermute | solution.py:363
  3.4 13.2 %collective-permute-start.1 = (bf16[1,928,1344]{2,1,0:T(8,128)(2,1)}, bf16[1,928,1344]{2,1,0:T(8,128)(2,1)S(1)}, u32[]{:S(2)}, u32[]{:S(2)}) collective-permute-start(bf16[1,928,1344]{2,1,0:T(8,128)(2,1)} %bitcast.9), channel_id=1, source_target_pairs={{0,1},{1,0},{2,3},{3,2},{4,5},{5,4},{6,7},{7,6},{8,9},{9,8},{10,11... | collective-permute-start | bytes 7483400 | tf_op jit(solution)/shard_map/ppermute | solution.py:363
  3.9 12.8 %collective-permute-start.2 = (bf16[1,928,1344]{2,1,0:T(8,128)(2,1)}, bf16[1,928,1344]{2,1,0:T(8,128)(2,1)S(1)}, u32[]{:S(2)}, u32[]{:S(2)}) collective-permute-start(bf16[1,928,1344]{2,1,0:T(8,128)(2,1)} %down_hbm.1), channel_id=1, source_target_pairs={{0,1},{1,0},{2,3},{3,2},{4,5},{5,4},{6,7},{7,6},{8,9},{9,8},{10,11... | collective-permute-start | bytes 7483400 | tf_op jit(solution)/shard_map/ppermute | solution.py:363
  4.0 8.6 %collective-permute-start.5 = (bf16[528,128]{1,0:T(8,128)(2,1)S(1)}, bf16[528,128]{1,0:T(8,128)(2,1)S(1)}, u32[]{:S(2)}, u32[]{:S(2)}) collective-permute-start(bf16[528,128]{1,0:T(8,128)(2,1)S(1)} %chip_state.1.rest_0_), channel_id=1, source_target_pairs={{0,18},{1,19},{2,16},{3,17},{16,2},{17,3},{18,0},{19,1},{4,22},{5,... | collective-permute-start | bytes 405512 | tf_op jit(solution)/shard_map/ppermute | solution.py:363
  7.8 7.1 %collective-permute-start.4 = (bf16[528,128]{1,0:T(8,128)(2,1)S(1)}, bf16[528,128]{1,0:T(8,128)(2,1)S(1)}, u32[]{:S(2)}, u32[]{:S(2)}) collective-permute-start(bf16[528,128]{1,0:T(8,128)(2,1)S(1)} %chip_state.1.rest_0_), channel_id=1, source_target_pairs={{0,16},{1,17},{2,18},{3,19},{16,0},{17,1},{18,2},{19,3},{4,20},{5,... | collective-permute-start | bytes 405512 | tf_op jit(solution)/shard_map/ppermute | solution.py:363
  8.4 6.5 %collective-permute-start.3 = (bf16[528,128]{1,0:T(8,128)(2,1)S(1)}, bf16[528,128]{1,0:T(8,128)(2,1)S(1)}, u32[]{:S(2)}, u32[]{:S(2)}) collective-permute-start(bf16[528,128]{1,0:T(8,128)(2,1)S(1)} %chip_state.1.rest_0_), channel_id=1, source_target_pairs={{0,2},{1,3},{2,0},{3,1},{16,18},{17,19},{18,16},{19,17},{4,6},{5,7... | collective-permute-start | bytes 405512 | tf_op jit(solution)/shard_map/ppermute | solution.py:363
  15.2 1.4 %collective-permute-start.6 = (bf16[4,128,128]{2,1,0:T(8,128)(2,1)S(1)}, bf16[4,128,128]{2,1,0:T(8,128)(2,1)S(1)}, u32[]{:S(2)}, u32[]{:S(2)}) collective-permute-start(bf16[4,128,128]{2,1,0:T(8,128)(2,1)S(1)} %get-tuple-element.57), channel_id=1, source_target_pairs={{0,1},{1,0},{2,3},{3,2},{4,5},{5,4},{6,7},{7,6},{8,9},{9,8},{10,11... | collective-permute-start | bytes 393224 | tf_op jit(solution)/shard_map/ppermute | solution.py:363
  17.5 5.6 %collective-permute-start.7 = (bf16[32,1344]{1,0:T(8,128)(2,1)S(1)}, bf16[32,1344]{1,0:T(8,128)(2,1)S(1)}, u32[]{:S(2)}, u32[]{:S(2)}) collective-permute-start(bf16[32,1344]{1,0:T(8,128)(2,1)S(1)} %get-tuple-element.63), channel_id=1, source_target_pairs={{0,4},{1,9},{2,6},{3,11},{4,0},{5,13},{6,2},{7,15},{8,12},{9,1},{1... | collective-permute-start | bytes 258056 | tf_op jit(solution)/shard_map/ppermute | solution.py:373
  19.1 8.2 %collective-permute-start.8 = (bf16[32,1344]{1,0:T(8,128)(2,1)S(1)}, bf16[32,1344]{1,0:T(8,128)(2,1)S(1)}, u32[]{:S(2)}, u32[]{:S(2)}) collective-permute-start(bf16[32,1344]{1,0:T(8,128)(2,1)S(1)} %get-tuple-element.64), channel_id=1, source_target_pairs={{0,4},{1,13},{2,6},{3,15},{4,0},{5,9},{6,2},{7,11},{8,12},{9,5},{1... | collective-permute-start | bytes 258056 | tf_op jit(solution)/shard_map/ppermute | solution.py:373
  23.1 5.7 %collective-permute-start.9 = (bf16[32,1344]{1,0:T(8,128)(2,1)S(1)}, bf16[32,1344]{1,0:T(8,128)(2,1)S(1)}, u32[]{:S(2)}, u32[]{:S(2)}) collective-permute-start(bf16[32,1344]{1,0:T(8,128)(2,1)S(1)} %relay.1), channel_id=1, source_target_pairs={{0,8},{1,5},{2,10},{3,7},{4,12},{5,1},{6,14},{7,3},{8,0},{9,13},{1... | collective-permute-start | bytes 258056 | tf_op jit(solution)/shard_map/ppermute | solution.py:373
  29.0 5.6 %collective-permute-start.13 = (bf16[32,1408]{1,0:T(8,128)(2,1)S(1)}, bf16[32,1408]{1,0:T(8,128)(2,1)S(1)}, u32[]{:S(2)}, u32[]{:S(2)}) collective-permute-start(bf16[32,1408]{1,0:T(8,128)(2,1)S(1)} %get-tuple-element.68.rest_0_), channel_id=1, source_target_pairs={{0,8},{4,12},{8,0},{12,4},{1,9},{5,13},{9,1},{13,5},{2,10},{6,14},... | collective-permute-start | bytes 270344 | tf_op jit(solution)/shard_map/ppermute | solution.py:363
  30.5 7.9 %collective-permute-start.12 = (bf16[32,1408]{1,0:T(8,128)(2,1)S(1)}, bf16[32,1408]{1,0:T(8,128)(2,1)S(1)}, u32[]{:S(2)}, u32[]{:S(2)}) collective-permute-start(bf16[32,1408]{1,0:T(8,128)(2,1)S(1)} %get-tuple-element.68.rest_0_), channel_id=1, source_target_pairs={{0,6},{1,7},{2,4},{3,5},{4,2},{5,3},{6,0},{7,1},{8,14},{9,15},{10,... | collective-permute-start | bytes 270344 | tf_op jit(solution)/shard_map/ppermute | solution.py:363
  33.8 5.6 %collective-permute-start.11 = (bf16[32,1408]{1,0:T(8,128)(2,1)S(1)}, bf16[32,1408]{1,0:T(8,128)(2,1)S(1)}, u32[]{:S(2)}, u32[]{:S(2)}) collective-permute-start(bf16[32,1408]{1,0:T(8,128)(2,1)S(1)} %get-tuple-element.68.rest_0_), channel_id=1, source_target_pairs={{0,4},{1,5},{2,6},{3,7},{4,0},{5,1},{6,2},{7,3},{8,12},{9,13},{10,... | collective-permute-start | bytes 270344 | tf_op jit(solution)/shard_map/ppermute | solution.py:363
  33.8 7.1 %collective-permute-start.10 = (bf16[32,1408]{1,0:T(8,128)(2,1)S(1)}, bf16[32,1408]{1,0:T(8,128)(2,1)S(1)}, u32[]{:S(2)}, u32[]{:S(2)}) collective-permute-start(bf16[32,1408]{1,0:T(8,128)(2,1)S(1)} %get-tuple-element.68.rest_0_), channel_id=1, source_target_pairs={{0,2},{1,3},{2,0},{3,1},{4,6},{5,7},{6,4},{7,5},{8,10},{9,11},{10,... | collective-permute-start | bytes 270344 | tf_op jit(solution)/shard_map/ppermute | solution.py:363
  34.6 9.1 %collective-permute-start.16 = (bf16[32,1408]{1,0:T(8,128)(2,1)S(1)}, bf16[32,1408]{1,0:T(8,128)(2,1)S(1)}, u32[]{:S(2)}, u32[]{:S(2)}) collective-permute-start(bf16[32,1408]{1,0:T(8,128)(2,1)S(1)} %collective-permute-done.13.rest_0_), channel_id=1, source_target_pairs={{0,6},{1,7},{2,4},{3,5},{4,2},{5,3},{6,0},{7,1},{8,14},{9,15},{10,... | collective-permute-start | bytes 270344 | tf_op jit(solution)/shard_map/ppermute | solution.py:363
  37.3 6.3 %collective-permute-start.15 = (bf16[32,1408]{1,0:T(8,128)(2,1)S(1)}, bf16[32,1408]{1,0:T(8,128)(2,1)S(1)}, u32[]{:S(2)}, u32[]{:S(2)}) collective-permute-start(bf16[32,1408]{1,0:T(8,128)(2,1)S(1)} %collective-permute-done.13.rest_0_), channel_id=1, source_target_pairs={{0,4},{1,5},{2,6},{3,7},{4,0},{5,1},{6,2},{7,3},{8,12},{9,13},{10,... | collective-permute-start | bytes 270344 | tf_op jit(solution)/shard_map/ppermute | solution.py:363
  38.4 5.2 %collective-permute-start.14 = (bf16[32,1408]{1,0:T(8,128)(2,1)S(1)}, bf16[32,1408]{1,0:T(8,128)(2,1)S(1)}, u32[]{:S(2)}, u32[]{:S(2)}) collective-permute-start(bf16[32,1408]{1,0:T(8,128)(2,1)S(1)} %collective-permute-done.13.rest_0_), channel_id=1, source_target_pairs={{0,2},{1,3},{2,0},{3,1},{4,6},{5,7},{6,4},{7,5},{8,10},{9,11},{10,... | collective-permute-start | bytes 270344 | tf_op jit(solution)/shard_map/ppermute | solution.py:363
  46.4 7.4 %collective-permute-start.17 = (bf16[64,1344]{1,0:T(8,128)(2,1)S(1)}, bf16[64,1344]{1,0:T(8,128)(2,1)S(1)}, u32[]{:S(2)}, u32[]{:S(2)}) collective-permute-start(bf16[64,1344]{1,0:T(8,128)(2,1)S(1)} %get-tuple-element.79), channel_id=1, source_target_pairs={{0,4},{1,5},{2,6},{3,7},{4,0},{5,1},{6,2},{7,3},{8,12},{9,13},{10,... | collective-permute-start | bytes 516104 | tf_op jit(solution)/shard_map/ppermute | solution.py:363
  46.7 6.6 %collective-permute-start.18 = (bf16[32,1344]{1,0:T(8,128)(2,1)S(1)}, bf16[32,1344]{1,0:T(8,128)(2,1)S(1)}, u32[]{:S(2)}, u32[]{:S(2)}) collective-permute-start(bf16[32,1344]{1,0:T(8,128)(2,1)S(1)} %get-tuple-element.81), channel_id=1, source_target_pairs={{0,6},{1,7},{2,4},{3,5},{4,2},{5,3},{6,0},{7,1},{8,14},{9,15},{10,... | collective-permute-start | bytes 258056 | tf_op jit(solution)/shard_map/ppermute | solution.py:363
  47.8 6.0 %collective-permute-start.19 = (bf16[32,1344]{1,0:T(8,128)(2,1)S(1)}, bf16[32,1344]{1,0:T(8,128)(2,1)S(1)}, u32[]{:S(2)}, u32[]{:S(2)}) collective-permute-start(bf16[32,1344]{1,0:T(8,128)(2,1)S(1)} %get-tuple-element.82), channel_id=1, source_target_pairs={{0,2},{1,3},{2,0},{3,1},{4,6},{5,7},{6,4},{7,5},{8,10},{9,11},{10,... | collective-permute-start | bytes 258056 | tf_op jit(solution)/shard_map/ppermute | solution.py:363
  49.9 7.3 %collective-permute-start.21 = (bf16[32,1344]{1,0:T(8,128)(2,1)S(1)}, bf16[32,1344]{1,0:T(8,128)(2,1)S(1)}, u32[]{:S(2)}, u32[]{:S(2)}) collective-permute-start(bf16[32,1344]{1,0:T(8,128)(2,1)S(1)} %get-tuple-element.85), channel_id=1, source_target_pairs={{0,6},{1,7},{2,4},{3,5},{4,2},{5,3},{6,0},{7,1},{8,14},{9,15},{10,... | collective-permute-start | bytes 258056 | tf_op jit(solution)/shard_map/ppermute | solution.py:363
  53.8 5.5 %collective-permute-start.20 = (bf16[32,1344]{1,0:T(8,128)(2,1)S(1)}, bf16[32,1344]{1,0:T(8,128)(2,1)S(1)}, u32[]{:S(2)}, u32[]{:S(2)}) collective-permute-start(bf16[32,1344]{1,0:T(8,128)(2,1)S(1)} %sum.1), channel_id=1, source_target_pairs={{0,8},{4,12},{8,0},{12,4},{1,9},{5,13},{9,1},{13,5},{2,10},{6,14},... | collective-permute-start | bytes 258056 | tf_op jit(solution)/shard_map/ppermute | solution.py:363
  54.8 4.9 %collective-permute-start.22 = (bf16[32,1344]{1,0:T(8,128)(2,1)S(1)}, bf16[32,1344]{1,0:T(8,128)(2,1)S(1)}, u32[]{:S(2)}, u32[]{:S(2)}) collective-permute-start(bf16[32,1344]{1,0:T(8,128)(2,1)S(1)} %get-tuple-element.86), channel_id=1, source_target_pairs={{0,2},{1,3},{2,0},{3,1},{4,6},{5,7},{6,4},{7,5},{8,10},{9,11},{10,... | collective-permute-start | bytes 258056 | tf_op jit(solution)/shard_map/ppermute | solution.py:363

commit v23 on v22

--- a/solution.py
+++ b/solution.py
@@ -518,7 +518,6 @@
         got = [swap(piece, both, mask) for piece, mask in zip(pieces[:0:-1], group[::-1])]
         total = call(sum_kernel, "sum", struct((rows, model), BF16), [(VMEM, v) for v in (pieces[0], *got)])
         if high == 2:
-            total, apart = lax.optimization_barrier((total, apart))
             arrived += [part for part, mask in zip(got, group[::-1]) if mask == exp_size]
         arrived.append(swap(total, "head", high))
     arrived += [swap(near[at], both, mask) for at, mask in enumerate(group, 1) if mask > exp_size]

time: 60.8 us -> 60.3 us (level)
  starting transfers between devices: 26.7 us -> 25 us
  waiting for transfers between devices: 15.5 us -> 16.7 us
    ppermute x20, starting transfers between devices: 22.9 us -> 21.2 us  [swap(): return lax.ppermute(value, axis, [(i, i ^ mask) for i in range(size)])]
    ppermute x20, waiting for transfers between devices: 10.6 us -> 11.8 us  [swap(): return lax.ppermute(value, axis, [(i, i ^ mask) for i in range(size)])]
  transfers between devices with their start and end apart: 23 -> 23, of which waited for: 11 -> 12; matrix products, arithmetic and copies ran while one was open for 0% -> 0% of each run, Pallas kernels for 19% -> 20%
where the time goes in v23:
time: 60.3 us; the launch traced here: 60 us
  starting transfers between devices  25 us (41%)
  Pallas kernels  18.1 us (30%)
  waiting for transfers between devices  16.7 us (28%)
    ppermute x20, starting transfers between devices, swap(): return lax.ppermute(value, axis, [(i, i ^ mask) for i in range(size)])  21.2 us
    pallas_call x15, Pallas kernels, call(): pl.pallas_call(kernel, out_shape=jax.tree.map(lambda out: pltpu.VMEM(out....  18.1 us
    ppermute x20, waiting for transfers between devices, swap(): return lax.ppermute(value, axis, [(i, i ^ mask) for i in range(size)])  11.8 us
    ppermute x3, waiting for transfers between devices, swap_slot(): return lax.ppermute(value, ('head', 'exp'), pairs)  4.89 us
    ppermute x3, starting transfers between devices, swap_slot(): return lax.ppermute(value, ('head', 'exp'), pairs)  3.79 us
  transfers between devices with their start and end apart: 23, of which 12 were waited for; matrix products, arithmetic and copies ran while one was open for 0% of the time, Pallas kernels for 20%

profile of v23, /device:TPU:0, one launch (start us, length us, event | category | flops | bytes accessed | tf_op | source)
XLA Modules:
  0.0 60.0 jit_solution(3860405966625318599)
XLA Ops:
  0.0 1.8 %state.1 = (bf16[528,128]{1,0:T(8,128)(2,1)S(1)}, bf16[528,128]{1,0:T(8,128)(2,1)S(1)}) custom-call(bf16[128,1024]{1,0:T(8,128)(2,1)} %x_hbm.3, bf16[128,256]{1,0:T(8,128)(2,1)} %b_hbm.3, f32[16,128]{1,0:T(8,128)} %bitcast.11, f32[1,16]{1,0:T(1,128)} %bitcast.16), custom_call_target="tpu_custom_call" | custom-call | tf_op jit(solution)/shard_map/state/pallas_call | solution.py:29
  1.8 0.5 collective-permute-start
  2.4 1.0 %prep.1 = (bf16[32,128]{1,0:T(8,128)(2,1)S(1)}, bf16[1,32,1344]{2,1,0:T(8,128)(2,1)S(1)}, f32[1,1344]{1,0:T(1,128)S(1)}) custom-call(bf16[528,128]{1,0:T(8,128)(2,1)S(1)} %get-tuple-element.44.after_ref.keep_ref, bf16[1,32,1344]{2,1,0:T(8,128)(2,1)} %resid_hbm.1, s32[6,1,32]{2,1,0:T(1,128)} %bitcast.14, f32[6,1,32]{2,1,0:T(1,128)} %bitcast.15, f32[1344]{0:T(1024)} %gain_hbm.1), custom_call_target="tpu_custom_call" | custom-call | tf_op jit(solution)/shard_map/prep/pallas_call | solution.py:29
  3.3 0.0 collective-permute-done.got_ref
  3.3 0.1 chip_state.1.rest_0_
  3.4 0.4 collective-permute-start.1
  3.9 0.1 collective-permute-start.2
  4.0 3.8 %collective-permute-start.5 = (bf16[528,128]{1,0:T(8,128)(2,1)S(1)}, bf16[528,128]{1,0:T(8,128)(2,1)S(1)}, u32[]{:S(2)}, u32[]{:S(2)}) collective-permute-start(bf16[528,128]{1,0:T(8,128)(2,1)S(1)} %chip_state.1.rest_0_), channel_id=1, source_target_pairs={{0,18},{1,19},{2,16},{3,17},{16,2},{17,3},{18,0},{19,1},{4,22},{5,... | collective-permute-start | bytes 405512 | tf_op jit(solution)/shard_map/ppermute | solution.py:363
  7.8 0.5 collective-permute-start.4
  8.4 0.0 collective-permute-start.3
  8.4 1.8 %projection.1 = (f32[1,1024]{1,0:T(1,128)S(1)}, bf16[1344,1024]{1,0:T(8,128)(2,1)S(1)}) custom-call(f32[1,1024]{1,0:T(1,128)} %bitcast.13, bf16[1344,1024]{1,0:T(8,128)(2,1)} %bitcast.8), custom_call_target="tpu_custom_call" | custom-call | tf_op jit(solution)/shard_map/projection/pallas_call | solution.py:29
  10.2 2.4 %inside.1 = (f32[128,1024]{1,0:T(8,128)S(1)}, f32[128,1024]{1,0:T(8,128)S(1)}, bf16[128,256]{1,0:T(8,128)(2,1)S(1)}) custom-call(bf16[128,1024]{1,0:T(8,128)(2,1)} %x_hbm.3, bf16[128,1024]{1,0:T(8,128)(2,1)} %z_hbm.1, bf16[128,256]{1,0:T(8,128)(2,1)} %b_hbm.3, bf16[128,256]{1,0:T(8,128)(2,1)} %c_hbm.1, f32[16,128]{1,0:T(8,128)} %bitcast.12, ...), custom_call_target="tpu_custom_call" | custom-call | tf_op jit(solution)/shard_map/inside/pallas_call | solution.py:29
  12.7 0.0 collective-permute-done.5.rest_3_
  12.7 2.2 %collective-permute-done.4.rest_2_ = bf16[528,128]{1,0:T(8,128)(2,1)S(1)} collective-permute-done((bf16[528,128]{1,0:T(8,128)(2,1)S(1)}, bf16[528,128]{1,0:T(8,128)(2,1)S(1)}, u32[]{:S(2)}, u32[]{:S(2)}) %collective-permute-start.4) | collective-permute-done | bytes 135200 | tf_op jit(solution)/shard_map/ppermute | solution.py:363
  14.9 0.3 before.1
  15.2 0.1 collective-permute-start.6
  15.3 0.8 %first_half.1.first_ref = f32[128,1344]{1,0:T(8,128)S(1)} custom-call(f32[128,1024]{1,0:T(8,128)S(1)} %get-tuple-element.49.local_ref, f32[128,1024]{1,0:T(8,128)S(1)} %get-tuple-element.50.grown_ref, bf16[128,256]{1,0:T(8,128)(2,1)S(1)} %get-tuple-element.51.after_b.c_ref, f32[1,1024]{1,0:T(1,128)S(1)} %get-tuple-element.52.after_a.norm_ref, ...), custom_call_target="tpu_custom_call" | custom-call | tf_op jit(solution)/shard_map/first_half/pallas_call | solution.py:29
  16.1 0.5 collective-permute-done.6.got_ref
  16.6 0.9 %mixed.1 = (bf16[32,1344]{1,0:T(8,128)(2,1)S(1)}, bf16[32,1344]{1,0:T(8,128)(2,1)S(1)}, bf16[32,1344]{1,0:T(8,128)(2,1)S(1)}, bf16[32,1344]{1,0:T(8,128)(2,1)S(1)}) custom-call(bf16[1,928,1344]{2,1,0:T(8,128)(2,1)S(1)} %collective-permute-done.1.after_up.other_up_ref, bf16[1,928,1344]{2,1,0:T(8,128)(2,1)S(1)} %collective-permute-done.2.after_down.other_down_ref, ...), custom_call_target="tpu_custom_call" | custom-call | tf_op jit(solution)/shard_map/mixed/pallas_call | solution.py:29
  17.5 1.6 %collective-permute-start.7 = (bf16[32,1344]{1,0:T(8,128)(2,1)S(1)}, bf16[32,1344]{1,0:T(8,128)(2,1)S(1)}, u32[]{:S(2)}, u32[]{:S(2)}) collective-permute-start(bf16[32,1344]{1,0:T(8,128)(2,1)S(1)} %get-tuple-element.61), channel_id=1, source_target_pairs={{0,4},{1,9},{2,6},{3,11},{4,0},{5,13},{6,2},{7,15},{8,12},{9,1},{1... | collective-permute-start | bytes 258056 | tf_op jit(solution)/shard_map/ppermute | solution.py:373
  19.1 0.5 collective-permute-start.8
  19.6 3.5 %collective-permute-done.7.got_ref.rest_1_ = bf16[32,1344]{1,0:T(8,128)(2,1)S(1)} collective-permute-done((bf16[32,1344]{1,0:T(8,128)(2,1)S(1)}, bf16[32,1344]{1,0:T(8,128)(2,1)S(1)}, u32[]{:S(2)}, u32[]{:S(2)}) %collective-permute-start.7) | collective-permute-done | bytes 86048 | tf_op jit(solution)/shard_map/ppermute | solution.py:373
  23.1 1.7 %collective-permute-start.9 = (bf16[32,1344]{1,0:T(8,128)(2,1)S(1)}, bf16[32,1344]{1,0:T(8,128)(2,1)S(1)}, u32[]{:S(2)}, u32[]{:S(2)}) collective-permute-start(bf16[32,1344]{1,0:T(8,128)(2,1)S(1)} %relay.1), channel_id=1, source_target_pairs={{0,8},{1,5},{2,10},{3,7},{4,12},{5,1},{6,14},{7,3},{8,0},{9,13},{1... | collective-permute-start | bytes 258056 | tf_op jit(solution)/shard_map/ppermute | solution.py:373
  24.8 2.5 %weights.1 = (bf16[1,928,1344]{2,1,0:T(8,128)(2,1)S(1)}, bf16[1,928,1344]{2,1,0:T(8,128)(2,1)S(1)}) custom-call(bf16[32,1344]{1,0:T(8,128)(2,1)S(1)} %get-tuple-element.57.after_ref.rest_0_, bf16[1,928,1344]{2,1,0:T(8,128)(2,1)} %bitcast.10, bf16[1,928,1344]{2,1,0:T(8,128)(2,1)} %down_hbm.1), custom_call_target="tpu_custom_call" | custom-call | tf_op jit(solution)/shard_map/weights/pallas_call | solution.py:29
  27.4 1.4 %collective-permute-done.9.rest_3_ = bf16[32,1344]{1,0:T(8,128)(2,1)S(1)} collective-permute-done((bf16[32,1344]{1,0:T(8,128)(2,1)S(1)}, bf16[32,1344]{1,0:T(8,128)(2,1)S(1)}, u32[]{:S(2)}, u32[]{:S(2)}) %collective-permute-start.9) | collective-permute-done | bytes 86048 | tf_op jit(solution)/shard_map/ppermute | solution.py:373
  28.8 0.2 rows.1
  29.0 1.5 %collective-permute-start.13 = (bf16[32,1408]{1,0:T(8,128)(2,1)S(1)}, bf16[32,1408]{1,0:T(8,128)(2,1)S(1)}, u32[]{:S(2)}, u32[]{:S(2)}) collective-permute-start(bf16[32,1408]{1,0:T(8,128)(2,1)S(1)} %get-tuple-element.66.rest_0_), channel_id=1, source_target_pairs={{0,8},{4,12},{8,0},{12,4},{1,9},{5,13},{9,1},{13,5},{2,10},{6,14},... | collective-permute-start | bytes 270344 | tf_op jit(solution)/shard_map/ppermute | solution.py:363
  30.5 3.3 %collective-permute-start.12 = (bf16[32,1408]{1,0:T(8,128)(2,1)S(1)}, bf16[32,1408]{1,0:T(8,128)(2,1)S(1)}, u32[]{:S(2)}, u32[]{:S(2)}) collective-permute-start(bf16[32,1408]{1,0:T(8,128)(2,1)S(1)} %get-tuple-element.66.rest_0_), channel_id=1, source_target_pairs={{0,6},{1,7},{2,4},{3,5},{4,2},{5,3},{6,0},{7,1},{8,14},{9,15},{10,... | collective-permute-start | bytes 270344 | tf_op jit(solution)/shard_map/ppermute | solution.py:363
  33.8 0.6 %collective-permute-start.10 = (bf16[32,1408]{1,0:T(8,128)(2,1)S(1)}, bf16[32,1408]{1,0:T(8,128)(2,1)S(1)}, u32[]{:S(2)}, u32[]{:S(2)}) collective-permute-start(bf16[32,1408]{1,0:T(8,128)(2,1)S(1)} %get-tuple-element.66.rest_0_), channel_id=1, source_target_pairs={{0,2},{1,3},{2,0},{3,1},{4,6},{5,7},{6,4},{7,5},{8,10},{9,11},{10,... | collective-permute-start | bytes 270344 | tf_op jit(solution)/shard_map/ppermute | solution.py:363
  34.4 0.1 collective-permute-done.13.rest_0_
  34.6 2.7 %collective-permute-start.16 = (bf16[32,1408]{1,0:T(8,128)(2,1)S(1)}, bf16[32,1408]{1,0:T(8,128)(2,1)S(1)}, u32[]{:S(2)}, u32[]{:S(2)}) collective-permute-start(bf16[32,1408]{1,0:T(8,128)(2,1)S(1)} %collective-permute-done.13.rest_0_), channel_id=1, source_target_pairs={{0,6},{1,7},{2,4},{3,5},{4,2},{5,3},{6,0},{7,1},{8,14},{9,15},{10,... | collective-permute-start | bytes 270344 | tf_op jit(solution)/shard_map/ppermute | solution.py:363
  37.3 1.1 %collective-permute-start.15 = (bf16[32,1408]{1,0:T(8,128)(2,1)S(1)}, bf16[32,1408]{1,0:T(8,128)(2,1)S(1)}, u32[]{:S(2)}, u32[]{:S(2)}) collective-permute-start(bf16[32,1408]{1,0:T(8,128)(2,1)S(1)} %collective-permute-done.13.rest_0_), channel_id=1, source_target_pairs={{0,4},{1,5},{2,6},{3,7},{4,0},{5,1},{6,2},{7,3},{8,12},{9,13},{10,... | collective-permute-start | bytes 270344 | tf_op jit(solution)/shard_map/ppermute | solution.py:363
  38.4 0.9 %collective-permute-done.11.rest_2_ = bf16[32,1408]{1,0:T(8,128)(2,1)S(1)} collective-permute-done((bf16[32,1408]{1,0:T(8,128)(2,1)S(1)}, bf16[32,1408]{1,0:T(8,128)(2,1)S(1)}, u32[]{:S(2)}, u32[]{:S(2)}) %collective-permute-start.11) | collective-permute-done | bytes 90144 | tf_op jit(solution)/shard_map/ppermute | solution.py:363
  39.4 1.5 %collective-permute-done.10.rest_1_ = bf16[32,1408]{1,0:T(8,128)(2,1)S(1)} collective-permute-done((bf16[32,1408]{1,0:T(8,128)(2,1)S(1)}, bf16[32,1408]{1,0:T(8,128)(2,1)S(1)}, u32[]{:S(2)}, u32[]{:S(2)}) %collective-permute-start.10) | collective-permute-done | bytes 90144 | tf_op jit(solution)/shard_map/ppermute | solution.py:363
  40.9 2.7 %experts.2 = (bf16[32,1344]{1,0:T(8,128)(2,1)S(1)}, bf16[32,1344]{1,0:T(8,128)(2,1)S(1)}, bf16[32,1344]{1,0:T(8,128)(2,1)S(1)}, bf16[32,1344]{1,0:T(8,128)(2,1)S(1)}) custom-call(bf16[1,928,1344]{2,1,0:T(8,128)(2,1)S(1)} %get-tuple-element.58.after_ref.up_ref, bf16[1,928,1344]{2,1,0:T(8,128)(2,1)S(1)} %get-tuple-element.65.down_ref, ...), custom_call_target="tpu_custom_call" | custom-call | tf_op jit(solution)/shard_map/experts/pallas_call | solution.py:29
  43.7 2.7 %experts.3 = (bf16[32,1344]{1,0:T(8,128)(2,1)S(1)}, bf16[32,1344]{1,0:T(8,128)(2,1)S(1)}, bf16[64,1344]{1,0:T(8,128)(2,1)S(1)}, bf16[32,1344]{1,0:T(8,128)(2,1)S(1)}) custom-call(bf16[1,928,1344]{2,1,0:T(8,128)(2,1)S(1)} %get-tuple-element.58.after_ref.up_ref, bf16[1,928,1344]{2,1,0:T(8,128)(2,1)S(1)} %get-tuple-element.65.down_ref, ...), custom_call_target="tpu_custom_call" | custom-call | tf_op jit(solution)/shard_map/experts/pallas_call | solution.py:29
  46.4 0.3 collective-permute-start.17
  46.7 1.0 %collective-permute-start.18 = (bf16[32,1344]{1,0:T(8,128)(2,1)S(1)}, bf16[32,1344]{1,0:T(8,128)(2,1)S(1)}, u32[]{:S(2)}, u32[]{:S(2)}) collective-permute-start(bf16[32,1344]{1,0:T(8,128)(2,1)S(1)} %get-tuple-element.79), channel_id=1, source_target_pairs={{0,6},{1,7},{2,4},{3,5},{4,2},{5,3},{6,0},{7,1},{8,14},{9,15},{10,... | collective-permute-start | bytes 258056 | tf_op jit(solution)/shard_map/ppermute | solution.py:363
  47.8 2.2 %collective-permute-start.19 = (bf16[32,1344]{1,0:T(8,128)(2,1)S(1)}, bf16[32,1344]{1,0:T(8,128)(2,1)S(1)}, u32[]{:S(2)}, u32[]{:S(2)}) collective-permute-start(bf16[32,1344]{1,0:T(8,128)(2,1)S(1)} %get-tuple-element.80), channel_id=1, source_target_pairs={{0,2},{1,3},{2,0},{3,1},{4,6},{5,7},{6,4},{7,5},{8,10},{9,11},{10,... | collective-permute-start | bytes 258056 | tf_op jit(solution)/shard_map/ppermute | solution.py:363
  49.9 1.1 %collective-permute-start.21 = (bf16[32,1344]{1,0:T(8,128)(2,1)S(1)}, bf16[32,1344]{1,0:T(8,128)(2,1)S(1)}, u32[]{:S(2)}, u32[]{:S(2)}) collective-permute-start(bf16[32,1344]{1,0:T(8,128)(2,1)S(1)} %get-tuple-element.81), channel_id=1, source_target_pairs={{0,6},{1,7},{2,4},{3,5},{4,2},{5,3},{6,0},{7,1},{8,14},{9,15},{10,... | collective-permute-start | bytes 258056 | tf_op jit(solution)/shard_map/ppermute | solution.py:363
  51.1 0.6 %collective-permute-start.22 = (bf16[32,1344]{1,0:T(8,128)(2,1)S(1)}, bf16[32,1344]{1,0:T(8,128)(2,1)S(1)}, u32[]{:S(2)}, u32[]{:S(2)}) collective-permute-start(bf16[32,1344]{1,0:T(8,128)(2,1)S(1)} %get-tuple-element.82), channel_id=1, source_target_pairs={{0,2},{1,3},{2,0},{3,1},{4,6},{5,7},{6,4},{7,5},{8,10},{9,11},{10,... | collective-permute-start | bytes 258056 | tf_op jit(solution)/shard_map/ppermute | solution.py:363
  51.7 1.6 %collective-permute-done.18.refs_1_ = bf16[32,1344]{1,0:T(8,128)(2,1)S(1)} collective-permute-done((bf16[32,1344]{1,0:T(8,128)(2,1)S(1)}, bf16[32,1344]{1,0:T(8,128)(2,1)S(1)}, u32[]{:S(2)}, u32[]{:S(2)}) %collective-permute-start.18) | collective-permute-done | bytes 86048 | tf_op jit(solution)/shard_map/ppermute | solution.py:363
  53.3 0.4 collective-permute-done.19.refs_3_
  53.8 1.1 %collective-permute-start.20 = (bf16[32,1344]{1,0:T(8,128)(2,1)S(1)}, bf16[32,1344]{1,0:T(8,128)(2,1)S(1)}, u32[]{:S(2)}, u32[]{:S(2)}) collective-permute-start(bf16[32,1344]{1,0:T(8,128)(2,1)S(1)} %sum.1), channel_id=1, source_target_pairs={{0,8},{4,12},{8,0},{12,4},{1,9},{5,13},{9,1},{13,5},{2,10},{6,14},... | collective-permute-start | bytes 258056 | tf_op jit(solution)/shard_map/ppermute | solution.py:363
  54.8 0.6 %collective-permute-done.21.rest_3_ = bf16[32,1344]{1,0:T(8,128)(2,1)S(1)} collective-permute-done((bf16[32,1344]{1,0:T(8,128)(2,1)S(1)}, bf16[32,1344]{1,0:T(8,128)(2,1)S(1)}, u32[]{:S(2)}, u32[]{:S(2)}) %collective-permute-start.21) | collective-permute-done | bytes 86048 | tf_op jit(solution)/shard_map/ppermute | solution.py:363
  55.4 0.9 %collective-permute-done.22.rest_4_ = bf16[32,1344]{1,0:T(8,128)(2,1)S(1)} collective-permute-done((bf16[32,1344]{1,0:T(8,128)(2,1)S(1)}, bf16[32,1344]{1,0:T(8,128)(2,1)S(1)}, u32[]{:S(2)}, u32[]{:S(2)}) %collective-permute-start.22) | collective-permute-done | bytes 86048 | tf_op jit(solution)/shard_map/ppermute | solution.py:363
  56.3 2.9 %collective-permute-done.20.rest_2_ = bf16[32,1344]{1,0:T(8,128)(2,1)S(1)} collective-permute-done((bf16[32,1344]{1,0:T(8,128)(2,1)S(1)}, bf16[32,1344]{1,0:T(8,128)(2,1)S(1)}, u32[]{:S(2)}, u32[]{:S(2)}) %collective-permute-start.20) | collective-permute-done | bytes 86048 | tf_op jit(solution)/shard_map/ppermute | solution.py:363
  59.2 0.7 %last.1 = bf16[1,32,1344]{2,1,0:T(8,128)(2,1)} custom-call(bf16[32,1344]{1,0:T(8,128)(2,1)S(1)} %get-tuple-element.64.hidden_ref, bf16[32,1344]{1,0:T(8,128)(2,1)S(1)} %get-tuple-element.71.rest_0_, bf16[64,1344]{1,0:T(8,128)(2,1)S(1)} %collective-permute-done.17.refs_2_.rest_1_, bf16[32,1344]{1,0:T(8,128)(2,1)S(1)} %collective-permute-done.20.rest_2_, ...), custom_call_target="tpu_custom_call" | custom-call | tf_op jit(solution)/shard_map/last/pallas_call | solution.py:29
  (13 shorter events, 0.1 us)
Async XLA Ops:
  1.8 1.5 %collective-permute-start = (bf16[528,128]{1,0:T(8,128)(2,1)S(1)}, bf16[528,128]{1,0:T(8,128)(2,1)S(1)}, u32[]{:S(2)}, u32[]{:S(2)}) collective-permute-start(bf16[528,128]{1,0:T(8,128)(2,1)S(1)} %get-tuple-element.46), channel_id=1, source_target_pairs={{0,1},{1,0},{2,3},{3,2},{4,5},{5,4},{6,7},{7,6},{8,9},{9,8},{10,11... | collective-permute-start | bytes 405512 | tf_op jit(solution)/shard_map/ppermute | solution.py:363
  3.4 13.2 %collective-permute-start.1 = (bf16[1,928,1344]{2,1,0:T(8,128)(2,1)}, bf16[1,928,1344]{2,1,0:T(8,128)(2,1)S(1)}, u32[]{:S(2)}, u32[]{:S(2)}) collective-permute-start(bf16[1,928,1344]{2,1,0:T(8,128)(2,1)} %bitcast.9), channel_id=1, source_target_pairs={{0,1},{1,0},{2,3},{3,2},{4,5},{5,4},{6,7},{7,6},{8,9},{9,8},{10,11... | collective-permute-start | bytes 7483400 | tf_op jit(solution)/shard_map/ppermute | solution.py:363
  3.9 12.8 %collective-permute-start.2 = (bf16[1,928,1344]{2,1,0:T(8,128)(2,1)}, bf16[1,928,1344]{2,1,0:T(8,128)(2,1)S(1)}, u32[]{:S(2)}, u32[]{:S(2)}) collective-permute-start(bf16[1,928,1344]{2,1,0:T(8,128)(2,1)} %down_hbm.1), channel_id=1, source_target_pairs={{0,1},{1,0},{2,3},{3,2},{4,5},{5,4},{6,7},{7,6},{8,9},{9,8},{10,11... | collective-permute-start | bytes 7483400 | tf_op jit(solution)/shard_map/ppermute | solution.py:363
  4.0 8.6 %collective-permute-start.5 = (bf16[528,128]{1,0:T(8,128)(2,1)S(1)}, bf16[528,128]{1,0:T(8,128)(2,1)S(1)}, u32[]{:S(2)}, u32[]{:S(2)}) collective-permute-start(bf16[528,128]{1,0:T(8,128)(2,1)S(1)} %chip_state.1.rest_0_), channel_id=1, source_target_pairs={{0,18},{1,19},{2,16},{3,17},{16,2},{17,3},{18,0},{19,1},{4,22},{5,... | collective-permute-start | bytes 405512 | tf_op jit(solution)/shard_map/ppermute | solution.py:363
  7.8 7.1 %collective-permute-start.4 = (bf16[528,128]{1,0:T(8,128)(2,1)S(1)}, bf16[528,128]{1,0:T(8,128)(2,1)S(1)}, u32[]{:S(2)}, u32[]{:S(2)}) collective-permute-start(bf16[528,128]{1,0:T(8,128)(2,1)S(1)} %chip_state.1.rest_0_), channel_id=1, source_target_pairs={{0,16},{1,17},{2,18},{3,19},{16,0},{17,1},{18,2},{19,3},{4,20},{5,... | collective-permute-start | bytes 405512 | tf_op jit(solution)/shard_map/ppermute | solution.py:363
  8.4 6.5 %collective-permute-start.3 = (bf16[528,128]{1,0:T(8,128)(2,1)S(1)}, bf16[528,128]{1,0:T(8,128)(2,1)S(1)}, u32[]{:S(2)}, u32[]{:S(2)}) collective-permute-start(bf16[528,128]{1,0:T(8,128)(2,1)S(1)} %chip_state.1.rest_0_), channel_id=1, source_target_pairs={{0,2},{1,3},{2,0},{3,1},{16,18},{17,19},{18,16},{19,17},{4,6},{5,7... | collective-permute-start | bytes 405512 | tf_op jit(solution)/shard_map/ppermute | solution.py:363
  15.2 1.4 %collective-permute-start.6 = (bf16[4,128,128]{2,1,0:T(8,128)(2,1)S(1)}, bf16[4,128,128]{2,1,0:T(8,128)(2,1)S(1)}, u32[]{:S(2)}, u32[]{:S(2)}) collective-permute-start(bf16[4,128,128]{2,1,0:T(8,128)(2,1)S(1)} %get-tuple-element.55), channel_id=1, source_target_pairs={{0,1},{1,0},{2,3},{3,2},{4,5},{5,4},{6,7},{7,6},{8,9},{9,8},{10,11... | collective-permute-start | bytes 393224 | tf_op jit(solution)/shard_map/ppermute | solution.py:363
  17.5 5.6 %collective-permute-start.7 = (bf16[32,1344]{1,0:T(8,128)(2,1)S(1)}, bf16[32,1344]{1,0:T(8,128)(2,1)S(1)}, u32[]{:S(2)}, u32[]{:S(2)}) collective-permute-start(bf16[32,1344]{1,0:T(8,128)(2,1)S(1)} %get-tuple-element.61), channel_id=1, source_target_pairs={{0,4},{1,9},{2,6},{3,11},{4,0},{5,13},{6,2},{7,15},{8,12},{9,1},{1... | collective-permute-start | bytes 258056 | tf_op jit(solution)/shard_map/ppermute | solution.py:373
  19.1 8.2 %collective-permute-start.8 = (bf16[32,1344]{1,0:T(8,128)(2,1)S(1)}, bf16[32,1344]{1,0:T(8,128)(2,1)S(1)}, u32[]{:S(2)}, u32[]{:S(2)}) collective-permute-start(bf16[32,1344]{1,0:T(8,128)(2,1)S(1)} %get-tuple-element.62), channel_id=1, source_target_pairs={{0,4},{1,13},{2,6},{3,15},{4,0},{5,9},{6,2},{7,11},{8,12},{9,5},{1... | collective-permute-start | bytes 258056 | tf_op jit(solution)/shard_map/ppermute | solution.py:373
  23.1 5.7 %collective-permute-start.9 = (bf16[32,1344]{1,0:T(8,128)(2,1)S(1)}, bf16[32,1344]{1,0:T(8,128)(2,1)S(1)}, u32[]{:S(2)}, u32[]{:S(2)}) collective-permute-start(bf16[32,1344]{1,0:T(8,128)(2,1)S(1)} %relay.1), channel_id=1, source_target_pairs={{0,8},{1,5},{2,10},{3,7},{4,12},{5,1},{6,14},{7,3},{8,0},{9,13},{1... | collective-permute-start | bytes 258056 | tf_op jit(solution)/shard_map/ppermute | solution.py:373
  29.0 5.6 %collective-permute-start.13 = (bf16[32,1408]{1,0:T(8,128)(2,1)S(1)}, bf16[32,1408]{1,0:T(8,128)(2,1)S(1)}, u32[]{:S(2)}, u32[]{:S(2)}) collective-permute-start(bf16[32,1408]{1,0:T(8,128)(2,1)S(1)} %get-tuple-element.66.rest_0_), channel_id=1, source_target_pairs={{0,8},{4,12},{8,0},{12,4},{1,9},{5,13},{9,1},{13,5},{2,10},{6,14},... | collective-permute-start | bytes 270344 | tf_op jit(solution)/shard_map/ppermute | solution.py:363
  30.5 7.9 %collective-permute-start.12 = (bf16[32,1408]{1,0:T(8,128)(2,1)S(1)}, bf16[32,1408]{1,0:T(8,128)(2,1)S(1)}, u32[]{:S(2)}, u32[]{:S(2)}) collective-permute-start(bf16[32,1408]{1,0:T(8,128)(2,1)S(1)} %get-tuple-element.66.rest_0_), channel_id=1, source_target_pairs={{0,6},{1,7},{2,4},{3,5},{4,2},{5,3},{6,0},{7,1},{8,14},{9,15},{10,... | collective-permute-start | bytes 270344 | tf_op jit(solution)/shard_map/ppermute | solution.py:363
  33.8 5.6 %collective-permute-start.11 = (bf16[32,1408]{1,0:T(8,128)(2,1)S(1)}, bf16[32,1408]{1,0:T(8,128)(2,1)S(1)}, u32[]{:S(2)}, u32[]{:S(2)}) collective-permute-start(bf16[32,1408]{1,0:T(8,128)(2,1)S(1)} %get-tuple-element.66.rest_0_), channel_id=1, source_target_pairs={{0,4},{1,5},{2,6},{3,7},{4,0},{5,1},{6,2},{7,3},{8,12},{9,13},{10,... | collective-permute-start | bytes 270344 | tf_op jit(solution)/shard_map/ppermute | solution.py:363
  33.8 7.1 %collective-permute-start.10 = (bf16[32,1408]{1,0:T(8,128)(2,1)S(1)}, bf16[32,1408]{1,0:T(8,128)(2,1)S(1)}, u32[]{:S(2)}, u32[]{:S(2)}) collective-permute-start(bf16[32,1408]{1,0:T(8,128)(2,1)S(1)} %get-tuple-element.66.rest_0_), channel_id=1, source_target_pairs={{0,2},{1,3},{2,0},{3,1},{4,6},{5,7},{6,4},{7,5},{8,10},{9,11},{10,... | collective-permute-start | bytes 270344 | tf_op jit(solution)/shard_map/ppermute | solution.py:363
  34.6 9.1 %collective-permute-start.16 = (bf16[32,1408]{1,0:T(8,128)(2,1)S(1)}, bf16[32,1408]{1,0:T(8,128)(2,1)S(1)}, u32[]{:S(2)}, u32[]{:S(2)}) collective-permute-start(bf16[32,1408]{1,0:T(8,128)(2,1)S(1)} %collective-permute-done.13.rest_0_), channel_id=1, source_target_pairs={{0,6},{1,7},{2,4},{3,5},{4,2},{5,3},{6,0},{7,1},{8,14},{9,15},{10,... | collective-permute-start | bytes 270344 | tf_op jit(solution)/shard_map/ppermute | solution.py:363
  37.3 6.3 %collective-permute-start.15 = (bf16[32,1408]{1,0:T(8,128)(2,1)S(1)}, bf16[32,1408]{1,0:T(8,128)(2,1)S(1)}, u32[]{:S(2)}, u32[]{:S(2)}) collective-permute-start(bf16[32,1408]{1,0:T(8,128)(2,1)S(1)} %collective-permute-done.13.rest_0_), channel_id=1, source_target_pairs={{0,4},{1,5},{2,6},{3,7},{4,0},{5,1},{6,2},{7,3},{8,12},{9,13},{10,... | collective-permute-start | bytes 270344 | tf_op jit(solution)/shard_map/ppermute | solution.py:363
  38.4 5.2 %collective-permute-start.14 = (bf16[32,1408]{1,0:T(8,128)(2,1)S(1)}, bf16[32,1408]{1,0:T(8,128)(2,1)S(1)}, u32[]{:S(2)}, u32[]{:S(2)}) collective-permute-start(bf16[32,1408]{1,0:T(8,128)(2,1)S(1)} %collective-permute-done.13.rest_0_), channel_id=1, source_target_pairs={{0,2},{1,3},{2,0},{3,1},{4,6},{5,7},{6,4},{7,5},{8,10},{9,11},{10,... | collective-permute-start | bytes 270344 | tf_op jit(solution)/shard_map/ppermute | solution.py:363
  46.4 7.3 %collective-permute-start.17 = (bf16[64,1344]{1,0:T(8,128)(2,1)S(1)}, bf16[64,1344]{1,0:T(8,128)(2,1)S(1)}, u32[]{:S(2)}, u32[]{:S(2)}) collective-permute-start(bf16[64,1344]{1,0:T(8,128)(2,1)S(1)} %get-tuple-element.77), channel_id=1, source_target_pairs={{0,4},{1,5},{2,6},{3,7},{4,0},{5,1},{6,2},{7,3},{8,12},{9,13},{10,... | collective-permute-start | bytes 516104 | tf_op jit(solution)/shard_map/ppermute | solution.py:363
  46.7 6.5 %collective-permute-start.18 = (bf16[32,1344]{1,0:T(8,128)(2,1)S(1)}, bf16[32,1344]{1,0:T(8,128)(2,1)S(1)}, u32[]{:S(2)}, u32[]{:S(2)}) collective-permute-start(bf16[32,1344]{1,0:T(8,128)(2,1)S(1)} %get-tuple-element.79), channel_id=1, source_target_pairs={{0,6},{1,7},{2,4},{3,5},{4,2},{5,3},{6,0},{7,1},{8,14},{9,15},{10,... | collective-permute-start | bytes 258056 | tf_op jit(solution)/shard_map/ppermute | solution.py:363
  47.8 5.9 %collective-permute-start.19 = (bf16[32,1344]{1,0:T(8,128)(2,1)S(1)}, bf16[32,1344]{1,0:T(8,128)(2,1)S(1)}, u32[]{:S(2)}, u32[]{:S(2)}) collective-permute-start(bf16[32,1344]{1,0:T(8,128)(2,1)S(1)} %get-tuple-element.80), channel_id=1, source_target_pairs={{0,2},{1,3},{2,0},{3,1},{4,6},{5,7},{6,4},{7,5},{8,10},{9,11},{10,... | collective-permute-start | bytes 258056 | tf_op jit(solution)/shard_map/ppermute | solution.py:363
  49.9 5.5 %collective-permute-start.21 = (bf16[32,1344]{1,0:T(8,128)(2,1)S(1)}, bf16[32,1344]{1,0:T(8,128)(2,1)S(1)}, u32[]{:S(2)}, u32[]{:S(2)}) collective-permute-start(bf16[32,1344]{1,0:T(8,128)(2,1)S(1)} %get-tuple-element.81), channel_id=1, source_target_pairs={{0,6},{1,7},{2,4},{3,5},{4,2},{5,3},{6,0},{7,1},{8,14},{9,15},{10,... | collective-permute-start | bytes 258056 | tf_op jit(solution)/shard_map/ppermute | solution.py:363
  51.1 5.3 %collective-permute-start.22 = (bf16[32,1344]{1,0:T(8,128)(2,1)S(1)}, bf16[32,1344]{1,0:T(8,128)(2,1)S(1)}, u32[]{:S(2)}, u32[]{:S(2)}) collective-permute-start(bf16[32,1344]{1,0:T(8,128)(2,1)S(1)} %get-tuple-element.82), channel_id=1, source_target_pairs={{0,2},{1,3},{2,0},{3,1},{4,6},{5,7},{6,4},{7,5},{8,10},{9,11},{10,... | collective-permute-start | bytes 258056 | tf_op jit(solution)/shard_map/ppermute | solution.py:363
  53.8 5.5 %collective-permute-start.20 = (bf16[32,1344]{1,0:T(8,128)(2,1)S(1)}, bf16[32,1344]{1,0:T(8,128)(2,1)S(1)}, u32[]{:S(2)}, u32[]{:S(2)}) collective-permute-start(bf16[32,1344]{1,0:T(8,128)(2,1)S(1)} %sum.1), channel_id=1, source_target_pairs={{0,8},{4,12},{8,0},{12,4},{1,9},{5,13},{9,1},{13,5},{2,10},{6,14},... | collective-permute-start | bytes 258056 | tf_op jit(solution)/shard_map/ppermute | solution.py:363

commit v24 on v23

--- a/solution.py
+++ b/solution.py
@@ -515,10 +515,10 @@
     apart = [near[at] for at in later]
     for high, members in zip(range(2, head_size, 2), sets):
         pieces = through_experts(members, [(at, near[at]) for at in joined] if high == 2 else ())
-        got = [swap(piece, both, mask) for piece, mask in zip(pieces[:0:-1], group[::-1])]
+        got = [swap(piece, both, mask) for piece, mask in zip(pieces[1:], group)]
         total = call(sum_kernel, "sum", struct((rows, model), BF16), [(VMEM, v) for v in (pieces[0], *got)])
         if high == 2:
-            arrived += [part for part, mask in zip(got, group[::-1]) if mask == exp_size]
+            arrived += [part for part, mask in zip(got, group) if mask == exp_size]
         arrived.append(swap(total, "head", high))
     arrived += [swap(near[at], both, mask) for at, mask in enumerate(group, 1) if mask > exp_size]
     arrived += [swap(piece, both, group[at - 1]) for piece, at in zip(apart, later)]

time: 60.3 us -> 60.1 us (level)
  waiting for transfers between devices: 16.7 us -> 15.6 us
  starting transfers between devices: 25 us -> 26 us
    ppermute x20, waiting for transfers between devices: 11.8 us -> 10.7 us  [swap(): return lax.ppermute(value, axis, [(i, i ^ mask) for i in range(size)])]
    ppermute x20, starting transfers between devices: 21.2 us -> 22.2 us  [swap(): return lax.ppermute(value, axis, [(i, i ^ mask) for i in range(size)])]
where the time goes in v24:
time: 60.1 us; the launch traced here: 59.8 us
  starting transfers between devices  26 us (43%)
  Pallas kernels  18.1 us (30%)
  waiting for transfers between devices  15.6 us (26%)
    ppermute x20, starting transfers between devices, swap(): return lax.ppermute(value, axis, [(i, i ^ mask) for i in range(size)])  22.2 us
    pallas_call x15, Pallas kernels, call(): pl.pallas_call(kernel, out_shape=jax.tree.map(lambda out: pltpu.VMEM(out....  18.1 us
    ppermute x20, waiting for transfers between devices, swap(): return lax.ppermute(value, axis, [(i, i ^ mask) for i in range(size)])  10.7 us
    ppermute x3, waiting for transfers between devices, swap_slot(): return lax.ppermute(value, ('head', 'exp'), pairs)  4.89 us
    ppermute x3, starting transfers between devices, swap_slot(): return lax.ppermute(value, ('head', 'exp'), pairs)  3.79 us
  transfers between devices with their start and end apart: 23, of which 12 were waited for; matrix products, arithmetic and copies ran while one was open for 0% of the time, Pallas kernels for 20%

profile of v24, /device:TPU:0, one launch (start us, length us, event | category | flops | bytes accessed | tf_op | source)
XLA Modules:
  0.0 59.8 jit_solution(8838676455854546630)
XLA Ops:
  0.0 1.8 %state.1 = (bf16[528,128]{1,0:T(8,128)(2,1)S(1)}, bf16[528,128]{1,0:T(8,128)(2,1)S(1)}) custom-call(bf16[128,1024]{1,0:T(8,128)(2,1)} %x_hbm.3, bf16[128,256]{1,0:T(8,128)(2,1)} %b_hbm.3, f32[16,128]{1,0:T(8,128)} %bitcast.11, f32[1,16]{1,0:T(1,128)} %bitcast.16), custom_call_target="tpu_custom_call" | custom-call | tf_op jit(solution)/shard_map/state/pallas_call | solution.py:29
  1.8 0.5 collective-permute-start
  2.4 1.0 %prep.1 = (bf16[32,128]{1,0:T(8,128)(2,1)S(1)}, bf16[1,32,1344]{2,1,0:T(8,128)(2,1)S(1)}, f32[1,1344]{1,0:T(1,128)S(1)}) custom-call(bf16[528,128]{1,0:T(8,128)(2,1)S(1)} %get-tuple-element.44.after_ref.keep_ref, bf16[1,32,1344]{2,1,0:T(8,128)(2,1)} %resid_hbm.1, s32[6,1,32]{2,1,0:T(1,128)} %bitcast.14, f32[6,1,32]{2,1,0:T(1,128)} %bitcast.15, f32[1344]{0:T(1024)} %gain_hbm.1), custom_call_target="tpu_custom_call" | custom-call | tf_op jit(solution)/shard_map/prep/pallas_call | solution.py:29
  3.3 0.0 collective-permute-done.got_ref
  3.3 0.1 chip_state.1.rest_0_
  3.4 0.4 collective-permute-start.1
  3.9 0.1 collective-permute-start.2
  4.0 3.8 %collective-permute-start.5 = (bf16[528,128]{1,0:T(8,128)(2,1)S(1)}, bf16[528,128]{1,0:T(8,128)(2,1)S(1)}, u32[]{:S(2)}, u32[]{:S(2)}) collective-permute-start(bf16[528,128]{1,0:T(8,128)(2,1)S(1)} %chip_state.1.rest_0_), channel_id=1, source_target_pairs={{0,18},{1,19},{2,16},{3,17},{16,2},{17,3},{18,0},{19,1},{4,22},{5,... | collective-permute-start | bytes 405512 | tf_op jit(solution)/shard_map/ppermute | solution.py:363
  7.8 0.5 collective-permute-start.4
  8.4 0.0 collective-permute-start.3
  8.4 1.8 %projection.1 = (f32[1,1024]{1,0:T(1,128)S(1)}, bf16[1344,1024]{1,0:T(8,128)(2,1)S(1)}) custom-call(f32[1,1024]{1,0:T(1,128)} %bitcast.13, bf16[1344,1024]{1,0:T(8,128)(2,1)} %bitcast.8), custom_call_target="tpu_custom_call" | custom-call | tf_op jit(solution)/shard_map/projection/pallas_call | solution.py:29
  10.2 2.4 %inside.1 = (f32[128,1024]{1,0:T(8,128)S(1)}, f32[128,1024]{1,0:T(8,128)S(1)}, bf16[128,256]{1,0:T(8,128)(2,1)S(1)}) custom-call(bf16[128,1024]{1,0:T(8,128)(2,1)} %x_hbm.3, bf16[128,1024]{1,0:T(8,128)(2,1)} %z_hbm.1, bf16[128,256]{1,0:T(8,128)(2,1)} %b_hbm.3, bf16[128,256]{1,0:T(8,128)(2,1)} %c_hbm.1, f32[16,128]{1,0:T(8,128)} %bitcast.12, ...), custom_call_target="tpu_custom_call" | custom-call | tf_op jit(solution)/shard_map/inside/pallas_call | solution.py:29
  12.7 0.0 collective-permute-done.5.rest_3_
  12.7 2.2 %collective-permute-done.4.rest_2_ = bf16[528,128]{1,0:T(8,128)(2,1)S(1)} collective-permute-done((bf16[528,128]{1,0:T(8,128)(2,1)S(1)}, bf16[528,128]{1,0:T(8,128)(2,1)S(1)}, u32[]{:S(2)}, u32[]{:S(2)}) %collective-permute-start.4) | collective-permute-done | bytes 135200 | tf_op jit(solution)/shard_map/ppermute | solution.py:363
  14.9 0.3 before.1
  15.2 0.1 collective-permute-start.6
  15.3 0.8 %first_half.1.first_ref = f32[128,1344]{1,0:T(8,128)S(1)} custom-call(f32[128,1024]{1,0:T(8,128)S(1)} %get-tuple-element.49.local_ref, f32[128,1024]{1,0:T(8,128)S(1)} %get-tuple-element.50.grown_ref, bf16[128,256]{1,0:T(8,128)(2,1)S(1)} %get-tuple-element.51.after_b.c_ref, f32[1,1024]{1,0:T(1,128)S(1)} %get-tuple-element.52.after_a.norm_ref, ...), custom_call_target="tpu_custom_call" | custom-call | tf_op jit(solution)/shard_map/first_half/pallas_call | solution.py:29
  16.1 0.5 collective-permute-done.6.got_ref
  16.6 0.9 %mixed.1 = (bf16[32,1344]{1,0:T(8,128)(2,1)S(1)}, bf16[32,1344]{1,0:T(8,128)(2,1)S(1)}, bf16[32,1344]{1,0:T(8,128)(2,1)S(1)}, bf16[32,1344]{1,0:T(8,128)(2,1)S(1)}) custom-call(bf16[1,928,1344]{2,1,0:T(8,128)(2,1)S(1)} %collective-permute-done.1.after_up.other_up_ref, bf16[1,928,1344]{2,1,0:T(8,128)(2,1)S(1)} %collective-permute-done.2.after_down.other_down_ref, ...), custom_call_target="tpu_custom_call" | custom-call | tf_op jit(solution)/shard_map/mixed/pallas_call | solution.py:29
  17.5 1.6 %collective-permute-start.7 = (bf16[32,1344]{1,0:T(8,128)(2,1)S(1)}, bf16[32,1344]{1,0:T(8,128)(2,1)S(1)}, u32[]{:S(2)}, u32[]{:S(2)}) collective-permute-start(bf16[32,1344]{1,0:T(8,128)(2,1)S(1)} %get-tuple-element.61), channel_id=1, source_target_pairs={{0,4},{1,9},{2,6},{3,11},{4,0},{5,13},{6,2},{7,15},{8,12},{9,1},{1... | collective-permute-start | bytes 258056 | tf_op jit(solution)/shard_map/ppermute | solution.py:373
  19.1 0.5 collective-permute-start.8
  19.6 3.5 %collective-permute-done.7.got_ref.rest_1_ = bf16[32,1344]{1,0:T(8,128)(2,1)S(1)} collective-permute-done((bf16[32,1344]{1,0:T(8,128)(2,1)S(1)}, bf16[32,1344]{1,0:T(8,128)(2,1)S(1)}, u32[]{:S(2)}, u32[]{:S(2)}) %collective-permute-start.7) | collective-permute-done | bytes 86048 | tf_op jit(solution)/shard_map/ppermute | solution.py:373
  23.1 1.7 %collective-permute-start.9 = (bf16[32,1344]{1,0:T(8,128)(2,1)S(1)}, bf16[32,1344]{1,0:T(8,128)(2,1)S(1)}, u32[]{:S(2)}, u32[]{:S(2)}) collective-permute-start(bf16[32,1344]{1,0:T(8,128)(2,1)S(1)} %relay.1), channel_id=1, source_target_pairs={{0,8},{1,5},{2,10},{3,7},{4,12},{5,1},{6,14},{7,3},{8,0},{9,13},{1... | collective-permute-start | bytes 258056 | tf_op jit(solution)/shard_map/ppermute | solution.py:373
  24.8 2.5 %weights.1 = (bf16[1,928,1344]{2,1,0:T(8,128)(2,1)S(1)}, bf16[1,928,1344]{2,1,0:T(8,128)(2,1)S(1)}) custom-call(bf16[32,1344]{1,0:T(8,128)(2,1)S(1)} %get-tuple-element.57.after_ref.rest_0_, bf16[1,928,1344]{2,1,0:T(8,128)(2,1)} %bitcast.10, bf16[1,928,1344]{2,1,0:T(8,128)(2,1)} %down_hbm.1), custom_call_target="tpu_custom_call" | custom-call | tf_op jit(solution)/shard_map/weights/pallas_call | solution.py:29
  27.4 1.4 %collective-permute-done.9.rest_3_ = bf16[32,1344]{1,0:T(8,128)(2,1)S(1)} collective-permute-done((bf16[32,1344]{1,0:T(8,128)(2,1)S(1)}, bf16[32,1344]{1,0:T(8,128)(2,1)S(1)}, u32[]{:S(2)}, u32[]{:S(2)}) %collective-permute-start.9) | collective-permute-done | bytes 86048 | tf_op jit(solution)/shard_map/ppermute | solution.py:373
  28.8 0.2 rows.1
  29.0 1.5 %collective-permute-start.13 = (bf16[32,1408]{1,0:T(8,128)(2,1)S(1)}, bf16[32,1408]{1,0:T(8,128)(2,1)S(1)}, u32[]{:S(2)}, u32[]{:S(2)}) collective-permute-start(bf16[32,1408]{1,0:T(8,128)(2,1)S(1)} %get-tuple-element.66.rest_0_), channel_id=1, source_target_pairs={{0,8},{4,12},{8,0},{12,4},{1,9},{5,13},{9,1},{13,5},{2,10},{6,14},... | collective-permute-start | bytes 270344 | tf_op jit(solution)/shard_map/ppermute | solution.py:363
  30.5 3.3 %collective-permute-start.12 = (bf16[32,1408]{1,0:T(8,128)(2,1)S(1)}, bf16[32,1408]{1,0:T(8,128)(2,1)S(1)}, u32[]{:S(2)}, u32[]{:S(2)}) collective-permute-start(bf16[32,1408]{1,0:T(8,128)(2,1)S(1)} %get-tuple-element.66.rest_0_), channel_id=1, source_target_pairs={{0,6},{1,7},{2,4},{3,5},{4,2},{5,3},{6,0},{7,1},{8,14},{9,15},{10,... | collective-permute-start | bytes 270344 | tf_op jit(solution)/shard_map/ppermute | solution.py:363
  33.8 0.6 %collective-permute-start.10 = (bf16[32,1408]{1,0:T(8,128)(2,1)S(1)}, bf16[32,1408]{1,0:T(8,128)(2,1)S(1)}, u32[]{:S(2)}, u32[]{:S(2)}) collective-permute-start(bf16[32,1408]{1,0:T(8,128)(2,1)S(1)} %get-tuple-element.66.rest_0_), channel_id=1, source_target_pairs={{0,2},{1,3},{2,0},{3,1},{4,6},{5,7},{6,4},{7,5},{8,10},{9,11},{10,... | collective-permute-start | bytes 270344 | tf_op jit(solution)/shard_map/ppermute | solution.py:363
  34.4 0.1 collective-permute-done.13.rest_0_
  34.6 2.7 %collective-permute-start.16 = (bf16[32,1408]{1,0:T(8,128)(2,1)S(1)}, bf16[32,1408]{1,0:T(8,128)(2,1)S(1)}, u32[]{:S(2)}, u32[]{:S(2)}) collective-permute-start(bf16[32,1408]{1,0:T(8,128)(2,1)S(1)} %collective-permute-done.13.rest_0_), channel_id=1, source_target_pairs={{0,6},{1,7},{2,4},{3,5},{4,2},{5,3},{6,0},{7,1},{8,14},{9,15},{10,... | collective-permute-start | bytes 270344 | tf_op jit(solution)/shard_map/ppermute | solution.py:363
  37.3 1.1 %collective-permute-start.15 = (bf16[32,1408]{1,0:T(8,128)(2,1)S(1)}, bf16[32,1408]{1,0:T(8,128)(2,1)S(1)}, u32[]{:S(2)}, u32[]{:S(2)}) collective-permute-start(bf16[32,1408]{1,0:T(8,128)(2,1)S(1)} %collective-permute-done.13.rest_0_), channel_id=1, source_target_pairs={{0,4},{1,5},{2,6},{3,7},{4,0},{5,1},{6,2},{7,3},{8,12},{9,13},{10,... | collective-permute-start | bytes 270344 | tf_op jit(solution)/shard_map/ppermute | solution.py:363
  38.4 0.9 %collective-permute-done.11.rest_2_ = bf16[32,1408]{1,0:T(8,128)(2,1)S(1)} collective-permute-done((bf16[32,1408]{1,0:T(8,128)(2,1)S(1)}, bf16[32,1408]{1,0:T(8,128)(2,1)S(1)}, u32[]{:S(2)}, u32[]{:S(2)}) %collective-permute-start.11) | collective-permute-done | bytes 90144 | tf_op jit(solution)/shard_map/ppermute | solution.py:363
  39.4 1.5 %collective-permute-done.10.rest_1_ = bf16[32,1408]{1,0:T(8,128)(2,1)S(1)} collective-permute-done((bf16[32,1408]{1,0:T(8,128)(2,1)S(1)}, bf16[32,1408]{1,0:T(8,128)(2,1)S(1)}, u32[]{:S(2)}, u32[]{:S(2)}) %collective-permute-start.10) | collective-permute-done | bytes 90144 | tf_op jit(solution)/shard_map/ppermute | solution.py:363
  40.9 2.7 %experts.2 = (bf16[32,1344]{1,0:T(8,128)(2,1)S(1)}, bf16[32,1344]{1,0:T(8,128)(2,1)S(1)}, bf16[32,1344]{1,0:T(8,128)(2,1)S(1)}, bf16[32,1344]{1,0:T(8,128)(2,1)S(1)}) custom-call(bf16[1,928,1344]{2,1,0:T(8,128)(2,1)S(1)} %get-tuple-element.58.after_ref.up_ref, bf16[1,928,1344]{2,1,0:T(8,128)(2,1)S(1)} %get-tuple-element.65.down_ref, ...), custom_call_target="tpu_custom_call" | custom-call | tf_op jit(solution)/shard_map/experts/pallas_call | solution.py:29
  43.7 2.7 %experts.3 = (bf16[32,1344]{1,0:T(8,128)(2,1)S(1)}, bf16[32,1344]{1,0:T(8,128)(2,1)S(1)}, bf16[64,1344]{1,0:T(8,128)(2,1)S(1)}, bf16[32,1344]{1,0:T(8,128)(2,1)S(1)}) custom-call(bf16[1,928,1344]{2,1,0:T(8,128)(2,1)S(1)} %get-tuple-element.58.after_ref.up_ref, bf16[1,928,1344]{2,1,0:T(8,128)(2,1)S(1)} %get-tuple-element.65.down_ref, ...), custom_call_target="tpu_custom_call" | custom-call | tf_op jit(solution)/shard_map/experts/pallas_call | solution.py:29
  46.4 0.3 collective-permute-start.17
  46.7 1.4 %collective-permute-start.18 = (bf16[32,1344]{1,0:T(8,128)(2,1)S(1)}, bf16[32,1344]{1,0:T(8,128)(2,1)S(1)}, u32[]{:S(2)}, u32[]{:S(2)}) collective-permute-start(bf16[32,1344]{1,0:T(8,128)(2,1)S(1)} %get-tuple-element.79), channel_id=1, source_target_pairs={{0,2},{1,3},{2,0},{3,1},{4,6},{5,7},{6,4},{7,5},{8,10},{9,11},{10,... | collective-permute-start | bytes 258056 | tf_op jit(solution)/shard_map/ppermute | solution.py:363
  48.1 1.8 %collective-permute-start.19 = (bf16[32,1344]{1,0:T(8,128)(2,1)S(1)}, bf16[32,1344]{1,0:T(8,128)(2,1)S(1)}, u32[]{:S(2)}, u32[]{:S(2)}) collective-permute-start(bf16[32,1344]{1,0:T(8,128)(2,1)S(1)} %get-tuple-element.80), channel_id=1, source_target_pairs={{0,6},{1,7},{2,4},{3,5},{4,2},{5,3},{6,0},{7,1},{8,14},{9,15},{10,... | collective-permute-start | bytes 258056 | tf_op jit(solution)/shard_map/ppermute | solution.py:363
  49.9 1.1 %collective-permute-start.21 = (bf16[32,1344]{1,0:T(8,128)(2,1)S(1)}, bf16[32,1344]{1,0:T(8,128)(2,1)S(1)}, u32[]{:S(2)}, u32[]{:S(2)}) collective-permute-start(bf16[32,1344]{1,0:T(8,128)(2,1)S(1)} %get-tuple-element.81), channel_id=1, source_target_pairs={{0,6},{1,7},{2,4},{3,5},{4,2},{5,3},{6,0},{7,1},{8,14},{9,15},{10,... | collective-permute-start | bytes 258056 | tf_op jit(solution)/shard_map/ppermute | solution.py:363
  51.1 0.6 %collective-permute-start.22 = (bf16[32,1344]{1,0:T(8,128)(2,1)S(1)}, bf16[32,1344]{1,0:T(8,128)(2,1)S(1)}, u32[]{:S(2)}, u32[]{:S(2)}) collective-permute-start(bf16[32,1344]{1,0:T(8,128)(2,1)S(1)} %get-tuple-element.82), channel_id=1, source_target_pairs={{0,2},{1,3},{2,0},{3,1},{4,6},{5,7},{6,4},{7,5},{8,10},{9,11},{10,... | collective-permute-start | bytes 258056 | tf_op jit(solution)/shard_map/ppermute | solution.py:363
  51.7 0.9 %collective-permute-done.18.refs_1_ = bf16[32,1344]{1,0:T(8,128)(2,1)S(1)} collective-permute-done((bf16[32,1344]{1,0:T(8,128)(2,1)S(1)}, bf16[32,1344]{1,0:T(8,128)(2,1)S(1)}, u32[]{:S(2)}, u32[]{:S(2)}) %collective-permute-start.18) | collective-permute-done | bytes 86048 | tf_op jit(solution)/shard_map/ppermute | solution.py:363
  52.5 1.0 %collective-permute-done.19.refs_3_ = bf16[32,1344]{1,0:T(8,128)(2,1)S(1)} collective-permute-done((bf16[32,1344]{1,0:T(8,128)(2,1)S(1)}, bf16[32,1344]{1,0:T(8,128)(2,1)S(1)}, u32[]{:S(2)}, u32[]{:S(2)}) %collective-permute-start.19) | collective-permute-done | bytes 86048 | tf_op jit(solution)/shard_map/ppermute | solution.py:363
  53.6 2.1 %collective-permute-start.20 = (bf16[32,1344]{1,0:T(8,128)(2,1)S(1)}, bf16[32,1344]{1,0:T(8,128)(2,1)S(1)}, u32[]{:S(2)}, u32[]{:S(2)}) collective-permute-start(bf16[32,1344]{1,0:T(8,128)(2,1)S(1)} %sum.1), channel_id=1, source_target_pairs={{0,8},{4,12},{8,0},{12,4},{1,9},{5,13},{9,1},{13,5},{2,10},{6,14},... | collective-permute-start | bytes 258056 | tf_op jit(solution)/shard_map/ppermute | solution.py:363
  55.7 0.1 collective-permute-done.21.rest_3_
  55.9 0.6 collective-permute-done.22.rest_4_
  56.4 2.7 %collective-permute-done.20.rest_2_ = bf16[32,1344]{1,0:T(8,128)(2,1)S(1)} collective-permute-done((bf16[32,1344]{1,0:T(8,128)(2,1)S(1)}, bf16[32,1344]{1,0:T(8,128)(2,1)S(1)}, u32[]{:S(2)}, u32[]{:S(2)}) %collective-permute-start.20) | collective-permute-done | bytes 86048 | tf_op jit(solution)/shard_map/ppermute | solution.py:363
  59.1 0.7 %last.1 = bf16[1,32,1344]{2,1,0:T(8,128)(2,1)} custom-call(bf16[32,1344]{1,0:T(8,128)(2,1)S(1)} %get-tuple-element.64.hidden_ref, bf16[32,1344]{1,0:T(8,128)(2,1)S(1)} %get-tuple-element.71.rest_0_, bf16[64,1344]{1,0:T(8,128)(2,1)S(1)} %collective-permute-done.17.refs_2_.rest_1_, bf16[32,1344]{1,0:T(8,128)(2,1)S(1)} %collective-permute-done.20.rest_2_, ...), custom_call_target="tpu_custom_call" | custom-call | tf_op jit(solution)/shard_map/last/pallas_call | solution.py:29
  (13 shorter events, 0.1 us)
Async XLA Ops:
  1.8 1.5 %collective-permute-start = (bf16[528,128]{1,0:T(8,128)(2,1)S(1)}, bf16[528,128]{1,0:T(8,128)(2,1)S(1)}, u32[]{:S(2)}, u32[]{:S(2)}) collective-permute-start(bf16[528,128]{1,0:T(8,128)(2,1)S(1)} %get-tuple-element.46), channel_id=1, source_target_pairs={{0,1},{1,0},{2,3},{3,2},{4,5},{5,4},{6,7},{7,6},{8,9},{9,8},{10,11... | collective-permute-start | bytes 405512 | tf_op jit(solution)/shard_map/ppermute | solution.py:363
  3.4 13.2 %collective-permute-start.1 = (bf16[1,928,1344]{2,1,0:T(8,128)(2,1)}, bf16[1,928,1344]{2,1,0:T(8,128)(2,1)S(1)}, u32[]{:S(2)}, u32[]{:S(2)}) collective-permute-start(bf16[1,928,1344]{2,1,0:T(8,128)(2,1)} %bitcast.9), channel_id=1, source_target_pairs={{0,1},{1,0},{2,3},{3,2},{4,5},{5,4},{6,7},{7,6},{8,9},{9,8},{10,11... | collective-permute-start | bytes 7483400 | tf_op jit(solution)/shard_map/ppermute | solution.py:363
  3.9 12.8 %collective-permute-start.2 = (bf16[1,928,1344]{2,1,0:T(8,128)(2,1)}, bf16[1,928,1344]{2,1,0:T(8,128)(2,1)S(1)}, u32[]{:S(2)}, u32[]{:S(2)}) collective-permute-start(bf16[1,928,1344]{2,1,0:T(8,128)(2,1)} %down_hbm.1), channel_id=1, source_target_pairs={{0,1},{1,0},{2,3},{3,2},{4,5},{5,4},{6,7},{7,6},{8,9},{9,8},{10,11... | collective-permute-start | bytes 7483400 | tf_op jit(solution)/shard_map/ppermute | solution.py:363
  4.0 8.6 %collective-permute-start.5 = (bf16[528,128]{1,0:T(8,128)(2,1)S(1)}, bf16[528,128]{1,0:T(8,128)(2,1)S(1)}, u32[]{:S(2)}, u32[]{:S(2)}) collective-permute-start(bf16[528,128]{1,0:T(8,128)(2,1)S(1)} %chip_state.1.rest_0_), channel_id=1, source_target_pairs={{0,18},{1,19},{2,16},{3,17},{16,2},{17,3},{18,0},{19,1},{4,22},{5,... | collective-permute-start | bytes 405512 | tf_op jit(solution)/shard_map/ppermute | solution.py:363
  7.8 7.1 %collective-permute-start.4 = (bf16[528,128]{1,0:T(8,128)(2,1)S(1)}, bf16[528,128]{1,0:T(8,128)(2,1)S(1)}, u32[]{:S(2)}, u32[]{:S(2)}) collective-permute-start(bf16[528,128]{1,0:T(8,128)(2,1)S(1)} %chip_state.1.rest_0_), channel_id=1, source_target_pairs={{0,16},{1,17},{2,18},{3,19},{16,0},{17,1},{18,2},{19,3},{4,20},{5,... | collective-permute-start | bytes 405512 | tf_op jit(solution)/shard_map/ppermute | solution.py:363
  8.4 6.5 %collective-permute-start.3 = (bf16[528,128]{1,0:T(8,128)(2,1)S(1)}, bf16[528,128]{1,0:T(8,128)(2,1)S(1)}, u32[]{:S(2)}, u32[]{:S(2)}) collective-permute-start(bf16[528,128]{1,0:T(8,128)(2,1)S(1)} %chip_state.1.rest_0_), channel_id=1, source_target_pairs={{0,2},{1,3},{2,0},{3,1},{16,18},{17,19},{18,16},{19,17},{4,6},{5,7... | collective-permute-start | bytes 405512 | tf_op jit(solution)/shard_map/ppermute | solution.py:363
  15.2 1.4 %collective-permute-start.6 = (bf16[4,128,128]{2,1,0:T(8,128)(2,1)S(1)}, bf16[4,128,128]{2,1,0:T(8,128)(2,1)S(1)}, u32[]{:S(2)}, u32[]{:S(2)}) collective-permute-start(bf16[4,128,128]{2,1,0:T(8,128)(2,1)S(1)} %get-tuple-element.55), channel_id=1, source_target_pairs={{0,1},{1,0},{2,3},{3,2},{4,5},{5,4},{6,7},{7,6},{8,9},{9,8},{10,11... | collective-permute-start | bytes 393224 | tf_op jit(solution)/shard_map/ppermute | solution.py:363
  17.5 5.6 %collective-permute-start.7 = (bf16[32,1344]{1,0:T(8,128)(2,1)S(1)}, bf16[32,1344]{1,0:T(8,128)(2,1)S(1)}, u32[]{:S(2)}, u32[]{:S(2)}) collective-permute-start(bf16[32,1344]{1,0:T(8,128)(2,1)S(1)} %get-tuple-element.61), channel_id=1, source_target_pairs={{0,4},{1,9},{2,6},{3,11},{4,0},{5,13},{6,2},{7,15},{8,12},{9,1},{1... | collective-permute-start | bytes 258056 | tf_op jit(solution)/shard_map/ppermute | solution.py:373
  19.1 8.2 %collective-permute-start.8 = (bf16[32,1344]{1,0:T(8,128)(2,1)S(1)}, bf16[32,1344]{1,0:T(8,128)(2,1)S(1)}, u32[]{:S(2)}, u32[]{:S(2)}) collective-permute-start(bf16[32,1344]{1,0:T(8,128)(2,1)S(1)} %get-tuple-element.62), channel_id=1, source_target_pairs={{0,4},{1,13},{2,6},{3,15},{4,0},{5,9},{6,2},{7,11},{8,12},{9,5},{1... | collective-permute-start | bytes 258056 | tf_op jit(solution)/shard_map/ppermute | solution.py:373
  23.1 5.7 %collective-permute-start.9 = (bf16[32,1344]{1,0:T(8,128)(2,1)S(1)}, bf16[32,1344]{1,0:T(8,128)(2,1)S(1)}, u32[]{:S(2)}, u32[]{:S(2)}) collective-permute-start(bf16[32,1344]{1,0:T(8,128)(2,1)S(1)} %relay.1), channel_id=1, source_target_pairs={{0,8},{1,5},{2,10},{3,7},{4,12},{5,1},{6,14},{7,3},{8,0},{9,13},{1... | collective-permute-start | bytes 258056 | tf_op jit(solution)/shard_map/ppermute | solution.py:373
  29.0 5.6 %collective-permute-start.13 = (bf16[32,1408]{1,0:T(8,128)(2,1)S(1)}, bf16[32,1408]{1,0:T(8,128)(2,1)S(1)}, u32[]{:S(2)}, u32[]{:S(2)}) collective-permute-start(bf16[32,1408]{1,0:T(8,128)(2,1)S(1)} %get-tuple-element.66.rest_0_), channel_id=1, source_target_pairs={{0,8},{4,12},{8,0},{12,4},{1,9},{5,13},{9,1},{13,5},{2,10},{6,14},... | collective-permute-start | bytes 270344 | tf_op jit(solution)/shard_map/ppermute | solution.py:363
  30.5 7.9 %collective-permute-start.12 = (bf16[32,1408]{1,0:T(8,128)(2,1)S(1)}, bf16[32,1408]{1,0:T(8,128)(2,1)S(1)}, u32[]{:S(2)}, u32[]{:S(2)}) collective-permute-start(bf16[32,1408]{1,0:T(8,128)(2,1)S(1)} %get-tuple-element.66.rest_0_), channel_id=1, source_target_pairs={{0,6},{1,7},{2,4},{3,5},{4,2},{5,3},{6,0},{7,1},{8,14},{9,15},{10,... | collective-permute-start | bytes 270344 | tf_op jit(solution)/shard_map/ppermute | solution.py:363
  33.8 5.6 %collective-permute-start.11 = (bf16[32,1408]{1,0:T(8,128)(2,1)S(1)}, bf16[32,1408]{1,0:T(8,128)(2,1)S(1)}, u32[]{:S(2)}, u32[]{:S(2)}) collective-permute-start(bf16[32,1408]{1,0:T(8,128)(2,1)S(1)} %get-tuple-element.66.rest_0_), channel_id=1, source_target_pairs={{0,4},{1,5},{2,6},{3,7},{4,0},{5,1},{6,2},{7,3},{8,12},{9,13},{10,... | collective-permute-start | bytes 270344 | tf_op jit(solution)/shard_map/ppermute | solution.py:363
  33.8 7.1 %collective-permute-start.10 = (bf16[32,1408]{1,0:T(8,128)(2,1)S(1)}, bf16[32,1408]{1,0:T(8,128)(2,1)S(1)}, u32[]{:S(2)}, u32[]{:S(2)}) collective-permute-start(bf16[32,1408]{1,0:T(8,128)(2,1)S(1)} %get-tuple-element.66.rest_0_), channel_id=1, source_target_pairs={{0,2},{1,3},{2,0},{3,1},{4,6},{5,7},{6,4},{7,5},{8,10},{9,11},{10,... | collective-permute-start | bytes 270344 | tf_op jit(solution)/shard_map/ppermute | solution.py:363
  34.6 9.1 %collective-permute-start.16 = (bf16[32,1408]{1,0:T(8,128)(2,1)S(1)}, bf16[32,1408]{1,0:T(8,128)(2,1)S(1)}, u32[]{:S(2)}, u32[]{:S(2)}) collective-permute-start(bf16[32,1408]{1,0:T(8,128)(2,1)S(1)} %collective-permute-done.13.rest_0_), channel_id=1, source_target_pairs={{0,6},{1,7},{2,4},{3,5},{4,2},{5,3},{6,0},{7,1},{8,14},{9,15},{10,... | collective-permute-start | bytes 270344 | tf_op jit(solution)/shard_map/ppermute | solution.py:363
  37.3 6.3 %collective-permute-start.15 = (bf16[32,1408]{1,0:T(8,128)(2,1)S(1)}, bf16[32,1408]{1,0:T(8,128)(2,1)S(1)}, u32[]{:S(2)}, u32[]{:S(2)}) collective-permute-start(bf16[32,1408]{1,0:T(8,128)(2,1)S(1)} %collective-permute-done.13.rest_0_), channel_id=1, source_target_pairs={{0,4},{1,5},{2,6},{3,7},{4,0},{5,1},{6,2},{7,3},{8,12},{9,13},{10,... | collective-permute-start | bytes 270344 | tf_op jit(solution)/shard_map/ppermute | solution.py:363
  38.4 5.2 %collective-permute-start.14 = (bf16[32,1408]{1,0:T(8,128)(2,1)S(1)}, bf16[32,1408]{1,0:T(8,128)(2,1)S(1)}, u32[]{:S(2)}, u32[]{:S(2)}) collective-permute-start(bf16[32,1408]{1,0:T(8,128)(2,1)S(1)} %collective-permute-done.13.rest_0_), channel_id=1, source_target_pairs={{0,2},{1,3},{2,0},{3,1},{4,6},{5,7},{6,4},{7,5},{8,10},{9,11},{10,... | collective-permute-start | bytes 270344 | tf_op jit(solution)/shard_map/ppermute | solution.py:363
  46.4 7.2 %collective-permute-start.17 = (bf16[64,1344]{1,0:T(8,128)(2,1)S(1)}, bf16[64,1344]{1,0:T(8,128)(2,1)S(1)}, u32[]{:S(2)}, u32[]{:S(2)}) collective-permute-start(bf16[64,1344]{1,0:T(8,128)(2,1)S(1)} %get-tuple-element.77), channel_id=1, source_target_pairs={{0,4},{1,5},{2,6},{3,7},{4,0},{5,1},{6,2},{7,3},{8,12},{9,13},{10,... | collective-permute-start | bytes 516104 | tf_op jit(solution)/shard_map/ppermute | solution.py:363
  46.7 5.8 %collective-permute-start.18 = (bf16[32,1344]{1,0:T(8,128)(2,1)S(1)}, bf16[32,1344]{1,0:T(8,128)(2,1)S(1)}, u32[]{:S(2)}, u32[]{:S(2)}) collective-permute-start(bf16[32,1344]{1,0:T(8,128)(2,1)S(1)} %get-tuple-element.79), channel_id=1, source_target_pairs={{0,2},{1,3},{2,0},{3,1},{4,6},{5,7},{6,4},{7,5},{8,10},{9,11},{10,... | collective-permute-start | bytes 258056 | tf_op jit(solution)/shard_map/ppermute | solution.py:363
  48.1 5.4 %collective-permute-start.19 = (bf16[32,1344]{1,0:T(8,128)(2,1)S(1)}, bf16[32,1344]{1,0:T(8,128)(2,1)S(1)}, u32[]{:S(2)}, u32[]{:S(2)}) collective-permute-start(bf16[32,1344]{1,0:T(8,128)(2,1)S(1)} %get-tuple-element.80), channel_id=1, source_target_pairs={{0,6},{1,7},{2,4},{3,5},{4,2},{5,3},{6,0},{7,1},{8,14},{9,15},{10,... | collective-permute-start | bytes 258056 | tf_op jit(solution)/shard_map/ppermute | solution.py:363
  49.9 5.9 %collective-permute-start.21 = (bf16[32,1344]{1,0:T(8,128)(2,1)S(1)}, bf16[32,1344]{1,0:T(8,128)(2,1)S(1)}, u32[]{:S(2)}, u32[]{:S(2)}) collective-permute-start(bf16[32,1344]{1,0:T(8,128)(2,1)S(1)} %get-tuple-element.81), channel_id=1, source_target_pairs={{0,6},{1,7},{2,4},{3,5},{4,2},{5,3},{6,0},{7,1},{8,14},{9,15},{10,... | collective-permute-start | bytes 258056 | tf_op jit(solution)/shard_map/ppermute | solution.py:363
  51.1 5.4 %collective-permute-start.22 = (bf16[32,1344]{1,0:T(8,128)(2,1)S(1)}, bf16[32,1344]{1,0:T(8,128)(2,1)S(1)}, u32[]{:S(2)}, u32[]{:S(2)}) collective-permute-start(bf16[32,1344]{1,0:T(8,128)(2,1)S(1)} %get-tuple-element.82), channel_id=1, source_target_pairs={{0,2},{1,3},{2,0},{3,1},{4,6},{5,7},{6,4},{7,5},{8,10},{9,11},{10,... | collective-permute-start | bytes 258056 | tf_op jit(solution)/shard_map/ppermute | solution.py:363
  53.6 5.5 %collective-permute-start.20 = (bf16[32,1344]{1,0:T(8,128)(2,1)S(1)}, bf16[32,1344]{1,0:T(8,128)(2,1)S(1)}, u32[]{:S(2)}, u32[]{:S(2)}) collective-permute-start(bf16[32,1344]{1,0:T(8,128)(2,1)S(1)} %sum.1), channel_id=1, source_target_pairs={{0,8},{4,12},{8,0},{12,4},{1,9},{5,13},{9,1},{13,5},{2,10},{6,14},... | collective-permute-start | bytes 258056 | tf_op jit(solution)/shard_map/ppermute | solution.py:363

commit v25 on v24

--- a/solution.py
+++ b/solution.py
@@ -508,8 +508,8 @@
         return [block] + [swap(block, both, mask) for mask in group]
 
     sets = [spread(swap(own_rows, "head", high)) for high in range(2, head_size, 2)]
-    near = through_experts(spread(own_rows))
-    near, sets = lax.optimization_barrier((near, sets))
+    near = through_experts([own_rows] + [swap(own_rows, both, mask) for mask in group[::-1]])
+    near, sets = lax.optimization_barrier(([near[0], *near[:0:-1]], sets))
     joined = [at for at, mask in enumerate(group, 1) if mask == exp_size]
     arrived, later = [], [at for at, mask in enumerate(group, 1) if mask < exp_size]
     apart = [near[at] for at in later]

time: 60.1 us -> 62.2 us (1.035)
  waiting for transfers between devices: 15.6 us -> 18 us
    ppermute x20, waiting for transfers between devices: 10.7 us -> 13.1 us  [swap(): return lax.ppermute(value, axis, [(i, i ^ mask) for i in range(size)])]
  transfers between devices with their start and end apart: 23 -> 23, of which waited for: 12 -> 9; matrix products, arithmetic and copies ran while one was open for 0% -> 0% of each run, Pallas kernels for 20% -> 19%
where the time goes in v25:
time: 62.2 us; the launch traced here: 61.8 us
  starting transfers between devices  25.6 us (41%)
  Pallas kernels  18.1 us (29%)
  waiting for transfers between devices  18 us (29%)
    ppermute x20, starting transfers between devices, swap(): return lax.ppermute(value, axis, [(i, i ^ mask) for i in range(size)])  21.8 us
    pallas_call x15, Pallas kernels, call(): pl.pallas_call(kernel, out_shape=jax.tree.map(lambda out: pltpu.VMEM(out....  18.1 us
    ppermute x20, waiting for transfers between devices, swap(): return lax.ppermute(value, axis, [(i, i ^ mask) for i in range(size)])  13.1 us
    ppermute x3, waiting for transfers between devices, swap_slot(): return lax.ppermute(value, ('head', 'exp'), pairs)  4.89 us
    ppermute x3, starting transfers between devices, swap_slot(): return lax.ppermute(value, ('head', 'exp'), pairs)  3.79 us
  transfers between devices with their start and end apart: 23, of which 9 were waited for; matrix products, arithmetic and copies ran while one was open for 0% of the time, Pallas kernels for 19%

profile of v25, /device:TPU:0, one launch (start us, length us, event | category | flops | bytes accessed | tf_op | source)
XLA Modules:
  0.0 61.8 jit_solution(15725412056352490523)
XLA Ops:
  0.0 1.8 %state.1 = (bf16[528,128]{1,0:T(8,128)(2,1)S(1)}, bf16[528,128]{1,0:T(8,128)(2,1)S(1)}) custom-call(bf16[128,1024]{1,0:T(8,128)(2,1)} %x_hbm.3, bf16[128,256]{1,0:T(8,128)(2,1)} %b_hbm.3, f32[16,128]{1,0:T(8,128)} %bitcast.11, f32[1,16]{1,0:T(1,128)} %bitcast.16), custom_call_target="tpu_custom_call" | custom-call | tf_op jit(solution)/shard_map/state/pallas_call | solution.py:29
  1.8 0.5 collective-permute-start
  2.4 1.0 %prep.1 = (bf16[32,128]{1,0:T(8,128)(2,1)S(1)}, bf16[1,32,1344]{2,1,0:T(8,128)(2,1)S(1)}, f32[1,1344]{1,0:T(1,128)S(1)}) custom-call(bf16[528,128]{1,0:T(8,128)(2,1)S(1)} %get-tuple-element.44.after_ref.keep_ref, bf16[1,32,1344]{2,1,0:T(8,128)(2,1)} %resid_hbm.1, s32[6,1,32]{2,1,0:T(1,128)} %bitcast.14, f32[6,1,32]{2,1,0:T(1,128)} %bitcast.15, f32[1344]{0:T(1024)} %gain_hbm.1), custom_call_target="tpu_custom_call" | custom-call | tf_op jit(solution)/shard_map/prep/pallas_call | solution.py:29
  3.3 0.0 collective-permute-done.got_ref
  3.3 0.1 chip_state.1.rest_0_
  3.4 0.4 collective-permute-start.1
  3.9 0.1 collective-permute-start.2
  4.0 3.8 %collective-permute-start.5 = (bf16[528,128]{1,0:T(8,128)(2,1)S(1)}, bf16[528,128]{1,0:T(8,128)(2,1)S(1)}, u32[]{:S(2)}, u32[]{:S(2)}) collective-permute-start(bf16[528,128]{1,0:T(8,128)(2,1)S(1)} %chip_state.1.rest_0_), channel_id=1, source_target_pairs={{0,18},{1,19},{2,16},{3,17},{16,2},{17,3},{18,0},{19,1},{4,22},{5,... | collective-permute-start | bytes 405512 | tf_op jit(solution)/shard_map/ppermute | solution.py:363
  7.8 0.5 collective-permute-start.4
  8.4 0.0 collective-permute-start.3
  8.4 1.8 %projection.1 = (f32[1,1024]{1,0:T(1,128)S(1)}, bf16[1344,1024]{1,0:T(8,128)(2,1)S(1)}) custom-call(f32[1,1024]{1,0:T(1,128)} %bitcast.13, bf16[1344,1024]{1,0:T(8,128)(2,1)} %bitcast.8), custom_call_target="tpu_custom_call" | custom-call | tf_op jit(solution)/shard_map/projection/pallas_call | solution.py:29
  10.2 2.4 %inside.1 = (f32[128,1024]{1,0:T(8,128)S(1)}, f32[128,1024]{1,0:T(8,128)S(1)}, bf16[128,256]{1,0:T(8,128)(2,1)S(1)}) custom-call(bf16[128,1024]{1,0:T(8,128)(2,1)} %x_hbm.3, bf16[128,1024]{1,0:T(8,128)(2,1)} %z_hbm.1, bf16[128,256]{1,0:T(8,128)(2,1)} %b_hbm.3, bf16[128,256]{1,0:T(8,128)(2,1)} %c_hbm.1, f32[16,128]{1,0:T(8,128)} %bitcast.12, ...), custom_call_target="tpu_custom_call" | custom-call | tf_op jit(solution)/shard_map/inside/pallas_call | solution.py:29
  12.7 2.2 %collective-permute-done.4.rest_2_ = bf16[528,128]{1,0:T(8,128)(2,1)S(1)} collective-permute-done((bf16[528,128]{1,0:T(8,128)(2,1)S(1)}, bf16[528,128]{1,0:T(8,128)(2,1)S(1)}, u32[]{:S(2)}, u32[]{:S(2)}) %collective-permute-start.4) | collective-permute-done | bytes 135200 | tf_op jit(solution)/shard_map/ppermute | solution.py:363
  14.9 0.0 collective-permute-done.3.rest_1_
  14.9 0.3 before.1
  15.2 0.1 collective-permute-start.6
  15.3 0.8 %first_half.1.first_ref = f32[128,1344]{1,0:T(8,128)S(1)} custom-call(f32[128,1024]{1,0:T(8,128)S(1)} %get-tuple-element.49.local_ref, f32[128,1024]{1,0:T(8,128)S(1)} %get-tuple-element.50.grown_ref, bf16[128,256]{1,0:T(8,128)(2,1)S(1)} %get-tuple-element.51.after_b.c_ref, f32[1,1024]{1,0:T(1,128)S(1)} %get-tuple-element.52.after_a.norm_ref, ...), custom_call_target="tpu_custom_call" | custom-call | tf_op jit(solution)/shard_map/first_half/pallas_call | solution.py:29
  16.1 0.5 collective-permute-done.6.got_ref
  16.6 0.0 collective-permute-done.1.after_up.other_up_ref
  16.6 0.9 %mixed.1 = (bf16[32,1344]{1,0:T(8,128)(2,1)S(1)}, bf16[32,1344]{1,0:T(8,128)(2,1)S(1)}, bf16[32,1344]{1,0:T(8,128)(2,1)S(1)}, bf16[32,1344]{1,0:T(8,128)(2,1)S(1)}) custom-call(bf16[1,928,1344]{2,1,0:T(8,128)(2,1)S(1)} %collective-permute-done.1.after_up.other_up_ref, bf16[1,928,1344]{2,1,0:T(8,128)(2,1)S(1)} %collective-permute-done.2.after_down.other_down_ref, ...), custom_call_target="tpu_custom_call" | custom-call | tf_op jit(solution)/shard_map/mixed/pallas_call | solution.py:29
  17.5 1.6 %collective-permute-start.7 = (bf16[32,1344]{1,0:T(8,128)(2,1)S(1)}, bf16[32,1344]{1,0:T(8,128)(2,1)S(1)}, u32[]{:S(2)}, u32[]{:S(2)}) collective-permute-start(bf16[32,1344]{1,0:T(8,128)(2,1)S(1)} %get-tuple-element.61), channel_id=1, source_target_pairs={{0,4},{1,9},{2,6},{3,11},{4,0},{5,13},{6,2},{7,15},{8,12},{9,1},{1... | collective-permute-start | bytes 258056 | tf_op jit(solution)/shard_map/ppermute | solution.py:373
  19.1 0.5 collective-permute-start.8
  19.6 3.5 %collective-permute-done.7.got_ref.rest_1_ = bf16[32,1344]{1,0:T(8,128)(2,1)S(1)} collective-permute-done((bf16[32,1344]{1,0:T(8,128)(2,1)S(1)}, bf16[32,1344]{1,0:T(8,128)(2,1)S(1)}, u32[]{:S(2)}, u32[]{:S(2)}) %collective-permute-start.7) | collective-permute-done | bytes 86048 | tf_op jit(solution)/shard_map/ppermute | solution.py:373
  23.1 1.7 %collective-permute-start.9 = (bf16[32,1344]{1,0:T(8,128)(2,1)S(1)}, bf16[32,1344]{1,0:T(8,128)(2,1)S(1)}, u32[]{:S(2)}, u32[]{:S(2)}) collective-permute-start(bf16[32,1344]{1,0:T(8,128)(2,1)S(1)} %relay.1), channel_id=1, source_target_pairs={{0,8},{1,5},{2,10},{3,7},{4,12},{5,1},{6,14},{7,3},{8,0},{9,13},{1... | collective-permute-start | bytes 258056 | tf_op jit(solution)/shard_map/ppermute | solution.py:373
  24.8 2.5 %weights.1 = (bf16[1,928,1344]{2,1,0:T(8,128)(2,1)S(1)}, bf16[1,928,1344]{2,1,0:T(8,128)(2,1)S(1)}) custom-call(bf16[32,1344]{1,0:T(8,128)(2,1)S(1)} %get-tuple-element.57.after_ref.rest_0_, bf16[1,928,1344]{2,1,0:T(8,128)(2,1)} %bitcast.10, bf16[1,928,1344]{2,1,0:T(8,128)(2,1)} %down_hbm.1), custom_call_target="tpu_custom_call" | custom-call | tf_op jit(solution)/shard_map/weights/pallas_call | solution.py:29
  27.4 1.4 %collective-permute-done.9.rest_3_ = bf16[32,1344]{1,0:T(8,128)(2,1)S(1)} collective-permute-done((bf16[32,1344]{1,0:T(8,128)(2,1)S(1)}, bf16[32,1344]{1,0:T(8,128)(2,1)S(1)}, u32[]{:S(2)}, u32[]{:S(2)}) %collective-permute-start.9) | collective-permute-done | bytes 86048 | tf_op jit(solution)/shard_map/ppermute | solution.py:373
  28.8 0.2 rows.1
  29.0 1.5 %collective-permute-start.13 = (bf16[32,1408]{1,0:T(8,128)(2,1)S(1)}, bf16[32,1408]{1,0:T(8,128)(2,1)S(1)}, u32[]{:S(2)}, u32[]{:S(2)}) collective-permute-start(bf16[32,1408]{1,0:T(8,128)(2,1)S(1)} %get-tuple-element.66.rest_0_), channel_id=1, source_target_pairs={{0,8},{4,12},{8,0},{12,4},{1,9},{5,13},{9,1},{13,5},{2,10},{6,14},... | collective-permute-start | bytes 270344 | tf_op jit(solution)/shard_map/ppermute | solution.py:363
  30.5 1.4 %collective-permute-start.12 = (bf16[32,1408]{1,0:T(8,128)(2,1)S(1)}, bf16[32,1408]{1,0:T(8,128)(2,1)S(1)}, u32[]{:S(2)}, u32[]{:S(2)}) collective-permute-start(bf16[32,1408]{1,0:T(8,128)(2,1)S(1)} %get-tuple-element.66.rest_0_), channel_id=1, source_target_pairs={{0,2},{1,3},{2,0},{3,1},{4,6},{5,7},{6,4},{7,5},{8,10},{9,11},{10,... | collective-permute-start | bytes 270344 | tf_op jit(solution)/shard_map/ppermute | solution.py:363
  31.9 2.4 %collective-permute-start.11 = (bf16[32,1408]{1,0:T(8,128)(2,1)S(1)}, bf16[32,1408]{1,0:T(8,128)(2,1)S(1)}, u32[]{:S(2)}, u32[]{:S(2)}) collective-permute-start(bf16[32,1408]{1,0:T(8,128)(2,1)S(1)} %get-tuple-element.66.rest_0_), channel_id=1, source_target_pairs={{0,4},{1,5},{2,6},{3,7},{4,0},{5,1},{6,2},{7,3},{8,12},{9,13},{10,... | collective-permute-start | bytes 270344 | tf_op jit(solution)/shard_map/ppermute | solution.py:363
  34.4 0.0 collective-permute-start.10
  34.4 0.2 collective-permute-done.13.rest_0_
  34.6 2.7 %collective-permute-start.16 = (bf16[32,1408]{1,0:T(8,128)(2,1)S(1)}, bf16[32,1408]{1,0:T(8,128)(2,1)S(1)}, u32[]{:S(2)}, u32[]{:S(2)}) collective-permute-start(bf16[32,1408]{1,0:T(8,128)(2,1)S(1)} %collective-permute-done.13.rest_0_), channel_id=1, source_target_pairs={{0,6},{1,7},{2,4},{3,5},{4,2},{5,3},{6,0},{7,1},{8,14},{9,15},{10,... | collective-permute-start | bytes 270344 | tf_op jit(solution)/shard_map/ppermute | solution.py:363
  37.3 0.2 collective-permute-start.15
  37.6 0.5 collective-permute-start.14
  38.1 2.2 %collective-permute-done.10.rest_1_ = bf16[32,1408]{1,0:T(8,128)(2,1)S(1)} collective-permute-done((bf16[32,1408]{1,0:T(8,128)(2,1)S(1)}, bf16[32,1408]{1,0:T(8,128)(2,1)S(1)}, u32[]{:S(2)}, u32[]{:S(2)}) %collective-permute-start.10) | collective-permute-done | bytes 90144 | tf_op jit(solution)/shard_map/ppermute | solution.py:363
  40.3 2.7 %experts.2 = (bf16[32,1344]{1,0:T(8,128)(2,1)S(1)}, bf16[32,1344]{1,0:T(8,128)(2,1)S(1)}, bf16[32,1344]{1,0:T(8,128)(2,1)S(1)}, bf16[32,1344]{1,0:T(8,128)(2,1)S(1)}) custom-call(bf16[1,928,1344]{2,1,0:T(8,128)(2,1)S(1)} %get-tuple-element.58.after_ref.up_ref, bf16[1,928,1344]{2,1,0:T(8,128)(2,1)S(1)} %get-tuple-element.65.down_ref, ...), custom_call_target="tpu_custom_call" | custom-call | tf_op jit(solution)/shard_map/experts/pallas_call | solution.py:29
  43.0 2.7 %experts.3 = (bf16[32,1344]{1,0:T(8,128)(2,1)S(1)}, bf16[32,1344]{1,0:T(8,128)(2,1)S(1)}, bf16[64,1344]{1,0:T(8,128)(2,1)S(1)}, bf16[32,1344]{1,0:T(8,128)(2,1)S(1)}) custom-call(bf16[1,928,1344]{2,1,0:T(8,128)(2,1)S(1)} %get-tuple-element.58.after_ref.up_ref, bf16[1,928,1344]{2,1,0:T(8,128)(2,1)S(1)} %get-tuple-element.65.down_ref, ...), custom_call_target="tpu_custom_call" | custom-call | tf_op jit(solution)/shard_map/experts/pallas_call | solution.py:29
  45.8 1.4 %collective-permute-start.17 = (bf16[64,1344]{1,0:T(8,128)(2,1)S(1)}, bf16[64,1344]{1,0:T(8,128)(2,1)S(1)}, u32[]{:S(2)}, u32[]{:S(2)}) collective-permute-start(bf16[64,1344]{1,0:T(8,128)(2,1)S(1)} %get-tuple-element.77), channel_id=1, source_target_pairs={{0,4},{1,5},{2,6},{3,7},{4,0},{5,1},{6,2},{7,3},{8,12},{9,13},{10,... | collective-permute-start | bytes 516104 | tf_op jit(solution)/shard_map/ppermute | solution.py:363
  47.1 1.4 %collective-permute-start.18 = (bf16[32,1344]{1,0:T(8,128)(2,1)S(1)}, bf16[32,1344]{1,0:T(8,128)(2,1)S(1)}, u32[]{:S(2)}, u32[]{:S(2)}) collective-permute-start(bf16[32,1344]{1,0:T(8,128)(2,1)S(1)} %get-tuple-element.79), channel_id=1, source_target_pairs={{0,2},{1,3},{2,0},{3,1},{4,6},{5,7},{6,4},{7,5},{8,10},{9,11},{10,... | collective-permute-start | bytes 258056 | tf_op jit(solution)/shard_map/ppermute | solution.py:363
  48.5 0.8 %collective-permute-start.19 = (bf16[32,1344]{1,0:T(8,128)(2,1)S(1)}, bf16[32,1344]{1,0:T(8,128)(2,1)S(1)}, u32[]{:S(2)}, u32[]{:S(2)}) collective-permute-start(bf16[32,1344]{1,0:T(8,128)(2,1)S(1)} %get-tuple-element.80), channel_id=1, source_target_pairs={{0,6},{1,7},{2,4},{3,5},{4,2},{5,3},{6,0},{7,1},{8,14},{9,15},{10,... | collective-permute-start | bytes 258056 | tf_op jit(solution)/shard_map/ppermute | solution.py:363
  49.3 2.2 %collective-permute-start.21 = (bf16[32,1344]{1,0:T(8,128)(2,1)S(1)}, bf16[32,1344]{1,0:T(8,128)(2,1)S(1)}, u32[]{:S(2)}, u32[]{:S(2)}) collective-permute-start(bf16[32,1344]{1,0:T(8,128)(2,1)S(1)} %get-tuple-element.81), channel_id=1, source_target_pairs={{0,6},{1,7},{2,4},{3,5},{4,2},{5,3},{6,0},{7,1},{8,14},{9,15},{10,... | collective-permute-start | bytes 258056 | tf_op jit(solution)/shard_map/ppermute | solution.py:363
  51.5 0.6 collective-permute-start.22
  52.1 2.9 %collective-permute-done.19.refs_3_ = bf16[32,1344]{1,0:T(8,128)(2,1)S(1)} collective-permute-done((bf16[32,1344]{1,0:T(8,128)(2,1)S(1)}, bf16[32,1344]{1,0:T(8,128)(2,1)S(1)}, u32[]{:S(2)}, u32[]{:S(2)}) %collective-permute-start.19) | collective-permute-done | bytes 86048 | tf_op jit(solution)/shard_map/ppermute | solution.py:363
  55.0 1.0 %collective-permute-start.20 = (bf16[32,1344]{1,0:T(8,128)(2,1)S(1)}, bf16[32,1344]{1,0:T(8,128)(2,1)S(1)}, u32[]{:S(2)}, u32[]{:S(2)}) collective-permute-start(bf16[32,1344]{1,0:T(8,128)(2,1)S(1)} %sum.1), channel_id=1, source_target_pairs={{0,8},{4,12},{8,0},{12,4},{1,9},{5,13},{9,1},{13,5},{2,10},{6,14},... | collective-permute-start | bytes 258056 | tf_op jit(solution)/shard_map/ppermute | solution.py:363
  56.0 0.8 %collective-permute-done.22.rest_4_ = bf16[32,1344]{1,0:T(8,128)(2,1)S(1)} collective-permute-done((bf16[32,1344]{1,0:T(8,128)(2,1)S(1)}, bf16[32,1344]{1,0:T(8,128)(2,1)S(1)}, u32[]{:S(2)}, u32[]{:S(2)}) %collective-permute-start.22) | collective-permute-done | bytes 86048 | tf_op jit(solution)/shard_map/ppermute | solution.py:363
  56.9 4.3 %collective-permute-done.20.rest_2_ = bf16[32,1344]{1,0:T(8,128)(2,1)S(1)} collective-permute-done((bf16[32,1344]{1,0:T(8,128)(2,1)S(1)}, bf16[32,1344]{1,0:T(8,128)(2,1)S(1)}, u32[]{:S(2)}, u32[]{:S(2)}) %collective-permute-start.20) | collective-permute-done | bytes 86048 | tf_op jit(solution)/shard_map/ppermute | solution.py:363
  61.1 0.7 %last.1 = bf16[1,32,1344]{2,1,0:T(8,128)(2,1)} custom-call(bf16[32,1344]{1,0:T(8,128)(2,1)S(1)} %get-tuple-element.64.hidden_ref, bf16[32,1344]{1,0:T(8,128)(2,1)S(1)} %get-tuple-element.71.rest_0_, bf16[64,1344]{1,0:T(8,128)(2,1)S(1)} %collective-permute-done.17.refs_2_.rest_1_, bf16[32,1344]{1,0:T(8,128)(2,1)S(1)} %collective-permute-done.20.rest_2_, ...), custom_call_target="tpu_custom_call" | custom-call | tf_op jit(solution)/shard_map/last/pallas_call | solution.py:29
  (13 shorter events, 0.1 us)
Async XLA Ops:
  1.8 1.5 %collective-permute-start = (bf16[528,128]{1,0:T(8,128)(2,1)S(1)}, bf16[528,128]{1,0:T(8,128)(2,1)S(1)}, u32[]{:S(2)}, u32[]{:S(2)}) collective-permute-start(bf16[528,128]{1,0:T(8,128)(2,1)S(1)} %get-tuple-element.46), channel_id=1, source_target_pairs={{0,1},{1,0},{2,3},{3,2},{4,5},{5,4},{6,7},{7,6},{8,9},{9,8},{10,11... | collective-permute-start | bytes 405512 | tf_op jit(solution)/shard_map/ppermute | solution.py:363
  3.4 13.2 %collective-permute-start.1 = (bf16[1,928,1344]{2,1,0:T(8,128)(2,1)}, bf16[1,928,1344]{2,1,0:T(8,128)(2,1)S(1)}, u32[]{:S(2)}, u32[]{:S(2)}) collective-permute-start(bf16[1,928,1344]{2,1,0:T(8,128)(2,1)} %bitcast.9), channel_id=1, source_target_pairs={{0,1},{1,0},{2,3},{3,2},{4,5},{5,4},{6,7},{7,6},{8,9},{9,8},{10,11... | collective-permute-start | bytes 7483400 | tf_op jit(solution)/shard_map/ppermute | solution.py:363
  3.9 12.8 %collective-permute-start.2 = (bf16[1,928,1344]{2,1,0:T(8,128)(2,1)}, bf16[1,928,1344]{2,1,0:T(8,128)(2,1)S(1)}, u32[]{:S(2)}, u32[]{:S(2)}) collective-permute-start(bf16[1,928,1344]{2,1,0:T(8,128)(2,1)} %down_hbm.1), channel_id=1, source_target_pairs={{0,1},{1,0},{2,3},{3,2},{4,5},{5,4},{6,7},{7,6},{8,9},{9,8},{10,11... | collective-permute-start | bytes 7483400 | tf_op jit(solution)/shard_map/ppermute | solution.py:363
  4.0 8.6 %collective-permute-start.5 = (bf16[528,128]{1,0:T(8,128)(2,1)S(1)}, bf16[528,128]{1,0:T(8,128)(2,1)S(1)}, u32[]{:S(2)}, u32[]{:S(2)}) collective-permute-start(bf16[528,128]{1,0:T(8,128)(2,1)S(1)} %chip_state.1.rest_0_), channel_id=1, source_target_pairs={{0,18},{1,19},{2,16},{3,17},{16,2},{17,3},{18,0},{19,1},{4,22},{5,... | collective-permute-start | bytes 405512 | tf_op jit(solution)/shard_map/ppermute | solution.py:363
  7.8 7.1 %collective-permute-start.4 = (bf16[528,128]{1,0:T(8,128)(2,1)S(1)}, bf16[528,128]{1,0:T(8,128)(2,1)S(1)}, u32[]{:S(2)}, u32[]{:S(2)}) collective-permute-start(bf16[528,128]{1,0:T(8,128)(2,1)S(1)} %chip_state.1.rest_0_), channel_id=1, source_target_pairs={{0,16},{1,17},{2,18},{3,19},{16,0},{17,1},{18,2},{19,3},{4,20},{5,... | collective-permute-start | bytes 405512 | tf_op jit(solution)/shard_map/ppermute | solution.py:363
  8.4 6.5 %collective-permute-start.3 = (bf16[528,128]{1,0:T(8,128)(2,1)S(1)}, bf16[528,128]{1,0:T(8,128)(2,1)S(1)}, u32[]{:S(2)}, u32[]{:S(2)}) collective-permute-start(bf16[528,128]{1,0:T(8,128)(2,1)S(1)} %chip_state.1.rest_0_), channel_id=1, source_target_pairs={{0,2},{1,3},{2,0},{3,1},{16,18},{17,19},{18,16},{19,17},{4,6},{5,7... | collective-permute-start | bytes 405512 | tf_op jit(solution)/shard_map/ppermute | solution.py:363
  15.2 1.4 %collective-permute-start.6 = (bf16[4,128,128]{2,1,0:T(8,128)(2,1)S(1)}, bf16[4,128,128]{2,1,0:T(8,128)(2,1)S(1)}, u32[]{:S(2)}, u32[]{:S(2)}) collective-permute-start(bf16[4,128,128]{2,1,0:T(8,128)(2,1)S(1)} %get-tuple-element.55), channel_id=1, source_target_pairs={{0,1},{1,0},{2,3},{3,2},{4,5},{5,4},{6,7},{7,6},{8,9},{9,8},{10,11... | collective-permute-start | bytes 393224 | tf_op jit(solution)/shard_map/ppermute | solution.py:363
  17.5 5.6 %collective-permute-start.7 = (bf16[32,1344]{1,0:T(8,128)(2,1)S(1)}, bf16[32,1344]{1,0:T(8,128)(2,1)S(1)}, u32[]{:S(2)}, u32[]{:S(2)}) collective-permute-start(bf16[32,1344]{1,0:T(8,128)(2,1)S(1)} %get-tuple-element.61), channel_id=1, source_target_pairs={{0,4},{1,9},{2,6},{3,11},{4,0},{5,13},{6,2},{7,15},{8,12},{9,1},{1... | collective-permute-start | bytes 258056 | tf_op jit(solution)/shard_map/ppermute | solution.py:373
  19.1 8.2 %collective-permute-start.8 = (bf16[32,1344]{1,0:T(8,128)(2,1)S(1)}, bf16[32,1344]{1,0:T(8,128)(2,1)S(1)}, u32[]{:S(2)}, u32[]{:S(2)}) collective-permute-start(bf16[32,1344]{1,0:T(8,128)(2,1)S(1)} %get-tuple-element.62), channel_id=1, source_target_pairs={{0,4},{1,13},{2,6},{3,15},{4,0},{5,9},{6,2},{7,11},{8,12},{9,5},{1... | collective-permute-start | bytes 258056 | tf_op jit(solution)/shard_map/ppermute | solution.py:373
  23.1 5.7 %collective-permute-start.9 = (bf16[32,1344]{1,0:T(8,128)(2,1)S(1)}, bf16[32,1344]{1,0:T(8,128)(2,1)S(1)}, u32[]{:S(2)}, u32[]{:S(2)}) collective-permute-start(bf16[32,1344]{1,0:T(8,128)(2,1)S(1)} %relay.1), channel_id=1, source_target_pairs={{0,8},{1,5},{2,10},{3,7},{4,12},{5,1},{6,14},{7,3},{8,0},{9,13},{1... | collective-permute-start | bytes 258056 | tf_op jit(solution)/shard_map/ppermute | solution.py:373
  29.0 5.6 %collective-permute-start.13 = (bf16[32,1408]{1,0:T(8,128)(2,1)S(1)}, bf16[32,1408]{1,0:T(8,128)(2,1)S(1)}, u32[]{:S(2)}, u32[]{:S(2)}) collective-permute-start(bf16[32,1408]{1,0:T(8,128)(2,1)S(1)} %get-tuple-element.66.rest_0_), channel_id=1, source_target_pairs={{0,8},{4,12},{8,0},{12,4},{1,9},{5,13},{9,1},{13,5},{2,10},{6,14},... | collective-permute-start | bytes 270344 | tf_op jit(solution)/shard_map/ppermute | solution.py:363
  30.5 7.1 %collective-permute-start.12 = (bf16[32,1408]{1,0:T(8,128)(2,1)S(1)}, bf16[32,1408]{1,0:T(8,128)(2,1)S(1)}, u32[]{:S(2)}, u32[]{:S(2)}) collective-permute-start(bf16[32,1408]{1,0:T(8,128)(2,1)S(1)} %get-tuple-element.66.rest_0_), channel_id=1, source_target_pairs={{0,2},{1,3},{2,0},{3,1},{4,6},{5,7},{6,4},{7,5},{8,10},{9,11},{10,... | collective-permute-start | bytes 270344 | tf_op jit(solution)/shard_map/ppermute | solution.py:363
  31.9 6.2 %collective-permute-start.11 = (bf16[32,1408]{1,0:T(8,128)(2,1)S(1)}, bf16[32,1408]{1,0:T(8,128)(2,1)S(1)}, u32[]{:S(2)}, u32[]{:S(2)}) collective-permute-start(bf16[32,1408]{1,0:T(8,128)(2,1)S(1)} %get-tuple-element.66.rest_0_), channel_id=1, source_target_pairs={{0,4},{1,5},{2,6},{3,7},{4,0},{5,1},{6,2},{7,3},{8,12},{9,13},{10,... | collective-permute-start | bytes 270344 | tf_op jit(solution)/shard_map/ppermute | solution.py:363
  34.4 5.9 %collective-permute-start.10 = (bf16[32,1408]{1,0:T(8,128)(2,1)S(1)}, bf16[32,1408]{1,0:T(8,128)(2,1)S(1)}, u32[]{:S(2)}, u32[]{:S(2)}) collective-permute-start(bf16[32,1408]{1,0:T(8,128)(2,1)S(1)} %get-tuple-element.66.rest_0_), channel_id=1, source_target_pairs={{0,6},{1,7},{2,4},{3,5},{4,2},{5,3},{6,0},{7,1},{8,14},{9,15},{10,... | collective-permute-start | bytes 270344 | tf_op jit(solution)/shard_map/ppermute | solution.py:363
  34.6 8.4 %collective-permute-start.16 = (bf16[32,1408]{1,0:T(8,128)(2,1)S(1)}, bf16[32,1408]{1,0:T(8,128)(2,1)S(1)}, u32[]{:S(2)}, u32[]{:S(2)}) collective-permute-start(bf16[32,1408]{1,0:T(8,128)(2,1)S(1)} %collective-permute-done.13.rest_0_), channel_id=1, source_target_pairs={{0,6},{1,7},{2,4},{3,5},{4,2},{5,3},{6,0},{7,1},{8,14},{9,15},{10,... | collective-permute-start | bytes 270344 | tf_op jit(solution)/shard_map/ppermute | solution.py:363
  37.3 5.7 %collective-permute-start.15 = (bf16[32,1408]{1,0:T(8,128)(2,1)S(1)}, bf16[32,1408]{1,0:T(8,128)(2,1)S(1)}, u32[]{:S(2)}, u32[]{:S(2)}) collective-permute-start(bf16[32,1408]{1,0:T(8,128)(2,1)S(1)} %collective-permute-done.13.rest_0_), channel_id=1, source_target_pairs={{0,4},{1,5},{2,6},{3,7},{4,0},{5,1},{6,2},{7,3},{8,12},{9,13},{10,... | collective-permute-start | bytes 270344 | tf_op jit(solution)/shard_map/ppermute | solution.py:363
  37.6 5.5 %collective-permute-start.14 = (bf16[32,1408]{1,0:T(8,128)(2,1)S(1)}, bf16[32,1408]{1,0:T(8,128)(2,1)S(1)}, u32[]{:S(2)}, u32[]{:S(2)}) collective-permute-start(bf16[32,1408]{1,0:T(8,128)(2,1)S(1)} %collective-permute-done.13.rest_0_), channel_id=1, source_target_pairs={{0,2},{1,3},{2,0},{3,1},{4,6},{5,7},{6,4},{7,5},{8,10},{9,11},{10,... | collective-permute-start | bytes 270344 | tf_op jit(solution)/shard_map/ppermute | solution.py:363
  45.8 9.2 %collective-permute-start.17 = (bf16[64,1344]{1,0:T(8,128)(2,1)S(1)}, bf16[64,1344]{1,0:T(8,128)(2,1)S(1)}, u32[]{:S(2)}, u32[]{:S(2)}) collective-permute-start(bf16[64,1344]{1,0:T(8,128)(2,1)S(1)} %get-tuple-element.77), channel_id=1, source_target_pairs={{0,4},{1,5},{2,6},{3,7},{4,0},{5,1},{6,2},{7,3},{8,12},{9,13},{10,... | collective-permute-start | bytes 516104 | tf_op jit(solution)/shard_map/ppermute | solution.py:363
  47.1 5.0 %collective-permute-start.18 = (bf16[32,1344]{1,0:T(8,128)(2,1)S(1)}, bf16[32,1344]{1,0:T(8,128)(2,1)S(1)}, u32[]{:S(2)}, u32[]{:S(2)}) collective-permute-start(bf16[32,1344]{1,0:T(8,128)(2,1)S(1)} %get-tuple-element.79), channel_id=1, source_target_pairs={{0,2},{1,3},{2,0},{3,1},{4,6},{5,7},{6,4},{7,5},{8,10},{9,11},{10,... | collective-permute-start | bytes 258056 | tf_op jit(solution)/shard_map/ppermute | solution.py:363
  48.5 6.4 %collective-permute-start.19 = (bf16[32,1344]{1,0:T(8,128)(2,1)S(1)}, bf16[32,1344]{1,0:T(8,128)(2,1)S(1)}, u32[]{:S(2)}, u32[]{:S(2)}) collective-permute-start(bf16[32,1344]{1,0:T(8,128)(2,1)S(1)} %get-tuple-element.80), channel_id=1, source_target_pairs={{0,6},{1,7},{2,4},{3,5},{4,2},{5,3},{6,0},{7,1},{8,14},{9,15},{10,... | collective-permute-start | bytes 258056 | tf_op jit(solution)/shard_map/ppermute | solution.py:363
  49.3 6.7 %collective-permute-start.21 = (bf16[32,1344]{1,0:T(8,128)(2,1)S(1)}, bf16[32,1344]{1,0:T(8,128)(2,1)S(1)}, u32[]{:S(2)}, u32[]{:S(2)}) collective-permute-start(bf16[32,1344]{1,0:T(8,128)(2,1)S(1)} %get-tuple-element.81), channel_id=1, source_target_pairs={{0,6},{1,7},{2,4},{3,5},{4,2},{5,3},{6,0},{7,1},{8,14},{9,15},{10,... | collective-permute-start | bytes 258056 | tf_op jit(solution)/shard_map/ppermute | solution.py:363
  51.5 5.4 %collective-permute-start.22 = (bf16[32,1344]{1,0:T(8,128)(2,1)S(1)}, bf16[32,1344]{1,0:T(8,128)(2,1)S(1)}, u32[]{:S(2)}, u32[]{:S(2)}) collective-permute-start(bf16[32,1344]{1,0:T(8,128)(2,1)S(1)} %get-tuple-element.82), channel_id=1, source_target_pairs={{0,2},{1,3},{2,0},{3,1},{4,6},{5,7},{6,4},{7,5},{8,10},{9,11},{10,... | collective-permute-start | bytes 258056 | tf_op jit(solution)/shard_map/ppermute | solution.py:363
  55.0 6.1 %collective-permute-start.20 = (bf16[32,1344]{1,0:T(8,128)(2,1)S(1)}, bf16[32,1344]{1,0:T(8,128)(2,1)S(1)}, u32[]{:S(2)}, u32[]{:S(2)}) collective-permute-start(bf16[32,1344]{1,0:T(8,128)(2,1)S(1)} %sum.1), channel_id=1, source_target_pairs={{0,8},{4,12},{8,0},{12,4},{1,9},{5,13},{9,1},{13,5},{2,10},{6,14},... | collective-permute-start | bytes 258056 | tf_op jit(solution)/shard_map/ppermute | solution.py:363

commit v26 on v24

--- a/solution.py
+++ b/solution.py
@@ -510,17 +510,15 @@
     sets = [spread(swap(own_rows, "head", high)) for high in range(2, head_size, 2)]
     near = through_experts(spread(own_rows))
     near, sets = lax.optimization_barrier((near, sets))
-    joined = [at for at, mask in enumerate(group, 1) if mask == exp_size]
+    joined = []
     arrived, later = [], [at for at, mask in enumerate(group, 1) if mask < exp_size]
     apart = [near[at] for at in later]
     for high, members in zip(range(2, head_size, 2), sets):
         pieces = through_experts(members, [(at, near[at]) for at in joined] if high == 2 else ())
         got = [swap(piece, both, mask) for piece, mask in zip(pieces[1:], group)]
         total = call(sum_kernel, "sum", struct((rows, model), BF16), [(VMEM, v) for v in (pieces[0], *got)])
-        if high == 2:
-            arrived += [part for part, mask in zip(got, group) if mask == exp_size]
         arrived.append(swap(total, "head", high))
-    arrived += [swap(near[at], both, mask) for at, mask in enumerate(group, 1) if mask > exp_size]
+    arrived += [swap(near[at], both, mask) for at, mask in enumerate(group, 1) if mask >= exp_size]
     arrived += [swap(piece, both, group[at - 1]) for piece, at in zip(apart, later)]
     return call(
         last_kernel,

time: 60.1 us -> 62.1 us (1.033)
  waiting for transfers between devices: 15.6 us -> 17.6 us
    ppermute x20 -> x21, waiting for transfers between devices: 10.7 us -> 12.7 us  [swap(): return lax.ppermute(value, axis, [(i, i ^ mask) for i in range(size)])]
    ppermute x20 -> x21, starting transfers between devices: 22.2 us -> 22.1 us  [swap(): return lax.ppermute(value, axis, [(i, i ^ mask) for i in range(size)])]
  transfers between devices with their start and end apart: 23 -> 24, of which waited for: 12 -> 12; matrix products, arithmetic and copies ran while one was open for 0% -> 0% of each run, Pallas kernels for 20% -> 19%
where the time goes in v26:
time: 62.1 us; the launch traced here: 61.8 us
  starting transfers between devices  25.9 us (42%)
  Pallas kernels  18.1 us (29%)
  waiting for transfers between devices  17.6 us (28%)
    ppermute x21, starting transfers between devices, swap(): return lax.ppermute(value, axis, [(i, i ^ mask) for i in range(size)])  22.1 us
    pallas_call x15, Pallas kernels, call(): pl.pallas_call(kernel, out_shape=jax.tree.map(lambda out: pltpu.VMEM(out....  18.1 us
    ppermute x21, waiting for transfers between devices, swap(): return lax.ppermute(value, axis, [(i, i ^ mask) for i in range(size)])  12.7 us
    ppermute x3, waiting for transfers between devices, swap_slot(): return lax.ppermute(value, ('head', 'exp'), pairs)  4.89 us
    ppermute x3, starting transfers between devices, swap_slot(): return lax.ppermute(value, ('head', 'exp'), pairs)  3.79 us
  transfers between devices with their start and end apart: 24, of which 12 were waited for; matrix products, arithmetic and copies ran while one was open for 0% of the time, Pallas kernels for 19%

profile of v26, /device:TPU:0, one launch (start us, length us, event | category | flops | bytes accessed | tf_op | source)
XLA Modules:
  0.0 61.8 jit_solution(259865243770228163)
XLA Ops:
  0.0 1.8 %state.1 = (bf16[528,128]{1,0:T(8,128)(2,1)S(1)}, bf16[528,128]{1,0:T(8,128)(2,1)S(1)}) custom-call(bf16[128,1024]{1,0:T(8,128)(2,1)} %x_hbm.3, bf16[128,256]{1,0:T(8,128)(2,1)} %b_hbm.3, f32[16,128]{1,0:T(8,128)} %bitcast.11, f32[1,16]{1,0:T(1,128)} %bitcast.16), custom_call_target="tpu_custom_call" | custom-call | tf_op jit(solution)/shard_map/state/pallas_call | solution.py:29
  1.8 0.5 collective-permute-start
  2.4 1.0 %prep.1 = (bf16[32,128]{1,0:T(8,128)(2,1)S(1)}, bf16[1,32,1344]{2,1,0:T(8,128)(2,1)S(1)}, f32[1,1344]{1,0:T(1,128)S(1)}) custom-call(bf16[528,128]{1,0:T(8,128)(2,1)S(1)} %get-tuple-element.44.after_ref.keep_ref, bf16[1,32,1344]{2,1,0:T(8,128)(2,1)} %resid_hbm.1, s32[6,1,32]{2,1,0:T(1,128)} %bitcast.14, f32[6,1,32]{2,1,0:T(1,128)} %bitcast.15, f32[1344]{0:T(1024)} %gain_hbm.1), custom_call_target="tpu_custom_call" | custom-call | tf_op jit(solution)/shard_map/prep/pallas_call | solution.py:29
  3.3 0.1 chip_state.1.rest_0_
  3.4 0.4 collective-permute-start.1
  3.9 0.1 collective-permute-start.2
  4.0 3.8 %collective-permute-start.5 = (bf16[528,128]{1,0:T(8,128)(2,1)S(1)}, bf16[528,128]{1,0:T(8,128)(2,1)S(1)}, u32[]{:S(2)}, u32[]{:S(2)}) collective-permute-start(bf16[528,128]{1,0:T(8,128)(2,1)S(1)} %chip_state.1.rest_0_), channel_id=1, source_target_pairs={{0,18},{1,19},{2,16},{3,17},{16,2},{17,3},{18,0},{19,1},{4,22},{5,... | collective-permute-start | bytes 405512 | tf_op jit(solution)/shard_map/ppermute | solution.py:363
  7.8 0.5 collective-permute-start.4
  8.4 0.0 collective-permute-start.3
  8.4 1.8 %projection.1 = (f32[1,1024]{1,0:T(1,128)S(1)}, bf16[1344,1024]{1,0:T(8,128)(2,1)S(1)}) custom-call(f32[1,1024]{1,0:T(1,128)} %bitcast.13, bf16[1344,1024]{1,0:T(8,128)(2,1)} %bitcast.8), custom_call_target="tpu_custom_call" | custom-call | tf_op jit(solution)/shard_map/projection/pallas_call | solution.py:29
  10.2 2.4 %inside.1 = (f32[128,1024]{1,0:T(8,128)S(1)}, f32[128,1024]{1,0:T(8,128)S(1)}, bf16[128,256]{1,0:T(8,128)(2,1)S(1)}) custom-call(bf16[128,1024]{1,0:T(8,128)(2,1)} %x_hbm.3, bf16[128,1024]{1,0:T(8,128)(2,1)} %z_hbm.1, bf16[128,256]{1,0:T(8,128)(2,1)} %b_hbm.3, bf16[128,256]{1,0:T(8,128)(2,1)} %c_hbm.1, f32[16,128]{1,0:T(8,128)} %bitcast.12, ...), custom_call_target="tpu_custom_call" | custom-call | tf_op jit(solution)/shard_map/inside/pallas_call | solution.py:29
  12.7 2.2 %collective-permute-done.4.rest_2_ = bf16[528,128]{1,0:T(8,128)(2,1)S(1)} collective-permute-done((bf16[528,128]{1,0:T(8,128)(2,1)S(1)}, bf16[528,128]{1,0:T(8,128)(2,1)S(1)}, u32[]{:S(2)}, u32[]{:S(2)}) %collective-permute-start.4) | collective-permute-done | bytes 135200 | tf_op jit(solution)/shard_map/ppermute | solution.py:363
  14.9 0.3 before.1
  15.2 0.1 collective-permute-start.6
  15.3 0.8 %first_half.1.first_ref = f32[128,1344]{1,0:T(8,128)S(1)} custom-call(f32[128,1024]{1,0:T(8,128)S(1)} %get-tuple-element.49.local_ref, f32[128,1024]{1,0:T(8,128)S(1)} %get-tuple-element.50.grown_ref, bf16[128,256]{1,0:T(8,128)(2,1)S(1)} %get-tuple-element.51.after_b.c_ref, f32[1,1024]{1,0:T(1,128)S(1)} %get-tuple-element.52.after_a.norm_ref, ...), custom_call_target="tpu_custom_call" | custom-call | tf_op jit(solution)/shard_map/first_half/pallas_call | solution.py:29
  16.1 0.5 collective-permute-done.6.got_ref
  16.6 0.9 %mixed.1 = (bf16[32,1344]{1,0:T(8,128)(2,1)S(1)}, bf16[32,1344]{1,0:T(8,128)(2,1)S(1)}, bf16[32,1344]{1,0:T(8,128)(2,1)S(1)}, bf16[32,1344]{1,0:T(8,128)(2,1)S(1)}) custom-call(bf16[1,928,1344]{2,1,0:T(8,128)(2,1)S(1)} %collective-permute-done.1.after_up.other_up_ref, bf16[1,928,1344]{2,1,0:T(8,128)(2,1)S(1)} %collective-permute-done.2.after_down.other_down_ref, ...), custom_call_target="tpu_custom_call" | custom-call | tf_op jit(solution)/shard_map/mixed/pallas_call | solution.py:29
  17.5 1.6 %collective-permute-start.7 = (bf16[32,1344]{1,0:T(8,128)(2,1)S(1)}, bf16[32,1344]{1,0:T(8,128)(2,1)S(1)}, u32[]{:S(2)}, u32[]{:S(2)}) collective-permute-start(bf16[32,1344]{1,0:T(8,128)(2,1)S(1)} %get-tuple-element.61), channel_id=1, source_target_pairs={{0,4},{1,9},{2,6},{3,11},{4,0},{5,13},{6,2},{7,15},{8,12},{9,1},{1... | collective-permute-start | bytes 258056 | tf_op jit(solution)/shard_map/ppermute | solution.py:373
  19.1 0.5 collective-permute-start.8
  19.6 3.5 %collective-permute-done.7.got_ref.rest_1_ = bf16[32,1344]{1,0:T(8,128)(2,1)S(1)} collective-permute-done((bf16[32,1344]{1,0:T(8,128)(2,1)S(1)}, bf16[32,1344]{1,0:T(8,128)(2,1)S(1)}, u32[]{:S(2)}, u32[]{:S(2)}) %collective-permute-start.7) | collective-permute-done | bytes 86048 | tf_op jit(solution)/shard_map/ppermute | solution.py:373
  23.1 1.7 %collective-permute-start.9 = (bf16[32,1344]{1,0:T(8,128)(2,1)S(1)}, bf16[32,1344]{1,0:T(8,128)(2,1)S(1)}, u32[]{:S(2)}, u32[]{:S(2)}) collective-permute-start(bf16[32,1344]{1,0:T(8,128)(2,1)S(1)} %relay.1), channel_id=1, source_target_pairs={{0,8},{1,5},{2,10},{3,7},{4,12},{5,1},{6,14},{7,3},{8,0},{9,13},{1... | collective-permute-start | bytes 258056 | tf_op jit(solution)/shard_map/ppermute | solution.py:373
  24.8 2.5 %weights.1 = (bf16[1,928,1344]{2,1,0:T(8,128)(2,1)S(1)}, bf16[1,928,1344]{2,1,0:T(8,128)(2,1)S(1)}) custom-call(bf16[32,1344]{1,0:T(8,128)(2,1)S(1)} %get-tuple-element.57.after_ref.rest_0_, bf16[1,928,1344]{2,1,0:T(8,128)(2,1)} %bitcast.10, bf16[1,928,1344]{2,1,0:T(8,128)(2,1)} %down_hbm.1), custom_call_target="tpu_custom_call" | custom-call | tf_op jit(solution)/shard_map/weights/pallas_call | solution.py:29
  27.4 1.4 %collective-permute-done.9.rest_3_ = bf16[32,1344]{1,0:T(8,128)(2,1)S(1)} collective-permute-done((bf16[32,1344]{1,0:T(8,128)(2,1)S(1)}, bf16[32,1344]{1,0:T(8,128)(2,1)S(1)}, u32[]{:S(2)}, u32[]{:S(2)}) %collective-permute-start.9) | collective-permute-done | bytes 86048 | tf_op jit(solution)/shard_map/ppermute | solution.py:373
  28.8 0.2 rows.1
  29.0 1.5 %collective-permute-start.13 = (bf16[32,1408]{1,0:T(8,128)(2,1)S(1)}, bf16[32,1408]{1,0:T(8,128)(2,1)S(1)}, u32[]{:S(2)}, u32[]{:S(2)}) collective-permute-start(bf16[32,1408]{1,0:T(8,128)(2,1)S(1)} %get-tuple-element.66.rest_0_), channel_id=1, source_target_pairs={{0,8},{4,12},{8,0},{12,4},{1,9},{5,13},{9,1},{13,5},{2,10},{6,14},... | collective-permute-start | bytes 270344 | tf_op jit(solution)/shard_map/ppermute | solution.py:363
  30.5 3.3 %collective-permute-start.12 = (bf16[32,1408]{1,0:T(8,128)(2,1)S(1)}, bf16[32,1408]{1,0:T(8,128)(2,1)S(1)}, u32[]{:S(2)}, u32[]{:S(2)}) collective-permute-start(bf16[32,1408]{1,0:T(8,128)(2,1)S(1)} %get-tuple-element.66.rest_0_), channel_id=1, source_target_pairs={{0,6},{1,7},{2,4},{3,5},{4,2},{5,3},{6,0},{7,1},{8,14},{9,15},{10,... | collective-permute-start | bytes 270344 | tf_op jit(solution)/shard_map/ppermute | solution.py:363
  33.8 0.6 collective-permute-start.10
  34.4 0.1 collective-permute-done.13.rest_0_
  34.6 2.7 %collective-permute-start.16 = (bf16[32,1408]{1,0:T(8,128)(2,1)S(1)}, bf16[32,1408]{1,0:T(8,128)(2,1)S(1)}, u32[]{:S(2)}, u32[]{:S(2)}) collective-permute-start(bf16[32,1408]{1,0:T(8,128)(2,1)S(1)} %collective-permute-done.13.rest_0_), channel_id=1, source_target_pairs={{0,6},{1,7},{2,4},{3,5},{4,2},{5,3},{6,0},{7,1},{8,14},{9,15},{10,... | collective-permute-start | bytes 270344 | tf_op jit(solution)/shard_map/ppermute | solution.py:363
  37.3 1.1 %collective-permute-start.15 = (bf16[32,1408]{1,0:T(8,128)(2,1)S(1)}, bf16[32,1408]{1,0:T(8,128)(2,1)S(1)}, u32[]{:S(2)}, u32[]{:S(2)}) collective-permute-start(bf16[32,1408]{1,0:T(8,128)(2,1)S(1)} %collective-permute-done.13.rest_0_), channel_id=1, source_target_pairs={{0,4},{1,5},{2,6},{3,7},{4,0},{5,1},{6,2},{7,3},{8,12},{9,13},{10,... | collective-permute-start | bytes 270344 | tf_op jit(solution)/shard_map/ppermute | solution.py:363
  38.4 0.9 %collective-permute-done.11.rest_2_ = bf16[32,1408]{1,0:T(8,128)(2,1)S(1)} collective-permute-done((bf16[32,1408]{1,0:T(8,128)(2,1)S(1)}, bf16[32,1408]{1,0:T(8,128)(2,1)S(1)}, u32[]{:S(2)}, u32[]{:S(2)}) %collective-permute-start.11) | collective-permute-done | bytes 90144 | tf_op jit(solution)/shard_map/ppermute | solution.py:363
  39.4 1.5 %collective-permute-done.10.rest_1_ = bf16[32,1408]{1,0:T(8,128)(2,1)S(1)} collective-permute-done((bf16[32,1408]{1,0:T(8,128)(2,1)S(1)}, bf16[32,1408]{1,0:T(8,128)(2,1)S(1)}, u32[]{:S(2)}, u32[]{:S(2)}) %collective-permute-start.10) | collective-permute-done | bytes 90144 | tf_op jit(solution)/shard_map/ppermute | solution.py:363
  40.9 2.7 %experts.2 = (bf16[32,1344]{1,0:T(8,128)(2,1)S(1)}, bf16[32,1344]{1,0:T(8,128)(2,1)S(1)}, bf16[32,1344]{1,0:T(8,128)(2,1)S(1)}, bf16[32,1344]{1,0:T(8,128)(2,1)S(1)}) custom-call(bf16[1,928,1344]{2,1,0:T(8,128)(2,1)S(1)} %get-tuple-element.58.after_ref.up_ref, bf16[1,928,1344]{2,1,0:T(8,128)(2,1)S(1)} %get-tuple-element.65.down_ref, ...), custom_call_target="tpu_custom_call" | custom-call | tf_op jit(solution)/shard_map/experts/pallas_call | solution.py:29
  43.6 2.7 %experts.3 = (bf16[32,1344]{1,0:T(8,128)(2,1)S(1)}, bf16[32,1344]{1,0:T(8,128)(2,1)S(1)}, bf16[32,1344]{1,0:T(8,128)(2,1)S(1)}, bf16[32,1344]{1,0:T(8,128)(2,1)S(1)}) custom-call(bf16[1,928,1344]{2,1,0:T(8,128)(2,1)S(1)} %get-tuple-element.58.after_ref.up_ref, bf16[1,928,1344]{2,1,0:T(8,128)(2,1)S(1)} %get-tuple-element.65.down_ref, ...), custom_call_target="tpu_custom_call" | custom-call | tf_op jit(solution)/shard_map/experts/pallas_call | solution.py:29
  46.4 0.1 collective-permute-start.17
  46.4 1.7 %collective-permute-start.18 = (bf16[32,1344]{1,0:T(8,128)(2,1)S(1)}, bf16[32,1344]{1,0:T(8,128)(2,1)S(1)}, u32[]{:S(2)}, u32[]{:S(2)}) collective-permute-start(bf16[32,1344]{1,0:T(8,128)(2,1)S(1)} %get-tuple-element.78), channel_id=1, source_target_pairs={{0,4},{1,5},{2,6},{3,7},{4,0},{5,1},{6,2},{7,3},{8,12},{9,13},{10,... | collective-permute-start | bytes 258056 | tf_op jit(solution)/shard_map/ppermute | solution.py:363
  48.1 1.8 %collective-permute-start.19 = (bf16[32,1344]{1,0:T(8,128)(2,1)S(1)}, bf16[32,1344]{1,0:T(8,128)(2,1)S(1)}, u32[]{:S(2)}, u32[]{:S(2)}) collective-permute-start(bf16[32,1344]{1,0:T(8,128)(2,1)S(1)} %get-tuple-element.79), channel_id=1, source_target_pairs={{0,6},{1,7},{2,4},{3,5},{4,2},{5,3},{6,0},{7,1},{8,14},{9,15},{10,... | collective-permute-start | bytes 258056 | tf_op jit(solution)/shard_map/ppermute | solution.py:363
  49.9 0.3 collective-permute-start.21
  50.2 1.3 %collective-permute-start.22 = (bf16[32,1344]{1,0:T(8,128)(2,1)S(1)}, bf16[32,1344]{1,0:T(8,128)(2,1)S(1)}, u32[]{:S(2)}, u32[]{:S(2)}) collective-permute-start(bf16[32,1344]{1,0:T(8,128)(2,1)S(1)} %get-tuple-element.81), channel_id=1, source_target_pairs={{0,6},{1,7},{2,4},{3,5},{4,2},{5,3},{6,0},{7,1},{8,14},{9,15},{10,... | collective-permute-start | bytes 258056 | tf_op jit(solution)/shard_map/ppermute | solution.py:363
  51.5 0.9 %collective-permute-done.17.refs_1_ = bf16[32,1344]{1,0:T(8,128)(2,1)S(1)} collective-permute-done((bf16[32,1344]{1,0:T(8,128)(2,1)S(1)}, bf16[32,1344]{1,0:T(8,128)(2,1)S(1)}, u32[]{:S(2)}, u32[]{:S(2)}) %collective-permute-start.17) | collective-permute-done | bytes 86048 | tf_op jit(solution)/shard_map/ppermute | solution.py:363
  52.4 1.0 %collective-permute-start.23 = (bf16[32,1344]{1,0:T(8,128)(2,1)S(1)}, bf16[32,1344]{1,0:T(8,128)(2,1)S(1)}, u32[]{:S(2)}, u32[]{:S(2)}) collective-permute-start(bf16[32,1344]{1,0:T(8,128)(2,1)S(1)} %get-tuple-element.82), channel_id=1, source_target_pairs={{0,2},{1,3},{2,0},{3,1},{4,6},{5,7},{6,4},{7,5},{8,10},{9,11},{10,... | collective-permute-start | bytes 258056 | tf_op jit(solution)/shard_map/ppermute | solution.py:363
  53.4 1.1 %collective-permute-done.19.refs_3_ = bf16[32,1344]{1,0:T(8,128)(2,1)S(1)} collective-permute-done((bf16[32,1344]{1,0:T(8,128)(2,1)S(1)}, bf16[32,1344]{1,0:T(8,128)(2,1)S(1)}, u32[]{:S(2)}, u32[]{:S(2)}) %collective-permute-start.19) | collective-permute-done | bytes 86048 | tf_op jit(solution)/shard_map/ppermute | solution.py:363
  54.5 0.1 sum.1
  54.6 1.2 %collective-permute-start.20 = (bf16[32,1344]{1,0:T(8,128)(2,1)S(1)}, bf16[32,1344]{1,0:T(8,128)(2,1)S(1)}, u32[]{:S(2)}, u32[]{:S(2)}) collective-permute-start(bf16[32,1344]{1,0:T(8,128)(2,1)S(1)} %sum.1), channel_id=1, source_target_pairs={{0,8},{4,12},{8,0},{12,4},{1,9},{5,13},{9,1},{13,5},{2,10},{6,14},... | collective-permute-start | bytes 258056 | tf_op jit(solution)/shard_map/ppermute | solution.py:363
  55.8 0.7 %collective-permute-done.22.rest_3_ = bf16[32,1344]{1,0:T(8,128)(2,1)S(1)} collective-permute-done((bf16[32,1344]{1,0:T(8,128)(2,1)S(1)}, bf16[32,1344]{1,0:T(8,128)(2,1)S(1)}, u32[]{:S(2)}, u32[]{:S(2)}) %collective-permute-start.22) | collective-permute-done | bytes 86048 | tf_op jit(solution)/shard_map/ppermute | solution.py:363
  56.5 0.9 %collective-permute-done.23.rest_4_ = bf16[32,1344]{1,0:T(8,128)(2,1)S(1)} collective-permute-done((bf16[32,1344]{1,0:T(8,128)(2,1)S(1)}, bf16[32,1344]{1,0:T(8,128)(2,1)S(1)}, u32[]{:S(2)}, u32[]{:S(2)}) %collective-permute-start.23) | collective-permute-done | bytes 86048 | tf_op jit(solution)/shard_map/ppermute | solution.py:363
  57.4 3.6 %collective-permute-done.20.rest_1_ = bf16[32,1344]{1,0:T(8,128)(2,1)S(1)} collective-permute-done((bf16[32,1344]{1,0:T(8,128)(2,1)S(1)}, bf16[32,1344]{1,0:T(8,128)(2,1)S(1)}, u32[]{:S(2)}, u32[]{:S(2)}) %collective-permute-start.20) | collective-permute-done | bytes 86048 | tf_op jit(solution)/shard_map/ppermute | solution.py:363
  61.0 0.7 %last.1 = bf16[1,32,1344]{2,1,0:T(8,128)(2,1)} custom-call(bf16[32,1344]{1,0:T(8,128)(2,1)S(1)} %get-tuple-element.64.hidden_ref, bf16[32,1344]{1,0:T(8,128)(2,1)S(1)} %get-tuple-element.71.rest_0_, bf16[32,1344]{1,0:T(8,128)(2,1)S(1)} %collective-permute-done.20.rest_1_, bf16[32,1344]{1,0:T(8,128)(2,1)S(1)} %collective-permute-done.21.rest_2_, ...), custom_call_target="tpu_custom_call" | custom-call | tf_op jit(solution)/shard_map/last/pallas_call | solution.py:29
  (15 shorter events, 0.1 us)
Async XLA Ops:
  1.8 1.5 %collective-permute-start = (bf16[528,128]{1,0:T(8,128)(2,1)S(1)}, bf16[528,128]{1,0:T(8,128)(2,1)S(1)}, u32[]{:S(2)}, u32[]{:S(2)}) collective-permute-start(bf16[528,128]{1,0:T(8,128)(2,1)S(1)} %get-tuple-element.46), channel_id=1, source_target_pairs={{0,1},{1,0},{2,3},{3,2},{4,5},{5,4},{6,7},{7,6},{8,9},{9,8},{10,11... | collective-permute-start | bytes 405512 | tf_op jit(solution)/shard_map/ppermute | solution.py:363
  3.4 13.2 %collective-permute-start.1 = (bf16[1,928,1344]{2,1,0:T(8,128)(2,1)}, bf16[1,928,1344]{2,1,0:T(8,128)(2,1)S(1)}, u32[]{:S(2)}, u32[]{:S(2)}) collective-permute-start(bf16[1,928,1344]{2,1,0:T(8,128)(2,1)} %bitcast.9), channel_id=1, source_target_pairs={{0,1},{1,0},{2,3},{3,2},{4,5},{5,4},{6,7},{7,6},{8,9},{9,8},{10,11... | collective-permute-start | bytes 7483400 | tf_op jit(solution)/shard_map/ppermute | solution.py:363
  3.9 12.8 %collective-permute-start.2 = (bf16[1,928,1344]{2,1,0:T(8,128)(2,1)}, bf16[1,928,1344]{2,1,0:T(8,128)(2,1)S(1)}, u32[]{:S(2)}, u32[]{:S(2)}) collective-permute-start(bf16[1,928,1344]{2,1,0:T(8,128)(2,1)} %down_hbm.1), channel_id=1, source_target_pairs={{0,1},{1,0},{2,3},{3,2},{4,5},{5,4},{6,7},{7,6},{8,9},{9,8},{10,11... | collective-permute-start | bytes 7483400 | tf_op jit(solution)/shard_map/ppermute | solution.py:363
  4.0 8.6 %collective-permute-start.5 = (bf16[528,128]{1,0:T(8,128)(2,1)S(1)}, bf16[528,128]{1,0:T(8,128)(2,1)S(1)}, u32[]{:S(2)}, u32[]{:S(2)}) collective-permute-start(bf16[528,128]{1,0:T(8,128)(2,1)S(1)} %chip_state.1.rest_0_), channel_id=1, source_target_pairs={{0,18},{1,19},{2,16},{3,17},{16,2},{17,3},{18,0},{19,1},{4,22},{5,... | collective-permute-start | bytes 405512 | tf_op jit(solution)/shard_map/ppermute | solution.py:363
  7.8 7.1 %collective-permute-start.4 = (bf16[528,128]{1,0:T(8,128)(2,1)S(1)}, bf16[528,128]{1,0:T(8,128)(2,1)S(1)}, u32[]{:S(2)}, u32[]{:S(2)}) collective-permute-start(bf16[528,128]{1,0:T(8,128)(2,1)S(1)} %chip_state.1.rest_0_), channel_id=1, source_target_pairs={{0,16},{1,17},{2,18},{3,19},{16,0},{17,1},{18,2},{19,3},{4,20},{5,... | collective-permute-start | bytes 405512 | tf_op jit(solution)/shard_map/ppermute | solution.py:363
  8.4 6.5 %collective-permute-start.3 = (bf16[528,128]{1,0:T(8,128)(2,1)S(1)}, bf16[528,128]{1,0:T(8,128)(2,1)S(1)}, u32[]{:S(2)}, u32[]{:S(2)}) collective-permute-start(bf16[528,128]{1,0:T(8,128)(2,1)S(1)} %chip_state.1.rest_0_), channel_id=1, source_target_pairs={{0,2},{1,3},{2,0},{3,1},{16,18},{17,19},{18,16},{19,17},{4,6},{5,7... | collective-permute-start | bytes 405512 | tf_op jit(solution)/shard_map/ppermute | solution.py:363
  15.2 1.4 %collective-permute-start.6 = (bf16[4,128,128]{2,1,0:T(8,128)(2,1)S(1)}, bf16[4,128,128]{2,1,0:T(8,128)(2,1)S(1)}, u32[]{:S(2)}, u32[]{:S(2)}) collective-permute-start(bf16[4,128,128]{2,1,0:T(8,128)(2,1)S(1)} %get-tuple-element.55), channel_id=1, source_target_pairs={{0,1},{1,0},{2,3},{3,2},{4,5},{5,4},{6,7},{7,6},{8,9},{9,8},{10,11... | collective-permute-start | bytes 393224 | tf_op jit(solution)/shard_map/ppermute | solution.py:363
  17.5 5.6 %collective-permute-start.7 = (bf16[32,1344]{1,0:T(8,128)(2,1)S(1)}, bf16[32,1344]{1,0:T(8,128)(2,1)S(1)}, u32[]{:S(2)}, u32[]{:S(2)}) collective-permute-start(bf16[32,1344]{1,0:T(8,128)(2,1)S(1)} %get-tuple-element.61), channel_id=1, source_target_pairs={{0,4},{1,9},{2,6},{3,11},{4,0},{5,13},{6,2},{7,15},{8,12},{9,1},{1... | collective-permute-start | bytes 258056 | tf_op jit(solution)/shard_map/ppermute | solution.py:373
  19.1 8.2 %collective-permute-start.8 = (bf16[32,1344]{1,0:T(8,128)(2,1)S(1)}, bf16[32,1344]{1,0:T(8,128)(2,1)S(1)}, u32[]{:S(2)}, u32[]{:S(2)}) collective-permute-start(bf16[32,1344]{1,0:T(8,128)(2,1)S(1)} %get-tuple-element.62), channel_id=1, source_target_pairs={{0,4},{1,13},{2,6},{3,15},{4,0},{5,9},{6,2},{7,11},{8,12},{9,5},{1... | collective-permute-start | bytes 258056 | tf_op jit(solution)/shard_map/ppermute | solution.py:373
  23.1 5.7 %collective-permute-start.9 = (bf16[32,1344]{1,0:T(8,128)(2,1)S(1)}, bf16[32,1344]{1,0:T(8,128)(2,1)S(1)}, u32[]{:S(2)}, u32[]{:S(2)}) collective-permute-start(bf16[32,1344]{1,0:T(8,128)(2,1)S(1)} %relay.1), channel_id=1, source_target_pairs={{0,8},{1,5},{2,10},{3,7},{4,12},{5,1},{6,14},{7,3},{8,0},{9,13},{1... | collective-permute-start | bytes 258056 | tf_op jit(solution)/shard_map/ppermute | solution.py:373
  29.0 5.6 %collective-permute-start.13 = (bf16[32,1408]{1,0:T(8,128)(2,1)S(1)}, bf16[32,1408]{1,0:T(8,128)(2,1)S(1)}, u32[]{:S(2)}, u32[]{:S(2)}) collective-permute-start(bf16[32,1408]{1,0:T(8,128)(2,1)S(1)} %get-tuple-element.66.rest_0_), channel_id=1, source_target_pairs={{0,8},{4,12},{8,0},{12,4},{1,9},{5,13},{9,1},{13,5},{2,10},{6,14},... | collective-permute-start | bytes 270344 | tf_op jit(solution)/shard_map/ppermute | solution.py:363
  30.5 7.9 %collective-permute-start.12 = (bf16[32,1408]{1,0:T(8,128)(2,1)S(1)}, bf16[32,1408]{1,0:T(8,128)(2,1)S(1)}, u32[]{:S(2)}, u32[]{:S(2)}) collective-permute-start(bf16[32,1408]{1,0:T(8,128)(2,1)S(1)} %get-tuple-element.66.rest_0_), channel_id=1, source_target_pairs={{0,6},{1,7},{2,4},{3,5},{4,2},{5,3},{6,0},{7,1},{8,14},{9,15},{10,... | collective-permute-start | bytes 270344 | tf_op jit(solution)/shard_map/ppermute | solution.py:363
  33.8 5.6 %collective-permute-start.11 = (bf16[32,1408]{1,0:T(8,128)(2,1)S(1)}, bf16[32,1408]{1,0:T(8,128)(2,1)S(1)}, u32[]{:S(2)}, u32[]{:S(2)}) collective-permute-start(bf16[32,1408]{1,0:T(8,128)(2,1)S(1)} %get-tuple-element.66.rest_0_), channel_id=1, source_target_pairs={{0,4},{1,5},{2,6},{3,7},{4,0},{5,1},{6,2},{7,3},{8,12},{9,13},{10,... | collective-permute-start | bytes 270344 | tf_op jit(solution)/shard_map/ppermute | solution.py:363
  33.8 7.1 %collective-permute-start.10 = (bf16[32,1408]{1,0:T(8,128)(2,1)S(1)}, bf16[32,1408]{1,0:T(8,128)(2,1)S(1)}, u32[]{:S(2)}, u32[]{:S(2)}) collective-permute-start(bf16[32,1408]{1,0:T(8,128)(2,1)S(1)} %get-tuple-element.66.rest_0_), channel_id=1, source_target_pairs={{0,2},{1,3},{2,0},{3,1},{4,6},{5,7},{6,4},{7,5},{8,10},{9,11},{10,... | collective-permute-start | bytes 270344 | tf_op jit(solution)/shard_map/ppermute | solution.py:363
  34.6 9.0 %collective-permute-start.16 = (bf16[32,1408]{1,0:T(8,128)(2,1)S(1)}, bf16[32,1408]{1,0:T(8,128)(2,1)S(1)}, u32[]{:S(2)}, u32[]{:S(2)}) collective-permute-start(bf16[32,1408]{1,0:T(8,128)(2,1)S(1)} %collective-permute-done.13.rest_0_), channel_id=1, source_target_pairs={{0,6},{1,7},{2,4},{3,5},{4,2},{5,3},{6,0},{7,1},{8,14},{9,15},{10,... | collective-permute-start | bytes 270344 | tf_op jit(solution)/shard_map/ppermute | solution.py:363
  37.3 6.3 %collective-permute-start.15 = (bf16[32,1408]{1,0:T(8,128)(2,1)S(1)}, bf16[32,1408]{1,0:T(8,128)(2,1)S(1)}, u32[]{:S(2)}, u32[]{:S(2)}) collective-permute-start(bf16[32,1408]{1,0:T(8,128)(2,1)S(1)} %collective-permute-done.13.rest_0_), channel_id=1, source_target_pairs={{0,4},{1,5},{2,6},{3,7},{4,0},{5,1},{6,2},{7,3},{8,12},{9,13},{10,... | collective-permute-start | bytes 270344 | tf_op jit(solution)/shard_map/ppermute | solution.py:363
  38.4 5.2 %collective-permute-start.14 = (bf16[32,1408]{1,0:T(8,128)(2,1)S(1)}, bf16[32,1408]{1,0:T(8,128)(2,1)S(1)}, u32[]{:S(2)}, u32[]{:S(2)}) collective-permute-start(bf16[32,1408]{1,0:T(8,128)(2,1)S(1)} %collective-permute-done.13.rest_0_), channel_id=1, source_target_pairs={{0,2},{1,3},{2,0},{3,1},{4,6},{5,7},{6,4},{7,5},{8,10},{9,11},{10,... | collective-permute-start | bytes 270344 | tf_op jit(solution)/shard_map/ppermute | solution.py:363
  46.4 6.0 %collective-permute-start.17 = (bf16[32,1344]{1,0:T(8,128)(2,1)S(1)}, bf16[32,1344]{1,0:T(8,128)(2,1)S(1)}, u32[]{:S(2)}, u32[]{:S(2)}) collective-permute-start(bf16[32,1344]{1,0:T(8,128)(2,1)S(1)} %get-tuple-element.77), channel_id=1, source_target_pairs={{0,2},{1,3},{2,0},{3,1},{4,6},{5,7},{6,4},{7,5},{8,10},{9,11},{10,... | collective-permute-start | bytes 258056 | tf_op jit(solution)/shard_map/ppermute | solution.py:363
  46.4 7.0 %collective-permute-start.18 = (bf16[32,1344]{1,0:T(8,128)(2,1)S(1)}, bf16[32,1344]{1,0:T(8,128)(2,1)S(1)}, u32[]{:S(2)}, u32[]{:S(2)}) collective-permute-start(bf16[32,1344]{1,0:T(8,128)(2,1)S(1)} %get-tuple-element.78), channel_id=1, source_target_pairs={{0,4},{1,5},{2,6},{3,7},{4,0},{5,1},{6,2},{7,3},{8,12},{9,13},{10,... | collective-permute-start | bytes 258056 | tf_op jit(solution)/shard_map/ppermute | solution.py:363
  48.1 6.4 %collective-permute-start.19 = (bf16[32,1344]{1,0:T(8,128)(2,1)S(1)}, bf16[32,1344]{1,0:T(8,128)(2,1)S(1)}, u32[]{:S(2)}, u32[]{:S(2)}) collective-permute-start(bf16[32,1344]{1,0:T(8,128)(2,1)S(1)} %get-tuple-element.79), channel_id=1, source_target_pairs={{0,6},{1,7},{2,4},{3,5},{4,2},{5,3},{6,0},{7,1},{8,14},{9,15},{10,... | collective-permute-start | bytes 258056 | tf_op jit(solution)/shard_map/ppermute | solution.py:363
  49.9 5.9 %collective-permute-start.21 = (bf16[32,1344]{1,0:T(8,128)(2,1)S(1)}, bf16[32,1344]{1,0:T(8,128)(2,1)S(1)}, u32[]{:S(2)}, u32[]{:S(2)}) collective-permute-start(bf16[32,1344]{1,0:T(8,128)(2,1)S(1)} %get-tuple-element.80), channel_id=1, source_target_pairs={{0,4},{1,5},{2,6},{3,7},{4,0},{5,1},{6,2},{7,3},{8,12},{9,13},{10,... | collective-permute-start | bytes 258056 | tf_op jit(solution)/shard_map/ppermute | solution.py:363
  50.2 6.3 %collective-permute-start.22 = (bf16[32,1344]{1,0:T(8,128)(2,1)S(1)}, bf16[32,1344]{1,0:T(8,128)(2,1)S(1)}, u32[]{:S(2)}, u32[]{:S(2)}) collective-permute-start(bf16[32,1344]{1,0:T(8,128)(2,1)S(1)} %get-tuple-element.81), channel_id=1, source_target_pairs={{0,6},{1,7},{2,4},{3,5},{4,2},{5,3},{6,0},{7,1},{8,14},{9,15},{10,... | collective-permute-start | bytes 258056 | tf_op jit(solution)/shard_map/ppermute | solution.py:363
  52.4 5.0 %collective-permute-start.23 = (bf16[32,1344]{1,0:T(8,128)(2,1)S(1)}, bf16[32,1344]{1,0:T(8,128)(2,1)S(1)}, u32[]{:S(2)}, u32[]{:S(2)}) collective-permute-start(bf16[32,1344]{1,0:T(8,128)(2,1)S(1)} %get-tuple-element.82), channel_id=1, source_target_pairs={{0,2},{1,3},{2,0},{3,1},{4,6},{5,7},{6,4},{7,5},{8,10},{9,11},{10,... | collective-permute-start | bytes 258056 | tf_op jit(solution)/shard_map/ppermute | solution.py:363
  54.6 6.5 %collective-permute-start.20 = (bf16[32,1344]{1,0:T(8,128)(2,1)S(1)}, bf16[32,1344]{1,0:T(8,128)(2,1)S(1)}, u32[]{:S(2)}, u32[]{:S(2)}) collective-permute-start(bf16[32,1344]{1,0:T(8,128)(2,1)S(1)} %sum.1), channel_id=1, source_target_pairs={{0,8},{4,12},{8,0},{12,4},{1,9},{5,13},{9,1},{13,5},{2,10},{6,14},... | collective-permute-start | bytes 258056 | tf_op jit(solution)/shard_map/ppermute | solution.py:363
